TPU v7x, 32 devices: a whole 2x2x4 slice. The times are simulated.
32 devices in a mesh: dp: 4 (over y, x), ctx: 8 (over z, core).
Axes of the slice: x: 2, y: 2, z: 4, core: 2. Of those that a mesh axis runs over, the one named last changes fastest.
Arguments:
- queries: bfloat16 [4, 2048, 512], P('dp', 'ctx'), may hold values from -6 to 6
- keys: bfloat16 [4, 2048, 512], P('dp', 'ctx'), may hold values from -6 to 6
- values: bfloat16 [4, 2048, 512], P('dp', 'ctx'), may hold values from -24 to 24
- out_grad: bfloat16 [4, 2048, 1024], P('dp', 'ctx'), may hold values from -6 to 6
- w_out: bfloat16 [512, 1024], replicated, may hold values from -0.25 to 0.25
- block_mask: int32 [4, 16, 3], P('dp'), may hold values 0 or 1
Outputs:
- output: bfloat16 [4, 2048, 1024], P('dp', 'ctx')
- query_grad: bfloat16 [4, 2048, 512], P('dp', 'ctx')
- key_grad: bfloat16 [4, 2048, 512], P('dp', 'ctx')
- value_grad: bfloat16 [4, 2048, 512], P('dp', 'ctx')
- weight_grad: float32 [512, 1024], P('ctx')
All inputs are finite; a program needn't handle non-finite values. No bound on the sum of `block_mask` on one device may be relied on, other than what follows from the above.
Results may differ from a plain program's by a relative error of at most 0.038.
Values may be sent and summed in bfloat16 or wider, within the bound.
No kernel may reach another device: no remote copies, remote signals or barrier semaphores. Data moves between devices by JAX's collectives and lax.ppermute only.
A program may use at most 64 MiB of HBM per device.

v0:
```python
import jax
import jax.numpy as jnp
from jax import lax
from jax.sharding import PartitionSpec as P

HEADS = 8
HD = 64
BLK = 128
RAD = 1


big_negative = -1e30


def with_halo(block, sides, width):
    for axis, dim in sides:
        count = lax.axis_size(axis)
        forward = [(i, i + 1) for i in range(count - 1)]
        forward.append((count - 1, 0))
        backward = [(target, source) for source, target in forward]
        low = lax.ppermute(
            lax.slice_in_dim(block, block.shape[dim] - width, None, axis=dim), axis, forward
        )
        high = lax.ppermute(lax.slice_in_dim(block, 0, width, axis=dim), axis, backward)
        block = jnp.concatenate([low, block, high], axis=dim)
    return block


def shifted(value, axis, steps):
    count = lax.axis_size(axis)
    pairs = [(source, (source + steps) % count) for source in range(count)]
    return lax.ppermute(value, axis, pairs)


def allowed_keys(mask_rows):
    centre = (jnp.arange(2 * RAD + 1) == RAD)[None, :]
    allowed = (mask_rows == 1) | centre
    return jnp.repeat(allowed, BLK, axis=1)


def body(queries, keys, values, out_grad, w_out, block_mask):
    query_rows = queries[0]
    key_rows = keys[0]
    value_rows = values[0]
    grad_rows = out_grad[0]
    tok_count = query_rows.shape[0]
    feat_count = query_rows.shape[1]
    blocks_here = tok_count // BLK
    rim_rows = RAD * BLK
    span_rows = (2 * RAD + 1) * BLK
    group_width = 2 * HD
    score_scale = HD ** (-0.5)
    position = lax.axis_index("ctx")
    pattern = block_mask[0]
    pattern_pad = jnp.concatenate([pattern[-RAD:], pattern, pattern[:RAD]], axis=0)
    own_pattern = lax.dynamic_slice_in_dim(
        pattern_pad, position * blocks_here + RAD, blocks_here, 0
    )
    query_allow = allowed_keys(own_pattern)
    key_value = jnp.stack([key_rows, value_rows])
    extended = with_halo(key_value, (("ctx", 1),), rim_rows)
    windows = jnp.stack(
        [
            extended[:, row_block * BLK : row_block * BLK + span_rows]
            for row_block in range(blocks_here)
        ]
    )
    attn_grad = lax.dot_general(
        grad_rows, w_out, (((1,), (1,)), ((), ())), preferred_element_type=jnp.float32
    ).astype(jnp.bfloat16)
    attn_parts = []
    query_parts = []
    key_parts = []
    value_parts = []
    for head_group in range(HEADS // 2):
        columns = slice(head_group * group_width, (head_group + 1) * group_width)
        q_block = query_rows[:, columns].reshape(blocks_here, BLK, 2, HD)
        k_window = windows[:, 0, :, columns].reshape(blocks_here, span_rows, 2, HD)
        v_window = windows[:, 1, :, columns].reshape(blocks_here, span_rows, 2, HD)
        g_block = attn_grad[:, columns].reshape(blocks_here, BLK, 2, HD)
        scores = (
            jnp.einsum("bqhd,bkhd->bhqk", q_block, k_window, preferred_element_type=jnp.float32)
            * score_scale
        )
        scores = jnp.where(query_allow[:, None, None, :], scores, big_negative)
        row_max = jnp.max(scores, axis=-1, keepdims=True)
        log_total = row_max + jnp.log(jnp.sum(jnp.exp(scores - row_max), axis=-1, keepdims=True))
        probs = jnp.exp(scores - log_total)
        probs_bf = probs.astype(jnp.bfloat16)
        attn_block = jnp.einsum(
            "bhqk,bkhd->bqhd", probs_bf, v_window, preferred_element_type=jnp.float32
        ).astype(jnp.bfloat16)
        row_delta = jnp.sum(g_block.astype(jnp.float32) * attn_block.astype(jnp.float32), axis=-1)
        row_delta = jnp.transpose(row_delta, (0, 2, 1))[..., None]
        dprob = jnp.einsum("bqhd,bkhd->bhqk", g_block, v_window, preferred_element_type=jnp.float32)
        dscore = (probs * (dprob - row_delta) * score_scale).astype(jnp.bfloat16)
        query_part = jnp.einsum(
            "bhqk,bkhd->bqhd", dscore, k_window, preferred_element_type=jnp.float32
        )
        attn_parts.append(attn_block.reshape(tok_count, group_width))
        query_parts.append(query_part.reshape(tok_count, group_width).astype(jnp.bfloat16))
        key_window_part = jnp.einsum(
            "bhqk,bqhd->bkhd", dscore, q_block, preferred_element_type=jnp.float32
        )
        value_window_part = jnp.einsum(
            "bhqk,bqhd->bkhd", probs_bf, g_block, preferred_element_type=jnp.float32
        )
        key_parts.append(key_window_part.reshape(blocks_here, span_rows, group_width))
        value_parts.append(value_window_part.reshape(blocks_here, span_rows, group_width))
    attn = jnp.concatenate(attn_parts, axis=1)
    output = jnp.dot(attn, w_out, preferred_element_type=jnp.float32).astype(jnp.bfloat16)
    query_grad = jnp.concatenate(query_parts, axis=1)
    key_windows = jnp.concatenate(key_parts, axis=2)
    value_windows = jnp.concatenate(value_parts, axis=2)
    window_pairs = jnp.stack([key_windows, value_windows], axis=1)
    window_sums = jnp.zeros((2, tok_count + 2 * rim_rows, feat_count), jnp.float32)
    for row_block in range(blocks_here):
        first_row = row_block * BLK
        window_sums = window_sums.at[:, first_row : first_row + span_rows].add(
            window_pairs[row_block]
        )
    from_right = shifted(window_sums[:, :rim_rows], "ctx", -1)
    from_left = shifted(window_sums[:, rim_rows + tok_count :], "ctx", 1)
    own_sums = window_sums[:, rim_rows : rim_rows + tok_count]
    own_sums = own_sums.at[:, tok_count - rim_rows :].add(from_right)
    own_sums = own_sums.at[:, :rim_rows].add(from_left)
    key_grad = own_sums[0].astype(jnp.bfloat16)
    value_grad = own_sums[1].astype(jnp.bfloat16)
    weight_share = lax.psum_scatter(
        lax.dot_general(
            attn, grad_rows, (((0,), (0,)), ((), ())), preferred_element_type=jnp.float32
        ),
        "ctx",
        scatter_dimension=0,
        tiled=True,
    )
    weight_total = lax.psum(weight_share, "dp")
    weight_grad = weight_total * (lax.axis_size("dp") * tok_count * lax.axis_size("ctx")) ** (-0.5)
    return (output[None], query_grad[None], key_grad[None], value_grad[None], weight_grad)


def solution(mesh):
    placed = (
        P("dp", "ctx", None),
        P("dp", "ctx", None),
        P("dp", "ctx", None),
        P("dp", "ctx", None),
        P(),
        P("dp", None, None),
    )
    return jax.shard_map(
        body,
        mesh=mesh,
        in_specs=placed,
        out_specs=(
            P("dp", "ctx", None),
            P("dp", "ctx", None),
            P("dp", "ctx", None),
            P("dp", "ctx", None),
            P("ctx", None),
        ),
        check_vma=False,
    )
```

profile of v0, /device:TPU:0, one launch (start us, length us, event | category | flops | bytes accessed | tf_op | source)
XLA Modules:
  0.0 129.8 jit_solution(3972699179603455071)
XLA Ops:
  7.2 1.1 constant_dynamic-update-slice_fusion.1
  8.3 1.0 constant_dynamic-update-slice_fusion
  9.3 0.7 fusion.64
  10.0 4.5 %collective-permute-start.1 = (bf16[2,128,512]{2,1,0:T(8,128)(2,1)}, bf16[2,128,512]{2,1,0:T(8,128)(2,1)S(1)}, u32[]{:S(2)}, u32[]{:S(2)}) collective-permute-start(bf16[2,128,512]{2,1,0:T(8,128)(2,1)} %get-tuple-element.72), channel_id=1, source_target_pairs={{1,0},{2,1},{3,2},{4,3},{5,4},{6,5},{7,6},{0,7},{9,8},{10,9},{11,1... | collective-permute-start | bytes 786440 | tf_op jit(solution)/shard_map/ppermute | solution.py:24
  14.9 0.5 convolution_convert_fusion.1
  16.6 0.7 copy.74
  17.7 0.7 copy.62
  18.5 0.7 copy.56
  19.4 3.1 %collective-permute-done = bf16[2,128,512]{2,1,0:T(8,128)(2,1)S(1)} collective-permute-done((bf16[2,128,512]{2,1,0:T(8,128)(2,1)S(1)}, bf16[2,128,512]{2,1,0:T(8,128)(2,1)S(1)}, u32[]{:S(2)}, u32[]{:S(2)}) %collective-permute-start) | collective-permute-done | bytes 262176 | tf_op jit(solution)/shard_map/ppermute | solution.py:21
  22.6 0.4 pad_maximum_fusion.1
  23.3 0.4 fusion.70
  24.2 0.9 multiply_reduce_fusion.1
  25.4 0.9 fusion.31
  26.6 0.8 copy.72
  28.2 0.8 copy.71
  29.0 1.5 %copy.70 = bf16[2,128,2,64]{1,0,3,2:T(2,128)(2,1)} copy(bf16[2,128,2,64]{1,3,2,0:T(8,128)(2,1)} %get-tuple-element.95) | data formatting | bytes 131072 | tf_op jit(solution)/shard_map/convert_element_type | solution.py:92
  30.5 0.9 copy.111
  31.5 0.6 copy.187
  32.2 0.9 copy.123
  33.6 0.9 multiply_reduce_fusion.2
  34.6 0.4 fusion.68
  35.5 0.4 fusion.71
  36.1 0.9 multiply_reduce_fusion
  37.1 0.7 copy-done.21
  37.8 1.8 %fusion.39 = f32[512,1024]{1,0:T(8,128)} fusion(bf16[256,512]{0,1:T(8,128)(2,1)S(1)} %bitcast_dynamic-update-slice_fusion, bf16[1,256,1024]{2,1,0:T(8,128)(2,1)S(1)} %copy-done.6), kind=kOutput, calls=%fused_computation.89 | convolution fusion | flops 268435456 | bytes 2883584 | tf_op jit(solution)/shard_map/dot_general | solution.py:130
  39.7 1.3 fusion.21
  41.0 0.7 copy-done.1
  41.7 1.9 %fusion.73 = f32[2,2,384,64]{2,3,1,0:T(8,128)} fusion(bf16[2,2,128,384]{2,3,1,0:T(8,128)(2,1)S(1)} %fusion.21, bf16[2,128,2,64]{1,3,2,0:T(8,128)(2,1)} %copy.62), kind=kOutput, calls=%fused_computation.144 | convolution fusion | flops 25165824 | bytes 851968 | tf_op jit(solution)/shard_map/bhqk,bqhd->bkhd/dot_general | solution.py:102
  43.6 1.9 %copy.110 = f32[2,384,128]{2,1,0:T(8,128)} copy(f32[2,384,128]{1,2,0:T(8,128)} %bitcast.213) | data formatting | bytes 786432 | tf_op jit(solution)/shard_map/reshape | solution.py:108
  45.5 1.9 %fusion.55 = f32[2,2,64,384]{3,2,1,0:T(8,128)} fusion(bf16[2,128,2,64]{1,3,2,0:T(8,128)(2,1)} %copy-done.23, f32[2,2,128,384]{2,3,1,0:T(8,128)S(1)} %get-tuple-element.87, f32[2,2,128]{2,1,0:T(2,128)S(1)} %log_add_fusion.2), kind=kOutput, calls=%fused_computation.108 | convolution fusion | flops 25559040 | bytes 1247232 | tf_op jit(solution)/shard_map/bhqk,bqhd->bkhd/dot_general | solution.py:105
  47.4 1.9 %copy.122 = f32[2,384,128]{2,1,0:T(8,128)} copy(f32[2,384,128]{1,2,0:T(8,128)} %bitcast.209) | data formatting | bytes 786432 | tf_op jit(solution)/shard_map/reshape | solution.py:109
  49.3 1.3 fusion.20
  50.6 1.1 fusion.72
  51.7 2.0 %copy.109 = f32[2,384,128]{2,1,0:T(8,128)} copy(f32[2,384,128]{1,2,0:T(8,128)} %bitcast.214) | data formatting | bytes 786432 | tf_op jit(solution)/shard_map/reshape | solution.py:108
  53.7 1.1 fusion.58
  54.7 2.0 %copy.121 = f32[2,384,128]{2,1,0:T(8,128)} copy(f32[2,384,128]{1,2,0:T(8,128)} %bitcast.210) | data formatting | bytes 786432 | tf_op jit(solution)/shard_map/reshape | solution.py:109
  56.7 0.4 fusion.23
  57.4 0.9 copy.112
  58.8 1.4 %maximum_bitcast_fusion = f32[2,1,384,512]{3,2,1,0:T(8,128)S(1)} fusion(f32[2,384,128]{2,1,0:T(8,128)} %copy.112, f32[2,384,128]{2,1,0:T(8,128)S(1)} %copy-done.17, f32[2,384,128]{2,1,0:T(8,128)} %copy.110, f32[2,384,128]{2,1,0:T(8,128)} %copy.109), kind=kLoop, calls=%fused_computation.22 | loop fusion | flops 1179648 | bytes 3145728 | tf_op jit(solution)/shard_map/stack | solution.py:115
  60.7 0.7 collective-permute-start.2
  62.6 11.1 %collective-permute-done.2 = f32[2,128,512]{2,1,0:T(8,128)S(1)} collective-permute-done((f32[2,128,512]{2,1,0:T(8,128)S(1)}, f32[2,128,512]{2,1,0:T(8,128)S(1)}, u32[]{:S(2)}, u32[]{:S(2)}) %collective-permute-start.2) | collective-permute-done | bytes 524320 | tf_op jit(solution)/shard_map/ppermute | solution.py:32
  74.5 0.8 copy.125
  75.3 1.3 fusion.24
  76.6 8.0 %collective-permute-done.3 = f32[2,128,512]{2,1,0:T(8,128)} collective-permute-done((f32[2,128,512]{2,1,0:T(8,128)S(1)}, f32[2,128,512]{2,1,0:T(8,128)}, u32[]{:S(2)}, u32[]{:S(2)}) %collective-permute-start.3) | collective-permute-done | bytes 524320 | tf_op jit(solution)/shard_map/ppermute | solution.py:32
  84.6 1.2 fusion.37
  85.8 0.8 fusion.63
  86.6 34.6 %all-reduce.3.cloned.1.call-done = f32[64,1024]{1,0:T(8,128)} async-done(((f32[64,1024]{1,0:T(8,128)}), f32[64,1024]{1,0:T(8,128)}) %all-reduce.3.cloned.1.call-update) | async-done | bytes 262160 | tf_op jit(solution)/shard_map/psum | solution.py:137
  121.3 1.7 %broadcast_multiply_fusion = f32[64,1024]{1,0:T(8,128)} fusion(f32[64,1024]{1,0:T(8,128)} %all-reduce.3.cloned.1.call-done), kind=kLoop, calls=%fused_computation.101 | loop fusion | flops 65536 | bytes 524288 | tf_op jit(solution)/shard_map/mul | solution.py:138
  (148 shorter events, 9.0 us)
Async XLA Ops:
  7.2 7.7 %copy-start = (bf16[512,1024]{1,0:T(8,128)(2,1)S(1)}, bf16[512,1024]{1,0:T(8,128)(2,1)}, u32[]{:S(2)}) copy-start(bf16[512,1024]{1,0:T(8,128)(2,1)} %param.18) | copy-start | bytes 3145732
  7.2 7.4 %copy-start.33 = (s32[1,16,3]{1,0,2:T(1,128)S(1)}, s32[1,16,3]{1,0,2:T(1,128)}, u32[]{:S(2)}) copy-start(s32[1,16,3]{1,0,2:T(1,128)} %param.19) | copy-start | bytes 580
  7.2 7.7 %copy-start.5 = (bf16[1,256,1024]{2,1,0:T(8,128)(2,1)S(1)}, bf16[1,256,1024]{2,1,0:T(8,128)(2,1)}, u32[]{:S(2)}) copy-start(bf16[1,256,1024]{2,1,0:T(8,128)(2,1)} %param.17) | copy-start | bytes 1572868
  7.2 69.4 %reduce-scatter.2.cloned.1.call-start = ((), (), s32[]{:S(2)}) async-start(), calls=%async_computation.1 | async-start | bytes 2359296 | tf_op jit(solution)/shard_map/reduce_scatter | solution.py:129
  10.0 9.3 %collective-permute-start.1 = (bf16[2,128,512]{2,1,0:T(8,128)(2,1)}, bf16[2,128,512]{2,1,0:T(8,128)(2,1)S(1)}, u32[]{:S(2)}, u32[]{:S(2)}) collective-permute-start(bf16[2,128,512]{2,1,0:T(8,128)(2,1)} %get-tuple-element.72), channel_id=1, source_target_pairs={{1,0},{2,1},{3,2},{4,3},{5,4},{6,5},{7,6},{0,7},{9,8},{10,9},{11,1... | collective-permute-start | bytes 786440 | tf_op jit(solution)/shard_map/ppermute | solution.py:24
  14.5 7.9 %collective-permute-start = (bf16[2,128,512]{2,1,0:T(8,128)(2,1)S(1)}, bf16[2,128,512]{2,1,0:T(8,128)(2,1)S(1)}, u32[]{:S(2)}, u32[]{:S(2)}) collective-permute-start(bf16[2,128,512]{2,1,0:T(8,128)(2,1)S(1)} %get-tuple-element.73), channel_id=1, source_target_pairs={{0,1},{1,2},{2,3},{3,4},{4,5},{5,6},{6,7},{7,0},{8,9},{9,10},{10,1... | collective-permute-start | bytes 786440 | tf_op jit(solution)/shard_map/ppermute | solution.py:21
  14.9 1.5 %copy-start.30 = (bf16[1,256,512]{2,1,0:T(8,128)(2,1)S(1)}, bf16[1,256,512]{2,1,0:T(8,128)(2,1)}, u32[]{:S(2)}) copy-start(bf16[1,256,512]{2,1,0:T(8,128)(2,1)} %param.14) | copy-start | bytes 786436
  16.4 17.2 %copy-start.23 = (bf16[2,128,2,64]{1,3,2,0:T(8,128)(2,1)}, bf16[2,128,2,64]{1,3,2,0:T(8,128)(2,1)S(1)}, u32[]{:S(2)}) copy-start(bf16[2,128,2,64]{1,3,2,0:T(8,128)(2,1)S(1)} %copy.84) | copy-start | bytes 196612
  27.4 4.1 %copy-start.29 = (bf16[2,128,2,64]{1,3,2,0:T(8,128)(2,1)S(1)}, bf16[2,128,2,64]{1,3,2,0:T(8,128)(2,1)}, u32[]{:S(2)}) copy-start(bf16[2,128,2,64]{1,3,2,0:T(8,128)(2,1)} %fusion.31) | copy-start | bytes 196612
  27.6 7.5 %copy-start.15 = (bf16[2,1,384,128]{2,3,0,1:T(8,128)(2,1)}, bf16[2,1,384,128]{2,3,0,1:T(8,128)(2,1)S(1)}, u32[]{:S(2)}) copy-start(bf16[2,1,384,128]{2,3,0,1:T(8,128)(2,1)S(1)} %copy.50) | copy-start | bytes 589828
  27.8 6.8 %copy-start.9 = (bf16[2,1,384,128]{2,3,0,1:T(8,128)(2,1)}, bf16[2,1,384,128]{2,3,0,1:T(8,128)(2,1)S(1)}, u32[]{:S(2)}) copy-start(bf16[2,1,384,128]{2,3,0,1:T(8,128)(2,1)S(1)} %copy.54) | copy-start | bytes 589828
  27.8 5.3 %copy-start.28 = (bf16[2,128,2,64]{1,3,2,0:T(8,128)(2,1)S(1)}, bf16[2,128,2,64]{1,3,2,0:T(8,128)(2,1)}, u32[]{:S(2)}) copy-start(bf16[2,128,2,64]{1,3,2,0:T(8,128)(2,1)} %copy.62) | copy-start | bytes 196612
  28.0 5.7 %copy-start.16 = (bf16[2,1,384,128]{2,3,0,1:T(8,128)(2,1)}, bf16[2,1,384,128]{2,3,0,1:T(8,128)(2,1)S(1)}, u32[]{:S(2)}) copy-start(bf16[2,1,384,128]{2,3,0,1:T(8,128)(2,1)S(1)} %copy.59) | copy-start | bytes 589828
  28.1 5.3 %copy-start.11 = (bf16[2,1,384,128]{2,3,0,1:T(8,128)(2,1)}, bf16[2,1,384,128]{2,3,0,1:T(8,128)(2,1)S(1)}, u32[]{:S(2)}) copy-start(bf16[2,1,384,128]{2,3,0,1:T(8,128)(2,1)S(1)} %copy.60) | copy-start | bytes 589828
  33.1 1.5 %copy-start.26 = (bf16[2,128,2,64]{1,3,2,0:T(8,128)(2,1)S(1)}, bf16[2,128,2,64]{1,3,2,0:T(8,128)(2,1)}, u32[]{:S(2)}) copy-start(bf16[2,128,2,64]{1,3,2,0:T(8,128)(2,1)} %copy.56) | copy-start | bytes 196612
  34.6 0.9 copy-start.7
  34.6 0.9 copy-start.24
  35.1 1.0 copy-start.13
  35.5 1.5 %copy-start.31 = (bf16[2,128,2,64]{1,0,3,2:T(2,128)(2,1)S(1)}, bf16[2,128,2,64]{1,0,3,2:T(2,128)(2,1)}, u32[]{:S(2)}) copy-start(bf16[2,128,2,64]{1,0,3,2:T(2,128)(2,1)} %copy.70) | copy-start | bytes 196612
  35.5 2.3 %copy-start.6 = (bf16[1,256,1024]{2,1,0:T(8,128)(2,1)S(1)}, bf16[1,256,1024]{2,1,0:T(8,128)(2,1)}, u32[]{:S(2)}) copy-start(bf16[1,256,1024]{2,1,0:T(8,128)(2,1)} %param.17) | copy-start | bytes 1572868
  37.1 0.7 copy-start.21
  39.6 81.7 %all-reduce.3.cloned.1.call-start = ((), (), s32[]{:S(2)}) async-start(), calls=%async_computation.2 | async-start | bytes 524288 | tf_op jit(solution)/shard_map/psum | solution.py:137
  40.9 0.7 copy-start.1
  47.4 3.2 %copy-start.27 = (bf16[2,128,2,64]{1,3,2,0:T(8,128)(2,1)S(1)}, bf16[2,128,2,64]{1,3,2,0:T(8,128)(2,1)}, u32[]{:S(2)}) copy-start(bf16[2,128,2,64]{1,3,2,0:T(8,128)(2,1)} %copy.56) | copy-start | bytes 196612
  50.6 6.1 %copy-start.3 = (bf16[2,2,128,384]{2,3,1,0:T(8,128)(2,1)}, bf16[2,2,128,384]{2,3,1,0:T(8,128)(2,1)S(1)}, u32[]{:S(2)}) copy-start(bf16[2,2,128,384]{2,3,1,0:T(8,128)(2,1)S(1)} %fusion.20) | copy-start | bytes 1179652
  51.7 5.0 %copy-start.14 = (bf16[2,1,384,128]{2,3,0,1:T(8,128)(2,1)S(1)}, bf16[2,1,384,128]{2,3,0,1:T(8,128)(2,1)}, u32[]{:S(2)}) copy-start(bf16[2,1,384,128]{2,3,0,1:T(8,128)(2,1)} %copy.71) | copy-start | bytes 589828
  51.7 5.0 %copy-start.34 = (f32[2,128,2]{1,2,0:T(2,128)S(1)}, f32[2,128,2]{1,2,0:T(2,128)}, u32[]{:S(2)}) copy-start(f32[2,128,2]{1,2,0:T(2,128)} %get-tuple-element.92) | copy-start | bytes 6148
  54.7 2.3 %copy-start.25 = (bf16[2,128,2,64]{1,3,2,0:T(8,128)(2,1)S(1)}, bf16[2,128,2,64]{1,3,2,0:T(8,128)(2,1)}, u32[]{:S(2)}) copy-start(bf16[2,128,2,64]{1,3,2,0:T(8,128)(2,1)} %copy.74) | copy-start | bytes 196612
  57.4 1.4 %copy-start.17 = (f32[2,384,128]{2,1,0:T(8,128)S(1)}, f32[2,384,128]{2,1,0:T(8,128)}, u32[]{:S(2)}) copy-start(f32[2,384,128]{2,1,0:T(8,128)} %copy.111) | copy-start | bytes 1179652
  58.8 1.5 %copy-start.18 = (f32[2,384,128]{2,1,0:T(8,128)S(1)}, f32[2,384,128]{2,1,0:T(8,128)}, u32[]{:S(2)}) copy-start(f32[2,384,128]{2,1,0:T(8,128)} %copy.123) | copy-start | bytes 1179652
  58.8 1.5 %copy-start.19 = (f32[2,384,128]{2,1,0:T(8,128)S(1)}, f32[2,384,128]{2,1,0:T(8,128)}, u32[]{:S(2)}) copy-start(f32[2,384,128]{2,1,0:T(8,128)} %copy.122) | copy-start | bytes 1179652
  58.8 1.6 %copy-start.20 = (f32[2,384,128]{2,1,0:T(8,128)S(1)}, f32[2,384,128]{2,1,0:T(8,128)}, u32[]{:S(2)}) copy-start(f32[2,384,128]{2,1,0:T(8,128)} %copy.121) | copy-start | bytes 1179652
  60.5 1.0 copy-start.2
  60.5 1.0 copy-start.12
  60.7 1.2 copy-start.4
  60.7 1.2 copy-start.10
  60.7 12.9 %collective-permute-start.2 = (f32[2,128,512]{2,1,0:T(8,128)S(1)}, f32[2,128,512]{2,1,0:T(8,128)S(1)}, u32[]{:S(2)}, u32[]{:S(2)}) collective-permute-start(f32[2,128,512]{2,1,0:T(8,128)S(1)} %slice.252), channel_id=1, source_target_pairs={{0,7},{1,0},{2,1},{3,2},{4,3},{5,4},{6,5},{7,6},{8,15},{9,8},{10,9... | collective-permute-start | bytes 1572872 | tf_op jit(solution)/shard_map/ppermute | solution.py:32
  62.6 11.5 %copy-start.8 = (bf16[2,1,384,128]{2,3,0,1:T(8,128)(2,1)S(1)}, bf16[2,1,384,128]{2,3,0,1:T(8,128)(2,1)}, u32[]{:S(2)}) copy-start(bf16[2,1,384,128]{2,3,0,1:T(8,128)(2,1)} %copy.72) | copy-start | bytes 589828
  62.6 11.9 %copy-start.32 = (bf16[16,8,2,128]{3,1,2,0:T(8,128)(2,1)S(1)}, bf16[16,8,2,128]{3,1,2,0:T(8,128)(2,1)}, u32[]{:S(2)}) copy-start(bf16[16,8,2,128]{3,1,2,0:T(8,128)(2,1)} %copy.187) | copy-start | bytes 196612
  73.8 1.5 %copy-start.22 = (bf16[256,512]{0,1:T(8,128)(2,1)S(1)}, bf16[256,512]{0,1:T(8,128)(2,1)}, u32[]{:S(2)}) copy-start(bf16[256,512]{0,1:T(8,128)(2,1)} %copy-done.21) | copy-start | bytes 786436
  73.8 10.7 %collective-permute-start.3 = (f32[2,128,512]{2,1,0:T(8,128)S(1)}, f32[2,128,512]{2,1,0:T(8,128)}, u32[]{:S(2)}, u32[]{:S(2)}) collective-permute-start(f32[2,128,512]{2,1,0:T(8,128)S(1)} %get-tuple-element.58), channel_id=1, source_target_pairs={{0,1},{1,2},{2,3},{3,4},{4,5},{5,6},{6,7},{7,0},{8,9},{9,10},{10,1... | collective-permute-start | bytes 1572872 | tf_op jit(solution)/shard_map/ppermute | solution.py:32
Sparse Core Ops, SparseCore 0:
  39.7 36.2 reduce-scatter.1
  79.0 42.2 all-reduce.2
where the time goes:
time: 130 us
  waiting for transfers between devices  56.9 us (44%)
  local copies, waits for them, and re-layouts  26.5 us (20%)
  matrix products  19.7 us (15%)
  between operations  14.9 us (11%)
  other arithmetic  6.24 us (5%)
  starting transfers between devices  5.52 us (4%)
    psum x1, waiting for transfers between devices, body(): weight_total = lax.psum(weight_share, 'dp')  34.6 us
    ppermute x2, waiting for transfers between devices, shifted(): return lax.ppermute(value, axis, pairs)  19 us
    reshape x4, local copies, waits for them, and re-layouts, body(): key_window_part.reshape(blocks_here, span_rows, group_width)  5.76 us
    reshape x4, local copies, waits for them, and re-layouts, body(): value_window_part.reshape(blocks_here, span_rows, group_width)  4.98 us
    unnamed x83, local copies, waits for them, and re-layouts  4.65 us
    ppermute x1, starting transfers between devices, with_halo(): lax.ppermute(lax.slice_in_dim(block, 0, width, axis=dim), axis, backward)  4.49 us
    dot_general x4, matrix products, body(): jnp.einsum('bhqk,bqhd->bkhd', probs_bf, g_block, preferred_element_type=j...  3.57 us
    dot_general x4, matrix products, body(): jnp.einsum('bhqk,bqhd->bkhd', dscore, q_block, preferred_element_type=jnp...  3.51 us
  transfers between devices with their start and end apart: 6, of which 5 were waited for; matrix products, arithmetic and copies ran while one was open for 23% of the time, Pallas kernels for 0%

commit v1 on v0

v1 whole, which is shorter than its diff:
```python
import functools

import jax
import jax.numpy as jnp
from jax import lax
from jax.experimental import pallas as pl
from jax.experimental.pallas import tpu as pltpu
from jax.sharding import PartitionSpec as P

HEADS = 8
HD = 64
BLK = 128
RAD = 1
PAIR = 2 * HD
SPAN = (2 * RAD + 1) * BLK
RIM = RAD * BLK
BIG_NEGATIVE = -1e30
SCALE = HD ** (-0.5)
BF16 = jnp.bfloat16
F32 = jnp.float32


def dot(a, b, contract):
    return lax.dot_general(a, b, (contract, ((), ())), preferred_element_type=F32)


def two_heads(block):
    lane = lax.broadcasted_iota(jnp.int32, block.shape, 1)
    zero = jnp.zeros_like(block)
    return jnp.concatenate(
        [jnp.where(lane < HD, block, zero), jnp.where(lane < HD, zero, block)], axis=0
    )


def own_features(both):
    return jnp.concatenate([both[:HD, :BLK], both[HD:, BLK:]], axis=0)


def extend(ext, own, low, high, which):
    rows = own.shape[0]
    ext[:RIM] = low[which]
    ext[RIM : RIM + rows] = own[...]
    ext[RIM + rows :] = high[which]


def probabilities(mask, b, q2, k_win):
    scores = dot(k_win, q2, ((1,), (1,)))
    parts = []
    for c in range(2 * RAD + 1):
        part = scores[c * BLK : (c + 1) * BLK]
        if c != RAD:
            part = jnp.where(mask[b, c] == 1, part, BIG_NEGATIVE)
        parts.append(part)
    scores = jnp.concatenate(parts, axis=0)
    top = jnp.max(scores, axis=0, keepdims=True)
    e = jnp.exp(scores - top)
    return e * (1.0 / jnp.sum(e, axis=0, keepdims=True))


def forward_kernel(mask, q, k, v, low, high, g, attn_t, part, k_ext, v_ext):
    extend(k_ext, k, low, high, 0)
    extend(v_ext, v, low, high, 1)
    for b in range(q.shape[0] // BLK):
        rows = slice(b * BLK, (b + 1) * BLK)
        window = slice(b * BLK, b * BLK + SPAN)
        for p in range(HEADS // 2):
            cols = slice(p * PAIR, (p + 1) * PAIR)
            q2 = two_heads(q[rows, cols] * SCALE)
            probs = probabilities(mask, b, q2, k_ext[window, cols]).astype(BF16)
            both = dot(v_ext[window, cols], probs, ((0,), (0,)))
            attn_t[cols, rows] = own_features(both).astype(BF16)
    part[...] = dot(attn_t[...], g[...], ((1,), (0,))).astype(BF16)


def backward_kernel(
    mask, q, k, v, low, high, ag, q_grad, k_own, v_own, to_low, to_high, k_ext, v_ext, dk, dv
):
    extend(k_ext, k, low, high, 0)
    extend(v_ext, v, low, high, 1)
    tokens = q.shape[0]
    for b in range(tokens // BLK):
        rows = slice(b * BLK, (b + 1) * BLK)
        window = slice(b * BLK, b * BLK + SPAN)
        old = slice(b * BLK, b * BLK + SPAN - BLK)
        new = slice(b * BLK + SPAN - BLK, b * BLK + SPAN)
        for p in range(HEADS // 2):
            cols = slice(p * PAIR, (p + 1) * PAIR)
            q2 = two_heads(q[rows, cols] * SCALE)
            g2 = two_heads(ag[rows, cols])
            k_win = k_ext[window, cols]
            v_win = v_ext[window, cols]
            probs = probabilities(mask, b, q2, k_win)
            dprob = dot(v_win, g2, ((1,), (1,)))
            delta = jnp.sum(probs * dprob, axis=0, keepdims=True)
            dscore = (probs * (dprob - delta)).astype(BF16)
            dq_t = dot(k_win, dscore, ((0,), (0,)))
            q_grad[rows, cols] = (own_features(dq_t) * SCALE).T.astype(BF16)
            k_part = dot(dscore, q2, ((1,), (0,)))
            v_part = dot(probs.astype(BF16), g2, ((1,), (0,)))
            if b == 0:
                dk[window, cols] = k_part
                dv[window, cols] = v_part
            else:
                dk[old, cols] += k_part[: SPAN - BLK]
                dv[old, cols] += v_part[: SPAN - BLK]
                dk[new, cols] = k_part[SPAN - BLK :]
                dv[new, cols] = v_part[SPAN - BLK :]
    k_own[...] = dk[RIM : RIM + tokens]
    v_own[...] = dv[RIM : RIM + tokens]
    to_low[0] = dk[:RIM].astype(BF16)
    to_low[1] = dv[:RIM].astype(BF16)
    to_high[0] = dk[RIM + tokens :].astype(BF16)
    to_high[1] = dv[RIM + tokens :].astype(BF16)


def call(kernel, outs, scratch, flops, *args):
    in_vmem = pl.BlockSpec(memory_space=pltpu.VMEM)
    return pl.pallas_call(
        kernel,
        out_shape=[jax.ShapeDtypeStruct(s, d) for s, d in outs],
        in_specs=[pl.BlockSpec(memory_space=pltpu.SMEM)] + [in_vmem] * (len(args) - 1),
        out_specs=[in_vmem] * len(outs),
        scratch_shapes=[pltpu.VMEM(s, d) for s, d in scratch],
        compiler_params=pltpu.CompilerParams(vmem_limit_bytes=32 * 1024 * 1024),
        cost_estimate=pl.CostEstimate(flops=flops, bytes_accessed=4 << 20, transcendentals=0),
    )(*args)


def ring(count, step):
    return [(i, (i + step) % count) for i in range(count)]


def swap(count, bits):
    return [(i, i ^ bits) for i in range(count)]


def total(parts):
    return functools.reduce(jnp.add, [p.astype(F32) for p in parts])


def body(queries, keys, values, out_grad, w_out, block_mask):
    q, k, v, g = queries[0], keys[0], values[0], out_grad[0]
    tokens, feats = q.shape
    width = g.shape[1]
    blocks = tokens // BLK
    ctx, dp = lax.axis_size("ctx"), lax.axis_size("dp")
    chips = ctx // 2
    at_ctx, at_dp = lax.axis_index("ctx"), lax.axis_index("dp")
    core, chip = at_ctx % 2, at_ctx // 2

    low = lax.ppermute(jnp.stack([k[-RIM:], v[-RIM:]]), "ctx", ring(ctx, 1))
    high = lax.ppermute(jnp.stack([k[:RIM], v[:RIM]]), "ctx", ring(ctx, -1))
    mask = lax.dynamic_slice_in_dim(block_mask[0], at_ctx * blocks, blocks, 0)
    ag = dot(g, w_out, ((1,), (1,))).astype(BF16)

    ext = (tokens + 2 * RIM, feats)
    attn_t, part = call(
        forward_kernel,
        [((feats, tokens), BF16), ((feats, width), BF16)],
        [(ext, BF16)] * 2,
        10**9,
        mask, q, k, v, low, high, g,
    )

    rows, cols = feats // ctx, width // dp
    part = part.reshape(chips, 2, rows, width)
    mine = lax.dynamic_index_in_dim(part, core, 1, keepdims=False)
    other = lax.dynamic_index_in_dim(part, 1 - core, 1, keepdims=False)
    other = lax.ppermute(other, "ctx", swap(ctx, 1))
    half = total([mine, other]).astype(BF16)

    q_grad, k_own, v_own, to_low, to_high = call(
        backward_kernel,
        [((tokens, feats), BF16)]
        + [((tokens, feats), F32)] * 2
        + [((2, RIM, feats), BF16)] * 2,
        [(ext, BF16)] * 2 + [(ext, F32)] * 2,
        2 * 10**9,
        mask, q, k, v, low, high, ag,
    )
    from_high = lax.ppermute(to_low, "ctx", ring(ctx, -1))
    from_low = lax.ppermute(to_high, "ctx", ring(ctx, 1))

    def columns(step):
        return lax.dynamic_slice_in_dim(half, (at_dp ^ step) * cols, cols, 2)

    quarter = total(
        [columns(0)] + [lax.ppermute(columns(s), "dp", swap(dp, s)) for s in range(1, dp)]
    ).astype(BF16)

    def of_chip(step):
        return lax.dynamic_index_in_dim(quarter, chip ^ step, 0, keepdims=False)

    piece = total(
        [of_chip(0)]
        + [lax.ppermute(of_chip(s), "ctx", swap(ctx, 2 * s)) for s in range(1, chips)]
    )
    piece = (piece * (dp * tokens * ctx) ** (-0.5)).astype(BF16)
    pieces = jnp.stack(
        [piece] + [lax.ppermute(piece, "dp", swap(dp, s)) for s in range(1, dp)]
    )
    step = 1
    while step < dp:
        turned = pieces[jnp.arange(dp) ^ step]
        pieces = jnp.where((at_dp & step) != 0, turned, pieces)
        step *= 2
    weight_grad = jnp.concatenate([pieces[d] for d in range(dp)], axis=1).astype(F32)

    output = dot(attn_t, w_out, ((0,), (0,))).astype(BF16)
    grads = []
    for which, own in enumerate((k_own, v_own)):
        own = own.at[:RIM].add(from_low[which].astype(F32))
        own = own.at[tokens - RIM :].add(from_high[which].astype(F32))
        grads.append(own.astype(BF16))
    return (output[None], q_grad[None], grads[0][None], grads[1][None], weight_grad)


def solution(mesh):
    rows = P("dp", "ctx", None)
    return jax.shard_map(
        body,
        mesh=mesh,
        in_specs=(rows, rows, rows, rows, P(), P("dp", None, None)),
        out_specs=(rows, rows, rows, rows, P("ctx", None)),
        check_vma=False,
    )
```

time: 130 us -> 58.9 us (0.45)
  waiting for transfers between devices: 56.9 us -> 20.1 us
  local copies, waits for them, and re-layouts: 26.5 us -> 3.34 us
  matrix products: 19.7 us -> 1.74 us
  starting transfers between devices: 5.52 us -> 19.8 us
  between operations: 14.9 us -> 0.94 us
  Pallas kernels: 0 us -> 9.96 us
  other arithmetic: 6.24 us -> 2.9 us
    psum x1 -> x0, waiting for transfers between devices: 34.6 us -> none  [body(): weight_total = lax.psum(weight_share, 'dp')]
    dot_general x27 -> x2, matrix products: 19.7 us -> 1.74 us  [dot(): lax.dot_general(a, b, (contract, ((), ())), preferred_element_type=F32)]
    ppermute x4 -> x14, starting transfers between devices: 5.44 us -> 19.8 us  [the longest x1 4.54 us: body(): high = lax.ppermute(jnp.stack([k[:RIM], v[:RIM]]), 'ctx', ring(ctx, -1))]
    reshape x24 -> x0, local copies, waits for them, and re-layouts: 14.2 us -> none  [the longest x4 5.76 us: body(): key_window_part.reshape(blocks_here, span_rows, group_width)]
    pallas_call x0 -> x2, Pallas kernels: none -> 9.96 us  [call(): pl.pallas_call(kernel, out_shape=[jax.ShapeDtypeStruct(s, d) for s, d in...]
    unnamed x83 -> x12, local copies, waits for them, and re-layouts: 4.65 us -> 0.71 us
    slice x15 -> x1, local copies, waits for them, and re-layouts: 4.54 us -> 1.22 us  [body(): high = lax.ppermute(jnp.stack([k[:RIM], v[:RIM]]), 'ctx', ring(ctx, -1))]
    ppermute x4 -> x14, waiting for transfers between devices: 22.3 us -> 20.1 us  [the longest x1 5.53 us: body(): from_low = lax.ppermute(to_high, 'ctx', ring(ctx, 1))]
  transfers between devices with their start and end apart: 6 -> 14, of which waited for: 5 -> 10; matrix products, arithmetic and copies ran while one was open for 23% -> 7% of each run, Pallas kernels for 0% -> 9%
where the time goes in v1:
time: 58.9 us; the launch traced here: 58.7 us
  waiting for transfers between devices  20.1 us (34%)
  starting transfers between devices  19.8 us (34%)
  Pallas kernels  9.96 us (17%)
  local copies, waits for them, and re-layouts  3.34 us (6%)
  other arithmetic  2.9 us (5%)
  matrix products  1.74 us (3%)
  between operations  0.94 us (2%)
    pallas_call x2, Pallas kernels, call(): pl.pallas_call(kernel, out_shape=[jax.ShapeDtypeStruct(s, d) for s, d in...  9.96 us
    ppermute x1, waiting for transfers between devices, body(): from_low = lax.ppermute(to_high, 'ctx', ring(ctx, 1))  5.53 us
    ppermute x3, waiting for transfers between devices, body(): lax.ppermute(columns(s), 'dp', swap(dp, s))  5.28 us
    ppermute x1, starting transfers between devices, body(): high = lax.ppermute(jnp.stack([k[:RIM], v[:RIM]]), 'ctx', ring(ctx, -1))  4.54 us
    ppermute x3, starting transfers between devices, body(): lax.ppermute(of_chip(s), 'ctx', swap(ctx, 2 * s))  4.44 us
    ppermute x3, starting transfers between devices, body(): lax.ppermute(columns(s), 'dp', swap(dp, s))  3.55 us
    ppermute x3, starting transfers between devices, body(): lax.ppermute(piece, 'dp', swap(dp, s))  3.55 us
    ppermute x1, waiting for transfers between devices, body(): high = lax.ppermute(jnp.stack([k[:RIM], v[:RIM]]), 'ctx', ring(ctx, -1))  3.24 us
  transfers between devices with their start and end apart: 14, of which 10 were waited for; matrix products, arithmetic and copies ran while one was open for 7% of the time, Pallas kernels for 9%

profile of v1, /device:TPU:0, one launch (start us, length us, event | category | flops | bytes accessed | tf_op | source)
XLA Modules:
  0.0 58.7 jit_solution(6105981991097675988)
XLA Ops:
  0.6 0.0 copy-start
  0.6 1.2 %fusion.13 = (bf16[1,128,512]{2,1,0:T(8,128)(2,1)S(1)}, bf16[1,128,512]{2,1,0:T(8,128)(2,1)S(1)}, bf16[1,128,512]{2,1,0:T(8,128)(2,1)S(1)}, bf16[1,128,512]{2,1,0:T(8,128)(2,1)S(1)}) fusion(bf16[1,256,512]{2,1,0:T(8,128)(2,1)} %param.15, bf16[1,256,512]{2,1,0:T(8,128)(2,1)} %param.16), kind=kLoop, calls=%fused_computation.52 | loop fusion | bytes 1048576 | tf_op jit(solution)/shard_map/slice | solution.py:152
  1.9 0.0 copy-start.1
  1.9 4.5 %collective-permute-start.1 = (bf16[2,128,512]{2,1,0:T(8,128)(2,1)S(1)}, bf16[2,128,512]{2,1,0:T(8,128)(2,1)S(1)}, u32[]{:S(2)}, u32[]{:S(2)}) collective-permute-start(bf16[2,128,512]{2,1,0:T(8,128)(2,1)S(1)} %pad_maximum_fusion.1), channel_id=1, source_target_pairs={{0,7},{1,0},{2,1},{3,2},{4,3},{5,4},{6,5},{7,6},{8,15},{9,8},{10,9... | collective-permute-start | bytes 786440 | tf_op jit(solution)/shard_map/ppermute | solution.py:152
  6.5 0.1 collective-permute-start
  6.6 0.0 copy-start.5
  6.6 0.7 %copy-done.5 = s32[1,16,3]{1,0,2:T(1,128)S(1)} copy-done((s32[1,16,3]{1,0,2:T(1,128)S(1)}, s32[1,16,3]{1,0,2:T(1,128)}, u32[]{:S(2)}) %copy-start.5) | copy-done | bytes 216
  7.3 0.1 constant_dynamic-slice_fusion.3
  7.4 0.1 copy.11
  7.5 0.0 copy-start.2
  7.5 0.0 copy-start.3
  7.5 0.0 copy-start.4
  7.5 0.5 convolution_convert_fusion.1.ag
  8.0 3.2 %collective-permute-done.1.high = bf16[2,128,512]{2,1,0:T(8,128)(2,1)S(1)} collective-permute-done((bf16[2,128,512]{2,1,0:T(8,128)(2,1)S(1)}, bf16[2,128,512]{2,1,0:T(8,128)(2,1)S(1)}, u32[]{:S(2)}, u32[]{:S(2)}) %collective-permute-start.1) | collective-permute-done | bytes 262176 | tf_op jit(solution)/shard_map/ppermute | solution.py:152
  11.3 2.9 %collective-permute-done.low = bf16[2,128,512]{2,1,0:T(8,128)(2,1)S(1)} collective-permute-done((bf16[2,128,512]{2,1,0:T(8,128)(2,1)S(1)}, bf16[2,128,512]{2,1,0:T(8,128)(2,1)S(1)}, u32[]{:S(2)}, u32[]{:S(2)}) %collective-permute-start) | collective-permute-done | bytes 262176 | tf_op jit(solution)/shard_map/ppermute | solution.py:151
  14.2 4.4 %shard_map.101 = (bf16[512,256]{1,0:T(8,128)(2,1)S(1)}, bf16[512,1024]{1,0:T(8,128)(2,1)S(1)}) custom-call(s32[2,3]{1,0:T(2,128)S(1)} %bitcast.77, bf16[256,512]{1,0:T(8,128)(2,1)S(1)} %bitcast.79, bf16[256,512]{1,0:T(8,128)(2,1)S(1)} %bitcast.73, bf16[256,512]{1,0:T(8,128)(2,1)S(1)} %bitcast.75, bf16[2,128,512]{2,1,0:T(8,128)(2,1)S(1)} %collective-permute-done.low, ...), custom_call_target="tpu_custom_call" | custom-call | flops 1000000000 | bytes 4194304 | tf_op jit(solution)/shard_map/pallas_call | solution.py:118
  18.7 0.1 collective-permute-start.4
  18.7 5.5 %shard_map.102 = (bf16[256,512]{1,0:T(8,128)(2,1)}, f32[256,512]{1,0:T(8,128)S(1)}, f32[256,512]{1,0:T(8,128)S(1)}, bf16[2,128,512]{2,1,0:T(8,128)(2,1)S(1)}, bf16[2,128,512]{2,1,0:T(8,128)(2,1)S(1)}) custom-call(s32[2,3]{1,0:T(2,128)S(1)} %bitcast.78, bf16[256,512]{1,0:T(8,128)(2,1)S(1)} %bitcast.80, bf16[256,512]{1,0:T(8,128)(2,1)S(1)} %bitcast.74, ...), custom_call_target="tpu_custom_call" | custom-call | flops 2000000000 | bytes 4194304 | tf_op jit(solution)/shard_map/pallas_call | solution.py:118
  24.3 0.5 collective-permute-start.2
  24.8 3.1 %collective-permute-start.3 = (bf16[2,128,512]{2,1,0:T(8,128)(2,1)S(1)}, bf16[2,128,512]{2,1,0:T(8,128)(2,1)S(1)}, u32[]{:S(2)}, u32[]{:S(2)}) collective-permute-start(bf16[2,128,512]{2,1,0:T(8,128)(2,1)S(1)} %get-tuple-element.64), channel_id=1, source_target_pairs={{0,7},{1,0},{2,1},{3,2},{4,3},{5,4},{6,5},{7,6},{8,15},{9,8},{10,9... | collective-permute-start | bytes 786440 | tf_op jit(solution)/shard_map/ppermute | solution.py:181
  27.8 1.3 %fusion = bf16[1,256,1024]{2,1,0:T(8,128)(2,1)} fusion(bf16[512,256]{1,0:T(8,128)(2,1)S(1)} %get-tuple-element.60, bf16[512,1024]{1,0:T(8,128)(2,1)S(1)} %copy-done), kind=kOutput, calls=%fused_computation.3 | convolution fusion | flops 268697600 | bytes 1835008 | tf_op jit(solution)/shard_map/dot_general | solution.py:24
  29.1 5.5 %collective-permute-done.2 = bf16[2,128,512]{2,1,0:T(8,128)(2,1)S(1)} collective-permute-done((bf16[2,128,512]{2,1,0:T(8,128)(2,1)S(1)}, bf16[2,128,512]{2,1,0:T(8,128)(2,1)S(1)}, u32[]{:S(2)}, u32[]{:S(2)}) %collective-permute-start.2) | collective-permute-done | bytes 262176 | tf_op jit(solution)/shard_map/ppermute | solution.py:182
  34.6 0.1 fusion.4
  34.8 0.2 fusion.1
  35.0 0.1 constant_dynamic-slice_fusion.2
  35.1 1.6 %collective-permute-start.5 = (bf16[4,64,256]{2,1,0:T(8,128)(2,1)S(1)}, bf16[4,64,256]{2,1,0:T(8,128)(2,1)S(1)}, u32[]{:S(2)}, u32[]{:S(2)}) collective-permute-start(bf16[4,64,256]{2,1,0:T(8,128)(2,1)S(1)} %get-tuple-element.67), channel_id=1, source_target_pairs={{0,8},{8,0},{16,24},{24,16},{1,9},{9,1},{17,25},{25,17},{2,10},{10... | collective-permute-start | bytes 393224 | tf_op jit(solution)/shard_map/ppermute | solution.py:188
  36.6 1.5 %collective-permute-start.6 = (bf16[4,64,256]{2,1,0:T(8,128)(2,1)S(1)}, bf16[4,64,256]{2,1,0:T(8,128)(2,1)S(1)}, u32[]{:S(2)}, u32[]{:S(2)}) collective-permute-start(bf16[4,64,256]{2,1,0:T(8,128)(2,1)S(1)} %get-tuple-element.69), channel_id=1, source_target_pairs={{0,16},{8,24},{16,0},{24,8},{1,17},{9,25},{17,1},{25,9},{2,18},{10... | collective-permute-start | bytes 393224 | tf_op jit(solution)/shard_map/ppermute | solution.py:188
  38.2 0.5 collective-permute-start.7
  38.6 0.1 fusion.2
  38.7 1.3 %collective-permute-done.5 = bf16[4,64,256]{2,1,0:T(8,128)(2,1)S(1)} collective-permute-done((bf16[4,64,256]{2,1,0:T(8,128)(2,1)S(1)}, bf16[4,64,256]{2,1,0:T(8,128)(2,1)S(1)}, u32[]{:S(2)}, u32[]{:S(2)}) %collective-permute-start.5) | collective-permute-done | bytes 131104 | tf_op jit(solution)/shard_map/ppermute | solution.py:188
  40.1 1.5 %collective-permute-done.6 = bf16[4,64,256]{2,1,0:T(8,128)(2,1)S(1)} collective-permute-done((bf16[4,64,256]{2,1,0:T(8,128)(2,1)S(1)}, bf16[4,64,256]{2,1,0:T(8,128)(2,1)S(1)}, u32[]{:S(2)}, u32[]{:S(2)}) %collective-permute-start.6) | collective-permute-done | bytes 131104 | tf_op jit(solution)/shard_map/ppermute | solution.py:188
  41.6 2.4 %collective-permute-done.7 = bf16[4,64,256]{2,1,0:T(8,128)(2,1)S(1)} collective-permute-done((bf16[4,64,256]{2,1,0:T(8,128)(2,1)S(1)}, bf16[4,64,256]{2,1,0:T(8,128)(2,1)S(1)}, u32[]{:S(2)}, u32[]{:S(2)}) %collective-permute-start.7) | collective-permute-done | bytes 131104 | tf_op jit(solution)/shard_map/ppermute | solution.py:188
  44.0 0.1 add_convert_fusion
  44.1 0.1 collective-permute-start.10
  44.2 0.1 collective-permute-start.8
  44.3 4.3 %collective-permute-start.9 = (bf16[64,256]{1,0:T(8,128)(2,1)S(1)}, bf16[64,256]{1,0:T(8,128)(2,1)S(1)}, u32[]{:S(2)}, u32[]{:S(2)}) collective-permute-start(bf16[64,256]{1,0:T(8,128)(2,1)S(1)} %get-tuple-element.84), channel_id=1, source_target_pairs={{0,4},{1,5},{2,6},{3,7},{4,0},{5,1},{6,2},{7,3},{8,12},{9,13},{10,... | collective-permute-start | bytes 98312 | tf_op jit(solution)/shard_map/ppermute | solution.py:196
  48.6 0.7 %convert_bitcast_fusion = bf16[1,256,512]{2,1,0:T(8,128)(2,1)} fusion(f32[256,512]{1,0:T(8,128)S(1)} %get-tuple-element.70), kind=kLoop, calls=%fused_computation.19 | loop fusion | flops 131072 | bytes 786432 | tf_op jit(solution)/shard_map/broadcast_in_dim | solution.py:215
  49.3 0.6 %collective-permute-done.10 = bf16[64,256]{1,0:T(8,128)(2,1)S(1)} collective-permute-done((bf16[64,256]{1,0:T(8,128)(2,1)S(1)}, bf16[64,256]{1,0:T(8,128)(2,1)S(1)}, u32[]{:S(2)}, u32[]{:S(2)}) %collective-permute-start.10) | collective-permute-done | bytes 32800 | tf_op jit(solution)/shard_map/ppermute | solution.py:196
  49.9 0.9 %collective-permute-done.9 = bf16[64,256]{1,0:T(8,128)(2,1)S(1)} collective-permute-done((bf16[64,256]{1,0:T(8,128)(2,1)S(1)}, bf16[64,256]{1,0:T(8,128)(2,1)S(1)}, u32[]{:S(2)}, u32[]{:S(2)}) %collective-permute-start.9) | collective-permute-done | bytes 32800 | tf_op jit(solution)/shard_map/ppermute | solution.py:196
  50.9 0.6 collective-permute-start.11
  51.4 0.5 collective-permute-start.12
  51.9 2.5 %collective-permute-start.13 = (bf16[64,256]{1,0:T(8,128)(2,1)S(1)}, bf16[64,256]{1,0:T(8,128)(2,1)S(1)}, u32[]{:S(2)}, u32[]{:S(2)}) collective-permute-start(bf16[64,256]{1,0:T(8,128)(2,1)S(1)} %fusion.9), channel_id=1, source_target_pairs={{0,24},{8,16},{16,8},{24,0},{1,25},{9,17},{17,9},{25,1},{2,26},{10... | collective-permute-start | bytes 98312 | tf_op jit(solution)/shard_map/ppermute | solution.py:200
  54.4 0.7 %convert_bitcast_fusion.1 = bf16[1,256,512]{2,1,0:T(8,128)(2,1)} fusion(f32[256,512]{1,0:T(8,128)S(1)} %get-tuple-element.71), kind=kLoop, calls=%fused_computation.20 | loop fusion | flops 131072 | bytes 786432 | tf_op jit(solution)/shard_map/broadcast_in_dim | solution.py:215
  55.1 0.2 collective-permute-done.12
  55.3 1.4 %collective-permute-done.13 = bf16[64,256]{1,0:T(8,128)(2,1)S(1)} collective-permute-done((bf16[64,256]{1,0:T(8,128)(2,1)S(1)}, bf16[64,256]{1,0:T(8,128)(2,1)S(1)}, u32[]{:S(2)}, u32[]{:S(2)}) %collective-permute-start.13) | collective-permute-done | bytes 32800 | tf_op jit(solution)/shard_map/ppermute | solution.py:200
  56.8 0.6 gather_fusion
  57.4 0.6 gather_fusion.1
  58.0 0.7 %maximum_convert_fusion = f32[64,1024]{1,0:T(8,128)} fusion(bf16[64,256]{1,0:T(8,128)(2,1)S(1)} %get-tuple-element.79, bf16[64,256]{1,0:T(8,128)(2,1)S(1)} %get-tuple-element.80, bf16[64,256]{1,0:T(8,128)(2,1)S(1)} %get-tuple-element.81, bf16[64,256]{1,0:T(8,128)(2,1)S(1)} %get-tuple-element.78), kind=kLoop, calls=%fused_computation.26 | loop fusion | flops 524288 | bytes 393216 | tf_op jit(solution)/shard_map/convert_element_type | solution.py:207
  (21 shorter events, 0.3 us)
Async XLA Ops:
  0.6 6.9 %copy-start = (bf16[512,1024]{1,0:T(8,128)(2,1)S(1)}, bf16[512,1024]{1,0:T(8,128)(2,1)}, u32[]{:S(2)}) copy-start(bf16[512,1024]{1,0:T(8,128)(2,1)} %param.18) | copy-start | bytes 3145732
  1.9 5.6 %copy-start.1 = (bf16[1,256,1024]{2,1,0:T(8,128)(2,1)S(1)}, bf16[1,256,1024]{2,1,0:T(8,128)(2,1)}, u32[]{:S(2)}) copy-start(bf16[1,256,1024]{2,1,0:T(8,128)(2,1)} %param.17) | copy-start | bytes 1572868
  1.9 9.4 %collective-permute-start.1 = (bf16[2,128,512]{2,1,0:T(8,128)(2,1)S(1)}, bf16[2,128,512]{2,1,0:T(8,128)(2,1)S(1)}, u32[]{:S(2)}, u32[]{:S(2)}) collective-permute-start(bf16[2,128,512]{2,1,0:T(8,128)(2,1)S(1)} %pad_maximum_fusion.1), channel_id=1, source_target_pairs={{0,7},{1,0},{2,1},{3,2},{4,3},{5,4},{6,5},{7,6},{8,15},{9,8},{10,9... | collective-permute-start | bytes 786440 | tf_op jit(solution)/shard_map/ppermute | solution.py:152
  6.5 7.7 %collective-permute-start = (bf16[2,128,512]{2,1,0:T(8,128)(2,1)S(1)}, bf16[2,128,512]{2,1,0:T(8,128)(2,1)S(1)}, u32[]{:S(2)}, u32[]{:S(2)}) collective-permute-start(bf16[2,128,512]{2,1,0:T(8,128)(2,1)S(1)} %pad_maximum_fusion), channel_id=1, source_target_pairs={{0,1},{1,2},{2,3},{3,4},{4,5},{5,6},{6,7},{7,0},{8,9},{9,10},{10,1... | collective-permute-start | bytes 786440 | tf_op jit(solution)/shard_map/ppermute | solution.py:151
  6.6 0.7 %copy-start.5 = (s32[1,16,3]{1,0,2:T(1,128)S(1)}, s32[1,16,3]{1,0,2:T(1,128)}, u32[]{:S(2)}) copy-start(s32[1,16,3]{1,0,2:T(1,128)} %param.19) | copy-start | bytes 580
  7.5 6.7 %copy-start.2 = (bf16[1,256,512]{2,1,0:T(8,128)(2,1)S(1)}, bf16[1,256,512]{2,1,0:T(8,128)(2,1)}, u32[]{:S(2)}) copy-start(bf16[1,256,512]{2,1,0:T(8,128)(2,1)} %param.15) | copy-start | bytes 786436
  7.5 6.7 %copy-start.3 = (bf16[1,256,512]{2,1,0:T(8,128)(2,1)S(1)}, bf16[1,256,512]{2,1,0:T(8,128)(2,1)}, u32[]{:S(2)}) copy-start(bf16[1,256,512]{2,1,0:T(8,128)(2,1)} %param.16) | copy-start | bytes 786436
  7.5 6.7 %copy-start.4 = (bf16[1,256,512]{2,1,0:T(8,128)(2,1)S(1)}, bf16[1,256,512]{2,1,0:T(8,128)(2,1)}, u32[]{:S(2)}) copy-start(bf16[1,256,512]{2,1,0:T(8,128)(2,1)} %param.14) | copy-start | bytes 786436
  18.7 16.1 %collective-permute-start.4 = (bf16[4,64,1024]{2,1,0:T(8,128)(2,1)S(1)}, bf16[4,64,1024]{2,1,0:T(8,128)(2,1)S(1)}, u32[]{:S(2)}, u32[]{:S(2)}) collective-permute-start(bf16[4,64,1024]{2,1,0:T(8,128)(2,1)S(1)} %dynamic-slice_bitcast_fusion), channel_id=1, source_target_pairs={{0,1},{1,0},{2,3},{3,2},{4,5},{5,4},{6,7},{7,6},{8,9},{9,8},{10,11... | collective-permute-start | bytes 1572872 | tf_op jit(solution)/shard_map/ppermute | solution.py:169
  24.3 10.3 %collective-permute-start.2 = (bf16[2,128,512]{2,1,0:T(8,128)(2,1)S(1)}, bf16[2,128,512]{2,1,0:T(8,128)(2,1)S(1)}, u32[]{:S(2)}, u32[]{:S(2)}) collective-permute-start(bf16[2,128,512]{2,1,0:T(8,128)(2,1)S(1)} %get-tuple-element.63), channel_id=1, source_target_pairs={{0,1},{1,2},{2,3},{3,4},{4,5},{5,6},{6,7},{7,0},{8,9},{9,10},{10,1... | collective-permute-start | bytes 786440 | tf_op jit(solution)/shard_map/ppermute | solution.py:182
  24.8 13.8 %collective-permute-start.3 = (bf16[2,128,512]{2,1,0:T(8,128)(2,1)S(1)}, bf16[2,128,512]{2,1,0:T(8,128)(2,1)S(1)}, u32[]{:S(2)}, u32[]{:S(2)}) collective-permute-start(bf16[2,128,512]{2,1,0:T(8,128)(2,1)S(1)} %get-tuple-element.64), channel_id=1, source_target_pairs={{0,7},{1,0},{2,1},{3,2},{4,3},{5,4},{6,5},{7,6},{8,15},{9,8},{10,9... | collective-permute-start | bytes 786440 | tf_op jit(solution)/shard_map/ppermute | solution.py:181
  35.1 5.0 %collective-permute-start.5 = (bf16[4,64,256]{2,1,0:T(8,128)(2,1)S(1)}, bf16[4,64,256]{2,1,0:T(8,128)(2,1)S(1)}, u32[]{:S(2)}, u32[]{:S(2)}) collective-permute-start(bf16[4,64,256]{2,1,0:T(8,128)(2,1)S(1)} %get-tuple-element.67), channel_id=1, source_target_pairs={{0,8},{8,0},{16,24},{24,16},{1,9},{9,1},{17,25},{25,17},{2,10},{10... | collective-permute-start | bytes 393224 | tf_op jit(solution)/shard_map/ppermute | solution.py:188
  36.6 5.0 %collective-permute-start.6 = (bf16[4,64,256]{2,1,0:T(8,128)(2,1)S(1)}, bf16[4,64,256]{2,1,0:T(8,128)(2,1)S(1)}, u32[]{:S(2)}, u32[]{:S(2)}) collective-permute-start(bf16[4,64,256]{2,1,0:T(8,128)(2,1)S(1)} %get-tuple-element.69), channel_id=1, source_target_pairs={{0,16},{8,24},{16,0},{24,8},{1,17},{9,25},{17,1},{25,9},{2,18},{10... | collective-permute-start | bytes 393224 | tf_op jit(solution)/shard_map/ppermute | solution.py:188
  38.2 5.9 %collective-permute-start.7 = (bf16[4,64,256]{2,1,0:T(8,128)(2,1)S(1)}, bf16[4,64,256]{2,1,0:T(8,128)(2,1)S(1)}, u32[]{:S(2)}, u32[]{:S(2)}) collective-permute-start(bf16[4,64,256]{2,1,0:T(8,128)(2,1)S(1)} %get-tuple-element.68), channel_id=1, source_target_pairs={{0,24},{8,16},{16,8},{24,0},{1,25},{9,17},{17,9},{25,1},{2,26},{10... | collective-permute-start | bytes 393224 | tf_op jit(solution)/shard_map/ppermute | solution.py:188
  44.1 5.8 %collective-permute-start.10 = (bf16[64,256]{1,0:T(8,128)(2,1)S(1)}, bf16[64,256]{1,0:T(8,128)(2,1)S(1)}, u32[]{:S(2)}, u32[]{:S(2)}) collective-permute-start(bf16[64,256]{1,0:T(8,128)(2,1)S(1)} %get-tuple-element.83), channel_id=1, source_target_pairs={{0,6},{1,7},{2,4},{3,5},{4,2},{5,3},{6,0},{7,1},{8,14},{9,15},{10,... | collective-permute-start | bytes 98312 | tf_op jit(solution)/shard_map/ppermute | solution.py:196
  44.2 5.7 %collective-permute-start.8 = (bf16[64,256]{1,0:T(8,128)(2,1)S(1)}, bf16[64,256]{1,0:T(8,128)(2,1)S(1)}, u32[]{:S(2)}, u32[]{:S(2)}) collective-permute-start(bf16[64,256]{1,0:T(8,128)(2,1)S(1)} %get-tuple-element.82), channel_id=1, source_target_pairs={{0,2},{1,3},{2,0},{3,1},{4,6},{5,7},{6,4},{7,5},{8,10},{9,11},{10,... | collective-permute-start | bytes 98312 | tf_op jit(solution)/shard_map/ppermute | solution.py:196
  44.3 6.5 %collective-permute-start.9 = (bf16[64,256]{1,0:T(8,128)(2,1)S(1)}, bf16[64,256]{1,0:T(8,128)(2,1)S(1)}, u32[]{:S(2)}, u32[]{:S(2)}) collective-permute-start(bf16[64,256]{1,0:T(8,128)(2,1)S(1)} %get-tuple-element.84), channel_id=1, source_target_pairs={{0,4},{1,5},{2,6},{3,7},{4,0},{5,1},{6,2},{7,3},{8,12},{9,13},{10,... | collective-permute-start | bytes 98312 | tf_op jit(solution)/shard_map/ppermute | solution.py:196
  50.9 4.3 %collective-permute-start.11 = (bf16[64,256]{1,0:T(8,128)(2,1)S(1)}, bf16[64,256]{1,0:T(8,128)(2,1)S(1)}, u32[]{:S(2)}, u32[]{:S(2)}) collective-permute-start(bf16[64,256]{1,0:T(8,128)(2,1)S(1)} %fusion.9), channel_id=1, source_target_pairs={{0,8},{8,0},{16,24},{24,16},{1,9},{9,1},{17,25},{25,17},{2,10},{10... | collective-permute-start | bytes 98312 | tf_op jit(solution)/shard_map/ppermute | solution.py:200
  51.4 3.9 %collective-permute-start.12 = (bf16[64,256]{1,0:T(8,128)(2,1)S(1)}, bf16[64,256]{1,0:T(8,128)(2,1)S(1)}, u32[]{:S(2)}, u32[]{:S(2)}) collective-permute-start(bf16[64,256]{1,0:T(8,128)(2,1)S(1)} %fusion.9), channel_id=1, source_target_pairs={{0,16},{8,24},{16,0},{24,8},{1,17},{9,25},{17,1},{25,9},{2,18},{10... | collective-permute-start | bytes 98312 | tf_op jit(solution)/shard_map/ppermute | solution.py:200
  51.9 4.8 %collective-permute-start.13 = (bf16[64,256]{1,0:T(8,128)(2,1)S(1)}, bf16[64,256]{1,0:T(8,128)(2,1)S(1)}, u32[]{:S(2)}, u32[]{:S(2)}) collective-permute-start(bf16[64,256]{1,0:T(8,128)(2,1)S(1)} %fusion.9), channel_id=1, source_target_pairs={{0,24},{8,16},{16,8},{24,0},{1,25},{9,17},{17,9},{25,1},{2,26},{10... | collective-permute-start | bytes 98312 | tf_op jit(solution)/shard_map/ppermute | solution.py:200

commit v2 on v1

--- a/solution.py
+++ b/solution.py
@@ -45,35 +45,91 @@
 
 def probabilities(mask, b, q2, k_win):
     scores = dot(k_win, q2, ((1,), (1,)))
-    parts = []
-    for c in range(2 * RAD + 1):
-        part = scores[c * BLK : (c + 1) * BLK]
-        if c != RAD:
-            part = jnp.where(mask[b, c] == 1, part, BIG_NEGATIVE)
-        parts.append(part)
-    scores = jnp.concatenate(parts, axis=0)
+    scores = jnp.concatenate(
+        [masked(mask, b, c, scores[c * BLK : (c + 1) * BLK]) for c in range(2 * RAD + 1)], axis=0
+    )
     top = jnp.max(scores, axis=0, keepdims=True)
     e = jnp.exp(scores - top)
     return e * (1.0 / jnp.sum(e, axis=0, keepdims=True))
 
 
-def forward_kernel(mask, q, k, v, low, high, g, attn_t, part, k_ext, v_ext):
-    extend(k_ext, k, low, high, 0)
-    extend(v_ext, v, low, high, 1)
-    for b in range(q.shape[0] // BLK):
+def own_candidates(b, blocks):
+    return max(0, RAD - b), min(2 * RAD, blocks - 1 - b + RAD)
+
+
+def masked(mask, b, c, part):
+    return part if c == RAD else jnp.where(mask[b, c] == 1, part, BIG_NEGATIVE)
+
+
+def own_kernel(mask, q, k, v, own_t, stats):
+    blocks = q.shape[0] // BLK
+    pairs = HEADS // 2
+    for b in range(blocks):
         rows = slice(b * BLK, (b + 1) * BLK)
-        window = slice(b * BLK, b * BLK + SPAN)
-        for p in range(HEADS // 2):
+        first, last = own_candidates(b, blocks)
+        here = slice((b + first - RAD) * BLK, (b + last - RAD + 1) * BLK)
+        for p in range(pairs):
             cols = slice(p * PAIR, (p + 1) * PAIR)
+            scores = dot(k[here, cols], two_heads(q[rows, cols] * SCALE), ((1,), (1,)))
+            scores = jnp.concatenate(
+                [
+                    masked(mask, b, c, scores[(c - first) * BLK : (c - first + 1) * BLK])
+                    for c in range(first, last + 1)
+                ],
+                axis=0,
+            )
+            top = jnp.max(scores, axis=0, keepdims=True)
+            e = jnp.exp(scores - top)
+            stats[0, b * pairs + p : b * pairs + p + 1] = top
+            stats[1, b * pairs + p : b * pairs + p + 1] = jnp.sum(e, axis=0, keepdims=True)
+            own_t[cols, rows] = own_features(dot(v[here, cols], e.astype(BF16), ((0,), (0,))))
+
+
+def spread(row):
+    return jnp.concatenate(
+        [
+            jnp.broadcast_to(row[:, :BLK], (HD, BLK)),
+            jnp.broadcast_to(row[:, BLK:], (HD, BLK)),
+        ],
+        axis=0,
+    )
+
+
+def forward_kernel(mask, q, low, high, own_t, stats, g, attn_t, part):
+    blocks = q.shape[0] // BLK
+    pairs = HEADS // 2
+    for b in range(blocks):
+        rows = slice(b * BLK, (b + 1) * BLK)
+        first, last = own_candidates(b, blocks)
+        rims = [(low, c) for c in range(first)] + [(high, c) for c in range(last + 1, 3)]
+        for p in range(pairs):
+            cols = slice(p * PAIR, (p + 1) * PAIR)
+            old = stats[0, b * pairs + p : b * pairs + p + 1]
             q2 = two_heads(q[rows, cols] * SCALE)
-            probs = probabilities(mask, b, q2, k_ext[window, cols]).astype(BF16)
-            both = dot(v_ext[window, cols], probs, ((0,), (0,)))
-            attn_t[cols, rows] = own_features(both).astype(BF16)
+            scores = [
+                masked(mask, b, c, dot(rim[0, :, cols], q2, ((1,), (1,)))) for rim, c in rims
+            ]
+            top = old
+            for part_scores in scores:
+                top = jnp.maximum(top, jnp.max(part_scores, axis=0, keepdims=True))
+            kept = jnp.exp(old - top)
+            count = stats[1, b * pairs + p : b * pairs + p + 1] * kept
+            both = None
+            for (rim, _), part_scores in zip(rims, scores):
+                e = jnp.exp(part_scores - top)
+                count = count + jnp.sum(e, axis=0, keepdims=True)
+                more = dot(rim[1, :, cols], e.astype(BF16), ((0,), (0,)))
+                both = more if both is None else both + more
+            share = 1.0 / count
+            attn = own_t[cols, rows] * spread(kept * share)
+            if both is not None:
+                attn = attn + own_features(both) * spread(share)
+            attn_t[cols, rows] = attn.astype(BF16)
     part[...] = dot(attn_t[...], g[...], ((1,), (0,))).astype(BF16)
 
 
 def backward_kernel(
-    mask, q, k, v, low, high, ag, q_grad, k_own, v_own, to_low, to_high, k_ext, v_ext, dk, dv
+    mask, q, k, v, low, high, ag, after, q_grad, k_own, v_own, to_low, to_high, k_ext, v_ext, dk, dv
 ):
     extend(k_ext, k, low, high, 0)
     extend(v_ext, v, low, high, 1)
@@ -113,25 +169,55 @@
     to_high[1] = dv[RIM + tokens :].astype(BF16)
 
 
-def call(kernel, outs, scratch, flops, *args):
+def rims_kernel(at, k_own, v_own, from_link, from_chip, after, k_grad, v_grad):
+    tokens = k_own.shape[0]
+    core = at[0]
+    for which, (own, grad) in enumerate(((k_own, k_grad), (v_own, v_grad))):
+        link = from_link[which].astype(F32)
+        chip = from_chip[which].astype(F32)
+        low = jnp.where(core == 0, link, chip)
+        high = jnp.where(core == 0, chip, link)
+        if tokens == RIM:
+            grad[...] = (own[...] + low + high).astype(BF16)
+        else:
+            grad[:RIM] = (own[:RIM] + low).astype(BF16)
+            if tokens > 2 * RIM:
+                grad[RIM : tokens - RIM] = own[RIM : tokens - RIM].astype(BF16)
+            grad[tokens - RIM :] = (own[tokens - RIM :] + high).astype(BF16)
+
+
+def columns_kernel(at, *refs):
+    pieces, out = refs[:-1], refs[-1]
+    cols = pieces[0].shape[1]
+    for d in range(len(pieces)):
+        value = pieces[0][...]
+        for s in range(1, len(pieces)):
+            value = jnp.where((at[1] ^ s) == d, pieces[s][...], value)
+        out[:, d * cols : (d + 1) * cols] = value.astype(F32)
+
+
+def call(kernel, outs, scratch, flops, *args, after=()):
     in_vmem = pl.BlockSpec(memory_space=pltpu.VMEM)
+    anywhere = pl.BlockSpec(memory_space=pl.ANY)
     return pl.pallas_call(
         kernel,
         out_shape=[jax.ShapeDtypeStruct(s, d) for s, d in outs],
-        in_specs=[pl.BlockSpec(memory_space=pltpu.SMEM)] + [in_vmem] * (len(args) - 1),
+        in_specs=[pl.BlockSpec(memory_space=pltpu.SMEM)]
+        + [in_vmem] * (len(args) - 1)
+        + [anywhere] * len(after),
         out_specs=[in_vmem] * len(outs),
         scratch_shapes=[pltpu.VMEM(s, d) for s, d in scratch],
         compiler_params=pltpu.CompilerParams(vmem_limit_bytes=32 * 1024 * 1024),
         cost_estimate=pl.CostEstimate(flops=flops, bytes_accessed=4 << 20, transcendentals=0),
-    )(*args)
-
-
-def ring(count, step):
-    return [(i, (i + step) % count) for i in range(count)]
+    )(*args, *after)
 
 
 def swap(count, bits):
     return [(i, i ^ bits) for i in range(count)]
+
+
+def over_links(count):
+    return [(i, (i - 1 if i % 2 == 0 else i + 1) % count) for i in range(count)]
 
 
 def total(parts):
@@ -147,19 +233,34 @@
     chips = ctx // 2
     at_ctx, at_dp = lax.axis_index("ctx"), lax.axis_index("dp")
     core, chip = at_ctx % 2, at_ctx // 2
-
-    low = lax.ppermute(jnp.stack([k[-RIM:], v[-RIM:]]), "ctx", ring(ctx, 1))
-    high = lax.ppermute(jnp.stack([k[:RIM], v[:RIM]]), "ctx", ring(ctx, -1))
+    at = jnp.stack([core, at_dp])
+
+    link_row = core * (tokens - RIM)
+    chip_row = tokens - RIM - link_row
+
+    def rim(row):
+        return jnp.stack([lax.dynamic_slice_in_dim(x, row, RIM, 0) for x in (k, v)])
+
+    from_link = lax.ppermute(rim(link_row), "ctx", over_links(ctx))
+    from_chip = lax.ppermute(rim(chip_row), "ctx", swap(ctx, 1))
+    low = jnp.where(core == 0, from_link, from_chip)
+    high = jnp.where(core == 0, from_chip, from_link)
+
     mask = lax.dynamic_slice_in_dim(block_mask[0], at_ctx * blocks, blocks, 0)
     ag = dot(g, w_out, ((1,), (1,))).astype(BF16)
-
-    ext = (tokens + 2 * RIM, feats)
+    own_t, stats = call(
+        own_kernel,
+        [((feats, tokens), F32), ((2, blocks * HEADS // 2, 2 * BLK), F32)],
+        [],
+        5 * 10**8,
+        mask, q, k, v,
+    )
     attn_t, part = call(
         forward_kernel,
         [((feats, tokens), BF16), ((feats, width), BF16)],
-        [(ext, BF16)] * 2,
+        [],
         10**9,
-        mask, q, k, v, low, high, g,
+        mask, q, low, high, own_t, stats, g,
     )
 
     rows, cols = feats // ctx, width // dp
@@ -169,6 +270,7 @@
     other = lax.ppermute(other, "ctx", swap(ctx, 1))
     half = total([mine, other]).astype(BF16)
 
+    ext = (tokens + 2 * RIM, feats)
     q_grad, k_own, v_own, to_low, to_high = call(
         backward_kernel,
         [((tokens, feats), BF16)]
@@ -177,9 +279,8 @@
         [(ext, BF16)] * 2 + [(ext, F32)] * 2,
         2 * 10**9,
         mask, q, k, v, low, high, ag,
-    )
-    from_high = lax.ppermute(to_low, "ctx", ring(ctx, -1))
-    from_low = lax.ppermute(to_high, "ctx", ring(ctx, 1))
+        after=(half,),
+    )
 
     def columns(step):
         return lax.dynamic_slice_in_dim(half, (at_dp ^ step) * cols, cols, 2)
@@ -188,6 +289,9 @@
         [columns(0)] + [lax.ppermute(columns(s), "dp", swap(dp, s)) for s in range(1, dp)]
     ).astype(BF16)
 
+    grad_link = lax.ppermute(jnp.where(core == 0, to_low, to_high), "ctx", over_links(ctx))
+    grad_chip = lax.ppermute(jnp.where(core == 0, to_high, to_low), "ctx", swap(ctx, 1))
+
     def of_chip(step):
         return lax.dynamic_index_in_dim(quarter, chip ^ step, 0, keepdims=False)
 
@@ -196,23 +300,19 @@
         + [lax.ppermute(of_chip(s), "ctx", swap(ctx, 2 * s)) for s in range(1, chips)]
     )
     piece = (piece * (dp * tokens * ctx) ** (-0.5)).astype(BF16)
-    pieces = jnp.stack(
-        [piece] + [lax.ppermute(piece, "dp", swap(dp, s)) for s in range(1, dp)]
-    )
-    step = 1
-    while step < dp:
-        turned = pieces[jnp.arange(dp) ^ step]
-        pieces = jnp.where((at_dp & step) != 0, turned, pieces)
-        step *= 2
-    weight_grad = jnp.concatenate([pieces[d] for d in range(dp)], axis=1).astype(F32)
+    pieces = [piece] + [lax.ppermute(piece, "dp", swap(dp, s)) for s in range(1, dp)]
+    (weight_grad,) = call(columns_kernel, [((rows, width), F32)], [], 10**6, at, *pieces)
 
     output = dot(attn_t, w_out, ((0,), (0,))).astype(BF16)
-    grads = []
-    for which, own in enumerate((k_own, v_own)):
-        own = own.at[:RIM].add(from_low[which].astype(F32))
-        own = own.at[tokens - RIM :].add(from_high[which].astype(F32))
-        grads.append(own.astype(BF16))
-    return (output[None], q_grad[None], grads[0][None], grads[1][None], weight_grad)
+    k_grad, v_grad = call(
+        rims_kernel,
+        [((tokens, feats), BF16)] * 2,
+        [],
+        10**6,
+        at, k_own, v_own, grad_link, grad_chip,
+        after=(piece,),
+    )
+    return (output[None], q_grad[None], k_grad[None], v_grad[None], weight_grad)
 
 
 def solution(mesh):

time: 58.9 us -> 47.1 us (0.80)
  waiting for transfers between devices: 20.1 us -> 8.76 us
  Pallas kernels: 9.96 us -> 13 us
  starting transfers between devices: 19.8 us -> 18 us
  other arithmetic: 2.9 us -> 1.54 us
    ppermute x4, waiting for transfers between devices: 11.7 us -> 2.26 us  [the longest x1 2.25 us: body(): from_link = lax.ppermute(rim(link_row), 'ctx', over_links(ctx))]
    ppermute x3, waiting for transfers between devices: 5.28 us -> 0.27 us  [body(): lax.ppermute(columns(s), 'dp', swap(dp, s))]
    pallas_call x2 -> x5, Pallas kernels: 9.96 us -> 13 us  [call(): pl.pallas_call(kernel, out_shape=[jax.ShapeDtypeStruct(s, d) for s, d in...]
    ppermute x4, starting transfers between devices: 8.14 us -> 6.43 us  [the longest x1 4.78 us: body(): from_link = lax.ppermute(rim(link_row), 'ctx', over_links(ctx))]
    ppermute x1, waiting for transfers between devices: 0.01 us -> 1.68 us  [body(): other = lax.ppermute(other, 'ctx', swap(ctx, 1))]
    broadcast_in_dim x2 -> x0, other arithmetic: 1.47 us -> none  [the longest x1 0.73 us: body(): grads[1][None]]
    ppermute x3, waiting for transfers between devices: 1.61 us -> 2.88 us  [body(): lax.ppermute(piece, 'dp', swap(dp, s))]
    slice x1 -> x0, local copies, waits for them, and re-layouts: 1.22 us -> none  [body(): high = lax.ppermute(jnp.stack([k[:RIM], v[:RIM]]), 'ctx', ring(ctx, -1))]
  transfers between devices with their start and end apart: 14 -> 14, of which waited for: 10 -> 8; matrix products, arithmetic and copies ran while one was open for 7% -> 4% of each run, Pallas kernels for 9% -> 21%
where the time goes in v2:
time: 47.1 us; the launch traced here: 46.9 us
  starting transfers between devices  18 us (38%)
  Pallas kernels  13 us (28%)
  waiting for transfers between devices  8.76 us (19%)
  local copies, waits for them, and re-layouts  3.05 us (6%)
  matrix products  1.74 us (4%)
  other arithmetic  1.54 us (3%)
  between operations  0.86 us (2%)
    pallas_call x5, Pallas kernels, call(): pl.pallas_call(kernel, out_shape=[jax.ShapeDtypeStruct(s, d) for s, d in...  13 us
    ppermute x1, starting transfers between devices, body(): from_link = lax.ppermute(rim(link_row), 'ctx', over_links(ctx))  4.78 us
    ppermute x3, starting transfers between devices, body(): lax.ppermute(of_chip(s), 'ctx', swap(ctx, 2 * s))  4.45 us
    ppermute x3, starting transfers between devices, body(): lax.ppermute(columns(s), 'dp', swap(dp, s))  3.55 us
    ppermute x3, starting transfers between devices, body(): lax.ppermute(piece, 'dp', swap(dp, s))  3.55 us
    ppermute x3, waiting for transfers between devices, body(): lax.ppermute(piece, 'dp', swap(dp, s))  2.88 us
    ppermute x1, waiting for transfers between devices, body(): from_link = lax.ppermute(rim(link_row), 'ctx', over_links(ctx))  2.25 us
    dot_general x2, matrix products, dot(): lax.dot_general(a, b, (contract, ((), ())), preferred_element_type=F32)  1.74 us
  transfers between devices with their start and end apart: 14, of which 8 were waited for; matrix products, arithmetic and copies ran while one was open for 4% of the time, Pallas kernels for 21%

profile of v2, /device:TPU:0, one launch (start us, length us, event | category | flops | bytes accessed | tf_op | source)
XLA Modules:
  0.0 46.9 jit_solution(12285558341309282772)
XLA Ops:
  0.6 0.0 copy-start
  0.7 1.2 %constant_dynamic-slice_fusion.3 = (bf16[1,128,512]{2,1,0:T(8,128)(2,1)S(1)}, bf16[1,128,512]{2,1,0:T(8,128)(2,1)S(1)}, bf16[1,128,512]{2,1,0:T(8,128)(2,1)S(1)}, bf16[1,128,512]{2,1,0:T(8,128)(2,1)S(1)}) fusion(bf16[1,256,512]{2,1,0:T(8,128)(2,1)} %param.8, s32[]{:T(128)S(6)} %select_n.78, s32[]{:T(128)S(6)} %select_n.77, bf16[1,256,512]{2,1,0:T(8,128)(2,1)} %param.7), kind=kLoop, calls=%fused_computation.24 | loop fusion | bytes 1048584 | tf_op jit(solution)/shard_map/dynamic_slice | solution.py:242
  1.9 0.0 copy-start.8
  1.9 0.5 %collective-permute-start.1 = (bf16[2,128,512]{2,1,0:T(8,128)(2,1)S(1)}, bf16[2,128,512]{2,1,0:T(8,128)(2,1)S(1)}, u32[]{:S(2)}, u32[]{:S(2)}) collective-permute-start(bf16[2,128,512]{2,1,0:T(8,128)(2,1)S(1)} %pad_maximum_fusion.1), channel_id=1, source_target_pairs={{0,1},{1,0},{2,3},{3,2},{4,5},{5,4},{6,7},{7,6},{8,9},{9,8},{10,11... | collective-permute-start | bytes 786440 | tf_op jit(solution)/shard_map/ppermute | solution.py:245
  2.5 4.8 %collective-permute-start = (bf16[2,128,512]{2,1,0:T(8,128)(2,1)S(1)}, bf16[2,128,512]{2,1,0:T(8,128)(2,1)S(1)}, u32[]{:S(2)}, u32[]{:S(2)}) collective-permute-start(bf16[2,128,512]{2,1,0:T(8,128)(2,1)S(1)} %pad_maximum_fusion), channel_id=1, source_target_pairs={{0,7},{1,2},{2,1},{3,4},{4,3},{5,6},{6,5},{7,0},{8,15},{9,10},{10,... | collective-permute-start | bytes 786440 | tf_op jit(solution)/shard_map/ppermute | solution.py:244
  7.3 0.7 %copy-done.11 = s32[1,16,3]{1,0,2:T(1,128)S(1)} copy-done((s32[1,16,3]{1,0,2:T(1,128)S(1)}, s32[1,16,3]{1,0,2:T(1,128)}, u32[]{:S(2)}) %copy-start.11) | copy-done | bytes 216
  7.9 0.1 constant_dynamic-slice_fusion.7
  8.0 0.1 copy.12
  8.1 3.0 %shard_map.101 = (f32[512,256]{1,0:T(8,128)S(1)}, f32[2,8,256]{2,1,0:T(8,128)S(1)}) custom-call(s32[2,3]{1,0:T(2,128)S(1)} %bitcast.41, bf16[256,512]{1,0:T(8,128)(2,1)S(1)} %bitcast.44, bf16[256,512]{1,0:T(8,128)(2,1)S(1)} %bitcast.39, bf16[256,512]{1,0:T(8,128)(2,1)S(1)} %bitcast.37), custom_call_target="tpu_custom_call" | custom-call | flops 500000000 | bytes 4194304 | tf_op jit(solution)/shard_map/pallas_call | solution.py:202
  11.1 0.0 copy-start.1
  11.2 0.0 copy-start.9
  11.2 2.3 %collective-permute-done = bf16[2,128,512]{2,1,0:T(8,128)(2,1)S(1)} collective-permute-done((bf16[2,128,512]{2,1,0:T(8,128)(2,1)S(1)}, bf16[2,128,512]{2,1,0:T(8,128)(2,1)S(1)}, u32[]{:S(2)}, u32[]{:S(2)}) %collective-permute-start) | collective-permute-done | bytes 262176 | tf_op jit(solution)/shard_map/ppermute | solution.py:244
  13.5 0.0 copy-start.4
  13.5 0.0 copy-start.6
  13.5 1.7 %shard_map.102 = (bf16[512,256]{1,0:T(8,128)(2,1)S(1)}, bf16[512,1024]{1,0:T(8,128)(2,1)S(1)}) custom-call(s32[2,3]{1,0:T(2,128)S(1)} %bitcast.42, bf16[256,512]{1,0:T(8,128)(2,1)S(1)} %bitcast.45, bf16[2,128,512]{2,1,0:T(8,128)(2,1)S(1)} %get-tuple-element.33.low, bf16[2,128,512]{2,1,0:T(8,128)(2,1)S(1)} %get-tuple-element.32.high, ...), custom_call_target="tpu_custom_call" | custom-call | flops 1000000000 | bytes 4194304 | tf_op jit(solution)/shard_map/pallas_call | solution.py:202
  15.3 0.8 %dynamic-slice_bitcast_fusion = bf16[4,64,1024]{2,1,0:T(8,128)(2,1)} fusion(bf16[4,2,64,1024]{3,2,1,0:T(8,128)(2,1)S(1)} %bitcast.34, s32[]{:T(128)S(6)} %select_n.82), kind=kLoop, calls=%fused_computation.5 | loop fusion | bytes 1048580 | tf_op jit(solution)/shard_map/jit(dynamic_index_in_dim)/squeeze | solution.py:269
  16.1 0.0 collective-permute-start.2
  16.1 0.1 pad_add_fusion.at
  16.2 0.5 %convolution_convert_fusion.1.ag = bf16[256,512]{1,0:T(8,128)(2,1)S(1)} fusion(bf16[512,1024]{1,0:T(8,128)(2,1)S(1)} %copy-done, bf16[1,256,1024]{2,1,0:T(8,128)(2,1)S(1)} %copy-done.1), kind=kOutput, calls=%fused_computation.2 | convolution fusion | flops 268566528 | bytes 1835008 | tf_op jit(solution)/shard_map/dot_general | solution.py:24
  16.7 1.7 %collective-permute-done.2 = bf16[4,64,1024]{2,1,0:T(8,128)(2,1)} collective-permute-done((bf16[4,64,1024]{2,1,0:T(8,128)(2,1)}, bf16[4,64,1024]{2,1,0:T(8,128)(2,1)}, u32[]{:S(2)}, u32[]{:S(2)}) %collective-permute-start.2) | collective-permute-done | bytes 524320 | tf_op jit(solution)/shard_map/ppermute | solution.py:270
  18.3 1.2 %fusion.1.after = bf16[4,64,1024]{2,1,0:T(8,128)(2,1)S(1)} fusion(bf16[4,64,1024]{2,1,0:T(8,128)(2,1)} %collective-permute-done.2, bf16[4,2,64,1024]{3,2,1,0:T(8,128)(2,1)S(1)} %bitcast.35, s32[]{:T(128)S(6)} %select_n.81), kind=kLoop, calls=%fused_computation.4 | loop fusion | flops 1048576 | bytes 1572868 | tf_op jit(solution)/shard_map/convert_element_type | solution.py:271
  19.6 0.0 copy-start.5
  19.6 0.0 copy-start.7
  19.6 0.0 copy-start.10
  19.6 0.1 constant_dynamic-slice_fusion.2
  19.7 2.5 %collective-permute-start.7 = (bf16[4,64,256]{2,1,0:T(8,128)(2,1)S(1)}, bf16[4,64,256]{2,1,0:T(8,128)(2,1)S(1)}, u32[]{:S(2)}, u32[]{:S(2)}) collective-permute-start(bf16[4,64,256]{2,1,0:T(8,128)(2,1)S(1)} %get-tuple-element.28), channel_id=1, source_target_pairs={{0,24},{8,16},{16,8},{24,0},{1,25},{9,17},{17,9},{25,1},{2,26},{10... | collective-permute-start | bytes 393224 | tf_op jit(solution)/shard_map/ppermute | solution.py:289
  22.2 0.5 %collective-permute-start.6 = (bf16[4,64,256]{2,1,0:T(8,128)(2,1)S(1)}, bf16[4,64,256]{2,1,0:T(8,128)(2,1)S(1)}, u32[]{:S(2)}, u32[]{:S(2)}) collective-permute-start(bf16[4,64,256]{2,1,0:T(8,128)(2,1)S(1)} %get-tuple-element.29), channel_id=1, source_target_pairs={{0,16},{8,24},{16,0},{24,8},{1,17},{9,25},{17,1},{25,9},{2,18},{10... | collective-permute-start | bytes 393224 | tf_op jit(solution)/shard_map/ppermute | solution.py:289
  22.7 0.5 %collective-permute-start.5 = (bf16[4,64,256]{2,1,0:T(8,128)(2,1)S(1)}, bf16[4,64,256]{2,1,0:T(8,128)(2,1)S(1)}, u32[]{:S(2)}, u32[]{:S(2)}) collective-permute-start(bf16[4,64,256]{2,1,0:T(8,128)(2,1)S(1)} %get-tuple-element.27), channel_id=1, source_target_pairs={{0,8},{8,0},{16,24},{24,16},{1,9},{9,1},{17,25},{25,17},{2,10},{10... | collective-permute-start | bytes 393224 | tf_op jit(solution)/shard_map/ppermute | solution.py:289
  23.3 5.6 %shard_map.103 = (bf16[256,512]{1,0:T(8,128)(2,1)}, f32[256,512]{1,0:T(8,128)S(1)}, f32[256,512]{1,0:T(8,128)S(1)}, bf16[2,128,512]{2,1,0:T(8,128)(2,1)S(1)}, bf16[2,128,512]{2,1,0:T(8,128)(2,1)S(1)}) custom-call(s32[2,3]{1,0:T(2,128)S(1)} %bitcast.43, bf16[256,512]{1,0:T(8,128)(2,1)S(1)} %bitcast.46, bf16[256,512]{1,0:T(8,128)(2,1)S(1)} %bitcast.40, ...), custom_call_target="tpu_custom_call" | custom-call | flops 2000000000 | bytes 4194304 | tf_op jit(solution)/shard_map/pallas_call | solution.py:202
  28.8 0.0 collective-permute-done.7
  28.8 0.2 collective-permute-done.6
  29.0 0.1 collective-permute-done.5
  29.1 0.1 add_convert_fusion
  29.2 2.4 %collective-permute-start.10 = (bf16[64,256]{1,0:T(8,128)(2,1)S(1)}, bf16[64,256]{1,0:T(8,128)(2,1)S(1)}, u32[]{:S(2)}, u32[]{:S(2)}) collective-permute-start(bf16[64,256]{1,0:T(8,128)(2,1)S(1)} %get-tuple-element.39), channel_id=1, source_target_pairs={{0,6},{1,7},{2,4},{3,5},{4,2},{5,3},{6,0},{7,1},{8,14},{9,15},{10,... | collective-permute-start | bytes 98312 | tf_op jit(solution)/shard_map/ppermute | solution.py:300
  31.6 0.0 collective-permute-start.9
  31.6 2.0 %collective-permute-start.8 = (bf16[64,256]{1,0:T(8,128)(2,1)S(1)}, bf16[64,256]{1,0:T(8,128)(2,1)S(1)}, u32[]{:S(2)}, u32[]{:S(2)}) collective-permute-start(bf16[64,256]{1,0:T(8,128)(2,1)S(1)} %get-tuple-element.38), channel_id=1, source_target_pairs={{0,2},{1,3},{2,0},{3,1},{4,6},{5,7},{6,4},{7,5},{8,10},{9,11},{10,... | collective-permute-start | bytes 98312 | tf_op jit(solution)/shard_map/ppermute | solution.py:300
  33.7 1.1 %collective-permute-start.3 = (bf16[2,128,512]{2,1,0:T(8,128)(2,1)S(1)}, bf16[2,128,512]{2,1,0:T(8,128)(2,1)S(1)}, u32[]{:S(2)}, u32[]{:S(2)}) collective-permute-start(bf16[2,128,512]{2,1,0:T(8,128)(2,1)S(1)} %get-tuple-element.31), channel_id=1, source_target_pairs={{0,7},{1,2},{2,1},{3,4},{4,3},{5,6},{6,5},{7,0},{8,15},{9,10},{10,... | collective-permute-start | bytes 786440 | tf_op jit(solution)/shard_map/ppermute | solution.py:292
  34.8 0.0 collective-permute-start.4
  34.8 0.2 collective-permute-done.10
  35.0 1.5 %collective-permute-done.9 = bf16[64,256]{1,0:T(8,128)(2,1)S(1)} collective-permute-done((bf16[64,256]{1,0:T(8,128)(2,1)S(1)}, bf16[64,256]{1,0:T(8,128)(2,1)S(1)}, u32[]{:S(2)}, u32[]{:S(2)}) %collective-permute-start.9) | collective-permute-done | bytes 32800 | tf_op jit(solution)/shard_map/ppermute | solution.py:300
  36.5 1.6 %collective-permute-start.11 = (bf16[64,256]{1,0:T(8,128)(2,1)S(1)}, bf16[64,256]{1,0:T(8,128)(2,1)S(1)}, u32[]{:S(2)}, u32[]{:S(2)}) collective-permute-start(bf16[64,256]{1,0:T(8,128)(2,1)S(1)} %fusion.5.after.refs_0_), channel_id=1, source_target_pairs={{0,8},{8,0},{16,24},{24,16},{1,9},{9,1},{17,25},{25,17},{2,10},{10... | collective-permute-start | bytes 98312 | tf_op jit(solution)/shard_map/ppermute | solution.py:303
  38.1 1.3 %collective-permute-start.12 = (bf16[64,256]{1,0:T(8,128)(2,1)S(1)}, bf16[64,256]{1,0:T(8,128)(2,1)S(1)}, u32[]{:S(2)}, u32[]{:S(2)}) collective-permute-start(bf16[64,256]{1,0:T(8,128)(2,1)S(1)} %fusion.5.after.refs_0_), channel_id=1, source_target_pairs={{0,16},{8,24},{16,0},{24,8},{1,17},{9,25},{17,1},{25,9},{2,18},{10... | collective-permute-start | bytes 98312 | tf_op jit(solution)/shard_map/ppermute | solution.py:303
  39.4 0.7 %collective-permute-start.13 = (bf16[64,256]{1,0:T(8,128)(2,1)S(1)}, bf16[64,256]{1,0:T(8,128)(2,1)S(1)}, u32[]{:S(2)}, u32[]{:S(2)}) collective-permute-start(bf16[64,256]{1,0:T(8,128)(2,1)S(1)} %fusion.5.after.refs_0_), channel_id=1, source_target_pairs={{0,24},{8,16},{16,8},{24,0},{1,25},{9,17},{17,9},{25,1},{2,26},{10... | collective-permute-start | bytes 98312 | tf_op jit(solution)/shard_map/ppermute | solution.py:303
  40.1 1.3 %fusion = bf16[1,256,1024]{2,1,0:T(8,128)(2,1)} fusion(bf16[512,256]{1,0:T(8,128)(2,1)S(1)} %get-tuple-element.18, bf16[512,1024]{1,0:T(8,128)(2,1)S(1)} %copy-done), kind=kOutput, calls=%fused_computation.1 | convolution fusion | flops 268697600 | bytes 1835008 | tf_op jit(solution)/shard_map/dot_general | solution.py:24
  41.3 0.7 %collective-permute-done.12.refs_2_ = bf16[64,256]{1,0:T(8,128)(2,1)S(1)} collective-permute-done((bf16[64,256]{1,0:T(8,128)(2,1)S(1)}, bf16[64,256]{1,0:T(8,128)(2,1)S(1)}, u32[]{:S(2)}, u32[]{:S(2)}) %collective-permute-start.12) | collective-permute-done | bytes 32800 | tf_op jit(solution)/shard_map/ppermute | solution.py:303
  42.0 2.2 %collective-permute-done.13.refs_3_ = bf16[64,256]{1,0:T(8,128)(2,1)S(1)} collective-permute-done((bf16[64,256]{1,0:T(8,128)(2,1)S(1)}, bf16[64,256]{1,0:T(8,128)(2,1)S(1)}, u32[]{:S(2)}, u32[]{:S(2)}) %collective-permute-start.13) | collective-permute-done | bytes 32800 | tf_op jit(solution)/shard_map/ppermute | solution.py:303
  44.2 1.3 %shard_map.105 = f32[64,1024]{1,0:T(8,128)} custom-call(s32[2]{0:T(128)S(1)} %pad_add_fusion.at, bf16[64,256]{1,0:T(8,128)(2,1)S(1)} %fusion.5.after.refs_0_, bf16[64,256]{1,0:T(8,128)(2,1)S(1)} %collective-permute-done.11.refs_1_, bf16[64,256]{1,0:T(8,128)(2,1)S(1)} %collective-permute-done.12.refs_2_, bf16[64,256]{1,0:T(8,128)(2,1)S(1)} %collective-permute-done.13.refs_3_), custom_call_target="tpu_custom_call" | custom-call | flops 1000000 | bytes 4194304 | tf_op jit(solution)/shard_map/pallas_call | solution.py:202
  45.5 1.4 %shard_map.104 = (bf16[256,512]{1,0:T(8,128)(2,1)}, bf16[256,512]{1,0:T(8,128)(2,1)}) custom-call(s32[2]{0:T(128)S(1)} %pad_add_fusion.at, f32[256,512]{1,0:T(8,128)S(1)} %get-tuple-element.21.k_own, f32[256,512]{1,0:T(8,128)S(1)} %get-tuple-element.22.v_own, bf16[2,128,512]{2,1,0:T(8,128)(2,1)S(1)} %collective-permute-done.3.from_link, ...), custom_call_target="tpu_custom_call" | custom-call | flops 1000000 | bytes 4194304 | tf_op jit(solution)/shard_map/pallas_call | solution.py:202
  (25 shorter events, 0.2 us)
Async XLA Ops:
  0.6 15.5 %copy-start = (bf16[512,1024]{1,0:T(8,128)(2,1)S(1)}, bf16[512,1024]{1,0:T(8,128)(2,1)}, u32[]{:S(2)}) copy-start(bf16[512,1024]{1,0:T(8,128)(2,1)} %param.10) | copy-start | bytes 3145732
  1.9 6.2 %copy-start.8 = (bf16[1,256,512]{2,1,0:T(8,128)(2,1)S(1)}, bf16[1,256,512]{2,1,0:T(8,128)(2,1)}, u32[]{:S(2)}) copy-start(bf16[1,256,512]{2,1,0:T(8,128)(2,1)} %param.6) | copy-start | bytes 786436
  1.9 9.2 %collective-permute-start.1 = (bf16[2,128,512]{2,1,0:T(8,128)(2,1)S(1)}, bf16[2,128,512]{2,1,0:T(8,128)(2,1)S(1)}, u32[]{:S(2)}, u32[]{:S(2)}) collective-permute-start(bf16[2,128,512]{2,1,0:T(8,128)(2,1)S(1)} %pad_maximum_fusion.1), channel_id=1, source_target_pairs={{0,1},{1,0},{2,3},{3,2},{4,5},{5,4},{6,7},{7,6},{8,9},{9,8},{10,11... | collective-permute-start | bytes 786440 | tf_op jit(solution)/shard_map/ppermute | solution.py:245
  2.5 5.7 %copy-start.2 = (bf16[1,256,512]{2,1,0:T(8,128)(2,1)S(1)}, bf16[1,256,512]{2,1,0:T(8,128)(2,1)}, u32[]{:S(2)}) copy-start(bf16[1,256,512]{2,1,0:T(8,128)(2,1)} %param.8) | copy-start | bytes 786436
  2.5 5.7 %copy-start.3 = (bf16[1,256,512]{2,1,0:T(8,128)(2,1)S(1)}, bf16[1,256,512]{2,1,0:T(8,128)(2,1)}, u32[]{:S(2)}) copy-start(bf16[1,256,512]{2,1,0:T(8,128)(2,1)} %param.7) | copy-start | bytes 786436
  2.5 10.9 %collective-permute-start = (bf16[2,128,512]{2,1,0:T(8,128)(2,1)S(1)}, bf16[2,128,512]{2,1,0:T(8,128)(2,1)S(1)}, u32[]{:S(2)}, u32[]{:S(2)}) collective-permute-start(bf16[2,128,512]{2,1,0:T(8,128)(2,1)S(1)} %pad_maximum_fusion), channel_id=1, source_target_pairs={{0,7},{1,2},{2,1},{3,4},{4,3},{5,6},{6,5},{7,0},{8,15},{9,10},{10,... | collective-permute-start | bytes 786440 | tf_op jit(solution)/shard_map/ppermute | solution.py:244
  7.3 0.7 %copy-start.11 = (s32[1,16,3]{1,0,2:T(1,128)S(1)}, s32[1,16,3]{1,0,2:T(1,128)}, u32[]{:S(2)}) copy-start(s32[1,16,3]{1,0,2:T(1,128)} %param.11) | copy-start | bytes 580
  11.1 2.4 %copy-start.1 = (bf16[1,256,1024]{2,1,0:T(8,128)(2,1)S(1)}, bf16[1,256,1024]{2,1,0:T(8,128)(2,1)}, u32[]{:S(2)}) copy-start(bf16[1,256,1024]{2,1,0:T(8,128)(2,1)} %param.9) | copy-start | bytes 1572868
  11.2 2.4 %copy-start.9 = (bf16[1,256,512]{2,1,0:T(8,128)(2,1)S(1)}, bf16[1,256,512]{2,1,0:T(8,128)(2,1)}, u32[]{:S(2)}) copy-start(bf16[1,256,512]{2,1,0:T(8,128)(2,1)} %param.6) | copy-start | bytes 786436
  13.5 1.8 %copy-start.4 = (bf16[2,128,512]{2,1,0:T(8,128)(2,1)}, bf16[2,128,512]{2,1,0:T(8,128)(2,1)S(1)}, u32[]{:S(2)}) copy-start(bf16[2,128,512]{2,1,0:T(8,128)(2,1)S(1)} %get-tuple-element.32.high) | copy-start | bytes 786436
  13.5 1.8 %copy-start.6 = (bf16[2,128,512]{2,1,0:T(8,128)(2,1)}, bf16[2,128,512]{2,1,0:T(8,128)(2,1)S(1)}, u32[]{:S(2)}) copy-start(bf16[2,128,512]{2,1,0:T(8,128)(2,1)S(1)} %get-tuple-element.33.low) | copy-start | bytes 786436
  16.1 2.3 %collective-permute-start.2 = (bf16[4,64,1024]{2,1,0:T(8,128)(2,1)}, bf16[4,64,1024]{2,1,0:T(8,128)(2,1)}, u32[]{:S(2)}, u32[]{:S(2)}) collective-permute-start(bf16[4,64,1024]{2,1,0:T(8,128)(2,1)} %dynamic-slice_bitcast_fusion), channel_id=1, source_target_pairs={{0,1},{1,0},{2,3},{3,2},{4,5},{5,4},{6,7},{7,6},{8,9},{9,8},{10,11... | collective-permute-start | bytes 1572872 | tf_op jit(solution)/shard_map/ppermute | solution.py:270
  19.6 3.7 %copy-start.5 = (bf16[2,128,512]{2,1,0:T(8,128)(2,1)S(1)}, bf16[2,128,512]{2,1,0:T(8,128)(2,1)}, u32[]{:S(2)}) copy-start(bf16[2,128,512]{2,1,0:T(8,128)(2,1)} %copy-done.4) | copy-start | bytes 786436
  19.6 3.7 %copy-start.7 = (bf16[2,128,512]{2,1,0:T(8,128)(2,1)S(1)}, bf16[2,128,512]{2,1,0:T(8,128)(2,1)}, u32[]{:S(2)}) copy-start(bf16[2,128,512]{2,1,0:T(8,128)(2,1)} %copy-done.6) | copy-start | bytes 786436
  19.6 3.6 %copy-start.10 = (bf16[1,256,512]{2,1,0:T(8,128)(2,1)S(1)}, bf16[1,256,512]{2,1,0:T(8,128)(2,1)}, u32[]{:S(2)}) copy-start(bf16[1,256,512]{2,1,0:T(8,128)(2,1)} %param.6) | copy-start | bytes 786436
  19.7 9.1 %collective-permute-start.7 = (bf16[4,64,256]{2,1,0:T(8,128)(2,1)S(1)}, bf16[4,64,256]{2,1,0:T(8,128)(2,1)S(1)}, u32[]{:S(2)}, u32[]{:S(2)}) collective-permute-start(bf16[4,64,256]{2,1,0:T(8,128)(2,1)S(1)} %get-tuple-element.28), channel_id=1, source_target_pairs={{0,24},{8,16},{16,8},{24,0},{1,25},{9,17},{17,9},{25,1},{2,26},{10... | collective-permute-start | bytes 393224 | tf_op jit(solution)/shard_map/ppermute | solution.py:289
  22.2 6.8 %collective-permute-start.6 = (bf16[4,64,256]{2,1,0:T(8,128)(2,1)S(1)}, bf16[4,64,256]{2,1,0:T(8,128)(2,1)S(1)}, u32[]{:S(2)}, u32[]{:S(2)}) collective-permute-start(bf16[4,64,256]{2,1,0:T(8,128)(2,1)S(1)} %get-tuple-element.29), channel_id=1, source_target_pairs={{0,16},{8,24},{16,0},{24,8},{1,17},{9,25},{17,1},{25,9},{2,18},{10... | collective-permute-start | bytes 393224 | tf_op jit(solution)/shard_map/ppermute | solution.py:289
  22.7 6.4 %collective-permute-start.5 = (bf16[4,64,256]{2,1,0:T(8,128)(2,1)S(1)}, bf16[4,64,256]{2,1,0:T(8,128)(2,1)S(1)}, u32[]{:S(2)}, u32[]{:S(2)}) collective-permute-start(bf16[4,64,256]{2,1,0:T(8,128)(2,1)S(1)} %get-tuple-element.27), channel_id=1, source_target_pairs={{0,8},{8,0},{16,24},{24,16},{1,9},{9,1},{17,25},{25,17},{2,10},{10... | collective-permute-start | bytes 393224 | tf_op jit(solution)/shard_map/ppermute | solution.py:289
  29.2 5.8 %collective-permute-start.10 = (bf16[64,256]{1,0:T(8,128)(2,1)S(1)}, bf16[64,256]{1,0:T(8,128)(2,1)S(1)}, u32[]{:S(2)}, u32[]{:S(2)}) collective-permute-start(bf16[64,256]{1,0:T(8,128)(2,1)S(1)} %get-tuple-element.39), channel_id=1, source_target_pairs={{0,6},{1,7},{2,4},{3,5},{4,2},{5,3},{6,0},{7,1},{8,14},{9,15},{10,... | collective-permute-start | bytes 98312 | tf_op jit(solution)/shard_map/ppermute | solution.py:300
  31.6 4.9 %collective-permute-start.9 = (bf16[64,256]{1,0:T(8,128)(2,1)S(1)}, bf16[64,256]{1,0:T(8,128)(2,1)S(1)}, u32[]{:S(2)}, u32[]{:S(2)}) collective-permute-start(bf16[64,256]{1,0:T(8,128)(2,1)S(1)} %get-tuple-element.40), channel_id=1, source_target_pairs={{0,4},{1,5},{2,6},{3,7},{4,0},{5,1},{6,2},{7,3},{8,12},{9,13},{10,... | collective-permute-start | bytes 98312 | tf_op jit(solution)/shard_map/ppermute | solution.py:300
  31.6 4.9 %collective-permute-start.8 = (bf16[64,256]{1,0:T(8,128)(2,1)S(1)}, bf16[64,256]{1,0:T(8,128)(2,1)S(1)}, u32[]{:S(2)}, u32[]{:S(2)}) collective-permute-start(bf16[64,256]{1,0:T(8,128)(2,1)S(1)} %get-tuple-element.38), channel_id=1, source_target_pairs={{0,2},{1,3},{2,0},{3,1},{4,6},{5,7},{6,4},{7,5},{8,10},{9,11},{10,... | collective-permute-start | bytes 98312 | tf_op jit(solution)/shard_map/ppermute | solution.py:300
  33.7 11.8 %collective-permute-start.3 = (bf16[2,128,512]{2,1,0:T(8,128)(2,1)S(1)}, bf16[2,128,512]{2,1,0:T(8,128)(2,1)S(1)}, u32[]{:S(2)}, u32[]{:S(2)}) collective-permute-start(bf16[2,128,512]{2,1,0:T(8,128)(2,1)S(1)} %get-tuple-element.31), channel_id=1, source_target_pairs={{0,7},{1,2},{2,1},{3,4},{4,3},{5,6},{6,5},{7,0},{8,15},{9,10},{10,... | collective-permute-start | bytes 786440 | tf_op jit(solution)/shard_map/ppermute | solution.py:292
  34.8 10.7 %collective-permute-start.4 = (bf16[2,128,512]{2,1,0:T(8,128)(2,1)S(1)}, bf16[2,128,512]{2,1,0:T(8,128)(2,1)S(1)}, u32[]{:S(2)}, u32[]{:S(2)}) collective-permute-start(bf16[2,128,512]{2,1,0:T(8,128)(2,1)S(1)} %get-tuple-element.30), channel_id=1, source_target_pairs={{0,1},{1,0},{2,3},{3,2},{4,5},{5,4},{6,7},{7,6},{8,9},{9,8},{10,11... | collective-permute-start | bytes 786440 | tf_op jit(solution)/shard_map/ppermute | solution.py:293
  36.5 4.8 %collective-permute-start.11 = (bf16[64,256]{1,0:T(8,128)(2,1)S(1)}, bf16[64,256]{1,0:T(8,128)(2,1)S(1)}, u32[]{:S(2)}, u32[]{:S(2)}) collective-permute-start(bf16[64,256]{1,0:T(8,128)(2,1)S(1)} %fusion.5.after.refs_0_), channel_id=1, source_target_pairs={{0,8},{8,0},{16,24},{24,16},{1,9},{9,1},{17,25},{25,17},{2,10},{10... | collective-permute-start | bytes 98312 | tf_op jit(solution)/shard_map/ppermute | solution.py:303
  38.1 3.9 %collective-permute-start.12 = (bf16[64,256]{1,0:T(8,128)(2,1)S(1)}, bf16[64,256]{1,0:T(8,128)(2,1)S(1)}, u32[]{:S(2)}, u32[]{:S(2)}) collective-permute-start(bf16[64,256]{1,0:T(8,128)(2,1)S(1)} %fusion.5.after.refs_0_), channel_id=1, source_target_pairs={{0,16},{8,24},{16,0},{24,8},{1,17},{9,25},{17,1},{25,9},{2,18},{10... | collective-permute-start | bytes 98312 | tf_op jit(solution)/shard_map/ppermute | solution.py:303
  39.4 4.8 %collective-permute-start.13 = (bf16[64,256]{1,0:T(8,128)(2,1)S(1)}, bf16[64,256]{1,0:T(8,128)(2,1)S(1)}, u32[]{:S(2)}, u32[]{:S(2)}) collective-permute-start(bf16[64,256]{1,0:T(8,128)(2,1)S(1)} %fusion.5.after.refs_0_), channel_id=1, source_target_pairs={{0,24},{8,16},{16,8},{24,0},{1,25},{9,17},{17,9},{25,1},{2,26},{10... | collective-permute-start | bytes 98312 | tf_op jit(solution)/shard_map/ppermute | solution.py:303

commit v3 on v2

--- a/solution.py
+++ b/solution.py
@@ -95,7 +95,23 @@
     )
 
 
-def forward_kernel(mask, q, low, high, own_t, stats, g, attn_t, part):
+def pack_kernel(k, v, to_link, to_chip, sems):
+    tokens = k.shape[0]
+    link_row = lax.rem(lax.axis_index("ctx"), 2) * (tokens - RIM)
+    chip_row = tokens - RIM - link_row
+    copies = []
+    for which, source in enumerate((k, v)):
+        for out, row in ((to_link, link_row), (to_chip, chip_row)):
+            rows = pl.ds(pl.multiple_of(row, RIM), RIM)
+            copies.append(
+                pltpu.make_async_copy(source.at[rows], out.at[which], sems.at[len(copies)])
+            )
+            copies[-1].start()
+    for copy in copies:
+        copy.wait()
+
+
+def forward_kernel(mask, q, low, high, own_t, stats, g, attn_t, mine, other):
     blocks = q.shape[0] // BLK
     pairs = HEADS // 2
     for b in range(blocks):
@@ -125,7 +141,19 @@
             if both is not None:
                 attn = attn + own_features(both) * spread(share)
             attn_t[cols, rows] = attn.astype(BF16)
-    part[...] = dot(attn_t[...], g[...], ((1,), (0,))).astype(BF16)
+    part = dot(attn_t[...], g[...], ((1,), (0,))).astype(BF16)
+    core = lax.rem(lax.axis_index("ctx"), 2)
+    chips, rows, _ = mine.shape
+    for c in range(2 * chips):
+        value = part[c * rows : (c + 1) * rows]
+
+        @pl.when(core == c % 2)
+        def _():
+            mine[c // 2] = value
+
+        @pl.when(core != c % 2)
+        def _():
+            other[c // 2] = value
 
 
 def backward_kernel(
@@ -169,9 +197,9 @@
     to_high[1] = dv[RIM + tokens :].astype(BF16)
 
 
-def rims_kernel(at, k_own, v_own, from_link, from_chip, after, k_grad, v_grad):
+def last_kernel(k_own, v_own, from_link, from_chip, pieces, k_grad, v_grad, weight_grad):
     tokens = k_own.shape[0]
-    core = at[0]
+    core = lax.rem(lax.axis_index("ctx"), 2)
     for which, (own, grad) in enumerate(((k_own, k_grad), (v_own, v_grad))):
         link = from_link[which].astype(F32)
         chip = from_chip[which].astype(F32)
@@ -184,32 +212,35 @@
             if tokens > 2 * RIM:
                 grad[RIM : tokens - RIM] = own[RIM : tokens - RIM].astype(BF16)
             grad[tokens - RIM :] = (own[tokens - RIM :] + high).astype(BF16)
-
-
-def columns_kernel(at, *refs):
-    pieces, out = refs[:-1], refs[-1]
-    cols = pieces[0].shape[1]
-    for d in range(len(pieces)):
-        value = pieces[0][...]
-        for s in range(1, len(pieces)):
-            value = jnp.where((at[1] ^ s) == d, pieces[s][...], value)
-        out[:, d * cols : (d + 1) * cols] = value.astype(F32)
-
-
-def call(kernel, outs, scratch, flops, *args, after=()):
+    cols = pieces.shape[2]
+    for d in range(pieces.shape[0]):
+        weight_grad[:, d * cols : (d + 1) * cols] = pieces[d].astype(F32)
+
+
+def call(kernel, outs, scratch, flops, *args, first=pltpu.VMEM):
     in_vmem = pl.BlockSpec(memory_space=pltpu.VMEM)
-    anywhere = pl.BlockSpec(memory_space=pl.ANY)
     return pl.pallas_call(
         kernel,
         out_shape=[jax.ShapeDtypeStruct(s, d) for s, d in outs],
-        in_specs=[pl.BlockSpec(memory_space=pltpu.SMEM)]
-        + [in_vmem] * (len(args) - 1)
-        + [anywhere] * len(after),
+        in_specs=[pl.BlockSpec(memory_space=first)] + [in_vmem] * (len(args) - 1),
         out_specs=[in_vmem] * len(outs),
         scratch_shapes=[pltpu.VMEM(s, d) for s, d in scratch],
-        compiler_params=pltpu.CompilerParams(vmem_limit_bytes=32 * 1024 * 1024),
+        compiler_params=pltpu.CompilerParams(vmem_limit_bytes=16 * 1024 * 1024),
         cost_estimate=pl.CostEstimate(flops=flops, bytes_accessed=4 << 20, transcendentals=0),
-    )(*args, *after)
+    )(*args)
+
+
+def pack(k, v):
+    in_hbm = pl.BlockSpec(memory_space=pltpu.HBM)
+    in_vmem = pl.BlockSpec(memory_space=pltpu.VMEM)
+    rim = jax.ShapeDtypeStruct((2, RIM, k.shape[1]), k.dtype)
+    return pl.pallas_call(
+        pack_kernel,
+        out_shape=[rim, rim],
+        in_specs=[in_hbm, in_hbm],
+        out_specs=[in_vmem, in_vmem],
+        scratch_shapes=[pltpu.SemaphoreType.DMA((4,))],
+    )(k, v)
 
 
 def swap(count, bits):
@@ -232,17 +263,11 @@
     ctx, dp = lax.axis_size("ctx"), lax.axis_size("dp")
     chips = ctx // 2
     at_ctx, at_dp = lax.axis_index("ctx"), lax.axis_index("dp")
-    core, chip = at_ctx % 2, at_ctx // 2
-    at = jnp.stack([core, at_dp])
-
-    link_row = core * (tokens - RIM)
-    chip_row = tokens - RIM - link_row
-
-    def rim(row):
-        return jnp.stack([lax.dynamic_slice_in_dim(x, row, RIM, 0) for x in (k, v)])
-
-    from_link = lax.ppermute(rim(link_row), "ctx", over_links(ctx))
-    from_chip = lax.ppermute(rim(chip_row), "ctx", swap(ctx, 1))
+    core = at_ctx % 2
+
+    to_link, to_chip = pack(k, v)
+    from_link = lax.ppermute(to_link, "ctx", over_links(ctx))
+    from_chip = lax.ppermute(to_chip, "ctx", swap(ctx, 1))
     low = jnp.where(core == 0, from_link, from_chip)
     high = jnp.where(core == 0, from_chip, from_link)
 
@@ -254,19 +279,18 @@
         [],
         5 * 10**8,
         mask, q, k, v,
-    )
-    attn_t, part = call(
+        first=pltpu.SMEM,
+    )
+    rows, cols = feats // ctx, width // dp
+    attn_t, mine, other = call(
         forward_kernel,
-        [((feats, tokens), BF16), ((feats, width), BF16)],
+        [((feats, tokens), BF16)] + [((chips, rows, width), BF16)] * 2,
         [],
         10**9,
         mask, q, low, high, own_t, stats, g,
-    )
-
-    rows, cols = feats // ctx, width // dp
-    part = part.reshape(chips, 2, rows, width)
-    mine = lax.dynamic_index_in_dim(part, core, 1, keepdims=False)
-    other = lax.dynamic_index_in_dim(part, 1 - core, 1, keepdims=False)
+        first=pltpu.SMEM,
+    )
+
     other = lax.ppermute(other, "ctx", swap(ctx, 1))
     half = total([mine, other]).astype(BF16)
 
@@ -278,8 +302,8 @@
         + [((2, RIM, feats), BF16)] * 2,
         [(ext, BF16)] * 2 + [(ext, F32)] * 2,
         2 * 10**9,
-        mask, q, k, v, low, high, ag,
-        after=(half,),
+        mask, q, k, v, low, high, ag, half[0, :16, :128],
+        first=pltpu.SMEM,
     )
 
     def columns(step):
@@ -292,25 +316,19 @@
     grad_link = lax.ppermute(jnp.where(core == 0, to_low, to_high), "ctx", over_links(ctx))
     grad_chip = lax.ppermute(jnp.where(core == 0, to_high, to_low), "ctx", swap(ctx, 1))
 
-    def of_chip(step):
-        return lax.dynamic_index_in_dim(quarter, chip ^ step, 0, keepdims=False)
-
-    piece = total(
-        [of_chip(0)]
-        + [lax.ppermute(of_chip(s), "ctx", swap(ctx, 2 * s)) for s in range(1, chips)]
-    )
+    groups = [list(range(c, ctx, 2)) for c in range(2)]
+    over_chips = lax.all_to_all(quarter, "ctx", 0, 0, axis_index_groups=groups)
+    piece = total([over_chips[i] for i in range(chips)])
     piece = (piece * (dp * tokens * ctx) ** (-0.5)).astype(BF16)
-    pieces = [piece] + [lax.ppermute(piece, "dp", swap(dp, s)) for s in range(1, dp)]
-    (weight_grad,) = call(columns_kernel, [((rows, width), F32)], [], 10**6, at, *pieces)
+    pieces = lax.all_to_all(jnp.broadcast_to(piece[None], (dp, rows, cols)), "dp", 0, 0)
 
     output = dot(attn_t, w_out, ((0,), (0,))).astype(BF16)
-    k_grad, v_grad = call(
-        rims_kernel,
-        [((tokens, feats), BF16)] * 2,
+    k_grad, v_grad, weight_grad = call(
+        last_kernel,
+        [((tokens, feats), BF16)] * 2 + [((rows, width), F32)],
         [],
         10**6,
-        at, k_own, v_own, grad_link, grad_chip,
-        after=(piece,),
+        k_own, v_own, grad_link, grad_chip, pieces,
     )
     return (output[None], q_grad[None], k_grad[None], v_grad[None], weight_grad)
 

time: 47.1 us -> 54.8 us (1.16)
  waiting for transfers between devices: 8.76 us -> 12.5 us
  Pallas kernels: 13 us -> 14.2 us
  starting transfers between devices: 18 us -> 19.1 us
  local copies, waits for them, and re-layouts: 3.05 us -> 3.98 us
    all_to_all x0 -> x2, waiting for transfers between devices: none -> 9.43 us  [the longest x1 5.68 us: body(): over_chips = lax.all_to_all(quarter, 'ctx', 0, 0, axis_index_groups=groups)]
    ppermute x8 -> x2, starting transfers between devices: 13.3 us -> 4.56 us  [the longest x1 4.55 us: body(): from_link = lax.ppermute(to_link, 'ctx', over_links(ctx))]
    all_to_all x0 -> x2, starting transfers between devices: none -> 7.99 us  [the longest x1 4.07 us: body(): lax.all_to_all(jnp.broadcast_to(piece[None], (dp, rows, cols)), 'dp', 0, 0)]
    ppermute x8 -> x2, waiting for transfers between devices: 6.8 us -> 1.39 us  [the longest x1 1.39 us: body(): from_link = lax.ppermute(to_link, 'ctx', over_links(ctx))]
    unnamed x24, local copies, waits for them, and re-layouts: 0.75 us -> 3.08 us
    pallas_call x0 -> x1, Pallas kernels: none -> 2.04 us  [pack(): pl.pallas_call(pack_kernel, out_shape=[rim, rim], in_specs=[in_hbm, in_hb...]
    dynamic_slice x1 -> x0, local copies, waits for them, and re-layouts: 1.22 us -> none  [rim(): return jnp.stack([lax.dynamic_slice_in_dim(x, row, RIM, 0) for x in (k, v)])]
    ppermute x1, starting transfers between devices: 1.13 us -> 2.29 us  [body(): lax.ppermute(jnp.where(core == 0, to_low, to_high), 'ctx', over_links(ctx))]
  transfers between devices with their start and end apart: 14 -> 10, of which waited for: 8 -> 4; matrix products, arithmetic and copies ran while one was open for 4% -> 5% of each run, Pallas kernels for 21% -> 16%
where the time goes in v3:
time: 54.8 us; the launch traced here: 54.4 us
  starting transfers between devices  19.1 us (35%)
  Pallas kernels  14.2 us (26%)
  waiting for transfers between devices  12.5 us (23%)
  local copies, waits for them, and re-layouts  3.98 us (7%)
  other arithmetic  2.08 us (4%)
  matrix products  1.74 us (3%)
  between operations  0.79 us (1%)
    pallas_call x4, Pallas kernels, call(): pl.pallas_call(kernel, out_shape=[jax.ShapeDtypeStruct(s, d) for s, d in...  12.2 us
    all_to_all x1, waiting for transfers between devices, body(): over_chips = lax.all_to_all(quarter, 'ctx', 0, 0, axis_index_groups=groups)  5.68 us
    ppermute x1, starting transfers between devices, body(): from_link = lax.ppermute(to_link, 'ctx', over_links(ctx))  4.55 us
    ppermute x3, starting transfers between devices, body(): lax.ppermute(columns(s), 'dp', swap(dp, s))  4.16 us
    all_to_all x1, starting transfers between devices, body(): lax.all_to_all(jnp.broadcast_to(piece[None], (dp, rows, cols)), 'dp', 0, 0)  4.07 us
    all_to_all x1, starting transfers between devices, body(): over_chips = lax.all_to_all(quarter, 'ctx', 0, 0, axis_index_groups=groups)  3.93 us
    all_to_all x1, waiting for transfers between devices, body(): lax.all_to_all(jnp.broadcast_to(piece[None], (dp, rows, cols)), 'dp', 0, 0)  3.75 us
    unnamed x24, local copies, waits for them, and re-layouts  3.08 us
  transfers between devices with their start and end apart: 10, of which 4 were waited for; matrix products, arithmetic and copies ran while one was open for 5% of the time, Pallas kernels for 16%

profile of v3, /device:TPU:0, one launch (start us, length us, event | category | flops | bytes accessed | tf_op | source)
XLA Modules:
  0.0 54.4 jit_solution(8349716315241696408)
XLA Ops:
  0.6 0.0 copy-start
  0.6 0.0 copy-start.2
  0.7 0.0 copy-start.3
  0.7 2.0 %shard_map.101 = (bf16[2,128,512]{2,1,0:T(8,128)(2,1)}, bf16[2,128,512]{2,1,0:T(8,128)(2,1)}) custom-call(bf16[256,512]{1,0:T(8,128)(2,1)} %bitcast.20, bf16[256,512]{1,0:T(8,128)(2,1)} %bitcast.23), custom_call_target="tpu_custom_call" | custom-call | tf_op jit(solution)/shard_map/pallas_call | solution.py:237
  2.7 4.6 %collective-permute-start = (bf16[2,128,512]{2,1,0:T(8,128)(2,1)}, bf16[2,128,512]{2,1,0:T(8,128)(2,1)S(1)}, u32[]{:S(2)}, u32[]{:S(2)}) collective-permute-start(bf16[2,128,512]{2,1,0:T(8,128)(2,1)} %get-tuple-element.20), channel_id=1, source_target_pairs={{0,7},{1,2},{2,1},{3,4},{4,3},{5,6},{6,5},{7,0},{8,15},{9,10},{10,... | collective-permute-start | bytes 786440 | tf_op jit(solution)/shard_map/ppermute | solution.py:269
  7.3 0.0 collective-permute-start.1
  7.3 0.7 %copy-done.11 = s32[1,16,3]{1,0,2:T(1,128)S(1)} copy-done((s32[1,16,3]{1,0,2:T(1,128)S(1)}, s32[1,16,3]{1,0,2:T(1,128)}, u32[]{:S(2)}) %copy-start.11) | copy-done | bytes 216
  8.0 0.1 constant_dynamic-slice_fusion.3
  8.0 0.1 copy.11
  8.1 0.0 copy-done.2
  8.1 0.0 copy-done.3
  8.1 1.0 %copy-done.8 = bf16[1,256,512]{2,1,0:T(8,128)(2,1)S(1)} copy-done((bf16[1,256,512]{2,1,0:T(8,128)(2,1)S(1)}, bf16[1,256,512]{2,1,0:T(8,128)(2,1)}, u32[]{:S(2)}) %copy-start.8) | copy-done | bytes 262168
  9.1 3.0 %shard_map.102 = (f32[512,256]{1,0:T(8,128)S(1)}, f32[2,8,256]{2,1,0:T(8,128)S(1)}) custom-call(s32[2,3]{1,0:T(2,128)S(1)} %bitcast.26, bf16[256,512]{1,0:T(8,128)(2,1)S(1)} %bitcast.29, bf16[256,512]{1,0:T(8,128)(2,1)S(1)} %bitcast.21, bf16[256,512]{1,0:T(8,128)(2,1)S(1)} %bitcast.24), custom_call_target="tpu_custom_call" | custom-call | flops 500000000 | bytes 4194304 | tf_op jit(solution)/shard_map/pallas_call | solution.py:222
  12.1 0.0 copy-start.1
  12.1 0.0 copy-start.9
  12.1 1.4 %collective-permute-done = bf16[2,128,512]{2,1,0:T(8,128)(2,1)S(1)} collective-permute-done((bf16[2,128,512]{2,1,0:T(8,128)(2,1)}, bf16[2,128,512]{2,1,0:T(8,128)(2,1)S(1)}, u32[]{:S(2)}, u32[]{:S(2)}) %collective-permute-start) | collective-permute-done | bytes 262176 | tf_op jit(solution)/shard_map/ppermute | solution.py:269
  13.5 0.0 collective-permute-done.1
  13.6 0.0 copy-done.1
  13.6 0.0 copy-done.9
  13.6 2.6 %shard_map.103 = (bf16[512,256]{1,0:T(8,128)(2,1)S(1)}, bf16[4,64,1024]{2,1,0:T(8,128)(2,1)S(1)}, bf16[4,64,1024]{2,1,0:T(8,128)(2,1)}) custom-call(s32[2,3]{1,0:T(2,128)S(1)} %bitcast.27, bf16[256,512]{1,0:T(8,128)(2,1)S(1)} %bitcast.30, bf16[2,128,512]{2,1,0:T(8,128)(2,1)S(1)} %get-tuple-element.41.low, bf16[2,128,512]{2,1,0:T(8,128)(2,1)S(1)} %get-tuple-element.40.high, ...), custom_call_target="tpu_custom_call" | custom-call | flops 1000000000 | bytes 4194304 | tf_op jit(solution)/shard_map/pallas_call | solution.py:222
  16.2 0.1 collective-permute-start.2
  16.3 0.0 copy-done
  16.3 0.5 convolution_convert_fusion.1.ag
  16.8 1.6 %collective-permute-done.2 = bf16[4,64,1024]{2,1,0:T(8,128)(2,1)} collective-permute-done((bf16[4,64,1024]{2,1,0:T(8,128)(2,1)}, bf16[4,64,1024]{2,1,0:T(8,128)(2,1)}, u32[]{:S(2)}, u32[]{:S(2)}) %collective-permute-start.2) | collective-permute-done | bytes 524320 | tf_op jit(solution)/shard_map/ppermute | solution.py:294
  18.5 1.2 %add_convert_fusion = bf16[4,64,1024]{2,1,0:T(8,128)(2,1)S(1)} fusion(bf16[4,64,1024]{2,1,0:T(8,128)(2,1)} %collective-permute-done.2, bf16[4,64,1024]{2,1,0:T(8,128)(2,1)S(1)} %get-tuple-element.25), kind=kLoop, calls=%fused_computation.3 | loop fusion | flops 1048576 | bytes 1572864 | tf_op jit(solution)/shard_map/convert_element_type | solution.py:295
  19.7 0.0 copy-start.10
  19.7 0.1 constant_dynamic-slice_fusion.2
  19.8 2.6 %collective-permute-start.5 = (bf16[4,64,256]{2,1,0:T(8,128)(2,1)S(1)}, bf16[4,64,256]{2,1,0:T(8,128)(2,1)S(1)}, u32[]{:S(2)}, u32[]{:S(2)}) collective-permute-start(bf16[4,64,256]{2,1,0:T(8,128)(2,1)S(1)} %get-tuple-element.35), channel_id=1, source_target_pairs={{0,8},{8,0},{16,24},{24,16},{1,9},{9,1},{17,25},{25,17},{2,10},{10... | collective-permute-start | bytes 393224 | tf_op jit(solution)/shard_map/ppermute | solution.py:313
  22.4 1.5 %collective-permute-start.6 = (bf16[4,64,256]{2,1,0:T(8,128)(2,1)S(1)}, bf16[4,64,256]{2,1,0:T(8,128)(2,1)S(1)}, u32[]{:S(2)}, u32[]{:S(2)}) collective-permute-start(bf16[4,64,256]{2,1,0:T(8,128)(2,1)S(1)} %get-tuple-element.37), channel_id=1, source_target_pairs={{0,16},{8,24},{16,0},{24,8},{1,17},{9,25},{17,1},{25,9},{2,18},{10... | collective-permute-start | bytes 393224 | tf_op jit(solution)/shard_map/ppermute | solution.py:313
  23.9 0.0 collective-permute-start.7
  24.0 5.6 %shard_map.104 = (bf16[256,512]{1,0:T(8,128)(2,1)}, f32[256,512]{1,0:T(8,128)S(1)}, f32[256,512]{1,0:T(8,128)S(1)}, bf16[2,128,512]{2,1,0:T(8,128)(2,1)S(1)}, bf16[2,128,512]{2,1,0:T(8,128)(2,1)S(1)}) custom-call(s32[2,3]{1,0:T(2,128)S(1)} %bitcast.28, bf16[256,512]{1,0:T(8,128)(2,1)S(1)} %bitcast.31, bf16[256,512]{1,0:T(8,128)(2,1)S(1)} %bitcast.22, ...), custom_call_target="tpu_custom_call" | custom-call | flops 2000000000 | bytes 4194304 | tf_op jit(solution)/shard_map/pallas_call | solution.py:222
  29.5 0.7 %copy-done.4 = bf16[2,128,512]{2,1,0:T(8,128)(2,1)} copy-done((bf16[2,128,512]{2,1,0:T(8,128)(2,1)}, bf16[2,128,512]{2,1,0:T(8,128)(2,1)S(1)}, u32[]{:S(2)}) %copy-start.4) | copy-done | bytes 262168
  30.2 0.7 %copy-done.6 = bf16[2,128,512]{2,1,0:T(8,128)(2,1)} copy-done((bf16[2,128,512]{2,1,0:T(8,128)(2,1)}, bf16[2,128,512]{2,1,0:T(8,128)(2,1)S(1)}, u32[]{:S(2)}) %copy-start.6) | copy-done | bytes 262168
  30.9 0.0 collective-permute-done.5
  30.9 0.0 collective-permute-done.6
  30.9 0.0 collective-permute-done.7
  30.9 0.7 %add_convert_fusion.1 = bf16[4,64,256]{2,1,0:T(8,128)(2,1)} fusion(bf16[4,64,256]{2,1,0:T(8,128)(2,1)S(1)} %collective-permute-done.7, bf16[4,64,256]{2,1,0:T(8,128)(2,1)S(1)} %collective-permute-done.6, bf16[4,64,256]{2,1,0:T(8,128)(2,1)S(1)} %collective-permute-done.5, bf16[4,64,1024]{2,1,0:T(8,128)(2,1)S(1)} %add_convert_fusion, s32[]{:T(128)S(6)} %select_n.49), kind=kLoop, calls=%fused_computation.4 | loop fusion | flops 524288 | bytes 655364 | tf_op jit(solution)/shard_map/convert_element_type | solution.py:314
  31.7 3.9 %all-to-all-start = ((bf16[4,64,256]{2,1,0:T(8,128)(2,1)}), bf16[4,64,256]{2,1,0:T(8,128)(2,1)S(1)}, u32[]{:S(2)}, u32[]{:S(2)}) async-start(bf16[4,64,256]{2,1,0:T(8,128)(2,1)} %add_convert_fusion.1), calls=%async_computation | async-start | bytes 262144 | tf_op jit(solution)/shard_map/all_to_all | solution.py:320
  35.7 2.3 %collective-permute-start.3 = (bf16[2,128,512]{2,1,0:T(8,128)(2,1)S(1)}, bf16[2,128,512]{2,1,0:T(8,128)(2,1)S(1)}, u32[]{:S(2)}, u32[]{:S(2)}) collective-permute-start(bf16[2,128,512]{2,1,0:T(8,128)(2,1)S(1)} %get-tuple-element.39), channel_id=1, source_target_pairs={{0,7},{1,2},{2,1},{3,4},{4,3},{5,6},{6,5},{7,0},{8,15},{9,10},{10,... | collective-permute-start | bytes 786440 | tf_op jit(solution)/shard_map/ppermute | solution.py:316
  38.0 0.0 collective-permute-start.4
  38.0 5.7 %all-to-all-done = bf16[4,64,256]{2,1,0:T(8,128)(2,1)S(1)} async-done(((bf16[4,64,256]{2,1,0:T(8,128)(2,1)}), bf16[4,64,256]{2,1,0:T(8,128)(2,1)S(1)}, u32[]{:S(2)}, u32[]{:S(2)}) %all-to-all-start) | async-done | bytes 131104 | tf_op jit(solution)/shard_map/all_to_all | solution.py:320
  43.7 0.7 %broadcast_in_dim.23 = bf16[4,64,256]{2,1,0:T(8,128)(2,1)} broadcast(bf16[64,256]{1,0:T(8,128)(2,1)S(1)} %fusion.1), dimensions={1,2} | broadcast | bytes 163840 | tf_op jit(solution)/shard_map/broadcast_in_dim | solution.py:323
  44.3 4.1 %all-to-all-start.1 = ((bf16[4,64,256]{2,1,0:T(8,128)(2,1)}), bf16[4,64,256]{2,1,0:T(8,128)(2,1)S(1)}, u32[]{:S(2)}, u32[]{:S(2)}) async-start(bf16[4,64,256]{2,1,0:T(8,128)(2,1)} %broadcast_in_dim.23), calls=%async_computation.1 | async-start | bytes 262144 | tf_op jit(solution)/shard_map/all_to_all | solution.py:323
  48.4 1.3 %fusion = bf16[1,256,1024]{2,1,0:T(8,128)(2,1)} fusion(bf16[512,256]{1,0:T(8,128)(2,1)S(1)} %get-tuple-element.24, bf16[512,1024]{1,0:T(8,128)(2,1)S(1)} %copy-done), kind=kOutput, calls=%fused_computation.1 | convolution fusion | flops 268697600 | bytes 1835008 | tf_op jit(solution)/shard_map/dot_general | solution.py:24
  49.7 0.0 collective-permute-done.3.from_link
  49.7 0.0 collective-permute-done.4.from_chip
  49.7 3.8 %all-to-all-done.1.pieces = bf16[4,64,256]{2,1,0:T(8,128)(2,1)S(1)} async-done(((bf16[4,64,256]{2,1,0:T(8,128)(2,1)}), bf16[4,64,256]{2,1,0:T(8,128)(2,1)S(1)}, u32[]{:S(2)}, u32[]{:S(2)}) %all-to-all-start.1) | async-done | bytes 131104 | tf_op jit(solution)/shard_map/all_to_all | solution.py:323
  53.4 1.0 %shard_map.105 = (bf16[256,512]{1,0:T(8,128)(2,1)}, bf16[256,512]{1,0:T(8,128)(2,1)}, f32[64,1024]{1,0:T(8,128)}) custom-call(f32[256,512]{1,0:T(8,128)S(1)} %get-tuple-element.28.k_own, f32[256,512]{1,0:T(8,128)S(1)} %get-tuple-element.29.v_own, bf16[2,128,512]{2,1,0:T(8,128)(2,1)S(1)} %collective-permute-done.3.from_link, ...), custom_call_target="tpu_custom_call" | custom-call | flops 1000000 | bytes 4194304 | tf_op jit(solution)/shard_map/pallas_call | solution.py:222
  (13 shorter events, 0.1 us)
Async XLA Ops:
  0.6 15.7 %copy-start = (bf16[512,1024]{1,0:T(8,128)(2,1)S(1)}, bf16[512,1024]{1,0:T(8,128)(2,1)}, u32[]{:S(2)}) copy-start(bf16[512,1024]{1,0:T(8,128)(2,1)} %param.10) | copy-start | bytes 3145732
  0.6 7.5 %copy-start.2 = (bf16[1,256,512]{2,1,0:T(8,128)(2,1)S(1)}, bf16[1,256,512]{2,1,0:T(8,128)(2,1)}, u32[]{:S(2)}) copy-start(bf16[1,256,512]{2,1,0:T(8,128)(2,1)} %param.7) | copy-start | bytes 786436
  0.7 7.5 %copy-start.3 = (bf16[1,256,512]{2,1,0:T(8,128)(2,1)S(1)}, bf16[1,256,512]{2,1,0:T(8,128)(2,1)}, u32[]{:S(2)}) copy-start(bf16[1,256,512]{2,1,0:T(8,128)(2,1)} %param.8) | copy-start | bytes 786436
  2.7 10.8 %collective-permute-start = (bf16[2,128,512]{2,1,0:T(8,128)(2,1)}, bf16[2,128,512]{2,1,0:T(8,128)(2,1)S(1)}, u32[]{:S(2)}, u32[]{:S(2)}) collective-permute-start(bf16[2,128,512]{2,1,0:T(8,128)(2,1)} %get-tuple-element.20), channel_id=1, source_target_pairs={{0,7},{1,2},{2,1},{3,4},{4,3},{5,6},{6,5},{7,0},{8,15},{9,10},{10,... | collective-permute-start | bytes 786440 | tf_op jit(solution)/shard_map/ppermute | solution.py:269
  7.3 6.2 %collective-permute-start.1 = (bf16[2,128,512]{2,1,0:T(8,128)(2,1)}, bf16[2,128,512]{2,1,0:T(8,128)(2,1)S(1)}, u32[]{:S(2)}, u32[]{:S(2)}) collective-permute-start(bf16[2,128,512]{2,1,0:T(8,128)(2,1)} %get-tuple-element.21), channel_id=1, source_target_pairs={{0,1},{1,0},{2,3},{3,2},{4,5},{5,4},{6,7},{7,6},{8,9},{9,8},{10,11... | collective-permute-start | bytes 786440 | tf_op jit(solution)/shard_map/ppermute | solution.py:270
  7.3 0.7 %copy-start.11 = (s32[1,16,3]{1,0,2:T(1,128)S(1)}, s32[1,16,3]{1,0,2:T(1,128)}, u32[]{:S(2)}) copy-start(s32[1,16,3]{1,0,2:T(1,128)} %param.11) | copy-start | bytes 580
  8.1 1.0 %copy-start.8 = (bf16[1,256,512]{2,1,0:T(8,128)(2,1)S(1)}, bf16[1,256,512]{2,1,0:T(8,128)(2,1)}, u32[]{:S(2)}) copy-start(bf16[1,256,512]{2,1,0:T(8,128)(2,1)} %param.6) | copy-start | bytes 786436
  12.1 1.5 %copy-start.1 = (bf16[1,256,1024]{2,1,0:T(8,128)(2,1)S(1)}, bf16[1,256,1024]{2,1,0:T(8,128)(2,1)}, u32[]{:S(2)}) copy-start(bf16[1,256,1024]{2,1,0:T(8,128)(2,1)} %param.9) | copy-start | bytes 1572868
  12.1 1.5 %copy-start.9 = (bf16[1,256,512]{2,1,0:T(8,128)(2,1)S(1)}, bf16[1,256,512]{2,1,0:T(8,128)(2,1)}, u32[]{:S(2)}) copy-start(bf16[1,256,512]{2,1,0:T(8,128)(2,1)} %param.6) | copy-start | bytes 786436
  16.2 2.3 %collective-permute-start.2 = (bf16[4,64,1024]{2,1,0:T(8,128)(2,1)}, bf16[4,64,1024]{2,1,0:T(8,128)(2,1)}, u32[]{:S(2)}, u32[]{:S(2)}) collective-permute-start(bf16[4,64,1024]{2,1,0:T(8,128)(2,1)} %get-tuple-element.26), channel_id=1, source_target_pairs={{0,1},{1,0},{2,3},{3,2},{4,5},{5,4},{6,7},{7,6},{8,9},{9,8},{10,11... | collective-permute-start | bytes 1572872 | tf_op jit(solution)/shard_map/ppermute | solution.py:294
  19.7 4.2 %copy-start.10 = (bf16[1,256,512]{2,1,0:T(8,128)(2,1)S(1)}, bf16[1,256,512]{2,1,0:T(8,128)(2,1)}, u32[]{:S(2)}) copy-start(bf16[1,256,512]{2,1,0:T(8,128)(2,1)} %param.6) | copy-start | bytes 786436
  19.8 11.1 %collective-permute-start.5 = (bf16[4,64,256]{2,1,0:T(8,128)(2,1)S(1)}, bf16[4,64,256]{2,1,0:T(8,128)(2,1)S(1)}, u32[]{:S(2)}, u32[]{:S(2)}) collective-permute-start(bf16[4,64,256]{2,1,0:T(8,128)(2,1)S(1)} %get-tuple-element.35), channel_id=1, source_target_pairs={{0,8},{8,0},{16,24},{24,16},{1,9},{9,1},{17,25},{25,17},{2,10},{10... | collective-permute-start | bytes 393224 | tf_op jit(solution)/shard_map/ppermute | solution.py:313
  22.4 8.5 %collective-permute-start.6 = (bf16[4,64,256]{2,1,0:T(8,128)(2,1)S(1)}, bf16[4,64,256]{2,1,0:T(8,128)(2,1)S(1)}, u32[]{:S(2)}, u32[]{:S(2)}) collective-permute-start(bf16[4,64,256]{2,1,0:T(8,128)(2,1)S(1)} %get-tuple-element.37), channel_id=1, source_target_pairs={{0,16},{8,24},{16,0},{24,8},{1,17},{9,25},{17,1},{25,9},{2,18},{10... | collective-permute-start | bytes 393224 | tf_op jit(solution)/shard_map/ppermute | solution.py:313
  23.9 7.0 %collective-permute-start.7 = (bf16[4,64,256]{2,1,0:T(8,128)(2,1)S(1)}, bf16[4,64,256]{2,1,0:T(8,128)(2,1)S(1)}, u32[]{:S(2)}, u32[]{:S(2)}) collective-permute-start(bf16[4,64,256]{2,1,0:T(8,128)(2,1)S(1)} %get-tuple-element.36), channel_id=1, source_target_pairs={{0,24},{8,16},{16,8},{24,0},{1,25},{9,17},{17,9},{25,1},{2,26},{10... | collective-permute-start | bytes 393224 | tf_op jit(solution)/shard_map/ppermute | solution.py:313
  29.5 0.7 %copy-start.4 = (bf16[2,128,512]{2,1,0:T(8,128)(2,1)}, bf16[2,128,512]{2,1,0:T(8,128)(2,1)S(1)}, u32[]{:S(2)}) copy-start(bf16[2,128,512]{2,1,0:T(8,128)(2,1)S(1)} %get-tuple-element.30) | copy-start | bytes 786436
  30.2 0.7 %copy-start.6 = (bf16[2,128,512]{2,1,0:T(8,128)(2,1)}, bf16[2,128,512]{2,1,0:T(8,128)(2,1)S(1)}, u32[]{:S(2)}) copy-start(bf16[2,128,512]{2,1,0:T(8,128)(2,1)S(1)} %get-tuple-element.31) | copy-start | bytes 786436
  30.9 4.7 %copy-start.7 = (bf16[2,128,512]{2,1,0:T(8,128)(2,1)S(1)}, bf16[2,128,512]{2,1,0:T(8,128)(2,1)}, u32[]{:S(2)}) copy-start(bf16[2,128,512]{2,1,0:T(8,128)(2,1)} %copy-done.6) | copy-start | bytes 786436
  31.7 3.9 %copy-start.5 = (bf16[2,128,512]{2,1,0:T(8,128)(2,1)S(1)}, bf16[2,128,512]{2,1,0:T(8,128)(2,1)}, u32[]{:S(2)}) copy-start(bf16[2,128,512]{2,1,0:T(8,128)(2,1)} %copy-done.4) | copy-start | bytes 786436
  31.7 11.9 %all-to-all-start = ((bf16[4,64,256]{2,1,0:T(8,128)(2,1)}), bf16[4,64,256]{2,1,0:T(8,128)(2,1)S(1)}, u32[]{:S(2)}, u32[]{:S(2)}) async-start(bf16[4,64,256]{2,1,0:T(8,128)(2,1)} %add_convert_fusion.1), calls=%async_computation | async-start | bytes 262144 | tf_op jit(solution)/shard_map/all_to_all | solution.py:320
  35.7 14.0 %collective-permute-start.3 = (bf16[2,128,512]{2,1,0:T(8,128)(2,1)S(1)}, bf16[2,128,512]{2,1,0:T(8,128)(2,1)S(1)}, u32[]{:S(2)}, u32[]{:S(2)}) collective-permute-start(bf16[2,128,512]{2,1,0:T(8,128)(2,1)S(1)} %get-tuple-element.39), channel_id=1, source_target_pairs={{0,7},{1,2},{2,1},{3,4},{4,3},{5,6},{6,5},{7,0},{8,15},{9,10},{10,... | collective-permute-start | bytes 786440 | tf_op jit(solution)/shard_map/ppermute | solution.py:316
  38.0 11.7 %collective-permute-start.4 = (bf16[2,128,512]{2,1,0:T(8,128)(2,1)S(1)}, bf16[2,128,512]{2,1,0:T(8,128)(2,1)S(1)}, u32[]{:S(2)}, u32[]{:S(2)}) collective-permute-start(bf16[2,128,512]{2,1,0:T(8,128)(2,1)S(1)} %get-tuple-element.38), channel_id=1, source_target_pairs={{0,1},{1,0},{2,3},{3,2},{4,5},{5,4},{6,7},{7,6},{8,9},{9,8},{10,11... | collective-permute-start | bytes 786440 | tf_op jit(solution)/shard_map/ppermute | solution.py:317
  44.3 9.1 %all-to-all-start.1 = ((bf16[4,64,256]{2,1,0:T(8,128)(2,1)}), bf16[4,64,256]{2,1,0:T(8,128)(2,1)S(1)}, u32[]{:S(2)}, u32[]{:S(2)}) async-start(bf16[4,64,256]{2,1,0:T(8,128)(2,1)} %broadcast_in_dim.23), calls=%async_computation.1 | async-start | bytes 262144 | tf_op jit(solution)/shard_map/all_to_all | solution.py:323

commit v4 on v1

v4 whole, which is shorter than its diff:
```python
import functools

import jax
import jax.numpy as jnp
from jax import lax
from jax.experimental import pallas as pl
from jax.experimental.pallas import tpu as pltpu
from jax.sharding import PartitionSpec as P

HEADS = 8
HD = 64
BLK = 128
RAD = 1
CAND = 2 * RAD + 1
PAIRS = HEADS // 2
PAIR = 2 * HD
RIM = RAD * BLK
BIG_NEGATIVE = -1e30
SCALE = HD ** (-0.5)
BF16 = jnp.bfloat16
F32 = jnp.float32


def dot(a, b, contract):
    return lax.dot_general(a, b, (contract, ((), ())), preferred_element_type=F32)


def two_heads(block, axis):
    feature = lax.broadcasted_iota(jnp.int32, block.shape, axis)
    zero = jnp.zeros_like(block)
    return jnp.concatenate(
        [jnp.where(feature < HD, block, zero), jnp.where(feature < HD, zero, block)], axis=1 - axis
    )


def own_features(both):
    return jnp.concatenate([both[:HD, :BLK], both[HD:, BLK:]], axis=0)


def spread(row):
    return jnp.concatenate(
        [
            jnp.broadcast_to(row[:, :BLK], (HD, BLK)),
            jnp.broadcast_to(row[:, BLK:], (HD, BLK)),
        ],
        axis=0,
    )


def own_candidates(b, blocks):
    return max(0, RAD - b), min(CAND - 1, blocks - 1 - b + RAD)


def own_rows(b, blocks):
    first, last = own_candidates(b, blocks)
    return slice((b + first - RAD) * BLK, (b + last - RAD + 1) * BLK)


def rim_candidates(b, blocks):
    first, last = own_candidates(b, blocks)
    return [(0, c) for c in range(first)] + [(1, c) for c in range(last + 1, CAND)]


def masked(mask, b, c, part):
    return part if c == RAD else jnp.where(mask[b, c] == 1, part, BIG_NEGATIVE)


def pairs_of(blocks):
    for b in range(blocks):
        for p in range(PAIRS):
            yield b, slice(b * BLK, (b + 1) * BLK), slice(p * PAIR, (p + 1) * PAIR), b * PAIRS + p


def at_core():
    return lax.rem(lax.axis_index("ctx"), 2)


def own_kernel(mask, q, k, v, g, w_out, own_t, stats, exps, grad_t):
    blocks = q.shape[0] // BLK
    for b, rows, cols, at in pairs_of(blocks):
        first, last = own_candidates(b, blocks)
        here = own_rows(b, blocks)
        scores = dot(k[here, cols], two_heads(q[rows, cols] * SCALE, 1), ((1,), (1,)))
        scores = jnp.concatenate(
            [
                masked(mask, b, c, scores[(c - first) * BLK : (c - first + 1) * BLK])
                for c in range(first, last + 1)
            ],
            axis=0,
        )
        top = jnp.max(scores, axis=0, keepdims=True)
        e = jnp.exp(scores - top)
        exps[at, : e.shape[0]] = e
        stats[0, at : at + 1] = top
        stats[1, at : at + 1] = jnp.sum(e, axis=0, keepdims=True)
        own_t[cols, rows] = own_features(dot(v[here, cols], e.astype(BF16), ((0,), (0,))))
    grad_t[...] = dot(w_out[...], g[...], ((1,), (1,))).astype(BF16)


def forward_kernel(mask, q, low, high, own_t, stats, g, attn_t, mine, other, exps, factors):
    blocks = q.shape[0] // BLK
    sides = (low, high)
    for b, rows, cols, at in pairs_of(blocks):
        rims = rim_candidates(b, blocks)
        old = stats[0, at : at + 1]
        q2 = two_heads(q[rows, cols] * SCALE, 1)
        scores = [masked(mask, b, c, dot(sides[s][0, :, cols], q2, ((1,), (1,)))) for s, c in rims]
        top = old
        for part in scores:
            top = jnp.maximum(top, jnp.max(part, axis=0, keepdims=True))
        kept = jnp.exp(old - top)
        count = stats[1, at : at + 1] * kept
        both = None
        for (s, _), part in zip(rims, scores):
            e = jnp.exp(part - top)
            exps[s, at % PAIRS] = e
            count = count + jnp.sum(e, axis=0, keepdims=True)
            more = dot(sides[s][1, :, cols], e.astype(BF16), ((0,), (0,)))
            both = more if both is None else both + more
        share = 1.0 / count
        factors[0, at : at + 1] = kept * share
        factors[1, at : at + 1] = share
        attn = own_t[cols, rows] * spread(kept * share)
        if both is not None:
            attn = attn + own_features(both) * spread(share)
        attn_t[cols, rows] = attn.astype(BF16)
    part = dot(attn_t[...], g[...], ((1,), (0,))).astype(BF16)
    core = at_core()
    chips, rows, _ = mine.shape
    for c in range(2 * chips):
        value = part[c * rows : (c + 1) * rows]

        @pl.when(core == c % 2)
        def _():
            mine[c // 2] = value

        @pl.when(core != c % 2)
        def _():
            other[c // 2] = value


def backward(probs, delta, k, v, q2, g2_t):
    dprob = dot(v, g2_t, ((1,), (0,)))
    dscore = (probs * (dprob - delta)).astype(BF16)
    query_t = own_features(dot(k, dscore, ((0,), (0,)))) * SCALE
    return query_t, dot(dscore, q2, ((1,), (0,))), dot(probs.astype(BF16), g2_t, ((1,), (1,)))


def rim_kernel(q, low, high, grad_t, attn_t, exps, factors, to_link, to_chip, deltas, query_t):
    blocks = q.shape[0] // BLK
    first_core = at_core() == 0
    parts = {}
    for b, rows, cols, at in pairs_of(blocks):
        product = grad_t[cols, rows].astype(F32) * attn_t[cols, rows].astype(F32)
        delta = jnp.concatenate(
            [
                jnp.sum(product[:HD], axis=0, keepdims=True),
                jnp.sum(product[HD:], axis=0, keepdims=True),
            ],
            axis=1,
        )
        deltas[at : at + 1] = delta
        q2 = two_heads(q[rows, cols] * SCALE, 1)
        g2_t = two_heads(grad_t[cols, rows], 0)
        total_t = jnp.zeros((PAIR, BLK), F32)
        for s, _ in rim_candidates(b, blocks):
            rim = (low, high)[s]
            probs = exps[s, at % PAIRS] * factors[1, at : at + 1]
            part_t, k_part, v_part = backward(
                probs, delta, rim[0, :, cols], rim[1, :, cols], q2, g2_t
            )
            total_t = total_t + part_t
            parts[s, at % PAIRS] = (k_part.astype(BF16), v_part.astype(BF16))
            if len(parts) > PAIRS and (1 - s, at % PAIRS) in parts:
                for which in range(2):
                    below = parts[0, at % PAIRS][which]
                    above = parts[1, at % PAIRS][which]
                    to_link[which, :, cols] = jnp.where(first_core, below, above)
                    to_chip[which, :, cols] = jnp.where(first_core, above, below)
        query_t[cols, rows] = total_t


def own_backward_kernel(
    q, k, v, grad_t, attn_t, exps, factors, deltas, rim_t, w_out, before,
    q_grad, k_own, v_own, output, after,
):
    blocks = q.shape[0] // BLK
    k_own[...] = jnp.zeros_like(k_own)
    v_own[...] = jnp.zeros_like(v_own)
    for b, rows, cols, at in pairs_of(blocks):
        here = own_rows(b, blocks)
        probs = exps[at, : here.stop - here.start] * factors[0, at : at + 1]
        q2 = two_heads(q[rows, cols] * SCALE, 1)
        g2_t = two_heads(grad_t[cols, rows], 0)
        part_t, k_part, v_part = backward(
            probs, deltas[at : at + 1], k[here, cols], v[here, cols], q2, g2_t
        )
        q_grad[rows, cols] = (part_t + rim_t[cols, rows]).T.astype(BF16)
        k_own[here, cols] += k_part
        v_own[here, cols] += v_part
    output[...] = dot(attn_t[...], w_out[...], ((0,), (0,))).astype(BF16)
    after[...] = jnp.zeros_like(after)


def halves_kernel(mine, other, before, *outs):
    pieces, after = outs[:-1], outs[-1]
    at_dp = lax.axis_index("dp")
    cols = pieces[0].shape[2]
    for d in range(len(pieces)):
        at = slice(d * cols, (d + 1) * cols)
        value = (mine[:, :, at].astype(F32) + other[:, :, at].astype(F32)).astype(BF16)
        for s in range(len(pieces)):

            @pl.when((at_dp ^ s) == d)
            def _(s=s, value=value):
                pieces[s][...] = value

    after[...] = jnp.zeros_like(after)


def chips_kernel(*refs):
    parts, outs = refs[: lax.axis_size("dp")], refs[lax.axis_size("dp") + 3 :]
    chip = lax.div(lax.axis_index("ctx"), 2)
    for s, out in enumerate(outs):
        out[...] = total([part[chip ^ s] for part in parts]).astype(BF16)


def rim_sum_kernel(k_own, v_own, from_link, from_chip, before, k_grad, v_grad):
    tokens = k_own.shape[0]
    first_core = at_core() == 0
    for which, (own, grad) in enumerate(((k_own, k_grad), (v_own, v_grad))):
        link = from_link[which].astype(F32)
        chip = from_chip[which].astype(F32)
        low = jnp.where(first_core, link, chip)
        high = jnp.where(first_core, chip, link)
        if tokens == RIM:
            grad[...] = (own[...] + low + high).astype(BF16)
        else:
            grad[:RIM] = (own[:RIM] + low).astype(BF16)
            if tokens > 2 * RIM:
                grad[RIM : tokens - RIM] = own[RIM : tokens - RIM].astype(BF16)
            grad[tokens - RIM :] = (own[tokens - RIM :] + high).astype(BF16)


def columns_kernel(*refs):
    pieces, out = refs[:-1], refs[-1]
    at_dp = lax.axis_index("dp")
    cols = pieces[0].shape[1]
    for d in range(len(pieces)):
        value = pieces[0][...]
        for s in range(1, len(pieces)):
            value = jnp.where((at_dp ^ s) == d, pieces[s][...], value)
        out[:, d * cols : (d + 1) * cols] = value.astype(F32)


def vmem(*shape, dtype=BF16):
    return pltpu.VMEM(shape, dtype)


def hbm(*shape, dtype=BF16):
    return jax.ShapeDtypeStruct(shape, dtype)


def call(kernel, outs, flops, *args, mask=None):
    in_vmem = pl.BlockSpec(memory_space=pltpu.VMEM)
    in_smem = pl.BlockSpec(memory_space=pltpu.SMEM)
    masks = () if mask is None else (mask,)
    return pl.pallas_call(
        kernel,
        out_shape=outs,
        in_specs=[in_smem] * len(masks) + [in_vmem] * len(args),
        out_specs=[in_vmem] * len(outs),
        compiler_params=pltpu.CompilerParams(vmem_limit_bytes=24 * 1024 * 1024),
        cost_estimate=pl.CostEstimate(flops=flops, bytes_accessed=4 << 20, transcendentals=0),
    )(*masks, *args)


def swap(count, bits):
    return [(i, i ^ bits) for i in range(count)]


def over_links(count):
    return [(i, (i - 1 if i % 2 == 0 else i + 1) % count) for i in range(count)]


def total(parts):
    return functools.reduce(jnp.add, [p.astype(F32) for p in parts])


def body(queries, keys, values, out_grad, w_out, block_mask):
    q, k, v, g = queries[0], keys[0], values[0], out_grad[0]
    tokens, feats = q.shape
    width = g.shape[1]
    blocks = tokens // BLK
    ctx, dp = lax.axis_size("ctx"), lax.axis_size("dp")
    chips = ctx // 2
    at_ctx = lax.axis_index("ctx")
    core = at_ctx % 2
    rows, cols = feats // ctx, width // dp
    groups = blocks * PAIRS

    link_row = core * (tokens - RIM)
    chip_row = tokens - RIM - link_row

    def rim(row):
        return jnp.stack([lax.dynamic_slice_in_dim(x, row, RIM, 0) for x in (k, v)])

    from_link = lax.ppermute(rim(link_row), "ctx", over_links(ctx))
    from_chip = lax.ppermute(rim(chip_row), "ctx", swap(ctx, 1))
    low = jnp.where(core == 0, from_link, from_chip)
    high = jnp.where(core == 0, from_chip, from_link)

    mask = lax.dynamic_slice_in_dim(block_mask[0], at_ctx * blocks, blocks, 0)
    own_t, stats, own_exps, grad_t = call(
        own_kernel,
        [
            vmem(feats, tokens, dtype=F32),
            vmem(2, groups, 2 * BLK, dtype=F32),
            vmem(groups, min(CAND, blocks) * BLK, 2 * BLK, dtype=F32),
            vmem(feats, tokens),
        ],
        10**9,
        q, k, v, g, w_out,
        mask=mask,
    )
    attn_t, mine, other, rim_exps, factors = call(
        forward_kernel,
        [
            vmem(feats, tokens),
            vmem(chips, rows, width),
            vmem(chips, rows, width),
            vmem(2, PAIRS, RIM, 2 * BLK, dtype=F32),
            vmem(2, groups, 2 * BLK, dtype=F32),
        ],
        10**9,
        q, low, high, own_t, stats, g,
        mask=mask,
    )

    other = lax.ppermute(other, "ctx", swap(ctx, 1))
    other = pltpu.with_memory_space_constraint(other, pltpu.VMEM)
    to_link, to_chip, deltas, rim_t = call(
        rim_kernel,
        [
            vmem(2, RIM, feats),
            vmem(2, RIM, feats),
            vmem(groups, 2 * BLK, dtype=F32),
            vmem(feats, tokens, dtype=F32),
        ],
        10**9,
        q, low, high, grad_t, attn_t, rim_exps, factors,
    )
    *halves, after = call(
        halves_kernel,
        [vmem(chips, rows, cols)] * dp + [vmem(8, 128, dtype=F32)],
        10**6,
        mine, other, deltas,
    )
    grad_link = lax.ppermute(to_link, "ctx", over_links(ctx))
    grad_chip = lax.ppermute(to_chip, "ctx", swap(ctx, 1))

    q_grad, k_own, v_own, output, after = call(
        own_backward_kernel,
        [
            hbm(tokens, feats),
            vmem(tokens, feats, dtype=F32),
            vmem(tokens, feats, dtype=F32),
            hbm(tokens, width),
            vmem(8, 128, dtype=F32),
        ],
        2 * 10**9,
        q, k, v, grad_t, attn_t, own_exps, factors, deltas, rim_t, w_out, after,
    )

    halves = [halves[0]] + [lax.ppermute(halves[s], "dp", swap(dp, s)) for s in range(1, dp)]
    quarters = call(chips_kernel, [vmem(rows, cols)] * chips, 10**6, *halves, after, grad_link, grad_chip)
    k_grad, v_grad = call(
        rim_sum_kernel,
        [hbm(tokens, feats), hbm(tokens, feats)],
        10**6,
        k_own, v_own, grad_link, grad_chip, quarters[0],
    )
    piece = total(
        [quarters[0]]
        + [lax.ppermute(quarters[s], "ctx", swap(ctx, 2 * s)) for s in range(1, chips)]
    )
    piece = (piece * (dp * tokens * ctx) ** (-0.5)).astype(BF16)
    pieces = [piece] + [lax.ppermute(piece, "dp", swap(dp, s)) for s in range(1, dp)]
    (weight_grad,) = call(columns_kernel, [hbm(rows, width, dtype=F32)], 10**6, *pieces)
    return (output[None], q_grad[None], k_grad[None], v_grad[None], weight_grad)


def solution(mesh):
    rows = P("dp", "ctx", None)
    return jax.shard_map(
        body,
        mesh=mesh,
        in_specs=(rows, rows, rows, rows, P(), P("dp", None, None)),
        out_specs=(rows, rows, rows, rows, P("ctx", None)),
        check_vma=False,
    )
```

time: 58.9 us -> 45 us (0.76)
  waiting for transfers between devices: 20.1 us -> 9.69 us
  other arithmetic: 2.9 us -> 0.11 us
  Pallas kernels: 9.96 us -> 12.2 us
  matrix products: 1.74 us -> 0 us
  local copies, waits for them, and re-layouts: 3.34 us -> 2.42 us
    ppermute x10, waiting for transfers between devices: 18.5 us -> 7.46 us  [the longest x3 3.15 us: body(): lax.ppermute(quarters[s], 'ctx', swap(ctx, 2 * s))]
    pallas_call x2 -> x8, Pallas kernels: 9.96 us -> 12.2 us  [call(): pl.pallas_call(kernel, out_shape=outs, in_specs=[in_smem] * len(masks) +...]
    dot_general x2 -> x0, matrix products: 1.74 us -> none  [dot(): lax.dot_general(a, b, (contract, ((), ())), preferred_element_type=F32)]
    broadcast_in_dim x2 -> x0, other arithmetic: 1.47 us -> none  [the longest x1 0.73 us: body(): grads[1][None]]
    slice x1 -> x0, local copies, waits for them, and re-layouts: 1.22 us -> none  [body(): high = lax.ppermute(jnp.stack([k[:RIM], v[:RIM]]), 'ctx', ring(ctx, -1))]
    dynamic_slice x1, local copies, waits for them, and re-layouts: 0.06 us -> 1.27 us  [rim(): return jnp.stack([lax.dynamic_slice_in_dim(x, row, RIM, 0) for x in (k, v)])]
    gather x2 -> x0, local copies, waits for them, and re-layouts: 1.11 us -> none  [body(): turned = pieces[jnp.arange(dp) ^ step]]
    convert_element_type x3 -> x0, other arithmetic: 1.01 us -> none  [the longest x1 0.72 us: body(): jnp.concatenate([pieces[d] for d in range(dp)], axis=1).astype(F32)]
  transfers between devices with their start and end apart: 14 -> 14, of which waited for: 10 -> 7; matrix products, arithmetic and copies ran while one was open for 7% -> 0% of each run, Pallas kernels for 9% -> 21%
where the time goes in v4:
time: 45 us; the launch traced here: 44.8 us
  starting transfers between devices  19.5 us (43%)
  Pallas kernels  12.2 us (27%)
  waiting for transfers between devices  9.69 us (22%)
  local copies, waits for them, and re-layouts  2.42 us (5%)
  between operations  0.82 us (2%)
    pallas_call x8, Pallas kernels, call(): pl.pallas_call(kernel, out_shape=outs, in_specs=[in_smem] * len(masks) +...  12.2 us
    ppermute x1, starting transfers between devices, body(): from_link = lax.ppermute(rim(link_row), 'ctx', over_links(ctx))  4.55 us
    ppermute x3, starting transfers between devices, body(): lax.ppermute(quarters[s], 'ctx', swap(ctx, 2 * s))  4.44 us
    ppermute x3, starting transfers between devices, body(): lax.ppermute(piece, 'dp', swap(dp, s))  3.55 us
    ppermute x3, starting transfers between devices, body(): lax.ppermute(halves[s], 'dp', swap(dp, s))  3.55 us
    ppermute x1, starting transfers between devices, body(): grad_link = lax.ppermute(to_link, 'ctx', over_links(ctx))  3.3 us
    ppermute x3, waiting for transfers between devices, body(): lax.ppermute(quarters[s], 'ctx', swap(ctx, 2 * s))  3.15 us
    ppermute x3, waiting for transfers between devices, body(): lax.ppermute(halves[s], 'dp', swap(dp, s))  2.88 us
  transfers between devices with their start and end apart: 14, of which 7 were waited for; matrix products, arithmetic and copies ran while one was open for 0% of the time, Pallas kernels for 21%

profile of v4, /device:TPU:0, one launch (start us, length us, event | category | flops | bytes accessed | tf_op | source)
XLA Modules:
  0.0 44.8 jit_solution(7361897131734439418)
XLA Ops:
  0.6 0.0 copy-start
  0.6 0.0 copy-start.2
  0.7 0.0 copy-start.1
  0.7 0.0 copy-start.3
  0.7 0.0 copy-start.4
  0.7 1.3 %constant_dynamic-slice_fusion = (bf16[1,128,512]{2,1,0:T(8,128)(2,1)S(1)}, bf16[1,128,512]{2,1,0:T(8,128)(2,1)S(1)}, bf16[1,128,512]{2,1,0:T(8,128)(2,1)S(1)}, bf16[1,128,512]{2,1,0:T(8,128)(2,1)S(1)}) fusion(bf16[1,256,512]{2,1,0:T(8,128)(2,1)} %param.8, s32[]{:T(128)S(6)} %select_n.34, s32[]{:T(128)S(6)} %select_n.33, bf16[1,256,512]{2,1,0:T(8,128)(2,1)} %param.7), kind=kLoop, calls=%fused_computation.5 | loop fusion | bytes 1048584 | tf_op jit(solution)/shard_map/dynamic_slice | solution.py:306
  2.0 4.6 %collective-permute-start = (bf16[2,128,512]{2,1,0:T(8,128)(2,1)S(1)}, bf16[2,128,512]{2,1,0:T(8,128)(2,1)S(1)}, u32[]{:S(2)}, u32[]{:S(2)}) collective-permute-start(bf16[2,128,512]{2,1,0:T(8,128)(2,1)S(1)} %pad_maximum_fusion), channel_id=1, source_target_pairs={{0,7},{1,2},{2,1},{3,4},{4,3},{5,6},{6,5},{7,0},{8,15},{9,10},{10,... | collective-permute-start | bytes 786440 | tf_op jit(solution)/shard_map/ppermute | solution.py:308
  6.6 0.1 collective-permute-start.1
  6.7 0.0 copy-done
  6.7 0.1 constant_dynamic-slice_fusion.4
  6.8 0.1 copy.11
  6.9 0.0 copy-done.1
  6.9 0.0 copy-start.5
  6.9 0.9 %copy-done.5 = bf16[1,256,512]{2,1,0:T(8,128)(2,1)S(1)} copy-done((bf16[1,256,512]{2,1,0:T(8,128)(2,1)S(1)}, bf16[1,256,512]{2,1,0:T(8,128)(2,1)}, u32[]{:S(2)}) %copy-start.5) | copy-done | bytes 262168
  7.8 3.3 %shard_map.101 = (f32[512,256]{1,0:T(8,128)S(1)}, f32[2,8,256]{2,1,0:T(8,128)S(1)}, f32[8,256,256]{2,1,0:T(8,128)S(1)}, bf16[512,256]{1,0:T(8,128)(2,1)S(1)}) custom-call(s32[2,3]{1,0:T(2,128)S(1)} %bitcast.13, bf16[256,512]{1,0:T(8,128)(2,1)S(1)} %bitcast.17, bf16[256,512]{1,0:T(8,128)(2,1)S(1)} %bitcast.9, bf16[256,512]{1,0:T(8,128)(2,1)S(1)} %bitcast.11, ...), custom_call_target="tpu_custom_call" | custom-call | flops 1000000000 | bytes 4194304 | tf_op jit(solution)/shard_map/pallas_call | solution.py:268
  11.2 1.4 %collective-permute-done = bf16[2,128,512]{2,1,0:T(8,128)(2,1)S(1)} collective-permute-done((bf16[2,128,512]{2,1,0:T(8,128)(2,1)S(1)}, bf16[2,128,512]{2,1,0:T(8,128)(2,1)S(1)}, u32[]{:S(2)}, u32[]{:S(2)}) %collective-permute-start) | collective-permute-done | bytes 262176 | tf_op jit(solution)/shard_map/ppermute | solution.py:308
  12.6 0.0 collective-permute-done.1
  12.7 1.9 %shard_map.102 = (bf16[512,256]{1,0:T(8,128)(2,1)S(1)}, bf16[4,64,1024]{2,1,0:T(8,128)(2,1)S(1)}, bf16[4,64,1024]{2,1,0:T(8,128)(2,1)S(1)}, f32[2,4,128,256]{3,2,1,0:T(8,128)S(1)}, f32[2,8,256]{2,1,0:T(8,128)S(1)}) custom-call(s32[2,3]{1,0:T(2,128)S(1)} %bitcast.14, bf16[256,512]{1,0:T(8,128)(2,1)S(1)} %bitcast.18, ...), custom_call_target="tpu_custom_call" | custom-call | flops 1000000000 | bytes 4194304 | tf_op jit(solution)/shard_map/pallas_call | solution.py:268
  14.5 0.1 collective-permute-start.2
  14.6 1.5 %shard_map.103 = (bf16[2,128,512]{2,1,0:T(8,128)(2,1)S(1)}, bf16[2,128,512]{2,1,0:T(8,128)(2,1)S(1)}, f32[8,256]{1,0:T(8,128)S(1)}, f32[512,256]{1,0:T(8,128)S(1)}) custom-call(bf16[256,512]{1,0:T(8,128)(2,1)S(1)} %bitcast.19, bf16[2,128,512]{2,1,0:T(8,128)(2,1)S(1)} %get-tuple-element.64.low, bf16[2,128,512]{2,1,0:T(8,128)(2,1)S(1)} %get-tuple-element.63.high, ...), custom_call_target="tpu_custom_call" | custom-call | flops 1000000000 | bytes 4194304 | tf_op jit(solution)/shard_map/pallas_call | solution.py:268
  16.1 3.3 %collective-permute-start.3 = (bf16[2,128,512]{2,1,0:T(8,128)(2,1)S(1)}, bf16[2,128,512]{2,1,0:T(8,128)(2,1)S(1)}, u32[]{:S(2)}, u32[]{:S(2)}) collective-permute-start(bf16[2,128,512]{2,1,0:T(8,128)(2,1)S(1)} %get-tuple-element.50), channel_id=1, source_target_pairs={{0,7},{1,2},{2,1},{3,4},{4,3},{5,6},{6,5},{7,0},{8,15},{9,10},{10,... | collective-permute-start | bytes 786440 | tf_op jit(solution)/shard_map/ppermute | solution.py:359
  19.4 0.0 collective-permute-start.4
  19.4 0.0 collective-permute-done.2.other
  19.4 0.3 shard_map.104
  19.7 1.6 %collective-permute-start.5 = (bf16[4,64,256]{2,1,0:T(8,128)(2,1)S(1)}, bf16[4,64,256]{2,1,0:T(8,128)(2,1)S(1)}, u32[]{:S(2)}, u32[]{:S(2)}) collective-permute-start(bf16[4,64,256]{2,1,0:T(8,128)(2,1)S(1)} %get-tuple-element.53), channel_id=1, source_target_pairs={{0,8},{8,0},{16,24},{24,16},{1,9},{9,1},{17,25},{25,17},{2,10},{10... | collective-permute-start | bytes 393224 | tf_op jit(solution)/shard_map/ppermute | solution.py:375
  21.3 1.5 %collective-permute-start.6 = (bf16[4,64,256]{2,1,0:T(8,128)(2,1)S(1)}, bf16[4,64,256]{2,1,0:T(8,128)(2,1)S(1)}, u32[]{:S(2)}, u32[]{:S(2)}) collective-permute-start(bf16[4,64,256]{2,1,0:T(8,128)(2,1)S(1)} %get-tuple-element.54), channel_id=1, source_target_pairs={{0,16},{8,24},{16,0},{24,8},{1,17},{9,25},{17,1},{25,9},{2,18},{10... | collective-permute-start | bytes 393224 | tf_op jit(solution)/shard_map/ppermute | solution.py:375
  22.8 0.5 %collective-permute-start.7 = (bf16[4,64,256]{2,1,0:T(8,128)(2,1)S(1)}, bf16[4,64,256]{2,1,0:T(8,128)(2,1)S(1)}, u32[]{:S(2)}, u32[]{:S(2)}) collective-permute-start(bf16[4,64,256]{2,1,0:T(8,128)(2,1)S(1)} %get-tuple-element.55), channel_id=1, source_target_pairs={{0,24},{8,16},{16,8},{24,0},{1,25},{9,17},{17,9},{25,1},{2,26},{10... | collective-permute-start | bytes 393224 | tf_op jit(solution)/shard_map/ppermute | solution.py:375
  23.3 3.6 %shard_map.105 = (bf16[256,512]{1,0:T(8,128)(2,1)}, f32[256,512]{1,0:T(8,128)S(1)}, f32[256,512]{1,0:T(8,128)S(1)}, bf16[256,1024]{1,0:T(8,128)(2,1)}, f32[8,128]{1,0:T(8,128)S(1)}) custom-call(bf16[256,512]{1,0:T(8,128)(2,1)S(1)} %bitcast.20, bf16[256,512]{1,0:T(8,128)(2,1)S(1)} %bitcast.10, bf16[256,512]{1,0:T(8,128)(2,1)S(1)} %bitcast.12, ...), custom_call_target="tpu_custom_call" | custom-call | flops 2000000000 | bytes 4194304 | tf_op jit(solution)/shard_map/pallas_call | solution.py:268
  26.8 0.0 collective-permute-done.3.refs_5_.from_link
  26.8 0.0 collective-permute-done.4.refs_6_.from_chip
  26.8 0.0 collective-permute-done.5.refs_1_
  26.8 2.9 %collective-permute-done.6.refs_2_ = bf16[4,64,256]{2,1,0:T(8,128)(2,1)S(1)} collective-permute-done((bf16[4,64,256]{2,1,0:T(8,128)(2,1)S(1)}, bf16[4,64,256]{2,1,0:T(8,128)(2,1)S(1)}, u32[]{:S(2)}, u32[]{:S(2)}) %collective-permute-start.6) | collective-permute-done | bytes 131104 | tf_op jit(solution)/shard_map/ppermute | solution.py:375
  29.7 0.0 collective-permute-done.7.refs_3_
  29.7 0.1 shard_map.106
  29.8 0.1 collective-permute-start.8
  29.9 1.8 %collective-permute-start.9 = (bf16[64,256]{1,0:T(8,128)(2,1)S(1)}, bf16[64,256]{1,0:T(8,128)(2,1)S(1)}, u32[]{:S(2)}, u32[]{:S(2)}) collective-permute-start(bf16[64,256]{1,0:T(8,128)(2,1)S(1)} %get-tuple-element.61), channel_id=1, source_target_pairs={{0,4},{1,5},{2,6},{3,7},{4,0},{5,1},{6,2},{7,3},{8,12},{9,13},{10,... | collective-permute-start | bytes 98312 | tf_op jit(solution)/shard_map/ppermute | solution.py:385
  31.7 2.6 %collective-permute-start.10 = (bf16[64,256]{1,0:T(8,128)(2,1)S(1)}, bf16[64,256]{1,0:T(8,128)(2,1)S(1)}, u32[]{:S(2)}, u32[]{:S(2)}) collective-permute-start(bf16[64,256]{1,0:T(8,128)(2,1)S(1)} %get-tuple-element.62), channel_id=1, source_target_pairs={{0,6},{1,7},{2,4},{3,5},{4,2},{5,3},{6,0},{7,1},{8,14},{9,15},{10,... | collective-permute-start | bytes 98312 | tf_op jit(solution)/shard_map/ppermute | solution.py:385
  34.2 0.0 collective-permute-done.8
  34.2 0.7 %collective-permute-done.9 = bf16[64,256]{1,0:T(8,128)(2,1)S(1)} collective-permute-done((bf16[64,256]{1,0:T(8,128)(2,1)S(1)}, bf16[64,256]{1,0:T(8,128)(2,1)S(1)}, u32[]{:S(2)}, u32[]{:S(2)}) %collective-permute-start.9) | collective-permute-done | bytes 32800 | tf_op jit(solution)/shard_map/ppermute | solution.py:385
  34.9 2.5 %collective-permute-done.10 = bf16[64,256]{1,0:T(8,128)(2,1)S(1)} collective-permute-done((bf16[64,256]{1,0:T(8,128)(2,1)S(1)}, bf16[64,256]{1,0:T(8,128)(2,1)S(1)}, u32[]{:S(2)}, u32[]{:S(2)}) %collective-permute-start.10) | collective-permute-done | bytes 32800 | tf_op jit(solution)/shard_map/ppermute | solution.py:385
  37.4 1.6 %collective-permute-start.13 = (bf16[64,256]{1,0:T(8,128)(2,1)S(1)}, bf16[64,256]{1,0:T(8,128)(2,1)S(1)}, u32[]{:S(2)}, u32[]{:S(2)}) collective-permute-start(bf16[64,256]{1,0:T(8,128)(2,1)S(1)} %multiply_convert_fusion.refs_0_), channel_id=1, source_target_pairs={{0,24},{8,16},{16,8},{24,0},{1,25},{9,17},{17,9},{25,1},{2,26},{10... | collective-permute-start | bytes 98312 | tf_op jit(solution)/shard_map/ppermute | solution.py:388
  39.0 1.2 %collective-permute-start.12 = (bf16[64,256]{1,0:T(8,128)(2,1)S(1)}, bf16[64,256]{1,0:T(8,128)(2,1)S(1)}, u32[]{:S(2)}, u32[]{:S(2)}) collective-permute-start(bf16[64,256]{1,0:T(8,128)(2,1)S(1)} %multiply_convert_fusion.refs_0_), channel_id=1, source_target_pairs={{0,16},{8,24},{16,0},{24,8},{1,17},{9,25},{17,1},{25,9},{2,18},{10... | collective-permute-start | bytes 98312 | tf_op jit(solution)/shard_map/ppermute | solution.py:388
  40.2 0.8 %collective-permute-start.11 = (bf16[64,256]{1,0:T(8,128)(2,1)S(1)}, bf16[64,256]{1,0:T(8,128)(2,1)S(1)}, u32[]{:S(2)}, u32[]{:S(2)}) collective-permute-start(bf16[64,256]{1,0:T(8,128)(2,1)S(1)} %multiply_convert_fusion.refs_0_), channel_id=1, source_target_pairs={{0,8},{8,0},{16,24},{24,16},{1,9},{9,1},{17,25},{25,17},{2,10},{10... | collective-permute-start | bytes 98312 | tf_op jit(solution)/shard_map/ppermute | solution.py:388
  41.0 0.9 %shard_map.107 = (bf16[256,512]{1,0:T(8,128)(2,1)}, bf16[256,512]{1,0:T(8,128)(2,1)}) custom-call(f32[256,512]{1,0:T(8,128)S(1)} %get-tuple-element.48.k_own, f32[256,512]{1,0:T(8,128)S(1)} %get-tuple-element.49.v_own, bf16[2,128,512]{2,1,0:T(8,128)(2,1)S(1)} %collective-permute-done.3.refs_5_.from_link, ...), custom_call_target="tpu_custom_call" | custom-call | flops 1000000 | bytes 4194304 | tf_op jit(solution)/shard_map/pallas_call | solution.py:268
  41.9 0.4 collective-permute-done.13.refs_3_
  42.3 0.6 %collective-permute-done.12.refs_2_ = bf16[64,256]{1,0:T(8,128)(2,1)S(1)} collective-permute-done((bf16[64,256]{1,0:T(8,128)(2,1)S(1)}, bf16[64,256]{1,0:T(8,128)(2,1)S(1)}, u32[]{:S(2)}, u32[]{:S(2)}) %collective-permute-start.12) | collective-permute-done | bytes 32800 | tf_op jit(solution)/shard_map/ppermute | solution.py:388
  42.9 1.2 %collective-permute-done.11.refs_1_ = bf16[64,256]{1,0:T(8,128)(2,1)S(1)} collective-permute-done((bf16[64,256]{1,0:T(8,128)(2,1)S(1)}, bf16[64,256]{1,0:T(8,128)(2,1)S(1)}, u32[]{:S(2)}, u32[]{:S(2)}) %collective-permute-start.11) | collective-permute-done | bytes 32800 | tf_op jit(solution)/shard_map/ppermute | solution.py:388
  44.1 0.7 %shard_map.108 = f32[64,1024]{1,0:T(8,128)} custom-call(bf16[64,256]{1,0:T(8,128)(2,1)S(1)} %multiply_convert_fusion.refs_0_, bf16[64,256]{1,0:T(8,128)(2,1)S(1)} %collective-permute-done.11.refs_1_, bf16[64,256]{1,0:T(8,128)(2,1)S(1)} %collective-permute-done.12.refs_2_, bf16[64,256]{1,0:T(8,128)(2,1)S(1)} %collective-permute-done.13.refs_3_), custom_call_target="tpu_custom_call" | custom-call | flops 1000000 | bytes 4194304 | tf_op jit(solution)/shard_map/pallas_call | solution.py:268
  (7 shorter events, 0.1 us)
Async XLA Ops:
  0.6 6.1 %copy-start = (s32[1,16,3]{1,0,2:T(1,128)S(1)}, s32[1,16,3]{1,0,2:T(1,128)}, u32[]{:S(2)}) copy-start(s32[1,16,3]{1,0,2:T(1,128)} %param.11) | copy-start | bytes 580
  0.6 6.2 %copy-start.2 = (bf16[1,256,512]{2,1,0:T(8,128)(2,1)S(1)}, bf16[1,256,512]{2,1,0:T(8,128)(2,1)}, u32[]{:S(2)}) copy-start(bf16[1,256,512]{2,1,0:T(8,128)(2,1)} %param.8) | copy-start | bytes 786436
  0.7 6.2 %copy-start.1 = (bf16[1,256,512]{2,1,0:T(8,128)(2,1)S(1)}, bf16[1,256,512]{2,1,0:T(8,128)(2,1)}, u32[]{:S(2)}) copy-start(bf16[1,256,512]{2,1,0:T(8,128)(2,1)} %param.7) | copy-start | bytes 786436
  0.7 6.2 %copy-start.3 = (bf16[512,1024]{1,0:T(8,128)(2,1)S(1)}, bf16[512,1024]{1,0:T(8,128)(2,1)}, u32[]{:S(2)}) copy-start(bf16[512,1024]{1,0:T(8,128)(2,1)} %w_out.3) | copy-start | bytes 3145732
  0.7 6.2 %copy-start.4 = (bf16[1,256,1024]{2,1,0:T(8,128)(2,1)S(1)}, bf16[1,256,1024]{2,1,0:T(8,128)(2,1)}, u32[]{:S(2)}) copy-start(bf16[1,256,1024]{2,1,0:T(8,128)(2,1)} %param.9) | copy-start | bytes 1572868
  2.0 10.6 %collective-permute-start = (bf16[2,128,512]{2,1,0:T(8,128)(2,1)S(1)}, bf16[2,128,512]{2,1,0:T(8,128)(2,1)S(1)}, u32[]{:S(2)}, u32[]{:S(2)}) collective-permute-start(bf16[2,128,512]{2,1,0:T(8,128)(2,1)S(1)} %pad_maximum_fusion), channel_id=1, source_target_pairs={{0,7},{1,2},{2,1},{3,4},{4,3},{5,6},{6,5},{7,0},{8,15},{9,10},{10,... | collective-permute-start | bytes 786440 | tf_op jit(solution)/shard_map/ppermute | solution.py:308
  6.6 6.0 %collective-permute-start.1 = (bf16[2,128,512]{2,1,0:T(8,128)(2,1)S(1)}, bf16[2,128,512]{2,1,0:T(8,128)(2,1)S(1)}, u32[]{:S(2)}, u32[]{:S(2)}) collective-permute-start(bf16[2,128,512]{2,1,0:T(8,128)(2,1)S(1)} %pad_maximum_fusion.1), channel_id=1, source_target_pairs={{0,1},{1,0},{2,3},{3,2},{4,5},{5,4},{6,7},{7,6},{8,9},{9,8},{10,11... | collective-permute-start | bytes 786440 | tf_op jit(solution)/shard_map/ppermute | solution.py:309
  6.9 1.0 %copy-start.5 = (bf16[1,256,512]{2,1,0:T(8,128)(2,1)S(1)}, bf16[1,256,512]{2,1,0:T(8,128)(2,1)}, u32[]{:S(2)}) copy-start(bf16[1,256,512]{2,1,0:T(8,128)(2,1)} %param.6) | copy-start | bytes 786436
  14.5 4.9 %collective-permute-start.2 = (bf16[4,64,1024]{2,1,0:T(8,128)(2,1)S(1)}, bf16[4,64,1024]{2,1,0:T(8,128)(2,1)S(1)}, u32[]{:S(2)}, u32[]{:S(2)}) collective-permute-start(bf16[4,64,1024]{2,1,0:T(8,128)(2,1)S(1)} %get-tuple-element.44), channel_id=1, source_target_pairs={{0,1},{1,0},{2,3},{3,2},{4,5},{5,4},{6,7},{7,6},{8,9},{9,8},{10,11... | collective-permute-start | bytes 1572872 | tf_op jit(solution)/shard_map/ppermute | solution.py:340
  16.1 10.7 %collective-permute-start.3 = (bf16[2,128,512]{2,1,0:T(8,128)(2,1)S(1)}, bf16[2,128,512]{2,1,0:T(8,128)(2,1)S(1)}, u32[]{:S(2)}, u32[]{:S(2)}) collective-permute-start(bf16[2,128,512]{2,1,0:T(8,128)(2,1)S(1)} %get-tuple-element.50), channel_id=1, source_target_pairs={{0,7},{1,2},{2,1},{3,4},{4,3},{5,6},{6,5},{7,0},{8,15},{9,10},{10,... | collective-permute-start | bytes 786440 | tf_op jit(solution)/shard_map/ppermute | solution.py:359
  19.4 7.4 %collective-permute-start.4 = (bf16[2,128,512]{2,1,0:T(8,128)(2,1)S(1)}, bf16[2,128,512]{2,1,0:T(8,128)(2,1)S(1)}, u32[]{:S(2)}, u32[]{:S(2)}) collective-permute-start(bf16[2,128,512]{2,1,0:T(8,128)(2,1)S(1)} %get-tuple-element.51), channel_id=1, source_target_pairs={{0,1},{1,0},{2,3},{3,2},{4,5},{5,4},{6,7},{7,6},{8,9},{9,8},{10,11... | collective-permute-start | bytes 786440 | tf_op jit(solution)/shard_map/ppermute | solution.py:360
  19.7 7.1 %collective-permute-start.5 = (bf16[4,64,256]{2,1,0:T(8,128)(2,1)S(1)}, bf16[4,64,256]{2,1,0:T(8,128)(2,1)S(1)}, u32[]{:S(2)}, u32[]{:S(2)}) collective-permute-start(bf16[4,64,256]{2,1,0:T(8,128)(2,1)S(1)} %get-tuple-element.53), channel_id=1, source_target_pairs={{0,8},{8,0},{16,24},{24,16},{1,9},{9,1},{17,25},{25,17},{2,10},{10... | collective-permute-start | bytes 393224 | tf_op jit(solution)/shard_map/ppermute | solution.py:375
  21.3 8.4 %collective-permute-start.6 = (bf16[4,64,256]{2,1,0:T(8,128)(2,1)S(1)}, bf16[4,64,256]{2,1,0:T(8,128)(2,1)S(1)}, u32[]{:S(2)}, u32[]{:S(2)}) collective-permute-start(bf16[4,64,256]{2,1,0:T(8,128)(2,1)S(1)} %get-tuple-element.54), channel_id=1, source_target_pairs={{0,16},{8,24},{16,0},{24,8},{1,17},{9,25},{17,1},{25,9},{2,18},{10... | collective-permute-start | bytes 393224 | tf_op jit(solution)/shard_map/ppermute | solution.py:375
  22.8 6.9 %collective-permute-start.7 = (bf16[4,64,256]{2,1,0:T(8,128)(2,1)S(1)}, bf16[4,64,256]{2,1,0:T(8,128)(2,1)S(1)}, u32[]{:S(2)}, u32[]{:S(2)}) collective-permute-start(bf16[4,64,256]{2,1,0:T(8,128)(2,1)S(1)} %get-tuple-element.55), channel_id=1, source_target_pairs={{0,24},{8,16},{16,8},{24,0},{1,25},{9,17},{17,9},{25,1},{2,26},{10... | collective-permute-start | bytes 393224 | tf_op jit(solution)/shard_map/ppermute | solution.py:375
  29.8 4.5 %collective-permute-start.8 = (bf16[64,256]{1,0:T(8,128)(2,1)S(1)}, bf16[64,256]{1,0:T(8,128)(2,1)S(1)}, u32[]{:S(2)}, u32[]{:S(2)}) collective-permute-start(bf16[64,256]{1,0:T(8,128)(2,1)S(1)} %get-tuple-element.60), channel_id=1, source_target_pairs={{0,2},{1,3},{2,0},{3,1},{4,6},{5,7},{6,4},{7,5},{8,10},{9,11},{10,... | collective-permute-start | bytes 98312 | tf_op jit(solution)/shard_map/ppermute | solution.py:385
  29.9 5.1 %collective-permute-start.9 = (bf16[64,256]{1,0:T(8,128)(2,1)S(1)}, bf16[64,256]{1,0:T(8,128)(2,1)S(1)}, u32[]{:S(2)}, u32[]{:S(2)}) collective-permute-start(bf16[64,256]{1,0:T(8,128)(2,1)S(1)} %get-tuple-element.61), channel_id=1, source_target_pairs={{0,4},{1,5},{2,6},{3,7},{4,0},{5,1},{6,2},{7,3},{8,12},{9,13},{10,... | collective-permute-start | bytes 98312 | tf_op jit(solution)/shard_map/ppermute | solution.py:385
  31.7 5.7 %collective-permute-start.10 = (bf16[64,256]{1,0:T(8,128)(2,1)S(1)}, bf16[64,256]{1,0:T(8,128)(2,1)S(1)}, u32[]{:S(2)}, u32[]{:S(2)}) collective-permute-start(bf16[64,256]{1,0:T(8,128)(2,1)S(1)} %get-tuple-element.62), channel_id=1, source_target_pairs={{0,6},{1,7},{2,4},{3,5},{4,2},{5,3},{6,0},{7,1},{8,14},{9,15},{10,... | collective-permute-start | bytes 98312 | tf_op jit(solution)/shard_map/ppermute | solution.py:385
  37.4 4.9 %collective-permute-start.13 = (bf16[64,256]{1,0:T(8,128)(2,1)S(1)}, bf16[64,256]{1,0:T(8,128)(2,1)S(1)}, u32[]{:S(2)}, u32[]{:S(2)}) collective-permute-start(bf16[64,256]{1,0:T(8,128)(2,1)S(1)} %multiply_convert_fusion.refs_0_), channel_id=1, source_target_pairs={{0,24},{8,16},{16,8},{24,0},{1,25},{9,17},{17,9},{25,1},{2,26},{10... | collective-permute-start | bytes 98312 | tf_op jit(solution)/shard_map/ppermute | solution.py:388
  39.0 3.9 %collective-permute-start.12 = (bf16[64,256]{1,0:T(8,128)(2,1)S(1)}, bf16[64,256]{1,0:T(8,128)(2,1)S(1)}, u32[]{:S(2)}, u32[]{:S(2)}) collective-permute-start(bf16[64,256]{1,0:T(8,128)(2,1)S(1)} %multiply_convert_fusion.refs_0_), channel_id=1, source_target_pairs={{0,16},{8,24},{16,0},{24,8},{1,17},{9,25},{17,1},{25,9},{2,18},{10... | collective-permute-start | bytes 98312 | tf_op jit(solution)/shard_map/ppermute | solution.py:388
  40.2 3.9 %collective-permute-start.11 = (bf16[64,256]{1,0:T(8,128)(2,1)S(1)}, bf16[64,256]{1,0:T(8,128)(2,1)S(1)}, u32[]{:S(2)}, u32[]{:S(2)}) collective-permute-start(bf16[64,256]{1,0:T(8,128)(2,1)S(1)} %multiply_convert_fusion.refs_0_), channel_id=1, source_target_pairs={{0,8},{8,0},{16,24},{24,16},{1,9},{9,1},{17,25},{25,17},{2,10},{10... | collective-permute-start | bytes 98312 | tf_op jit(solution)/shard_map/ppermute | solution.py:388

commit v5 on v4

--- a/solution.py
+++ b/solution.py
@@ -218,11 +218,30 @@
     after[...] = jnp.zeros_like(after)
 
 
+def cut_chips(parts, kept, sent):
+    left = parts[0].shape[0]
+    bit = lax.rem(lax.div(lax.axis_index("ctx"), lax.axis_size("ctx") // left), 2)
+    for i in range(left // 2):
+        kept[i] = total([part[2 * i + bit] for part in parts]).astype(BF16)
+        sent[i] = total([part[2 * i + 1 - bit] for part in parts]).astype(BF16)
+
+
 def chips_kernel(*refs):
-    parts, outs = refs[: lax.axis_size("dp")], refs[lax.axis_size("dp") + 3 :]
-    chip = lax.div(lax.axis_index("ctx"), 2)
-    for s, out in enumerate(outs):
-        out[...] = total([part[chip ^ s] for part in parts]).astype(BF16)
+    cut_chips(refs[: lax.axis_size("dp")], *refs[-2:])
+
+
+def chips_step_kernel(kept, got, *outs):
+    cut_chips((kept, got), *outs)
+
+
+def piece_kernel(scale, kept, got, piece):
+    piece[...] = (total([kept[0], got[0]]) * scale).astype(BF16)[None]
+
+
+def join_kernel(held, got, out):
+    count = held.shape[0]
+    out[:count] = held[...]
+    out[count:] = got[...]
 
 
 def rim_sum_kernel(k_own, v_own, from_link, from_chip, before, k_grad, v_grad):
@@ -242,14 +261,14 @@
             grad[tokens - RIM :] = (own[tokens - RIM :] + high).astype(BF16)
 
 
-def columns_kernel(*refs):
-    pieces, out = refs[:-1], refs[-1]
+def columns_kernel(held, got, out):
     at_dp = lax.axis_index("dp")
-    cols = pieces[0].shape[1]
+    pieces = [part[i] for part in (held, got) for i in range(part.shape[0])]
+    cols = held.shape[2]
     for d in range(len(pieces)):
-        value = pieces[0][...]
+        value = pieces[0]
         for s in range(1, len(pieces)):
-            value = jnp.where((at_dp ^ s) == d, pieces[s][...], value)
+            value = jnp.where((at_dp ^ s) == d, pieces[s], value)
         out[:, d * cols : (d + 1) * cols] = value.astype(F32)
 
 
@@ -373,20 +392,39 @@
     )
 
     halves = [halves[0]] + [lax.ppermute(halves[s], "dp", swap(dp, s)) for s in range(1, dp)]
-    quarters = call(chips_kernel, [vmem(rows, cols)] * chips, 10**6, *halves, after, grad_link, grad_chip)
+    kept, sent = call(
+        chips_kernel,
+        [vmem(chips // 2, rows, cols)] * 2,
+        10**6,
+        *halves, after, grad_link, grad_chip,
+    )
     k_grad, v_grad = call(
         rim_sum_kernel,
         [hbm(tokens, feats), hbm(tokens, feats)],
         10**6,
-        k_own, v_own, grad_link, grad_chip, quarters[0],
-    )
-    piece = total(
-        [quarters[0]]
-        + [lax.ppermute(quarters[s], "ctx", swap(ctx, 2 * s)) for s in range(1, chips)]
-    )
-    piece = (piece * (dp * tokens * ctx) ** (-0.5)).astype(BF16)
-    pieces = [piece] + [lax.ppermute(piece, "dp", swap(dp, s)) for s in range(1, dp)]
-    (weight_grad,) = call(columns_kernel, [hbm(rows, width, dtype=F32)], 10**6, *pieces)
+        k_own, v_own, grad_link, grad_chip, kept,
+    )
+    bits = 2
+    while 2 * bits < ctx:
+        got = lax.ppermute(sent, "ctx", swap(ctx, bits))
+        kept, sent = call(
+            chips_step_kernel, [vmem(kept.shape[0] // 2, rows, cols)] * 2, 10**6, kept, got
+        )
+        bits *= 2
+    got = lax.ppermute(sent, "ctx", swap(ctx, bits))
+    (held,) = call(
+        functools.partial(piece_kernel, (dp * tokens * ctx) ** (-0.5)),
+        [vmem(1, rows, cols)],
+        10**6,
+        kept, got,
+    )
+    bits = 1
+    while 2 * bits < dp:
+        got = lax.ppermute(held, "dp", swap(dp, bits))
+        (held,) = call(join_kernel, [vmem(2 * bits, rows, cols)], 10**6, held, got)
+        bits *= 2
+    got = lax.ppermute(held, "dp", swap(dp, bits))
+    (weight_grad,) = call(columns_kernel, [hbm(rows, width, dtype=F32)], 10**6, held, got)
     return (output[None], q_grad[None], k_grad[None], v_grad[None], weight_grad)
 
 

time: 45 us -> 48.2 us (1.071)
  waiting for transfers between devices: 9.69 us -> 17.9 us
  starting transfers between devices: 19.5 us -> 14.6 us
    ppermute x6 -> x4, waiting for transfers between devices: 5.37 us -> 13.5 us  [the longest x2 8.99 us: body(): got = lax.ppermute(sent, 'ctx', swap(ctx, bits))]
    ppermute x6 -> x4, starting transfers between devices: 8 us -> 3.01 us  [the longest x2 2.8 us: body(): got = lax.ppermute(held, 'dp', swap(dp, bits))]
    pallas_call x8 -> x11, Pallas kernels: 12.2 us -> 12.3 us  [call(): pl.pallas_call(kernel, out_shape=outs, in_specs=[in_smem] * len(masks) +...]
  transfers between devices with their start and end apart: 14 -> 12, of which waited for: 7 -> 6; matrix products, arithmetic and copies ran while one was open for 0% -> 0% of each run, Pallas kernels for 21% -> 20%
where the time goes in v5:
time: 48.2 us; the launch traced here: 48 us
  waiting for transfers between devices  17.9 us (37%)
  starting transfers between devices  14.6 us (30%)
  Pallas kernels  12.3 us (26%)
  local copies, waits for them, and re-layouts  2.42 us (5%)
  between operations  0.82 us (2%)
    pallas_call x11, Pallas kernels, call(): pl.pallas_call(kernel, out_shape=outs, in_specs=[in_smem] * len(masks) +...  12.3 us
    ppermute x2, waiting for transfers between devices, body(): got = lax.ppermute(sent, 'ctx', swap(ctx, bits))  8.99 us
    ppermute x2, waiting for transfers between devices, body(): got = lax.ppermute(held, 'dp', swap(dp, bits))  4.56 us
    ppermute x1, starting transfers between devices, body(): from_link = lax.ppermute(rim(link_row), 'ctx', over_links(ctx))  4.55 us
    ppermute x3, starting transfers between devices, body(): lax.ppermute(halves[s], 'dp', swap(dp, s))  3.55 us
    ppermute x1, starting transfers between devices, body(): grad_link = lax.ppermute(to_link, 'ctx', over_links(ctx))  3.3 us
    ppermute x3, waiting for transfers between devices, body(): lax.ppermute(halves[s], 'dp', swap(dp, s))  2.88 us
    ppermute x2, starting transfers between devices, body(): got = lax.ppermute(held, 'dp', swap(dp, bits))  2.8 us
  transfers between devices with their start and end apart: 12, of which 6 were waited for; matrix products, arithmetic and copies ran while one was open for 0% of the time, Pallas kernels for 20%

profile of v5, /device:TPU:0, one launch (start us, length us, event | category | flops | bytes accessed | tf_op | source)
XLA Modules:
  0.0 48.0 jit_solution(9448005056829413728)
XLA Ops:
  0.6 0.0 copy-start
  0.6 0.0 copy-start.2
  0.7 0.0 copy-start.1
  0.7 0.0 copy-start.3
  0.7 0.0 copy-start.4
  0.7 1.3 %constant_dynamic-slice_fusion = (bf16[1,128,512]{2,1,0:T(8,128)(2,1)S(1)}, bf16[1,128,512]{2,1,0:T(8,128)(2,1)S(1)}, bf16[1,128,512]{2,1,0:T(8,128)(2,1)S(1)}, bf16[1,128,512]{2,1,0:T(8,128)(2,1)S(1)}) fusion(bf16[1,256,512]{2,1,0:T(8,128)(2,1)} %param.8, s32[]{:T(128)S(6)} %select_n.34, s32[]{:T(128)S(6)} %select_n.33, bf16[1,256,512]{2,1,0:T(8,128)(2,1)} %param.7), kind=kLoop, calls=%fused_computation.4 | loop fusion | bytes 1048584 | tf_op jit(solution)/shard_map/dynamic_slice | solution.py:325
  2.0 4.6 %collective-permute-start = (bf16[2,128,512]{2,1,0:T(8,128)(2,1)S(1)}, bf16[2,128,512]{2,1,0:T(8,128)(2,1)S(1)}, u32[]{:S(2)}, u32[]{:S(2)}) collective-permute-start(bf16[2,128,512]{2,1,0:T(8,128)(2,1)S(1)} %pad_maximum_fusion), channel_id=1, source_target_pairs={{0,7},{1,2},{2,1},{3,4},{4,3},{5,6},{6,5},{7,0},{8,15},{9,10},{10,... | collective-permute-start | bytes 786440 | tf_op jit(solution)/shard_map/ppermute | solution.py:327
  6.6 0.1 collective-permute-start.1
  6.7 0.0 copy-done
  6.7 0.1 constant_dynamic-slice_fusion.4
  6.8 0.1 copy.11
  6.9 0.0 copy-done.2
  6.9 0.0 copy-done.1
  6.9 0.0 copy-done.3
  6.9 0.0 copy-done.4
  6.9 0.0 copy-start.5
  6.9 0.9 %copy-done.5 = bf16[1,256,512]{2,1,0:T(8,128)(2,1)S(1)} copy-done((bf16[1,256,512]{2,1,0:T(8,128)(2,1)S(1)}, bf16[1,256,512]{2,1,0:T(8,128)(2,1)}, u32[]{:S(2)}) %copy-start.5) | copy-done | bytes 262168
  7.8 3.3 %shard_map.101 = (f32[512,256]{1,0:T(8,128)S(1)}, f32[2,8,256]{2,1,0:T(8,128)S(1)}, f32[8,256,256]{2,1,0:T(8,128)S(1)}, bf16[512,256]{1,0:T(8,128)(2,1)S(1)}) custom-call(s32[2,3]{1,0:T(2,128)S(1)} %bitcast.13, bf16[256,512]{1,0:T(8,128)(2,1)S(1)} %bitcast.17, bf16[256,512]{1,0:T(8,128)(2,1)S(1)} %bitcast.9, bf16[256,512]{1,0:T(8,128)(2,1)S(1)} %bitcast.11, ...), custom_call_target="tpu_custom_call" | custom-call | flops 1000000000 | bytes 4194304 | tf_op jit(solution)/shard_map/pallas_call | solution.py:287
  11.2 1.4 %collective-permute-done = bf16[2,128,512]{2,1,0:T(8,128)(2,1)S(1)} collective-permute-done((bf16[2,128,512]{2,1,0:T(8,128)(2,1)S(1)}, bf16[2,128,512]{2,1,0:T(8,128)(2,1)S(1)}, u32[]{:S(2)}, u32[]{:S(2)}) %collective-permute-start) | collective-permute-done | bytes 262176 | tf_op jit(solution)/shard_map/ppermute | solution.py:327
  12.6 0.0 collective-permute-done.1
  12.7 1.9 %shard_map.102 = (bf16[512,256]{1,0:T(8,128)(2,1)S(1)}, bf16[4,64,1024]{2,1,0:T(8,128)(2,1)S(1)}, bf16[4,64,1024]{2,1,0:T(8,128)(2,1)S(1)}, f32[2,4,128,256]{3,2,1,0:T(8,128)S(1)}, f32[2,8,256]{2,1,0:T(8,128)S(1)}) custom-call(s32[2,3]{1,0:T(2,128)S(1)} %bitcast.14, bf16[256,512]{1,0:T(8,128)(2,1)S(1)} %bitcast.18, ...), custom_call_target="tpu_custom_call" | custom-call | flops 1000000000 | bytes 4194304 | tf_op jit(solution)/shard_map/pallas_call | solution.py:287
  14.5 0.1 collective-permute-start.2
  14.6 1.5 %shard_map.103 = (bf16[2,128,512]{2,1,0:T(8,128)(2,1)S(1)}, bf16[2,128,512]{2,1,0:T(8,128)(2,1)S(1)}, f32[8,256]{1,0:T(8,128)S(1)}, f32[512,256]{1,0:T(8,128)S(1)}) custom-call(bf16[256,512]{1,0:T(8,128)(2,1)S(1)} %bitcast.19, bf16[2,128,512]{2,1,0:T(8,128)(2,1)S(1)} %get-tuple-element.64.low, bf16[2,128,512]{2,1,0:T(8,128)(2,1)S(1)} %get-tuple-element.63.high, ...), custom_call_target="tpu_custom_call" | custom-call | flops 1000000000 | bytes 4194304 | tf_op jit(solution)/shard_map/pallas_call | solution.py:287
  16.1 3.3 %collective-permute-start.3 = (bf16[2,128,512]{2,1,0:T(8,128)(2,1)S(1)}, bf16[2,128,512]{2,1,0:T(8,128)(2,1)S(1)}, u32[]{:S(2)}, u32[]{:S(2)}) collective-permute-start(bf16[2,128,512]{2,1,0:T(8,128)(2,1)S(1)} %get-tuple-element.50), channel_id=1, source_target_pairs={{0,7},{1,2},{2,1},{3,4},{4,3},{5,6},{6,5},{7,0},{8,15},{9,10},{10,... | collective-permute-start | bytes 786440 | tf_op jit(solution)/shard_map/ppermute | solution.py:378
  19.4 0.0 collective-permute-start.4
  19.4 0.0 collective-permute-done.2.other
  19.4 0.3 shard_map.104
  19.7 1.6 %collective-permute-start.5 = (bf16[4,64,256]{2,1,0:T(8,128)(2,1)S(1)}, bf16[4,64,256]{2,1,0:T(8,128)(2,1)S(1)}, u32[]{:S(2)}, u32[]{:S(2)}) collective-permute-start(bf16[4,64,256]{2,1,0:T(8,128)(2,1)S(1)} %get-tuple-element.53), channel_id=1, source_target_pairs={{0,8},{8,0},{16,24},{24,16},{1,9},{9,1},{17,25},{25,17},{2,10},{10... | collective-permute-start | bytes 393224 | tf_op jit(solution)/shard_map/ppermute | solution.py:394
  21.3 1.5 %collective-permute-start.6 = (bf16[4,64,256]{2,1,0:T(8,128)(2,1)S(1)}, bf16[4,64,256]{2,1,0:T(8,128)(2,1)S(1)}, u32[]{:S(2)}, u32[]{:S(2)}) collective-permute-start(bf16[4,64,256]{2,1,0:T(8,128)(2,1)S(1)} %get-tuple-element.54), channel_id=1, source_target_pairs={{0,16},{8,24},{16,0},{24,8},{1,17},{9,25},{17,1},{25,9},{2,18},{10... | collective-permute-start | bytes 393224 | tf_op jit(solution)/shard_map/ppermute | solution.py:394
  22.8 0.5 %collective-permute-start.7 = (bf16[4,64,256]{2,1,0:T(8,128)(2,1)S(1)}, bf16[4,64,256]{2,1,0:T(8,128)(2,1)S(1)}, u32[]{:S(2)}, u32[]{:S(2)}) collective-permute-start(bf16[4,64,256]{2,1,0:T(8,128)(2,1)S(1)} %get-tuple-element.55), channel_id=1, source_target_pairs={{0,24},{8,16},{16,8},{24,0},{1,25},{9,17},{17,9},{25,1},{2,26},{10... | collective-permute-start | bytes 393224 | tf_op jit(solution)/shard_map/ppermute | solution.py:394
  23.3 3.6 %shard_map.105 = (bf16[256,512]{1,0:T(8,128)(2,1)}, f32[256,512]{1,0:T(8,128)S(1)}, f32[256,512]{1,0:T(8,128)S(1)}, bf16[256,1024]{1,0:T(8,128)(2,1)}, f32[8,128]{1,0:T(8,128)S(1)}) custom-call(bf16[256,512]{1,0:T(8,128)(2,1)S(1)} %bitcast.20, bf16[256,512]{1,0:T(8,128)(2,1)S(1)} %bitcast.10, bf16[256,512]{1,0:T(8,128)(2,1)S(1)} %bitcast.12, ...), custom_call_target="tpu_custom_call" | custom-call | flops 2000000000 | bytes 4194304 | tf_op jit(solution)/shard_map/pallas_call | solution.py:287
  26.8 0.0 collective-permute-done.3.refs_5_.from_link
  26.8 0.0 collective-permute-done.4.refs_6_.from_chip
  26.8 0.0 collective-permute-done.5.refs_1_
  26.8 2.9 %collective-permute-done.6.refs_2_ = bf16[4,64,256]{2,1,0:T(8,128)(2,1)S(1)} collective-permute-done((bf16[4,64,256]{2,1,0:T(8,128)(2,1)S(1)}, bf16[4,64,256]{2,1,0:T(8,128)(2,1)S(1)}, u32[]{:S(2)}, u32[]{:S(2)}) %collective-permute-start.6) | collective-permute-done | bytes 131104 | tf_op jit(solution)/shard_map/ppermute | solution.py:394
  29.7 0.0 collective-permute-done.7.refs_3_
  29.7 0.1 shard_map.106
  29.8 0.1 collective-permute-start.8
  29.9 4.3 %collective-permute-done.8.got = bf16[2,64,256]{2,1,0:T(8,128)(2,1)S(1)} collective-permute-done((bf16[2,64,256]{2,1,0:T(8,128)(2,1)S(1)}, bf16[2,64,256]{2,1,0:T(8,128)(2,1)S(1)}, u32[]{:S(2)}, u32[]{:S(2)}) %collective-permute-start.8) | collective-permute-done | bytes 65568 | tf_op jit(solution)/shard_map/ppermute | solution.py:409
  34.1 0.1 collective-permute-start.9
  34.3 4.7 %collective-permute-done.9.got = bf16[1,64,256]{2,1,0:T(8,128)(2,1)S(1)} collective-permute-done((bf16[1,64,256]{2,1,0:T(8,128)(2,1)S(1)}, bf16[1,64,256]{2,1,0:T(8,128)(2,1)S(1)}, u32[]{:S(2)}, u32[]{:S(2)}) %collective-permute-start.9) | collective-permute-done | bytes 32800 | tf_op jit(solution)/shard_map/ppermute | solution.py:414
  39.0 1.3 %collective-permute-start.10 = (bf16[1,64,256]{2,1,0:T(8,128)(2,1)S(1)}, bf16[1,64,256]{2,1,0:T(8,128)(2,1)S(1)}, u32[]{:S(2)}, u32[]{:S(2)}) collective-permute-start(bf16[1,64,256]{2,1,0:T(8,128)(2,1)S(1)} %shard_map.109.held), channel_id=1, source_target_pairs={{0,8},{8,0},{16,24},{24,16},{1,9},{9,1},{17,25},{25,17},{2,10},{10... | collective-permute-start | bytes 98312 | tf_op jit(solution)/shard_map/ppermute | solution.py:423
  40.3 2.7 %collective-permute-done.10.got = bf16[1,64,256]{2,1,0:T(8,128)(2,1)S(1)} collective-permute-done((bf16[1,64,256]{2,1,0:T(8,128)(2,1)S(1)}, bf16[1,64,256]{2,1,0:T(8,128)(2,1)S(1)}, u32[]{:S(2)}, u32[]{:S(2)}) %collective-permute-start.10) | collective-permute-done | bytes 32800 | tf_op jit(solution)/shard_map/ppermute | solution.py:423
  43.0 1.5 %collective-permute-start.11 = (bf16[2,64,256]{2,1,0:T(8,128)(2,1)S(1)}, bf16[2,64,256]{2,1,0:T(8,128)(2,1)S(1)}, u32[]{:S(2)}, u32[]{:S(2)}) collective-permute-start(bf16[2,64,256]{2,1,0:T(8,128)(2,1)S(1)} %shard_map.110.held), channel_id=1, source_target_pairs={{0,16},{8,24},{16,0},{24,8},{1,17},{9,25},{17,1},{25,9},{2,18},{10... | collective-permute-start | bytes 196616 | tf_op jit(solution)/shard_map/ppermute | solution.py:426
  44.5 0.9 %shard_map.107 = (bf16[256,512]{1,0:T(8,128)(2,1)}, bf16[256,512]{1,0:T(8,128)(2,1)}) custom-call(f32[256,512]{1,0:T(8,128)S(1)} %get-tuple-element.48.k_own, f32[256,512]{1,0:T(8,128)S(1)} %get-tuple-element.49.v_own, bf16[2,128,512]{2,1,0:T(8,128)(2,1)S(1)} %collective-permute-done.3.refs_5_.from_link, ...), custom_call_target="tpu_custom_call" | custom-call | flops 1000000 | bytes 4194304 | tf_op jit(solution)/shard_map/pallas_call | solution.py:287
  45.4 1.9 %collective-permute-done.11.got = bf16[2,64,256]{2,1,0:T(8,128)(2,1)S(1)} collective-permute-done((bf16[2,64,256]{2,1,0:T(8,128)(2,1)S(1)}, bf16[2,64,256]{2,1,0:T(8,128)(2,1)S(1)}, u32[]{:S(2)}, u32[]{:S(2)}) %collective-permute-start.11) | collective-permute-done | bytes 65568 | tf_op jit(solution)/shard_map/ppermute | solution.py:426
  47.3 0.7 %shard_map.111 = f32[64,1024]{1,0:T(8,128)} custom-call(bf16[2,64,256]{2,1,0:T(8,128)(2,1)S(1)} %shard_map.110.held, bf16[2,64,256]{2,1,0:T(8,128)(2,1)S(1)} %collective-permute-done.11.got), custom_call_target="tpu_custom_call" | custom-call | flops 1000000 | bytes 4194304 | tf_op jit(solution)/shard_map/pallas_call | solution.py:287
  (6 shorter events, 0.1 us)
Async XLA Ops:
  0.6 6.1 %copy-start = (s32[1,16,3]{1,0,2:T(1,128)S(1)}, s32[1,16,3]{1,0,2:T(1,128)}, u32[]{:S(2)}) copy-start(s32[1,16,3]{1,0,2:T(1,128)} %param.11) | copy-start | bytes 580
  0.6 6.2 %copy-start.2 = (bf16[1,256,512]{2,1,0:T(8,128)(2,1)S(1)}, bf16[1,256,512]{2,1,0:T(8,128)(2,1)}, u32[]{:S(2)}) copy-start(bf16[1,256,512]{2,1,0:T(8,128)(2,1)} %param.8) | copy-start | bytes 786436
  0.7 6.2 %copy-start.1 = (bf16[1,256,512]{2,1,0:T(8,128)(2,1)S(1)}, bf16[1,256,512]{2,1,0:T(8,128)(2,1)}, u32[]{:S(2)}) copy-start(bf16[1,256,512]{2,1,0:T(8,128)(2,1)} %param.7) | copy-start | bytes 786436
  0.7 6.2 %copy-start.3 = (bf16[512,1024]{1,0:T(8,128)(2,1)S(1)}, bf16[512,1024]{1,0:T(8,128)(2,1)}, u32[]{:S(2)}) copy-start(bf16[512,1024]{1,0:T(8,128)(2,1)} %w_out.3) | copy-start | bytes 3145732
  0.7 6.2 %copy-start.4 = (bf16[1,256,1024]{2,1,0:T(8,128)(2,1)S(1)}, bf16[1,256,1024]{2,1,0:T(8,128)(2,1)}, u32[]{:S(2)}) copy-start(bf16[1,256,1024]{2,1,0:T(8,128)(2,1)} %param.9) | copy-start | bytes 1572868
  2.0 10.6 %collective-permute-start = (bf16[2,128,512]{2,1,0:T(8,128)(2,1)S(1)}, bf16[2,128,512]{2,1,0:T(8,128)(2,1)S(1)}, u32[]{:S(2)}, u32[]{:S(2)}) collective-permute-start(bf16[2,128,512]{2,1,0:T(8,128)(2,1)S(1)} %pad_maximum_fusion), channel_id=1, source_target_pairs={{0,7},{1,2},{2,1},{3,4},{4,3},{5,6},{6,5},{7,0},{8,15},{9,10},{10,... | collective-permute-start | bytes 786440 | tf_op jit(solution)/shard_map/ppermute | solution.py:327
  6.6 6.0 %collective-permute-start.1 = (bf16[2,128,512]{2,1,0:T(8,128)(2,1)S(1)}, bf16[2,128,512]{2,1,0:T(8,128)(2,1)S(1)}, u32[]{:S(2)}, u32[]{:S(2)}) collective-permute-start(bf16[2,128,512]{2,1,0:T(8,128)(2,1)S(1)} %pad_maximum_fusion.1), channel_id=1, source_target_pairs={{0,1},{1,0},{2,3},{3,2},{4,5},{5,4},{6,7},{7,6},{8,9},{9,8},{10,11... | collective-permute-start | bytes 786440 | tf_op jit(solution)/shard_map/ppermute | solution.py:328
  6.9 1.0 %copy-start.5 = (bf16[1,256,512]{2,1,0:T(8,128)(2,1)S(1)}, bf16[1,256,512]{2,1,0:T(8,128)(2,1)}, u32[]{:S(2)}) copy-start(bf16[1,256,512]{2,1,0:T(8,128)(2,1)} %param.6) | copy-start | bytes 786436
  14.5 4.9 %collective-permute-start.2 = (bf16[4,64,1024]{2,1,0:T(8,128)(2,1)S(1)}, bf16[4,64,1024]{2,1,0:T(8,128)(2,1)S(1)}, u32[]{:S(2)}, u32[]{:S(2)}) collective-permute-start(bf16[4,64,1024]{2,1,0:T(8,128)(2,1)S(1)} %get-tuple-element.44), channel_id=1, source_target_pairs={{0,1},{1,0},{2,3},{3,2},{4,5},{5,4},{6,7},{7,6},{8,9},{9,8},{10,11... | collective-permute-start | bytes 1572872 | tf_op jit(solution)/shard_map/ppermute | solution.py:359
  16.1 10.7 %collective-permute-start.3 = (bf16[2,128,512]{2,1,0:T(8,128)(2,1)S(1)}, bf16[2,128,512]{2,1,0:T(8,128)(2,1)S(1)}, u32[]{:S(2)}, u32[]{:S(2)}) collective-permute-start(bf16[2,128,512]{2,1,0:T(8,128)(2,1)S(1)} %get-tuple-element.50), channel_id=1, source_target_pairs={{0,7},{1,2},{2,1},{3,4},{4,3},{5,6},{6,5},{7,0},{8,15},{9,10},{10,... | collective-permute-start | bytes 786440 | tf_op jit(solution)/shard_map/ppermute | solution.py:378
  19.4 7.4 %collective-permute-start.4 = (bf16[2,128,512]{2,1,0:T(8,128)(2,1)S(1)}, bf16[2,128,512]{2,1,0:T(8,128)(2,1)S(1)}, u32[]{:S(2)}, u32[]{:S(2)}) collective-permute-start(bf16[2,128,512]{2,1,0:T(8,128)(2,1)S(1)} %get-tuple-element.51), channel_id=1, source_target_pairs={{0,1},{1,0},{2,3},{3,2},{4,5},{5,4},{6,7},{7,6},{8,9},{9,8},{10,11... | collective-permute-start | bytes 786440 | tf_op jit(solution)/shard_map/ppermute | solution.py:379
  19.7 7.1 %collective-permute-start.5 = (bf16[4,64,256]{2,1,0:T(8,128)(2,1)S(1)}, bf16[4,64,256]{2,1,0:T(8,128)(2,1)S(1)}, u32[]{:S(2)}, u32[]{:S(2)}) collective-permute-start(bf16[4,64,256]{2,1,0:T(8,128)(2,1)S(1)} %get-tuple-element.53), channel_id=1, source_target_pairs={{0,8},{8,0},{16,24},{24,16},{1,9},{9,1},{17,25},{25,17},{2,10},{10... | collective-permute-start | bytes 393224 | tf_op jit(solution)/shard_map/ppermute | solution.py:394
  21.3 8.4 %collective-permute-start.6 = (bf16[4,64,256]{2,1,0:T(8,128)(2,1)S(1)}, bf16[4,64,256]{2,1,0:T(8,128)(2,1)S(1)}, u32[]{:S(2)}, u32[]{:S(2)}) collective-permute-start(bf16[4,64,256]{2,1,0:T(8,128)(2,1)S(1)} %get-tuple-element.54), channel_id=1, source_target_pairs={{0,16},{8,24},{16,0},{24,8},{1,17},{9,25},{17,1},{25,9},{2,18},{10... | collective-permute-start | bytes 393224 | tf_op jit(solution)/shard_map/ppermute | solution.py:394
  22.8 6.9 %collective-permute-start.7 = (bf16[4,64,256]{2,1,0:T(8,128)(2,1)S(1)}, bf16[4,64,256]{2,1,0:T(8,128)(2,1)S(1)}, u32[]{:S(2)}, u32[]{:S(2)}) collective-permute-start(bf16[4,64,256]{2,1,0:T(8,128)(2,1)S(1)} %get-tuple-element.55), channel_id=1, source_target_pairs={{0,24},{8,16},{16,8},{24,0},{1,25},{9,17},{17,9},{25,1},{2,26},{10... | collective-permute-start | bytes 393224 | tf_op jit(solution)/shard_map/ppermute | solution.py:394
  29.8 4.3 %collective-permute-start.8 = (bf16[2,64,256]{2,1,0:T(8,128)(2,1)S(1)}, bf16[2,64,256]{2,1,0:T(8,128)(2,1)S(1)}, u32[]{:S(2)}, u32[]{:S(2)}) collective-permute-start(bf16[2,64,256]{2,1,0:T(8,128)(2,1)S(1)} %get-tuple-element.60), channel_id=1, source_target_pairs={{0,2},{1,3},{2,0},{3,1},{4,6},{5,7},{6,4},{7,5},{8,10},{9,11},{10,... | collective-permute-start | bytes 196616 | tf_op jit(solution)/shard_map/ppermute | solution.py:409
  34.1 4.9 %collective-permute-start.9 = (bf16[1,64,256]{2,1,0:T(8,128)(2,1)S(1)}, bf16[1,64,256]{2,1,0:T(8,128)(2,1)S(1)}, u32[]{:S(2)}, u32[]{:S(2)}) collective-permute-start(bf16[1,64,256]{2,1,0:T(8,128)(2,1)S(1)} %get-tuple-element.62), channel_id=1, source_target_pairs={{0,4},{1,5},{2,6},{3,7},{4,0},{5,1},{6,2},{7,3},{8,12},{9,13},{10,... | collective-permute-start | bytes 98312 | tf_op jit(solution)/shard_map/ppermute | solution.py:414
  39.0 4.0 %collective-permute-start.10 = (bf16[1,64,256]{2,1,0:T(8,128)(2,1)S(1)}, bf16[1,64,256]{2,1,0:T(8,128)(2,1)S(1)}, u32[]{:S(2)}, u32[]{:S(2)}) collective-permute-start(bf16[1,64,256]{2,1,0:T(8,128)(2,1)S(1)} %shard_map.109.held), channel_id=1, source_target_pairs={{0,8},{8,0},{16,24},{24,16},{1,9},{9,1},{17,25},{25,17},{2,10},{10... | collective-permute-start | bytes 98312 | tf_op jit(solution)/shard_map/ppermute | solution.py:423
  43.0 4.3 %collective-permute-start.11 = (bf16[2,64,256]{2,1,0:T(8,128)(2,1)S(1)}, bf16[2,64,256]{2,1,0:T(8,128)(2,1)S(1)}, u32[]{:S(2)}, u32[]{:S(2)}) collective-permute-start(bf16[2,64,256]{2,1,0:T(8,128)(2,1)S(1)} %shard_map.110.held), channel_id=1, source_target_pairs={{0,16},{8,24},{16,0},{24,8},{1,17},{9,25},{17,1},{25,9},{2,18},{10... | collective-permute-start | bytes 196616 | tf_op jit(solution)/shard_map/ppermute | solution.py:426

commit v6 on v4

--- a/solution.py
+++ b/solution.py
@@ -146,7 +146,9 @@
     return query_t, dot(dscore, q2, ((1,), (0,))), dot(probs.astype(BF16), g2_t, ((1,), (1,)))
 
 
-def rim_kernel(q, low, high, grad_t, attn_t, exps, factors, to_link, to_chip, deltas, query_t):
+def rim_kernel(
+    q, low, high, grad_t, attn_t, exps, factors, before, to_link, to_chip, deltas, query_t
+):
     blocks = q.shape[0] // BLK
     first_core = at_core() == 0
     parts = {}
@@ -202,7 +204,7 @@
     after[...] = jnp.zeros_like(after)
 
 
-def halves_kernel(mine, other, before, *outs):
+def halves_kernel(mine, other, *outs):
     pieces, after = outs[:-1], outs[-1]
     at_dp = lax.axis_index("dp")
     cols = pieces[0].shape[2]
@@ -219,13 +221,14 @@
 
 
 def chips_kernel(*refs):
-    parts, outs = refs[: lax.axis_size("dp")], refs[lax.axis_size("dp") + 3 :]
+    parts, outs = refs[: lax.axis_size("dp")], refs[lax.axis_size("dp") + 1 :]
     chip = lax.div(lax.axis_index("ctx"), 2)
     for s, out in enumerate(outs):
         out[...] = total([part[chip ^ s] for part in parts]).astype(BF16)
 
 
-def rim_sum_kernel(k_own, v_own, from_link, from_chip, before, k_grad, v_grad):
+def last_kernel(k_own, v_own, from_link, from_chip, *refs):
+    pieces, (k_grad, v_grad, weight_grad) = refs[:-3], refs[-3:]
     tokens = k_own.shape[0]
     first_core = at_core() == 0
     for which, (own, grad) in enumerate(((k_own, k_grad), (v_own, v_grad))):
@@ -240,17 +243,13 @@
             if tokens > 2 * RIM:
                 grad[RIM : tokens - RIM] = own[RIM : tokens - RIM].astype(BF16)
             grad[tokens - RIM :] = (own[tokens - RIM :] + high).astype(BF16)
-
-
-def columns_kernel(*refs):
-    pieces, out = refs[:-1], refs[-1]
     at_dp = lax.axis_index("dp")
     cols = pieces[0].shape[1]
     for d in range(len(pieces)):
         value = pieces[0][...]
         for s in range(1, len(pieces)):
             value = jnp.where((at_dp ^ s) == d, pieces[s][...], value)
-        out[:, d * cols : (d + 1) * cols] = value.astype(F32)
+        weight_grad[:, d * cols : (d + 1) * cols] = value.astype(F32)
 
 
 def vmem(*shape, dtype=BF16):
@@ -271,7 +270,7 @@
         in_specs=[in_smem] * len(masks) + [in_vmem] * len(args),
         out_specs=[in_vmem] * len(outs),
         compiler_params=pltpu.CompilerParams(vmem_limit_bytes=24 * 1024 * 1024),
-        cost_estimate=pl.CostEstimate(flops=flops, bytes_accessed=4 << 20, transcendentals=0),
+        cost_estimate=pl.CostEstimate(flops=flops, bytes_accessed=flops // 250, transcendentals=0),
     )(*masks, *args)
 
 
@@ -339,6 +338,12 @@
 
     other = lax.ppermute(other, "ctx", swap(ctx, 1))
     other = pltpu.with_memory_space_constraint(other, pltpu.VMEM)
+    *halves, after = call(
+        halves_kernel,
+        [vmem(chips, rows, cols)] * dp + [vmem(8, 128, dtype=F32)],
+        10**6,
+        mine, other,
+    )
     to_link, to_chip, deltas, rim_t = call(
         rim_kernel,
         [
@@ -347,14 +352,8 @@
             vmem(groups, 2 * BLK, dtype=F32),
             vmem(feats, tokens, dtype=F32),
         ],
-        10**9,
-        q, low, high, grad_t, attn_t, rim_exps, factors,
-    )
-    *halves, after = call(
-        halves_kernel,
-        [vmem(chips, rows, cols)] * dp + [vmem(8, 128, dtype=F32)],
         10**6,
-        mine, other, deltas,
+        q, low, high, grad_t, attn_t, rim_exps, factors, after,
     )
     grad_link = lax.ppermute(to_link, "ctx", over_links(ctx))
     grad_chip = lax.ppermute(to_chip, "ctx", swap(ctx, 1))
@@ -368,25 +367,24 @@
             hbm(tokens, width),
             vmem(8, 128, dtype=F32),
         ],
-        2 * 10**9,
+        10**6,
         q, k, v, grad_t, attn_t, own_exps, factors, deltas, rim_t, w_out, after,
     )
 
     halves = [halves[0]] + [lax.ppermute(halves[s], "dp", swap(dp, s)) for s in range(1, dp)]
-    quarters = call(chips_kernel, [vmem(rows, cols)] * chips, 10**6, *halves, after, grad_link, grad_chip)
-    k_grad, v_grad = call(
-        rim_sum_kernel,
-        [hbm(tokens, feats), hbm(tokens, feats)],
-        10**6,
-        k_own, v_own, grad_link, grad_chip, quarters[0],
-    )
+    quarters = call(chips_kernel, [vmem(rows, cols)] * chips, 10**6, *halves, after)
     piece = total(
         [quarters[0]]
         + [lax.ppermute(quarters[s], "ctx", swap(ctx, 2 * s)) for s in range(1, chips)]
     )
     piece = (piece * (dp * tokens * ctx) ** (-0.5)).astype(BF16)
     pieces = [piece] + [lax.ppermute(piece, "dp", swap(dp, s)) for s in range(1, dp)]
-    (weight_grad,) = call(columns_kernel, [hbm(rows, width, dtype=F32)], 10**6, *pieces)
+    k_grad, v_grad, weight_grad = call(
+        last_kernel,
+        [hbm(tokens, feats), hbm(tokens, feats), hbm(rows, width, dtype=F32)],
+        10**6,
+        k_own, v_own, grad_link, grad_chip, *pieces,
+    )
     return (output[None], q_grad[None], k_grad[None], v_grad[None], weight_grad)
 
 

time: 45 us -> 44 us (0.978)
  starting transfers between devices: 19.5 us -> 16.9 us
  waiting for transfers between devices: 9.69 us -> 11.9 us
  Pallas kernels: 12.2 us -> 11.6 us
    ppermute x1, starting transfers between devices: 3.3 us -> 0.01 us  [body(): grad_link = lax.ppermute(to_link, 'ctx', over_links(ctx))]
    ppermute x1, waiting for transfers between devices: 0.01 us -> 1.9 us  [body(): other = lax.ppermute(other, 'ctx', swap(ctx, 1))]
    ppermute x3, waiting for transfers between devices: 2.88 us -> 1.48 us  [body(): lax.ppermute(halves[s], 'dp', swap(dp, s))]
    ppermute x3, waiting for transfers between devices: 3.15 us -> 4.08 us  [body(): lax.ppermute(quarters[s], 'ctx', swap(ctx, 2 * s))]
    ppermute x3, waiting for transfers between devices: 2.22 us -> 3.12 us  [body(): lax.ppermute(piece, 'dp', swap(dp, s))]
    pallas_call x8 -> x7, Pallas kernels: 12.2 us -> 11.6 us  [call(): pl.pallas_call(kernel, out_shape=outs, in_specs=[in_smem] * len(masks) +...]
    ppermute x3, starting transfers between devices: 3.55 us -> 4.16 us  [body(): lax.ppermute(halves[s], 'dp', swap(dp, s))]
  transfers between devices with their start and end apart: 14 -> 14, of which waited for: 7 -> 8; matrix products, arithmetic and copies ran while one was open for 0% -> 0% of each run, Pallas kernels for 21% -> 19%
where the time goes in v6:
time: 44 us; the launch traced here: 43.8 us
  starting transfers between devices  16.9 us (38%)
  waiting for transfers between devices  11.9 us (27%)
  Pallas kernels  11.6 us (26%)
  local copies, waits for them, and re-layouts  2.49 us (6%)
  between operations  0.82 us (2%)
    pallas_call x7, Pallas kernels, call(): pl.pallas_call(kernel, out_shape=outs, in_specs=[in_smem] * len(masks) +...  11.6 us
    ppermute x1, starting transfers between devices, body(): from_link = lax.ppermute(rim(link_row), 'ctx', over_links(ctx))  4.55 us
    ppermute x3, starting transfers between devices, body(): lax.ppermute(quarters[s], 'ctx', swap(ctx, 2 * s))  4.44 us
    ppermute x3, starting transfers between devices, body(): lax.ppermute(halves[s], 'dp', swap(dp, s))  4.16 us
    ppermute x3, waiting for transfers between devices, body(): lax.ppermute(quarters[s], 'ctx', swap(ctx, 2 * s))  4.08 us
    ppermute x3, starting transfers between devices, body(): lax.ppermute(piece, 'dp', swap(dp, s))  3.55 us
    ppermute x3, waiting for transfers between devices, body(): lax.ppermute(piece, 'dp', swap(dp, s))  3.12 us
    ppermute x1, waiting for transfers between devices, body(): other = lax.ppermute(other, 'ctx', swap(ctx, 1))  1.9 us
  transfers between devices with their start and end apart: 14, of which 8 were waited for; matrix products, arithmetic and copies ran while one was open for 0% of the time, Pallas kernels for 19%

profile of v6, /device:TPU:0, one launch (start us, length us, event | category | flops | bytes accessed | tf_op | source)
XLA Modules:
  0.0 43.8 jit_solution(10869431839721344716)
XLA Ops:
  0.6 0.0 copy-start
  0.6 0.0 copy-start.3
  0.7 0.0 copy-start.2
  0.7 0.0 copy-start.4
  0.7 0.0 copy-start.1
  0.7 1.3 %constant_dynamic-slice_fusion = (bf16[1,128,512]{2,1,0:T(8,128)(2,1)S(1)}, bf16[1,128,512]{2,1,0:T(8,128)(2,1)S(1)}, bf16[1,128,512]{2,1,0:T(8,128)(2,1)S(1)}, bf16[1,128,512]{2,1,0:T(8,128)(2,1)S(1)}) fusion(bf16[1,256,512]{2,1,0:T(8,128)(2,1)} %param.8, s32[]{:T(128)S(6)} %select_n.34, s32[]{:T(128)S(6)} %select_n.33, bf16[1,256,512]{2,1,0:T(8,128)(2,1)} %param.7), kind=kLoop, calls=%fused_computation.5 | loop fusion | bytes 1048584 | tf_op jit(solution)/shard_map/dynamic_slice | solution.py:305
  2.0 4.6 %collective-permute-start = (bf16[2,128,512]{2,1,0:T(8,128)(2,1)S(1)}, bf16[2,128,512]{2,1,0:T(8,128)(2,1)S(1)}, u32[]{:S(2)}, u32[]{:S(2)}) collective-permute-start(bf16[2,128,512]{2,1,0:T(8,128)(2,1)S(1)} %pad_maximum_fusion), channel_id=1, source_target_pairs={{0,7},{1,2},{2,1},{3,4},{4,3},{5,6},{6,5},{7,0},{8,15},{9,10},{10,... | collective-permute-start | bytes 786440 | tf_op jit(solution)/shard_map/ppermute | solution.py:307
  6.6 0.1 collective-permute-start.1
  6.7 0.0 copy-done
  6.7 0.1 constant_dynamic-slice_fusion.4
  6.8 0.1 copy.11
  6.9 0.0 copy-done.3
  6.9 0.0 copy-done.2
  6.9 0.0 copy-start.5
  6.9 1.0 %copy-done.5 = bf16[1,256,1024]{2,1,0:T(8,128)(2,1)S(1)} copy-done((bf16[1,256,1024]{2,1,0:T(8,128)(2,1)S(1)}, bf16[1,256,1024]{2,1,0:T(8,128)(2,1)}, u32[]{:S(2)}) %copy-start.5) | copy-done | bytes 524312
  7.9 3.3 %shard_map.101 = (f32[512,256]{1,0:T(8,128)S(1)}, f32[2,8,256]{2,1,0:T(8,128)S(1)}, f32[8,256,256]{2,1,0:T(8,128)S(1)}, bf16[512,256]{1,0:T(8,128)(2,1)S(1)}) custom-call(s32[2,3]{1,0:T(2,128)S(1)} %bitcast.17, bf16[256,512]{1,0:T(8,128)(2,1)S(1)} %bitcast.9, bf16[256,512]{1,0:T(8,128)(2,1)S(1)} %bitcast.13, bf16[256,512]{1,0:T(8,128)(2,1)S(1)} %bitcast.15, ...), custom_call_target="tpu_custom_call" | custom-call | flops 1000000000 | bytes 4000000 | tf_op jit(solution)/shard_map/pallas_call | solution.py:267
  11.3 1.3 %collective-permute-done = bf16[2,128,512]{2,1,0:T(8,128)(2,1)S(1)} collective-permute-done((bf16[2,128,512]{2,1,0:T(8,128)(2,1)S(1)}, bf16[2,128,512]{2,1,0:T(8,128)(2,1)S(1)}, u32[]{:S(2)}, u32[]{:S(2)}) %collective-permute-start) | collective-permute-done | bytes 262176 | tf_op jit(solution)/shard_map/ppermute | solution.py:307
  12.6 0.0 collective-permute-done.1
  12.6 1.8 %shard_map.102 = (bf16[512,256]{1,0:T(8,128)(2,1)S(1)}, bf16[4,64,1024]{2,1,0:T(8,128)(2,1)S(1)}, bf16[4,64,1024]{2,1,0:T(8,128)(2,1)S(1)}, f32[2,4,128,256]{3,2,1,0:T(8,128)S(1)}, f32[2,8,256]{2,1,0:T(8,128)S(1)}) custom-call(s32[2,3]{1,0:T(2,128)S(1)} %bitcast.18, bf16[256,512]{1,0:T(8,128)(2,1)S(1)} %bitcast.10, ...), custom_call_target="tpu_custom_call" | custom-call | flops 1000000000 | bytes 4000000 | tf_op jit(solution)/shard_map/pallas_call | solution.py:267
  14.5 0.1 collective-permute-start.2
  14.6 1.9 %collective-permute-done.2.other = bf16[4,64,1024]{2,1,0:T(8,128)(2,1)S(1)} collective-permute-done((bf16[4,64,1024]{2,1,0:T(8,128)(2,1)S(1)}, bf16[4,64,1024]{2,1,0:T(8,128)(2,1)S(1)}, u32[]{:S(2)}, u32[]{:S(2)}) %collective-permute-start.2) | collective-permute-done | bytes 524320 | tf_op jit(solution)/shard_map/ppermute | solution.py:339
  16.5 0.3 shard_map.103
  16.8 2.6 %collective-permute-start.5 = (bf16[4,64,256]{2,1,0:T(8,128)(2,1)S(1)}, bf16[4,64,256]{2,1,0:T(8,128)(2,1)S(1)}, u32[]{:S(2)}, u32[]{:S(2)}) collective-permute-start(bf16[4,64,256]{2,1,0:T(8,128)(2,1)S(1)} %get-tuple-element.54), channel_id=1, source_target_pairs={{0,8},{8,0},{16,24},{24,16},{1,9},{9,1},{17,25},{25,17},{2,10},{10... | collective-permute-start | bytes 393224 | tf_op jit(solution)/shard_map/ppermute | solution.py:374
  19.4 1.5 %collective-permute-start.6 = (bf16[4,64,256]{2,1,0:T(8,128)(2,1)S(1)}, bf16[4,64,256]{2,1,0:T(8,128)(2,1)S(1)}, u32[]{:S(2)}, u32[]{:S(2)}) collective-permute-start(bf16[4,64,256]{2,1,0:T(8,128)(2,1)S(1)} %get-tuple-element.55), channel_id=1, source_target_pairs={{0,16},{8,24},{16,0},{24,8},{1,17},{9,25},{17,1},{25,9},{2,18},{10... | collective-permute-start | bytes 393224 | tf_op jit(solution)/shard_map/ppermute | solution.py:374
  20.9 0.0 collective-permute-start.7
  20.9 1.5 %shard_map.104 = (bf16[2,128,512]{2,1,0:T(8,128)(2,1)S(1)}, bf16[2,128,512]{2,1,0:T(8,128)(2,1)S(1)}, f32[8,256]{1,0:T(8,128)S(1)}, f32[512,256]{1,0:T(8,128)S(1)}) custom-call(bf16[256,512]{1,0:T(8,128)(2,1)S(1)} %bitcast.11, bf16[2,128,512]{2,1,0:T(8,128)(2,1)S(1)} %get-tuple-element.66.low, bf16[2,128,512]{2,1,0:T(8,128)(2,1)S(1)} %get-tuple-element.65.high, ...), custom_call_target="tpu_custom_call" | custom-call | flops 1000000 | bytes 4000 | tf_op jit(solution)/shard_map/pallas_call | solution.py:267
  22.4 3.6 %shard_map.105 = (bf16[256,512]{1,0:T(8,128)(2,1)}, f32[256,512]{1,0:T(8,128)S(1)}, f32[256,512]{1,0:T(8,128)S(1)}, bf16[256,1024]{1,0:T(8,128)(2,1)}, f32[8,128]{1,0:T(8,128)S(1)}) custom-call(bf16[256,512]{1,0:T(8,128)(2,1)S(1)} %bitcast.12, bf16[256,512]{1,0:T(8,128)(2,1)S(1)} %bitcast.14, bf16[256,512]{1,0:T(8,128)(2,1)S(1)} %bitcast.16, ...), custom_call_target="tpu_custom_call" | custom-call | flops 1000000 | bytes 4000 | tf_op jit(solution)/shard_map/pallas_call | solution.py:267
  26.0 0.0 collective-permute-done.5.refs_1_
  26.0 1.5 %collective-permute-done.6.refs_2_ = bf16[4,64,256]{2,1,0:T(8,128)(2,1)S(1)} collective-permute-done((bf16[4,64,256]{2,1,0:T(8,128)(2,1)S(1)}, bf16[4,64,256]{2,1,0:T(8,128)(2,1)S(1)}, u32[]{:S(2)}, u32[]{:S(2)}) %collective-permute-start.6) | collective-permute-done | bytes 131104 | tf_op jit(solution)/shard_map/ppermute | solution.py:374
  27.5 0.0 collective-permute-done.7.refs_3_
  27.5 0.1 shard_map.106
  27.5 0.1 collective-permute-start.8
  27.6 2.6 %collective-permute-start.9 = (bf16[64,256]{1,0:T(8,128)(2,1)S(1)}, bf16[64,256]{1,0:T(8,128)(2,1)S(1)}, u32[]{:S(2)}, u32[]{:S(2)}) collective-permute-start(bf16[64,256]{1,0:T(8,128)(2,1)S(1)} %get-tuple-element.60), channel_id=1, source_target_pairs={{0,4},{1,5},{2,6},{3,7},{4,0},{5,1},{6,2},{7,3},{8,12},{9,13},{10,... | collective-permute-start | bytes 98312 | tf_op jit(solution)/shard_map/ppermute | solution.py:378
  30.3 1.8 %collective-permute-start.10 = (bf16[64,256]{1,0:T(8,128)(2,1)S(1)}, bf16[64,256]{1,0:T(8,128)(2,1)S(1)}, u32[]{:S(2)}, u32[]{:S(2)}) collective-permute-start(bf16[64,256]{1,0:T(8,128)(2,1)S(1)} %get-tuple-element.61), channel_id=1, source_target_pairs={{0,6},{1,7},{2,4},{3,5},{4,2},{5,3},{6,0},{7,1},{8,14},{9,15},{10,... | collective-permute-start | bytes 98312 | tf_op jit(solution)/shard_map/ppermute | solution.py:378
  32.0 0.0 collective-permute-start.3
  32.0 0.0 collective-permute-start.4
  32.0 0.0 collective-permute-done.8
  32.0 0.5 %collective-permute-done.9 = bf16[64,256]{1,0:T(8,128)(2,1)S(1)} collective-permute-done((bf16[64,256]{1,0:T(8,128)(2,1)S(1)}, bf16[64,256]{1,0:T(8,128)(2,1)S(1)}, u32[]{:S(2)}, u32[]{:S(2)}) %collective-permute-start.9) | collective-permute-done | bytes 32800 | tf_op jit(solution)/shard_map/ppermute | solution.py:378
  32.5 3.6 %collective-permute-done.10 = bf16[64,256]{1,0:T(8,128)(2,1)S(1)} collective-permute-done((bf16[64,256]{1,0:T(8,128)(2,1)S(1)}, bf16[64,256]{1,0:T(8,128)(2,1)S(1)}, u32[]{:S(2)}, u32[]{:S(2)}) %collective-permute-start.10) | collective-permute-done | bytes 32800 | tf_op jit(solution)/shard_map/ppermute | solution.py:378
  36.1 1.6 %collective-permute-start.13 = (bf16[64,256]{1,0:T(8,128)(2,1)S(1)}, bf16[64,256]{1,0:T(8,128)(2,1)S(1)}, u32[]{:S(2)}, u32[]{:S(2)}) collective-permute-start(bf16[64,256]{1,0:T(8,128)(2,1)S(1)} %multiply_convert_fusion.refs_0_), channel_id=1, source_target_pairs={{0,24},{8,16},{16,8},{24,0},{1,25},{9,17},{17,9},{25,1},{2,26},{10... | collective-permute-start | bytes 98312 | tf_op jit(solution)/shard_map/ppermute | solution.py:381
  37.7 1.2 %collective-permute-start.12 = (bf16[64,256]{1,0:T(8,128)(2,1)S(1)}, bf16[64,256]{1,0:T(8,128)(2,1)S(1)}, u32[]{:S(2)}, u32[]{:S(2)}) collective-permute-start(bf16[64,256]{1,0:T(8,128)(2,1)S(1)} %multiply_convert_fusion.refs_0_), channel_id=1, source_target_pairs={{0,16},{8,24},{16,0},{24,8},{1,17},{9,25},{17,1},{25,9},{2,18},{10... | collective-permute-start | bytes 98312 | tf_op jit(solution)/shard_map/ppermute | solution.py:381
  38.9 0.8 %collective-permute-start.11 = (bf16[64,256]{1,0:T(8,128)(2,1)S(1)}, bf16[64,256]{1,0:T(8,128)(2,1)S(1)}, u32[]{:S(2)}, u32[]{:S(2)}) collective-permute-start(bf16[64,256]{1,0:T(8,128)(2,1)S(1)} %multiply_convert_fusion.refs_0_), channel_id=1, source_target_pairs={{0,8},{8,0},{16,24},{24,16},{1,9},{9,1},{17,25},{25,17},{2,10},{10... | collective-permute-start | bytes 98312 | tf_op jit(solution)/shard_map/ppermute | solution.py:381
  39.7 1.3 %collective-permute-done.13.refs_3_ = bf16[64,256]{1,0:T(8,128)(2,1)S(1)} collective-permute-done((bf16[64,256]{1,0:T(8,128)(2,1)S(1)}, bf16[64,256]{1,0:T(8,128)(2,1)S(1)}, u32[]{:S(2)}, u32[]{:S(2)}) %collective-permute-start.13) | collective-permute-done | bytes 32800 | tf_op jit(solution)/shard_map/ppermute | solution.py:381
  41.0 0.6 %collective-permute-done.12.refs_2_ = bf16[64,256]{1,0:T(8,128)(2,1)S(1)} collective-permute-done((bf16[64,256]{1,0:T(8,128)(2,1)S(1)}, bf16[64,256]{1,0:T(8,128)(2,1)S(1)}, u32[]{:S(2)}, u32[]{:S(2)}) %collective-permute-start.12) | collective-permute-done | bytes 32800 | tf_op jit(solution)/shard_map/ppermute | solution.py:381
  41.6 1.2 %collective-permute-done.11.refs_1_ = bf16[64,256]{1,0:T(8,128)(2,1)S(1)} collective-permute-done((bf16[64,256]{1,0:T(8,128)(2,1)S(1)}, bf16[64,256]{1,0:T(8,128)(2,1)S(1)}, u32[]{:S(2)}, u32[]{:S(2)}) %collective-permute-start.11) | collective-permute-done | bytes 32800 | tf_op jit(solution)/shard_map/ppermute | solution.py:381
  42.8 0.0 collective-permute-done.3.from_link
  42.8 0.0 collective-permute-done.4.from_chip
  42.8 1.0 %shard_map.107 = (bf16[256,512]{1,0:T(8,128)(2,1)}, bf16[256,512]{1,0:T(8,128)(2,1)}, f32[64,1024]{1,0:T(8,128)}) custom-call(f32[256,512]{1,0:T(8,128)S(1)} %get-tuple-element.49.k_own, f32[256,512]{1,0:T(8,128)S(1)} %get-tuple-element.50.v_own, bf16[2,128,512]{2,1,0:T(8,128)(2,1)S(1)} %collective-permute-done.3.from_link, ...), custom_call_target="tpu_custom_call" | custom-call | flops 1000000 | bytes 4000 | tf_op jit(solution)/shard_map/pallas_call | solution.py:267
  (6 shorter events, 0.1 us)
Async XLA Ops:
  0.6 6.0 %copy-start = (s32[1,16,3]{1,0,2:T(1,128)S(1)}, s32[1,16,3]{1,0,2:T(1,128)}, u32[]{:S(2)}) copy-start(s32[1,16,3]{1,0,2:T(1,128)} %param.11) | copy-start | bytes 580
  0.6 6.2 %copy-start.3 = (bf16[1,256,512]{2,1,0:T(8,128)(2,1)S(1)}, bf16[1,256,512]{2,1,0:T(8,128)(2,1)}, u32[]{:S(2)}) copy-start(bf16[1,256,512]{2,1,0:T(8,128)(2,1)} %param.8) | copy-start | bytes 786436
  0.7 6.2 %copy-start.2 = (bf16[1,256,512]{2,1,0:T(8,128)(2,1)S(1)}, bf16[1,256,512]{2,1,0:T(8,128)(2,1)}, u32[]{:S(2)}) copy-start(bf16[1,256,512]{2,1,0:T(8,128)(2,1)} %param.7) | copy-start | bytes 786436
  0.7 6.2 %copy-start.4 = (bf16[512,1024]{1,0:T(8,128)(2,1)S(1)}, bf16[512,1024]{1,0:T(8,128)(2,1)}, u32[]{:S(2)}) copy-start(bf16[512,1024]{1,0:T(8,128)(2,1)} %w_out.3) | copy-start | bytes 3145732
  0.7 6.2 %copy-start.1 = (bf16[1,256,512]{2,1,0:T(8,128)(2,1)S(1)}, bf16[1,256,512]{2,1,0:T(8,128)(2,1)}, u32[]{:S(2)}) copy-start(bf16[1,256,512]{2,1,0:T(8,128)(2,1)} %param.6) | copy-start | bytes 786436
  2.0 10.6 %collective-permute-start = (bf16[2,128,512]{2,1,0:T(8,128)(2,1)S(1)}, bf16[2,128,512]{2,1,0:T(8,128)(2,1)S(1)}, u32[]{:S(2)}, u32[]{:S(2)}) collective-permute-start(bf16[2,128,512]{2,1,0:T(8,128)(2,1)S(1)} %pad_maximum_fusion), channel_id=1, source_target_pairs={{0,7},{1,2},{2,1},{3,4},{4,3},{5,6},{6,5},{7,0},{8,15},{9,10},{10,... | collective-permute-start | bytes 786440 | tf_op jit(solution)/shard_map/ppermute | solution.py:307
  6.6 6.0 %collective-permute-start.1 = (bf16[2,128,512]{2,1,0:T(8,128)(2,1)S(1)}, bf16[2,128,512]{2,1,0:T(8,128)(2,1)S(1)}, u32[]{:S(2)}, u32[]{:S(2)}) collective-permute-start(bf16[2,128,512]{2,1,0:T(8,128)(2,1)S(1)} %pad_maximum_fusion.1), channel_id=1, source_target_pairs={{0,1},{1,0},{2,3},{3,2},{4,5},{5,4},{6,7},{7,6},{8,9},{9,8},{10,11... | collective-permute-start | bytes 786440 | tf_op jit(solution)/shard_map/ppermute | solution.py:308
  6.9 1.0 %copy-start.5 = (bf16[1,256,1024]{2,1,0:T(8,128)(2,1)S(1)}, bf16[1,256,1024]{2,1,0:T(8,128)(2,1)}, u32[]{:S(2)}) copy-start(bf16[1,256,1024]{2,1,0:T(8,128)(2,1)} %param.9) | copy-start | bytes 1572868
  14.5 2.0 %collective-permute-start.2 = (bf16[4,64,1024]{2,1,0:T(8,128)(2,1)S(1)}, bf16[4,64,1024]{2,1,0:T(8,128)(2,1)S(1)}, u32[]{:S(2)}, u32[]{:S(2)}) collective-permute-start(bf16[4,64,1024]{2,1,0:T(8,128)(2,1)S(1)} %get-tuple-element.43), channel_id=1, source_target_pairs={{0,1},{1,0},{2,3},{3,2},{4,5},{5,4},{6,7},{7,6},{8,9},{9,8},{10,11... | collective-permute-start | bytes 1572872 | tf_op jit(solution)/shard_map/ppermute | solution.py:339
  16.8 9.2 %collective-permute-start.5 = (bf16[4,64,256]{2,1,0:T(8,128)(2,1)S(1)}, bf16[4,64,256]{2,1,0:T(8,128)(2,1)S(1)}, u32[]{:S(2)}, u32[]{:S(2)}) collective-permute-start(bf16[4,64,256]{2,1,0:T(8,128)(2,1)S(1)} %get-tuple-element.54), channel_id=1, source_target_pairs={{0,8},{8,0},{16,24},{24,16},{1,9},{9,1},{17,25},{25,17},{2,10},{10... | collective-permute-start | bytes 393224 | tf_op jit(solution)/shard_map/ppermute | solution.py:374
  19.4 8.1 %collective-permute-start.6 = (bf16[4,64,256]{2,1,0:T(8,128)(2,1)S(1)}, bf16[4,64,256]{2,1,0:T(8,128)(2,1)S(1)}, u32[]{:S(2)}, u32[]{:S(2)}) collective-permute-start(bf16[4,64,256]{2,1,0:T(8,128)(2,1)S(1)} %get-tuple-element.55), channel_id=1, source_target_pairs={{0,16},{8,24},{16,0},{24,8},{1,17},{9,25},{17,1},{25,9},{2,18},{10... | collective-permute-start | bytes 393224 | tf_op jit(solution)/shard_map/ppermute | solution.py:374
  20.9 6.6 %collective-permute-start.7 = (bf16[4,64,256]{2,1,0:T(8,128)(2,1)S(1)}, bf16[4,64,256]{2,1,0:T(8,128)(2,1)S(1)}, u32[]{:S(2)}, u32[]{:S(2)}) collective-permute-start(bf16[4,64,256]{2,1,0:T(8,128)(2,1)S(1)} %get-tuple-element.56), channel_id=1, source_target_pairs={{0,24},{8,16},{16,8},{24,0},{1,25},{9,17},{17,9},{25,1},{2,26},{10... | collective-permute-start | bytes 393224 | tf_op jit(solution)/shard_map/ppermute | solution.py:374
  27.5 4.5 %collective-permute-start.8 = (bf16[64,256]{1,0:T(8,128)(2,1)S(1)}, bf16[64,256]{1,0:T(8,128)(2,1)S(1)}, u32[]{:S(2)}, u32[]{:S(2)}) collective-permute-start(bf16[64,256]{1,0:T(8,128)(2,1)S(1)} %get-tuple-element.59), channel_id=1, source_target_pairs={{0,2},{1,3},{2,0},{3,1},{4,6},{5,7},{6,4},{7,5},{8,10},{9,11},{10,... | collective-permute-start | bytes 98312 | tf_op jit(solution)/shard_map/ppermute | solution.py:378
  27.6 4.9 %collective-permute-start.9 = (bf16[64,256]{1,0:T(8,128)(2,1)S(1)}, bf16[64,256]{1,0:T(8,128)(2,1)S(1)}, u32[]{:S(2)}, u32[]{:S(2)}) collective-permute-start(bf16[64,256]{1,0:T(8,128)(2,1)S(1)} %get-tuple-element.60), channel_id=1, source_target_pairs={{0,4},{1,5},{2,6},{3,7},{4,0},{5,1},{6,2},{7,3},{8,12},{9,13},{10,... | collective-permute-start | bytes 98312 | tf_op jit(solution)/shard_map/ppermute | solution.py:378
  30.3 5.8 %collective-permute-start.10 = (bf16[64,256]{1,0:T(8,128)(2,1)S(1)}, bf16[64,256]{1,0:T(8,128)(2,1)S(1)}, u32[]{:S(2)}, u32[]{:S(2)}) collective-permute-start(bf16[64,256]{1,0:T(8,128)(2,1)S(1)} %get-tuple-element.61), channel_id=1, source_target_pairs={{0,6},{1,7},{2,4},{3,5},{4,2},{5,3},{6,0},{7,1},{8,14},{9,15},{10,... | collective-permute-start | bytes 98312 | tf_op jit(solution)/shard_map/ppermute | solution.py:378
  32.0 10.8 %collective-permute-start.3 = (bf16[2,128,512]{2,1,0:T(8,128)(2,1)S(1)}, bf16[2,128,512]{2,1,0:T(8,128)(2,1)S(1)}, u32[]{:S(2)}, u32[]{:S(2)}) collective-permute-start(bf16[2,128,512]{2,1,0:T(8,128)(2,1)S(1)} %get-tuple-element.51), channel_id=1, source_target_pairs={{0,7},{1,2},{2,1},{3,4},{4,3},{5,6},{6,5},{7,0},{8,15},{9,10},{10,... | collective-permute-start | bytes 786440 | tf_op jit(solution)/shard_map/ppermute | solution.py:358
  32.0 10.8 %collective-permute-start.4 = (bf16[2,128,512]{2,1,0:T(8,128)(2,1)S(1)}, bf16[2,128,512]{2,1,0:T(8,128)(2,1)S(1)}, u32[]{:S(2)}, u32[]{:S(2)}) collective-permute-start(bf16[2,128,512]{2,1,0:T(8,128)(2,1)S(1)} %get-tuple-element.52), channel_id=1, source_target_pairs={{0,1},{1,0},{2,3},{3,2},{4,5},{5,4},{6,7},{7,6},{8,9},{9,8},{10,11... | collective-permute-start | bytes 786440 | tf_op jit(solution)/shard_map/ppermute | solution.py:359
  36.1 4.9 %collective-permute-start.13 = (bf16[64,256]{1,0:T(8,128)(2,1)S(1)}, bf16[64,256]{1,0:T(8,128)(2,1)S(1)}, u32[]{:S(2)}, u32[]{:S(2)}) collective-permute-start(bf16[64,256]{1,0:T(8,128)(2,1)S(1)} %multiply_convert_fusion.refs_0_), channel_id=1, source_target_pairs={{0,24},{8,16},{16,8},{24,0},{1,25},{9,17},{17,9},{25,1},{2,26},{10... | collective-permute-start | bytes 98312 | tf_op jit(solution)/shard_map/ppermute | solution.py:381
  37.7 3.9 %collective-permute-start.12 = (bf16[64,256]{1,0:T(8,128)(2,1)S(1)}, bf16[64,256]{1,0:T(8,128)(2,1)S(1)}, u32[]{:S(2)}, u32[]{:S(2)}) collective-permute-start(bf16[64,256]{1,0:T(8,128)(2,1)S(1)} %multiply_convert_fusion.refs_0_), channel_id=1, source_target_pairs={{0,16},{8,24},{16,0},{24,8},{1,17},{9,25},{17,1},{25,9},{2,18},{10... | collective-permute-start | bytes 98312 | tf_op jit(solution)/shard_map/ppermute | solution.py:381
  38.9 3.9 %collective-permute-start.11 = (bf16[64,256]{1,0:T(8,128)(2,1)S(1)}, bf16[64,256]{1,0:T(8,128)(2,1)S(1)}, u32[]{:S(2)}, u32[]{:S(2)}) collective-permute-start(bf16[64,256]{1,0:T(8,128)(2,1)S(1)} %multiply_convert_fusion.refs_0_), channel_id=1, source_target_pairs={{0,8},{8,0},{16,24},{24,16},{1,9},{9,1},{17,25},{25,17},{2,10},{10... | collective-permute-start | bytes 98312 | tf_op jit(solution)/shard_map/ppermute | solution.py:381

commit v7 on v6

--- a/solution.py
+++ b/solution.py
@@ -97,7 +97,9 @@
     grad_t[...] = dot(w_out[...], g[...], ((1,), (1,))).astype(BF16)
 
 
-def forward_kernel(mask, q, low, high, own_t, stats, g, attn_t, mine, other, exps, factors):
+def forward_kernel(
+    mask, q, low, high, own_t, stats, before, attn_t, mine, other, exps, factors
+):
     blocks = q.shape[0] // BLK
     sides = (low, high)
     for b, rows, cols, at in pairs_of(blocks):
@@ -124,19 +126,27 @@
         if both is not None:
             attn = attn + own_features(both) * spread(share)
         attn_t[cols, rows] = attn.astype(BF16)
-    part = dot(attn_t[...], g[...], ((1,), (0,))).astype(BF16)
     core = at_core()
     chips, rows, _ = mine.shape
     for c in range(2 * chips):
-        value = part[c * rows : (c + 1) * rows]
+        value = attn_t[c * rows : (c + 1) * rows]
 
         @pl.when(core == c % 2)
-        def _():
+        def _(c=c, value=value):
             mine[c // 2] = value
 
         @pl.when(core != c % 2)
-        def _():
+        def _(c=c, value=value):
             other[c // 2] = value
+
+
+def flat_dot(attn, g):
+    chips, rows, tokens = attn.shape
+    return dot(attn[...].reshape(chips * rows, tokens), g[...], ((1,), (0,)))
+
+
+def product_kernel(mine, g, product):
+    product[...] = flat_dot(mine, g)
 
 
 def backward(probs, delta, k, v, q2, g2_t):
@@ -204,13 +214,13 @@
     after[...] = jnp.zeros_like(after)
 
 
-def halves_kernel(mine, other, *outs):
+def halves_kernel(product, other, g, *outs):
     pieces, after = outs[:-1], outs[-1]
     at_dp = lax.axis_index("dp")
-    cols = pieces[0].shape[2]
+    chips, rows, cols = pieces[0].shape
+    both = (product[...] + flat_dot(other, g)).astype(BF16)
     for d in range(len(pieces)):
-        at = slice(d * cols, (d + 1) * cols)
-        value = (mine[:, :, at].astype(F32) + other[:, :, at].astype(F32)).astype(BF16)
+        value = both[:, d * cols : (d + 1) * cols].reshape(chips, rows, cols)
         for s in range(len(pieces)):
 
             @pl.when((at_dp ^ s) == d)
@@ -306,6 +316,8 @@
 
     from_link = lax.ppermute(rim(link_row), "ctx", over_links(ctx))
     from_chip = lax.ppermute(rim(chip_row), "ctx", swap(ctx, 1))
+    sibling_g = lax.ppermute(g, "ctx", swap(ctx, 1))
+    sibling_g = pltpu.with_memory_space_constraint(sibling_g, pltpu.VMEM)
     low = jnp.where(core == 0, from_link, from_chip)
     high = jnp.where(core == 0, from_chip, from_link)
 
@@ -326,23 +338,24 @@
         forward_kernel,
         [
             vmem(feats, tokens),
-            vmem(chips, rows, width),
-            vmem(chips, rows, width),
+            vmem(chips, rows, tokens),
+            vmem(chips, rows, tokens),
             vmem(2, PAIRS, RIM, 2 * BLK, dtype=F32),
             vmem(2, groups, 2 * BLK, dtype=F32),
         ],
         10**9,
-        q, low, high, own_t, stats, g,
+        q, low, high, own_t, stats, sibling_g,
         mask=mask,
     )
 
     other = lax.ppermute(other, "ctx", swap(ctx, 1))
     other = pltpu.with_memory_space_constraint(other, pltpu.VMEM)
+    (product,) = call(product_kernel, [vmem(chips * rows, width, dtype=F32)], 10**6, mine, g)
     *halves, after = call(
         halves_kernel,
         [vmem(chips, rows, cols)] * dp + [vmem(8, 128, dtype=F32)],
         10**6,
-        mine, other,
+        product, other, sibling_g,
     )
     to_link, to_chip, deltas, rim_t = call(
         rim_kernel,
@@ -375,7 +388,7 @@
     quarters = call(chips_kernel, [vmem(rows, cols)] * chips, 10**6, *halves, after)
     piece = total(
         [quarters[0]]
-        + [lax.ppermute(quarters[s], "ctx", swap(ctx, 2 * s)) for s in range(1, chips)]
+        + [lax.ppermute(quarters[s], "ctx", swap(ctx, 2 * s)) for s in range(chips - 1, 0, -1)]
     )
     piece = (piece * (dp * tokens * ctx) ** (-0.5)).astype(BF16)
     pieces = [piece] + [lax.ppermute(piece, "dp", swap(dp, s)) for s in range(1, dp)]

time: 44 us -> 42 us (0.955)
  waiting for transfers between devices: 11.9 us -> 9.22 us
  starting transfers between devices: 16.9 us -> 17.5 us
    ppermute x3, waiting for transfers between devices: 4.08 us -> 2.39 us  [body(): lax.ppermute(quarters[s], 'ctx', swap(ctx, 2 * s))]
    ppermute x1, waiting for transfers between devices: 1.9 us -> 1.02 us  [body(): other = lax.ppermute(other, 'ctx', swap(ctx, 1))]
    ppermute x1, starting transfers between devices: 0.07 us -> 0.57 us  [body(): from_chip = lax.ppermute(rim(chip_row), 'ctx', swap(ctx, 1))]
    ppermute x1, waiting for transfers between devices: 1.34 us -> 0.86 us  [body(): from_link = lax.ppermute(rim(link_row), 'ctx', over_links(ctx))]
    pallas_call x7 -> x8, Pallas kernels: 11.6 us -> 11.6 us  [call(): pl.pallas_call(kernel, out_shape=outs, in_specs=[in_smem] * len(masks) +...]
    unnamed x12 -> x14, local copies, waits for them, and re-layouts: 1.06 us -> 1.07 us
  transfers between devices with their start and end apart: 14 -> 15, of which waited for: 8 -> 9; matrix products, arithmetic and copies ran while one was open for 0% -> 1% of each run, Pallas kernels for 19% -> 21%
where the time goes in v7:
time: 42 us; the launch traced here: 41.8 us
  starting transfers between devices  17.5 us (42%)
  Pallas kernels  11.6 us (28%)
  waiting for transfers between devices  9.22 us (22%)
  local copies, waits for them, and re-layouts  2.5 us (6%)
  between operations  0.82 us (2%)
    pallas_call x8, Pallas kernels, call(): pl.pallas_call(kernel, out_shape=outs, in_specs=[in_smem] * len(masks) +...  11.6 us
    ppermute x1, starting transfers between devices, body(): from_link = lax.ppermute(rim(link_row), 'ctx', over_links(ctx))  4.55 us
    ppermute x3, starting transfers between devices, body(): lax.ppermute(quarters[s], 'ctx', swap(ctx, 2 * s))  4.45 us
    ppermute x3, starting transfers between devices, body(): lax.ppermute(halves[s], 'dp', swap(dp, s))  4.15 us
    ppermute x3, starting transfers between devices, body(): lax.ppermute(piece, 'dp', swap(dp, s))  3.55 us
    ppermute x3, waiting for transfers between devices, body(): lax.ppermute(piece, 'dp', swap(dp, s))  3.18 us
    ppermute x3, waiting for transfers between devices, body(): lax.ppermute(quarters[s], 'ctx', swap(ctx, 2 * s))  2.39 us
    ppermute x3, waiting for transfers between devices, body(): lax.ppermute(halves[s], 'dp', swap(dp, s))  1.49 us
  transfers between devices with their start and end apart: 15, of which 9 were waited for; matrix products, arithmetic and copies ran while one was open for 1% of the time, Pallas kernels for 21%

profile of v7, /device:TPU:0, one launch (start us, length us, event | category | flops | bytes accessed | tf_op | source)
XLA Modules:
  0.0 41.8 jit_solution(5529792807334947872)
XLA Ops:
  0.6 0.0 copy-start
  0.6 0.0 copy-start.3
  0.7 0.0 copy-start.2
  0.7 0.0 copy-start.4
  0.7 1.3 %constant_dynamic-slice_fusion = (bf16[1,128,512]{2,1,0:T(8,128)(2,1)S(1)}, bf16[1,128,512]{2,1,0:T(8,128)(2,1)S(1)}, bf16[1,128,512]{2,1,0:T(8,128)(2,1)S(1)}, bf16[1,128,512]{2,1,0:T(8,128)(2,1)S(1)}) fusion(bf16[1,256,512]{2,1,0:T(8,128)(2,1)} %param.8, s32[]{:T(128)S(6)} %select_n.34, s32[]{:T(128)S(6)} %select_n.33, bf16[1,256,512]{2,1,0:T(8,128)(2,1)} %param.7), kind=kLoop, calls=%fused_computation.5 | loop fusion | bytes 1048584 | tf_op jit(solution)/shard_map/dynamic_slice | solution.py:315
  2.0 4.6 %collective-permute-start = (bf16[2,128,512]{2,1,0:T(8,128)(2,1)S(1)}, bf16[2,128,512]{2,1,0:T(8,128)(2,1)S(1)}, u32[]{:S(2)}, u32[]{:S(2)}) collective-permute-start(bf16[2,128,512]{2,1,0:T(8,128)(2,1)S(1)} %pad_maximum_fusion), channel_id=1, source_target_pairs={{0,7},{1,2},{2,1},{3,4},{4,3},{5,6},{6,5},{7,0},{8,15},{9,10},{10,... | collective-permute-start | bytes 786440 | tf_op jit(solution)/shard_map/ppermute | solution.py:317
  6.6 0.0 collective-permute-start.2
  6.6 0.6 %collective-permute-start.1 = (bf16[2,128,512]{2,1,0:T(8,128)(2,1)S(1)}, bf16[2,128,512]{2,1,0:T(8,128)(2,1)S(1)}, u32[]{:S(2)}, u32[]{:S(2)}) collective-permute-start(bf16[2,128,512]{2,1,0:T(8,128)(2,1)S(1)} %pad_maximum_fusion.1), channel_id=1, source_target_pairs={{0,1},{1,0},{2,3},{3,2},{4,5},{5,4},{6,7},{7,6},{8,9},{9,8},{10,11... | collective-permute-start | bytes 786440 | tf_op jit(solution)/shard_map/ppermute | solution.py:318
  7.2 0.1 constant_dynamic-slice_fusion.4
  7.2 0.1 copy.11
  7.4 0.0 copy-start.5
  7.4 1.0 %copy-done.5 = bf16[1,256,1024]{2,1,0:T(8,128)(2,1)S(1)} copy-done((bf16[1,256,1024]{2,1,0:T(8,128)(2,1)S(1)}, bf16[1,256,1024]{2,1,0:T(8,128)(2,1)}, u32[]{:S(2)}) %copy-start.5) | copy-done | bytes 524312
  8.4 3.3 %shard_map.101 = (f32[512,256]{1,0:T(8,128)S(1)}, f32[2,8,256]{2,1,0:T(8,128)S(1)}, f32[8,256,256]{2,1,0:T(8,128)S(1)}, bf16[512,256]{1,0:T(8,128)(2,1)S(1)}) custom-call(s32[2,3]{1,0:T(2,128)S(1)} %bitcast.20, bf16[256,512]{1,0:T(8,128)(2,1)S(1)} %bitcast.9, bf16[256,512]{1,0:T(8,128)(2,1)S(1)} %bitcast.13, bf16[256,512]{1,0:T(8,128)(2,1)S(1)} %bitcast.15, ...), custom_call_target="tpu_custom_call" | custom-call | flops 1000000000 | bytes 4000000 | tf_op jit(solution)/shard_map/pallas_call | solution.py:277
  11.7 0.9 %collective-permute-done = bf16[2,128,512]{2,1,0:T(8,128)(2,1)S(1)} collective-permute-done((bf16[2,128,512]{2,1,0:T(8,128)(2,1)S(1)}, bf16[2,128,512]{2,1,0:T(8,128)(2,1)S(1)}, u32[]{:S(2)}, u32[]{:S(2)}) %collective-permute-start) | collective-permute-done | bytes 262176 | tf_op jit(solution)/shard_map/ppermute | solution.py:317
  12.6 0.0 collective-permute-done.1
  12.6 0.0 copy-start.6
  12.7 0.0 collective-permute-done.2.before.g
  12.7 1.5 %shard_map.102 = (bf16[512,256]{1,0:T(8,128)(2,1)S(1)}, bf16[4,64,256]{2,1,0:T(8,128)(2,1)S(1)}, bf16[4,64,256]{2,1,0:T(8,128)(2,1)S(1)}, f32[2,4,128,256]{3,2,1,0:T(8,128)S(1)}, f32[2,8,256]{2,1,0:T(8,128)S(1)}) custom-call(s32[2,3]{1,0:T(2,128)S(1)} %bitcast.21, bf16[256,512]{1,0:T(8,128)(2,1)S(1)} %bitcast.10, ...), custom_call_target="tpu_custom_call" | custom-call | flops 1000000000 | bytes 4000000 | tf_op jit(solution)/shard_map/pallas_call | solution.py:277
  14.1 0.1 collective-permute-start.3
  14.2 0.3 shard_map.103.product
  14.5 1.0 %collective-permute-done.3.other = bf16[4,64,256]{2,1,0:T(8,128)(2,1)S(1)} collective-permute-done((bf16[4,64,256]{2,1,0:T(8,128)(2,1)S(1)}, bf16[4,64,256]{2,1,0:T(8,128)(2,1)S(1)}, u32[]{:S(2)}, u32[]{:S(2)}) %collective-permute-start.3) | collective-permute-done | bytes 131104 | tf_op jit(solution)/shard_map/ppermute | solution.py:351
  15.5 0.4 %shard_map.104 = (bf16[4,64,256]{2,1,0:T(8,128)(2,1)S(1)}, bf16[4,64,256]{2,1,0:T(8,128)(2,1)S(1)}, bf16[4,64,256]{2,1,0:T(8,128)(2,1)S(1)}, bf16[4,64,256]{2,1,0:T(8,128)(2,1)S(1)}, f32[8,128]{1,0:T(8,128)S(1)}) custom-call(f32[256,1024]{1,0:T(8,128)S(1)} %shard_map.103.product, bf16[4,64,256]{2,1,0:T(8,128)(2,1)S(1)} %collective-permute-done.3.other, ...), custom_call_target="tpu_custom_call" | custom-call | flops 1000000 | bytes 4000 | tf_op jit(solution)/shard_map/pallas_call | solution.py:277
  16.0 2.6 %collective-permute-start.6 = (bf16[4,64,256]{2,1,0:T(8,128)(2,1)S(1)}, bf16[4,64,256]{2,1,0:T(8,128)(2,1)S(1)}, u32[]{:S(2)}, u32[]{:S(2)}) collective-permute-start(bf16[4,64,256]{2,1,0:T(8,128)(2,1)S(1)} %get-tuple-element.54), channel_id=1, source_target_pairs={{0,8},{8,0},{16,24},{24,16},{1,9},{9,1},{17,25},{25,17},{2,10},{10... | collective-permute-start | bytes 393224 | tf_op jit(solution)/shard_map/ppermute | solution.py:387
  18.6 1.5 %collective-permute-start.7 = (bf16[4,64,256]{2,1,0:T(8,128)(2,1)S(1)}, bf16[4,64,256]{2,1,0:T(8,128)(2,1)S(1)}, u32[]{:S(2)}, u32[]{:S(2)}) collective-permute-start(bf16[4,64,256]{2,1,0:T(8,128)(2,1)S(1)} %get-tuple-element.55), channel_id=1, source_target_pairs={{0,16},{8,24},{16,0},{24,8},{1,17},{9,25},{17,1},{25,9},{2,18},{10... | collective-permute-start | bytes 393224 | tf_op jit(solution)/shard_map/ppermute | solution.py:387
  20.1 0.0 collective-permute-start.8
  20.1 1.5 %shard_map.105 = (bf16[2,128,512]{2,1,0:T(8,128)(2,1)S(1)}, bf16[2,128,512]{2,1,0:T(8,128)(2,1)S(1)}, f32[8,256]{1,0:T(8,128)S(1)}, f32[512,256]{1,0:T(8,128)S(1)}) custom-call(bf16[256,512]{1,0:T(8,128)(2,1)S(1)} %bitcast.11, bf16[2,128,512]{2,1,0:T(8,128)(2,1)S(1)} %get-tuple-element.66.low, bf16[2,128,512]{2,1,0:T(8,128)(2,1)S(1)} %get-tuple-element.65.high, ...), custom_call_target="tpu_custom_call" | custom-call | flops 1000000 | bytes 4000 | tf_op jit(solution)/shard_map/pallas_call | solution.py:277
  21.6 3.6 %shard_map.106 = (bf16[256,512]{1,0:T(8,128)(2,1)}, f32[256,512]{1,0:T(8,128)S(1)}, f32[256,512]{1,0:T(8,128)S(1)}, bf16[256,1024]{1,0:T(8,128)(2,1)}, f32[8,128]{1,0:T(8,128)S(1)}) custom-call(bf16[256,512]{1,0:T(8,128)(2,1)S(1)} %bitcast.12, bf16[256,512]{1,0:T(8,128)(2,1)S(1)} %bitcast.14, bf16[256,512]{1,0:T(8,128)(2,1)S(1)} %bitcast.16, ...), custom_call_target="tpu_custom_call" | custom-call | flops 1000000 | bytes 4000 | tf_op jit(solution)/shard_map/pallas_call | solution.py:277
  25.2 0.0 collective-permute-done.6.refs_1_
  25.2 1.5 %collective-permute-done.7.refs_2_ = bf16[4,64,256]{2,1,0:T(8,128)(2,1)S(1)} collective-permute-done((bf16[4,64,256]{2,1,0:T(8,128)(2,1)S(1)}, bf16[4,64,256]{2,1,0:T(8,128)(2,1)S(1)}, u32[]{:S(2)}, u32[]{:S(2)}) %collective-permute-start.7) | collective-permute-done | bytes 131104 | tf_op jit(solution)/shard_map/ppermute | solution.py:387
  26.7 0.0 collective-permute-done.8.refs_3_
  26.7 0.1 shard_map.107
  26.7 2.1 %collective-permute-start.9 = (bf16[64,256]{1,0:T(8,128)(2,1)S(1)}, bf16[64,256]{1,0:T(8,128)(2,1)S(1)}, u32[]{:S(2)}, u32[]{:S(2)}) collective-permute-start(bf16[64,256]{1,0:T(8,128)(2,1)S(1)} %get-tuple-element.59), channel_id=1, source_target_pairs={{0,6},{1,7},{2,4},{3,5},{4,2},{5,3},{6,0},{7,1},{8,14},{9,15},{10,... | collective-permute-start | bytes 98312 | tf_op jit(solution)/shard_map/ppermute | solution.py:391
  28.9 0.0 collective-permute-start.10
  28.9 2.3 %collective-permute-start.11 = (bf16[64,256]{1,0:T(8,128)(2,1)S(1)}, bf16[64,256]{1,0:T(8,128)(2,1)S(1)}, u32[]{:S(2)}, u32[]{:S(2)}) collective-permute-start(bf16[64,256]{1,0:T(8,128)(2,1)S(1)} %get-tuple-element.61), channel_id=1, source_target_pairs={{0,2},{1,3},{2,0},{3,1},{4,6},{5,7},{6,4},{7,5},{8,10},{9,11},{10,... | collective-permute-start | bytes 98312 | tf_op jit(solution)/shard_map/ppermute | solution.py:391
  31.2 0.0 collective-permute-start.4
  31.2 0.1 collective-permute-start.5
  31.4 1.6 %collective-permute-done.9 = bf16[64,256]{1,0:T(8,128)(2,1)S(1)} collective-permute-done((bf16[64,256]{1,0:T(8,128)(2,1)S(1)}, bf16[64,256]{1,0:T(8,128)(2,1)S(1)}, u32[]{:S(2)}, u32[]{:S(2)}) %collective-permute-start.9) | collective-permute-done | bytes 32800 | tf_op jit(solution)/shard_map/ppermute | solution.py:391
  33.0 0.8 %collective-permute-done.10 = bf16[64,256]{1,0:T(8,128)(2,1)S(1)} collective-permute-done((bf16[64,256]{1,0:T(8,128)(2,1)S(1)}, bf16[64,256]{1,0:T(8,128)(2,1)S(1)}, u32[]{:S(2)}, u32[]{:S(2)}) %collective-permute-start.10) | collective-permute-done | bytes 32800 | tf_op jit(solution)/shard_map/ppermute | solution.py:391
  33.7 0.0 collective-permute-done.11
  33.8 1.6 %collective-permute-start.14 = (bf16[64,256]{1,0:T(8,128)(2,1)S(1)}, bf16[64,256]{1,0:T(8,128)(2,1)S(1)}, u32[]{:S(2)}, u32[]{:S(2)}) collective-permute-start(bf16[64,256]{1,0:T(8,128)(2,1)S(1)} %multiply_convert_fusion.refs_0_), channel_id=1, source_target_pairs={{0,24},{8,16},{16,8},{24,0},{1,25},{9,17},{17,9},{25,1},{2,26},{10... | collective-permute-start | bytes 98312 | tf_op jit(solution)/shard_map/ppermute | solution.py:394
  35.4 1.2 %collective-permute-start.13 = (bf16[64,256]{1,0:T(8,128)(2,1)S(1)}, bf16[64,256]{1,0:T(8,128)(2,1)S(1)}, u32[]{:S(2)}, u32[]{:S(2)}) collective-permute-start(bf16[64,256]{1,0:T(8,128)(2,1)S(1)} %multiply_convert_fusion.refs_0_), channel_id=1, source_target_pairs={{0,16},{8,24},{16,0},{24,8},{1,17},{9,25},{17,1},{25,9},{2,18},{10... | collective-permute-start | bytes 98312 | tf_op jit(solution)/shard_map/ppermute | solution.py:394
  36.6 0.7 %collective-permute-start.12 = (bf16[64,256]{1,0:T(8,128)(2,1)S(1)}, bf16[64,256]{1,0:T(8,128)(2,1)S(1)}, u32[]{:S(2)}, u32[]{:S(2)}) collective-permute-start(bf16[64,256]{1,0:T(8,128)(2,1)S(1)} %multiply_convert_fusion.refs_0_), channel_id=1, source_target_pairs={{0,8},{8,0},{16,24},{24,16},{1,9},{9,1},{17,25},{25,17},{2,10},{10... | collective-permute-start | bytes 98312 | tf_op jit(solution)/shard_map/ppermute | solution.py:394
  37.3 1.3 %collective-permute-done.14.refs_3_ = bf16[64,256]{1,0:T(8,128)(2,1)S(1)} collective-permute-done((bf16[64,256]{1,0:T(8,128)(2,1)S(1)}, bf16[64,256]{1,0:T(8,128)(2,1)S(1)}, u32[]{:S(2)}, u32[]{:S(2)}) %collective-permute-start.14) | collective-permute-done | bytes 32800 | tf_op jit(solution)/shard_map/ppermute | solution.py:394
  38.6 0.7 %collective-permute-done.13.refs_2_ = bf16[64,256]{1,0:T(8,128)(2,1)S(1)} collective-permute-done((bf16[64,256]{1,0:T(8,128)(2,1)S(1)}, bf16[64,256]{1,0:T(8,128)(2,1)S(1)}, u32[]{:S(2)}, u32[]{:S(2)}) %collective-permute-start.13) | collective-permute-done | bytes 32800 | tf_op jit(solution)/shard_map/ppermute | solution.py:394
  39.3 1.2 %collective-permute-done.12.refs_1_ = bf16[64,256]{1,0:T(8,128)(2,1)S(1)} collective-permute-done((bf16[64,256]{1,0:T(8,128)(2,1)S(1)}, bf16[64,256]{1,0:T(8,128)(2,1)S(1)}, u32[]{:S(2)}, u32[]{:S(2)}) %collective-permute-start.12) | collective-permute-done | bytes 32800 | tf_op jit(solution)/shard_map/ppermute | solution.py:394
  40.5 0.3 collective-permute-done.4.from_link
  40.8 0.0 collective-permute-done.5.from_chip
  40.8 1.0 %shard_map.108 = (bf16[256,512]{1,0:T(8,128)(2,1)}, bf16[256,512]{1,0:T(8,128)(2,1)}, f32[64,1024]{1,0:T(8,128)}) custom-call(f32[256,512]{1,0:T(8,128)S(1)} %get-tuple-element.49.k_own, f32[256,512]{1,0:T(8,128)S(1)} %get-tuple-element.50.v_own, bf16[2,128,512]{2,1,0:T(8,128)(2,1)S(1)} %collective-permute-done.4.from_link, ...), custom_call_target="tpu_custom_call" | custom-call | flops 1000000 | bytes 4000 | tf_op jit(solution)/shard_map/pallas_call | solution.py:277
  (11 shorter events, 0.1 us)
Async XLA Ops:
  0.6 6.5 %copy-start = (s32[1,16,3]{1,0,2:T(1,128)S(1)}, s32[1,16,3]{1,0,2:T(1,128)}, u32[]{:S(2)}) copy-start(s32[1,16,3]{1,0,2:T(1,128)} %param.11) | copy-start | bytes 580
  0.6 6.7 %copy-start.3 = (bf16[1,256,512]{2,1,0:T(8,128)(2,1)S(1)}, bf16[1,256,512]{2,1,0:T(8,128)(2,1)}, u32[]{:S(2)}) copy-start(bf16[1,256,512]{2,1,0:T(8,128)(2,1)} %param.8) | copy-start | bytes 786436
  0.7 6.7 %copy-start.2 = (bf16[1,256,512]{2,1,0:T(8,128)(2,1)S(1)}, bf16[1,256,512]{2,1,0:T(8,128)(2,1)}, u32[]{:S(2)}) copy-start(bf16[1,256,512]{2,1,0:T(8,128)(2,1)} %param.7) | copy-start | bytes 786436
  0.7 6.7 %copy-start.4 = (bf16[512,1024]{1,0:T(8,128)(2,1)S(1)}, bf16[512,1024]{1,0:T(8,128)(2,1)}, u32[]{:S(2)}) copy-start(bf16[512,1024]{1,0:T(8,128)(2,1)} %w_out.3) | copy-start | bytes 3145732
  0.7 6.7 %copy-start.1 = (bf16[1,256,512]{2,1,0:T(8,128)(2,1)S(1)}, bf16[1,256,512]{2,1,0:T(8,128)(2,1)}, u32[]{:S(2)}) copy-start(bf16[1,256,512]{2,1,0:T(8,128)(2,1)} %param.6) | copy-start | bytes 786436
  2.0 10.6 %collective-permute-start = (bf16[2,128,512]{2,1,0:T(8,128)(2,1)S(1)}, bf16[2,128,512]{2,1,0:T(8,128)(2,1)S(1)}, u32[]{:S(2)}, u32[]{:S(2)}) collective-permute-start(bf16[2,128,512]{2,1,0:T(8,128)(2,1)S(1)} %pad_maximum_fusion), channel_id=1, source_target_pairs={{0,7},{1,2},{2,1},{3,4},{4,3},{5,6},{6,5},{7,0},{8,15},{9,10},{10,... | collective-permute-start | bytes 786440 | tf_op jit(solution)/shard_map/ppermute | solution.py:317
  6.6 6.1 %collective-permute-start.2 = (bf16[256,1024]{1,0:T(8,128)(2,1)}, bf16[256,1024]{1,0:T(8,128)(2,1)S(1)}, u32[]{:S(2)}, u32[]{:S(2)}) collective-permute-start(bf16[256,1024]{1,0:T(8,128)(2,1)} %bitcast.17), channel_id=1, source_target_pairs={{0,1},{1,0},{2,3},{3,2},{4,5},{5,4},{6,7},{7,6},{8,9},{9,8},{10,11... | collective-permute-start | bytes 1572872 | tf_op jit(solution)/shard_map/ppermute | solution.py:319
  6.6 6.0 %collective-permute-start.1 = (bf16[2,128,512]{2,1,0:T(8,128)(2,1)S(1)}, bf16[2,128,512]{2,1,0:T(8,128)(2,1)S(1)}, u32[]{:S(2)}, u32[]{:S(2)}) collective-permute-start(bf16[2,128,512]{2,1,0:T(8,128)(2,1)S(1)} %pad_maximum_fusion.1), channel_id=1, source_target_pairs={{0,1},{1,0},{2,3},{3,2},{4,5},{5,4},{6,7},{7,6},{8,9},{9,8},{10,11... | collective-permute-start | bytes 786440 | tf_op jit(solution)/shard_map/ppermute | solution.py:318
  7.4 1.0 %copy-start.5 = (bf16[1,256,1024]{2,1,0:T(8,128)(2,1)S(1)}, bf16[1,256,1024]{2,1,0:T(8,128)(2,1)}, u32[]{:S(2)}) copy-start(bf16[1,256,1024]{2,1,0:T(8,128)(2,1)} %param.9) | copy-start | bytes 1572868
  12.6 1.6 %copy-start.6 = (bf16[1,256,1024]{2,1,0:T(8,128)(2,1)S(1)}, bf16[1,256,1024]{2,1,0:T(8,128)(2,1)}, u32[]{:S(2)}) copy-start(bf16[1,256,1024]{2,1,0:T(8,128)(2,1)} %param.9) | copy-start | bytes 1572868
  14.1 1.4 %collective-permute-start.3 = (bf16[4,64,256]{2,1,0:T(8,128)(2,1)S(1)}, bf16[4,64,256]{2,1,0:T(8,128)(2,1)S(1)}, u32[]{:S(2)}, u32[]{:S(2)}) collective-permute-start(bf16[4,64,256]{2,1,0:T(8,128)(2,1)S(1)} %get-tuple-element.43), channel_id=1, source_target_pairs={{0,1},{1,0},{2,3},{3,2},{4,5},{5,4},{6,7},{7,6},{8,9},{9,8},{10,11... | collective-permute-start | bytes 393224 | tf_op jit(solution)/shard_map/ppermute | solution.py:351
  16.0 9.2 %collective-permute-start.6 = (bf16[4,64,256]{2,1,0:T(8,128)(2,1)S(1)}, bf16[4,64,256]{2,1,0:T(8,128)(2,1)S(1)}, u32[]{:S(2)}, u32[]{:S(2)}) collective-permute-start(bf16[4,64,256]{2,1,0:T(8,128)(2,1)S(1)} %get-tuple-element.54), channel_id=1, source_target_pairs={{0,8},{8,0},{16,24},{24,16},{1,9},{9,1},{17,25},{25,17},{2,10},{10... | collective-permute-start | bytes 393224 | tf_op jit(solution)/shard_map/ppermute | solution.py:387
  18.6 8.1 %collective-permute-start.7 = (bf16[4,64,256]{2,1,0:T(8,128)(2,1)S(1)}, bf16[4,64,256]{2,1,0:T(8,128)(2,1)S(1)}, u32[]{:S(2)}, u32[]{:S(2)}) collective-permute-start(bf16[4,64,256]{2,1,0:T(8,128)(2,1)S(1)} %get-tuple-element.55), channel_id=1, source_target_pairs={{0,16},{8,24},{16,0},{24,8},{1,17},{9,25},{17,1},{25,9},{2,18},{10... | collective-permute-start | bytes 393224 | tf_op jit(solution)/shard_map/ppermute | solution.py:387
  20.1 6.6 %collective-permute-start.8 = (bf16[4,64,256]{2,1,0:T(8,128)(2,1)S(1)}, bf16[4,64,256]{2,1,0:T(8,128)(2,1)S(1)}, u32[]{:S(2)}, u32[]{:S(2)}) collective-permute-start(bf16[4,64,256]{2,1,0:T(8,128)(2,1)S(1)} %get-tuple-element.56), channel_id=1, source_target_pairs={{0,24},{8,16},{16,8},{24,0},{1,25},{9,17},{17,9},{25,1},{2,26},{10... | collective-permute-start | bytes 393224 | tf_op jit(solution)/shard_map/ppermute | solution.py:387
  26.7 6.2 %collective-permute-start.9 = (bf16[64,256]{1,0:T(8,128)(2,1)S(1)}, bf16[64,256]{1,0:T(8,128)(2,1)S(1)}, u32[]{:S(2)}, u32[]{:S(2)}) collective-permute-start(bf16[64,256]{1,0:T(8,128)(2,1)S(1)} %get-tuple-element.59), channel_id=1, source_target_pairs={{0,6},{1,7},{2,4},{3,5},{4,2},{5,3},{6,0},{7,1},{8,14},{9,15},{10,... | collective-permute-start | bytes 98312 | tf_op jit(solution)/shard_map/ppermute | solution.py:391
  28.9 4.9 %collective-permute-start.10 = (bf16[64,256]{1,0:T(8,128)(2,1)S(1)}, bf16[64,256]{1,0:T(8,128)(2,1)S(1)}, u32[]{:S(2)}, u32[]{:S(2)}) collective-permute-start(bf16[64,256]{1,0:T(8,128)(2,1)S(1)} %get-tuple-element.60), channel_id=1, source_target_pairs={{0,4},{1,5},{2,6},{3,7},{4,0},{5,1},{6,2},{7,3},{8,12},{9,13},{10,... | collective-permute-start | bytes 98312 | tf_op jit(solution)/shard_map/ppermute | solution.py:391
  28.9 4.9 %collective-permute-start.11 = (bf16[64,256]{1,0:T(8,128)(2,1)S(1)}, bf16[64,256]{1,0:T(8,128)(2,1)S(1)}, u32[]{:S(2)}, u32[]{:S(2)}) collective-permute-start(bf16[64,256]{1,0:T(8,128)(2,1)S(1)} %get-tuple-element.61), channel_id=1, source_target_pairs={{0,2},{1,3},{2,0},{3,1},{4,6},{5,7},{6,4},{7,5},{8,10},{9,11},{10,... | collective-permute-start | bytes 98312 | tf_op jit(solution)/shard_map/ppermute | solution.py:391
  31.2 9.6 %collective-permute-start.4 = (bf16[2,128,512]{2,1,0:T(8,128)(2,1)S(1)}, bf16[2,128,512]{2,1,0:T(8,128)(2,1)S(1)}, u32[]{:S(2)}, u32[]{:S(2)}) collective-permute-start(bf16[2,128,512]{2,1,0:T(8,128)(2,1)S(1)} %get-tuple-element.51), channel_id=1, source_target_pairs={{0,7},{1,2},{2,1},{3,4},{4,3},{5,6},{6,5},{7,0},{8,15},{9,10},{10,... | collective-permute-start | bytes 786440 | tf_op jit(solution)/shard_map/ppermute | solution.py:371
  31.2 9.6 %collective-permute-start.5 = (bf16[2,128,512]{2,1,0:T(8,128)(2,1)S(1)}, bf16[2,128,512]{2,1,0:T(8,128)(2,1)S(1)}, u32[]{:S(2)}, u32[]{:S(2)}) collective-permute-start(bf16[2,128,512]{2,1,0:T(8,128)(2,1)S(1)} %get-tuple-element.52), channel_id=1, source_target_pairs={{0,1},{1,0},{2,3},{3,2},{4,5},{5,4},{6,7},{7,6},{8,9},{9,8},{10,11... | collective-permute-start | bytes 786440 | tf_op jit(solution)/shard_map/ppermute | solution.py:372
  33.8 4.9 %collective-permute-start.14 = (bf16[64,256]{1,0:T(8,128)(2,1)S(1)}, bf16[64,256]{1,0:T(8,128)(2,1)S(1)}, u32[]{:S(2)}, u32[]{:S(2)}) collective-permute-start(bf16[64,256]{1,0:T(8,128)(2,1)S(1)} %multiply_convert_fusion.refs_0_), channel_id=1, source_target_pairs={{0,24},{8,16},{16,8},{24,0},{1,25},{9,17},{17,9},{25,1},{2,26},{10... | collective-permute-start | bytes 98312 | tf_op jit(solution)/shard_map/ppermute | solution.py:394
  35.4 3.9 %collective-permute-start.13 = (bf16[64,256]{1,0:T(8,128)(2,1)S(1)}, bf16[64,256]{1,0:T(8,128)(2,1)S(1)}, u32[]{:S(2)}, u32[]{:S(2)}) collective-permute-start(bf16[64,256]{1,0:T(8,128)(2,1)S(1)} %multiply_convert_fusion.refs_0_), channel_id=1, source_target_pairs={{0,16},{8,24},{16,0},{24,8},{1,17},{9,25},{17,1},{25,9},{2,18},{10... | collective-permute-start | bytes 98312 | tf_op jit(solution)/shard_map/ppermute | solution.py:394
  36.6 3.9 %collective-permute-start.12 = (bf16[64,256]{1,0:T(8,128)(2,1)S(1)}, bf16[64,256]{1,0:T(8,128)(2,1)S(1)}, u32[]{:S(2)}, u32[]{:S(2)}) collective-permute-start(bf16[64,256]{1,0:T(8,128)(2,1)S(1)} %multiply_convert_fusion.refs_0_), channel_id=1, source_target_pairs={{0,8},{8,0},{16,24},{24,16},{1,9},{9,1},{17,25},{25,17},{2,10},{10... | collective-permute-start | bytes 98312 | tf_op jit(solution)/shard_map/ppermute | solution.py:394

commit v8 on v7

--- a/solution.py
+++ b/solution.py
@@ -193,8 +193,7 @@
 
 
 def own_backward_kernel(
-    q, k, v, grad_t, attn_t, exps, factors, deltas, rim_t, w_out, before,
-    q_grad, k_own, v_own, output, after,
+    q, k, v, grad_t, exps, factors, deltas, rim_t, before, q_grad, k_own, v_own, after
 ):
     blocks = q.shape[0] // BLK
     k_own[...] = jnp.zeros_like(k_own)
@@ -210,8 +209,11 @@
         q_grad[rows, cols] = (part_t + rim_t[cols, rows]).T.astype(BF16)
         k_own[here, cols] += k_part
         v_own[here, cols] += v_part
+    after[...] = jnp.zeros_like(after)
+
+
+def output_kernel(attn_t, w_out, before, output):
     output[...] = dot(attn_t[...], w_out[...], ((0,), (0,))).astype(BF16)
-    after[...] = jnp.zeros_like(after)
 
 
 def halves_kernel(product, other, g, *outs):
@@ -371,21 +373,21 @@
     grad_link = lax.ppermute(to_link, "ctx", over_links(ctx))
     grad_chip = lax.ppermute(to_chip, "ctx", swap(ctx, 1))
 
-    q_grad, k_own, v_own, output, after = call(
+    q_grad, k_own, v_own, after = call(
         own_backward_kernel,
         [
             hbm(tokens, feats),
             vmem(tokens, feats, dtype=F32),
             vmem(tokens, feats, dtype=F32),
-            hbm(tokens, width),
             vmem(8, 128, dtype=F32),
         ],
         10**6,
-        q, k, v, grad_t, attn_t, own_exps, factors, deltas, rim_t, w_out, after,
-    )
-
-    halves = [halves[0]] + [lax.ppermute(halves[s], "dp", swap(dp, s)) for s in range(1, dp)]
+        q, k, v, grad_t, own_exps, factors, deltas, rim_t, after,
+    )
+
+    halves = [halves[0]] + [lax.ppermute(halves[s], "dp", swap(dp, s)) for s in range(dp - 1, 0, -1)]
     quarters = call(chips_kernel, [vmem(rows, cols)] * chips, 10**6, *halves, after)
+    (output,) = call(output_kernel, [hbm(tokens, width)], 10**6, attn_t, w_out, quarters[0])
     piece = total(
         [quarters[0]]
         + [lax.ppermute(quarters[s], "ctx", swap(ctx, 2 * s)) for s in range(chips - 1, 0, -1)]

time: 42 us -> 41.7 us (level)
  waiting for transfers between devices: 9.22 us -> 7.44 us
  Pallas kernels: 11.6 us -> 12.5 us
  starting transfers between devices: 17.5 us -> 18.2 us
    ppermute x3, waiting for transfers between devices: 3.18 us -> 2.12 us  [body(): lax.ppermute(piece, 'dp', swap(dp, s))]
    pallas_call x8 -> x9, Pallas kernels: 11.6 us -> 12.5 us  [call(): pl.pallas_call(kernel, out_shape=outs, in_specs=[in_smem] * len(masks) +...]
    ppermute x1, starting transfers between devices: 0.01 us -> 0.77 us  [body(): grad_link = lax.ppermute(to_link, 'ctx', over_links(ctx))]
    ppermute x3, waiting for transfers between devices: 2.39 us -> 1.77 us  [body(): lax.ppermute(quarters[s], 'ctx', swap(ctx, 2 * s))]
  transfers between devices with their start and end apart: 15 -> 15, of which waited for: 9 -> 10; matrix products, arithmetic and copies ran while one was open for 1% -> 1% of each run, Pallas kernels for 21% -> 23%
where the time goes in v8:
time: 41.7 us; the launch traced here: 41.5 us
  starting transfers between devices  18.2 us (44%)
  Pallas kernels  12.5 us (30%)
  waiting for transfers between devices  7.44 us (18%)
  local copies, waits for them, and re-layouts  2.5 us (6%)
  between operations  0.82 us (2%)
    pallas_call x9, Pallas kernels, call(): pl.pallas_call(kernel, out_shape=outs, in_specs=[in_smem] * len(masks) +...  12.5 us
    ppermute x1, starting transfers between devices, body(): from_link = lax.ppermute(rim(link_row), 'ctx', over_links(ctx))  4.55 us
    ppermute x3, starting transfers between devices, body(): lax.ppermute(quarters[s], 'ctx', swap(ctx, 2 * s))  4.45 us
    ppermute x3, starting transfers between devices, body(): lax.ppermute(halves[s], 'dp', swap(dp, s))  4.21 us
    ppermute x3, starting transfers between devices, body(): lax.ppermute(piece, 'dp', swap(dp, s))  3.55 us
    ppermute x3, waiting for transfers between devices, body(): lax.ppermute(piece, 'dp', swap(dp, s))  2.12 us
    ppermute x3, waiting for transfers between devices, body(): lax.ppermute(quarters[s], 'ctx', swap(ctx, 2 * s))  1.77 us
    ppermute x3, waiting for transfers between devices, body(): lax.ppermute(halves[s], 'dp', swap(dp, s))  1.59 us
  transfers between devices with their start and end apart: 15, of which 10 were waited for; matrix products, arithmetic and copies ran while one was open for 1% of the time, Pallas kernels for 23%

profile of v8, /device:TPU:0, one launch (start us, length us, event | category | flops | bytes accessed | tf_op | source)
XLA Modules:
  0.0 41.5 jit_solution(8967402866035175064)
XLA Ops:
  0.6 0.0 copy-start
  0.6 0.0 copy-start.2
  0.7 1.3 %constant_dynamic-slice_fusion = (bf16[1,128,512]{2,1,0:T(8,128)(2,1)S(1)}, bf16[1,128,512]{2,1,0:T(8,128)(2,1)S(1)}, bf16[1,128,512]{2,1,0:T(8,128)(2,1)S(1)}, bf16[1,128,512]{2,1,0:T(8,128)(2,1)S(1)}) fusion(bf16[1,256,512]{2,1,0:T(8,128)(2,1)} %param.8, s32[]{:T(128)S(6)} %select_n.34, s32[]{:T(128)S(6)} %select_n.33, bf16[1,256,512]{2,1,0:T(8,128)(2,1)} %param.7), kind=kLoop, calls=%fused_computation.5 | loop fusion | bytes 1048584 | tf_op jit(solution)/shard_map/dynamic_slice | solution.py:317
  2.0 4.6 %collective-permute-start = (bf16[2,128,512]{2,1,0:T(8,128)(2,1)S(1)}, bf16[2,128,512]{2,1,0:T(8,128)(2,1)S(1)}, u32[]{:S(2)}, u32[]{:S(2)}) collective-permute-start(bf16[2,128,512]{2,1,0:T(8,128)(2,1)S(1)} %pad_maximum_fusion), channel_id=1, source_target_pairs={{0,7},{1,2},{2,1},{3,4},{4,3},{5,6},{6,5},{7,0},{8,15},{9,10},{10,... | collective-permute-start | bytes 786440 | tf_op jit(solution)/shard_map/ppermute | solution.py:319
  6.6 0.0 collective-permute-start.2
  6.6 0.6 %collective-permute-start.1 = (bf16[2,128,512]{2,1,0:T(8,128)(2,1)S(1)}, bf16[2,128,512]{2,1,0:T(8,128)(2,1)S(1)}, u32[]{:S(2)}, u32[]{:S(2)}) collective-permute-start(bf16[2,128,512]{2,1,0:T(8,128)(2,1)S(1)} %pad_maximum_fusion.1), channel_id=1, source_target_pairs={{0,1},{1,0},{2,3},{3,2},{4,5},{5,4},{6,7},{7,6},{8,9},{9,8},{10,11... | collective-permute-start | bytes 786440 | tf_op jit(solution)/shard_map/ppermute | solution.py:320
  7.2 0.1 constant_dynamic-slice_fusion.4
  7.2 0.1 copy.11
  7.3 0.0 copy-done.1
  7.4 0.0 copy-start.5
  7.4 1.0 %copy-done.5 = bf16[1,256,1024]{2,1,0:T(8,128)(2,1)S(1)} copy-done((bf16[1,256,1024]{2,1,0:T(8,128)(2,1)S(1)}, bf16[1,256,1024]{2,1,0:T(8,128)(2,1)}, u32[]{:S(2)}) %copy-start.5) | copy-done | bytes 524312
  8.4 3.3 %shard_map.101 = (f32[512,256]{1,0:T(8,128)S(1)}, f32[2,8,256]{2,1,0:T(8,128)S(1)}, f32[8,256,256]{2,1,0:T(8,128)S(1)}, bf16[512,256]{1,0:T(8,128)(2,1)S(1)}) custom-call(s32[2,3]{1,0:T(2,128)S(1)} %bitcast.20, bf16[256,512]{1,0:T(8,128)(2,1)S(1)} %bitcast.9, bf16[256,512]{1,0:T(8,128)(2,1)S(1)} %bitcast.15, bf16[256,512]{1,0:T(8,128)(2,1)S(1)} %bitcast.13, ...), custom_call_target="tpu_custom_call" | custom-call | flops 1000000000 | bytes 4000000 | tf_op jit(solution)/shard_map/pallas_call | solution.py:279
  11.7 0.9 %collective-permute-done = bf16[2,128,512]{2,1,0:T(8,128)(2,1)S(1)} collective-permute-done((bf16[2,128,512]{2,1,0:T(8,128)(2,1)S(1)}, bf16[2,128,512]{2,1,0:T(8,128)(2,1)S(1)}, u32[]{:S(2)}, u32[]{:S(2)}) %collective-permute-start) | collective-permute-done | bytes 262176 | tf_op jit(solution)/shard_map/ppermute | solution.py:319
  12.6 0.0 collective-permute-done.1
  12.6 0.0 copy-start.6
  12.7 0.0 collective-permute-done.2.before.g
  12.7 1.5 %shard_map.102 = (bf16[512,256]{1,0:T(8,128)(2,1)S(1)}, bf16[4,64,256]{2,1,0:T(8,128)(2,1)S(1)}, bf16[4,64,256]{2,1,0:T(8,128)(2,1)S(1)}, f32[2,4,128,256]{3,2,1,0:T(8,128)S(1)}, f32[2,8,256]{2,1,0:T(8,128)S(1)}) custom-call(s32[2,3]{1,0:T(2,128)S(1)} %bitcast.21, bf16[256,512]{1,0:T(8,128)(2,1)S(1)} %bitcast.10, ...), custom_call_target="tpu_custom_call" | custom-call | flops 1000000000 | bytes 4000000 | tf_op jit(solution)/shard_map/pallas_call | solution.py:279
  14.1 0.1 collective-permute-start.3
  14.2 0.3 shard_map.103.product
  14.5 1.0 %collective-permute-done.3.other = bf16[4,64,256]{2,1,0:T(8,128)(2,1)S(1)} collective-permute-done((bf16[4,64,256]{2,1,0:T(8,128)(2,1)S(1)}, bf16[4,64,256]{2,1,0:T(8,128)(2,1)S(1)}, u32[]{:S(2)}, u32[]{:S(2)}) %collective-permute-start.3) | collective-permute-done | bytes 131104 | tf_op jit(solution)/shard_map/ppermute | solution.py:353
  15.5 0.4 %shard_map.104 = (bf16[4,64,256]{2,1,0:T(8,128)(2,1)S(1)}, bf16[4,64,256]{2,1,0:T(8,128)(2,1)S(1)}, bf16[4,64,256]{2,1,0:T(8,128)(2,1)S(1)}, bf16[4,64,256]{2,1,0:T(8,128)(2,1)S(1)}, f32[8,128]{1,0:T(8,128)S(1)}) custom-call(f32[256,1024]{1,0:T(8,128)S(1)} %shard_map.103.product, bf16[4,64,256]{2,1,0:T(8,128)(2,1)S(1)} %collective-permute-done.3.other, ...), custom_call_target="tpu_custom_call" | custom-call | flops 1000000 | bytes 4000 | tf_op jit(solution)/shard_map/pallas_call | solution.py:279
  16.0 3.6 %collective-permute-start.4 = (bf16[4,64,256]{2,1,0:T(8,128)(2,1)S(1)}, bf16[4,64,256]{2,1,0:T(8,128)(2,1)S(1)}, u32[]{:S(2)}, u32[]{:S(2)}) collective-permute-start(bf16[4,64,256]{2,1,0:T(8,128)(2,1)S(1)} %get-tuple-element.40), channel_id=1, source_target_pairs={{0,24},{8,16},{16,8},{24,0},{1,25},{9,17},{17,9},{25,1},{2,26},{10... | collective-permute-start | bytes 393224 | tf_op jit(solution)/shard_map/ppermute | solution.py:388
  19.5 0.5 %collective-permute-start.5 = (bf16[4,64,256]{2,1,0:T(8,128)(2,1)S(1)}, bf16[4,64,256]{2,1,0:T(8,128)(2,1)S(1)}, u32[]{:S(2)}, u32[]{:S(2)}) collective-permute-start(bf16[4,64,256]{2,1,0:T(8,128)(2,1)S(1)} %get-tuple-element.41), channel_id=1, source_target_pairs={{0,16},{8,24},{16,0},{24,8},{1,17},{9,25},{17,1},{25,9},{2,18},{10... | collective-permute-start | bytes 393224 | tf_op jit(solution)/shard_map/ppermute | solution.py:388
  20.0 0.1 collective-permute-start.6
  20.2 1.5 %shard_map.105 = (bf16[2,128,512]{2,1,0:T(8,128)(2,1)S(1)}, bf16[2,128,512]{2,1,0:T(8,128)(2,1)S(1)}, f32[8,256]{1,0:T(8,128)S(1)}, f32[512,256]{1,0:T(8,128)S(1)}) custom-call(bf16[256,512]{1,0:T(8,128)(2,1)S(1)} %bitcast.11, bf16[2,128,512]{2,1,0:T(8,128)(2,1)S(1)} %get-tuple-element.64.low, bf16[2,128,512]{2,1,0:T(8,128)(2,1)S(1)} %get-tuple-element.63.high, ...), custom_call_target="tpu_custom_call" | custom-call | flops 1000000 | bytes 4000 | tf_op jit(solution)/shard_map/pallas_call | solution.py:279
  21.7 3.2 %shard_map.106 = (bf16[256,512]{1,0:T(8,128)(2,1)}, f32[256,512]{1,0:T(8,128)S(1)}, f32[256,512]{1,0:T(8,128)S(1)}, f32[8,128]{1,0:T(8,128)S(1)}) custom-call(bf16[256,512]{1,0:T(8,128)(2,1)S(1)} %bitcast.12, bf16[256,512]{1,0:T(8,128)(2,1)S(1)} %bitcast.16, bf16[256,512]{1,0:T(8,128)(2,1)S(1)} %bitcast.14, bf16[512,256]{1,0:T(8,128)(2,1)S(1)} %get-tuple-element.43.grad_t, ...), custom_call_target="tpu_custom_call" | custom-call | flops 1000000 | bytes 4000 | tf_op jit(solution)/shard_map/pallas_call | solution.py:279
  24.9 0.0 collective-permute-done.4.refs_1_
  24.9 1.3 %collective-permute-done.5.refs_2_ = bf16[4,64,256]{2,1,0:T(8,128)(2,1)S(1)} collective-permute-done((bf16[4,64,256]{2,1,0:T(8,128)(2,1)S(1)}, bf16[4,64,256]{2,1,0:T(8,128)(2,1)S(1)}, u32[]{:S(2)}, u32[]{:S(2)}) %collective-permute-start.5) | collective-permute-done | bytes 131104 | tf_op jit(solution)/shard_map/ppermute | solution.py:388
  26.2 0.3 collective-permute-done.6.refs_3_
  26.4 0.1 shard_map.107
  26.5 2.1 %collective-permute-start.9 = (bf16[64,256]{1,0:T(8,128)(2,1)S(1)}, bf16[64,256]{1,0:T(8,128)(2,1)S(1)}, u32[]{:S(2)}, u32[]{:S(2)}) collective-permute-start(bf16[64,256]{1,0:T(8,128)(2,1)S(1)} %get-tuple-element.57), channel_id=1, source_target_pairs={{0,6},{1,7},{2,4},{3,5},{4,2},{5,3},{6,0},{7,1},{8,14},{9,15},{10,... | collective-permute-start | bytes 98312 | tf_op jit(solution)/shard_map/ppermute | solution.py:393
  28.7 0.0 collective-permute-start.10
  28.7 2.3 %collective-permute-start.11 = (bf16[64,256]{1,0:T(8,128)(2,1)S(1)}, bf16[64,256]{1,0:T(8,128)(2,1)S(1)}, u32[]{:S(2)}, u32[]{:S(2)}) collective-permute-start(bf16[64,256]{1,0:T(8,128)(2,1)S(1)} %get-tuple-element.59), channel_id=1, source_target_pairs={{0,2},{1,3},{2,0},{3,1},{4,6},{5,7},{6,4},{7,5},{8,10},{9,11},{10,... | collective-permute-start | bytes 98312 | tf_op jit(solution)/shard_map/ppermute | solution.py:393
  31.0 0.8 %collective-permute-start.7 = (bf16[2,128,512]{2,1,0:T(8,128)(2,1)S(1)}, bf16[2,128,512]{2,1,0:T(8,128)(2,1)S(1)}, u32[]{:S(2)}, u32[]{:S(2)}) collective-permute-start(bf16[2,128,512]{2,1,0:T(8,128)(2,1)S(1)} %get-tuple-element.55), channel_id=1, source_target_pairs={{0,7},{1,2},{2,1},{3,4},{4,3},{5,6},{6,5},{7,0},{8,15},{9,10},{10,... | collective-permute-start | bytes 786440 | tf_op jit(solution)/shard_map/ppermute | solution.py:373
  31.7 0.0 collective-permute-start.8
  31.7 0.7 %collective-permute-done.9 = bf16[64,256]{1,0:T(8,128)(2,1)S(1)} collective-permute-done((bf16[64,256]{1,0:T(8,128)(2,1)S(1)}, bf16[64,256]{1,0:T(8,128)(2,1)S(1)}, u32[]{:S(2)}, u32[]{:S(2)}) %collective-permute-start.9) | collective-permute-done | bytes 32800 | tf_op jit(solution)/shard_map/ppermute | solution.py:393
  32.4 1.1 %collective-permute-done.10 = bf16[64,256]{1,0:T(8,128)(2,1)S(1)} collective-permute-done((bf16[64,256]{1,0:T(8,128)(2,1)S(1)}, bf16[64,256]{1,0:T(8,128)(2,1)S(1)}, u32[]{:S(2)}, u32[]{:S(2)}) %collective-permute-start.10) | collective-permute-done | bytes 32800 | tf_op jit(solution)/shard_map/ppermute | solution.py:393
  33.5 0.0 collective-permute-done.11
  33.5 1.8 %collective-permute-start.14 = (bf16[64,256]{1,0:T(8,128)(2,1)S(1)}, bf16[64,256]{1,0:T(8,128)(2,1)S(1)}, u32[]{:S(2)}, u32[]{:S(2)}) collective-permute-start(bf16[64,256]{1,0:T(8,128)(2,1)S(1)} %multiply_convert_fusion.refs_0_), channel_id=1, source_target_pairs={{0,24},{8,16},{16,8},{24,0},{1,25},{9,17},{17,9},{25,1},{2,26},{10... | collective-permute-start | bytes 98312 | tf_op jit(solution)/shard_map/ppermute | solution.py:396
  35.3 1.2 %collective-permute-start.13 = (bf16[64,256]{1,0:T(8,128)(2,1)S(1)}, bf16[64,256]{1,0:T(8,128)(2,1)S(1)}, u32[]{:S(2)}, u32[]{:S(2)}) collective-permute-start(bf16[64,256]{1,0:T(8,128)(2,1)S(1)} %multiply_convert_fusion.refs_0_), channel_id=1, source_target_pairs={{0,16},{8,24},{16,0},{24,8},{1,17},{9,25},{17,1},{25,9},{2,18},{10... | collective-permute-start | bytes 98312 | tf_op jit(solution)/shard_map/ppermute | solution.py:396
  36.6 0.5 %collective-permute-start.12 = (bf16[64,256]{1,0:T(8,128)(2,1)S(1)}, bf16[64,256]{1,0:T(8,128)(2,1)S(1)}, u32[]{:S(2)}, u32[]{:S(2)}) collective-permute-start(bf16[64,256]{1,0:T(8,128)(2,1)S(1)} %multiply_convert_fusion.refs_0_), channel_id=1, source_target_pairs={{0,8},{8,0},{16,24},{24,16},{1,9},{9,1},{17,25},{25,17},{2,10},{10... | collective-permute-start | bytes 98312 | tf_op jit(solution)/shard_map/ppermute | solution.py:396
  37.1 1.3 %shard_map.108 = bf16[256,1024]{1,0:T(8,128)(2,1)} custom-call(bf16[512,256]{1,0:T(8,128)(2,1)S(1)} %get-tuple-element.36.attn_t, bf16[512,1024]{1,0:T(8,128)(2,1)S(1)} %copy-done.4, bf16[64,256]{1,0:T(8,128)(2,1)S(1)} %get-tuple-element.51.before), custom_call_target="tpu_custom_call" | custom-call | flops 1000000 | bytes 4000 | tf_op jit(solution)/shard_map/pallas_call | solution.py:279
  38.4 0.1 collective-permute-done.14.refs_3_
  38.4 0.8 %collective-permute-done.13.refs_2_ = bf16[64,256]{1,0:T(8,128)(2,1)S(1)} collective-permute-done((bf16[64,256]{1,0:T(8,128)(2,1)S(1)}, bf16[64,256]{1,0:T(8,128)(2,1)S(1)}, u32[]{:S(2)}, u32[]{:S(2)}) %collective-permute-start.13) | collective-permute-done | bytes 32800 | tf_op jit(solution)/shard_map/ppermute | solution.py:396
  39.2 1.2 %collective-permute-done.12.refs_1_ = bf16[64,256]{1,0:T(8,128)(2,1)S(1)} collective-permute-done((bf16[64,256]{1,0:T(8,128)(2,1)S(1)}, bf16[64,256]{1,0:T(8,128)(2,1)S(1)}, u32[]{:S(2)}, u32[]{:S(2)}) %collective-permute-start.12) | collective-permute-done | bytes 32800 | tf_op jit(solution)/shard_map/ppermute | solution.py:396
  40.5 0.1 collective-permute-done.7.from_link
  40.5 0.0 collective-permute-done.8.from_chip
  40.5 1.0 %shard_map.109 = (bf16[256,512]{1,0:T(8,128)(2,1)}, bf16[256,512]{1,0:T(8,128)(2,1)}, f32[64,1024]{1,0:T(8,128)}) custom-call(f32[256,512]{1,0:T(8,128)S(1)} %get-tuple-element.53.k_own, f32[256,512]{1,0:T(8,128)S(1)} %get-tuple-element.54.v_own, bf16[2,128,512]{2,1,0:T(8,128)(2,1)S(1)} %collective-permute-done.7.from_link, ...), custom_call_target="tpu_custom_call" | custom-call | flops 1000000 | bytes 4000 | tf_op jit(solution)/shard_map/pallas_call | solution.py:279
  (12 shorter events, 0.1 us)
Async XLA Ops:
  0.6 6.5 %copy-start = (s32[1,16,3]{1,0,2:T(1,128)S(1)}, s32[1,16,3]{1,0,2:T(1,128)}, u32[]{:S(2)}) copy-start(s32[1,16,3]{1,0,2:T(1,128)} %param.11) | copy-start | bytes 580
  0.6 6.7 %copy-start.2 = (bf16[1,256,512]{2,1,0:T(8,128)(2,1)S(1)}, bf16[1,256,512]{2,1,0:T(8,128)(2,1)}, u32[]{:S(2)}) copy-start(bf16[1,256,512]{2,1,0:T(8,128)(2,1)} %param.8) | copy-start | bytes 786436
  0.7 6.7 %copy-start.3 = (bf16[1,256,512]{2,1,0:T(8,128)(2,1)S(1)}, bf16[1,256,512]{2,1,0:T(8,128)(2,1)}, u32[]{:S(2)}) copy-start(bf16[1,256,512]{2,1,0:T(8,128)(2,1)} %param.7) | copy-start | bytes 786436
  0.7 6.7 %copy-start.4 = (bf16[512,1024]{1,0:T(8,128)(2,1)S(1)}, bf16[512,1024]{1,0:T(8,128)(2,1)}, u32[]{:S(2)}) copy-start(bf16[512,1024]{1,0:T(8,128)(2,1)} %w_out.3) | copy-start | bytes 3145732
  0.7 6.7 %copy-start.1 = (bf16[1,256,512]{2,1,0:T(8,128)(2,1)S(1)}, bf16[1,256,512]{2,1,0:T(8,128)(2,1)}, u32[]{:S(2)}) copy-start(bf16[1,256,512]{2,1,0:T(8,128)(2,1)} %param.6) | copy-start | bytes 786436
  2.0 10.6 %collective-permute-start = (bf16[2,128,512]{2,1,0:T(8,128)(2,1)S(1)}, bf16[2,128,512]{2,1,0:T(8,128)(2,1)S(1)}, u32[]{:S(2)}, u32[]{:S(2)}) collective-permute-start(bf16[2,128,512]{2,1,0:T(8,128)(2,1)S(1)} %pad_maximum_fusion), channel_id=1, source_target_pairs={{0,7},{1,2},{2,1},{3,4},{4,3},{5,6},{6,5},{7,0},{8,15},{9,10},{10,... | collective-permute-start | bytes 786440 | tf_op jit(solution)/shard_map/ppermute | solution.py:319
  6.6 6.1 %collective-permute-start.2 = (bf16[256,1024]{1,0:T(8,128)(2,1)}, bf16[256,1024]{1,0:T(8,128)(2,1)S(1)}, u32[]{:S(2)}, u32[]{:S(2)}) collective-permute-start(bf16[256,1024]{1,0:T(8,128)(2,1)} %bitcast.17), channel_id=1, source_target_pairs={{0,1},{1,0},{2,3},{3,2},{4,5},{5,4},{6,7},{7,6},{8,9},{9,8},{10,11... | collective-permute-start | bytes 1572872 | tf_op jit(solution)/shard_map/ppermute | solution.py:321
  6.6 6.0 %collective-permute-start.1 = (bf16[2,128,512]{2,1,0:T(8,128)(2,1)S(1)}, bf16[2,128,512]{2,1,0:T(8,128)(2,1)S(1)}, u32[]{:S(2)}, u32[]{:S(2)}) collective-permute-start(bf16[2,128,512]{2,1,0:T(8,128)(2,1)S(1)} %pad_maximum_fusion.1), channel_id=1, source_target_pairs={{0,1},{1,0},{2,3},{3,2},{4,5},{5,4},{6,7},{7,6},{8,9},{9,8},{10,11... | collective-permute-start | bytes 786440 | tf_op jit(solution)/shard_map/ppermute | solution.py:320
  7.4 1.0 %copy-start.5 = (bf16[1,256,1024]{2,1,0:T(8,128)(2,1)S(1)}, bf16[1,256,1024]{2,1,0:T(8,128)(2,1)}, u32[]{:S(2)}) copy-start(bf16[1,256,1024]{2,1,0:T(8,128)(2,1)} %param.9) | copy-start | bytes 1572868
  12.6 1.6 %copy-start.6 = (bf16[1,256,1024]{2,1,0:T(8,128)(2,1)S(1)}, bf16[1,256,1024]{2,1,0:T(8,128)(2,1)}, u32[]{:S(2)}) copy-start(bf16[1,256,1024]{2,1,0:T(8,128)(2,1)} %param.9) | copy-start | bytes 1572868
  14.1 1.4 %collective-permute-start.3 = (bf16[4,64,256]{2,1,0:T(8,128)(2,1)S(1)}, bf16[4,64,256]{2,1,0:T(8,128)(2,1)S(1)}, u32[]{:S(2)}, u32[]{:S(2)}) collective-permute-start(bf16[4,64,256]{2,1,0:T(8,128)(2,1)S(1)} %get-tuple-element.38), channel_id=1, source_target_pairs={{0,1},{1,0},{2,3},{3,2},{4,5},{5,4},{6,7},{7,6},{8,9},{9,8},{10,11... | collective-permute-start | bytes 393224 | tf_op jit(solution)/shard_map/ppermute | solution.py:353
  16.0 8.9 %collective-permute-start.4 = (bf16[4,64,256]{2,1,0:T(8,128)(2,1)S(1)}, bf16[4,64,256]{2,1,0:T(8,128)(2,1)S(1)}, u32[]{:S(2)}, u32[]{:S(2)}) collective-permute-start(bf16[4,64,256]{2,1,0:T(8,128)(2,1)S(1)} %get-tuple-element.40), channel_id=1, source_target_pairs={{0,24},{8,16},{16,8},{24,0},{1,25},{9,17},{17,9},{25,1},{2,26},{10... | collective-permute-start | bytes 393224 | tf_op jit(solution)/shard_map/ppermute | solution.py:388
  19.5 6.6 %collective-permute-start.5 = (bf16[4,64,256]{2,1,0:T(8,128)(2,1)S(1)}, bf16[4,64,256]{2,1,0:T(8,128)(2,1)S(1)}, u32[]{:S(2)}, u32[]{:S(2)}) collective-permute-start(bf16[4,64,256]{2,1,0:T(8,128)(2,1)S(1)} %get-tuple-element.41), channel_id=1, source_target_pairs={{0,16},{8,24},{16,0},{24,8},{1,17},{9,25},{17,1},{25,9},{2,18},{10... | collective-permute-start | bytes 393224 | tf_op jit(solution)/shard_map/ppermute | solution.py:388
  20.0 6.4 %collective-permute-start.6 = (bf16[4,64,256]{2,1,0:T(8,128)(2,1)S(1)}, bf16[4,64,256]{2,1,0:T(8,128)(2,1)S(1)}, u32[]{:S(2)}, u32[]{:S(2)}) collective-permute-start(bf16[4,64,256]{2,1,0:T(8,128)(2,1)S(1)} %get-tuple-element.42), channel_id=1, source_target_pairs={{0,8},{8,0},{16,24},{24,16},{1,9},{9,1},{17,25},{25,17},{2,10},{10... | collective-permute-start | bytes 393224 | tf_op jit(solution)/shard_map/ppermute | solution.py:388
  26.5 5.9 %collective-permute-start.9 = (bf16[64,256]{1,0:T(8,128)(2,1)S(1)}, bf16[64,256]{1,0:T(8,128)(2,1)S(1)}, u32[]{:S(2)}, u32[]{:S(2)}) collective-permute-start(bf16[64,256]{1,0:T(8,128)(2,1)S(1)} %get-tuple-element.57), channel_id=1, source_target_pairs={{0,6},{1,7},{2,4},{3,5},{4,2},{5,3},{6,0},{7,1},{8,14},{9,15},{10,... | collective-permute-start | bytes 98312 | tf_op jit(solution)/shard_map/ppermute | solution.py:393
  28.7 4.9 %collective-permute-start.10 = (bf16[64,256]{1,0:T(8,128)(2,1)S(1)}, bf16[64,256]{1,0:T(8,128)(2,1)S(1)}, u32[]{:S(2)}, u32[]{:S(2)}) collective-permute-start(bf16[64,256]{1,0:T(8,128)(2,1)S(1)} %get-tuple-element.58), channel_id=1, source_target_pairs={{0,4},{1,5},{2,6},{3,7},{4,0},{5,1},{6,2},{7,3},{8,12},{9,13},{10,... | collective-permute-start | bytes 98312 | tf_op jit(solution)/shard_map/ppermute | solution.py:393
  28.7 4.9 %collective-permute-start.11 = (bf16[64,256]{1,0:T(8,128)(2,1)S(1)}, bf16[64,256]{1,0:T(8,128)(2,1)S(1)}, u32[]{:S(2)}, u32[]{:S(2)}) collective-permute-start(bf16[64,256]{1,0:T(8,128)(2,1)S(1)} %get-tuple-element.59), channel_id=1, source_target_pairs={{0,2},{1,3},{2,0},{3,1},{4,6},{5,7},{6,4},{7,5},{8,10},{9,11},{10,... | collective-permute-start | bytes 98312 | tf_op jit(solution)/shard_map/ppermute | solution.py:393
  31.0 9.6 %collective-permute-start.7 = (bf16[2,128,512]{2,1,0:T(8,128)(2,1)S(1)}, bf16[2,128,512]{2,1,0:T(8,128)(2,1)S(1)}, u32[]{:S(2)}, u32[]{:S(2)}) collective-permute-start(bf16[2,128,512]{2,1,0:T(8,128)(2,1)S(1)} %get-tuple-element.55), channel_id=1, source_target_pairs={{0,7},{1,2},{2,1},{3,4},{4,3},{5,6},{6,5},{7,0},{8,15},{9,10},{10,... | collective-permute-start | bytes 786440 | tf_op jit(solution)/shard_map/ppermute | solution.py:373
  31.7 8.8 %collective-permute-start.8 = (bf16[2,128,512]{2,1,0:T(8,128)(2,1)S(1)}, bf16[2,128,512]{2,1,0:T(8,128)(2,1)S(1)}, u32[]{:S(2)}, u32[]{:S(2)}) collective-permute-start(bf16[2,128,512]{2,1,0:T(8,128)(2,1)S(1)} %get-tuple-element.56), channel_id=1, source_target_pairs={{0,1},{1,0},{2,3},{3,2},{4,5},{5,4},{6,7},{7,6},{8,9},{9,8},{10,11... | collective-permute-start | bytes 786440 | tf_op jit(solution)/shard_map/ppermute | solution.py:374
  33.5 4.9 %collective-permute-start.14 = (bf16[64,256]{1,0:T(8,128)(2,1)S(1)}, bf16[64,256]{1,0:T(8,128)(2,1)S(1)}, u32[]{:S(2)}, u32[]{:S(2)}) collective-permute-start(bf16[64,256]{1,0:T(8,128)(2,1)S(1)} %multiply_convert_fusion.refs_0_), channel_id=1, source_target_pairs={{0,24},{8,16},{16,8},{24,0},{1,25},{9,17},{17,9},{25,1},{2,26},{10... | collective-permute-start | bytes 98312 | tf_op jit(solution)/shard_map/ppermute | solution.py:396
  35.3 3.9 %collective-permute-start.13 = (bf16[64,256]{1,0:T(8,128)(2,1)S(1)}, bf16[64,256]{1,0:T(8,128)(2,1)S(1)}, u32[]{:S(2)}, u32[]{:S(2)}) collective-permute-start(bf16[64,256]{1,0:T(8,128)(2,1)S(1)} %multiply_convert_fusion.refs_0_), channel_id=1, source_target_pairs={{0,16},{8,24},{16,0},{24,8},{1,17},{9,25},{17,1},{25,9},{2,18},{10... | collective-permute-start | bytes 98312 | tf_op jit(solution)/shard_map/ppermute | solution.py:396
  36.6 3.9 %collective-permute-start.12 = (bf16[64,256]{1,0:T(8,128)(2,1)S(1)}, bf16[64,256]{1,0:T(8,128)(2,1)S(1)}, u32[]{:S(2)}, u32[]{:S(2)}) collective-permute-start(bf16[64,256]{1,0:T(8,128)(2,1)S(1)} %multiply_convert_fusion.refs_0_), channel_id=1, source_target_pairs={{0,8},{8,0},{16,24},{24,16},{1,9},{9,1},{17,25},{25,17},{2,10},{10... | collective-permute-start | bytes 98312 | tf_op jit(solution)/shard_map/ppermute | solution.py:396

commit v9 on v8

--- a/solution.py
+++ b/solution.py
@@ -56,11 +56,6 @@
     return slice((b + first - RAD) * BLK, (b + last - RAD + 1) * BLK)
 
 
-def rim_candidates(b, blocks):
-    first, last = own_candidates(b, blocks)
-    return [(0, c) for c in range(first)] + [(1, c) for c in range(last + 1, CAND)]
-
-
 def masked(mask, b, c, part):
     return part if c == RAD else jnp.where(mask[b, c] == 1, part, BIG_NEGATIVE)
 
@@ -68,16 +63,49 @@
 def pairs_of(blocks):
     for b in range(blocks):
         for p in range(PAIRS):
-            yield b, slice(b * BLK, (b + 1) * BLK), slice(p * PAIR, (p + 1) * PAIR), b * PAIRS + p
+            yield b, slice(b * BLK, (b + 1) * BLK), slice(p * PAIR, (p + 1) * PAIR), p
 
 
 def at_core():
     return lax.rem(lax.axis_index("ctx"), 2)
 
 
+def rim_block(blocks, over_link):
+    core = at_core()
+    upper = core if over_link else 1 - core
+    return upper * (blocks - 1), upper * (CAND - 1)
+
+
+def rows_of(b):
+    return pl.ds(pl.multiple_of(b * BLK, BLK), BLK)
+
+
+def copy_all(pairs, sems):
+    copies = [pltpu.make_async_copy(a, b, sems.at[i]) for i, (a, b) in enumerate(pairs)]
+    for copy in copies:
+        copy.start()
+    for copy in copies:
+        copy.wait()
+
+
+def pack_link_kernel(k, v, out, sems):
+    rows = rows_of(rim_block(k.shape[0] // BLK, True)[0])
+    copy_all([(k.at[rows], out.at[0]), (v.at[rows], out.at[1])], sems)
+
+
+def pack_chip_kernel(k, v, k_out, v_out, sems):
+    rows = rows_of(rim_block(k.shape[0] // BLK, False)[0])
+    copy_all([(k.at[rows], k_out), (v.at[rows], v_out)], sems)
+
+
+def load_kernel(*refs):
+    count = len(refs) // 2
+    copy_all(list(zip(refs[:count], refs[count:-1])), refs[-1])
+
+
 def own_kernel(mask, q, k, v, g, w_out, own_t, stats, exps, grad_t):
     blocks = q.shape[0] // BLK
-    for b, rows, cols, at in pairs_of(blocks):
+    for b, rows, cols, p in pairs_of(blocks):
         first, last = own_candidates(b, blocks)
         here = own_rows(b, blocks)
         scores = dot(k[here, cols], two_heads(q[rows, cols] * SCALE, 1), ((1,), (1,)))
@@ -90,54 +118,88 @@
         )
         top = jnp.max(scores, axis=0, keepdims=True)
         e = jnp.exp(scores - top)
-        exps[at, : e.shape[0]] = e
-        stats[0, at : at + 1] = top
-        stats[1, at : at + 1] = jnp.sum(e, axis=0, keepdims=True)
-        own_t[cols, rows] = own_features(dot(v[here, cols], e.astype(BF16), ((0,), (0,))))
-    grad_t[...] = dot(w_out[...], g[...], ((1,), (1,))).astype(BF16)
+        exps[b, p, : e.shape[0]] = e
+        stats[0, b, p : p + 1] = top
+        stats[1, b, p : p + 1] = jnp.sum(e, axis=0, keepdims=True)
+        own_t[b, cols] = own_features(dot(v[here, cols], e.astype(BF16), ((0,), (0,))))
+    for b in range(blocks):
+        rows = slice(b * BLK, (b + 1) * BLK)
+        grad_t[b] = dot(w_out[...], g[rows], ((1,), (1,))).astype(BF16)
+
+
+def with_rim(mask, q, rim_k, rim_v, b, c, p, old_top, old_sum):
+    cols = slice(p * PAIR, (p + 1) * PAIR)
+    scores = dot(rim_k[:, cols], two_heads(q[rows_of(b), cols] * SCALE, 1), ((1,), (1,)))
+    scores = jnp.where(mask[b, c] == 1, scores, BIG_NEGATIVE)
+    top = jnp.maximum(old_top, jnp.max(scores, axis=0, keepdims=True))
+    kept = jnp.exp(old_top - top)
+    e = jnp.exp(scores - top)
+    count = old_sum * kept + jnp.sum(e, axis=0, keepdims=True)
+    part = own_features(dot(rim_v[:, cols], e.astype(BF16), ((0,), (0,))))
+    return top, kept, count, e, part
+
+
+def chip_kernel(mask, q, rim_k, rim_v, own_t, stats, chip_t, chip_stats, exps):
+    b, c = rim_block(q.shape[0] // BLK, False)
+    for p in range(PAIRS):
+        cols = slice(p * PAIR, (p + 1) * PAIR)
+        top, kept, count, e, part = with_rim(
+            mask, q, rim_k, rim_v, b, c, p, stats[0, b, p : p + 1], stats[1, b, p : p + 1]
+        )
+        chip_t[cols] = own_t[b, cols] * spread(kept) + part
+        chip_stats[0, p : p + 1] = top
+        chip_stats[1, p : p + 1] = count
+        exps[p] = e
 
 
 def forward_kernel(
-    mask, q, low, high, own_t, stats, before, attn_t, mine, other, exps, factors
+    mask, q, rim, own_t, stats, chip_t, chip_stats,
+    attn_t, mine, other, exps, own_factors, rim_factors,
 ):
     blocks = q.shape[0] // BLK
-    sides = (low, high)
-    for b, rows, cols, at in pairs_of(blocks):
-        rims = rim_candidates(b, blocks)
-        old = stats[0, at : at + 1]
-        q2 = two_heads(q[rows, cols] * SCALE, 1)
-        scores = [masked(mask, b, c, dot(sides[s][0, :, cols], q2, ((1,), (1,)))) for s, c in rims]
-        top = old
-        for part in scores:
-            top = jnp.maximum(top, jnp.max(part, axis=0, keepdims=True))
-        kept = jnp.exp(old - top)
-        count = stats[1, at : at + 1] * kept
-        both = None
-        for (s, _), part in zip(rims, scores):
-            e = jnp.exp(part - top)
-            exps[s, at % PAIRS] = e
-            count = count + jnp.sum(e, axis=0, keepdims=True)
-            more = dot(sides[s][1, :, cols], e.astype(BF16), ((0,), (0,)))
-            both = more if both is None else both + more
+    b, c = rim_block(blocks, True)
+    at_chip, _ = rim_block(blocks, False)
+    for p in range(PAIRS):
+        at = slice(p, p + 1)
+        cols = slice(p * PAIR, (p + 1) * PAIR)
+        if blocks == 1:
+            base, old_top, old_sum = chip_t[cols], chip_stats[0, at], chip_stats[1, at]
+        else:
+            base, old_top, old_sum = own_t[b, cols], stats[0, b, at], stats[1, b, at]
+        top, kept, count, e, part = with_rim(
+            mask, q, rim.at[0], rim.at[1], b, c, p, old_top, old_sum
+        )
         share = 1.0 / count
-        factors[0, at : at + 1] = kept * share
-        factors[1, at : at + 1] = share
-        attn = own_t[cols, rows] * spread(kept * share)
-        if both is not None:
-            attn = attn + own_features(both) * spread(share)
-        attn_t[cols, rows] = attn.astype(BF16)
+        attn_t[b, cols] = (base * spread(kept * share) + part * spread(share)).astype(BF16)
+        exps[p] = e
+        rim_factors[0, at] = share
+        if blocks == 1:
+            rim_factors[1, at] = kept * share
+            own_factors[0, at] = jnp.exp(stats[0, 0, at] - top) * share
+        else:
+            own_factors[b, at] = kept * share
+            share = 1.0 / chip_stats[1, at]
+            attn_t[at_chip, cols] = (chip_t[cols] * spread(share)).astype(BF16)
+            rim_factors[1, at] = share
+            own_factors[at_chip, at] = jnp.exp(stats[0, at_chip, at] - chip_stats[0, at]) * share
+        for inner in range(1, blocks - 1):
+            share = 1.0 / stats[1, inner, at]
+            attn_t[inner, cols] = (own_t[inner, cols] * spread(share)).astype(BF16)
+            own_factors[inner, at] = share
     core = at_core()
     chips, rows, _ = mine.shape
     for c in range(2 * chips):
-        value = attn_t[c * rows : (c + 1) * rows]
-
-        @pl.when(core == c % 2)
-        def _(c=c, value=value):
-            mine[c // 2] = value
-
-        @pl.when(core != c % 2)
-        def _(c=c, value=value):
-            other[c // 2] = value
+        for i in range(blocks):
+            value = attn_t[i, c * rows : (c + 1) * rows]
+            tokens = slice(i * BLK, (i + 1) * BLK)
+
+            @pl.when(core == c % 2)
+            def _(c=c, value=value, tokens=tokens):
+                mine[c // 2, :, tokens] = value
+
+            @pl.when(core != c % 2)
+            def _(c=c, value=value, tokens=tokens):
+                other[c // 2, :, tokens] = value
 
 
 def flat_dot(attn, g):
@@ -157,39 +219,38 @@
 
 
 def rim_kernel(
-    q, low, high, grad_t, attn_t, exps, factors, before, to_link, to_chip, deltas, query_t
+    q, link, chip_k, chip_v, grad_t, attn_t, link_exps, chip_exps, rim_factors, before,
+    to_link, to_chip, deltas, query_t,
 ):
     blocks = q.shape[0] // BLK
-    first_core = at_core() == 0
-    parts = {}
-    for b, rows, cols, at in pairs_of(blocks):
-        product = grad_t[cols, rows].astype(F32) * attn_t[cols, rows].astype(F32)
-        delta = jnp.concatenate(
+    for b, _, cols, p in pairs_of(blocks):
+        product = grad_t[b, cols].astype(F32) * attn_t[b, cols].astype(F32)
+        deltas[b, p : p + 1] = jnp.concatenate(
             [
                 jnp.sum(product[:HD], axis=0, keepdims=True),
                 jnp.sum(product[HD:], axis=0, keepdims=True),
             ],
             axis=1,
         )
-        deltas[at : at + 1] = delta
-        q2 = two_heads(q[rows, cols] * SCALE, 1)
-        g2_t = two_heads(grad_t[cols, rows], 0)
-        total_t = jnp.zeros((PAIR, BLK), F32)
-        for s, _ in rim_candidates(b, blocks):
-            rim = (low, high)[s]
-            probs = exps[s, at % PAIRS] * factors[1, at : at + 1]
+    query_t[...] = jnp.zeros_like(query_t)
+    link_side = (link.at[0], link.at[1], link_exps, to_link)
+    for i, (rim_k, rim_v, exps, back) in enumerate(
+        (link_side, (chip_k, chip_v, chip_exps, to_chip))
+    ):
+        b, _ = rim_block(blocks, i == 0)
+        for p in range(PAIRS):
+            cols = slice(p * PAIR, (p + 1) * PAIR)
             part_t, k_part, v_part = backward(
-                probs, delta, rim[0, :, cols], rim[1, :, cols], q2, g2_t
+                exps[p] * rim_factors[i, p : p + 1],
+                deltas[b, p : p + 1],
+                rim_k[:, cols],
+                rim_v[:, cols],
+                two_heads(q[rows_of(b), cols] * SCALE, 1),
+                two_heads(grad_t[b, cols], 0),
             )
-            total_t = total_t + part_t
-            parts[s, at % PAIRS] = (k_part.astype(BF16), v_part.astype(BF16))
-            if len(parts) > PAIRS and (1 - s, at % PAIRS) in parts:
-                for which in range(2):
-                    below = parts[0, at % PAIRS][which]
-                    above = parts[1, at % PAIRS][which]
-                    to_link[which, :, cols] = jnp.where(first_core, below, above)
-                    to_chip[which, :, cols] = jnp.where(first_core, above, below)
-        query_t[cols, rows] = total_t
+            query_t[b, cols] += part_t
+            back[0, :, cols] = k_part.astype(BF16)
+            back[1, :, cols] = v_part.astype(BF16)
 
 
 def own_backward_kernel(
@@ -198,22 +259,26 @@
     blocks = q.shape[0] // BLK
     k_own[...] = jnp.zeros_like(k_own)
     v_own[...] = jnp.zeros_like(v_own)
-    for b, rows, cols, at in pairs_of(blocks):
+    for b, rows, cols, p in pairs_of(blocks):
         here = own_rows(b, blocks)
-        probs = exps[at, : here.stop - here.start] * factors[0, at : at + 1]
-        q2 = two_heads(q[rows, cols] * SCALE, 1)
-        g2_t = two_heads(grad_t[cols, rows], 0)
         part_t, k_part, v_part = backward(
-            probs, deltas[at : at + 1], k[here, cols], v[here, cols], q2, g2_t
+            exps[b, p, : here.stop - here.start] * factors[b, p : p + 1],
+            deltas[b, p : p + 1],
+            k[here, cols],
+            v[here, cols],
+            two_heads(q[rows, cols] * SCALE, 1),
+            two_heads(grad_t[b, cols], 0),
         )
-        q_grad[rows, cols] = (part_t + rim_t[cols, rows]).T.astype(BF16)
+        q_grad[rows, cols] = (part_t + rim_t[b, cols]).T.astype(BF16)
         k_own[here, cols] += k_part
         v_own[here, cols] += v_part
     after[...] = jnp.zeros_like(after)
 
 
 def output_kernel(attn_t, w_out, before, output):
-    output[...] = dot(attn_t[...], w_out[...], ((0,), (0,))).astype(BF16)
+    for b in range(attn_t.shape[0]):
+        part = dot(attn_t[b], w_out[...], ((0,), (0,)))
+        output[b * BLK : (b + 1) * BLK] = part.astype(BF16)
 
 
 def halves_kernel(product, other, g, *outs):
@@ -240,7 +305,7 @@
 
 
 def last_kernel(k_own, v_own, from_link, from_chip, *refs):
-    pieces, (k_grad, v_grad, weight_grad) = refs[:-3], refs[-3:]
+    pieces, (k_grad, v_grad, weight_grad) = refs[:1] + refs[-4:0:-1], refs[-3:]
     tokens = k_own.shape[0]
     first_core = at_core() == 0
     for which, (own, grad) in enumerate(((k_own, k_grad), (v_own, v_grad))):
@@ -286,6 +351,18 @@
     )(*masks, *args)
 
 
+def from_hbm(kernel, outs, *args):
+    return pl.pallas_call(
+        kernel,
+        out_shape=outs,
+        in_specs=[pl.BlockSpec(memory_space=pltpu.HBM)] * len(args),
+        out_specs=[pl.BlockSpec(memory_space=pltpu.VMEM)] * len(outs),
+        scratch_shapes=[pltpu.SemaphoreType.DMA((len(args),))],
+        compiler_params=pltpu.CompilerParams(vmem_limit_bytes=1024 * 1024),
+        cost_estimate=pl.CostEstimate(flops=0, bytes_accessed=4096, transcendentals=0),
+    )(*(pltpu.with_memory_space_constraint(x, pltpu.HBM) for x in args))
+
+
 def swap(count, bits):
     return [(i, i ^ bits) for i in range(count)]
 
@@ -306,47 +383,53 @@
     ctx, dp = lax.axis_size("ctx"), lax.axis_size("dp")
     chips = ctx // 2
     at_ctx = lax.axis_index("ctx")
-    core = at_ctx % 2
     rows, cols = feats // ctx, width // dp
-    groups = blocks * PAIRS
-
-    link_row = core * (tokens - RIM)
-    chip_row = tokens - RIM - link_row
-
-    def rim(row):
-        return jnp.stack([lax.dynamic_slice_in_dim(x, row, RIM, 0) for x in (k, v)])
-
-    from_link = lax.ppermute(rim(link_row), "ctx", over_links(ctx))
-    from_chip = lax.ppermute(rim(chip_row), "ctx", swap(ctx, 1))
+
+    (to_link,) = from_hbm(pack_link_kernel, [vmem(2, RIM, feats)], k, v)
+    link = lax.ppermute(to_link, "ctx", over_links(ctx))
+    to_chip = from_hbm(pack_chip_kernel, [vmem(RIM, feats)] * 2, k, v)
+    chip_k, chip_v = (lax.ppermute(x, "ctx", swap(ctx, 1)) for x in to_chip)
     sibling_g = lax.ppermute(g, "ctx", swap(ctx, 1))
     sibling_g = pltpu.with_memory_space_constraint(sibling_g, pltpu.VMEM)
-    low = jnp.where(core == 0, from_link, from_chip)
-    high = jnp.where(core == 0, from_chip, from_link)
+    args = (q, k, v, g, w_out)
+    q, k, v, g, w_out = from_hbm(load_kernel, [vmem(*x.shape) for x in args], *args)
 
     mask = lax.dynamic_slice_in_dim(block_mask[0], at_ctx * blocks, blocks, 0)
     own_t, stats, own_exps, grad_t = call(
         own_kernel,
         [
-            vmem(feats, tokens, dtype=F32),
-            vmem(2, groups, 2 * BLK, dtype=F32),
-            vmem(groups, min(CAND, blocks) * BLK, 2 * BLK, dtype=F32),
-            vmem(feats, tokens),
-        ],
-        10**9,
+            vmem(blocks, feats, BLK, dtype=F32),
+            vmem(2, blocks, PAIRS, 2 * BLK, dtype=F32),
+            vmem(blocks, PAIRS, min(CAND, blocks) * BLK, 2 * BLK, dtype=F32),
+            vmem(blocks, feats, BLK),
+        ],
+        10**6,
         q, k, v, g, w_out,
         mask=mask,
     )
-    attn_t, mine, other, rim_exps, factors = call(
+    chip_t, chip_stats, chip_exps = call(
+        chip_kernel,
+        [
+            vmem(feats, BLK, dtype=F32),
+            vmem(2, PAIRS, 2 * BLK, dtype=F32),
+            vmem(PAIRS, RIM, 2 * BLK, dtype=F32),
+        ],
+        10**6,
+        q, chip_k, chip_v, own_t, stats,
+        mask=mask,
+    )
+    attn_t, mine, other, link_exps, own_factors, rim_factors = call(
         forward_kernel,
         [
-            vmem(feats, tokens),
+            vmem(blocks, feats, BLK),
             vmem(chips, rows, tokens),
             vmem(chips, rows, tokens),
-            vmem(2, PAIRS, RIM, 2 * BLK, dtype=F32),
-            vmem(2, groups, 2 * BLK, dtype=F32),
-        ],
-        10**9,
-        q, low, high, own_t, stats, sibling_g,
+            vmem(PAIRS, RIM, 2 * BLK, dtype=F32),
+            vmem(blocks, PAIRS, 2 * BLK, dtype=F32),
+            vmem(2, PAIRS, 2 * BLK, dtype=F32),
+        ],
+        10**6,
+        q, link, own_t, stats, chip_t, chip_stats,
         mask=mask,
     )
 
@@ -364,11 +447,11 @@
         [
             vmem(2, RIM, feats),
             vmem(2, RIM, feats),
-            vmem(groups, 2 * BLK, dtype=F32),
-            vmem(feats, tokens, dtype=F32),
-        ],
-        10**6,
-        q, low, high, grad_t, attn_t, rim_exps, factors, after,
+            vmem(blocks, PAIRS, 2 * BLK, dtype=F32),
+            vmem(blocks, feats, BLK, dtype=F32),
+        ],
+        10**6,
+        q, link, chip_k, chip_v, grad_t, attn_t, link_exps, chip_exps, rim_factors, after,
     )
     grad_link = lax.ppermute(to_link, "ctx", over_links(ctx))
     grad_chip = lax.ppermute(to_chip, "ctx", swap(ctx, 1))
@@ -382,7 +465,7 @@
             vmem(8, 128, dtype=F32),
         ],
         10**6,
-        q, k, v, grad_t, own_exps, factors, deltas, rim_t, after,
+        q, k, v, grad_t, own_exps, own_factors, deltas, rim_t, after,
     )
 
     halves = [halves[0]] + [lax.ppermute(halves[s], "dp", swap(dp, s)) for s in range(dp - 1, 0, -1)]
@@ -393,7 +476,7 @@
         + [lax.ppermute(quarters[s], "ctx", swap(ctx, 2 * s)) for s in range(chips - 1, 0, -1)]
     )
     piece = (piece * (dp * tokens * ctx) ** (-0.5)).astype(BF16)
-    pieces = [piece] + [lax.ppermute(piece, "dp", swap(dp, s)) for s in range(1, dp)]
+    pieces = [piece] + [lax.ppermute(piece, "dp", swap(dp, s)) for s in range(dp - 1, 0, -1)]
     k_grad, v_grad, weight_grad = call(
         last_kernel,
         [hbm(tokens, feats), hbm(tokens, feats), hbm(rows, width, dtype=F32)],

time: 41.7 us -> 42.4 us (1.017)
  Pallas kernels: 12.5 us -> 17.5 us
  local copies, waits for them, and re-layouts: 2.5 us -> 0.18 us
  waiting for transfers between devices: 7.44 us -> 6.03 us
  starting transfers between devices: 18.2 us -> 17.7 us
    pallas_call x0 -> x3, Pallas kernels: none -> 3.64 us  [from_hbm(): pl.pallas_call(kernel, out_shape=outs, in_specs=[pl.BlockSpec(memory_spac...]
    pallas_call x9 -> x10, Pallas kernels: 12.5 us -> 13.9 us  [call(): pl.pallas_call(kernel, out_shape=outs, in_specs=[in_smem] * len(masks) +...]
    dynamic_slice x1 -> x0, local copies, waits for them, and re-layouts: 1.26 us -> none  [rim(): return jnp.stack([lax.dynamic_slice_in_dim(x, row, RIM, 0) for x in (k, v)])]
    unnamed x14 -> x2, local copies, waits for them, and re-layouts: 1.07 us -> 0.01 us
    ppermute x2 -> x3, waiting for transfers between devices: 0.86 us -> 0.01 us  [the longest x2 0.01 us: body(): chip_k, chip_v = (lax.ppermute(x, 'ctx', swap(ctx, 1)) for x in to_chip)]
    ppermute x1, starting transfers between devices: 0.77 us -> 0.01 us  [body(): grad_link = lax.ppermute(to_link, 'ctx', over_links(ctx))]
    ppermute x3, starting transfers between devices: 4.21 us -> 3.55 us  [body(): lax.ppermute(halves[s], 'dp', swap(dp, s))]
    ppermute x1, starting transfers between devices: 0.01 us -> 0.52 us  [body(): sibling_g = lax.ppermute(g, 'ctx', swap(ctx, 1))]
  transfers between devices with their start and end apart: 15 -> 16, of which waited for: 10 -> 7; matrix products, arithmetic and copies ran while one was open for 1% -> 0% of each run, Pallas kernels for 23% -> 38%
where the time goes in v9:
time: 42.4 us; the launch traced here: 42.2 us
  starting transfers between devices  17.7 us (42%)
  Pallas kernels  17.5 us (41%)
  waiting for transfers between devices  6.03 us (14%)
  between operations  0.75 us (2%)
    pallas_call x10, Pallas kernels, call(): pl.pallas_call(kernel, out_shape=outs, in_specs=[in_smem] * len(masks) +...  13.9 us
    ppermute x1, starting transfers between devices, body(): link = lax.ppermute(to_link, 'ctx', over_links(ctx))  4.78 us
    ppermute x3, starting transfers between devices, body(): lax.ppermute(quarters[s], 'ctx', swap(ctx, 2 * s))  4.45 us
    pallas_call x3, Pallas kernels, from_hbm(): pl.pallas_call(kernel, out_shape=outs, in_specs=[pl.BlockSpec(memory_spac...  3.64 us
    ppermute x3, starting transfers between devices, body(): lax.ppermute(halves[s], 'dp', swap(dp, s))  3.55 us
    ppermute x3, starting transfers between devices, body(): lax.ppermute(piece, 'dp', swap(dp, s))  3.55 us
    ppermute x3, waiting for transfers between devices, body(): lax.ppermute(piece, 'dp', swap(dp, s))  2.11 us
    ppermute x3, waiting for transfers between devices, body(): lax.ppermute(quarters[s], 'ctx', swap(ctx, 2 * s))  1.74 us
  transfers between devices with their start and end apart: 16, of which 7 were waited for; matrix products, arithmetic and copies ran while one was open for 0% of the time, Pallas kernels for 38%

profile of v9, /device:TPU:0, one launch (start us, length us, event | category | flops | bytes accessed | tf_op | source)
XLA Modules:
  0.0 42.2 jit_solution(4786993510684198900)
XLA Ops:
  0.6 0.0 copy-start
  0.6 0.5 %collective-permute-start.4 = (bf16[256,1024]{1,0:T(8,128)(2,1)}, bf16[256,1024]{1,0:T(8,128)(2,1)S(1)}, u32[]{:S(2)}, u32[]{:S(2)}) collective-permute-start(bf16[256,1024]{1,0:T(8,128)(2,1)} %bitcast.19), channel_id=1, source_target_pairs={{0,1},{1,0},{2,3},{3,2},{4,5},{5,4},{6,7},{7,6},{8,9},{9,8},{10,11... | collective-permute-start | bytes 1572872 | tf_op jit(solution)/shard_map/ppermute | solution.py:392
  1.2 1.0 %shard_map.102 = bf16[2,128,512]{2,1,0:T(8,128)(2,1)S(1)} custom-call(bf16[256,512]{1,0:T(8,128)(2,1)} %bitcast.12, bf16[256,512]{1,0:T(8,128)(2,1)} %bitcast.15), custom_call_target="tpu_custom_call" | custom-call | bytes 4096 | tf_op jit(solution)/shard_map/pallas_call | solution.py:355
  2.2 4.8 %collective-permute-start = (bf16[2,128,512]{2,1,0:T(8,128)(2,1)S(1)}, bf16[2,128,512]{2,1,0:T(8,128)(2,1)S(1)}, u32[]{:S(2)}, u32[]{:S(2)}) collective-permute-start(bf16[2,128,512]{2,1,0:T(8,128)(2,1)S(1)} %shard_map.102), channel_id=1, source_target_pairs={{0,7},{1,2},{2,1},{3,4},{4,3},{5,6},{6,5},{7,0},{8,15},{9,10},{10,... | collective-permute-start | bytes 786440 | tf_op jit(solution)/shard_map/ppermute | solution.py:389
  6.9 1.0 %shard_map.104 = (bf16[128,512]{1,0:T(8,128)(2,1)S(1)}, bf16[128,512]{1,0:T(8,128)(2,1)S(1)}) custom-call(bf16[256,512]{1,0:T(8,128)(2,1)} %bitcast.13, bf16[256,512]{1,0:T(8,128)(2,1)} %bitcast.16), custom_call_target="tpu_custom_call" | custom-call | bytes 4096 | tf_op jit(solution)/shard_map/pallas_call | solution.py:355
  7.9 0.1 collective-permute-start.1
  8.0 0.5 %collective-permute-start.2 = (bf16[128,512]{1,0:T(8,128)(2,1)S(1)}, bf16[128,512]{1,0:T(8,128)(2,1)S(1)}, u32[]{:S(2)}, u32[]{:S(2)}) collective-permute-start(bf16[128,512]{1,0:T(8,128)(2,1)S(1)} %get-tuple-element.53), channel_id=1, source_target_pairs={{0,1},{1,0},{2,3},{3,2},{4,5},{5,4},{6,7},{7,6},{8,9},{9,8},{10,11... | collective-permute-start | bytes 393224 | tf_op jit(solution)/shard_map/ppermute | solution.py:391
  8.5 0.1 constant_dynamic-slice_fusion
  8.6 0.1 copy.11
  8.7 1.7 %shard_map.101 = (bf16[256,512]{1,0:T(8,128)(2,1)S(1)}, bf16[256,512]{1,0:T(8,128)(2,1)S(1)}, bf16[256,512]{1,0:T(8,128)(2,1)S(1)}, bf16[256,1024]{1,0:T(8,128)(2,1)S(1)}, bf16[512,1024]{1,0:T(8,128)(2,1)S(1)}) custom-call(bf16[256,512]{1,0:T(8,128)(2,1)} %bitcast.21, bf16[256,512]{1,0:T(8,128)(2,1)} %bitcast.14, bf16[256,512]{1,0:T(8,128)(2,1)} %bitcast.17, ...), custom_call_target="tpu_custom_call" | custom-call | bytes 4096 | tf_op jit(solution)/shard_map/pallas_call | solution.py:355
  10.4 3.6 %shard_map.103 = (f32[2,512,128]{2,1,0:T(8,128)S(1)}, f32[2,2,4,256]{3,2,1,0:T(4,128)S(1)}, f32[2,4,256,256]{3,2,1,0:T(8,128)S(1)}, bf16[2,512,128]{2,1,0:T(8,128)(2,1)S(1)}) custom-call(s32[2,3]{1,0:T(2,128)S(1)} %bitcast.9, bf16[256,512]{1,0:T(8,128)(2,1)S(1)} %get-tuple-element.45.q, bf16[256,512]{1,0:T(8,128)(2,1)S(1)} %get-tuple-element.46.k, ...), custom_call_target="tpu_custom_call" | custom-call | flops 1000000 | bytes 4000 | tf_op jit(solution)/shard_map/pallas_call | solution.py:344
  13.9 0.0 collective-permute-done.1.rim_k.chip_k
  13.9 0.0 collective-permute-done.2.rim_v.chip_v
  13.9 1.2 %shard_map.105 = (f32[512,128]{1,0:T(8,128)S(1)}, f32[2,4,256]{2,1,0:T(4,128)S(1)}, f32[4,128,256]{2,1,0:T(8,128)S(1)}) custom-call(s32[2,3]{1,0:T(2,128)S(1)} %bitcast.10, bf16[256,512]{1,0:T(8,128)(2,1)S(1)} %get-tuple-element.45.q, bf16[128,512]{1,0:T(8,128)(2,1)S(1)} %collective-permute-done.1.rim_k.chip_k, ...), custom_call_target="tpu_custom_call" | custom-call | flops 1000000 | bytes 4000 | tf_op jit(solution)/shard_map/pallas_call | solution.py:344
  15.2 0.0 collective-permute-done.rim.link
  15.2 1.4 %shard_map.106 = (bf16[2,512,128]{2,1,0:T(8,128)(2,1)S(1)}, bf16[4,64,256]{2,1,0:T(8,128)(2,1)S(1)}, bf16[4,64,256]{2,1,0:T(8,128)(2,1)S(1)}, f32[4,128,256]{2,1...) custom-call(s32[2,3]{1,0:T(2,128)S(1)} %bitcast.11, bf16[256,512]{1,0:T(8,128)(2,1)S(1)} %get-tuple-element.45.q, ...), custom_call_target="tpu_custom_call" | custom-call | flops 1000000 | bytes 4000 | tf_op jit(solution)/shard_map/pallas_call | solution.py:344
  16.6 0.1 collective-permute-start.3
  16.7 0.3 shard_map.107.product
  17.0 1.0 %collective-permute-done.3.other = bf16[4,64,256]{2,1,0:T(8,128)(2,1)S(1)} collective-permute-done((bf16[4,64,256]{2,1,0:T(8,128)(2,1)S(1)}, bf16[4,64,256]{2,1,0:T(8,128)(2,1)S(1)}, u32[]{:S(2)}, u32[]{:S(2)}) %collective-permute-start.3) | collective-permute-done | bytes 131104 | tf_op jit(solution)/shard_map/ppermute | solution.py:436
  18.0 0.0 collective-permute-done.4.g
  18.0 0.4 %shard_map.108 = (bf16[4,64,256]{2,1,0:T(8,128)(2,1)S(1)}, bf16[4,64,256]{2,1,0:T(8,128)(2,1)S(1)}, bf16[4,64,256]{2,1,0:T(8,128)(2,1)S(1)}, bf16[4,64,256]{2,1,0:T(8,128)(2,1)S(1)}, f32[8,128]{1,0:T(8,128)S(1)}) custom-call(f32[256,1024]{1,0:T(8,128)S(1)} %shard_map.107.product, bf16[4,64,256]{2,1,0:T(8,128)(2,1)S(1)} %collective-permute-done.3.other, ...), custom_call_target="tpu_custom_call" | custom-call | flops 1000000 | bytes 4000 | tf_op jit(solution)/shard_map/pallas_call | solution.py:344
  18.4 2.5 %collective-permute-start.5 = (bf16[4,64,256]{2,1,0:T(8,128)(2,1)S(1)}, bf16[4,64,256]{2,1,0:T(8,128)(2,1)S(1)}, u32[]{:S(2)}, u32[]{:S(2)}) collective-permute-start(bf16[4,64,256]{2,1,0:T(8,128)(2,1)S(1)} %get-tuple-element.60), channel_id=1, source_target_pairs={{0,24},{8,16},{16,8},{24,0},{1,25},{9,17},{17,9},{25,1},{2,26},{10... | collective-permute-start | bytes 393224 | tf_op jit(solution)/shard_map/ppermute | solution.py:471
  20.9 0.5 %collective-permute-start.6 = (bf16[4,64,256]{2,1,0:T(8,128)(2,1)S(1)}, bf16[4,64,256]{2,1,0:T(8,128)(2,1)S(1)}, u32[]{:S(2)}, u32[]{:S(2)}) collective-permute-start(bf16[4,64,256]{2,1,0:T(8,128)(2,1)S(1)} %get-tuple-element.61), channel_id=1, source_target_pairs={{0,16},{8,24},{16,0},{24,8},{1,17},{9,25},{17,1},{25,9},{2,18},{10... | collective-permute-start | bytes 393224 | tf_op jit(solution)/shard_map/ppermute | solution.py:471
  21.4 0.5 %collective-permute-start.7 = (bf16[4,64,256]{2,1,0:T(8,128)(2,1)S(1)}, bf16[4,64,256]{2,1,0:T(8,128)(2,1)S(1)}, u32[]{:S(2)}, u32[]{:S(2)}) collective-permute-start(bf16[4,64,256]{2,1,0:T(8,128)(2,1)S(1)} %get-tuple-element.62), channel_id=1, source_target_pairs={{0,8},{8,0},{16,24},{24,16},{1,9},{9,1},{17,25},{25,17},{2,10},{10... | collective-permute-start | bytes 393224 | tf_op jit(solution)/shard_map/ppermute | solution.py:471
  22.0 1.5 %shard_map.109 = (bf16[2,128,512]{2,1,0:T(8,128)(2,1)S(1)}, bf16[2,128,512]{2,1,0:T(8,128)(2,1)S(1)}, f32[2,4,256]{2,1,0:T(4,128)S(1)}, f32[2,512,128]{2,1,0:T(8,128)S(1)}) custom-call(bf16[256,512]{1,0:T(8,128)(2,1)S(1)} %get-tuple-element.45.q, bf16[2,128,512]{2,1,0:T(8,128)(2,1)S(1)} %collective-permute-done.rim.link, ...), custom_call_target="tpu_custom_call" | custom-call | flops 1000000 | bytes 4000 | tf_op jit(solution)/shard_map/pallas_call | solution.py:344
  23.4 3.2 %shard_map.110 = (bf16[256,512]{1,0:T(8,128)(2,1)}, f32[256,512]{1,0:T(8,128)S(1)}, f32[256,512]{1,0:T(8,128)S(1)}, f32[8,128]{1,0:T(8,128)S(1)}) custom-call(bf16[256,512]{1,0:T(8,128)(2,1)S(1)} %get-tuple-element.45.q, bf16[256,512]{1,0:T(8,128)(2,1)S(1)} %get-tuple-element.46.k, bf16[256,512]{1,0:T(8,128)(2,1)S(1)} %get-tuple-element.47.v, ...), custom_call_target="tpu_custom_call" | custom-call | flops 1000000 | bytes 4000 | tf_op jit(solution)/shard_map/pallas_call | solution.py:344
  26.6 0.0 collective-permute-done.5.refs_1_
  26.6 1.1 %collective-permute-done.6.refs_2_ = bf16[4,64,256]{2,1,0:T(8,128)(2,1)S(1)} collective-permute-done((bf16[4,64,256]{2,1,0:T(8,128)(2,1)S(1)}, bf16[4,64,256]{2,1,0:T(8,128)(2,1)S(1)}, u32[]{:S(2)}, u32[]{:S(2)}) %collective-permute-start.6) | collective-permute-done | bytes 131104 | tf_op jit(solution)/shard_map/ppermute | solution.py:471
  27.7 0.1 collective-permute-done.7.refs_3_
  27.8 0.1 shard_map.111
  27.9 0.5 %collective-permute-start.10 = (bf16[64,256]{1,0:T(8,128)(2,1)S(1)}, bf16[64,256]{1,0:T(8,128)(2,1)S(1)}, u32[]{:S(2)}, u32[]{:S(2)}) collective-permute-start(bf16[64,256]{1,0:T(8,128)(2,1)S(1)} %get-tuple-element.79), channel_id=1, source_target_pairs={{0,6},{1,7},{2,4},{3,5},{4,2},{5,3},{6,0},{7,1},{8,14},{9,15},{10,... | collective-permute-start | bytes 98312 | tf_op jit(solution)/shard_map/ppermute | solution.py:476
  28.4 0.5 %collective-permute-start.11 = (bf16[64,256]{1,0:T(8,128)(2,1)S(1)}, bf16[64,256]{1,0:T(8,128)(2,1)S(1)}, u32[]{:S(2)}, u32[]{:S(2)}) collective-permute-start(bf16[64,256]{1,0:T(8,128)(2,1)S(1)} %get-tuple-element.80), channel_id=1, source_target_pairs={{0,4},{1,5},{2,6},{3,7},{4,0},{5,1},{6,2},{7,3},{8,12},{9,13},{10,... | collective-permute-start | bytes 98312 | tf_op jit(solution)/shard_map/ppermute | solution.py:476
  28.9 3.5 %collective-permute-start.12 = (bf16[64,256]{1,0:T(8,128)(2,1)S(1)}, bf16[64,256]{1,0:T(8,128)(2,1)S(1)}, u32[]{:S(2)}, u32[]{:S(2)}) collective-permute-start(bf16[64,256]{1,0:T(8,128)(2,1)S(1)} %get-tuple-element.81), channel_id=1, source_target_pairs={{0,2},{1,3},{2,0},{3,1},{4,6},{5,7},{6,4},{7,5},{8,10},{9,11},{10,... | collective-permute-start | bytes 98312 | tf_op jit(solution)/shard_map/ppermute | solution.py:476
  32.4 0.0 collective-permute-start.8
  32.4 0.1 collective-permute-start.9
  32.5 1.2 %collective-permute-done.10 = bf16[64,256]{1,0:T(8,128)(2,1)S(1)} collective-permute-done((bf16[64,256]{1,0:T(8,128)(2,1)S(1)}, bf16[64,256]{1,0:T(8,128)(2,1)S(1)}, u32[]{:S(2)}, u32[]{:S(2)}) %collective-permute-start.10) | collective-permute-done | bytes 32800 | tf_op jit(solution)/shard_map/ppermute | solution.py:476
  33.7 0.0 collective-permute-done.11
  33.7 0.5 %collective-permute-done.12 = bf16[64,256]{1,0:T(8,128)(2,1)S(1)} collective-permute-done((bf16[64,256]{1,0:T(8,128)(2,1)S(1)}, bf16[64,256]{1,0:T(8,128)(2,1)S(1)}, u32[]{:S(2)}, u32[]{:S(2)}) %collective-permute-start.12) | collective-permute-done | bytes 32800 | tf_op jit(solution)/shard_map/ppermute | solution.py:476
  34.3 1.7 %collective-permute-start.13 = (bf16[64,256]{1,0:T(8,128)(2,1)S(1)}, bf16[64,256]{1,0:T(8,128)(2,1)S(1)}, u32[]{:S(2)}, u32[]{:S(2)}) collective-permute-start(bf16[64,256]{1,0:T(8,128)(2,1)S(1)} %multiply_convert_fusion.refs_0_), channel_id=1, source_target_pairs={{0,24},{8,16},{16,8},{24,0},{1,25},{9,17},{17,9},{25,1},{2,26},{10... | collective-permute-start | bytes 98312 | tf_op jit(solution)/shard_map/ppermute | solution.py:479
  36.0 1.3 %collective-permute-start.14 = (bf16[64,256]{1,0:T(8,128)(2,1)S(1)}, bf16[64,256]{1,0:T(8,128)(2,1)S(1)}, u32[]{:S(2)}, u32[]{:S(2)}) collective-permute-start(bf16[64,256]{1,0:T(8,128)(2,1)S(1)} %multiply_convert_fusion.refs_0_), channel_id=1, source_target_pairs={{0,16},{8,24},{16,0},{24,8},{1,17},{9,25},{17,1},{25,9},{2,18},{10... | collective-permute-start | bytes 98312 | tf_op jit(solution)/shard_map/ppermute | solution.py:479
  37.3 0.5 %collective-permute-start.15 = (bf16[64,256]{1,0:T(8,128)(2,1)S(1)}, bf16[64,256]{1,0:T(8,128)(2,1)S(1)}, u32[]{:S(2)}, u32[]{:S(2)}) collective-permute-start(bf16[64,256]{1,0:T(8,128)(2,1)S(1)} %multiply_convert_fusion.refs_0_), channel_id=1, source_target_pairs={{0,8},{8,0},{16,24},{24,16},{1,9},{9,1},{17,25},{25,17},{2,10},{10... | collective-permute-start | bytes 98312 | tf_op jit(solution)/shard_map/ppermute | solution.py:479
  37.8 1.3 %shard_map.112 = bf16[256,1024]{1,0:T(8,128)(2,1)} custom-call(bf16[2,512,128]{2,1,0:T(8,128)(2,1)S(1)} %get-tuple-element.56.attn_t, bf16[512,1024]{1,0:T(8,128)(2,1)S(1)} %get-tuple-element.49.w_out, bf16[64,256]{1,0:T(8,128)(2,1)S(1)} %get-tuple-element.73.before), custom_call_target="tpu_custom_call" | custom-call | flops 1000000 | bytes 4000 | tf_op jit(solution)/shard_map/pallas_call | solution.py:344
  39.1 0.0 collective-permute-done.13.refs_1_
  39.1 0.8 %collective-permute-done.14.refs_2_ = bf16[64,256]{1,0:T(8,128)(2,1)S(1)} collective-permute-done((bf16[64,256]{1,0:T(8,128)(2,1)S(1)}, bf16[64,256]{1,0:T(8,128)(2,1)S(1)}, u32[]{:S(2)}, u32[]{:S(2)}) %collective-permute-start.14) | collective-permute-done | bytes 32800 | tf_op jit(solution)/shard_map/ppermute | solution.py:479
  39.9 1.3 %collective-permute-done.15.refs_3_ = bf16[64,256]{1,0:T(8,128)(2,1)S(1)} collective-permute-done((bf16[64,256]{1,0:T(8,128)(2,1)S(1)}, bf16[64,256]{1,0:T(8,128)(2,1)S(1)}, u32[]{:S(2)}, u32[]{:S(2)}) %collective-permute-start.15) | collective-permute-done | bytes 32800 | tf_op jit(solution)/shard_map/ppermute | solution.py:479
  41.2 0.0 collective-permute-done.8.from_link
  41.2 0.0 collective-permute-done.9.from_chip
  41.2 1.0 %shard_map.113 = (bf16[256,512]{1,0:T(8,128)(2,1)}, bf16[256,512]{1,0:T(8,128)(2,1)}, f32[64,1024]{1,0:T(8,128)}) custom-call(f32[256,512]{1,0:T(8,128)S(1)} %get-tuple-element.75.k_own, f32[256,512]{1,0:T(8,128)S(1)} %get-tuple-element.76.v_own, bf16[2,128,512]{2,1,0:T(8,128)(2,1)S(1)} %collective-permute-done.8.from_link, ...), custom_call_target="tpu_custom_call" | custom-call | flops 1000000 | bytes 4000 | tf_op jit(solution)/shard_map/pallas_call | solution.py:344
  (2 shorter events, 0.0 us)
Async XLA Ops:
  0.6 7.9 %copy-start = (s32[1,16,3]{1,0,2:T(1,128)S(1)}, s32[1,16,3]{1,0,2:T(1,128)}, u32[]{:S(2)}) copy-start(s32[1,16,3]{1,0,2:T(1,128)} %param.11) | copy-start | bytes 580
  0.6 17.3 %collective-permute-start.4 = (bf16[256,1024]{1,0:T(8,128)(2,1)}, bf16[256,1024]{1,0:T(8,128)(2,1)S(1)}, u32[]{:S(2)}, u32[]{:S(2)}) collective-permute-start(bf16[256,1024]{1,0:T(8,128)(2,1)} %bitcast.19), channel_id=1, source_target_pairs={{0,1},{1,0},{2,3},{3,2},{4,5},{5,4},{6,7},{7,6},{8,9},{9,8},{10,11... | collective-permute-start | bytes 1572872 | tf_op jit(solution)/shard_map/ppermute | solution.py:392
  2.2 13.0 %collective-permute-start = (bf16[2,128,512]{2,1,0:T(8,128)(2,1)S(1)}, bf16[2,128,512]{2,1,0:T(8,128)(2,1)S(1)}, u32[]{:S(2)}, u32[]{:S(2)}) collective-permute-start(bf16[2,128,512]{2,1,0:T(8,128)(2,1)S(1)} %shard_map.102), channel_id=1, source_target_pairs={{0,7},{1,2},{2,1},{3,4},{4,3},{5,6},{6,5},{7,0},{8,15},{9,10},{10,... | collective-permute-start | bytes 786440 | tf_op jit(solution)/shard_map/ppermute | solution.py:389
  7.9 6.0 %collective-permute-start.1 = (bf16[128,512]{1,0:T(8,128)(2,1)S(1)}, bf16[128,512]{1,0:T(8,128)(2,1)S(1)}, u32[]{:S(2)}, u32[]{:S(2)}) collective-permute-start(bf16[128,512]{1,0:T(8,128)(2,1)S(1)} %get-tuple-element.52), channel_id=1, source_target_pairs={{0,1},{1,0},{2,3},{3,2},{4,5},{5,4},{6,7},{7,6},{8,9},{9,8},{10,11... | collective-permute-start | bytes 393224 | tf_op jit(solution)/shard_map/ppermute | solution.py:391
  8.0 5.9 %collective-permute-start.2 = (bf16[128,512]{1,0:T(8,128)(2,1)S(1)}, bf16[128,512]{1,0:T(8,128)(2,1)S(1)}, u32[]{:S(2)}, u32[]{:S(2)}) collective-permute-start(bf16[128,512]{1,0:T(8,128)(2,1)S(1)} %get-tuple-element.53), channel_id=1, source_target_pairs={{0,1},{1,0},{2,3},{3,2},{4,5},{5,4},{6,7},{7,6},{8,9},{9,8},{10,11... | collective-permute-start | bytes 393224 | tf_op jit(solution)/shard_map/ppermute | solution.py:391
  16.6 1.4 %collective-permute-start.3 = (bf16[4,64,256]{2,1,0:T(8,128)(2,1)S(1)}, bf16[4,64,256]{2,1,0:T(8,128)(2,1)S(1)}, u32[]{:S(2)}, u32[]{:S(2)}) collective-permute-start(bf16[4,64,256]{2,1,0:T(8,128)(2,1)S(1)} %get-tuple-element.58), channel_id=1, source_target_pairs={{0,1},{1,0},{2,3},{3,2},{4,5},{5,4},{6,7},{7,6},{8,9},{9,8},{10,11... | collective-permute-start | bytes 393224 | tf_op jit(solution)/shard_map/ppermute | solution.py:436
  18.4 8.2 %collective-permute-start.5 = (bf16[4,64,256]{2,1,0:T(8,128)(2,1)S(1)}, bf16[4,64,256]{2,1,0:T(8,128)(2,1)S(1)}, u32[]{:S(2)}, u32[]{:S(2)}) collective-permute-start(bf16[4,64,256]{2,1,0:T(8,128)(2,1)S(1)} %get-tuple-element.60), channel_id=1, source_target_pairs={{0,24},{8,16},{16,8},{24,0},{1,25},{9,17},{17,9},{25,1},{2,26},{10... | collective-permute-start | bytes 393224 | tf_op jit(solution)/shard_map/ppermute | solution.py:471
  20.9 6.8 %collective-permute-start.6 = (bf16[4,64,256]{2,1,0:T(8,128)(2,1)S(1)}, bf16[4,64,256]{2,1,0:T(8,128)(2,1)S(1)}, u32[]{:S(2)}, u32[]{:S(2)}) collective-permute-start(bf16[4,64,256]{2,1,0:T(8,128)(2,1)S(1)} %get-tuple-element.61), channel_id=1, source_target_pairs={{0,16},{8,24},{16,0},{24,8},{1,17},{9,25},{17,1},{25,9},{2,18},{10... | collective-permute-start | bytes 393224 | tf_op jit(solution)/shard_map/ppermute | solution.py:471
  21.4 6.4 %collective-permute-start.7 = (bf16[4,64,256]{2,1,0:T(8,128)(2,1)S(1)}, bf16[4,64,256]{2,1,0:T(8,128)(2,1)S(1)}, u32[]{:S(2)}, u32[]{:S(2)}) collective-permute-start(bf16[4,64,256]{2,1,0:T(8,128)(2,1)S(1)} %get-tuple-element.62), channel_id=1, source_target_pairs={{0,8},{8,0},{16,24},{24,16},{1,9},{9,1},{17,25},{25,17},{2,10},{10... | collective-permute-start | bytes 393224 | tf_op jit(solution)/shard_map/ppermute | solution.py:471
  27.9 5.8 %collective-permute-start.10 = (bf16[64,256]{1,0:T(8,128)(2,1)S(1)}, bf16[64,256]{1,0:T(8,128)(2,1)S(1)}, u32[]{:S(2)}, u32[]{:S(2)}) collective-permute-start(bf16[64,256]{1,0:T(8,128)(2,1)S(1)} %get-tuple-element.79), channel_id=1, source_target_pairs={{0,6},{1,7},{2,4},{3,5},{4,2},{5,3},{6,0},{7,1},{8,14},{9,15},{10,... | collective-permute-start | bytes 98312 | tf_op jit(solution)/shard_map/ppermute | solution.py:476
  28.4 5.3 %collective-permute-start.11 = (bf16[64,256]{1,0:T(8,128)(2,1)S(1)}, bf16[64,256]{1,0:T(8,128)(2,1)S(1)}, u32[]{:S(2)}, u32[]{:S(2)}) collective-permute-start(bf16[64,256]{1,0:T(8,128)(2,1)S(1)} %get-tuple-element.80), channel_id=1, source_target_pairs={{0,4},{1,5},{2,6},{3,7},{4,0},{5,1},{6,2},{7,3},{8,12},{9,13},{10,... | collective-permute-start | bytes 98312 | tf_op jit(solution)/shard_map/ppermute | solution.py:476
  28.9 5.4 %collective-permute-start.12 = (bf16[64,256]{1,0:T(8,128)(2,1)S(1)}, bf16[64,256]{1,0:T(8,128)(2,1)S(1)}, u32[]{:S(2)}, u32[]{:S(2)}) collective-permute-start(bf16[64,256]{1,0:T(8,128)(2,1)S(1)} %get-tuple-element.81), channel_id=1, source_target_pairs={{0,2},{1,3},{2,0},{3,1},{4,6},{5,7},{6,4},{7,5},{8,10},{9,11},{10,... | collective-permute-start | bytes 98312 | tf_op jit(solution)/shard_map/ppermute | solution.py:476
  32.4 8.9 %collective-permute-start.8 = (bf16[2,128,512]{2,1,0:T(8,128)(2,1)S(1)}, bf16[2,128,512]{2,1,0:T(8,128)(2,1)S(1)}, u32[]{:S(2)}, u32[]{:S(2)}) collective-permute-start(bf16[2,128,512]{2,1,0:T(8,128)(2,1)S(1)} %get-tuple-element.77), channel_id=1, source_target_pairs={{0,7},{1,2},{2,1},{3,4},{4,3},{5,6},{6,5},{7,0},{8,15},{9,10},{10,... | collective-permute-start | bytes 786440 | tf_op jit(solution)/shard_map/ppermute | solution.py:456
  32.4 8.9 %collective-permute-start.9 = (bf16[2,128,512]{2,1,0:T(8,128)(2,1)S(1)}, bf16[2,128,512]{2,1,0:T(8,128)(2,1)S(1)}, u32[]{:S(2)}, u32[]{:S(2)}) collective-permute-start(bf16[2,128,512]{2,1,0:T(8,128)(2,1)S(1)} %get-tuple-element.78), channel_id=1, source_target_pairs={{0,1},{1,0},{2,3},{3,2},{4,5},{5,4},{6,7},{7,6},{8,9},{9,8},{10,11... | collective-permute-start | bytes 786440 | tf_op jit(solution)/shard_map/ppermute | solution.py:457
  34.3 4.9 %collective-permute-start.13 = (bf16[64,256]{1,0:T(8,128)(2,1)S(1)}, bf16[64,256]{1,0:T(8,128)(2,1)S(1)}, u32[]{:S(2)}, u32[]{:S(2)}) collective-permute-start(bf16[64,256]{1,0:T(8,128)(2,1)S(1)} %multiply_convert_fusion.refs_0_), channel_id=1, source_target_pairs={{0,24},{8,16},{16,8},{24,0},{1,25},{9,17},{17,9},{25,1},{2,26},{10... | collective-permute-start | bytes 98312 | tf_op jit(solution)/shard_map/ppermute | solution.py:479
  36.0 3.9 %collective-permute-start.14 = (bf16[64,256]{1,0:T(8,128)(2,1)S(1)}, bf16[64,256]{1,0:T(8,128)(2,1)S(1)}, u32[]{:S(2)}, u32[]{:S(2)}) collective-permute-start(bf16[64,256]{1,0:T(8,128)(2,1)S(1)} %multiply_convert_fusion.refs_0_), channel_id=1, source_target_pairs={{0,16},{8,24},{16,0},{24,8},{1,17},{9,25},{17,1},{25,9},{2,18},{10... | collective-permute-start | bytes 98312 | tf_op jit(solution)/shard_map/ppermute | solution.py:479
  37.3 3.9 %collective-permute-start.15 = (bf16[64,256]{1,0:T(8,128)(2,1)S(1)}, bf16[64,256]{1,0:T(8,128)(2,1)S(1)}, u32[]{:S(2)}, u32[]{:S(2)}) collective-permute-start(bf16[64,256]{1,0:T(8,128)(2,1)S(1)} %multiply_convert_fusion.refs_0_), channel_id=1, source_target_pairs={{0,8},{8,0},{16,24},{24,16},{1,9},{9,1},{17,25},{25,17},{2,10},{10... | collective-permute-start | bytes 98312 | tf_op jit(solution)/shard_map/ppermute | solution.py:479

commit v10 on v9

--- a/solution.py
+++ b/solution.py
@@ -80,98 +80,122 @@
     return pl.ds(pl.multiple_of(b * BLK, BLK), BLK)
 
 
-def copy_all(pairs, sems):
-    copies = [pltpu.make_async_copy(a, b, sems.at[i]) for i, (a, b) in enumerate(pairs)]
+def pack_kernel(k, v, to_link, chip_k, chip_v, sems):
+    blocks = k.shape[0] // BLK
+    link_rows = rows_of(rim_block(blocks, True)[0])
+    chip_rows = rows_of(rim_block(blocks, False)[0])
+    pairs = (
+        (k.at[link_rows], to_link.at[0]),
+        (v.at[link_rows], to_link.at[1]),
+        (k.at[chip_rows], chip_k),
+        (v.at[chip_rows], chip_v),
+    )
+    copies = [pltpu.make_async_copy(x, y, sems.at[i]) for i, (x, y) in enumerate(pairs)]
     for copy in copies:
         copy.start()
     for copy in copies:
         copy.wait()
 
 
-def pack_link_kernel(k, v, out, sems):
-    rows = rows_of(rim_block(k.shape[0] // BLK, True)[0])
-    copy_all([(k.at[rows], out.at[0]), (v.at[rows], out.at[1])], sems)
-
-
-def pack_chip_kernel(k, v, k_out, v_out, sems):
-    rows = rows_of(rim_block(k.shape[0] // BLK, False)[0])
-    copy_all([(k.at[rows], k_out), (v.at[rows], v_out)], sems)
-
-
-def load_kernel(*refs):
-    count = len(refs) // 2
-    copy_all(list(zip(refs[:count], refs[count:-1])), refs[-1])
-
-
-def own_kernel(mask, q, k, v, g, w_out, own_t, stats, exps, grad_t):
+def own_kernel(
+    mask, q_arg, k_arg, v_arg, g_arg, w_arg,
+    q, k, v, g, w_out, own_t, stats, exps, grad_t, rounded, sems,
+):
+    pairs = ((q_arg, q), (k_arg, k), (v_arg, v), (g_arg, g), (w_arg, w_out))
+    copies = [pltpu.make_async_copy(x, y, sems.at[i]) for i, (x, y) in enumerate(pairs)]
+    for copy in copies:
+        copy.start()
+    copies[0].wait()
+    copies[1].wait()
     blocks = q.shape[0] // BLK
     for b, rows, cols, p in pairs_of(blocks):
         first, last = own_candidates(b, blocks)
         here = own_rows(b, blocks)
         scores = dot(k[here, cols], two_heads(q[rows, cols] * SCALE, 1), ((1,), (1,)))
-        scores = jnp.concatenate(
-            [
-                masked(mask, b, c, scores[(c - first) * BLK : (c - first + 1) * BLK])
-                for c in range(first, last + 1)
-            ],
-            axis=0,
-        )
+        for c in range(first, last + 1):
+            part = slice((c - first) * BLK, (c - first + 1) * BLK)
+            exps[b, p, part] = masked(mask, b, c, scores[part])
+    for b, rows, cols, p in pairs_of(blocks):
+        here = own_rows(b, blocks)
+        keys = slice(0, here.stop - here.start)
+        scores = exps[b, p, keys]
         top = jnp.max(scores, axis=0, keepdims=True)
         e = jnp.exp(scores - top)
-        exps[b, p, : e.shape[0]] = e
+        exps[b, p, keys] = e
+        rounded[b, p, keys] = e.astype(BF16)
         stats[0, b, p : p + 1] = top
         stats[1, b, p : p + 1] = jnp.sum(e, axis=0, keepdims=True)
-        own_t[b, cols] = own_features(dot(v[here, cols], e.astype(BF16), ((0,), (0,))))
+    copies[2].wait()
+    for b, rows, cols, p in pairs_of(blocks):
+        here = own_rows(b, blocks)
+        e = rounded[b, p, : here.stop - here.start]
+        own_t[b, cols] = own_features(dot(v[here, cols], e, ((0,), (0,))))
+    copies[3].wait()
+    copies[4].wait()
     for b in range(blocks):
         rows = slice(b * BLK, (b + 1) * BLK)
         grad_t[b] = dot(w_out[...], g[rows], ((1,), (1,))).astype(BF16)
 
 
-def with_rim(mask, q, rim_k, rim_v, b, c, p, old_top, old_sum):
-    cols = slice(p * PAIR, (p + 1) * PAIR)
-    scores = dot(rim_k[:, cols], two_heads(q[rows_of(b), cols] * SCALE, 1), ((1,), (1,)))
-    scores = jnp.where(mask[b, c] == 1, scores, BIG_NEGATIVE)
-    top = jnp.maximum(old_top, jnp.max(scores, axis=0, keepdims=True))
-    kept = jnp.exp(old_top - top)
-    e = jnp.exp(scores - top)
-    count = old_sum * kept + jnp.sum(e, axis=0, keepdims=True)
-    part = own_features(dot(rim_v[:, cols], e.astype(BF16), ((0,), (0,))))
-    return top, kept, count, e, part
-
-
-def chip_kernel(mask, q, rim_k, rim_v, own_t, stats, chip_t, chip_stats, exps):
+def pair_cols(p):
+    return slice(p * PAIR, (p + 1) * PAIR)
+
+
+def with_rim(mask, q, rim_k, rim_v, b, c, old, exps, rounded):
+    for p in range(PAIRS):
+        q2 = two_heads(q[rows_of(b), pair_cols(p)] * SCALE, 1)
+        scores = dot(rim_k[:, pair_cols(p)], q2, ((1,), (1,)))
+        exps[p] = jnp.where(mask[b, c] == 1, scores, BIG_NEGATIVE)
+    results = []
+    for p in range(PAIRS):
+        old_top, old_sum = old(p)
+        scores = exps[p]
+        top = jnp.maximum(old_top, jnp.max(scores, axis=0, keepdims=True))
+        kept = jnp.exp(old_top - top)
+        e = jnp.exp(scores - top)
+        exps[p] = e
+        rounded[p] = e.astype(BF16)
+        results.append((top, kept, old_sum * kept + jnp.sum(e, axis=0, keepdims=True)))
+    parts = [
+        own_features(dot(rim_v[:, pair_cols(p)], rounded[p], ((0,), (0,)))) for p in range(PAIRS)
+    ]
+    return [(*result, part) for result, part in zip(results, parts)]
+
+
+def chip_kernel(mask, q, rim_k, rim_v, own_t, stats, chip_t, chip_stats, exps, rounded):
     b, c = rim_block(q.shape[0] // BLK, False)
-    for p in range(PAIRS):
-        cols = slice(p * PAIR, (p + 1) * PAIR)
-        top, kept, count, e, part = with_rim(
-            mask, q, rim_k, rim_v, b, c, p, stats[0, b, p : p + 1], stats[1, b, p : p + 1]
-        )
-        chip_t[cols] = own_t[b, cols] * spread(kept) + part
+
+    def old(p):
+        return stats[0, b, p : p + 1], stats[1, b, p : p + 1]
+
+    results = with_rim(mask, q, rim_k, rim_v, b, c, old, exps, rounded)
+    for p, (top, kept, count, part) in enumerate(results):
+        chip_t[pair_cols(p)] = own_t[b, pair_cols(p)] * spread(kept) + part
         chip_stats[0, p : p + 1] = top
         chip_stats[1, p : p + 1] = count
-        exps[p] = e
 
 
 def forward_kernel(
     mask, q, rim, own_t, stats, chip_t, chip_stats,
-    attn_t, mine, other, exps, own_factors, rim_factors,
+    attn_t, mine, other, exps, own_factors, rim_factors, rounded,
 ):
     blocks = q.shape[0] // BLK
     b, c = rim_block(blocks, True)
     at_chip, _ = rim_block(blocks, False)
-    for p in range(PAIRS):
+
+    def old(p):
         at = slice(p, p + 1)
-        cols = slice(p * PAIR, (p + 1) * PAIR)
         if blocks == 1:
-            base, old_top, old_sum = chip_t[cols], chip_stats[0, at], chip_stats[1, at]
-        else:
-            base, old_top, old_sum = own_t[b, cols], stats[0, b, at], stats[1, b, at]
-        top, kept, count, e, part = with_rim(
-            mask, q, rim.at[0], rim.at[1], b, c, p, old_top, old_sum
-        )
+            return chip_stats[0, at], chip_stats[1, at]
+        return stats[0, b, at], stats[1, b, at]
+
+    results = with_rim(mask, q, rim.at[0], rim.at[1], b, c, old, exps, rounded)
+    for p, (top, kept, count, part) in enumerate(results):
+        at = slice(p, p + 1)
+        cols = pair_cols(p)
+        base = chip_t[cols] if blocks == 1 else own_t[b, cols]
         share = 1.0 / count
         attn_t[b, cols] = (base * spread(kept * share) + part * spread(share)).astype(BF16)
-        exps[p] = e
         rim_factors[0, at] = share
         if blocks == 1:
             rim_factors[1, at] = kept * share
@@ -186,20 +210,15 @@
             share = 1.0 / stats[1, inner, at]
             attn_t[inner, cols] = (own_t[inner, cols] * spread(share)).astype(BF16)
             own_factors[inner, at] = share
-    core = at_core()
+    first_core = at_core() == 0
     chips, rows, _ = mine.shape
-    for c in range(2 * chips):
-        for i in range(blocks):
-            value = attn_t[i, c * rows : (c + 1) * rows]
-            tokens = slice(i * BLK, (i + 1) * BLK)
-
-            @pl.when(core == c % 2)
-            def _(c=c, value=value, tokens=tokens):
-                mine[c // 2, :, tokens] = value
-
-            @pl.when(core != c % 2)
-            def _(c=c, value=value, tokens=tokens):
-                other[c // 2, :, tokens] = value
+    for i in range(chips):
+        for block in range(blocks):
+            tokens = slice(block * BLK, (block + 1) * BLK)
+            even = attn_t[block, 2 * i * rows : (2 * i + 1) * rows]
+            odd = attn_t[block, (2 * i + 1) * rows : (2 * i + 2) * rows]
+            mine[i, :, tokens] = jnp.where(first_core, even, odd)
+            other[i, :, tokens] = jnp.where(first_core, odd, even)
 
 
 def flat_dot(attn, g):
@@ -211,18 +230,23 @@
     product[...] = flat_dot(mine, g)
 
 
-def backward(probs, delta, k, v, q2, g2_t):
-    dprob = dot(v, g2_t, ((1,), (0,)))
-    dscore = (probs * (dprob - delta)).astype(BF16)
-    query_t = own_features(dot(k, dscore, ((0,), (0,)))) * SCALE
-    return query_t, dot(dscore, q2, ((1,), (0,))), dot(probs.astype(BF16), g2_t, ((1,), (1,)))
+def score_grads(probs, dprob, delta):
+    return (probs * (dprob - delta)).astype(BF16), probs.astype(BF16)
 
 
 def rim_kernel(
     q, link, chip_k, chip_v, grad_t, attn_t, link_exps, chip_exps, rim_factors, before,
-    to_link, to_chip, deltas, query_t,
+    to_link, to_chip, deltas, query_t, dprobs, dscores, rounded,
 ):
     blocks = q.shape[0] // BLK
+    sides = (
+        (rim_block(blocks, True)[0], link.at[0], link.at[1], link_exps, to_link),
+        (rim_block(blocks, False)[0], chip_k, chip_v, chip_exps, to_chip),
+    )
+    for i, (b, _, rim_v, _, _) in enumerate(sides):
+        for p in range(PAIRS):
+            g2_t = two_heads(grad_t[b, pair_cols(p)], 0)
+            dprobs[i, p] = dot(rim_v[:, pair_cols(p)], g2_t, ((1,), (0,)))
     for b, _, cols, p in pairs_of(blocks):
         product = grad_t[b, cols].astype(F32) * attn_t[b, cols].astype(F32)
         deltas[b, p : p + 1] = jnp.concatenate(
@@ -233,45 +257,55 @@
             axis=1,
         )
     query_t[...] = jnp.zeros_like(query_t)
-    link_side = (link.at[0], link.at[1], link_exps, to_link)
-    for i, (rim_k, rim_v, exps, back) in enumerate(
-        (link_side, (chip_k, chip_v, chip_exps, to_chip))
-    ):
-        b, _ = rim_block(blocks, i == 0)
+    for i, (b, _, _, exps, _) in enumerate(sides):
         for p in range(PAIRS):
-            cols = slice(p * PAIR, (p + 1) * PAIR)
-            part_t, k_part, v_part = backward(
-                exps[p] * rim_factors[i, p : p + 1],
-                deltas[b, p : p + 1],
-                rim_k[:, cols],
-                rim_v[:, cols],
-                two_heads(q[rows_of(b), cols] * SCALE, 1),
-                two_heads(grad_t[b, cols], 0),
+            at = slice(p, p + 1)
+            dscores[i, p], rounded[i, p] = score_grads(
+                exps[p] * rim_factors[i, at], dprobs[i, p], deltas[b, at]
             )
-            query_t[b, cols] += part_t
-            back[0, :, cols] = k_part.astype(BF16)
-            back[1, :, cols] = v_part.astype(BF16)
+    for i, (b, rim_k, _, _, back) in enumerate(sides):
+        for p in range(PAIRS):
+            cols = pair_cols(p)
+            q2 = two_heads(q[rows_of(b), cols] * SCALE, 1)
+            g2_t = two_heads(grad_t[b, cols], 0)
+            back[0, :, cols] = dot(dscores[i, p], q2, ((1,), (0,))).astype(BF16)
+            back[1, :, cols] = dot(rounded[i, p], g2_t, ((1,), (1,))).astype(BF16)
+            query_t[b, cols] += own_features(dot(rim_k[:, cols], dscores[i, p], ((0,), (0,))))
 
 
 def own_backward_kernel(
-    q, k, v, grad_t, exps, factors, deltas, rim_t, before, q_grad, k_own, v_own, after
+    q, k, v, grad_t, exps, factors, deltas, rim_t, before,
+    q_grad, k_own, v_own, after, dprobs, dscores, rounded,
 ):
     blocks = q.shape[0] // BLK
-    k_own[...] = jnp.zeros_like(k_own)
-    v_own[...] = jnp.zeros_like(v_own)
+    for b, _, cols, p in pairs_of(blocks):
+        here = own_rows(b, blocks)
+        g2_t = two_heads(grad_t[b, cols], 0)
+        dprobs[b, p, : here.stop - here.start] = dot(v[here, cols], g2_t, ((1,), (0,)))
+    for b, _, _, p in pairs_of(blocks):
+        here = own_rows(b, blocks)
+        keys = slice(0, here.stop - here.start)
+        dscores[b, p, keys], rounded[b, p, keys] = score_grads(
+            exps[b, p, keys] * factors[b, p : p + 1], dprobs[b, p, keys], deltas[b, p : p + 1]
+        )
+    k_sums, v_sums = {}, {}
     for b, rows, cols, p in pairs_of(blocks):
         here = own_rows(b, blocks)
-        part_t, k_part, v_part = backward(
-            exps[b, p, : here.stop - here.start] * factors[b, p : p + 1],
-            deltas[b, p : p + 1],
-            k[here, cols],
-            v[here, cols],
-            two_heads(q[rows, cols] * SCALE, 1),
-            two_heads(grad_t[b, cols], 0),
-        )
-        q_grad[rows, cols] = (part_t + rim_t[b, cols]).T.astype(BF16)
-        k_own[here, cols] += k_part
-        v_own[here, cols] += v_part
+        keys = slice(0, here.stop - here.start)
+        q2 = two_heads(q[rows, cols] * SCALE, 1)
+        g2_t = two_heads(grad_t[b, cols], 0)
+        dscore = dscores[b, p, keys]
+        k_part = dot(dscore, q2, ((1,), (0,)))
+        v_part = dot(rounded[b, p, keys], g2_t, ((1,), (1,)))
+        for at in range(here.start, here.stop, BLK):
+            part = slice(at - here.start, at - here.start + BLK)
+            for sums, value in ((k_sums, k_part), (v_sums, v_part)):
+                sums.setdefault((at, p), []).append(value[part])
+        query_t = own_features(dot(k[here, cols], dscore, ((0,), (0,)))) + rim_t[b, cols]
+        q_grad[rows, cols] = (query_t * SCALE).T.astype(BF16)
+    for out, sums in ((k_own, k_sums), (v_own, v_sums)):
+        for (at, p), values in sums.items():
+            out[at : at + BLK, pair_cols(p)] = functools.reduce(jnp.add, values)
     after[...] = jnp.zeros_like(after)
 
 
@@ -337,7 +371,7 @@
     return jax.ShapeDtypeStruct(shape, dtype)
 
 
-def call(kernel, outs, flops, *args, mask=None):
+def call(kernel, outs, flops, *args, mask=None, scratch=()):
     in_vmem = pl.BlockSpec(memory_space=pltpu.VMEM)
     in_smem = pl.BlockSpec(memory_space=pltpu.SMEM)
     masks = () if mask is None else (mask,)
@@ -346,21 +380,24 @@
         out_shape=outs,
         in_specs=[in_smem] * len(masks) + [in_vmem] * len(args),
         out_specs=[in_vmem] * len(outs),
+        scratch_shapes=list(scratch),
         compiler_params=pltpu.CompilerParams(vmem_limit_bytes=24 * 1024 * 1024),
         cost_estimate=pl.CostEstimate(flops=flops, bytes_accessed=flops // 250, transcendentals=0),
     )(*masks, *args)
 
 
-def from_hbm(kernel, outs, *args):
+def call_on_hbm(kernel, outs, *args, mask=None, scratch=()):
+    masks = () if mask is None else (mask,)
     return pl.pallas_call(
         kernel,
         out_shape=outs,
-        in_specs=[pl.BlockSpec(memory_space=pltpu.HBM)] * len(args),
+        in_specs=[pl.BlockSpec(memory_space=pltpu.SMEM)] * len(masks)
+        + [pl.BlockSpec(memory_space=pltpu.HBM)] * len(args),
         out_specs=[pl.BlockSpec(memory_space=pltpu.VMEM)] * len(outs),
-        scratch_shapes=[pltpu.SemaphoreType.DMA((len(args),))],
-        compiler_params=pltpu.CompilerParams(vmem_limit_bytes=1024 * 1024),
-        cost_estimate=pl.CostEstimate(flops=0, bytes_accessed=4096, transcendentals=0),
-    )(*(pltpu.with_memory_space_constraint(x, pltpu.HBM) for x in args))
+        scratch_shapes=list(scratch),
+        compiler_params=pltpu.CompilerParams(vmem_limit_bytes=8 * 1024 * 1024),
+        cost_estimate=pl.CostEstimate(flops=10**6, bytes_accessed=4096, transcendentals=0),
+    )(*masks, *(pltpu.with_memory_space_constraint(x, pltpu.HBM) for x in args))
 
 
 def swap(count, bits):
@@ -385,38 +422,47 @@
     at_ctx = lax.axis_index("ctx")
     rows, cols = feats // ctx, width // dp
 
-    (to_link,) = from_hbm(pack_link_kernel, [vmem(2, RIM, feats)], k, v)
+    rim = vmem(RIM, feats)
+    to_link, *to_chip = call_on_hbm(
+        pack_kernel,
+        [vmem(2, RIM, feats), rim, rim],
+        k, v,
+        scratch=[pltpu.SemaphoreType.DMA((4,))],
+    )
     link = lax.ppermute(to_link, "ctx", over_links(ctx))
-    to_chip = from_hbm(pack_chip_kernel, [vmem(RIM, feats)] * 2, k, v)
     chip_k, chip_v = (lax.ppermute(x, "ctx", swap(ctx, 1)) for x in to_chip)
     sibling_g = lax.ppermute(g, "ctx", swap(ctx, 1))
     sibling_g = pltpu.with_memory_space_constraint(sibling_g, pltpu.VMEM)
+
+    mask = lax.dynamic_slice_in_dim(block_mask[0], at_ctx * blocks, blocks, 0)
     args = (q, k, v, g, w_out)
-    q, k, v, g, w_out = from_hbm(load_kernel, [vmem(*x.shape) for x in args], *args)
-
-    mask = lax.dynamic_slice_in_dim(block_mask[0], at_ctx * blocks, blocks, 0)
-    own_t, stats, own_exps, grad_t = call(
+    own_keys = min(CAND, blocks) * BLK
+    own_scores = (blocks, PAIRS, own_keys, 2 * BLK)
+    rim_scores = (PAIRS, RIM, 2 * BLK)
+    q, k, v, g, w_out, own_t, stats, own_exps, grad_t = call_on_hbm(
         own_kernel,
-        [
+        [vmem(*x.shape) for x in args]
+        + [
             vmem(blocks, feats, BLK, dtype=F32),
             vmem(2, blocks, PAIRS, 2 * BLK, dtype=F32),
-            vmem(blocks, PAIRS, min(CAND, blocks) * BLK, 2 * BLK, dtype=F32),
+            vmem(*own_scores, dtype=F32),
             vmem(blocks, feats, BLK),
         ],
-        10**6,
-        q, k, v, g, w_out,
+        *args,
         mask=mask,
+        scratch=[vmem(*own_scores), pltpu.SemaphoreType.DMA((len(args),))],
     )
     chip_t, chip_stats, chip_exps = call(
         chip_kernel,
         [
             vmem(feats, BLK, dtype=F32),
             vmem(2, PAIRS, 2 * BLK, dtype=F32),
-            vmem(PAIRS, RIM, 2 * BLK, dtype=F32),
+            vmem(*rim_scores, dtype=F32),
         ],
         10**6,
         q, chip_k, chip_v, own_t, stats,
         mask=mask,
+        scratch=[vmem(*rim_scores)],
     )
     attn_t, mine, other, link_exps, own_factors, rim_factors = call(
         forward_kernel,
@@ -424,13 +470,14 @@
             vmem(blocks, feats, BLK),
             vmem(chips, rows, tokens),
             vmem(chips, rows, tokens),
-            vmem(PAIRS, RIM, 2 * BLK, dtype=F32),
+            vmem(*rim_scores, dtype=F32),
             vmem(blocks, PAIRS, 2 * BLK, dtype=F32),
             vmem(2, PAIRS, 2 * BLK, dtype=F32),
         ],
         10**6,
         q, link, own_t, stats, chip_t, chip_stats,
         mask=mask,
+        scratch=[vmem(*rim_scores)],
     )
 
     other = lax.ppermute(other, "ctx", swap(ctx, 1))
@@ -452,6 +499,7 @@
         ],
         10**6,
         q, link, chip_k, chip_v, grad_t, attn_t, link_exps, chip_exps, rim_factors, after,
+        scratch=[vmem(2, *rim_scores, dtype=F32), vmem(2, *rim_scores), vmem(2, *rim_scores)],
     )
     grad_link = lax.ppermute(to_link, "ctx", over_links(ctx))
     grad_chip = lax.ppermute(to_chip, "ctx", swap(ctx, 1))
@@ -466,6 +514,7 @@
         ],
         10**6,
         q, k, v, grad_t, own_exps, own_factors, deltas, rim_t, after,
+        scratch=[vmem(*own_scores, dtype=F32), vmem(*own_scores), vmem(*own_scores)],
     )
 
     halves = [halves[0]] + [lax.ppermute(halves[s], "dp", swap(dp, s)) for s in range(dp - 1, 0, -1)]

time: 42.4 us -> 41.2 us (0.972)
  Pallas kernels: 17.5 us -> 13 us
  waiting for transfers between devices: 6.03 us -> 8.54 us
  starting transfers between devices: 17.7 us -> 18.5 us
    pallas_call x10 -> x9, Pallas kernels: 13.9 us -> 8.32 us  [call(): pl.pallas_call(kernel, out_shape=outs, in_specs=[in_smem] * len(masks) +...]
    ppermute x3, waiting for transfers between devices: 1.2 us -> 2.76 us  [body(): lax.ppermute(halves[s], 'dp', swap(dp, s))]
    pallas_call x3 -> x2, Pallas kernels: 3.64 us -> 4.71 us  [call_on_hbm(): pl.pallas_call(kernel, out_shape=outs, in_specs=[pl.BlockSpec(memory_spac...]
    ppermute x1, starting transfers between devices: 0.01 us -> 1.06 us  [body(): grad_link = lax.ppermute(to_link, 'ctx', over_links(ctx))]
    ppermute x1, waiting for transfers between devices: 0.01 us -> 0.79 us  [body(): link = lax.ppermute(to_link, 'ctx', over_links(ctx))]
  transfers between devices with their start and end apart: 16 -> 16, of which waited for: 7 -> 11; matrix products, arithmetic and copies ran while one was open for 0% -> 0% of each run, Pallas kernels for 38% -> 28%
where the time goes in v10:
time: 41.2 us; the launch traced here: 41 us
  starting transfers between devices  18.5 us (45%)
  Pallas kernels  13 us (32%)
  waiting for transfers between devices  8.54 us (21%)
  between operations  0.73 us (2%)
    pallas_call x9, Pallas kernels, call(): pl.pallas_call(kernel, out_shape=outs, in_specs=[in_smem] * len(masks) +...  8.32 us
    ppermute x1, starting transfers between devices, body(): link = lax.ppermute(to_link, 'ctx', over_links(ctx))  4.78 us
    pallas_call x2, Pallas kernels, call_on_hbm(): pl.pallas_call(kernel, out_shape=outs, in_specs=[pl.BlockSpec(memory_spac...  4.71 us
    ppermute x3, starting transfers between devices, body(): lax.ppermute(quarters[s], 'ctx', swap(ctx, 2 * s))  4.45 us
    ppermute x3, starting transfers between devices, body(): lax.ppermute(halves[s], 'dp', swap(dp, s))  3.55 us
    ppermute x3, starting transfers between devices, body(): lax.ppermute(piece, 'dp', swap(dp, s))  3.55 us
    ppermute x3, waiting for transfers between devices, body(): lax.ppermute(halves[s], 'dp', swap(dp, s))  2.76 us
    ppermute x3, waiting for transfers between devices, body(): lax.ppermute(piece, 'dp', swap(dp, s))  2.12 us
  transfers between devices with their start and end apart: 16, of which 11 were waited for; matrix products, arithmetic and copies ran while one was open for 0% of the time, Pallas kernels for 28%

profile of v10, /device:TPU:0, one launch (start us, length us, event | category | flops | bytes accessed | tf_op | source)
XLA Modules:
  0.0 41.0 jit_solution(17031412330808153143)
XLA Ops:
  0.6 0.0 copy-start
  0.6 0.5 %collective-permute-start.4 = (bf16[256,1024]{1,0:T(8,128)(2,1)}, bf16[256,1024]{1,0:T(8,128)(2,1)S(1)}, u32[]{:S(2)}, u32[]{:S(2)}) collective-permute-start(bf16[256,1024]{1,0:T(8,128)(2,1)} %bitcast.17), channel_id=1, source_target_pairs={{0,1},{1,0},{2,3},{3,2},{4,5},{5,4},{6,7},{7,6},{8,9},{9,8},{10,11... | collective-permute-start | bytes 1572872 | tf_op jit(solution)/shard_map/ppermute | solution.py:434
  1.2 1.1 %shard_map.102 = (bf16[2,128,512]{2,1,0:T(8,128)(2,1)S(1)}, bf16[128,512]{1,0:T(8,128)(2,1)S(1)}, bf16[128,512]{1,0:T(8,128)(2,1)S(1)}) custom-call(bf16[256,512]{1,0:T(8,128)(2,1)} %bitcast.12, bf16[256,512]{1,0:T(8,128)(2,1)} %bitcast.14), custom_call_target="tpu_custom_call" | custom-call | flops 1000000 | bytes 4096 | tf_op jit(solution)/shard_map/pallas_call | solution.py:391
  2.3 4.8 %collective-permute-start = (bf16[2,128,512]{2,1,0:T(8,128)(2,1)S(1)}, bf16[2,128,512]{2,1,0:T(8,128)(2,1)S(1)}, u32[]{:S(2)}, u32[]{:S(2)}) collective-permute-start(bf16[2,128,512]{2,1,0:T(8,128)(2,1)S(1)} %get-tuple-element.47), channel_id=1, source_target_pairs={{0,7},{1,2},{2,1},{3,4},{4,3},{5,6},{6,5},{7,0},{8,15},{9,10},{10,... | collective-permute-start | bytes 786440 | tf_op jit(solution)/shard_map/ppermute | solution.py:432
  7.1 0.0 collective-permute-start.1
  7.1 0.5 %collective-permute-start.2 = (bf16[128,512]{1,0:T(8,128)(2,1)S(1)}, bf16[128,512]{1,0:T(8,128)(2,1)S(1)}, u32[]{:S(2)}, u32[]{:S(2)}) collective-permute-start(bf16[128,512]{1,0:T(8,128)(2,1)S(1)} %get-tuple-element.51), channel_id=1, source_target_pairs={{0,1},{1,0},{2,3},{3,2},{4,5},{5,4},{6,7},{7,6},{8,9},{9,8},{10,11... | collective-permute-start | bytes 393224 | tf_op jit(solution)/shard_map/ppermute | solution.py:433
  7.6 0.0 copy-done
  7.6 0.1 constant_dynamic-slice_fusion
  7.7 0.1 copy.11
  7.8 3.6 %shard_map.101 = (bf16[256,512]{1,0:T(8,128)(2,1)S(1)}, bf16[256,512]{1,0:T(8,128)(2,1)S(1)}, bf16[256,512]{1,0:T(8,128)(2,1)S(1)}, bf16[256,1024]{1,0:T(8,128)(...) custom-call(s32[2,3]{1,0:T(2,128)S(1)} %bitcast.9, ...), custom_call_target="tpu_custom_call" | custom-call | flops 1000000 | bytes 4096 | tf_op jit(solution)/shard_map/pallas_call | solution.py:391
  11.4 0.0 collective-permute-done.1.rim_k.chip_k
  11.4 0.0 collective-permute-done.2.rim_v.chip_v
  11.4 1.1 %shard_map.103 = (f32[512,128]{1,0:T(8,128)S(1)}, f32[2,4,256]{2,1,0:T(4,128)S(1)}, f32[4,128,256]{2,1,0:T(8,128)S(1)}) custom-call(s32[2,3]{1,0:T(2,128)S(1)} %bitcast.10, bf16[256,512]{1,0:T(8,128)(2,1)S(1)} %get-tuple-element.46.q, bf16[128,512]{1,0:T(8,128)(2,1)S(1)} %collective-permute-done.1.rim_k.chip_k, ...), custom_call_target="tpu_custom_call" | custom-call | flops 1000000 | bytes 4000 | tf_op jit(solution)/shard_map/pallas_call | solution.py:378
  12.4 0.8 %collective-permute-done.rim.link = bf16[2,128,512]{2,1,0:T(8,128)(2,1)S(1)} collective-permute-done((bf16[2,128,512]{2,1,0:T(8,128)(2,1)S(1)}, bf16[2,128,512]{2,1,0:T(8,128)(2,1)S(1)}, u32[]{:S(2)}, u32[]{:S(2)}) %collective-permute-start) | collective-permute-done | bytes 262176 | tf_op jit(solution)/shard_map/ppermute | solution.py:432
  13.2 1.1 %shard_map.104 = (bf16[2,512,128]{2,1,0:T(8,128)(2,1)S(1)}, bf16[4,64,256]{2,1,0:T(8,128)(2,1)S(1)}, bf16[4,64,256]{2,1,0:T(8,128)(2,1)S(1)}, f32[4,128,256]{2,1...) custom-call(s32[2,3]{1,0:T(2,128)S(1)} %bitcast.11, bf16[256,512]{1,0:T(8,128)(2,1)S(1)} %get-tuple-element.46.q, ...), custom_call_target="tpu_custom_call" | custom-call | flops 1000000 | bytes 4000 | tf_op jit(solution)/shard_map/pallas_call | solution.py:378
  14.4 0.1 collective-permute-start.3
  14.4 0.3 shard_map.105.product
  14.7 1.0 %collective-permute-done.3.other = bf16[4,64,256]{2,1,0:T(8,128)(2,1)S(1)} collective-permute-done((bf16[4,64,256]{2,1,0:T(8,128)(2,1)S(1)}, bf16[4,64,256]{2,1,0:T(8,128)(2,1)S(1)}, u32[]{:S(2)}, u32[]{:S(2)}) %collective-permute-start.3) | collective-permute-done | bytes 131104 | tf_op jit(solution)/shard_map/ppermute | solution.py:483
  15.8 0.0 collective-permute-done.4.g
  15.8 0.4 %shard_map.106 = (bf16[4,64,256]{2,1,0:T(8,128)(2,1)S(1)}, bf16[4,64,256]{2,1,0:T(8,128)(2,1)S(1)}, bf16[4,64,256]{2,1,0:T(8,128)(2,1)S(1)}, bf16[4,64,256]{2,1,0:T(8,128)(2,1)S(1)}, f32[8,128]{1,0:T(8,128)S(1)}) custom-call(f32[256,1024]{1,0:T(8,128)S(1)} %shard_map.105.product, bf16[4,64,256]{2,1,0:T(8,128)(2,1)S(1)} %collective-permute-done.3.other, ...), custom_call_target="tpu_custom_call" | custom-call | flops 1000000 | bytes 4000 | tf_op jit(solution)/shard_map/pallas_call | solution.py:378
  16.2 2.5 %collective-permute-start.5 = (bf16[4,64,256]{2,1,0:T(8,128)(2,1)S(1)}, bf16[4,64,256]{2,1,0:T(8,128)(2,1)S(1)}, u32[]{:S(2)}, u32[]{:S(2)}) collective-permute-start(bf16[4,64,256]{2,1,0:T(8,128)(2,1)S(1)} %get-tuple-element.60), channel_id=1, source_target_pairs={{0,24},{8,16},{16,8},{24,0},{1,25},{9,17},{17,9},{25,1},{2,26},{10... | collective-permute-start | bytes 393224 | tf_op jit(solution)/shard_map/ppermute | solution.py:520
  18.7 0.5 %collective-permute-start.6 = (bf16[4,64,256]{2,1,0:T(8,128)(2,1)S(1)}, bf16[4,64,256]{2,1,0:T(8,128)(2,1)S(1)}, u32[]{:S(2)}, u32[]{:S(2)}) collective-permute-start(bf16[4,64,256]{2,1,0:T(8,128)(2,1)S(1)} %get-tuple-element.61), channel_id=1, source_target_pairs={{0,16},{8,24},{16,0},{24,8},{1,17},{9,25},{17,1},{25,9},{2,18},{10... | collective-permute-start | bytes 393224 | tf_op jit(solution)/shard_map/ppermute | solution.py:520
  19.2 0.5 %collective-permute-start.7 = (bf16[4,64,256]{2,1,0:T(8,128)(2,1)S(1)}, bf16[4,64,256]{2,1,0:T(8,128)(2,1)S(1)}, u32[]{:S(2)}, u32[]{:S(2)}) collective-permute-start(bf16[4,64,256]{2,1,0:T(8,128)(2,1)S(1)} %get-tuple-element.62), channel_id=1, source_target_pairs={{0,8},{8,0},{16,24},{24,16},{1,9},{9,1},{17,25},{25,17},{2,10},{10... | collective-permute-start | bytes 393224 | tf_op jit(solution)/shard_map/ppermute | solution.py:520
  19.8 0.9 %shard_map.107 = (bf16[2,128,512]{2,1,0:T(8,128)(2,1)S(1)}, bf16[2,128,512]{2,1,0:T(8,128)(2,1)S(1)}, f32[2,4,256]{2,1,0:T(4,128)S(1)}, f32[2,512,128]{2,1,0:T(8,128)S(1)}) custom-call(bf16[256,512]{1,0:T(8,128)(2,1)S(1)} %get-tuple-element.46.q, bf16[2,128,512]{2,1,0:T(8,128)(2,1)S(1)} %collective-permute-done.rim.link, ...), custom_call_target="tpu_custom_call" | custom-call | flops 1000000 | bytes 4000 | tf_op jit(solution)/shard_map/pallas_call | solution.py:378
  20.7 2.2 %shard_map.108 = (bf16[256,512]{1,0:T(8,128)(2,1)}, f32[256,512]{1,0:T(8,128)S(1)}, f32[256,512]{1,0:T(8,128)S(1)}, f32[8,128]{1,0:T(8,128)S(1)}) custom-call(bf16[256,512]{1,0:T(8,128)(2,1)S(1)} %get-tuple-element.46.q, bf16[256,512]{1,0:T(8,128)(2,1)S(1)} %get-tuple-element.63.k, bf16[256,512]{1,0:T(8,128)(2,1)S(1)} %get-tuple-element.64.v, ...), custom_call_target="tpu_custom_call" | custom-call | flops 1000000 | bytes 4000 | tf_op jit(solution)/shard_map/pallas_call | solution.py:378
  22.9 0.2 collective-permute-done.5.refs_1_
  23.0 2.5 %collective-permute-done.6.refs_2_ = bf16[4,64,256]{2,1,0:T(8,128)(2,1)S(1)} collective-permute-done((bf16[4,64,256]{2,1,0:T(8,128)(2,1)S(1)}, bf16[4,64,256]{2,1,0:T(8,128)(2,1)S(1)}, u32[]{:S(2)}, u32[]{:S(2)}) %collective-permute-start.6) | collective-permute-done | bytes 131104 | tf_op jit(solution)/shard_map/ppermute | solution.py:520
  25.5 0.1 collective-permute-done.7.refs_3_
  25.6 0.1 shard_map.109
  25.7 2.4 %collective-permute-start.10 = (bf16[64,256]{1,0:T(8,128)(2,1)S(1)}, bf16[64,256]{1,0:T(8,128)(2,1)S(1)}, u32[]{:S(2)}, u32[]{:S(2)}) collective-permute-start(bf16[64,256]{1,0:T(8,128)(2,1)S(1)} %get-tuple-element.81), channel_id=1, source_target_pairs={{0,6},{1,7},{2,4},{3,5},{4,2},{5,3},{6,0},{7,1},{8,14},{9,15},{10,... | collective-permute-start | bytes 98312 | tf_op jit(solution)/shard_map/ppermute | solution.py:525
  28.1 0.0 collective-permute-start.11
  28.1 2.0 %collective-permute-start.12 = (bf16[64,256]{1,0:T(8,128)(2,1)S(1)}, bf16[64,256]{1,0:T(8,128)(2,1)S(1)}, u32[]{:S(2)}, u32[]{:S(2)}) collective-permute-start(bf16[64,256]{1,0:T(8,128)(2,1)S(1)} %get-tuple-element.83), channel_id=1, source_target_pairs={{0,2},{1,3},{2,0},{3,1},{4,6},{5,7},{6,4},{7,5},{8,10},{9,11},{10,... | collective-permute-start | bytes 98312 | tf_op jit(solution)/shard_map/ppermute | solution.py:525
  30.1 1.1 %collective-permute-start.8 = (bf16[2,128,512]{2,1,0:T(8,128)(2,1)S(1)}, bf16[2,128,512]{2,1,0:T(8,128)(2,1)S(1)}, u32[]{:S(2)}, u32[]{:S(2)}) collective-permute-start(bf16[2,128,512]{2,1,0:T(8,128)(2,1)S(1)} %get-tuple-element.79), channel_id=1, source_target_pairs={{0,7},{1,2},{2,1},{3,4},{4,3},{5,6},{6,5},{7,0},{8,15},{9,10},{10,... | collective-permute-start | bytes 786440 | tf_op jit(solution)/shard_map/ppermute | solution.py:504
  31.2 0.0 collective-permute-start.9
  31.2 0.3 collective-permute-done.10
  31.5 1.5 %collective-permute-done.11 = bf16[64,256]{1,0:T(8,128)(2,1)S(1)} collective-permute-done((bf16[64,256]{1,0:T(8,128)(2,1)S(1)}, bf16[64,256]{1,0:T(8,128)(2,1)S(1)}, u32[]{:S(2)}, u32[]{:S(2)}) %collective-permute-start.11) | collective-permute-done | bytes 32800 | tf_op jit(solution)/shard_map/ppermute | solution.py:525
  33.0 0.0 collective-permute-done.12
  33.0 1.8 %collective-permute-start.13 = (bf16[64,256]{1,0:T(8,128)(2,1)S(1)}, bf16[64,256]{1,0:T(8,128)(2,1)S(1)}, u32[]{:S(2)}, u32[]{:S(2)}) collective-permute-start(bf16[64,256]{1,0:T(8,128)(2,1)S(1)} %multiply_convert_fusion.refs_0_), channel_id=1, source_target_pairs={{0,24},{8,16},{16,8},{24,0},{1,25},{9,17},{17,9},{25,1},{2,26},{10... | collective-permute-start | bytes 98312 | tf_op jit(solution)/shard_map/ppermute | solution.py:528
  34.8 1.2 %collective-permute-start.14 = (bf16[64,256]{1,0:T(8,128)(2,1)S(1)}, bf16[64,256]{1,0:T(8,128)(2,1)S(1)}, u32[]{:S(2)}, u32[]{:S(2)}) collective-permute-start(bf16[64,256]{1,0:T(8,128)(2,1)S(1)} %multiply_convert_fusion.refs_0_), channel_id=1, source_target_pairs={{0,16},{8,24},{16,0},{24,8},{1,17},{9,25},{17,1},{25,9},{2,18},{10... | collective-permute-start | bytes 98312 | tf_op jit(solution)/shard_map/ppermute | solution.py:528
  36.0 0.5 %collective-permute-start.15 = (bf16[64,256]{1,0:T(8,128)(2,1)S(1)}, bf16[64,256]{1,0:T(8,128)(2,1)S(1)}, u32[]{:S(2)}, u32[]{:S(2)}) collective-permute-start(bf16[64,256]{1,0:T(8,128)(2,1)S(1)} %multiply_convert_fusion.refs_0_), channel_id=1, source_target_pairs={{0,8},{8,0},{16,24},{24,16},{1,9},{9,1},{17,25},{25,17},{2,10},{10... | collective-permute-start | bytes 98312 | tf_op jit(solution)/shard_map/ppermute | solution.py:528
  36.6 1.3 %shard_map.110 = bf16[256,1024]{1,0:T(8,128)(2,1)} custom-call(bf16[2,512,128]{2,1,0:T(8,128)(2,1)S(1)} %get-tuple-element.54.attn_t, bf16[512,1024]{1,0:T(8,128)(2,1)S(1)} %get-tuple-element.55.w_out, bf16[64,256]{1,0:T(8,128)(2,1)S(1)} %get-tuple-element.75.before), custom_call_target="tpu_custom_call" | custom-call | flops 1000000 | bytes 4000 | tf_op jit(solution)/shard_map/pallas_call | solution.py:378
  37.8 0.1 collective-permute-done.13.refs_1_
  37.9 0.8 %collective-permute-done.14.refs_2_ = bf16[64,256]{1,0:T(8,128)(2,1)S(1)} collective-permute-done((bf16[64,256]{1,0:T(8,128)(2,1)S(1)}, bf16[64,256]{1,0:T(8,128)(2,1)S(1)}, u32[]{:S(2)}, u32[]{:S(2)}) %collective-permute-start.14) | collective-permute-done | bytes 32800 | tf_op jit(solution)/shard_map/ppermute | solution.py:528
  38.7 1.2 %collective-permute-done.15.refs_3_ = bf16[64,256]{1,0:T(8,128)(2,1)S(1)} collective-permute-done((bf16[64,256]{1,0:T(8,128)(2,1)S(1)}, bf16[64,256]{1,0:T(8,128)(2,1)S(1)}, u32[]{:S(2)}, u32[]{:S(2)}) %collective-permute-start.15) | collective-permute-done | bytes 32800 | tf_op jit(solution)/shard_map/ppermute | solution.py:528
  39.9 0.1 collective-permute-done.8.from_link
  40.0 0.0 collective-permute-done.9.from_chip
  40.0 1.0 %shard_map.111 = (bf16[256,512]{1,0:T(8,128)(2,1)}, bf16[256,512]{1,0:T(8,128)(2,1)}, f32[64,1024]{1,0:T(8,128)}) custom-call(f32[256,512]{1,0:T(8,128)S(1)} %get-tuple-element.77.k_own, f32[256,512]{1,0:T(8,128)S(1)} %get-tuple-element.78.v_own, bf16[2,128,512]{2,1,0:T(8,128)(2,1)S(1)} %collective-permute-done.8.from_link, ...), custom_call_target="tpu_custom_call" | custom-call | flops 1000000 | bytes 4000 | tf_op jit(solution)/shard_map/pallas_call | solution.py:378
  (1 shorter events, 0.0 us)
Async XLA Ops:
  0.6 7.0 %copy-start = (s32[1,16,3]{1,0,2:T(1,128)S(1)}, s32[1,16,3]{1,0,2:T(1,128)}, u32[]{:S(2)}) copy-start(s32[1,16,3]{1,0,2:T(1,128)} %param.11) | copy-start | bytes 580
  0.6 15.1 %collective-permute-start.4 = (bf16[256,1024]{1,0:T(8,128)(2,1)}, bf16[256,1024]{1,0:T(8,128)(2,1)S(1)}, u32[]{:S(2)}, u32[]{:S(2)}) collective-permute-start(bf16[256,1024]{1,0:T(8,128)(2,1)} %bitcast.17), channel_id=1, source_target_pairs={{0,1},{1,0},{2,3},{3,2},{4,5},{5,4},{6,7},{7,6},{8,9},{9,8},{10,11... | collective-permute-start | bytes 1572872 | tf_op jit(solution)/shard_map/ppermute | solution.py:434
  2.3 10.9 %collective-permute-start = (bf16[2,128,512]{2,1,0:T(8,128)(2,1)S(1)}, bf16[2,128,512]{2,1,0:T(8,128)(2,1)S(1)}, u32[]{:S(2)}, u32[]{:S(2)}) collective-permute-start(bf16[2,128,512]{2,1,0:T(8,128)(2,1)S(1)} %get-tuple-element.47), channel_id=1, source_target_pairs={{0,7},{1,2},{2,1},{3,4},{4,3},{5,6},{6,5},{7,0},{8,15},{9,10},{10,... | collective-permute-start | bytes 786440 | tf_op jit(solution)/shard_map/ppermute | solution.py:432
  7.1 4.3 %collective-permute-start.1 = (bf16[128,512]{1,0:T(8,128)(2,1)S(1)}, bf16[128,512]{1,0:T(8,128)(2,1)S(1)}, u32[]{:S(2)}, u32[]{:S(2)}) collective-permute-start(bf16[128,512]{1,0:T(8,128)(2,1)S(1)} %get-tuple-element.50), channel_id=1, source_target_pairs={{0,1},{1,0},{2,3},{3,2},{4,5},{5,4},{6,7},{7,6},{8,9},{9,8},{10,11... | collective-permute-start | bytes 393224 | tf_op jit(solution)/shard_map/ppermute | solution.py:433
  7.1 4.3 %collective-permute-start.2 = (bf16[128,512]{1,0:T(8,128)(2,1)S(1)}, bf16[128,512]{1,0:T(8,128)(2,1)S(1)}, u32[]{:S(2)}, u32[]{:S(2)}) collective-permute-start(bf16[128,512]{1,0:T(8,128)(2,1)S(1)} %get-tuple-element.51), channel_id=1, source_target_pairs={{0,1},{1,0},{2,3},{3,2},{4,5},{5,4},{6,7},{7,6},{8,9},{9,8},{10,11... | collective-permute-start | bytes 393224 | tf_op jit(solution)/shard_map/ppermute | solution.py:433
  14.4 1.4 %collective-permute-start.3 = (bf16[4,64,256]{2,1,0:T(8,128)(2,1)S(1)}, bf16[4,64,256]{2,1,0:T(8,128)(2,1)S(1)}, u32[]{:S(2)}, u32[]{:S(2)}) collective-permute-start(bf16[4,64,256]{2,1,0:T(8,128)(2,1)S(1)} %get-tuple-element.58), channel_id=1, source_target_pairs={{0,1},{1,0},{2,3},{3,2},{4,5},{5,4},{6,7},{7,6},{8,9},{9,8},{10,11... | collective-permute-start | bytes 393224 | tf_op jit(solution)/shard_map/ppermute | solution.py:483
  16.2 6.8 %collective-permute-start.5 = (bf16[4,64,256]{2,1,0:T(8,128)(2,1)S(1)}, bf16[4,64,256]{2,1,0:T(8,128)(2,1)S(1)}, u32[]{:S(2)}, u32[]{:S(2)}) collective-permute-start(bf16[4,64,256]{2,1,0:T(8,128)(2,1)S(1)} %get-tuple-element.60), channel_id=1, source_target_pairs={{0,24},{8,16},{16,8},{24,0},{1,25},{9,17},{17,9},{25,1},{2,26},{10... | collective-permute-start | bytes 393224 | tf_op jit(solution)/shard_map/ppermute | solution.py:520
  18.7 6.8 %collective-permute-start.6 = (bf16[4,64,256]{2,1,0:T(8,128)(2,1)S(1)}, bf16[4,64,256]{2,1,0:T(8,128)(2,1)S(1)}, u32[]{:S(2)}, u32[]{:S(2)}) collective-permute-start(bf16[4,64,256]{2,1,0:T(8,128)(2,1)S(1)} %get-tuple-element.61), channel_id=1, source_target_pairs={{0,16},{8,24},{16,0},{24,8},{1,17},{9,25},{17,1},{25,9},{2,18},{10... | collective-permute-start | bytes 393224 | tf_op jit(solution)/shard_map/ppermute | solution.py:520
  19.2 6.4 %collective-permute-start.7 = (bf16[4,64,256]{2,1,0:T(8,128)(2,1)S(1)}, bf16[4,64,256]{2,1,0:T(8,128)(2,1)S(1)}, u32[]{:S(2)}, u32[]{:S(2)}) collective-permute-start(bf16[4,64,256]{2,1,0:T(8,128)(2,1)S(1)} %get-tuple-element.62), channel_id=1, source_target_pairs={{0,8},{8,0},{16,24},{24,16},{1,9},{9,1},{17,25},{25,17},{2,10},{10... | collective-permute-start | bytes 393224 | tf_op jit(solution)/shard_map/ppermute | solution.py:520
  25.7 5.8 %collective-permute-start.10 = (bf16[64,256]{1,0:T(8,128)(2,1)S(1)}, bf16[64,256]{1,0:T(8,128)(2,1)S(1)}, u32[]{:S(2)}, u32[]{:S(2)}) collective-permute-start(bf16[64,256]{1,0:T(8,128)(2,1)S(1)} %get-tuple-element.81), channel_id=1, source_target_pairs={{0,6},{1,7},{2,4},{3,5},{4,2},{5,3},{6,0},{7,1},{8,14},{9,15},{10,... | collective-permute-start | bytes 98312 | tf_op jit(solution)/shard_map/ppermute | solution.py:525
  28.1 4.9 %collective-permute-start.11 = (bf16[64,256]{1,0:T(8,128)(2,1)S(1)}, bf16[64,256]{1,0:T(8,128)(2,1)S(1)}, u32[]{:S(2)}, u32[]{:S(2)}) collective-permute-start(bf16[64,256]{1,0:T(8,128)(2,1)S(1)} %get-tuple-element.82), channel_id=1, source_target_pairs={{0,4},{1,5},{2,6},{3,7},{4,0},{5,1},{6,2},{7,3},{8,12},{9,13},{10,... | collective-permute-start | bytes 98312 | tf_op jit(solution)/shard_map/ppermute | solution.py:525
  28.1 4.9 %collective-permute-start.12 = (bf16[64,256]{1,0:T(8,128)(2,1)S(1)}, bf16[64,256]{1,0:T(8,128)(2,1)S(1)}, u32[]{:S(2)}, u32[]{:S(2)}) collective-permute-start(bf16[64,256]{1,0:T(8,128)(2,1)S(1)} %get-tuple-element.83), channel_id=1, source_target_pairs={{0,2},{1,3},{2,0},{3,1},{4,6},{5,7},{6,4},{7,5},{8,10},{9,11},{10,... | collective-permute-start | bytes 98312 | tf_op jit(solution)/shard_map/ppermute | solution.py:525
  30.1 9.9 %collective-permute-start.8 = (bf16[2,128,512]{2,1,0:T(8,128)(2,1)S(1)}, bf16[2,128,512]{2,1,0:T(8,128)(2,1)S(1)}, u32[]{:S(2)}, u32[]{:S(2)}) collective-permute-start(bf16[2,128,512]{2,1,0:T(8,128)(2,1)S(1)} %get-tuple-element.79), channel_id=1, source_target_pairs={{0,7},{1,2},{2,1},{3,4},{4,3},{5,6},{6,5},{7,0},{8,15},{9,10},{10,... | collective-permute-start | bytes 786440 | tf_op jit(solution)/shard_map/ppermute | solution.py:504
  31.2 8.8 %collective-permute-start.9 = (bf16[2,128,512]{2,1,0:T(8,128)(2,1)S(1)}, bf16[2,128,512]{2,1,0:T(8,128)(2,1)S(1)}, u32[]{:S(2)}, u32[]{:S(2)}) collective-permute-start(bf16[2,128,512]{2,1,0:T(8,128)(2,1)S(1)} %get-tuple-element.80), channel_id=1, source_target_pairs={{0,1},{1,0},{2,3},{3,2},{4,5},{5,4},{6,7},{7,6},{8,9},{9,8},{10,11... | collective-permute-start | bytes 786440 | tf_op jit(solution)/shard_map/ppermute | solution.py:505
  33.0 4.9 %collective-permute-start.13 = (bf16[64,256]{1,0:T(8,128)(2,1)S(1)}, bf16[64,256]{1,0:T(8,128)(2,1)S(1)}, u32[]{:S(2)}, u32[]{:S(2)}) collective-permute-start(bf16[64,256]{1,0:T(8,128)(2,1)S(1)} %multiply_convert_fusion.refs_0_), channel_id=1, source_target_pairs={{0,24},{8,16},{16,8},{24,0},{1,25},{9,17},{17,9},{25,1},{2,26},{10... | collective-permute-start | bytes 98312 | tf_op jit(solution)/shard_map/ppermute | solution.py:528
  34.8 3.9 %collective-permute-start.14 = (bf16[64,256]{1,0:T(8,128)(2,1)S(1)}, bf16[64,256]{1,0:T(8,128)(2,1)S(1)}, u32[]{:S(2)}, u32[]{:S(2)}) collective-permute-start(bf16[64,256]{1,0:T(8,128)(2,1)S(1)} %multiply_convert_fusion.refs_0_), channel_id=1, source_target_pairs={{0,16},{8,24},{16,0},{24,8},{1,17},{9,25},{17,1},{25,9},{2,18},{10... | collective-permute-start | bytes 98312 | tf_op jit(solution)/shard_map/ppermute | solution.py:528
  36.0 3.9 %collective-permute-start.15 = (bf16[64,256]{1,0:T(8,128)(2,1)S(1)}, bf16[64,256]{1,0:T(8,128)(2,1)S(1)}, u32[]{:S(2)}, u32[]{:S(2)}) collective-permute-start(bf16[64,256]{1,0:T(8,128)(2,1)S(1)} %multiply_convert_fusion.refs_0_), channel_id=1, source_target_pairs={{0,8},{8,0},{16,24},{24,16},{1,9},{9,1},{17,25},{25,17},{2,10},{10... | collective-permute-start | bytes 98312 | tf_op jit(solution)/shard_map/ppermute | solution.py:528

commit v11 on v10

--- a/solution.py
+++ b/solution.py
@@ -56,8 +56,8 @@
     return slice((b + first - RAD) * BLK, (b + last - RAD + 1) * BLK)
 
 
-def masked(mask, b, c, part):
-    return part if c == RAD else jnp.where(mask[b, c] == 1, part, BIG_NEGATIVE)
+def masked(bias, b, c, part):
+    return part + bias[b * CAND + c]
 
 
 def pairs_of(blocks):
@@ -98,10 +98,18 @@
 
 
 def own_kernel(
-    mask, q_arg, k_arg, v_arg, g_arg, w_arg,
-    q, k, v, g, w_out, own_t, stats, exps, grad_t, rounded, sems,
+    bias, q_arg, k_arg, v_arg, g_arg, w_arg,
+    q, k, v, g_low, g_high, w_out, own_t, stats, exps, grad_t, rounded, sems,
 ):
-    pairs = ((q_arg, q), (k_arg, k), (v_arg, v), (g_arg, g), (w_arg, w_out))
+    half = g_low.shape[0]
+    pairs = (
+        (q_arg, q),
+        (k_arg, k),
+        (v_arg, v),
+        (g_arg.at[:half], g_low),
+        (g_arg.at[half:], g_high),
+        (w_arg, w_out),
+    )
     copies = [pltpu.make_async_copy(x, y, sems.at[i]) for i, (x, y) in enumerate(pairs)]
     for copy in copies:
         copy.start()
@@ -114,7 +122,8 @@
         scores = dot(k[here, cols], two_heads(q[rows, cols] * SCALE, 1), ((1,), (1,)))
         for c in range(first, last + 1):
             part = slice((c - first) * BLK, (c - first + 1) * BLK)
-            exps[b, p, part] = masked(mask, b, c, scores[part])
+            value = scores[part]
+            exps[b, p, part] = value if c == RAD else masked(bias, b, c, value)
     for b, rows, cols, p in pairs_of(blocks):
         here = own_rows(b, blocks)
         keys = slice(0, here.stop - here.start)
@@ -130,22 +139,23 @@
         here = own_rows(b, blocks)
         e = rounded[b, p, : here.stop - here.start]
         own_t[b, cols] = own_features(dot(v[here, cols], e, ((0,), (0,))))
-    copies[3].wait()
-    copies[4].wait()
+    for copy in copies[3:]:
+        copy.wait()
+    both = jnp.concatenate([g_low[...], g_high[...]], axis=0)
     for b in range(blocks):
         rows = slice(b * BLK, (b + 1) * BLK)
-        grad_t[b] = dot(w_out[...], g[rows], ((1,), (1,))).astype(BF16)
+        grad_t[b] = dot(w_out[...], both[rows], ((1,), (1,))).astype(BF16)
 
 
 def pair_cols(p):
     return slice(p * PAIR, (p + 1) * PAIR)
 
 
-def with_rim(mask, q, rim_k, rim_v, b, c, old, exps, rounded):
+def with_rim(bias, q, rim_k, rim_v, b, c, old, exps, rounded):
     for p in range(PAIRS):
         q2 = two_heads(q[rows_of(b), pair_cols(p)] * SCALE, 1)
         scores = dot(rim_k[:, pair_cols(p)], q2, ((1,), (1,)))
-        exps[p] = jnp.where(mask[b, c] == 1, scores, BIG_NEGATIVE)
+        exps[p] = masked(bias, b, c, scores)
     results = []
     for p in range(PAIRS):
         old_top, old_sum = old(p)
@@ -162,21 +172,28 @@
     return [(*result, part) for result, part in zip(results, parts)]
 
 
-def chip_kernel(mask, q, rim_k, rim_v, own_t, stats, chip_t, chip_stats, exps, rounded):
-    b, c = rim_block(q.shape[0] // BLK, False)
+def chip_kernel(bias, q, rim_k, rim_v, own_t, stats, chip_t, chip_stats, exps, rounded):
+    blocks = q.shape[0] // BLK
+    b, c = rim_block(blocks, False)
 
     def old(p):
         return stats[0, b, p : p + 1], stats[1, b, p : p + 1]
 
-    results = with_rim(mask, q, rim_k, rim_v, b, c, old, exps, rounded)
+    results = with_rim(bias, q, rim_k, rim_v, b, c, old, exps, rounded)
     for p, (top, kept, count, part) in enumerate(results):
-        chip_t[pair_cols(p)] = own_t[b, pair_cols(p)] * spread(kept) + part
-        chip_stats[0, p : p + 1] = top
-        chip_stats[1, p : p + 1] = count
+        at = slice(p, p + 1)
+        if blocks == 1:
+            chip_t[pair_cols(p)] = own_t[b, pair_cols(p)] * spread(kept) + part
+            chip_stats[0, at], chip_stats[1, at] = top, count
+        else:
+            share = 1.0 / count
+            attn = own_t[b, pair_cols(p)] * spread(kept * share) + part * spread(share)
+            chip_t[pair_cols(p)] = attn
+            chip_stats[0, at], chip_stats[1, at] = share, kept * share
 
 
 def forward_kernel(
-    mask, q, rim, own_t, stats, chip_t, chip_stats,
+    bias, q, rim, own_t, stats, chip_t, chip_stats,
     attn_t, mine, other, exps, own_factors, rim_factors, rounded,
 ):
     blocks = q.shape[0] // BLK
@@ -189,7 +206,7 @@
             return chip_stats[0, at], chip_stats[1, at]
         return stats[0, b, at], stats[1, b, at]
 
-    results = with_rim(mask, q, rim.at[0], rim.at[1], b, c, old, exps, rounded)
+    results = with_rim(bias, q, rim.at[0], rim.at[1], b, c, old, exps, rounded)
     for p, (top, kept, count, part) in enumerate(results):
         at = slice(p, p + 1)
         cols = pair_cols(p)
@@ -202,10 +219,9 @@
             own_factors[0, at] = jnp.exp(stats[0, 0, at] - top) * share
         else:
             own_factors[b, at] = kept * share
-            share = 1.0 / chip_stats[1, at]
-            attn_t[at_chip, cols] = (chip_t[cols] * spread(share)).astype(BF16)
-            rim_factors[1, at] = share
-            own_factors[at_chip, at] = jnp.exp(stats[0, at_chip, at] - chip_stats[0, at]) * share
+            attn_t[at_chip, cols] = chip_t[cols].astype(BF16)
+            rim_factors[1, at] = chip_stats[0, at]
+            own_factors[at_chip, at] = chip_stats[1, at]
         for inner in range(1, blocks - 1):
             share = 1.0 / stats[1, inner, at]
             attn_t[inner, cols] = (own_t[inner, cols] * spread(share)).astype(BF16)
@@ -221,13 +237,14 @@
             other[i, :, tokens] = jnp.where(first_core, odd, even)
 
 
-def flat_dot(attn, g):
+def flat_dot(attn, g_low, g_high):
     chips, rows, tokens = attn.shape
-    return dot(attn[...].reshape(chips * rows, tokens), g[...], ((1,), (0,)))
-
-
-def product_kernel(mine, g, product):
-    product[...] = flat_dot(mine, g)
+    g = jnp.concatenate([g_low[...], g_high[...]], axis=0)
+    return dot(attn[...].reshape(chips * rows, tokens), g, ((1,), (0,)))
+
+
+def product_kernel(mine, g_low, g_high, product):
+    product[...] = flat_dot(mine, g_low, g_high)
 
 
 def score_grads(probs, dprob, delta):
@@ -315,11 +332,11 @@
         output[b * BLK : (b + 1) * BLK] = part.astype(BF16)
 
 
-def halves_kernel(product, other, g, *outs):
+def halves_kernel(product, other, g_low, g_high, *outs):
     pieces, after = outs[:-1], outs[-1]
     at_dp = lax.axis_index("dp")
     chips, rows, cols = pieces[0].shape
-    both = (product[...] + flat_dot(other, g)).astype(BF16)
+    both = (product[...] + flat_dot(other, g_low, g_high)).astype(BF16)
     for d in range(len(pieces)):
         value = both[:, d * cols : (d + 1) * cols].reshape(chips, rows, cols)
         for s in range(len(pieces)):
@@ -371,33 +388,30 @@
     return jax.ShapeDtypeStruct(shape, dtype)
 
 
-def call(kernel, outs, flops, *args, mask=None, scratch=()):
+def call(kernel, outs, flops, *args, scratch=()):
     in_vmem = pl.BlockSpec(memory_space=pltpu.VMEM)
-    in_smem = pl.BlockSpec(memory_space=pltpu.SMEM)
-    masks = () if mask is None else (mask,)
     return pl.pallas_call(
         kernel,
         out_shape=outs,
-        in_specs=[in_smem] * len(masks) + [in_vmem] * len(args),
+        in_specs=[in_vmem] * len(args),
         out_specs=[in_vmem] * len(outs),
         scratch_shapes=list(scratch),
         compiler_params=pltpu.CompilerParams(vmem_limit_bytes=24 * 1024 * 1024),
         cost_estimate=pl.CostEstimate(flops=flops, bytes_accessed=flops // 250, transcendentals=0),
-    )(*masks, *args)
-
-
-def call_on_hbm(kernel, outs, *args, mask=None, scratch=()):
-    masks = () if mask is None else (mask,)
+    )(*args)
+
+
+def call_on_hbm(kernel, outs, *args, beside=(), scratch=()):
     return pl.pallas_call(
         kernel,
         out_shape=outs,
-        in_specs=[pl.BlockSpec(memory_space=pltpu.SMEM)] * len(masks)
+        in_specs=[pl.BlockSpec(memory_space=pltpu.VMEM)] * len(beside)
         + [pl.BlockSpec(memory_space=pltpu.HBM)] * len(args),
         out_specs=[pl.BlockSpec(memory_space=pltpu.VMEM)] * len(outs),
         scratch_shapes=list(scratch),
         compiler_params=pltpu.CompilerParams(vmem_limit_bytes=8 * 1024 * 1024),
         cost_estimate=pl.CostEstimate(flops=10**6, bytes_accessed=4096, transcendentals=0),
-    )(*masks, *(pltpu.with_memory_space_constraint(x, pltpu.HBM) for x in args))
+    )(*beside, *(pltpu.with_memory_space_constraint(x, pltpu.HBM) for x in args))
 
 
 def swap(count, bits):
@@ -431,27 +445,34 @@
     )
     link = lax.ppermute(to_link, "ctx", over_links(ctx))
     chip_k, chip_v = (lax.ppermute(x, "ctx", swap(ctx, 1)) for x in to_chip)
-    sibling_g = lax.ppermute(g, "ctx", swap(ctx, 1))
-    sibling_g = pltpu.with_memory_space_constraint(sibling_g, pltpu.VMEM)
-
     mask = lax.dynamic_slice_in_dim(block_mask[0], at_ctx * blocks, blocks, 0)
+    bias = jnp.where(mask == 1, 0.0, BIG_NEGATIVE).astype(F32).reshape(blocks * CAND, 1, 1)
+    bias = jnp.broadcast_to(bias, (blocks * CAND, 1, 2 * BLK))
     args = (q, k, v, g, w_out)
     own_keys = min(CAND, blocks) * BLK
     own_scores = (blocks, PAIRS, own_keys, 2 * BLK)
     rim_scores = (PAIRS, RIM, 2 * BLK)
-    q, k, v, g, w_out, own_t, stats, own_exps, grad_t = call_on_hbm(
+    half = vmem(tokens // 2, width)
+    q, k, v, g_low, g_high, w_out, own_t, stats, own_exps, grad_t = call_on_hbm(
         own_kernel,
-        [vmem(*x.shape) for x in args]
+        [vmem(tokens, feats)] * 3
         + [
+            half,
+            half,
+            vmem(feats, width),
             vmem(blocks, feats, BLK, dtype=F32),
             vmem(2, blocks, PAIRS, 2 * BLK, dtype=F32),
             vmem(*own_scores, dtype=F32),
             vmem(blocks, feats, BLK),
         ],
         *args,
-        mask=mask,
-        scratch=[vmem(*own_scores), pltpu.SemaphoreType.DMA((len(args),))],
-    )
+        beside=(bias,),
+        scratch=[vmem(*own_scores), pltpu.SemaphoreType.DMA((6,))],
+    )
+    sibling_g = [
+        pltpu.with_memory_space_constraint(lax.ppermute(x, "ctx", swap(ctx, 1)), pltpu.VMEM)
+        for x in (g_low, g_high)
+    ]
     chip_t, chip_stats, chip_exps = call(
         chip_kernel,
         [
@@ -460,8 +481,7 @@
             vmem(*rim_scores, dtype=F32),
         ],
         10**6,
-        q, chip_k, chip_v, own_t, stats,
-        mask=mask,
+        bias, q, chip_k, chip_v, own_t, stats,
         scratch=[vmem(*rim_scores)],
     )
     attn_t, mine, other, link_exps, own_factors, rim_factors = call(
@@ -475,19 +495,18 @@
             vmem(2, PAIRS, 2 * BLK, dtype=F32),
         ],
         10**6,
-        q, link, own_t, stats, chip_t, chip_stats,
-        mask=mask,
+        bias, q, link, own_t, stats, chip_t, chip_stats,
         scratch=[vmem(*rim_scores)],
     )
 
     other = lax.ppermute(other, "ctx", swap(ctx, 1))
     other = pltpu.with_memory_space_constraint(other, pltpu.VMEM)
-    (product,) = call(product_kernel, [vmem(chips * rows, width, dtype=F32)], 10**6, mine, g)
+    (product,) = call(product_kernel, [vmem(chips * rows, width, dtype=F32)], 10**6, mine, g_low, g_high)
     *halves, after = call(
         halves_kernel,
         [vmem(chips, rows, cols)] * dp + [vmem(8, 128, dtype=F32)],
         10**6,
-        product, other, sibling_g,
+        product, other, *sibling_g,
     )
     to_link, to_chip, deltas, rim_t = call(
         rim_kernel,

time: 41.2 us -> 40.5 us (0.983)
  Pallas kernels: 13 us -> 11.2 us
  starting transfers between devices: 18.5 us -> 20.1 us
  waiting for transfers between devices: 8.54 us -> 7.22 us
  other arithmetic: 0.02 us -> 0.78 us
    ppermute x3, waiting for transfers between devices: 1.76 us -> 0.31 us  [body(): lax.ppermute(quarters[s], 'ctx', swap(ctx, 2 * s))]
    pallas_call x9, Pallas kernels: 8.32 us -> 7.11 us  [call(): pl.pallas_call(kernel, out_shape=outs, in_specs=[in_vmem] * len(args), ou...]
    ppermute x1, starting transfers between devices: 1.06 us -> 2.18 us  [body(): grad_link = lax.ppermute(to_link, 'ctx', over_links(ctx))]
    select_n x0 -> x1, other arithmetic: none -> 0.75 us  [body(): jnp.where(mask == 1, 0.0, BIG_NEGATIVE).astype(F32)]
    ppermute x3, starting transfers between devices: 3.55 us -> 4.22 us  [body(): lax.ppermute(halves[s], 'dp', swap(dp, s))]
    pallas_call x2, Pallas kernels: 4.71 us -> 4.13 us  [call_on_hbm(): pl.pallas_call(kernel, out_shape=outs, in_specs=[pl.BlockSpec(memory_spac...]
    ppermute x3, waiting for transfers between devices: 2.76 us -> 3.26 us  [body(): lax.ppermute(halves[s], 'dp', swap(dp, s))]
  transfers between devices with their start and end apart: 16 -> 17, of which waited for: 11 -> 10; matrix products, arithmetic and copies ran while one was open for 0% -> 3% of each run, Pallas kernels for 28% -> 21%
where the time goes in v11:
time: 40.5 us; the launch traced here: 40.3 us
  starting transfers between devices  20.1 us (50%)
  Pallas kernels  11.2 us (28%)
  waiting for transfers between devices  7.22 us (18%)
  other arithmetic  0.78 us (2%)
  between operations  0.73 us (2%)
    pallas_call x9, Pallas kernels, call(): pl.pallas_call(kernel, out_shape=outs, in_specs=[in_vmem] * len(args), ou...  7.11 us
    ppermute x1, starting transfers between devices, body(): link = lax.ppermute(to_link, 'ctx', over_links(ctx))  4.55 us
    ppermute x3, starting transfers between devices, body(): lax.ppermute(quarters[s], 'ctx', swap(ctx, 2 * s))  4.45 us
    ppermute x3, starting transfers between devices, body(): lax.ppermute(halves[s], 'dp', swap(dp, s))  4.22 us
    pallas_call x2, Pallas kernels, call_on_hbm(): pl.pallas_call(kernel, out_shape=outs, in_specs=[pl.BlockSpec(memory_spac...  4.13 us
    ppermute x3, starting transfers between devices, body(): lax.ppermute(piece, 'dp', swap(dp, s))  3.55 us
    ppermute x3, waiting for transfers between devices, body(): lax.ppermute(halves[s], 'dp', swap(dp, s))  3.26 us
    ppermute x1, starting transfers between devices, body(): grad_link = lax.ppermute(to_link, 'ctx', over_links(ctx))  2.18 us
  transfers between devices with their start and end apart: 17, of which 10 were waited for; matrix products, arithmetic and copies ran while one was open for 3% of the time, Pallas kernels for 21%

profile of v11, /device:TPU:0, one launch (start us, length us, event | category | flops | bytes accessed | tf_op | source)
XLA Modules:
  0.0 40.3 jit_solution(12622284132876137502)
XLA Ops:
  0.6 1.1 %shard_map.102 = (bf16[2,128,512]{2,1,0:T(8,128)(2,1)S(1)}, bf16[128,512]{1,0:T(8,128)(2,1)S(1)}, bf16[128,512]{1,0:T(8,128)(2,1)S(1)}) custom-call(bf16[256,512]{1,0:T(8,128)(2,1)} %bitcast.8, bf16[256,512]{1,0:T(8,128)(2,1)} %bitcast.10), custom_call_target="tpu_custom_call" | custom-call | flops 1000000 | bytes 4096 | tf_op jit(solution)/shard_map/pallas_call | solution.py:405
  1.8 4.6 %collective-permute-start = (bf16[2,128,512]{2,1,0:T(8,128)(2,1)S(1)}, bf16[2,128,512]{2,1,0:T(8,128)(2,1)S(1)}, u32[]{:S(2)}, u32[]{:S(2)}) collective-permute-start(bf16[2,128,512]{2,1,0:T(8,128)(2,1)S(1)} %get-tuple-element.48), channel_id=1, source_target_pairs={{0,7},{1,2},{2,1},{3,4},{4,3},{5,6},{6,5},{7,0},{8,15},{9,10},{10,... | collective-permute-start | bytes 786440 | tf_op jit(solution)/shard_map/ppermute | solution.py:446
  6.3 0.0 collective-permute-start.1
  6.3 0.5 %collective-permute-start.2 = (bf16[128,512]{1,0:T(8,128)(2,1)S(1)}, bf16[128,512]{1,0:T(8,128)(2,1)S(1)}, u32[]{:S(2)}, u32[]{:S(2)}) collective-permute-start(bf16[128,512]{1,0:T(8,128)(2,1)S(1)} %get-tuple-element.52), channel_id=1, source_target_pairs={{0,1},{1,0},{2,3},{3,2},{4,5},{5,4},{6,7},{7,6},{8,9},{9,8},{10,11... | collective-permute-start | bytes 393224 | tf_op jit(solution)/shard_map/ppermute | solution.py:447
  6.8 0.8 %compare_select_fusion = f32[1,2,3]{1,0,2:T(1,128)S(1)} fusion(s32[1,16,3]{1,0,2:T(1,128)} %param.11, s32[]{:T(128)S(6)} %select_n.14), kind=kLoop, calls=%fused_computation.1 | loop fusion | flops 12 | bytes 52 | tf_op jit(solution)/shard_map/jit(_where)/select_n | solution.py:449
  7.6 0.1 copy.11
  7.7 0.1 select_n.16
  7.8 0.1 broadcast_in_dim.27.bias
  7.9 3.0 %shard_map.101 = (bf16[256,512]{1,0:T(8,128)(2,1)S(1)}, bf16[256,512]{1,0:T(8,128)(2,1)S(1)}, bf16[256,512]{1,0:T(8,128)(2,1)S(1)}, bf16[128,1024]{1,0:T(8,128)(...) custom-call(f32[6,1,256]{2,1,0:T(1,128)S(1)} %broadcast_in_dim.27.bi, ...), custom_call_target="tpu_custom_call" | custom-call | flops 1000000 | bytes 4096 | tf_op jit(solution)/shard_map/pallas_call | solution.py:405
  10.9 0.1 collective-permute-start.4
  10.9 0.5 %collective-permute-start.5 = (bf16[128,1024]{1,0:T(8,128)(2,1)S(1)}, bf16[128,1024]{1,0:T(8,128)(2,1)S(1)}, u32[]{:S(2)}, u32[]{:S(2)}) collective-permute-start(bf16[128,1024]{1,0:T(8,128)(2,1)S(1)} %get-tuple-element.59.g_high), channel_id=1, source_target_pairs={{0,1},{1,0},{2,3},{3,2},{4,5},{5,4},{6,7},{7,6},{8,9},{9,8},{10,11... | collective-permute-start | bytes 786440 | tf_op jit(solution)/shard_map/ppermute | solution.py:473
  11.4 0.0 collective-permute-done.1.rim_k.chip_k
  11.4 0.0 collective-permute-done.2.rim_v.chip_v
  11.4 0.5 %shard_map.103 = (f32[512,128]{1,0:T(8,128)S(1)}, f32[2,4,256]{2,1,0:T(4,128)S(1)}, f32[4,128,256]{2,1,0:T(8,128)S(1)}) custom-call(f32[6,1,256]{2,1,0:T(1,128)S(1)} %broadcast_in_dim.27.bias, bf16[256,512]{1,0:T(8,128)(2,1)S(1)} %get-tuple-element.47.q, bf16[128,512]{1,0:T(8,128)(2,1)S(1)} %collective-permute-done.1.rim_k.chip_k, ...), custom_call_target="tpu_custom_call" | custom-call | flops 1000000 | bytes 4000 | tf_op jit(solution)/shard_map/pallas_call | solution.py:393
  12.0 0.4 collective-permute-done.rim.link
  12.4 0.6 %shard_map.104 = (bf16[2,512,128]{2,1,0:T(8,128)(2,1)S(1)}, bf16[4,64,256]{2,1,0:T(8,128)(2,1)S(1)}, bf16[4,64,256]{2,1,0:T(8,128)(2,1)S(1)}, f32[4,128,256]{2,1...) custom-call(f32[6,1,256]{2,1,0:T(1,128)S(1)} %broadcast_in_dim.27.bias, ...), custom_call_target="tpu_custom_call" | custom-call | flops 1000000 | bytes 4000 | tf_op jit(solution)/shard_map/pallas_call | solution.py:393
  12.9 0.1 collective-permute-start.3
  13.0 0.3 shard_map.105.product
  13.3 0.0 collective-permute-done.4.g_low
  13.3 0.0 collective-permute-done.5.g_high
  13.3 1.0 %collective-permute-done.3.other = bf16[4,64,256]{2,1,0:T(8,128)(2,1)S(1)} collective-permute-done((bf16[4,64,256]{2,1,0:T(8,128)(2,1)S(1)}, bf16[4,64,256]{2,1,0:T(8,128)(2,1)S(1)}, u32[]{:S(2)}, u32[]{:S(2)}) %collective-permute-start.3) | collective-permute-done | bytes 131104 | tf_op jit(solution)/shard_map/ppermute | solution.py:502
  14.3 0.4 %shard_map.106 = (bf16[4,64,256]{2,1,0:T(8,128)(2,1)S(1)}, bf16[4,64,256]{2,1,0:T(8,128)(2,1)S(1)}, bf16[4,64,256]{2,1,0:T(8,128)(2,1)S(1)}, bf16[4,64,256]{2,1,0:T(8,128)(2,1)S(1)}, f32[8,128]{1,0:T(8,128)S(1)}) custom-call(f32[256,1024]{1,0:T(8,128)S(1)} %shard_map.105.product, bf16[4,64,256]{2,1,0:T(8,128)(2,1)S(1)} %collective-permute-done.3.other, ...), custom_call_target="tpu_custom_call" | custom-call | flops 1000000 | bytes 4000 | tf_op jit(solution)/shard_map/pallas_call | solution.py:393
  14.8 3.6 %collective-permute-start.6 = (bf16[4,64,256]{2,1,0:T(8,128)(2,1)S(1)}, bf16[4,64,256]{2,1,0:T(8,128)(2,1)S(1)}, u32[]{:S(2)}, u32[]{:S(2)}) collective-permute-start(bf16[4,64,256]{2,1,0:T(8,128)(2,1)S(1)} %get-tuple-element.62), channel_id=1, source_target_pairs={{0,24},{8,16},{16,8},{24,0},{1,25},{9,17},{17,9},{25,1},{2,26},{10... | collective-permute-start | bytes 393224 | tf_op jit(solution)/shard_map/ppermute | solution.py:539
  18.3 0.5 %collective-permute-start.7 = (bf16[4,64,256]{2,1,0:T(8,128)(2,1)S(1)}, bf16[4,64,256]{2,1,0:T(8,128)(2,1)S(1)}, u32[]{:S(2)}, u32[]{:S(2)}) collective-permute-start(bf16[4,64,256]{2,1,0:T(8,128)(2,1)S(1)} %get-tuple-element.63), channel_id=1, source_target_pairs={{0,16},{8,24},{16,0},{24,8},{1,17},{9,25},{17,1},{25,9},{2,18},{10... | collective-permute-start | bytes 393224 | tf_op jit(solution)/shard_map/ppermute | solution.py:539
  18.8 0.1 collective-permute-start.8
  19.0 0.9 %shard_map.107 = (bf16[2,128,512]{2,1,0:T(8,128)(2,1)S(1)}, bf16[2,128,512]{2,1,0:T(8,128)(2,1)S(1)}, f32[2,4,256]{2,1,0:T(4,128)S(1)}, f32[2,512,128]{2,1,0:T(8,128)S(1)}) custom-call(bf16[256,512]{1,0:T(8,128)(2,1)S(1)} %get-tuple-element.47.q, bf16[2,128,512]{2,1,0:T(8,128)(2,1)S(1)} %collective-permute-done.rim.link, ...), custom_call_target="tpu_custom_call" | custom-call | flops 1000000 | bytes 4000 | tf_op jit(solution)/shard_map/pallas_call | solution.py:393
  19.9 2.1 %shard_map.108 = (bf16[256,512]{1,0:T(8,128)(2,1)}, f32[256,512]{1,0:T(8,128)S(1)}, f32[256,512]{1,0:T(8,128)S(1)}, f32[8,128]{1,0:T(8,128)S(1)}) custom-call(bf16[256,512]{1,0:T(8,128)(2,1)S(1)} %get-tuple-element.47.q, bf16[256,512]{1,0:T(8,128)(2,1)S(1)} %get-tuple-element.65.k, bf16[256,512]{1,0:T(8,128)(2,1)S(1)} %get-tuple-element.66.v, ...), custom_call_target="tpu_custom_call" | custom-call | flops 1000000 | bytes 4000 | tf_op jit(solution)/shard_map/pallas_call | solution.py:393
  22.0 0.3 collective-permute-done.6.refs_1_
  22.3 2.7 %collective-permute-done.7.refs_2_ = bf16[4,64,256]{2,1,0:T(8,128)(2,1)S(1)} collective-permute-done((bf16[4,64,256]{2,1,0:T(8,128)(2,1)S(1)}, bf16[4,64,256]{2,1,0:T(8,128)(2,1)S(1)}, u32[]{:S(2)}, u32[]{:S(2)}) %collective-permute-start.7) | collective-permute-done | bytes 131104 | tf_op jit(solution)/shard_map/ppermute | solution.py:539
  25.0 0.3 collective-permute-done.8.refs_3_
  25.2 0.1 shard_map.109
  25.3 2.1 %collective-permute-start.11 = (bf16[64,256]{1,0:T(8,128)(2,1)S(1)}, bf16[64,256]{1,0:T(8,128)(2,1)S(1)}, u32[]{:S(2)}, u32[]{:S(2)}) collective-permute-start(bf16[64,256]{1,0:T(8,128)(2,1)S(1)} %get-tuple-element.83), channel_id=1, source_target_pairs={{0,6},{1,7},{2,4},{3,5},{4,2},{5,3},{6,0},{7,1},{8,14},{9,15},{10,... | collective-permute-start | bytes 98312 | tf_op jit(solution)/shard_map/ppermute | solution.py:544
  27.5 0.0 collective-permute-start.12
  27.5 2.3 %collective-permute-start.13 = (bf16[64,256]{1,0:T(8,128)(2,1)S(1)}, bf16[64,256]{1,0:T(8,128)(2,1)S(1)}, u32[]{:S(2)}, u32[]{:S(2)}) collective-permute-start(bf16[64,256]{1,0:T(8,128)(2,1)S(1)} %get-tuple-element.85), channel_id=1, source_target_pairs={{0,2},{1,3},{2,0},{3,1},{4,6},{5,7},{6,4},{7,5},{8,10},{9,11},{10,... | collective-permute-start | bytes 98312 | tf_op jit(solution)/shard_map/ppermute | solution.py:544
  29.8 0.0 collective-permute-start.10
  29.8 2.2 %collective-permute-start.9 = (bf16[2,128,512]{2,1,0:T(8,128)(2,1)S(1)}, bf16[2,128,512]{2,1,0:T(8,128)(2,1)S(1)}, u32[]{:S(2)}, u32[]{:S(2)}) collective-permute-start(bf16[2,128,512]{2,1,0:T(8,128)(2,1)S(1)} %get-tuple-element.81), channel_id=1, source_target_pairs={{0,7},{1,2},{2,1},{3,4},{4,3},{5,6},{6,5},{7,0},{8,15},{9,10},{10,... | collective-permute-start | bytes 786440 | tf_op jit(solution)/shard_map/ppermute | solution.py:523
  32.0 0.3 collective-permute-done.12
  32.3 0.0 collective-permute-done.13
  32.3 1.7 %collective-permute-start.14 = (bf16[64,256]{1,0:T(8,128)(2,1)S(1)}, bf16[64,256]{1,0:T(8,128)(2,1)S(1)}, u32[]{:S(2)}, u32[]{:S(2)}) collective-permute-start(bf16[64,256]{1,0:T(8,128)(2,1)S(1)} %multiply_convert_fusion.refs_0_), channel_id=1, source_target_pairs={{0,24},{8,16},{16,8},{24,0},{1,25},{9,17},{17,9},{25,1},{2,26},{10... | collective-permute-start | bytes 98312 | tf_op jit(solution)/shard_map/ppermute | solution.py:547
  34.0 1.3 %collective-permute-start.15 = (bf16[64,256]{1,0:T(8,128)(2,1)S(1)}, bf16[64,256]{1,0:T(8,128)(2,1)S(1)}, u32[]{:S(2)}, u32[]{:S(2)}) collective-permute-start(bf16[64,256]{1,0:T(8,128)(2,1)S(1)} %multiply_convert_fusion.refs_0_), channel_id=1, source_target_pairs={{0,16},{8,24},{16,0},{24,8},{1,17},{9,25},{17,1},{25,9},{2,18},{10... | collective-permute-start | bytes 98312 | tf_op jit(solution)/shard_map/ppermute | solution.py:547
  35.3 0.5 %collective-permute-start.16 = (bf16[64,256]{1,0:T(8,128)(2,1)S(1)}, bf16[64,256]{1,0:T(8,128)(2,1)S(1)}, u32[]{:S(2)}, u32[]{:S(2)}) collective-permute-start(bf16[64,256]{1,0:T(8,128)(2,1)S(1)} %multiply_convert_fusion.refs_0_), channel_id=1, source_target_pairs={{0,8},{8,0},{16,24},{24,16},{1,9},{9,1},{17,25},{25,17},{2,10},{10... | collective-permute-start | bytes 98312 | tf_op jit(solution)/shard_map/ppermute | solution.py:547
  35.9 1.3 %shard_map.110 = bf16[256,1024]{1,0:T(8,128)(2,1)} custom-call(bf16[2,512,128]{2,1,0:T(8,128)(2,1)S(1)} %get-tuple-element.55.attn_t, bf16[512,1024]{1,0:T(8,128)(2,1)S(1)} %get-tuple-element.56.w_out, bf16[64,256]{1,0:T(8,128)(2,1)S(1)} %get-tuple-element.77.before), custom_call_target="tpu_custom_call" | custom-call | flops 1000000 | bytes 4000 | tf_op jit(solution)/shard_map/pallas_call | solution.py:393
  37.1 0.1 collective-permute-done.14.refs_1_
  37.2 0.8 %collective-permute-done.15.refs_2_ = bf16[64,256]{1,0:T(8,128)(2,1)S(1)} collective-permute-done((bf16[64,256]{1,0:T(8,128)(2,1)S(1)}, bf16[64,256]{1,0:T(8,128)(2,1)S(1)}, u32[]{:S(2)}, u32[]{:S(2)}) %collective-permute-start.15) | collective-permute-done | bytes 32800 | tf_op jit(solution)/shard_map/ppermute | solution.py:547
  37.9 1.3 %collective-permute-done.16.refs_3_ = bf16[64,256]{1,0:T(8,128)(2,1)S(1)} collective-permute-done((bf16[64,256]{1,0:T(8,128)(2,1)S(1)}, bf16[64,256]{1,0:T(8,128)(2,1)S(1)}, u32[]{:S(2)}, u32[]{:S(2)}) %collective-permute-start.16) | collective-permute-done | bytes 32800 | tf_op jit(solution)/shard_map/ppermute | solution.py:547
  39.3 0.0 collective-permute-done.10.from_chip
  39.3 0.1 collective-permute-done.9.from_link
  39.4 1.0 %shard_map.111 = (bf16[256,512]{1,0:T(8,128)(2,1)}, bf16[256,512]{1,0:T(8,128)(2,1)}, f32[64,1024]{1,0:T(8,128)}) custom-call(f32[256,512]{1,0:T(8,128)S(1)} %get-tuple-element.79.k_own, f32[256,512]{1,0:T(8,128)S(1)} %get-tuple-element.80.v_own, bf16[2,128,512]{2,1,0:T(8,128)(2,1)S(1)} %collective-permute-done.9.from_link, ...), custom_call_target="tpu_custom_call" | custom-call | flops 1000000 | bytes 4000 | tf_op jit(solution)/shard_map/pallas_call | solution.py:393
  (2 shorter events, 0.0 us)
Async XLA Ops:
  1.8 10.6 %collective-permute-start = (bf16[2,128,512]{2,1,0:T(8,128)(2,1)S(1)}, bf16[2,128,512]{2,1,0:T(8,128)(2,1)S(1)}, u32[]{:S(2)}, u32[]{:S(2)}) collective-permute-start(bf16[2,128,512]{2,1,0:T(8,128)(2,1)S(1)} %get-tuple-element.48), channel_id=1, source_target_pairs={{0,7},{1,2},{2,1},{3,4},{4,3},{5,6},{6,5},{7,0},{8,15},{9,10},{10,... | collective-permute-start | bytes 786440 | tf_op jit(solution)/shard_map/ppermute | solution.py:446
  6.3 5.1 %collective-permute-start.1 = (bf16[128,512]{1,0:T(8,128)(2,1)S(1)}, bf16[128,512]{1,0:T(8,128)(2,1)S(1)}, u32[]{:S(2)}, u32[]{:S(2)}) collective-permute-start(bf16[128,512]{1,0:T(8,128)(2,1)S(1)} %get-tuple-element.51), channel_id=1, source_target_pairs={{0,1},{1,0},{2,3},{3,2},{4,5},{5,4},{6,7},{7,6},{8,9},{9,8},{10,11... | collective-permute-start | bytes 393224 | tf_op jit(solution)/shard_map/ppermute | solution.py:447
  6.3 5.1 %collective-permute-start.2 = (bf16[128,512]{1,0:T(8,128)(2,1)S(1)}, bf16[128,512]{1,0:T(8,128)(2,1)S(1)}, u32[]{:S(2)}, u32[]{:S(2)}) collective-permute-start(bf16[128,512]{1,0:T(8,128)(2,1)S(1)} %get-tuple-element.52), channel_id=1, source_target_pairs={{0,1},{1,0},{2,3},{3,2},{4,5},{5,4},{6,7},{7,6},{8,9},{9,8},{10,11... | collective-permute-start | bytes 393224 | tf_op jit(solution)/shard_map/ppermute | solution.py:447
  10.9 2.5 %collective-permute-start.4 = (bf16[128,1024]{1,0:T(8,128)(2,1)S(1)}, bf16[128,1024]{1,0:T(8,128)(2,1)S(1)}, u32[]{:S(2)}, u32[]{:S(2)}) collective-permute-start(bf16[128,1024]{1,0:T(8,128)(2,1)S(1)} %get-tuple-element.58.g_low), channel_id=1, source_target_pairs={{0,1},{1,0},{2,3},{3,2},{4,5},{5,4},{6,7},{7,6},{8,9},{9,8},{10,11... | collective-permute-start | bytes 786440 | tf_op jit(solution)/shard_map/ppermute | solution.py:473
  10.9 2.4 %collective-permute-start.5 = (bf16[128,1024]{1,0:T(8,128)(2,1)S(1)}, bf16[128,1024]{1,0:T(8,128)(2,1)S(1)}, u32[]{:S(2)}, u32[]{:S(2)}) collective-permute-start(bf16[128,1024]{1,0:T(8,128)(2,1)S(1)} %get-tuple-element.59.g_high), channel_id=1, source_target_pairs={{0,1},{1,0},{2,3},{3,2},{4,5},{5,4},{6,7},{7,6},{8,9},{9,8},{10,11... | collective-permute-start | bytes 786440 | tf_op jit(solution)/shard_map/ppermute | solution.py:473
  12.9 1.4 %collective-permute-start.3 = (bf16[4,64,256]{2,1,0:T(8,128)(2,1)S(1)}, bf16[4,64,256]{2,1,0:T(8,128)(2,1)S(1)}, u32[]{:S(2)}, u32[]{:S(2)}) collective-permute-start(bf16[4,64,256]{2,1,0:T(8,128)(2,1)S(1)} %get-tuple-element.60), channel_id=1, source_target_pairs={{0,1},{1,0},{2,3},{3,2},{4,5},{5,4},{6,7},{7,6},{8,9},{9,8},{10,11... | collective-permute-start | bytes 393224 | tf_op jit(solution)/shard_map/ppermute | solution.py:502
  14.8 7.5 %collective-permute-start.6 = (bf16[4,64,256]{2,1,0:T(8,128)(2,1)S(1)}, bf16[4,64,256]{2,1,0:T(8,128)(2,1)S(1)}, u32[]{:S(2)}, u32[]{:S(2)}) collective-permute-start(bf16[4,64,256]{2,1,0:T(8,128)(2,1)S(1)} %get-tuple-element.62), channel_id=1, source_target_pairs={{0,24},{8,16},{16,8},{24,0},{1,25},{9,17},{17,9},{25,1},{2,26},{10... | collective-permute-start | bytes 393224 | tf_op jit(solution)/shard_map/ppermute | solution.py:539
  18.3 6.6 %collective-permute-start.7 = (bf16[4,64,256]{2,1,0:T(8,128)(2,1)S(1)}, bf16[4,64,256]{2,1,0:T(8,128)(2,1)S(1)}, u32[]{:S(2)}, u32[]{:S(2)}) collective-permute-start(bf16[4,64,256]{2,1,0:T(8,128)(2,1)S(1)} %get-tuple-element.63), channel_id=1, source_target_pairs={{0,16},{8,24},{16,0},{24,8},{1,17},{9,25},{17,1},{25,9},{2,18},{10... | collective-permute-start | bytes 393224 | tf_op jit(solution)/shard_map/ppermute | solution.py:539
  18.8 6.4 %collective-permute-start.8 = (bf16[4,64,256]{2,1,0:T(8,128)(2,1)S(1)}, bf16[4,64,256]{2,1,0:T(8,128)(2,1)S(1)}, u32[]{:S(2)}, u32[]{:S(2)}) collective-permute-start(bf16[4,64,256]{2,1,0:T(8,128)(2,1)S(1)} %get-tuple-element.64), channel_id=1, source_target_pairs={{0,8},{8,0},{16,24},{24,16},{1,9},{9,1},{17,25},{25,17},{2,10},{10... | collective-permute-start | bytes 393224 | tf_op jit(solution)/shard_map/ppermute | solution.py:539
  25.3 6.6 %collective-permute-start.11 = (bf16[64,256]{1,0:T(8,128)(2,1)S(1)}, bf16[64,256]{1,0:T(8,128)(2,1)S(1)}, u32[]{:S(2)}, u32[]{:S(2)}) collective-permute-start(bf16[64,256]{1,0:T(8,128)(2,1)S(1)} %get-tuple-element.83), channel_id=1, source_target_pairs={{0,6},{1,7},{2,4},{3,5},{4,2},{5,3},{6,0},{7,1},{8,14},{9,15},{10,... | collective-permute-start | bytes 98312 | tf_op jit(solution)/shard_map/ppermute | solution.py:544
  27.5 4.8 %collective-permute-start.12 = (bf16[64,256]{1,0:T(8,128)(2,1)S(1)}, bf16[64,256]{1,0:T(8,128)(2,1)S(1)}, u32[]{:S(2)}, u32[]{:S(2)}) collective-permute-start(bf16[64,256]{1,0:T(8,128)(2,1)S(1)} %get-tuple-element.84), channel_id=1, source_target_pairs={{0,4},{1,5},{2,6},{3,7},{4,0},{5,1},{6,2},{7,3},{8,12},{9,13},{10,... | collective-permute-start | bytes 98312 | tf_op jit(solution)/shard_map/ppermute | solution.py:544
  27.5 4.8 %collective-permute-start.13 = (bf16[64,256]{1,0:T(8,128)(2,1)S(1)}, bf16[64,256]{1,0:T(8,128)(2,1)S(1)}, u32[]{:S(2)}, u32[]{:S(2)}) collective-permute-start(bf16[64,256]{1,0:T(8,128)(2,1)S(1)} %get-tuple-element.85), channel_id=1, source_target_pairs={{0,2},{1,3},{2,0},{3,1},{4,6},{5,7},{6,4},{7,5},{8,10},{9,11},{10,... | collective-permute-start | bytes 98312 | tf_op jit(solution)/shard_map/ppermute | solution.py:544
  29.8 9.5 %collective-permute-start.10 = (bf16[2,128,512]{2,1,0:T(8,128)(2,1)S(1)}, bf16[2,128,512]{2,1,0:T(8,128)(2,1)S(1)}, u32[]{:S(2)}, u32[]{:S(2)}) collective-permute-start(bf16[2,128,512]{2,1,0:T(8,128)(2,1)S(1)} %get-tuple-element.82), channel_id=1, source_target_pairs={{0,1},{1,0},{2,3},{3,2},{4,5},{5,4},{6,7},{7,6},{8,9},{9,8},{10,11... | collective-permute-start | bytes 786440 | tf_op jit(solution)/shard_map/ppermute | solution.py:524
  29.8 9.6 %collective-permute-start.9 = (bf16[2,128,512]{2,1,0:T(8,128)(2,1)S(1)}, bf16[2,128,512]{2,1,0:T(8,128)(2,1)S(1)}, u32[]{:S(2)}, u32[]{:S(2)}) collective-permute-start(bf16[2,128,512]{2,1,0:T(8,128)(2,1)S(1)} %get-tuple-element.81), channel_id=1, source_target_pairs={{0,7},{1,2},{2,1},{3,4},{4,3},{5,6},{6,5},{7,0},{8,15},{9,10},{10,... | collective-permute-start | bytes 786440 | tf_op jit(solution)/shard_map/ppermute | solution.py:523
  32.3 4.9 %collective-permute-start.14 = (bf16[64,256]{1,0:T(8,128)(2,1)S(1)}, bf16[64,256]{1,0:T(8,128)(2,1)S(1)}, u32[]{:S(2)}, u32[]{:S(2)}) collective-permute-start(bf16[64,256]{1,0:T(8,128)(2,1)S(1)} %multiply_convert_fusion.refs_0_), channel_id=1, source_target_pairs={{0,24},{8,16},{16,8},{24,0},{1,25},{9,17},{17,9},{25,1},{2,26},{10... | collective-permute-start | bytes 98312 | tf_op jit(solution)/shard_map/ppermute | solution.py:547
  34.0 3.9 %collective-permute-start.15 = (bf16[64,256]{1,0:T(8,128)(2,1)S(1)}, bf16[64,256]{1,0:T(8,128)(2,1)S(1)}, u32[]{:S(2)}, u32[]{:S(2)}) collective-permute-start(bf16[64,256]{1,0:T(8,128)(2,1)S(1)} %multiply_convert_fusion.refs_0_), channel_id=1, source_target_pairs={{0,16},{8,24},{16,0},{24,8},{1,17},{9,25},{17,1},{25,9},{2,18},{10... | collective-permute-start | bytes 98312 | tf_op jit(solution)/shard_map/ppermute | solution.py:547
  35.3 3.9 %collective-permute-start.16 = (bf16[64,256]{1,0:T(8,128)(2,1)S(1)}, bf16[64,256]{1,0:T(8,128)(2,1)S(1)}, u32[]{:S(2)}, u32[]{:S(2)}) collective-permute-start(bf16[64,256]{1,0:T(8,128)(2,1)S(1)} %multiply_convert_fusion.refs_0_), channel_id=1, source_target_pairs={{0,8},{8,0},{16,24},{24,16},{1,9},{9,1},{17,25},{25,17},{2,10},{10... | collective-permute-start | bytes 98312 | tf_op jit(solution)/shard_map/ppermute | solution.py:547

commit v12 on v11

--- a/solution.py
+++ b/solution.py
@@ -253,14 +253,14 @@
 
 def rim_kernel(
     q, link, chip_k, chip_v, grad_t, attn_t, link_exps, chip_exps, rim_factors, before,
-    to_link, to_chip, deltas, query_t, dprobs, dscores, rounded,
+    link_k_back, link_v_back, chip_back, deltas, query_t, dprobs, dscores, rounded,
 ):
     blocks = q.shape[0] // BLK
     sides = (
-        (rim_block(blocks, True)[0], link.at[0], link.at[1], link_exps, to_link),
-        (rim_block(blocks, False)[0], chip_k, chip_v, chip_exps, to_chip),
-    )
-    for i, (b, _, rim_v, _, _) in enumerate(sides):
+        (rim_block(blocks, True)[0], link.at[0], link.at[1], link_exps, link_k_back, link_v_back),
+        (rim_block(blocks, False)[0], chip_k, chip_v, chip_exps, chip_back.at[0], chip_back.at[1]),
+    )
+    for i, (b, _, rim_v, _, _, _) in enumerate(sides):
         for p in range(PAIRS):
             g2_t = two_heads(grad_t[b, pair_cols(p)], 0)
             dprobs[i, p] = dot(rim_v[:, pair_cols(p)], g2_t, ((1,), (0,)))
@@ -274,24 +274,24 @@
             axis=1,
         )
     query_t[...] = jnp.zeros_like(query_t)
-    for i, (b, _, _, exps, _) in enumerate(sides):
+    for i, (b, _, _, exps, _, _) in enumerate(sides):
         for p in range(PAIRS):
             at = slice(p, p + 1)
             dscores[i, p], rounded[i, p] = score_grads(
                 exps[p] * rim_factors[i, at], dprobs[i, p], deltas[b, at]
             )
-    for i, (b, rim_k, _, _, back) in enumerate(sides):
+    for i, (b, rim_k, _, _, k_back, v_back) in enumerate(sides):
         for p in range(PAIRS):
             cols = pair_cols(p)
             q2 = two_heads(q[rows_of(b), cols] * SCALE, 1)
             g2_t = two_heads(grad_t[b, cols], 0)
-            back[0, :, cols] = dot(dscores[i, p], q2, ((1,), (0,))).astype(BF16)
-            back[1, :, cols] = dot(rounded[i, p], g2_t, ((1,), (1,))).astype(BF16)
+            k_back[:, cols] = dot(dscores[i, p], q2, ((1,), (0,))).astype(BF16)
+            v_back[:, cols] = dot(rounded[i, p], g2_t, ((1,), (1,))).astype(BF16)
             query_t[b, cols] += own_features(dot(rim_k[:, cols], dscores[i, p], ((0,), (0,))))
 
 
 def own_backward_kernel(
-    q, k, v, grad_t, exps, factors, deltas, rim_t, before,
+    q, k, v, grad_t, exps, factors, deltas, rim_t,
     q_grad, k_own, v_own, after, dprobs, dscores, rounded,
 ):
     blocks = q.shape[0] // BLK
@@ -355,13 +355,16 @@
         out[...] = total([part[chip ^ s] for part in parts]).astype(BF16)
 
 
-def last_kernel(k_own, v_own, from_link, from_chip, *refs):
+def piece_kernel(scale, count, *refs):
+    refs[-1][...] = (total([part[...] for part in refs[:count]]) * scale).astype(BF16)
+
+
+def last_kernel(k_own, v_own, link_k, link_v, chip_kv, *refs):
     pieces, (k_grad, v_grad, weight_grad) = refs[:1] + refs[-4:0:-1], refs[-3:]
     tokens = k_own.shape[0]
     first_core = at_core() == 0
-    for which, (own, grad) in enumerate(((k_own, k_grad), (v_own, v_grad))):
-        link = from_link[which].astype(F32)
-        chip = from_chip[which].astype(F32)
+    for i, (own, rim, grad) in enumerate(((k_own, link_k, k_grad), (v_own, link_v, v_grad))):
+        link, chip = rim[...].astype(F32), chip_kv[i].astype(F32)
         low = jnp.where(first_core, link, chip)
         high = jnp.where(first_core, chip, link)
         if tokens == RIM:
@@ -508,10 +511,11 @@
         10**6,
         product, other, *sibling_g,
     )
-    to_link, to_chip, deltas, rim_t = call(
+    *back, deltas, rim_t = call(
         rim_kernel,
         [
-            vmem(2, RIM, feats),
+            rim,
+            rim,
             vmem(2, RIM, feats),
             vmem(blocks, PAIRS, 2 * BLK, dtype=F32),
             vmem(blocks, feats, BLK, dtype=F32),
@@ -520,9 +524,8 @@
         q, link, chip_k, chip_v, grad_t, attn_t, link_exps, chip_exps, rim_factors, after,
         scratch=[vmem(2, *rim_scores, dtype=F32), vmem(2, *rim_scores), vmem(2, *rim_scores)],
     )
-    grad_link = lax.ppermute(to_link, "ctx", over_links(ctx))
-    grad_chip = lax.ppermute(to_chip, "ctx", swap(ctx, 1))
-
+    link_back = [lax.ppermute(x, "ctx", over_links(ctx)) for x in back[:2]]
+    chip_back = lax.ppermute(back[2], "ctx", swap(ctx, 1))
     q_grad, k_own, v_own, after = call(
         own_backward_kernel,
         [
@@ -532,24 +535,28 @@
             vmem(8, 128, dtype=F32),
         ],
         10**6,
-        q, k, v, grad_t, own_exps, own_factors, deltas, rim_t, after,
+        q, k, v, grad_t, own_exps, own_factors, deltas, rim_t,
         scratch=[vmem(*own_scores, dtype=F32), vmem(*own_scores), vmem(*own_scores)],
     )
 
     halves = [halves[0]] + [lax.ppermute(halves[s], "dp", swap(dp, s)) for s in range(dp - 1, 0, -1)]
     quarters = call(chips_kernel, [vmem(rows, cols)] * chips, 10**6, *halves, after)
-    (output,) = call(output_kernel, [hbm(tokens, width)], 10**6, attn_t, w_out, quarters[0])
-    piece = total(
-        [quarters[0]]
-        + [lax.ppermute(quarters[s], "ctx", swap(ctx, 2 * s)) for s in range(chips - 1, 0, -1)]
-    )
-    piece = (piece * (dp * tokens * ctx) ** (-0.5)).astype(BF16)
+    (output,) = call(output_kernel, [hbm(tokens, width)], 5 * 10**9, attn_t, w_out, quarters[0])
+    quarters = [quarters[0]] + [
+        lax.ppermute(quarters[s], "ctx", swap(ctx, 2 * s)) for s in range(chips - 1, 0, -1)
+    ]
+    (piece,) = call(
+        functools.partial(piece_kernel, (dp * tokens * ctx) ** (-0.5), chips),
+        [vmem(rows, cols)],
+        10**6,
+        *quarters, *link_back,
+    )
     pieces = [piece] + [lax.ppermute(piece, "dp", swap(dp, s)) for s in range(dp - 1, 0, -1)]
     k_grad, v_grad, weight_grad = call(
         last_kernel,
         [hbm(tokens, feats), hbm(tokens, feats), hbm(rows, width, dtype=F32)],
         10**6,
-        k_own, v_own, grad_link, grad_chip, *pieces,
+        k_own, v_own, *link_back, chip_back, *pieces,
     )
     return (output[None], q_grad[None], k_grad[None], v_grad[None], weight_grad)
 

time: 40.5 us -> 40.8 us (level)
  starting transfers between devices: 20.1 us -> 21.5 us
  waiting for transfers between devices: 7.22 us -> 6.03 us
    ppermute x3, waiting for transfers between devices: 3.26 us -> 0.01 us  [body(): lax.ppermute(halves[s], 'dp', swap(dp, s))]
    ppermute x3, waiting for transfers between devices: 0.31 us -> 2.23 us  [body(): lax.ppermute(quarters[s], 'ctx', swap(ctx, 2 * s))]
    ppermute x2 -> x3, starting transfers between devices: 2.19 us -> 3.61 us  [the longest x2 3.61 us: body(): link_back = [lax.ppermute(x, 'ctx', over_links(ctx)) for x in back[:2]]]
    pallas_call x9 -> x10, Pallas kernels: 7.11 us -> 7.15 us  [call(): pl.pallas_call(kernel, out_shape=outs, in_specs=[in_vmem] * len(args), ou...]
  transfers between devices with their start and end apart: 17 -> 18, of which waited for: 10 -> 7; matrix products, arithmetic and copies ran while one was open for 3% -> 2% of each run, Pallas kernels for 21% -> 22%
where the time goes in v12:
time: 40.8 us; the launch traced here: 40.6 us
  starting transfers between devices  21.5 us (53%)
  Pallas kernels  11.3 us (28%)
  waiting for transfers between devices  6.03 us (15%)
  other arithmetic  0.75 us (2%)
  between operations  0.74 us (2%)
    pallas_call x10, Pallas kernels, call(): pl.pallas_call(kernel, out_shape=outs, in_specs=[in_vmem] * len(args), ou...  7.15 us
    ppermute x1, starting transfers between devices, body(): link = lax.ppermute(to_link, 'ctx', over_links(ctx))  4.55 us
    ppermute x3, starting transfers between devices, body(): lax.ppermute(quarters[s], 'ctx', swap(ctx, 2 * s))  4.45 us
    ppermute x3, starting transfers between devices, body(): lax.ppermute(halves[s], 'dp', swap(dp, s))  4.22 us
    pallas_call x2, Pallas kernels, call_on_hbm(): pl.pallas_call(kernel, out_shape=outs, in_specs=[pl.BlockSpec(memory_spac...  4.17 us
    ppermute x2, starting transfers between devices, body(): link_back = [lax.ppermute(x, 'ctx', over_links(ctx)) for x in back[:2]]  3.61 us
    ppermute x3, starting transfers between devices, body(): lax.ppermute(piece, 'dp', swap(dp, s))  3.55 us
    ppermute x3, waiting for transfers between devices, body(): lax.ppermute(piece, 'dp', swap(dp, s))  2.39 us
  transfers between devices with their start and end apart: 18, of which 7 were waited for; matrix products, arithmetic and copies ran while one was open for 2% of the time, Pallas kernels for 22%

profile of v12, /device:TPU:0, one launch (start us, length us, event | category | flops | bytes accessed | tf_op | source)
XLA Modules:
  0.0 40.6 jit_solution(6429424373403638328)
XLA Ops:
  0.6 1.1 %shard_map.102 = (bf16[2,128,512]{2,1,0:T(8,128)(2,1)S(1)}, bf16[128,512]{1,0:T(8,128)(2,1)S(1)}, bf16[128,512]{1,0:T(8,128)(2,1)S(1)}) custom-call(bf16[256,512]{1,0:T(8,128)(2,1)} %bitcast.8, bf16[256,512]{1,0:T(8,128)(2,1)} %bitcast.10), custom_call_target="tpu_custom_call" | custom-call | flops 1000000 | bytes 4096 | tf_op jit(solution)/shard_map/pallas_call | solution.py:408
  1.8 4.6 %collective-permute-start = (bf16[2,128,512]{2,1,0:T(8,128)(2,1)S(1)}, bf16[2,128,512]{2,1,0:T(8,128)(2,1)S(1)}, u32[]{:S(2)}, u32[]{:S(2)}) collective-permute-start(bf16[2,128,512]{2,1,0:T(8,128)(2,1)S(1)} %get-tuple-element.49), channel_id=1, source_target_pairs={{0,7},{1,2},{2,1},{3,4},{4,3},{5,6},{6,5},{7,0},{8,15},{9,10},{10,... | collective-permute-start | bytes 786440 | tf_op jit(solution)/shard_map/ppermute | solution.py:449
  6.3 0.0 collective-permute-start.1
  6.3 0.5 %collective-permute-start.2 = (bf16[128,512]{1,0:T(8,128)(2,1)S(1)}, bf16[128,512]{1,0:T(8,128)(2,1)S(1)}, u32[]{:S(2)}, u32[]{:S(2)}) collective-permute-start(bf16[128,512]{1,0:T(8,128)(2,1)S(1)} %get-tuple-element.53), channel_id=1, source_target_pairs={{0,1},{1,0},{2,3},{3,2},{4,5},{5,4},{6,7},{7,6},{8,9},{9,8},{10,11... | collective-permute-start | bytes 393224 | tf_op jit(solution)/shard_map/ppermute | solution.py:450
  6.8 0.8 %compare_select_fusion = f32[1,2,3]{1,0,2:T(1,128)S(1)} fusion(s32[1,16,3]{1,0,2:T(1,128)} %param.11, s32[]{:T(128)S(6)} %select_n.14), kind=kLoop, calls=%fused_computation | loop fusion | flops 12 | bytes 52 | tf_op jit(solution)/shard_map/jit(_where)/select_n | solution.py:452
  7.6 0.1 copy.11
  7.7 0.1 select_n.16
  7.8 0.1 broadcast_in_dim.27.bias
  7.9 3.0 %shard_map.101 = (bf16[256,512]{1,0:T(8,128)(2,1)S(1)}, bf16[256,512]{1,0:T(8,128)(2,1)S(1)}, bf16[256,512]{1,0:T(8,128)(2,1)S(1)}, bf16[128,1024]{1,0:T(8,128)(...) custom-call(f32[6,1,256]{2,1,0:T(1,128)S(1)} %broadcast_in_dim.27.bi, ...), custom_call_target="tpu_custom_call" | custom-call | flops 1000000 | bytes 4096 | tf_op jit(solution)/shard_map/pallas_call | solution.py:408
  10.9 0.1 collective-permute-start.4
  11.0 0.5 %collective-permute-start.5 = (bf16[128,1024]{1,0:T(8,128)(2,1)S(1)}, bf16[128,1024]{1,0:T(8,128)(2,1)S(1)}, u32[]{:S(2)}, u32[]{:S(2)}) collective-permute-start(bf16[128,1024]{1,0:T(8,128)(2,1)S(1)} %get-tuple-element.60.g_high), channel_id=1, source_target_pairs={{0,1},{1,0},{2,3},{3,2},{4,5},{5,4},{6,7},{7,6},{8,9},{9,8},{10,11... | collective-permute-start | bytes 786440 | tf_op jit(solution)/shard_map/ppermute | solution.py:476
  11.5 0.0 collective-permute-done.1.rim_k.chip_k
  11.5 0.0 collective-permute-done.2.rim_v.chip_v
  11.5 0.5 %shard_map.103 = (f32[512,128]{1,0:T(8,128)S(1)}, f32[2,4,256]{2,1,0:T(4,128)S(1)}, f32[4,128,256]{2,1,0:T(8,128)S(1)}) custom-call(f32[6,1,256]{2,1,0:T(1,128)S(1)} %broadcast_in_dim.27.bias, bf16[256,512]{1,0:T(8,128)(2,1)S(1)} %get-tuple-element.48.q, bf16[128,512]{1,0:T(8,128)(2,1)S(1)} %collective-permute-done.1.rim_k.chip_k, ...), custom_call_target="tpu_custom_call" | custom-call | flops 1000000 | bytes 4000 | tf_op jit(solution)/shard_map/pallas_call | solution.py:396
  12.0 0.4 collective-permute-done.rim.link
  12.4 0.6 %shard_map.104 = (bf16[2,512,128]{2,1,0:T(8,128)(2,1)S(1)}, bf16[4,64,256]{2,1,0:T(8,128)(2,1)S(1)}, bf16[4,64,256]{2,1,0:T(8,128)(2,1)S(1)}, f32[4,128,256]{2,1...) custom-call(f32[6,1,256]{2,1,0:T(1,128)S(1)} %broadcast_in_dim.27.bias, ...), custom_call_target="tpu_custom_call" | custom-call | flops 1000000 | bytes 4000 | tf_op jit(solution)/shard_map/pallas_call | solution.py:396
  12.9 0.1 collective-permute-start.3
  13.0 0.3 shard_map.105.product
  13.3 0.0 collective-permute-done.4.g_low
  13.3 0.0 collective-permute-done.5.g_high
  13.3 1.0 %collective-permute-done.3.other = bf16[4,64,256]{2,1,0:T(8,128)(2,1)S(1)} collective-permute-done((bf16[4,64,256]{2,1,0:T(8,128)(2,1)S(1)}, bf16[4,64,256]{2,1,0:T(8,128)(2,1)S(1)}, u32[]{:S(2)}, u32[]{:S(2)}) %collective-permute-start.3) | collective-permute-done | bytes 131104 | tf_op jit(solution)/shard_map/ppermute | solution.py:505
  14.3 0.4 %shard_map.106 = (bf16[4,64,256]{2,1,0:T(8,128)(2,1)S(1)}, bf16[4,64,256]{2,1,0:T(8,128)(2,1)S(1)}, bf16[4,64,256]{2,1,0:T(8,128)(2,1)S(1)}, bf16[4,64,256]{2,1,0:T(8,128)(2,1)S(1)}, f32[8,128]{1,0:T(8,128)S(1)}) custom-call(f32[256,1024]{1,0:T(8,128)S(1)} %shard_map.105.product, bf16[4,64,256]{2,1,0:T(8,128)(2,1)S(1)} %collective-permute-done.3.other, ...), custom_call_target="tpu_custom_call" | custom-call | flops 1000000 | bytes 4000 | tf_op jit(solution)/shard_map/pallas_call | solution.py:396
  14.8 3.6 %collective-permute-start.6 = (bf16[4,64,256]{2,1,0:T(8,128)(2,1)S(1)}, bf16[4,64,256]{2,1,0:T(8,128)(2,1)S(1)}, u32[]{:S(2)}, u32[]{:S(2)}) collective-permute-start(bf16[4,64,256]{2,1,0:T(8,128)(2,1)S(1)} %get-tuple-element.63), channel_id=1, source_target_pairs={{0,24},{8,16},{16,8},{24,0},{1,25},{9,17},{17,9},{25,1},{2,26},{10... | collective-permute-start | bytes 393224 | tf_op jit(solution)/shard_map/ppermute | solution.py:542
  18.3 0.5 %collective-permute-start.7 = (bf16[4,64,256]{2,1,0:T(8,128)(2,1)S(1)}, bf16[4,64,256]{2,1,0:T(8,128)(2,1)S(1)}, u32[]{:S(2)}, u32[]{:S(2)}) collective-permute-start(bf16[4,64,256]{2,1,0:T(8,128)(2,1)S(1)} %get-tuple-element.64), channel_id=1, source_target_pairs={{0,16},{8,24},{16,0},{24,8},{1,17},{9,25},{17,1},{25,9},{2,18},{10... | collective-permute-start | bytes 393224 | tf_op jit(solution)/shard_map/ppermute | solution.py:542
  18.9 0.1 collective-permute-start.8
  19.0 0.9 %shard_map.107 = (bf16[128,512]{1,0:T(8,128)(2,1)S(1)}, bf16[128,512]{1,0:T(8,128)(2,1)S(1)}, bf16[2,128,512]{2,1,0:T(8,128)(2,1)S(1)}, f32[2,4,256]{2,1,0:T(4,128)S(1)}, f32[2,512,128]{2,1,0:T(8,128)S(1)}) custom-call(bf16[256,512]{1,0:T(8,128)(2,1)S(1)} %get-tuple-element.48.q, bf16[2,128,512]{2,1,0:T(8,128)(2,1)S(1)} %collective-permute-done.rim.link, ...), custom_call_target="tpu_custom_call" | custom-call | flops 1000000 | bytes 4000 | tf_op jit(solution)/shard_map/pallas_call | solution.py:396
  19.9 1.5 %collective-permute-start.10 = (bf16[128,512]{1,0:T(8,128)(2,1)S(1)}, bf16[128,512]{1,0:T(8,128)(2,1)S(1)}, u32[]{:S(2)}, u32[]{:S(2)}) collective-permute-start(bf16[128,512]{1,0:T(8,128)(2,1)S(1)} %get-tuple-element.83), channel_id=1, source_target_pairs={{0,7},{1,2},{2,1},{3,4},{4,3},{5,6},{6,5},{7,0},{8,15},{9,10},{10,... | collective-permute-start | bytes 393224 | tf_op jit(solution)/shard_map/ppermute | solution.py:527
  21.3 2.2 %collective-permute-start.9 = (bf16[128,512]{1,0:T(8,128)(2,1)S(1)}, bf16[128,512]{1,0:T(8,128)(2,1)S(1)}, u32[]{:S(2)}, u32[]{:S(2)}) collective-permute-start(bf16[128,512]{1,0:T(8,128)(2,1)S(1)} %get-tuple-element.82), channel_id=1, source_target_pairs={{0,7},{1,2},{2,1},{3,4},{4,3},{5,6},{6,5},{7,0},{8,15},{9,10},{10,... | collective-permute-start | bytes 393224 | tf_op jit(solution)/shard_map/ppermute | solution.py:527
  23.5 2.1 %shard_map.108 = (bf16[256,512]{1,0:T(8,128)(2,1)}, f32[256,512]{1,0:T(8,128)S(1)}, f32[256,512]{1,0:T(8,128)S(1)}, f32[8,128]{1,0:T(8,128)S(1)}) custom-call(bf16[256,512]{1,0:T(8,128)(2,1)S(1)} %get-tuple-element.48.q, bf16[256,512]{1,0:T(8,128)(2,1)S(1)} %get-tuple-element.66.k, bf16[256,512]{1,0:T(8,128)(2,1)S(1)} %get-tuple-element.67.v, ...), custom_call_target="tpu_custom_call" | custom-call | flops 1000000 | bytes 4000 | tf_op jit(solution)/shard_map/pallas_call | solution.py:396
  25.6 0.0 collective-permute-done.6.refs_1_
  25.6 0.0 collective-permute-done.7.refs_2_
  25.6 0.1 shard_map.109
  25.7 1.8 %collective-permute-start.12 = (bf16[64,256]{1,0:T(8,128)(2,1)S(1)}, bf16[64,256]{1,0:T(8,128)(2,1)S(1)}, u32[]{:S(2)}, u32[]{:S(2)}) collective-permute-start(bf16[64,256]{1,0:T(8,128)(2,1)S(1)} %get-tuple-element.85), channel_id=1, source_target_pairs={{0,6},{1,7},{2,4},{3,5},{4,2},{5,3},{6,0},{7,1},{8,14},{9,15},{10,... | collective-permute-start | bytes 98312 | tf_op jit(solution)/shard_map/ppermute | solution.py:546
  27.5 2.7 %collective-permute-start.14 = (bf16[64,256]{1,0:T(8,128)(2,1)S(1)}, bf16[64,256]{1,0:T(8,128)(2,1)S(1)}, u32[]{:S(2)}, u32[]{:S(2)}) collective-permute-start(bf16[64,256]{1,0:T(8,128)(2,1)S(1)} %get-tuple-element.87), channel_id=1, source_target_pairs={{0,2},{1,3},{2,0},{3,1},{4,6},{5,7},{6,4},{7,5},{8,10},{9,11},{10,... | collective-permute-start | bytes 98312 | tf_op jit(solution)/shard_map/ppermute | solution.py:546
  30.2 0.0 collective-permute-done.10.refs_5_.link_v
  30.2 0.0 collective-permute-start.11
  30.2 0.0 collective-permute-done.9.refs_4_.link_k
  30.2 1.3 %collective-permute-done.12.refs_1_ = bf16[64,256]{1,0:T(8,128)(2,1)S(1)} collective-permute-done((bf16[64,256]{1,0:T(8,128)(2,1)S(1)}, bf16[64,256]{1,0:T(8,128)(2,1)S(1)}, u32[]{:S(2)}, u32[]{:S(2)}) %collective-permute-start.12) | collective-permute-done | bytes 32800 | tf_op jit(solution)/shard_map/ppermute | solution.py:546
  31.5 0.9 %collective-permute-done.13.refs_2_ = bf16[64,256]{1,0:T(8,128)(2,1)S(1)} collective-permute-done((bf16[64,256]{1,0:T(8,128)(2,1)S(1)}, bf16[64,256]{1,0:T(8,128)(2,1)S(1)}, u32[]{:S(2)}, u32[]{:S(2)}) %collective-permute-start.13) | collective-permute-done | bytes 32800 | tf_op jit(solution)/shard_map/ppermute | solution.py:546
  32.4 0.0 collective-permute-done.14.refs_3_
  32.4 2.6 %collective-permute-start.15 = (bf16[64,256]{1,0:T(8,128)(2,1)S(1)}, bf16[64,256]{1,0:T(8,128)(2,1)S(1)}, u32[]{:S(2)}, u32[]{:S(2)}) collective-permute-start(bf16[64,256]{1,0:T(8,128)(2,1)S(1)} %shard_map.111.refs_0_), channel_id=1, source_target_pairs={{0,24},{8,16},{16,8},{24,0},{1,25},{9,17},{17,9},{25,1},{2,26},{10... | collective-permute-start | bytes 98312 | tf_op jit(solution)/shard_map/ppermute | solution.py:554
  35.0 0.7 %collective-permute-start.16 = (bf16[64,256]{1,0:T(8,128)(2,1)S(1)}, bf16[64,256]{1,0:T(8,128)(2,1)S(1)}, u32[]{:S(2)}, u32[]{:S(2)}) collective-permute-start(bf16[64,256]{1,0:T(8,128)(2,1)S(1)} %shard_map.111.refs_0_), channel_id=1, source_target_pairs={{0,16},{8,24},{16,0},{24,8},{1,17},{9,25},{17,1},{25,9},{2,18},{10... | collective-permute-start | bytes 98312 | tf_op jit(solution)/shard_map/ppermute | solution.py:554
  35.7 0.3 collective-permute-start.17
  36.0 1.3 %shard_map.110 = bf16[256,1024]{1,0:T(8,128)(2,1)} custom-call(bf16[2,512,128]{2,1,0:T(8,128)(2,1)S(1)} %get-tuple-element.56.attn_t, bf16[512,1024]{1,0:T(8,128)(2,1)S(1)} %get-tuple-element.57.w_out, bf16[64,256]{1,0:T(8,128)(2,1)S(1)} %get-tuple-element.78.before.refs_0_), custom_call_target="tpu_custom_call" | custom-call | flops 5000000000 | bytes 20000000 | tf_op jit(solution)/shard_map/pallas_call | solution.py:396
  37.3 0.2 collective-permute-done.15.refs_1_
  37.5 1.4 %collective-permute-done.16.refs_2_ = bf16[64,256]{1,0:T(8,128)(2,1)S(1)} collective-permute-done((bf16[64,256]{1,0:T(8,128)(2,1)S(1)}, bf16[64,256]{1,0:T(8,128)(2,1)S(1)}, u32[]{:S(2)}, u32[]{:S(2)}) %collective-permute-start.16) | collective-permute-done | bytes 32800 | tf_op jit(solution)/shard_map/ppermute | solution.py:554
  38.9 0.7 %collective-permute-done.17.refs_3_ = bf16[64,256]{1,0:T(8,128)(2,1)S(1)} collective-permute-done((bf16[64,256]{1,0:T(8,128)(2,1)S(1)}, bf16[64,256]{1,0:T(8,128)(2,1)S(1)}, u32[]{:S(2)}, u32[]{:S(2)}) %collective-permute-start.17) | collective-permute-done | bytes 32800 | tf_op jit(solution)/shard_map/ppermute | solution.py:554
  39.6 1.0 %shard_map.112 = (bf16[256,512]{1,0:T(8,128)(2,1)}, bf16[256,512]{1,0:T(8,128)(2,1)}, f32[64,1024]{1,0:T(8,128)}) custom-call(f32[256,512]{1,0:T(8,128)S(1)} %get-tuple-element.80.k_own, f32[256,512]{1,0:T(8,128)S(1)} %get-tuple-element.81.v_own, bf16[128,512]{1,0:T(8,128)(2,1)S(1)} %collective-permute-done.9.refs_4_.link_k, ...), custom_call_target="tpu_custom_call" | custom-call | flops 1000000 | bytes 4000 | tf_op jit(solution)/shard_map/pallas_call | solution.py:396
  (4 shorter events, 0.0 us)
Async XLA Ops:
  1.8 10.6 %collective-permute-start = (bf16[2,128,512]{2,1,0:T(8,128)(2,1)S(1)}, bf16[2,128,512]{2,1,0:T(8,128)(2,1)S(1)}, u32[]{:S(2)}, u32[]{:S(2)}) collective-permute-start(bf16[2,128,512]{2,1,0:T(8,128)(2,1)S(1)} %get-tuple-element.49), channel_id=1, source_target_pairs={{0,7},{1,2},{2,1},{3,4},{4,3},{5,6},{6,5},{7,0},{8,15},{9,10},{10,... | collective-permute-start | bytes 786440 | tf_op jit(solution)/shard_map/ppermute | solution.py:449
  6.3 5.1 %collective-permute-start.1 = (bf16[128,512]{1,0:T(8,128)(2,1)S(1)}, bf16[128,512]{1,0:T(8,128)(2,1)S(1)}, u32[]{:S(2)}, u32[]{:S(2)}) collective-permute-start(bf16[128,512]{1,0:T(8,128)(2,1)S(1)} %get-tuple-element.52), channel_id=1, source_target_pairs={{0,1},{1,0},{2,3},{3,2},{4,5},{5,4},{6,7},{7,6},{8,9},{9,8},{10,11... | collective-permute-start | bytes 393224 | tf_op jit(solution)/shard_map/ppermute | solution.py:450
  6.3 5.1 %collective-permute-start.2 = (bf16[128,512]{1,0:T(8,128)(2,1)S(1)}, bf16[128,512]{1,0:T(8,128)(2,1)S(1)}, u32[]{:S(2)}, u32[]{:S(2)}) collective-permute-start(bf16[128,512]{1,0:T(8,128)(2,1)S(1)} %get-tuple-element.53), channel_id=1, source_target_pairs={{0,1},{1,0},{2,3},{3,2},{4,5},{5,4},{6,7},{7,6},{8,9},{9,8},{10,11... | collective-permute-start | bytes 393224 | tf_op jit(solution)/shard_map/ppermute | solution.py:450
  10.9 2.4 %collective-permute-start.4 = (bf16[128,1024]{1,0:T(8,128)(2,1)S(1)}, bf16[128,1024]{1,0:T(8,128)(2,1)S(1)}, u32[]{:S(2)}, u32[]{:S(2)}) collective-permute-start(bf16[128,1024]{1,0:T(8,128)(2,1)S(1)} %get-tuple-element.59.g_low), channel_id=1, source_target_pairs={{0,1},{1,0},{2,3},{3,2},{4,5},{5,4},{6,7},{7,6},{8,9},{9,8},{10,11... | collective-permute-start | bytes 786440 | tf_op jit(solution)/shard_map/ppermute | solution.py:476
  11.0 2.4 %collective-permute-start.5 = (bf16[128,1024]{1,0:T(8,128)(2,1)S(1)}, bf16[128,1024]{1,0:T(8,128)(2,1)S(1)}, u32[]{:S(2)}, u32[]{:S(2)}) collective-permute-start(bf16[128,1024]{1,0:T(8,128)(2,1)S(1)} %get-tuple-element.60.g_high), channel_id=1, source_target_pairs={{0,1},{1,0},{2,3},{3,2},{4,5},{5,4},{6,7},{7,6},{8,9},{9,8},{10,11... | collective-permute-start | bytes 786440 | tf_op jit(solution)/shard_map/ppermute | solution.py:476
  12.9 1.4 %collective-permute-start.3 = (bf16[4,64,256]{2,1,0:T(8,128)(2,1)S(1)}, bf16[4,64,256]{2,1,0:T(8,128)(2,1)S(1)}, u32[]{:S(2)}, u32[]{:S(2)}) collective-permute-start(bf16[4,64,256]{2,1,0:T(8,128)(2,1)S(1)} %get-tuple-element.61), channel_id=1, source_target_pairs={{0,1},{1,0},{2,3},{3,2},{4,5},{5,4},{6,7},{7,6},{8,9},{9,8},{10,11... | collective-permute-start | bytes 393224 | tf_op jit(solution)/shard_map/ppermute | solution.py:505
  14.8 10.8 %collective-permute-start.6 = (bf16[4,64,256]{2,1,0:T(8,128)(2,1)S(1)}, bf16[4,64,256]{2,1,0:T(8,128)(2,1)S(1)}, u32[]{:S(2)}, u32[]{:S(2)}) collective-permute-start(bf16[4,64,256]{2,1,0:T(8,128)(2,1)S(1)} %get-tuple-element.63), channel_id=1, source_target_pairs={{0,24},{8,16},{16,8},{24,0},{1,25},{9,17},{17,9},{25,1},{2,26},{10... | collective-permute-start | bytes 393224 | tf_op jit(solution)/shard_map/ppermute | solution.py:542
  18.3 7.3 %collective-permute-start.7 = (bf16[4,64,256]{2,1,0:T(8,128)(2,1)S(1)}, bf16[4,64,256]{2,1,0:T(8,128)(2,1)S(1)}, u32[]{:S(2)}, u32[]{:S(2)}) collective-permute-start(bf16[4,64,256]{2,1,0:T(8,128)(2,1)S(1)} %get-tuple-element.64), channel_id=1, source_target_pairs={{0,16},{8,24},{16,0},{24,8},{1,17},{9,25},{17,1},{25,9},{2,18},{10... | collective-permute-start | bytes 393224 | tf_op jit(solution)/shard_map/ppermute | solution.py:542
  18.9 6.8 %collective-permute-start.8 = (bf16[4,64,256]{2,1,0:T(8,128)(2,1)S(1)}, bf16[4,64,256]{2,1,0:T(8,128)(2,1)S(1)}, u32[]{:S(2)}, u32[]{:S(2)}) collective-permute-start(bf16[4,64,256]{2,1,0:T(8,128)(2,1)S(1)} %get-tuple-element.65), channel_id=1, source_target_pairs={{0,8},{8,0},{16,24},{24,16},{1,9},{9,1},{17,25},{25,17},{2,10},{10... | collective-permute-start | bytes 393224 | tf_op jit(solution)/shard_map/ppermute | solution.py:542
  19.9 10.3 %collective-permute-start.10 = (bf16[128,512]{1,0:T(8,128)(2,1)S(1)}, bf16[128,512]{1,0:T(8,128)(2,1)S(1)}, u32[]{:S(2)}, u32[]{:S(2)}) collective-permute-start(bf16[128,512]{1,0:T(8,128)(2,1)S(1)} %get-tuple-element.83), channel_id=1, source_target_pairs={{0,7},{1,2},{2,1},{3,4},{4,3},{5,6},{6,5},{7,0},{8,15},{9,10},{10,... | collective-permute-start | bytes 393224 | tf_op jit(solution)/shard_map/ppermute | solution.py:527
  21.3 8.8 %collective-permute-start.9 = (bf16[128,512]{1,0:T(8,128)(2,1)S(1)}, bf16[128,512]{1,0:T(8,128)(2,1)S(1)}, u32[]{:S(2)}, u32[]{:S(2)}) collective-permute-start(bf16[128,512]{1,0:T(8,128)(2,1)S(1)} %get-tuple-element.82), channel_id=1, source_target_pairs={{0,7},{1,2},{2,1},{3,4},{4,3},{5,6},{6,5},{7,0},{8,15},{9,10},{10,... | collective-permute-start | bytes 393224 | tf_op jit(solution)/shard_map/ppermute | solution.py:527
  25.7 5.8 %collective-permute-start.12 = (bf16[64,256]{1,0:T(8,128)(2,1)S(1)}, bf16[64,256]{1,0:T(8,128)(2,1)S(1)}, u32[]{:S(2)}, u32[]{:S(2)}) collective-permute-start(bf16[64,256]{1,0:T(8,128)(2,1)S(1)} %get-tuple-element.85), channel_id=1, source_target_pairs={{0,6},{1,7},{2,4},{3,5},{4,2},{5,3},{6,0},{7,1},{8,14},{9,15},{10,... | collective-permute-start | bytes 98312 | tf_op jit(solution)/shard_map/ppermute | solution.py:546
  27.5 4.9 %collective-permute-start.13 = (bf16[64,256]{1,0:T(8,128)(2,1)S(1)}, bf16[64,256]{1,0:T(8,128)(2,1)S(1)}, u32[]{:S(2)}, u32[]{:S(2)}) collective-permute-start(bf16[64,256]{1,0:T(8,128)(2,1)S(1)} %get-tuple-element.86), channel_id=1, source_target_pairs={{0,4},{1,5},{2,6},{3,7},{4,0},{5,1},{6,2},{7,3},{8,12},{9,13},{10,... | collective-permute-start | bytes 98312 | tf_op jit(solution)/shard_map/ppermute | solution.py:546
  27.5 4.9 %collective-permute-start.14 = (bf16[64,256]{1,0:T(8,128)(2,1)S(1)}, bf16[64,256]{1,0:T(8,128)(2,1)S(1)}, u32[]{:S(2)}, u32[]{:S(2)}) collective-permute-start(bf16[64,256]{1,0:T(8,128)(2,1)S(1)} %get-tuple-element.87), channel_id=1, source_target_pairs={{0,2},{1,3},{2,0},{3,1},{4,6},{5,7},{6,4},{7,5},{8,10},{9,11},{10,... | collective-permute-start | bytes 98312 | tf_op jit(solution)/shard_map/ppermute | solution.py:546
  30.2 9.5 %collective-permute-start.11 = (bf16[2,128,512]{2,1,0:T(8,128)(2,1)S(1)}, bf16[2,128,512]{2,1,0:T(8,128)(2,1)S(1)}, u32[]{:S(2)}, u32[]{:S(2)}) collective-permute-start(bf16[2,128,512]{2,1,0:T(8,128)(2,1)S(1)} %get-tuple-element.84), channel_id=1, source_target_pairs={{0,1},{1,0},{2,3},{3,2},{4,5},{5,4},{6,7},{7,6},{8,9},{9,8},{10,11... | collective-permute-start | bytes 786440 | tf_op jit(solution)/shard_map/ppermute | solution.py:528
  32.4 5.0 %collective-permute-start.15 = (bf16[64,256]{1,0:T(8,128)(2,1)S(1)}, bf16[64,256]{1,0:T(8,128)(2,1)S(1)}, u32[]{:S(2)}, u32[]{:S(2)}) collective-permute-start(bf16[64,256]{1,0:T(8,128)(2,1)S(1)} %shard_map.111.refs_0_), channel_id=1, source_target_pairs={{0,24},{8,16},{16,8},{24,0},{1,25},{9,17},{17,9},{25,1},{2,26},{10... | collective-permute-start | bytes 98312 | tf_op jit(solution)/shard_map/ppermute | solution.py:554
  35.0 3.9 %collective-permute-start.16 = (bf16[64,256]{1,0:T(8,128)(2,1)S(1)}, bf16[64,256]{1,0:T(8,128)(2,1)S(1)}, u32[]{:S(2)}, u32[]{:S(2)}) collective-permute-start(bf16[64,256]{1,0:T(8,128)(2,1)S(1)} %shard_map.111.refs_0_), channel_id=1, source_target_pairs={{0,16},{8,24},{16,0},{24,8},{1,17},{9,25},{17,1},{25,9},{2,18},{10... | collective-permute-start | bytes 98312 | tf_op jit(solution)/shard_map/ppermute | solution.py:554
  35.7 3.9 %collective-permute-start.17 = (bf16[64,256]{1,0:T(8,128)(2,1)S(1)}, bf16[64,256]{1,0:T(8,128)(2,1)S(1)}, u32[]{:S(2)}, u32[]{:S(2)}) collective-permute-start(bf16[64,256]{1,0:T(8,128)(2,1)S(1)} %shard_map.111.refs_0_), channel_id=1, source_target_pairs={{0,8},{8,0},{16,24},{24,16},{1,9},{9,1},{17,25},{25,17},{2,10},{10... | collective-permute-start | bytes 98312 | tf_op jit(solution)/shard_map/ppermute | solution.py:554

commit v13 on v12

--- a/solution.py
+++ b/solution.py
@@ -253,11 +253,11 @@
 
 def rim_kernel(
     q, link, chip_k, chip_v, grad_t, attn_t, link_exps, chip_exps, rim_factors, before,
-    link_k_back, link_v_back, chip_back, deltas, query_t, dprobs, dscores, rounded,
+    link_back, chip_back, deltas, query_t, dprobs, dscores, rounded,
 ):
     blocks = q.shape[0] // BLK
     sides = (
-        (rim_block(blocks, True)[0], link.at[0], link.at[1], link_exps, link_k_back, link_v_back),
+        (rim_block(blocks, True)[0], link.at[0], link.at[1], link_exps, link_back.at[0], link_back.at[1]),
         (rim_block(blocks, False)[0], chip_k, chip_v, chip_exps, chip_back.at[0], chip_back.at[1]),
     )
     for i, (b, _, rim_v, _, _, _) in enumerate(sides):
@@ -359,12 +359,12 @@
     refs[-1][...] = (total([part[...] for part in refs[:count]]) * scale).astype(BF16)
 
 
-def last_kernel(k_own, v_own, link_k, link_v, chip_kv, *refs):
+def last_kernel(k_own, v_own, link_kv, chip_kv, *refs):
     pieces, (k_grad, v_grad, weight_grad) = refs[:1] + refs[-4:0:-1], refs[-3:]
     tokens = k_own.shape[0]
     first_core = at_core() == 0
-    for i, (own, rim, grad) in enumerate(((k_own, link_k, k_grad), (v_own, link_v, v_grad))):
-        link, chip = rim[...].astype(F32), chip_kv[i].astype(F32)
+    for i, (own, grad) in enumerate(((k_own, k_grad), (v_own, v_grad))):
+        link, chip = link_kv[i].astype(F32), chip_kv[i].astype(F32)
         low = jnp.where(first_core, link, chip)
         high = jnp.where(first_core, chip, link)
         if tokens == RIM:
@@ -514,8 +514,7 @@
     *back, deltas, rim_t = call(
         rim_kernel,
         [
-            rim,
-            rim,
+            vmem(2, RIM, feats),
             vmem(2, RIM, feats),
             vmem(blocks, PAIRS, 2 * BLK, dtype=F32),
             vmem(blocks, feats, BLK, dtype=F32),
@@ -524,8 +523,8 @@
         q, link, chip_k, chip_v, grad_t, attn_t, link_exps, chip_exps, rim_factors, after,
         scratch=[vmem(2, *rim_scores, dtype=F32), vmem(2, *rim_scores), vmem(2, *rim_scores)],
     )
-    link_back = [lax.ppermute(x, "ctx", over_links(ctx)) for x in back[:2]]
-    chip_back = lax.ppermute(back[2], "ctx", swap(ctx, 1))
+    link_back = lax.ppermute(back[0], "ctx", over_links(ctx))
+    chip_back = lax.ppermute(back[1], "ctx", swap(ctx, 1))
     q_grad, k_own, v_own, after = call(
         own_backward_kernel,
         [
@@ -534,7 +533,7 @@
             vmem(tokens, feats, dtype=F32),
             vmem(8, 128, dtype=F32),
         ],
-        10**6,
+        5 * 10**9,
         q, k, v, grad_t, own_exps, own_factors, deltas, rim_t,
         scratch=[vmem(*own_scores, dtype=F32), vmem(*own_scores), vmem(*own_scores)],
     )
@@ -549,14 +548,14 @@
         functools.partial(piece_kernel, (dp * tokens * ctx) ** (-0.5), chips),
         [vmem(rows, cols)],
         10**6,
-        *quarters, *link_back,
+        *quarters, link_back,
     )
     pieces = [piece] + [lax.ppermute(piece, "dp", swap(dp, s)) for s in range(dp - 1, 0, -1)]
     k_grad, v_grad, weight_grad = call(
         last_kernel,
         [hbm(tokens, feats), hbm(tokens, feats), hbm(rows, width, dtype=F32)],
         10**6,
-        k_own, v_own, *link_back, chip_back, *pieces,
+        k_own, v_own, link_back, chip_back, *pieces,
     )
     return (output[None], q_grad[None], k_grad[None], v_grad[None], weight_grad)
 

time: 40.8 us -> 40.4 us (level)
  starting transfers between devices: 21.5 us -> 19.4 us
  waiting for transfers between devices: 6.03 us -> 7.8 us
    ppermute x3 -> x2, starting transfers between devices: 3.61 us -> 1.45 us  [the longest x1 1.45 us: body(): link_back = lax.ppermute(back[0], 'ctx', over_links(ctx))]
    ppermute x3, waiting for transfers between devices: 0.01 us -> 1.76 us  [body(): lax.ppermute(halves[s], 'dp', swap(dp, s))]
  transfers between devices with their start and end apart: 18 -> 17, of which waited for: 7 -> 9; matrix products, arithmetic and copies ran while one was open for 2% -> 3% of each run, Pallas kernels for 22% -> 22%
where the time goes in v13:
time: 40.4 us; the launch traced here: 40.2 us
  starting transfers between devices  19.4 us (48%)
  Pallas kernels  11.3 us (28%)
  waiting for transfers between devices  7.8 us (19%)
  other arithmetic  0.75 us (2%)
  between operations  0.73 us (2%)
    pallas_call x10, Pallas kernels, call(): pl.pallas_call(kernel, out_shape=outs, in_specs=[in_vmem] * len(args), ou...  7.17 us
    ppermute x1, starting transfers between devices, body(): link = lax.ppermute(to_link, 'ctx', over_links(ctx))  4.55 us
    ppermute x3, starting transfers between devices, body(): lax.ppermute(quarters[s], 'ctx', swap(ctx, 2 * s))  4.45 us
    ppermute x3, starting transfers between devices, body(): lax.ppermute(halves[s], 'dp', swap(dp, s))  4.22 us
    pallas_call x2, Pallas kernels, call_on_hbm(): pl.pallas_call(kernel, out_shape=outs, in_specs=[pl.BlockSpec(memory_spac...  4.15 us
    ppermute x3, starting transfers between devices, body(): lax.ppermute(piece, 'dp', swap(dp, s))  3.55 us
    ppermute x3, waiting for transfers between devices, body(): lax.ppermute(quarters[s], 'ctx', swap(ctx, 2 * s))  2.5 us
    ppermute x3, waiting for transfers between devices, body(): lax.ppermute(piece, 'dp', swap(dp, s))  2.12 us
  transfers between devices with their start and end apart: 17, of which 9 were waited for; matrix products, arithmetic and copies ran while one was open for 3% of the time, Pallas kernels for 22%

profile of v13, /device:TPU:0, one launch (start us, length us, event | category | flops | bytes accessed | tf_op | source)
XLA Modules:
  0.0 40.2 jit_solution(12166110891417699694)
XLA Ops:
  0.6 1.1 %shard_map.102 = (bf16[2,128,512]{2,1,0:T(8,128)(2,1)S(1)}, bf16[128,512]{1,0:T(8,128)(2,1)S(1)}, bf16[128,512]{1,0:T(8,128)(2,1)S(1)}) custom-call(bf16[256,512]{1,0:T(8,128)(2,1)} %bitcast.8, bf16[256,512]{1,0:T(8,128)(2,1)} %bitcast.10), custom_call_target="tpu_custom_call" | custom-call | flops 1000000 | bytes 4096 | tf_op jit(solution)/shard_map/pallas_call | solution.py:408
  1.8 4.6 %collective-permute-start = (bf16[2,128,512]{2,1,0:T(8,128)(2,1)S(1)}, bf16[2,128,512]{2,1,0:T(8,128)(2,1)S(1)}, u32[]{:S(2)}, u32[]{:S(2)}) collective-permute-start(bf16[2,128,512]{2,1,0:T(8,128)(2,1)S(1)} %get-tuple-element.48), channel_id=1, source_target_pairs={{0,7},{1,2},{2,1},{3,4},{4,3},{5,6},{6,5},{7,0},{8,15},{9,10},{10,... | collective-permute-start | bytes 786440 | tf_op jit(solution)/shard_map/ppermute | solution.py:449
  6.3 0.0 collective-permute-start.1
  6.3 0.5 %collective-permute-start.2 = (bf16[128,512]{1,0:T(8,128)(2,1)S(1)}, bf16[128,512]{1,0:T(8,128)(2,1)S(1)}, u32[]{:S(2)}, u32[]{:S(2)}) collective-permute-start(bf16[128,512]{1,0:T(8,128)(2,1)S(1)} %get-tuple-element.52), channel_id=1, source_target_pairs={{0,1},{1,0},{2,3},{3,2},{4,5},{5,4},{6,7},{7,6},{8,9},{9,8},{10,11... | collective-permute-start | bytes 393224 | tf_op jit(solution)/shard_map/ppermute | solution.py:450
  6.8 0.8 %compare_select_fusion = f32[1,2,3]{1,0,2:T(1,128)S(1)} fusion(s32[1,16,3]{1,0,2:T(1,128)} %param.11, s32[]{:T(128)S(6)} %select_n.14), kind=kLoop, calls=%fused_computation | loop fusion | flops 12 | bytes 52 | tf_op jit(solution)/shard_map/jit(_where)/select_n | solution.py:452
  7.6 0.1 copy.11
  7.7 0.1 select_n.16
  7.8 0.1 broadcast_in_dim.27.bias
  7.9 3.0 %shard_map.101 = (bf16[256,512]{1,0:T(8,128)(2,1)S(1)}, bf16[256,512]{1,0:T(8,128)(2,1)S(1)}, bf16[256,512]{1,0:T(8,128)(2,1)S(1)}, bf16[128,1024]{1,0:T(8,128)(...) custom-call(f32[6,1,256]{2,1,0:T(1,128)S(1)} %broadcast_in_dim.27.bi, ...), custom_call_target="tpu_custom_call" | custom-call | flops 1000000 | bytes 4096 | tf_op jit(solution)/shard_map/pallas_call | solution.py:408
  10.9 0.1 collective-permute-start.4
  10.9 0.5 %collective-permute-start.5 = (bf16[128,1024]{1,0:T(8,128)(2,1)S(1)}, bf16[128,1024]{1,0:T(8,128)(2,1)S(1)}, u32[]{:S(2)}, u32[]{:S(2)}) collective-permute-start(bf16[128,1024]{1,0:T(8,128)(2,1)S(1)} %get-tuple-element.59.g_high), channel_id=1, source_target_pairs={{0,1},{1,0},{2,3},{3,2},{4,5},{5,4},{6,7},{7,6},{8,9},{9,8},{10,11... | collective-permute-start | bytes 786440 | tf_op jit(solution)/shard_map/ppermute | solution.py:476
  11.4 0.0 collective-permute-done.1.rim_k.chip_k
  11.4 0.0 collective-permute-done.2.rim_v.chip_v
  11.4 0.5 %shard_map.103 = (f32[512,128]{1,0:T(8,128)S(1)}, f32[2,4,256]{2,1,0:T(4,128)S(1)}, f32[4,128,256]{2,1,0:T(8,128)S(1)}) custom-call(f32[6,1,256]{2,1,0:T(1,128)S(1)} %broadcast_in_dim.27.bias, bf16[256,512]{1,0:T(8,128)(2,1)S(1)} %get-tuple-element.47.q, bf16[128,512]{1,0:T(8,128)(2,1)S(1)} %collective-permute-done.1.rim_k.chip_k, ...), custom_call_target="tpu_custom_call" | custom-call | flops 1000000 | bytes 4000 | tf_op jit(solution)/shard_map/pallas_call | solution.py:396
  12.0 0.4 collective-permute-done.rim.link
  12.4 0.6 %shard_map.104 = (bf16[2,512,128]{2,1,0:T(8,128)(2,1)S(1)}, bf16[4,64,256]{2,1,0:T(8,128)(2,1)S(1)}, bf16[4,64,256]{2,1,0:T(8,128)(2,1)S(1)}, f32[4,128,256]{2,1...) custom-call(f32[6,1,256]{2,1,0:T(1,128)S(1)} %broadcast_in_dim.27.bias, ...), custom_call_target="tpu_custom_call" | custom-call | flops 1000000 | bytes 4000 | tf_op jit(solution)/shard_map/pallas_call | solution.py:396
  12.9 0.1 collective-permute-start.3
  13.0 0.3 shard_map.105.product
  13.3 0.0 collective-permute-done.4.g_low
  13.3 0.0 collective-permute-done.5.g_high
  13.3 1.0 %collective-permute-done.3.other = bf16[4,64,256]{2,1,0:T(8,128)(2,1)S(1)} collective-permute-done((bf16[4,64,256]{2,1,0:T(8,128)(2,1)S(1)}, bf16[4,64,256]{2,1,0:T(8,128)(2,1)S(1)}, u32[]{:S(2)}, u32[]{:S(2)}) %collective-permute-start.3) | collective-permute-done | bytes 131104 | tf_op jit(solution)/shard_map/ppermute | solution.py:505
  14.3 0.4 %shard_map.106 = (bf16[4,64,256]{2,1,0:T(8,128)(2,1)S(1)}, bf16[4,64,256]{2,1,0:T(8,128)(2,1)S(1)}, bf16[4,64,256]{2,1,0:T(8,128)(2,1)S(1)}, bf16[4,64,256]{2,1,0:T(8,128)(2,1)S(1)}, f32[8,128]{1,0:T(8,128)S(1)}) custom-call(f32[256,1024]{1,0:T(8,128)S(1)} %shard_map.105.product, bf16[4,64,256]{2,1,0:T(8,128)(2,1)S(1)} %collective-permute-done.3.other, ...), custom_call_target="tpu_custom_call" | custom-call | flops 1000000 | bytes 4000 | tf_op jit(solution)/shard_map/pallas_call | solution.py:396
  14.8 3.6 %collective-permute-start.6 = (bf16[4,64,256]{2,1,0:T(8,128)(2,1)S(1)}, bf16[4,64,256]{2,1,0:T(8,128)(2,1)S(1)}, u32[]{:S(2)}, u32[]{:S(2)}) collective-permute-start(bf16[4,64,256]{2,1,0:T(8,128)(2,1)S(1)} %get-tuple-element.62), channel_id=1, source_target_pairs={{0,24},{8,16},{16,8},{24,0},{1,25},{9,17},{17,9},{25,1},{2,26},{10... | collective-permute-start | bytes 393224 | tf_op jit(solution)/shard_map/ppermute | solution.py:541
  18.3 0.5 %collective-permute-start.7 = (bf16[4,64,256]{2,1,0:T(8,128)(2,1)S(1)}, bf16[4,64,256]{2,1,0:T(8,128)(2,1)S(1)}, u32[]{:S(2)}, u32[]{:S(2)}) collective-permute-start(bf16[4,64,256]{2,1,0:T(8,128)(2,1)S(1)} %get-tuple-element.63), channel_id=1, source_target_pairs={{0,16},{8,24},{16,0},{24,8},{1,17},{9,25},{17,1},{25,9},{2,18},{10... | collective-permute-start | bytes 393224 | tf_op jit(solution)/shard_map/ppermute | solution.py:541
  18.9 0.1 collective-permute-start.8
  19.0 0.9 %shard_map.107 = (bf16[2,128,512]{2,1,0:T(8,128)(2,1)S(1)}, bf16[2,128,512]{2,1,0:T(8,128)(2,1)S(1)}, f32[2,4,256]{2,1,0:T(4,128)S(1)}, f32[2,512,128]{2,1,0:T(8,128)S(1)}) custom-call(bf16[256,512]{1,0:T(8,128)(2,1)S(1)} %get-tuple-element.47.q, bf16[2,128,512]{2,1,0:T(8,128)(2,1)S(1)} %collective-permute-done.rim.link, ...), custom_call_target="tpu_custom_call" | custom-call | flops 1000000 | bytes 4000 | tf_op jit(solution)/shard_map/pallas_call | solution.py:396
  19.9 1.5 %collective-permute-start.9 = (bf16[2,128,512]{2,1,0:T(8,128)(2,1)S(1)}, bf16[2,128,512]{2,1,0:T(8,128)(2,1)S(1)}, u32[]{:S(2)}, u32[]{:S(2)}) collective-permute-start(bf16[2,128,512]{2,1,0:T(8,128)(2,1)S(1)} %get-tuple-element.81), channel_id=1, source_target_pairs={{0,7},{1,2},{2,1},{3,4},{4,3},{5,6},{6,5},{7,0},{8,15},{9,10},{10,... | collective-permute-start | bytes 786440 | tf_op jit(solution)/shard_map/ppermute | solution.py:526
  21.3 2.1 %shard_map.108 = (bf16[256,512]{1,0:T(8,128)(2,1)}, f32[256,512]{1,0:T(8,128)S(1)}, f32[256,512]{1,0:T(8,128)S(1)}, f32[8,128]{1,0:T(8,128)S(1)}) custom-call(bf16[256,512]{1,0:T(8,128)(2,1)S(1)} %get-tuple-element.47.q, bf16[256,512]{1,0:T(8,128)(2,1)S(1)} %get-tuple-element.65.k, bf16[256,512]{1,0:T(8,128)(2,1)S(1)} %get-tuple-element.66.v, ...), custom_call_target="tpu_custom_call" | custom-call | flops 5000000000 | bytes 20000000 | tf_op jit(solution)/shard_map/pallas_call | solution.py:396
  23.5 0.0 collective-permute-done.6.refs_1_
  23.5 1.5 %collective-permute-done.7.refs_2_ = bf16[4,64,256]{2,1,0:T(8,128)(2,1)S(1)} collective-permute-done((bf16[4,64,256]{2,1,0:T(8,128)(2,1)S(1)}, bf16[4,64,256]{2,1,0:T(8,128)(2,1)S(1)}, u32[]{:S(2)}, u32[]{:S(2)}) %collective-permute-start.7) | collective-permute-done | bytes 131104 | tf_op jit(solution)/shard_map/ppermute | solution.py:541
  25.0 0.3 collective-permute-done.8.refs_3_
  25.2 0.1 shard_map.109
  25.3 2.1 %collective-permute-start.11 = (bf16[64,256]{1,0:T(8,128)(2,1)S(1)}, bf16[64,256]{1,0:T(8,128)(2,1)S(1)}, u32[]{:S(2)}, u32[]{:S(2)}) collective-permute-start(bf16[64,256]{1,0:T(8,128)(2,1)S(1)} %get-tuple-element.83), channel_id=1, source_target_pairs={{0,6},{1,7},{2,4},{3,5},{4,2},{5,3},{6,0},{7,1},{8,14},{9,15},{10,... | collective-permute-start | bytes 98312 | tf_op jit(solution)/shard_map/ppermute | solution.py:545
  27.5 0.0 collective-permute-start.12
  27.5 2.3 %collective-permute-start.13 = (bf16[64,256]{1,0:T(8,128)(2,1)S(1)}, bf16[64,256]{1,0:T(8,128)(2,1)S(1)}, u32[]{:S(2)}, u32[]{:S(2)}) collective-permute-start(bf16[64,256]{1,0:T(8,128)(2,1)S(1)} %get-tuple-element.85), channel_id=1, source_target_pairs={{0,2},{1,3},{2,0},{3,1},{4,6},{5,7},{6,4},{7,5},{8,10},{9,11},{10,... | collective-permute-start | bytes 98312 | tf_op jit(solution)/shard_map/ppermute | solution.py:545
  29.8 1.4 %collective-permute-done.11.refs_1_ = bf16[64,256]{1,0:T(8,128)(2,1)S(1)} collective-permute-done((bf16[64,256]{1,0:T(8,128)(2,1)S(1)}, bf16[64,256]{1,0:T(8,128)(2,1)S(1)}, u32[]{:S(2)}, u32[]{:S(2)}) %collective-permute-start.11) | collective-permute-done | bytes 32800 | tf_op jit(solution)/shard_map/ppermute | solution.py:545
  31.2 1.1 %collective-permute-done.12.refs_2_ = bf16[64,256]{1,0:T(8,128)(2,1)S(1)} collective-permute-done((bf16[64,256]{1,0:T(8,128)(2,1)S(1)}, bf16[64,256]{1,0:T(8,128)(2,1)S(1)}, u32[]{:S(2)}, u32[]{:S(2)}) %collective-permute-start.12) | collective-permute-done | bytes 32800 | tf_op jit(solution)/shard_map/ppermute | solution.py:545
  32.3 0.0 collective-permute-done.13.refs_3_
  32.3 0.0 collective-permute-done.9.refs_4_.link_kv
  32.3 1.9 %collective-permute-start.14 = (bf16[64,256]{1,0:T(8,128)(2,1)S(1)}, bf16[64,256]{1,0:T(8,128)(2,1)S(1)}, u32[]{:S(2)}, u32[]{:S(2)}) collective-permute-start(bf16[64,256]{1,0:T(8,128)(2,1)S(1)} %shard_map.111.refs_0_), channel_id=1, source_target_pairs={{0,24},{8,16},{16,8},{24,0},{1,25},{9,17},{17,9},{25,1},{2,26},{10... | collective-permute-start | bytes 98312 | tf_op jit(solution)/shard_map/ppermute | solution.py:553
  34.2 1.1 %collective-permute-start.15 = (bf16[64,256]{1,0:T(8,128)(2,1)S(1)}, bf16[64,256]{1,0:T(8,128)(2,1)S(1)}, u32[]{:S(2)}, u32[]{:S(2)}) collective-permute-start(bf16[64,256]{1,0:T(8,128)(2,1)S(1)} %shard_map.111.refs_0_), channel_id=1, source_target_pairs={{0,16},{8,24},{16,0},{24,8},{1,17},{9,25},{17,1},{25,9},{2,18},{10... | collective-permute-start | bytes 98312 | tf_op jit(solution)/shard_map/ppermute | solution.py:553
  35.3 0.5 %collective-permute-start.16 = (bf16[64,256]{1,0:T(8,128)(2,1)S(1)}, bf16[64,256]{1,0:T(8,128)(2,1)S(1)}, u32[]{:S(2)}, u32[]{:S(2)}) collective-permute-start(bf16[64,256]{1,0:T(8,128)(2,1)S(1)} %shard_map.111.refs_0_), channel_id=1, source_target_pairs={{0,8},{8,0},{16,24},{24,16},{1,9},{9,1},{17,25},{25,17},{2,10},{10... | collective-permute-start | bytes 98312 | tf_op jit(solution)/shard_map/ppermute | solution.py:553
  35.9 1.3 %shard_map.110 = bf16[256,1024]{1,0:T(8,128)(2,1)} custom-call(bf16[2,512,128]{2,1,0:T(8,128)(2,1)S(1)} %get-tuple-element.55.attn_t, bf16[512,1024]{1,0:T(8,128)(2,1)S(1)} %get-tuple-element.56.w_out, bf16[64,256]{1,0:T(8,128)(2,1)S(1)} %get-tuple-element.77.before.refs_0_), custom_call_target="tpu_custom_call" | custom-call | flops 5000000000 | bytes 20000000 | tf_op jit(solution)/shard_map/pallas_call | solution.py:396
  37.1 0.0 collective-permute-done.10.chip_kv
  37.1 0.1 collective-permute-done.14.refs_1_
  37.2 0.9 %collective-permute-done.15.refs_2_ = bf16[64,256]{1,0:T(8,128)(2,1)S(1)} collective-permute-done((bf16[64,256]{1,0:T(8,128)(2,1)S(1)}, bf16[64,256]{1,0:T(8,128)(2,1)S(1)}, u32[]{:S(2)}, u32[]{:S(2)}) %collective-permute-start.15) | collective-permute-done | bytes 32800 | tf_op jit(solution)/shard_map/ppermute | solution.py:553
  38.2 1.1 %collective-permute-done.16.refs_3_ = bf16[64,256]{1,0:T(8,128)(2,1)S(1)} collective-permute-done((bf16[64,256]{1,0:T(8,128)(2,1)S(1)}, bf16[64,256]{1,0:T(8,128)(2,1)S(1)}, u32[]{:S(2)}, u32[]{:S(2)}) %collective-permute-start.16) | collective-permute-done | bytes 32800 | tf_op jit(solution)/shard_map/ppermute | solution.py:553
  39.3 1.0 %shard_map.112 = (bf16[256,512]{1,0:T(8,128)(2,1)}, bf16[256,512]{1,0:T(8,128)(2,1)}, f32[64,1024]{1,0:T(8,128)}) custom-call(f32[256,512]{1,0:T(8,128)S(1)} %get-tuple-element.79.k_own, f32[256,512]{1,0:T(8,128)S(1)} %get-tuple-element.80.v_own, bf16[2,128,512]{2,1,0:T(8,128)(2,1)S(1)} %collective-permute-done.9.refs_4_.link_kv, ...), custom_call_target="tpu_custom_call" | custom-call | flops 1000000 | bytes 4000 | tf_op jit(solution)/shard_map/pallas_call | solution.py:396
  (2 shorter events, 0.0 us)
Async XLA Ops:
  1.8 10.6 %collective-permute-start = (bf16[2,128,512]{2,1,0:T(8,128)(2,1)S(1)}, bf16[2,128,512]{2,1,0:T(8,128)(2,1)S(1)}, u32[]{:S(2)}, u32[]{:S(2)}) collective-permute-start(bf16[2,128,512]{2,1,0:T(8,128)(2,1)S(1)} %get-tuple-element.48), channel_id=1, source_target_pairs={{0,7},{1,2},{2,1},{3,4},{4,3},{5,6},{6,5},{7,0},{8,15},{9,10},{10,... | collective-permute-start | bytes 786440 | tf_op jit(solution)/shard_map/ppermute | solution.py:449
  6.3 5.1 %collective-permute-start.1 = (bf16[128,512]{1,0:T(8,128)(2,1)S(1)}, bf16[128,512]{1,0:T(8,128)(2,1)S(1)}, u32[]{:S(2)}, u32[]{:S(2)}) collective-permute-start(bf16[128,512]{1,0:T(8,128)(2,1)S(1)} %get-tuple-element.51), channel_id=1, source_target_pairs={{0,1},{1,0},{2,3},{3,2},{4,5},{5,4},{6,7},{7,6},{8,9},{9,8},{10,11... | collective-permute-start | bytes 393224 | tf_op jit(solution)/shard_map/ppermute | solution.py:450
  6.3 5.1 %collective-permute-start.2 = (bf16[128,512]{1,0:T(8,128)(2,1)S(1)}, bf16[128,512]{1,0:T(8,128)(2,1)S(1)}, u32[]{:S(2)}, u32[]{:S(2)}) collective-permute-start(bf16[128,512]{1,0:T(8,128)(2,1)S(1)} %get-tuple-element.52), channel_id=1, source_target_pairs={{0,1},{1,0},{2,3},{3,2},{4,5},{5,4},{6,7},{7,6},{8,9},{9,8},{10,11... | collective-permute-start | bytes 393224 | tf_op jit(solution)/shard_map/ppermute | solution.py:450
  10.9 2.5 %collective-permute-start.4 = (bf16[128,1024]{1,0:T(8,128)(2,1)S(1)}, bf16[128,1024]{1,0:T(8,128)(2,1)S(1)}, u32[]{:S(2)}, u32[]{:S(2)}) collective-permute-start(bf16[128,1024]{1,0:T(8,128)(2,1)S(1)} %get-tuple-element.58.g_low), channel_id=1, source_target_pairs={{0,1},{1,0},{2,3},{3,2},{4,5},{5,4},{6,7},{7,6},{8,9},{9,8},{10,11... | collective-permute-start | bytes 786440 | tf_op jit(solution)/shard_map/ppermute | solution.py:476
  10.9 2.4 %collective-permute-start.5 = (bf16[128,1024]{1,0:T(8,128)(2,1)S(1)}, bf16[128,1024]{1,0:T(8,128)(2,1)S(1)}, u32[]{:S(2)}, u32[]{:S(2)}) collective-permute-start(bf16[128,1024]{1,0:T(8,128)(2,1)S(1)} %get-tuple-element.59.g_high), channel_id=1, source_target_pairs={{0,1},{1,0},{2,3},{3,2},{4,5},{5,4},{6,7},{7,6},{8,9},{9,8},{10,11... | collective-permute-start | bytes 786440 | tf_op jit(solution)/shard_map/ppermute | solution.py:476
  12.9 1.4 %collective-permute-start.3 = (bf16[4,64,256]{2,1,0:T(8,128)(2,1)S(1)}, bf16[4,64,256]{2,1,0:T(8,128)(2,1)S(1)}, u32[]{:S(2)}, u32[]{:S(2)}) collective-permute-start(bf16[4,64,256]{2,1,0:T(8,128)(2,1)S(1)} %get-tuple-element.60), channel_id=1, source_target_pairs={{0,1},{1,0},{2,3},{3,2},{4,5},{5,4},{6,7},{7,6},{8,9},{9,8},{10,11... | collective-permute-start | bytes 393224 | tf_op jit(solution)/shard_map/ppermute | solution.py:505
  14.8 8.7 %collective-permute-start.6 = (bf16[4,64,256]{2,1,0:T(8,128)(2,1)S(1)}, bf16[4,64,256]{2,1,0:T(8,128)(2,1)S(1)}, u32[]{:S(2)}, u32[]{:S(2)}) collective-permute-start(bf16[4,64,256]{2,1,0:T(8,128)(2,1)S(1)} %get-tuple-element.62), channel_id=1, source_target_pairs={{0,24},{8,16},{16,8},{24,0},{1,25},{9,17},{17,9},{25,1},{2,26},{10... | collective-permute-start | bytes 393224 | tf_op jit(solution)/shard_map/ppermute | solution.py:541
  18.3 6.6 %collective-permute-start.7 = (bf16[4,64,256]{2,1,0:T(8,128)(2,1)S(1)}, bf16[4,64,256]{2,1,0:T(8,128)(2,1)S(1)}, u32[]{:S(2)}, u32[]{:S(2)}) collective-permute-start(bf16[4,64,256]{2,1,0:T(8,128)(2,1)S(1)} %get-tuple-element.63), channel_id=1, source_target_pairs={{0,16},{8,24},{16,0},{24,8},{1,17},{9,25},{17,1},{25,9},{2,18},{10... | collective-permute-start | bytes 393224 | tf_op jit(solution)/shard_map/ppermute | solution.py:541
  18.9 6.4 %collective-permute-start.8 = (bf16[4,64,256]{2,1,0:T(8,128)(2,1)S(1)}, bf16[4,64,256]{2,1,0:T(8,128)(2,1)S(1)}, u32[]{:S(2)}, u32[]{:S(2)}) collective-permute-start(bf16[4,64,256]{2,1,0:T(8,128)(2,1)S(1)} %get-tuple-element.64), channel_id=1, source_target_pairs={{0,8},{8,0},{16,24},{24,16},{1,9},{9,1},{17,25},{25,17},{2,10},{10... | collective-permute-start | bytes 393224 | tf_op jit(solution)/shard_map/ppermute | solution.py:541
  19.9 12.4 %collective-permute-start.9 = (bf16[2,128,512]{2,1,0:T(8,128)(2,1)S(1)}, bf16[2,128,512]{2,1,0:T(8,128)(2,1)S(1)}, u32[]{:S(2)}, u32[]{:S(2)}) collective-permute-start(bf16[2,128,512]{2,1,0:T(8,128)(2,1)S(1)} %get-tuple-element.81), channel_id=1, source_target_pairs={{0,7},{1,2},{2,1},{3,4},{4,3},{5,6},{6,5},{7,0},{8,15},{9,10},{10,... | collective-permute-start | bytes 786440 | tf_op jit(solution)/shard_map/ppermute | solution.py:526
  25.3 5.9 %collective-permute-start.11 = (bf16[64,256]{1,0:T(8,128)(2,1)S(1)}, bf16[64,256]{1,0:T(8,128)(2,1)S(1)}, u32[]{:S(2)}, u32[]{:S(2)}) collective-permute-start(bf16[64,256]{1,0:T(8,128)(2,1)S(1)} %get-tuple-element.83), channel_id=1, source_target_pairs={{0,6},{1,7},{2,4},{3,5},{4,2},{5,3},{6,0},{7,1},{8,14},{9,15},{10,... | collective-permute-start | bytes 98312 | tf_op jit(solution)/shard_map/ppermute | solution.py:545
  27.5 4.8 %collective-permute-start.12 = (bf16[64,256]{1,0:T(8,128)(2,1)S(1)}, bf16[64,256]{1,0:T(8,128)(2,1)S(1)}, u32[]{:S(2)}, u32[]{:S(2)}) collective-permute-start(bf16[64,256]{1,0:T(8,128)(2,1)S(1)} %get-tuple-element.84), channel_id=1, source_target_pairs={{0,4},{1,5},{2,6},{3,7},{4,0},{5,1},{6,2},{7,3},{8,12},{9,13},{10,... | collective-permute-start | bytes 98312 | tf_op jit(solution)/shard_map/ppermute | solution.py:545
  27.5 4.8 %collective-permute-start.13 = (bf16[64,256]{1,0:T(8,128)(2,1)S(1)}, bf16[64,256]{1,0:T(8,128)(2,1)S(1)}, u32[]{:S(2)}, u32[]{:S(2)}) collective-permute-start(bf16[64,256]{1,0:T(8,128)(2,1)S(1)} %get-tuple-element.85), channel_id=1, source_target_pairs={{0,2},{1,3},{2,0},{3,1},{4,6},{5,7},{6,4},{7,5},{8,10},{9,11},{10,... | collective-permute-start | bytes 98312 | tf_op jit(solution)/shard_map/ppermute | solution.py:545
  29.8 7.4 %collective-permute-start.10 = (bf16[2,128,512]{2,1,0:T(8,128)(2,1)S(1)}, bf16[2,128,512]{2,1,0:T(8,128)(2,1)S(1)}, u32[]{:S(2)}, u32[]{:S(2)}) collective-permute-start(bf16[2,128,512]{2,1,0:T(8,128)(2,1)S(1)} %get-tuple-element.82), channel_id=1, source_target_pairs={{0,1},{1,0},{2,3},{3,2},{4,5},{5,4},{6,7},{7,6},{8,9},{9,8},{10,11... | collective-permute-start | bytes 786440 | tf_op jit(solution)/shard_map/ppermute | solution.py:527
  32.3 4.9 %collective-permute-start.14 = (bf16[64,256]{1,0:T(8,128)(2,1)S(1)}, bf16[64,256]{1,0:T(8,128)(2,1)S(1)}, u32[]{:S(2)}, u32[]{:S(2)}) collective-permute-start(bf16[64,256]{1,0:T(8,128)(2,1)S(1)} %shard_map.111.refs_0_), channel_id=1, source_target_pairs={{0,24},{8,16},{16,8},{24,0},{1,25},{9,17},{17,9},{25,1},{2,26},{10... | collective-permute-start | bytes 98312 | tf_op jit(solution)/shard_map/ppermute | solution.py:553
  34.2 3.9 %collective-permute-start.15 = (bf16[64,256]{1,0:T(8,128)(2,1)S(1)}, bf16[64,256]{1,0:T(8,128)(2,1)S(1)}, u32[]{:S(2)}, u32[]{:S(2)}) collective-permute-start(bf16[64,256]{1,0:T(8,128)(2,1)S(1)} %shard_map.111.refs_0_), channel_id=1, source_target_pairs={{0,16},{8,24},{16,0},{24,8},{1,17},{9,25},{17,1},{25,9},{2,18},{10... | collective-permute-start | bytes 98312 | tf_op jit(solution)/shard_map/ppermute | solution.py:553
  35.3 3.9 %collective-permute-start.16 = (bf16[64,256]{1,0:T(8,128)(2,1)S(1)}, bf16[64,256]{1,0:T(8,128)(2,1)S(1)}, u32[]{:S(2)}, u32[]{:S(2)}) collective-permute-start(bf16[64,256]{1,0:T(8,128)(2,1)S(1)} %shard_map.111.refs_0_), channel_id=1, source_target_pairs={{0,8},{8,0},{16,24},{24,16},{1,9},{9,1},{17,25},{25,17},{2,10},{10... | collective-permute-start | bytes 98312 | tf_op jit(solution)/shard_map/ppermute | solution.py:553

commit v14 on v13

--- a/solution.py
+++ b/solution.py
@@ -336,14 +336,22 @@
     pieces, after = outs[:-1], outs[-1]
     at_dp = lax.axis_index("dp")
     chips, rows, cols = pieces[0].shape
-    both = (product[...] + flat_dot(other, g_low, g_high)).astype(BF16)
-    for d in range(len(pieces)):
-        value = both[:, d * cols : (d + 1) * cols].reshape(chips, rows, cols)
+    if cols % BLK == 0:
+        flat = other[...].reshape(chips * rows, other.shape[2])
         for s in range(len(pieces)):
-
-            @pl.when((at_dp ^ s) == d)
-            def _(s=s, value=value):
-                pieces[s][...] = value
+            at = pl.ds(pl.multiple_of((at_dp ^ s) * cols, BLK), cols)
+            g = jnp.concatenate([g_low[:, at], g_high[:, at]], axis=0)
+            value = product[:, at] + dot(flat, g, ((1,), (0,)))
+            pieces[s][...] = value.astype(BF16).reshape(chips, rows, cols)
+    else:
+        both = (product[...] + flat_dot(other, g_low, g_high)).astype(BF16)
+        for d in range(len(pieces)):
+            value = both[:, d * cols : (d + 1) * cols].reshape(chips, rows, cols)
+            for s in range(len(pieces)):
+
+                @pl.when((at_dp ^ s) == d)
+                def _(s=s, value=value):
+                    pieces[s][...] = value
 
     after[...] = jnp.zeros_like(after)
 
@@ -359,8 +367,7 @@
     refs[-1][...] = (total([part[...] for part in refs[:count]]) * scale).astype(BF16)
 
 
-def last_kernel(k_own, v_own, link_kv, chip_kv, *refs):
-    pieces, (k_grad, v_grad, weight_grad) = refs[:1] + refs[-4:0:-1], refs[-3:]
+def rim_sum_kernel(k_own, v_own, link_kv, chip_kv, k_grad, v_grad):
     tokens = k_own.shape[0]
     first_core = at_core() == 0
     for i, (own, grad) in enumerate(((k_own, k_grad), (v_own, v_grad))):
@@ -374,6 +381,10 @@
             if tokens > 2 * RIM:
                 grad[RIM : tokens - RIM] = own[RIM : tokens - RIM].astype(BF16)
             grad[tokens - RIM :] = (own[tokens - RIM :] + high).astype(BF16)
+
+
+def columns_kernel(*refs):
+    pieces, weight_grad = refs[:1] + refs[-2:0:-1], refs[-1]
     at_dp = lax.axis_index("dp")
     cols = pieces[0].shape[1]
     for d in range(len(pieces)):
@@ -551,12 +562,10 @@
         *quarters, link_back,
     )
     pieces = [piece] + [lax.ppermute(piece, "dp", swap(dp, s)) for s in range(dp - 1, 0, -1)]
-    k_grad, v_grad, weight_grad = call(
-        last_kernel,
-        [hbm(tokens, feats), hbm(tokens, feats), hbm(rows, width, dtype=F32)],
-        10**6,
-        k_own, v_own, link_back, chip_back, *pieces,
-    )
+    k_grad, v_grad = call(
+        rim_sum_kernel, [hbm(tokens, feats)] * 2, 10**6, k_own, v_own, link_back, chip_back
+    )
+    (weight_grad,) = call(columns_kernel, [hbm(rows, width, dtype=F32)], 10**6, *pieces)
     return (output[None], q_grad[None], k_grad[None], v_grad[None], weight_grad)
 
 

time: 40.4 us -> 40.1 us (level)
  waiting for transfers between devices: 7.8 us -> 6.92 us
  Pallas kernels: 11.3 us -> 11.8 us
    ppermute x3, waiting for transfers between devices: 2.12 us -> 1.24 us  [body(): lax.ppermute(piece, 'dp', swap(dp, s))]
    pallas_call x10 -> x11, Pallas kernels: 7.17 us -> 7.7 us  [call(): pl.pallas_call(kernel, out_shape=outs, in_specs=[in_vmem] * len(args), ou...]
  transfers between devices with their start and end apart: 17 -> 17, of which waited for: 9 -> 8; matrix products, arithmetic and copies ran while one was open for 3% -> 3% of each run, Pallas kernels for 22% -> 24%
where the time goes in v14:
time: 40.1 us; the launch traced here: 39.9 us
  starting transfers between devices  19.4 us (48%)
  Pallas kernels  11.8 us (29%)
  waiting for transfers between devices  6.92 us (17%)
  other arithmetic  0.75 us (2%)
  between operations  0.73 us (2%)
    pallas_call x11, Pallas kernels, call(): pl.pallas_call(kernel, out_shape=outs, in_specs=[in_vmem] * len(args), ou...  7.7 us
    ppermute x1, starting transfers between devices, body(): link = lax.ppermute(to_link, 'ctx', over_links(ctx))  4.55 us
    ppermute x3, starting transfers between devices, body(): lax.ppermute(quarters[s], 'ctx', swap(ctx, 2 * s))  4.45 us
    ppermute x3, starting transfers between devices, body(): lax.ppermute(halves[s], 'dp', swap(dp, s))  4.22 us
    pallas_call x2, Pallas kernels, call_on_hbm(): pl.pallas_call(kernel, out_shape=outs, in_specs=[pl.BlockSpec(memory_spac...  4.15 us
    ppermute x3, starting transfers between devices, body(): lax.ppermute(piece, 'dp', swap(dp, s))  3.55 us
    ppermute x3, waiting for transfers between devices, body(): lax.ppermute(quarters[s], 'ctx', swap(ctx, 2 * s))  2.5 us
    ppermute x3, waiting for transfers between devices, body(): lax.ppermute(halves[s], 'dp', swap(dp, s))  1.78 us
  transfers between devices with their start and end apart: 17, of which 8 were waited for; matrix products, arithmetic and copies ran while one was open for 3% of the time, Pallas kernels for 24%

profile of v14, /device:TPU:0, one launch (start us, length us, event | category | flops | bytes accessed | tf_op | source)
XLA Modules:
  0.0 39.9 jit_solution(15501496839933787341)
XLA Ops:
  0.6 1.1 %shard_map.102 = (bf16[2,128,512]{2,1,0:T(8,128)(2,1)S(1)}, bf16[128,512]{1,0:T(8,128)(2,1)S(1)}, bf16[128,512]{1,0:T(8,128)(2,1)S(1)}) custom-call(bf16[256,512]{1,0:T(8,128)(2,1)} %bitcast.8, bf16[256,512]{1,0:T(8,128)(2,1)} %bitcast.10), custom_call_target="tpu_custom_call" | custom-call | flops 1000000 | bytes 4096 | tf_op jit(solution)/shard_map/pallas_call | solution.py:419
  1.8 4.6 %collective-permute-start = (bf16[2,128,512]{2,1,0:T(8,128)(2,1)S(1)}, bf16[2,128,512]{2,1,0:T(8,128)(2,1)S(1)}, u32[]{:S(2)}, u32[]{:S(2)}) collective-permute-start(bf16[2,128,512]{2,1,0:T(8,128)(2,1)S(1)} %get-tuple-element.47), channel_id=1, source_target_pairs={{0,7},{1,2},{2,1},{3,4},{4,3},{5,6},{6,5},{7,0},{8,15},{9,10},{10,... | collective-permute-start | bytes 786440 | tf_op jit(solution)/shard_map/ppermute | solution.py:460
  6.3 0.0 collective-permute-start.1
  6.3 0.5 %collective-permute-start.2 = (bf16[128,512]{1,0:T(8,128)(2,1)S(1)}, bf16[128,512]{1,0:T(8,128)(2,1)S(1)}, u32[]{:S(2)}, u32[]{:S(2)}) collective-permute-start(bf16[128,512]{1,0:T(8,128)(2,1)S(1)} %get-tuple-element.51), channel_id=1, source_target_pairs={{0,1},{1,0},{2,3},{3,2},{4,5},{5,4},{6,7},{7,6},{8,9},{9,8},{10,11... | collective-permute-start | bytes 393224 | tf_op jit(solution)/shard_map/ppermute | solution.py:461
  6.8 0.8 %compare_select_fusion = f32[1,2,3]{1,0,2:T(1,128)S(1)} fusion(s32[1,16,3]{1,0,2:T(1,128)} %param.11, s32[]{:T(128)S(6)} %select_n.14), kind=kLoop, calls=%fused_computation | loop fusion | flops 12 | bytes 52 | tf_op jit(solution)/shard_map/jit(_where)/select_n | solution.py:463
  7.6 0.1 copy.11
  7.7 0.1 select_n.16
  7.8 0.1 broadcast_in_dim.27.bias
  7.9 3.0 %shard_map.101 = (bf16[256,512]{1,0:T(8,128)(2,1)S(1)}, bf16[256,512]{1,0:T(8,128)(2,1)S(1)}, bf16[256,512]{1,0:T(8,128)(2,1)S(1)}, bf16[128,1024]{1,0:T(8,128)(...) custom-call(f32[6,1,256]{2,1,0:T(1,128)S(1)} %broadcast_in_dim.27.bi, ...), custom_call_target="tpu_custom_call" | custom-call | flops 1000000 | bytes 4096 | tf_op jit(solution)/shard_map/pallas_call | solution.py:419
  10.9 0.1 collective-permute-start.4
  10.9 0.5 %collective-permute-start.5 = (bf16[128,1024]{1,0:T(8,128)(2,1)S(1)}, bf16[128,1024]{1,0:T(8,128)(2,1)S(1)}, u32[]{:S(2)}, u32[]{:S(2)}) collective-permute-start(bf16[128,1024]{1,0:T(8,128)(2,1)S(1)} %get-tuple-element.58.g_high), channel_id=1, source_target_pairs={{0,1},{1,0},{2,3},{3,2},{4,5},{5,4},{6,7},{7,6},{8,9},{9,8},{10,11... | collective-permute-start | bytes 786440 | tf_op jit(solution)/shard_map/ppermute | solution.py:487
  11.4 0.0 collective-permute-done.1.rim_k.chip_k
  11.4 0.0 collective-permute-done.2.rim_v.chip_v
  11.4 0.5 %shard_map.103 = (f32[512,128]{1,0:T(8,128)S(1)}, f32[2,4,256]{2,1,0:T(4,128)S(1)}, f32[4,128,256]{2,1,0:T(8,128)S(1)}) custom-call(f32[6,1,256]{2,1,0:T(1,128)S(1)} %broadcast_in_dim.27.bias, bf16[256,512]{1,0:T(8,128)(2,1)S(1)} %get-tuple-element.46.q, bf16[128,512]{1,0:T(8,128)(2,1)S(1)} %collective-permute-done.1.rim_k.chip_k, ...), custom_call_target="tpu_custom_call" | custom-call | flops 1000000 | bytes 4000 | tf_op jit(solution)/shard_map/pallas_call | solution.py:407
  12.0 0.4 collective-permute-done.rim.link
  12.4 0.6 %shard_map.104 = (bf16[2,512,128]{2,1,0:T(8,128)(2,1)S(1)}, bf16[4,64,256]{2,1,0:T(8,128)(2,1)S(1)}, bf16[4,64,256]{2,1,0:T(8,128)(2,1)S(1)}, f32[4,128,256]{2,1...) custom-call(f32[6,1,256]{2,1,0:T(1,128)S(1)} %broadcast_in_dim.27.bias, ...), custom_call_target="tpu_custom_call" | custom-call | flops 1000000 | bytes 4000 | tf_op jit(solution)/shard_map/pallas_call | solution.py:407
  12.9 0.1 collective-permute-start.3
  13.0 0.3 shard_map.105.product
  13.3 0.0 collective-permute-done.4.g_low
  13.3 0.0 collective-permute-done.5.g_high
  13.3 1.0 %collective-permute-done.3.other = bf16[4,64,256]{2,1,0:T(8,128)(2,1)S(1)} collective-permute-done((bf16[4,64,256]{2,1,0:T(8,128)(2,1)S(1)}, bf16[4,64,256]{2,1,0:T(8,128)(2,1)S(1)}, u32[]{:S(2)}, u32[]{:S(2)}) %collective-permute-start.3) | collective-permute-done | bytes 131104 | tf_op jit(solution)/shard_map/ppermute | solution.py:516
  14.3 0.3 shard_map.106
  14.7 3.6 %collective-permute-start.6 = (bf16[4,64,256]{2,1,0:T(8,128)(2,1)S(1)}, bf16[4,64,256]{2,1,0:T(8,128)(2,1)S(1)}, u32[]{:S(2)}, u32[]{:S(2)}) collective-permute-start(bf16[4,64,256]{2,1,0:T(8,128)(2,1)S(1)} %get-tuple-element.61), channel_id=1, source_target_pairs={{0,24},{8,16},{16,8},{24,0},{1,25},{9,17},{17,9},{25,1},{2,26},{10... | collective-permute-start | bytes 393224 | tf_op jit(solution)/shard_map/ppermute | solution.py:552
  18.2 0.5 %collective-permute-start.7 = (bf16[4,64,256]{2,1,0:T(8,128)(2,1)S(1)}, bf16[4,64,256]{2,1,0:T(8,128)(2,1)S(1)}, u32[]{:S(2)}, u32[]{:S(2)}) collective-permute-start(bf16[4,64,256]{2,1,0:T(8,128)(2,1)S(1)} %get-tuple-element.62), channel_id=1, source_target_pairs={{0,16},{8,24},{16,0},{24,8},{1,17},{9,25},{17,1},{25,9},{2,18},{10... | collective-permute-start | bytes 393224 | tf_op jit(solution)/shard_map/ppermute | solution.py:552
  18.7 0.1 collective-permute-start.8
  18.9 0.9 %shard_map.107 = (bf16[2,128,512]{2,1,0:T(8,128)(2,1)S(1)}, bf16[2,128,512]{2,1,0:T(8,128)(2,1)S(1)}, f32[2,4,256]{2,1,0:T(4,128)S(1)}, f32[2,512,128]{2,1,0:T(8,128)S(1)}) custom-call(bf16[256,512]{1,0:T(8,128)(2,1)S(1)} %get-tuple-element.46.q, bf16[2,128,512]{2,1,0:T(8,128)(2,1)S(1)} %collective-permute-done.rim.link, ...), custom_call_target="tpu_custom_call" | custom-call | flops 1000000 | bytes 4000 | tf_op jit(solution)/shard_map/pallas_call | solution.py:407
  19.8 1.4 %collective-permute-start.9 = (bf16[2,128,512]{2,1,0:T(8,128)(2,1)S(1)}, bf16[2,128,512]{2,1,0:T(8,128)(2,1)S(1)}, u32[]{:S(2)}, u32[]{:S(2)}) collective-permute-start(bf16[2,128,512]{2,1,0:T(8,128)(2,1)S(1)} %get-tuple-element.80), channel_id=1, source_target_pairs={{0,7},{1,2},{2,1},{3,4},{4,3},{5,6},{6,5},{7,0},{8,15},{9,10},{10,... | collective-permute-start | bytes 786440 | tf_op jit(solution)/shard_map/ppermute | solution.py:537
  21.2 2.1 %shard_map.108 = (bf16[256,512]{1,0:T(8,128)(2,1)}, f32[256,512]{1,0:T(8,128)S(1)}, f32[256,512]{1,0:T(8,128)S(1)}, f32[8,128]{1,0:T(8,128)S(1)}) custom-call(bf16[256,512]{1,0:T(8,128)(2,1)S(1)} %get-tuple-element.46.q, bf16[256,512]{1,0:T(8,128)(2,1)S(1)} %get-tuple-element.64.k, bf16[256,512]{1,0:T(8,128)(2,1)S(1)} %get-tuple-element.65.v, ...), custom_call_target="tpu_custom_call" | custom-call | flops 5000000000 | bytes 20000000 | tf_op jit(solution)/shard_map/pallas_call | solution.py:407
  23.4 0.0 collective-permute-done.6.refs_1_
  23.4 1.5 %collective-permute-done.7.refs_2_ = bf16[4,64,256]{2,1,0:T(8,128)(2,1)S(1)} collective-permute-done((bf16[4,64,256]{2,1,0:T(8,128)(2,1)S(1)}, bf16[4,64,256]{2,1,0:T(8,128)(2,1)S(1)}, u32[]{:S(2)}, u32[]{:S(2)}) %collective-permute-start.7) | collective-permute-done | bytes 131104 | tf_op jit(solution)/shard_map/ppermute | solution.py:552
  24.9 0.3 collective-permute-done.8.refs_3_
  25.1 0.1 shard_map.109
  25.2 2.1 %collective-permute-start.11 = (bf16[64,256]{1,0:T(8,128)(2,1)S(1)}, bf16[64,256]{1,0:T(8,128)(2,1)S(1)}, u32[]{:S(2)}, u32[]{:S(2)}) collective-permute-start(bf16[64,256]{1,0:T(8,128)(2,1)S(1)} %get-tuple-element.84), channel_id=1, source_target_pairs={{0,6},{1,7},{2,4},{3,5},{4,2},{5,3},{6,0},{7,1},{8,14},{9,15},{10,... | collective-permute-start | bytes 98312 | tf_op jit(solution)/shard_map/ppermute | solution.py:556
  27.3 0.0 collective-permute-start.12
  27.4 2.3 %collective-permute-start.13 = (bf16[64,256]{1,0:T(8,128)(2,1)S(1)}, bf16[64,256]{1,0:T(8,128)(2,1)S(1)}, u32[]{:S(2)}, u32[]{:S(2)}) collective-permute-start(bf16[64,256]{1,0:T(8,128)(2,1)S(1)} %get-tuple-element.86), channel_id=1, source_target_pairs={{0,2},{1,3},{2,0},{3,1},{4,6},{5,7},{6,4},{7,5},{8,10},{9,11},{10,... | collective-permute-start | bytes 98312 | tf_op jit(solution)/shard_map/ppermute | solution.py:556
  29.7 0.0 collective-permute-start.10
  29.7 1.4 %collective-permute-done.11.refs_1_ = bf16[64,256]{1,0:T(8,128)(2,1)S(1)} collective-permute-done((bf16[64,256]{1,0:T(8,128)(2,1)S(1)}, bf16[64,256]{1,0:T(8,128)(2,1)S(1)}, u32[]{:S(2)}, u32[]{:S(2)}) %collective-permute-start.11) | collective-permute-done | bytes 32800 | tf_op jit(solution)/shard_map/ppermute | solution.py:556
  31.1 1.1 %collective-permute-done.12.refs_2_ = bf16[64,256]{1,0:T(8,128)(2,1)S(1)} collective-permute-done((bf16[64,256]{1,0:T(8,128)(2,1)S(1)}, bf16[64,256]{1,0:T(8,128)(2,1)S(1)}, u32[]{:S(2)}, u32[]{:S(2)}) %collective-permute-start.12) | collective-permute-done | bytes 32800 | tf_op jit(solution)/shard_map/ppermute | solution.py:556
  32.2 0.0 collective-permute-done.13.refs_3_
  32.2 1.9 %collective-permute-start.14 = (bf16[64,256]{1,0:T(8,128)(2,1)S(1)}, bf16[64,256]{1,0:T(8,128)(2,1)S(1)}, u32[]{:S(2)}, u32[]{:S(2)}) collective-permute-start(bf16[64,256]{1,0:T(8,128)(2,1)S(1)} %shard_map.112.refs_0_), channel_id=1, source_target_pairs={{0,24},{8,16},{16,8},{24,0},{1,25},{9,17},{17,9},{25,1},{2,26},{10... | collective-permute-start | bytes 98312 | tf_op jit(solution)/shard_map/ppermute | solution.py:564
  34.1 1.1 %collective-permute-start.15 = (bf16[64,256]{1,0:T(8,128)(2,1)S(1)}, bf16[64,256]{1,0:T(8,128)(2,1)S(1)}, u32[]{:S(2)}, u32[]{:S(2)}) collective-permute-start(bf16[64,256]{1,0:T(8,128)(2,1)S(1)} %shard_map.112.refs_0_), channel_id=1, source_target_pairs={{0,16},{8,24},{16,0},{24,8},{1,17},{9,25},{17,1},{25,9},{2,18},{10... | collective-permute-start | bytes 98312 | tf_op jit(solution)/shard_map/ppermute | solution.py:564
  35.2 0.5 %collective-permute-start.16 = (bf16[64,256]{1,0:T(8,128)(2,1)S(1)}, bf16[64,256]{1,0:T(8,128)(2,1)S(1)}, u32[]{:S(2)}, u32[]{:S(2)}) collective-permute-start(bf16[64,256]{1,0:T(8,128)(2,1)S(1)} %shard_map.112.refs_0_), channel_id=1, source_target_pairs={{0,8},{8,0},{16,24},{24,16},{1,9},{9,1},{17,25},{25,17},{2,10},{10... | collective-permute-start | bytes 98312 | tf_op jit(solution)/shard_map/ppermute | solution.py:564
  35.8 1.3 %shard_map.110 = bf16[256,1024]{1,0:T(8,128)(2,1)} custom-call(bf16[2,512,128]{2,1,0:T(8,128)(2,1)S(1)} %get-tuple-element.54.attn_t, bf16[512,1024]{1,0:T(8,128)(2,1)S(1)} %get-tuple-element.55.w_out, bf16[64,256]{1,0:T(8,128)(2,1)S(1)} %get-tuple-element.76.before.refs_0_), custom_call_target="tpu_custom_call" | custom-call | flops 5000000000 | bytes 20000000 | tf_op jit(solution)/shard_map/pallas_call | solution.py:407
  37.0 0.0 collective-permute-done.10.chip_kv
  37.0 0.9 %shard_map.111 = (bf16[256,512]{1,0:T(8,128)(2,1)}, bf16[256,512]{1,0:T(8,128)(2,1)}) custom-call(f32[256,512]{1,0:T(8,128)S(1)} %get-tuple-element.78.k_own, f32[256,512]{1,0:T(8,128)S(1)} %get-tuple-element.79.v_own, bf16[2,128,512]{2,1,0:T(8,128)(2,1)S(1)} %collective-permute-done.9.link_kv.refs_4_, bf16[2,128,512]{2,1,0:T(8,128)(2,1)S(1)} %collective-permute-done.10.chip_kv), custom_call_target="tpu_custom_call" | custom-call | flops 1000000 | bytes 4000 | tf_op jit(solution)/shard_map/pallas_call | solution.py:407
  37.9 0.1 collective-permute-done.15.refs_2_
  38.0 1.1 %collective-permute-done.16.refs_3_ = bf16[64,256]{1,0:T(8,128)(2,1)S(1)} collective-permute-done((bf16[64,256]{1,0:T(8,128)(2,1)S(1)}, bf16[64,256]{1,0:T(8,128)(2,1)S(1)}, u32[]{:S(2)}, u32[]{:S(2)}) %collective-permute-start.16) | collective-permute-done | bytes 32800 | tf_op jit(solution)/shard_map/ppermute | solution.py:564
  39.1 0.7 %shard_map.113 = f32[64,1024]{1,0:T(8,128)} custom-call(bf16[64,256]{1,0:T(8,128)(2,1)S(1)} %shard_map.112.refs_0_, bf16[64,256]{1,0:T(8,128)(2,1)S(1)} %collective-permute-done.14.refs_1_, bf16[64,256]{1,0:T(8,128)(2,1)S(1)} %collective-permute-done.15.refs_2_, bf16[64,256]{1,0:T(8,128)(2,1)S(1)} %collective-permute-done.16.refs_3_), custom_call_target="tpu_custom_call" | custom-call | flops 1000000 | bytes 4000 | tf_op jit(solution)/shard_map/pallas_call | solution.py:407
  (3 shorter events, 0.0 us)
Async XLA Ops:
  1.8 10.6 %collective-permute-start = (bf16[2,128,512]{2,1,0:T(8,128)(2,1)S(1)}, bf16[2,128,512]{2,1,0:T(8,128)(2,1)S(1)}, u32[]{:S(2)}, u32[]{:S(2)}) collective-permute-start(bf16[2,128,512]{2,1,0:T(8,128)(2,1)S(1)} %get-tuple-element.47), channel_id=1, source_target_pairs={{0,7},{1,2},{2,1},{3,4},{4,3},{5,6},{6,5},{7,0},{8,15},{9,10},{10,... | collective-permute-start | bytes 786440 | tf_op jit(solution)/shard_map/ppermute | solution.py:460
  6.3 5.1 %collective-permute-start.1 = (bf16[128,512]{1,0:T(8,128)(2,1)S(1)}, bf16[128,512]{1,0:T(8,128)(2,1)S(1)}, u32[]{:S(2)}, u32[]{:S(2)}) collective-permute-start(bf16[128,512]{1,0:T(8,128)(2,1)S(1)} %get-tuple-element.50), channel_id=1, source_target_pairs={{0,1},{1,0},{2,3},{3,2},{4,5},{5,4},{6,7},{7,6},{8,9},{9,8},{10,11... | collective-permute-start | bytes 393224 | tf_op jit(solution)/shard_map/ppermute | solution.py:461
  6.3 5.1 %collective-permute-start.2 = (bf16[128,512]{1,0:T(8,128)(2,1)S(1)}, bf16[128,512]{1,0:T(8,128)(2,1)S(1)}, u32[]{:S(2)}, u32[]{:S(2)}) collective-permute-start(bf16[128,512]{1,0:T(8,128)(2,1)S(1)} %get-tuple-element.51), channel_id=1, source_target_pairs={{0,1},{1,0},{2,3},{3,2},{4,5},{5,4},{6,7},{7,6},{8,9},{9,8},{10,11... | collective-permute-start | bytes 393224 | tf_op jit(solution)/shard_map/ppermute | solution.py:461
  10.9 2.5 %collective-permute-start.4 = (bf16[128,1024]{1,0:T(8,128)(2,1)S(1)}, bf16[128,1024]{1,0:T(8,128)(2,1)S(1)}, u32[]{:S(2)}, u32[]{:S(2)}) collective-permute-start(bf16[128,1024]{1,0:T(8,128)(2,1)S(1)} %get-tuple-element.57.g_low), channel_id=1, source_target_pairs={{0,1},{1,0},{2,3},{3,2},{4,5},{5,4},{6,7},{7,6},{8,9},{9,8},{10,11... | collective-permute-start | bytes 786440 | tf_op jit(solution)/shard_map/ppermute | solution.py:487
  10.9 2.4 %collective-permute-start.5 = (bf16[128,1024]{1,0:T(8,128)(2,1)S(1)}, bf16[128,1024]{1,0:T(8,128)(2,1)S(1)}, u32[]{:S(2)}, u32[]{:S(2)}) collective-permute-start(bf16[128,1024]{1,0:T(8,128)(2,1)S(1)} %get-tuple-element.58.g_high), channel_id=1, source_target_pairs={{0,1},{1,0},{2,3},{3,2},{4,5},{5,4},{6,7},{7,6},{8,9},{9,8},{10,11... | collective-permute-start | bytes 786440 | tf_op jit(solution)/shard_map/ppermute | solution.py:487
  12.9 1.4 %collective-permute-start.3 = (bf16[4,64,256]{2,1,0:T(8,128)(2,1)S(1)}, bf16[4,64,256]{2,1,0:T(8,128)(2,1)S(1)}, u32[]{:S(2)}, u32[]{:S(2)}) collective-permute-start(bf16[4,64,256]{2,1,0:T(8,128)(2,1)S(1)} %get-tuple-element.59), channel_id=1, source_target_pairs={{0,1},{1,0},{2,3},{3,2},{4,5},{5,4},{6,7},{7,6},{8,9},{9,8},{10,11... | collective-permute-start | bytes 393224 | tf_op jit(solution)/shard_map/ppermute | solution.py:516
  14.7 8.7 %collective-permute-start.6 = (bf16[4,64,256]{2,1,0:T(8,128)(2,1)S(1)}, bf16[4,64,256]{2,1,0:T(8,128)(2,1)S(1)}, u32[]{:S(2)}, u32[]{:S(2)}) collective-permute-start(bf16[4,64,256]{2,1,0:T(8,128)(2,1)S(1)} %get-tuple-element.61), channel_id=1, source_target_pairs={{0,24},{8,16},{16,8},{24,0},{1,25},{9,17},{17,9},{25,1},{2,26},{10... | collective-permute-start | bytes 393224 | tf_op jit(solution)/shard_map/ppermute | solution.py:552
  18.2 6.6 %collective-permute-start.7 = (bf16[4,64,256]{2,1,0:T(8,128)(2,1)S(1)}, bf16[4,64,256]{2,1,0:T(8,128)(2,1)S(1)}, u32[]{:S(2)}, u32[]{:S(2)}) collective-permute-start(bf16[4,64,256]{2,1,0:T(8,128)(2,1)S(1)} %get-tuple-element.62), channel_id=1, source_target_pairs={{0,16},{8,24},{16,0},{24,8},{1,17},{9,25},{17,1},{25,9},{2,18},{10... | collective-permute-start | bytes 393224 | tf_op jit(solution)/shard_map/ppermute | solution.py:552
  18.7 6.4 %collective-permute-start.8 = (bf16[4,64,256]{2,1,0:T(8,128)(2,1)S(1)}, bf16[4,64,256]{2,1,0:T(8,128)(2,1)S(1)}, u32[]{:S(2)}, u32[]{:S(2)}) collective-permute-start(bf16[4,64,256]{2,1,0:T(8,128)(2,1)S(1)} %get-tuple-element.63), channel_id=1, source_target_pairs={{0,8},{8,0},{16,24},{24,16},{1,9},{9,1},{17,25},{25,17},{2,10},{10... | collective-permute-start | bytes 393224 | tf_op jit(solution)/shard_map/ppermute | solution.py:552
  19.8 12.4 %collective-permute-start.9 = (bf16[2,128,512]{2,1,0:T(8,128)(2,1)S(1)}, bf16[2,128,512]{2,1,0:T(8,128)(2,1)S(1)}, u32[]{:S(2)}, u32[]{:S(2)}) collective-permute-start(bf16[2,128,512]{2,1,0:T(8,128)(2,1)S(1)} %get-tuple-element.80), channel_id=1, source_target_pairs={{0,7},{1,2},{2,1},{3,4},{4,3},{5,6},{6,5},{7,0},{8,15},{9,10},{10,... | collective-permute-start | bytes 786440 | tf_op jit(solution)/shard_map/ppermute | solution.py:537
  25.2 5.9 %collective-permute-start.11 = (bf16[64,256]{1,0:T(8,128)(2,1)S(1)}, bf16[64,256]{1,0:T(8,128)(2,1)S(1)}, u32[]{:S(2)}, u32[]{:S(2)}) collective-permute-start(bf16[64,256]{1,0:T(8,128)(2,1)S(1)} %get-tuple-element.84), channel_id=1, source_target_pairs={{0,6},{1,7},{2,4},{3,5},{4,2},{5,3},{6,0},{7,1},{8,14},{9,15},{10,... | collective-permute-start | bytes 98312 | tf_op jit(solution)/shard_map/ppermute | solution.py:556
  27.3 4.8 %collective-permute-start.12 = (bf16[64,256]{1,0:T(8,128)(2,1)S(1)}, bf16[64,256]{1,0:T(8,128)(2,1)S(1)}, u32[]{:S(2)}, u32[]{:S(2)}) collective-permute-start(bf16[64,256]{1,0:T(8,128)(2,1)S(1)} %get-tuple-element.85), channel_id=1, source_target_pairs={{0,4},{1,5},{2,6},{3,7},{4,0},{5,1},{6,2},{7,3},{8,12},{9,13},{10,... | collective-permute-start | bytes 98312 | tf_op jit(solution)/shard_map/ppermute | solution.py:556
  27.4 4.8 %collective-permute-start.13 = (bf16[64,256]{1,0:T(8,128)(2,1)S(1)}, bf16[64,256]{1,0:T(8,128)(2,1)S(1)}, u32[]{:S(2)}, u32[]{:S(2)}) collective-permute-start(bf16[64,256]{1,0:T(8,128)(2,1)S(1)} %get-tuple-element.86), channel_id=1, source_target_pairs={{0,2},{1,3},{2,0},{3,1},{4,6},{5,7},{6,4},{7,5},{8,10},{9,11},{10,... | collective-permute-start | bytes 98312 | tf_op jit(solution)/shard_map/ppermute | solution.py:556
  29.7 7.4 %collective-permute-start.10 = (bf16[2,128,512]{2,1,0:T(8,128)(2,1)S(1)}, bf16[2,128,512]{2,1,0:T(8,128)(2,1)S(1)}, u32[]{:S(2)}, u32[]{:S(2)}) collective-permute-start(bf16[2,128,512]{2,1,0:T(8,128)(2,1)S(1)} %get-tuple-element.81), channel_id=1, source_target_pairs={{0,1},{1,0},{2,3},{3,2},{4,5},{5,4},{6,7},{7,6},{8,9},{9,8},{10,11... | collective-permute-start | bytes 786440 | tf_op jit(solution)/shard_map/ppermute | solution.py:538
  32.2 5.7 %collective-permute-start.14 = (bf16[64,256]{1,0:T(8,128)(2,1)S(1)}, bf16[64,256]{1,0:T(8,128)(2,1)S(1)}, u32[]{:S(2)}, u32[]{:S(2)}) collective-permute-start(bf16[64,256]{1,0:T(8,128)(2,1)S(1)} %shard_map.112.refs_0_), channel_id=1, source_target_pairs={{0,24},{8,16},{16,8},{24,0},{1,25},{9,17},{17,9},{25,1},{2,26},{10... | collective-permute-start | bytes 98312 | tf_op jit(solution)/shard_map/ppermute | solution.py:564
  34.1 3.9 %collective-permute-start.15 = (bf16[64,256]{1,0:T(8,128)(2,1)S(1)}, bf16[64,256]{1,0:T(8,128)(2,1)S(1)}, u32[]{:S(2)}, u32[]{:S(2)}) collective-permute-start(bf16[64,256]{1,0:T(8,128)(2,1)S(1)} %shard_map.112.refs_0_), channel_id=1, source_target_pairs={{0,16},{8,24},{16,0},{24,8},{1,17},{9,25},{17,1},{25,9},{2,18},{10... | collective-permute-start | bytes 98312 | tf_op jit(solution)/shard_map/ppermute | solution.py:564
  35.2 3.9 %collective-permute-start.16 = (bf16[64,256]{1,0:T(8,128)(2,1)S(1)}, bf16[64,256]{1,0:T(8,128)(2,1)S(1)}, u32[]{:S(2)}, u32[]{:S(2)}) collective-permute-start(bf16[64,256]{1,0:T(8,128)(2,1)S(1)} %shard_map.112.refs_0_), channel_id=1, source_target_pairs={{0,8},{8,0},{16,24},{24,16},{1,9},{9,1},{17,25},{25,17},{2,10},{10... | collective-permute-start | bytes 98312 | tf_op jit(solution)/shard_map/ppermute | solution.py:564

commit v15 on v14

--- a/solution.py
+++ b/solution.py
@@ -80,21 +80,22 @@
     return pl.ds(pl.multiple_of(b * BLK, BLK), BLK)
 
 
-def pack_kernel(k, v, to_link, chip_k, chip_v, sems):
-    blocks = k.shape[0] // BLK
-    link_rows = rows_of(rim_block(blocks, True)[0])
-    chip_rows = rows_of(rim_block(blocks, False)[0])
-    pairs = (
-        (k.at[link_rows], to_link.at[0]),
-        (v.at[link_rows], to_link.at[1]),
-        (k.at[chip_rows], chip_k),
-        (v.at[chip_rows], chip_v),
-    )
+def copy_all(pairs, sems):
     copies = [pltpu.make_async_copy(x, y, sems.at[i]) for i, (x, y) in enumerate(pairs)]
     for copy in copies:
         copy.start()
     for copy in copies:
         copy.wait()
+
+
+def pack_link_kernel(k, v, out, sems):
+    rows = rows_of(rim_block(k.shape[0] // BLK, True)[0])
+    copy_all(((k.at[rows], out.at[0]), (v.at[rows], out.at[1])), sems)
+
+
+def pack_chip_kernel(k, v, k_out, v_out, sems):
+    rows = rows_of(rim_block(k.shape[0] // BLK, False)[0])
+    copy_all(((k.at[rows], k_out), (v.at[rows], v_out)), sems)
 
 
 def own_kernel(
@@ -451,12 +452,9 @@
     rows, cols = feats // ctx, width // dp
 
     rim = vmem(RIM, feats)
-    to_link, *to_chip = call_on_hbm(
-        pack_kernel,
-        [vmem(2, RIM, feats), rim, rim],
-        k, v,
-        scratch=[pltpu.SemaphoreType.DMA((4,))],
-    )
+    sems = [pltpu.SemaphoreType.DMA((2,))]
+    (to_link,) = call_on_hbm(pack_link_kernel, [vmem(2, RIM, feats)], k, v, scratch=sems)
+    to_chip = call_on_hbm(pack_chip_kernel, [rim, rim], k, v, scratch=sems)
     link = lax.ppermute(to_link, "ctx", over_links(ctx))
     chip_k, chip_v = (lax.ppermute(x, "ctx", swap(ctx, 1)) for x in to_chip)
     mask = lax.dynamic_slice_in_dim(block_mask[0], at_ctx * blocks, blocks, 0)

time: 40.1 us -> 39.9 us (level)
  Pallas kernels: 11.8 us -> 12.7 us
  starting transfers between devices: 19.4 us -> 18.8 us
  waiting for transfers between devices: 6.92 us -> 6.47 us
    pallas_call x2 -> x3, Pallas kernels: 4.15 us -> 4.99 us  [call_on_hbm(): pl.pallas_call(kernel, out_shape=outs, in_specs=[pl.BlockSpec(memory_spac...]
    ppermute x3, starting transfers between devices: 4.22 us -> 3.55 us  [body(): lax.ppermute(halves[s], 'dp', swap(dp, s))]
  transfers between devices with their start and end apart: 17 -> 17, of which waited for: 8 -> 7; matrix products, arithmetic and copies ran while one was open for 3% -> 3% of each run, Pallas kernels for 24% -> 27%
where the time goes in v15:
time: 39.9 us; the launch traced here: 39.7 us
  starting transfers between devices  18.8 us (47%)
  Pallas kernels  12.7 us (32%)
  waiting for transfers between devices  6.47 us (16%)
  other arithmetic  0.75 us (2%)
  between operations  0.74 us (2%)
    pallas_call x11, Pallas kernels, call(): pl.pallas_call(kernel, out_shape=outs, in_specs=[in_vmem] * len(args), ou...  7.71 us
    pallas_call x3, Pallas kernels, call_on_hbm(): pl.pallas_call(kernel, out_shape=outs, in_specs=[pl.BlockSpec(memory_spac...  4.99 us
    ppermute x1, starting transfers between devices, body(): link = lax.ppermute(to_link, 'ctx', over_links(ctx))  4.55 us
    ppermute x3, starting transfers between devices, body(): lax.ppermute(quarters[s], 'ctx', swap(ctx, 2 * s))  4.45 us
    ppermute x3, starting transfers between devices, body(): lax.ppermute(halves[s], 'dp', swap(dp, s))  3.55 us
    ppermute x3, starting transfers between devices, body(): lax.ppermute(piece, 'dp', swap(dp, s))  3.55 us
    ppermute x3, waiting for transfers between devices, body(): lax.ppermute(quarters[s], 'ctx', swap(ctx, 2 * s))  2.5 us
    ppermute x3, waiting for transfers between devices, body(): lax.ppermute(halves[s], 'dp', swap(dp, s))  1.78 us
  transfers between devices with their start and end apart: 17, of which 7 were waited for; matrix products, arithmetic and copies ran while one was open for 3% of the time, Pallas kernels for 27%

profile of v15, /device:TPU:0, one launch (start us, length us, event | category | flops | bytes accessed | tf_op | source)
XLA Modules:
  0.0 39.7 jit_solution(14814307986706369111)
XLA Ops:
  0.6 1.0 %shard_map.102 = bf16[2,128,512]{2,1,0:T(8,128)(2,1)S(1)} custom-call(bf16[256,512]{1,0:T(8,128)(2,1)} %bitcast.8, bf16[256,512]{1,0:T(8,128)(2,1)} %bitcast.11), custom_call_target="tpu_custom_call" | custom-call | flops 1000000 | bytes 4096 | tf_op jit(solution)/shard_map/pallas_call | solution.py:420
  1.6 4.6 %collective-permute-start = (bf16[2,128,512]{2,1,0:T(8,128)(2,1)S(1)}, bf16[2,128,512]{2,1,0:T(8,128)(2,1)S(1)}, u32[]{:S(2)}, u32[]{:S(2)}) collective-permute-start(bf16[2,128,512]{2,1,0:T(8,128)(2,1)S(1)} %shard_map.102), channel_id=1, source_target_pairs={{0,7},{1,2},{2,1},{3,4},{4,3},{5,6},{6,5},{7,0},{8,15},{9,10},{10,... | collective-permute-start | bytes 786440 | tf_op jit(solution)/shard_map/ppermute | solution.py:458
  6.2 1.0 %shard_map.103 = (bf16[128,512]{1,0:T(8,128)(2,1)S(1)}, bf16[128,512]{1,0:T(8,128)(2,1)S(1)}) custom-call(bf16[256,512]{1,0:T(8,128)(2,1)} %bitcast.9, bf16[256,512]{1,0:T(8,128)(2,1)} %bitcast.12), custom_call_target="tpu_custom_call" | custom-call | flops 1000000 | bytes 4096 | tf_op jit(solution)/shard_map/pallas_call | solution.py:420
  7.2 0.1 collective-permute-start.1
  7.3 0.5 %collective-permute-start.2 = (bf16[128,512]{1,0:T(8,128)(2,1)S(1)}, bf16[128,512]{1,0:T(8,128)(2,1)S(1)}, u32[]{:S(2)}, u32[]{:S(2)}) collective-permute-start(bf16[128,512]{1,0:T(8,128)(2,1)S(1)} %get-tuple-element.49), channel_id=1, source_target_pairs={{0,1},{1,0},{2,3},{3,2},{4,5},{5,4},{6,7},{7,6},{8,9},{9,8},{10,11... | collective-permute-start | bytes 393224 | tf_op jit(solution)/shard_map/ppermute | solution.py:459
  7.8 0.8 %compare_select_fusion = f32[1,2,3]{1,0,2:T(1,128)S(1)} fusion(s32[1,16,3]{1,0,2:T(1,128)} %param.11, s32[]{:T(128)S(6)} %select_n.14), kind=kLoop, calls=%fused_computation | loop fusion | flops 12 | bytes 52 | tf_op jit(solution)/shard_map/jit(_where)/select_n | solution.py:461
  8.5 0.1 copy.11
  8.6 0.1 select_n.16
  8.7 0.1 broadcast_in_dim.27.bias
  8.8 3.0 %shard_map.101 = (bf16[256,512]{1,0:T(8,128)(2,1)S(1)}, bf16[256,512]{1,0:T(8,128)(2,1)S(1)}, bf16[256,512]{1,0:T(8,128)(2,1)S(1)}, bf16[128,1024]{1,0:T(8,128)(...) custom-call(f32[6,1,256]{2,1,0:T(1,128)S(1)} %broadcast_in_dim.27.bi, ...), custom_call_target="tpu_custom_call" | custom-call | flops 1000000 | bytes 4096 | tf_op jit(solution)/shard_map/pallas_call | solution.py:420
  11.8 0.1 collective-permute-start.4
  11.9 0.4 %collective-permute-start.5 = (bf16[128,1024]{1,0:T(8,128)(2,1)S(1)}, bf16[128,1024]{1,0:T(8,128)(2,1)S(1)}, u32[]{:S(2)}, u32[]{:S(2)}) collective-permute-start(bf16[128,1024]{1,0:T(8,128)(2,1)S(1)} %get-tuple-element.56.g_high), channel_id=1, source_target_pairs={{0,1},{1,0},{2,3},{3,2},{4,5},{5,4},{6,7},{7,6},{8,9},{9,8},{10,11... | collective-permute-start | bytes 786440 | tf_op jit(solution)/shard_map/ppermute | solution.py:485
  12.4 0.0 collective-permute-done.1.rim_k.chip_k
  12.4 0.0 collective-permute-done.2.rim_v.chip_v
  12.4 0.5 %shard_map.104 = (f32[512,128]{1,0:T(8,128)S(1)}, f32[2,4,256]{2,1,0:T(4,128)S(1)}, f32[4,128,256]{2,1,0:T(8,128)S(1)}) custom-call(f32[6,1,256]{2,1,0:T(1,128)S(1)} %broadcast_in_dim.27.bias, bf16[256,512]{1,0:T(8,128)(2,1)S(1)} %get-tuple-element.45.q, bf16[128,512]{1,0:T(8,128)(2,1)S(1)} %collective-permute-done.1.rim_k.chip_k, ...), custom_call_target="tpu_custom_call" | custom-call | flops 1000000 | bytes 4000 | tf_op jit(solution)/shard_map/pallas_call | solution.py:408
  12.9 0.0 collective-permute-done.rim.link
  12.9 0.6 %shard_map.105 = (bf16[2,512,128]{2,1,0:T(8,128)(2,1)S(1)}, bf16[4,64,256]{2,1,0:T(8,128)(2,1)S(1)}, bf16[4,64,256]{2,1,0:T(8,128)(2,1)S(1)}, f32[4,128,256]{2,1...) custom-call(f32[6,1,256]{2,1,0:T(1,128)S(1)} %broadcast_in_dim.27.bias, ...), custom_call_target="tpu_custom_call" | custom-call | flops 1000000 | bytes 4000 | tf_op jit(solution)/shard_map/pallas_call | solution.py:408
  13.5 0.1 collective-permute-start.3
  13.6 0.3 shard_map.106.product
  13.9 0.0 collective-permute-done.4.g_low
  13.9 0.0 collective-permute-done.5.g_high
  13.9 0.9 %collective-permute-done.3.other = bf16[4,64,256]{2,1,0:T(8,128)(2,1)S(1)} collective-permute-done((bf16[4,64,256]{2,1,0:T(8,128)(2,1)S(1)}, bf16[4,64,256]{2,1,0:T(8,128)(2,1)S(1)}, u32[]{:S(2)}, u32[]{:S(2)}) %collective-permute-start.3) | collective-permute-done | bytes 131104 | tf_op jit(solution)/shard_map/ppermute | solution.py:514
  14.9 0.3 shard_map.107
  15.2 2.9 %collective-permute-start.6 = (bf16[4,64,256]{2,1,0:T(8,128)(2,1)S(1)}, bf16[4,64,256]{2,1,0:T(8,128)(2,1)S(1)}, u32[]{:S(2)}, u32[]{:S(2)}) collective-permute-start(bf16[4,64,256]{2,1,0:T(8,128)(2,1)S(1)} %get-tuple-element.59), channel_id=1, source_target_pairs={{0,24},{8,16},{16,8},{24,0},{1,25},{9,17},{17,9},{25,1},{2,26},{10... | collective-permute-start | bytes 393224 | tf_op jit(solution)/shard_map/ppermute | solution.py:550
  18.1 0.5 %collective-permute-start.7 = (bf16[4,64,256]{2,1,0:T(8,128)(2,1)S(1)}, bf16[4,64,256]{2,1,0:T(8,128)(2,1)S(1)}, u32[]{:S(2)}, u32[]{:S(2)}) collective-permute-start(bf16[4,64,256]{2,1,0:T(8,128)(2,1)S(1)} %get-tuple-element.60), channel_id=1, source_target_pairs={{0,16},{8,24},{16,0},{24,8},{1,17},{9,25},{17,1},{25,9},{2,18},{10... | collective-permute-start | bytes 393224 | tf_op jit(solution)/shard_map/ppermute | solution.py:550
  18.6 0.2 collective-permute-start.8
  18.8 0.9 %shard_map.108 = (bf16[2,128,512]{2,1,0:T(8,128)(2,1)S(1)}, bf16[2,128,512]{2,1,0:T(8,128)(2,1)S(1)}, f32[2,4,256]{2,1,0:T(4,128)S(1)}, f32[2,512,128]{2,1,0:T(8,128)S(1)}) custom-call(bf16[256,512]{1,0:T(8,128)(2,1)S(1)} %get-tuple-element.45.q, bf16[2,128,512]{2,1,0:T(8,128)(2,1)S(1)} %collective-permute-done.rim.link, ...), custom_call_target="tpu_custom_call" | custom-call | flops 1000000 | bytes 4000 | tf_op jit(solution)/shard_map/pallas_call | solution.py:408
  19.7 1.4 %collective-permute-start.9 = (bf16[2,128,512]{2,1,0:T(8,128)(2,1)S(1)}, bf16[2,128,512]{2,1,0:T(8,128)(2,1)S(1)}, u32[]{:S(2)}, u32[]{:S(2)}) collective-permute-start(bf16[2,128,512]{2,1,0:T(8,128)(2,1)S(1)} %get-tuple-element.78), channel_id=1, source_target_pairs={{0,7},{1,2},{2,1},{3,4},{4,3},{5,6},{6,5},{7,0},{8,15},{9,10},{10,... | collective-permute-start | bytes 786440 | tf_op jit(solution)/shard_map/ppermute | solution.py:535
  21.1 2.1 %shard_map.109 = (bf16[256,512]{1,0:T(8,128)(2,1)}, f32[256,512]{1,0:T(8,128)S(1)}, f32[256,512]{1,0:T(8,128)S(1)}, f32[8,128]{1,0:T(8,128)S(1)}) custom-call(bf16[256,512]{1,0:T(8,128)(2,1)S(1)} %get-tuple-element.45.q, bf16[256,512]{1,0:T(8,128)(2,1)S(1)} %get-tuple-element.62.k, bf16[256,512]{1,0:T(8,128)(2,1)S(1)} %get-tuple-element.63.v, ...), custom_call_target="tpu_custom_call" | custom-call | flops 5000000000 | bytes 20000000 | tf_op jit(solution)/shard_map/pallas_call | solution.py:408
  23.2 0.0 collective-permute-done.6.refs_1_
  23.2 1.5 %collective-permute-done.7.refs_2_ = bf16[4,64,256]{2,1,0:T(8,128)(2,1)S(1)} collective-permute-done((bf16[4,64,256]{2,1,0:T(8,128)(2,1)S(1)}, bf16[4,64,256]{2,1,0:T(8,128)(2,1)S(1)}, u32[]{:S(2)}, u32[]{:S(2)}) %collective-permute-start.7) | collective-permute-done | bytes 131104 | tf_op jit(solution)/shard_map/ppermute | solution.py:550
  24.7 0.3 collective-permute-done.8.refs_3_
  25.0 0.1 shard_map.110
  25.1 2.1 %collective-permute-start.11 = (bf16[64,256]{1,0:T(8,128)(2,1)S(1)}, bf16[64,256]{1,0:T(8,128)(2,1)S(1)}, u32[]{:S(2)}, u32[]{:S(2)}) collective-permute-start(bf16[64,256]{1,0:T(8,128)(2,1)S(1)} %get-tuple-element.82), channel_id=1, source_target_pairs={{0,6},{1,7},{2,4},{3,5},{4,2},{5,3},{6,0},{7,1},{8,14},{9,15},{10,... | collective-permute-start | bytes 98312 | tf_op jit(solution)/shard_map/ppermute | solution.py:554
  27.2 2.3 %collective-permute-start.13 = (bf16[64,256]{1,0:T(8,128)(2,1)S(1)}, bf16[64,256]{1,0:T(8,128)(2,1)S(1)}, u32[]{:S(2)}, u32[]{:S(2)}) collective-permute-start(bf16[64,256]{1,0:T(8,128)(2,1)S(1)} %get-tuple-element.84), channel_id=1, source_target_pairs={{0,2},{1,3},{2,0},{3,1},{4,6},{5,7},{6,4},{7,5},{8,10},{9,11},{10,... | collective-permute-start | bytes 98312 | tf_op jit(solution)/shard_map/ppermute | solution.py:554
  29.5 0.0 collective-permute-start.10
  29.5 1.3 %collective-permute-done.11.refs_1_ = bf16[64,256]{1,0:T(8,128)(2,1)S(1)} collective-permute-done((bf16[64,256]{1,0:T(8,128)(2,1)S(1)}, bf16[64,256]{1,0:T(8,128)(2,1)S(1)}, u32[]{:S(2)}, u32[]{:S(2)}) %collective-permute-start.11) | collective-permute-done | bytes 32800 | tf_op jit(solution)/shard_map/ppermute | solution.py:554
  30.8 1.2 %collective-permute-done.12.refs_2_ = bf16[64,256]{1,0:T(8,128)(2,1)S(1)} collective-permute-done((bf16[64,256]{1,0:T(8,128)(2,1)S(1)}, bf16[64,256]{1,0:T(8,128)(2,1)S(1)}, u32[]{:S(2)}, u32[]{:S(2)}) %collective-permute-start.12) | collective-permute-done | bytes 32800 | tf_op jit(solution)/shard_map/ppermute | solution.py:554
  32.0 0.0 collective-permute-done.13.refs_3_
  32.0 0.0 collective-permute-done.9.link_kv.refs_4_
  32.1 1.9 %collective-permute-start.14 = (bf16[64,256]{1,0:T(8,128)(2,1)S(1)}, bf16[64,256]{1,0:T(8,128)(2,1)S(1)}, u32[]{:S(2)}, u32[]{:S(2)}) collective-permute-start(bf16[64,256]{1,0:T(8,128)(2,1)S(1)} %shard_map.113.refs_0_), channel_id=1, source_target_pairs={{0,24},{8,16},{16,8},{24,0},{1,25},{9,17},{17,9},{25,1},{2,26},{10... | collective-permute-start | bytes 98312 | tf_op jit(solution)/shard_map/ppermute | solution.py:562
  34.0 1.1 %collective-permute-start.15 = (bf16[64,256]{1,0:T(8,128)(2,1)S(1)}, bf16[64,256]{1,0:T(8,128)(2,1)S(1)}, u32[]{:S(2)}, u32[]{:S(2)}) collective-permute-start(bf16[64,256]{1,0:T(8,128)(2,1)S(1)} %shard_map.113.refs_0_), channel_id=1, source_target_pairs={{0,16},{8,24},{16,0},{24,8},{1,17},{9,25},{17,1},{25,9},{2,18},{10... | collective-permute-start | bytes 98312 | tf_op jit(solution)/shard_map/ppermute | solution.py:562
  35.1 0.5 %collective-permute-start.16 = (bf16[64,256]{1,0:T(8,128)(2,1)S(1)}, bf16[64,256]{1,0:T(8,128)(2,1)S(1)}, u32[]{:S(2)}, u32[]{:S(2)}) collective-permute-start(bf16[64,256]{1,0:T(8,128)(2,1)S(1)} %shard_map.113.refs_0_), channel_id=1, source_target_pairs={{0,8},{8,0},{16,24},{24,16},{1,9},{9,1},{17,25},{25,17},{2,10},{10... | collective-permute-start | bytes 98312 | tf_op jit(solution)/shard_map/ppermute | solution.py:562
  35.6 1.3 %shard_map.111 = bf16[256,1024]{1,0:T(8,128)(2,1)} custom-call(bf16[2,512,128]{2,1,0:T(8,128)(2,1)S(1)} %get-tuple-element.52.attn_t, bf16[512,1024]{1,0:T(8,128)(2,1)S(1)} %get-tuple-element.53.w_out, bf16[64,256]{1,0:T(8,128)(2,1)S(1)} %get-tuple-element.74.before.refs_0_), custom_call_target="tpu_custom_call" | custom-call | flops 5000000000 | bytes 20000000 | tf_op jit(solution)/shard_map/pallas_call | solution.py:408
  36.9 0.9 %shard_map.112 = (bf16[256,512]{1,0:T(8,128)(2,1)}, bf16[256,512]{1,0:T(8,128)(2,1)}) custom-call(f32[256,512]{1,0:T(8,128)S(1)} %get-tuple-element.76.k_own, f32[256,512]{1,0:T(8,128)S(1)} %get-tuple-element.77.v_own, bf16[2,128,512]{2,1,0:T(8,128)(2,1)S(1)} %collective-permute-done.9.link_kv.refs_4_, bf16[2,128,512]{2,1,0:T(8,128)(2,1)S(1)} %collective-permute-done.10.chip_kv), custom_call_target="tpu_custom_call" | custom-call | flops 1000000 | bytes 4000 | tf_op jit(solution)/shard_map/pallas_call | solution.py:408
  37.8 0.1 collective-permute-done.15.refs_2_
  37.9 1.1 %collective-permute-done.16.refs_3_ = bf16[64,256]{1,0:T(8,128)(2,1)S(1)} collective-permute-done((bf16[64,256]{1,0:T(8,128)(2,1)S(1)}, bf16[64,256]{1,0:T(8,128)(2,1)S(1)}, u32[]{:S(2)}, u32[]{:S(2)}) %collective-permute-start.16) | collective-permute-done | bytes 32800 | tf_op jit(solution)/shard_map/ppermute | solution.py:562
  39.0 0.7 %shard_map.114 = f32[64,1024]{1,0:T(8,128)} custom-call(bf16[64,256]{1,0:T(8,128)(2,1)S(1)} %shard_map.113.refs_0_, bf16[64,256]{1,0:T(8,128)(2,1)S(1)} %collective-permute-done.14.refs_1_, bf16[64,256]{1,0:T(8,128)(2,1)S(1)} %collective-permute-done.15.refs_2_, bf16[64,256]{1,0:T(8,128)(2,1)S(1)} %collective-permute-done.16.refs_3_), custom_call_target="tpu_custom_call" | custom-call | flops 1000000 | bytes 4000 | tf_op jit(solution)/shard_map/pallas_call | solution.py:408
  (4 shorter events, 0.0 us)
Async XLA Ops:
  1.6 11.3 %collective-permute-start = (bf16[2,128,512]{2,1,0:T(8,128)(2,1)S(1)}, bf16[2,128,512]{2,1,0:T(8,128)(2,1)S(1)}, u32[]{:S(2)}, u32[]{:S(2)}) collective-permute-start(bf16[2,128,512]{2,1,0:T(8,128)(2,1)S(1)} %shard_map.102), channel_id=1, source_target_pairs={{0,7},{1,2},{2,1},{3,4},{4,3},{5,6},{6,5},{7,0},{8,15},{9,10},{10,... | collective-permute-start | bytes 786440 | tf_op jit(solution)/shard_map/ppermute | solution.py:458
  7.2 5.2 %collective-permute-start.1 = (bf16[128,512]{1,0:T(8,128)(2,1)S(1)}, bf16[128,512]{1,0:T(8,128)(2,1)S(1)}, u32[]{:S(2)}, u32[]{:S(2)}) collective-permute-start(bf16[128,512]{1,0:T(8,128)(2,1)S(1)} %get-tuple-element.48), channel_id=1, source_target_pairs={{0,1},{1,0},{2,3},{3,2},{4,5},{5,4},{6,7},{7,6},{8,9},{9,8},{10,11... | collective-permute-start | bytes 393224 | tf_op jit(solution)/shard_map/ppermute | solution.py:459
  7.3 5.1 %collective-permute-start.2 = (bf16[128,512]{1,0:T(8,128)(2,1)S(1)}, bf16[128,512]{1,0:T(8,128)(2,1)S(1)}, u32[]{:S(2)}, u32[]{:S(2)}) collective-permute-start(bf16[128,512]{1,0:T(8,128)(2,1)S(1)} %get-tuple-element.49), channel_id=1, source_target_pairs={{0,1},{1,0},{2,3},{3,2},{4,5},{5,4},{6,7},{7,6},{8,9},{9,8},{10,11... | collective-permute-start | bytes 393224 | tf_op jit(solution)/shard_map/ppermute | solution.py:459
  11.8 2.1 %collective-permute-start.4 = (bf16[128,1024]{1,0:T(8,128)(2,1)S(1)}, bf16[128,1024]{1,0:T(8,128)(2,1)S(1)}, u32[]{:S(2)}, u32[]{:S(2)}) collective-permute-start(bf16[128,1024]{1,0:T(8,128)(2,1)S(1)} %get-tuple-element.55.g_low), channel_id=1, source_target_pairs={{0,1},{1,0},{2,3},{3,2},{4,5},{5,4},{6,7},{7,6},{8,9},{9,8},{10,11... | collective-permute-start | bytes 786440 | tf_op jit(solution)/shard_map/ppermute | solution.py:485
  11.9 2.0 %collective-permute-start.5 = (bf16[128,1024]{1,0:T(8,128)(2,1)S(1)}, bf16[128,1024]{1,0:T(8,128)(2,1)S(1)}, u32[]{:S(2)}, u32[]{:S(2)}) collective-permute-start(bf16[128,1024]{1,0:T(8,128)(2,1)S(1)} %get-tuple-element.56.g_high), channel_id=1, source_target_pairs={{0,1},{1,0},{2,3},{3,2},{4,5},{5,4},{6,7},{7,6},{8,9},{9,8},{10,11... | collective-permute-start | bytes 786440 | tf_op jit(solution)/shard_map/ppermute | solution.py:485
  13.5 1.4 %collective-permute-start.3 = (bf16[4,64,256]{2,1,0:T(8,128)(2,1)S(1)}, bf16[4,64,256]{2,1,0:T(8,128)(2,1)S(1)}, u32[]{:S(2)}, u32[]{:S(2)}) collective-permute-start(bf16[4,64,256]{2,1,0:T(8,128)(2,1)S(1)} %get-tuple-element.57), channel_id=1, source_target_pairs={{0,1},{1,0},{2,3},{3,2},{4,5},{5,4},{6,7},{7,6},{8,9},{9,8},{10,11... | collective-permute-start | bytes 393224 | tf_op jit(solution)/shard_map/ppermute | solution.py:514
  15.2 8.0 %collective-permute-start.6 = (bf16[4,64,256]{2,1,0:T(8,128)(2,1)S(1)}, bf16[4,64,256]{2,1,0:T(8,128)(2,1)S(1)}, u32[]{:S(2)}, u32[]{:S(2)}) collective-permute-start(bf16[4,64,256]{2,1,0:T(8,128)(2,1)S(1)} %get-tuple-element.59), channel_id=1, source_target_pairs={{0,24},{8,16},{16,8},{24,0},{1,25},{9,17},{17,9},{25,1},{2,26},{10... | collective-permute-start | bytes 393224 | tf_op jit(solution)/shard_map/ppermute | solution.py:550
  18.1 6.6 %collective-permute-start.7 = (bf16[4,64,256]{2,1,0:T(8,128)(2,1)S(1)}, bf16[4,64,256]{2,1,0:T(8,128)(2,1)S(1)}, u32[]{:S(2)}, u32[]{:S(2)}) collective-permute-start(bf16[4,64,256]{2,1,0:T(8,128)(2,1)S(1)} %get-tuple-element.60), channel_id=1, source_target_pairs={{0,16},{8,24},{16,0},{24,8},{1,17},{9,25},{17,1},{25,9},{2,18},{10... | collective-permute-start | bytes 393224 | tf_op jit(solution)/shard_map/ppermute | solution.py:550
  18.6 6.4 %collective-permute-start.8 = (bf16[4,64,256]{2,1,0:T(8,128)(2,1)S(1)}, bf16[4,64,256]{2,1,0:T(8,128)(2,1)S(1)}, u32[]{:S(2)}, u32[]{:S(2)}) collective-permute-start(bf16[4,64,256]{2,1,0:T(8,128)(2,1)S(1)} %get-tuple-element.61), channel_id=1, source_target_pairs={{0,8},{8,0},{16,24},{24,16},{1,9},{9,1},{17,25},{25,17},{2,10},{10... | collective-permute-start | bytes 393224 | tf_op jit(solution)/shard_map/ppermute | solution.py:550
  19.7 12.4 %collective-permute-start.9 = (bf16[2,128,512]{2,1,0:T(8,128)(2,1)S(1)}, bf16[2,128,512]{2,1,0:T(8,128)(2,1)S(1)}, u32[]{:S(2)}, u32[]{:S(2)}) collective-permute-start(bf16[2,128,512]{2,1,0:T(8,128)(2,1)S(1)} %get-tuple-element.78), channel_id=1, source_target_pairs={{0,7},{1,2},{2,1},{3,4},{4,3},{5,6},{6,5},{7,0},{8,15},{9,10},{10,... | collective-permute-start | bytes 786440 | tf_op jit(solution)/shard_map/ppermute | solution.py:535
  25.1 5.8 %collective-permute-start.11 = (bf16[64,256]{1,0:T(8,128)(2,1)S(1)}, bf16[64,256]{1,0:T(8,128)(2,1)S(1)}, u32[]{:S(2)}, u32[]{:S(2)}) collective-permute-start(bf16[64,256]{1,0:T(8,128)(2,1)S(1)} %get-tuple-element.82), channel_id=1, source_target_pairs={{0,6},{1,7},{2,4},{3,5},{4,2},{5,3},{6,0},{7,1},{8,14},{9,15},{10,... | collective-permute-start | bytes 98312 | tf_op jit(solution)/shard_map/ppermute | solution.py:554
  27.2 4.8 %collective-permute-start.12 = (bf16[64,256]{1,0:T(8,128)(2,1)S(1)}, bf16[64,256]{1,0:T(8,128)(2,1)S(1)}, u32[]{:S(2)}, u32[]{:S(2)}) collective-permute-start(bf16[64,256]{1,0:T(8,128)(2,1)S(1)} %get-tuple-element.83), channel_id=1, source_target_pairs={{0,4},{1,5},{2,6},{3,7},{4,0},{5,1},{6,2},{7,3},{8,12},{9,13},{10,... | collective-permute-start | bytes 98312 | tf_op jit(solution)/shard_map/ppermute | solution.py:554
  27.2 4.8 %collective-permute-start.13 = (bf16[64,256]{1,0:T(8,128)(2,1)S(1)}, bf16[64,256]{1,0:T(8,128)(2,1)S(1)}, u32[]{:S(2)}, u32[]{:S(2)}) collective-permute-start(bf16[64,256]{1,0:T(8,128)(2,1)S(1)} %get-tuple-element.84), channel_id=1, source_target_pairs={{0,2},{1,3},{2,0},{3,1},{4,6},{5,7},{6,4},{7,5},{8,10},{9,11},{10,... | collective-permute-start | bytes 98312 | tf_op jit(solution)/shard_map/ppermute | solution.py:554
  29.5 7.4 %collective-permute-start.10 = (bf16[2,128,512]{2,1,0:T(8,128)(2,1)S(1)}, bf16[2,128,512]{2,1,0:T(8,128)(2,1)S(1)}, u32[]{:S(2)}, u32[]{:S(2)}) collective-permute-start(bf16[2,128,512]{2,1,0:T(8,128)(2,1)S(1)} %get-tuple-element.79), channel_id=1, source_target_pairs={{0,1},{1,0},{2,3},{3,2},{4,5},{5,4},{6,7},{7,6},{8,9},{9,8},{10,11... | collective-permute-start | bytes 786440 | tf_op jit(solution)/shard_map/ppermute | solution.py:536
  32.1 5.7 %collective-permute-start.14 = (bf16[64,256]{1,0:T(8,128)(2,1)S(1)}, bf16[64,256]{1,0:T(8,128)(2,1)S(1)}, u32[]{:S(2)}, u32[]{:S(2)}) collective-permute-start(bf16[64,256]{1,0:T(8,128)(2,1)S(1)} %shard_map.113.refs_0_), channel_id=1, source_target_pairs={{0,24},{8,16},{16,8},{24,0},{1,25},{9,17},{17,9},{25,1},{2,26},{10... | collective-permute-start | bytes 98312 | tf_op jit(solution)/shard_map/ppermute | solution.py:562
  34.0 3.9 %collective-permute-start.15 = (bf16[64,256]{1,0:T(8,128)(2,1)S(1)}, bf16[64,256]{1,0:T(8,128)(2,1)S(1)}, u32[]{:S(2)}, u32[]{:S(2)}) collective-permute-start(bf16[64,256]{1,0:T(8,128)(2,1)S(1)} %shard_map.113.refs_0_), channel_id=1, source_target_pairs={{0,16},{8,24},{16,0},{24,8},{1,17},{9,25},{17,1},{25,9},{2,18},{10... | collective-permute-start | bytes 98312 | tf_op jit(solution)/shard_map/ppermute | solution.py:562
  35.1 3.9 %collective-permute-start.16 = (bf16[64,256]{1,0:T(8,128)(2,1)S(1)}, bf16[64,256]{1,0:T(8,128)(2,1)S(1)}, u32[]{:S(2)}, u32[]{:S(2)}) collective-permute-start(bf16[64,256]{1,0:T(8,128)(2,1)S(1)} %shard_map.113.refs_0_), channel_id=1, source_target_pairs={{0,8},{8,0},{16,24},{24,16},{1,9},{9,1},{17,25},{25,17},{2,10},{10... | collective-permute-start | bytes 98312 | tf_op jit(solution)/shard_map/ppermute | solution.py:562

commit v16 on v15

--- a/solution.py
+++ b/solution.py
@@ -547,7 +547,7 @@
         scratch=[vmem(*own_scores, dtype=F32), vmem(*own_scores), vmem(*own_scores)],
     )
 
-    halves = [halves[0]] + [lax.ppermute(halves[s], "dp", swap(dp, s)) for s in range(dp - 1, 0, -1)]
+    halves = [halves[0]] + [lax.ppermute(halves[s], "dp", swap(dp, s)) for s in range(1, dp)]
     quarters = call(chips_kernel, [vmem(rows, cols)] * chips, 10**6, *halves, after)
     (output,) = call(output_kernel, [hbm(tokens, width)], 5 * 10**9, attn_t, w_out, quarters[0])
     quarters = [quarters[0]] + [

time: 39.9 us -> 39.9 us (level)
  transfers between devices with their start and end apart: 17 -> 17, of which waited for: 7 -> 5; matrix products, arithmetic and copies ran while one was open for 3% -> 3% of each run, Pallas kernels for 27% -> 27%
where the time goes in v16:
time: 39.9 us; the launch traced here: 39.7 us
  starting transfers between devices  18.8 us (47%)
  Pallas kernels  12.7 us (32%)
  waiting for transfers between devices  6.44 us (16%)
  other arithmetic  0.75 us (2%)
  between operations  0.74 us (2%)
    pallas_call x11, Pallas kernels, call(): pl.pallas_call(kernel, out_shape=outs, in_specs=[in_vmem] * len(args), ou...  7.7 us
    pallas_call x3, Pallas kernels, call_on_hbm(): pl.pallas_call(kernel, out_shape=outs, in_specs=[pl.BlockSpec(memory_spac...  4.99 us
    ppermute x1, starting transfers between devices, body(): link = lax.ppermute(to_link, 'ctx', over_links(ctx))  4.55 us
    ppermute x3, starting transfers between devices, body(): lax.ppermute(quarters[s], 'ctx', swap(ctx, 2 * s))  4.45 us
    ppermute x3, starting transfers between devices, body(): lax.ppermute(piece, 'dp', swap(dp, s))  3.55 us
    ppermute x3, starting transfers between devices, body(): lax.ppermute(halves[s], 'dp', swap(dp, s))  3.55 us
    ppermute x3, waiting for transfers between devices, body(): lax.ppermute(quarters[s], 'ctx', swap(ctx, 2 * s))  2.49 us
    ppermute x3, waiting for transfers between devices, body(): lax.ppermute(halves[s], 'dp', swap(dp, s))  2 us
  transfers between devices with their start and end apart: 17, of which 5 were waited for; matrix products, arithmetic and copies ran while one was open for 3% of the time, Pallas kernels for 27%

profile of v16, /device:TPU:0, one launch (start us, length us, event | category | flops | bytes accessed | tf_op | source)
XLA Modules:
  0.0 39.7 jit_solution(11772474574036494359)
XLA Ops:
  0.6 1.0 %shard_map.102 = bf16[2,128,512]{2,1,0:T(8,128)(2,1)S(1)} custom-call(bf16[256,512]{1,0:T(8,128)(2,1)} %bitcast.8, bf16[256,512]{1,0:T(8,128)(2,1)} %bitcast.11), custom_call_target="tpu_custom_call" | custom-call | flops 1000000 | bytes 4096 | tf_op jit(solution)/shard_map/pallas_call | solution.py:420
  1.6 4.6 %collective-permute-start = (bf16[2,128,512]{2,1,0:T(8,128)(2,1)S(1)}, bf16[2,128,512]{2,1,0:T(8,128)(2,1)S(1)}, u32[]{:S(2)}, u32[]{:S(2)}) collective-permute-start(bf16[2,128,512]{2,1,0:T(8,128)(2,1)S(1)} %shard_map.102), channel_id=1, source_target_pairs={{0,7},{1,2},{2,1},{3,4},{4,3},{5,6},{6,5},{7,0},{8,15},{9,10},{10,... | collective-permute-start | bytes 786440 | tf_op jit(solution)/shard_map/ppermute | solution.py:458
  6.2 1.0 %shard_map.103 = (bf16[128,512]{1,0:T(8,128)(2,1)S(1)}, bf16[128,512]{1,0:T(8,128)(2,1)S(1)}) custom-call(bf16[256,512]{1,0:T(8,128)(2,1)} %bitcast.9, bf16[256,512]{1,0:T(8,128)(2,1)} %bitcast.12), custom_call_target="tpu_custom_call" | custom-call | flops 1000000 | bytes 4096 | tf_op jit(solution)/shard_map/pallas_call | solution.py:420
  7.2 0.1 collective-permute-start.1
  7.3 0.5 %collective-permute-start.2 = (bf16[128,512]{1,0:T(8,128)(2,1)S(1)}, bf16[128,512]{1,0:T(8,128)(2,1)S(1)}, u32[]{:S(2)}, u32[]{:S(2)}) collective-permute-start(bf16[128,512]{1,0:T(8,128)(2,1)S(1)} %get-tuple-element.49), channel_id=1, source_target_pairs={{0,1},{1,0},{2,3},{3,2},{4,5},{5,4},{6,7},{7,6},{8,9},{9,8},{10,11... | collective-permute-start | bytes 393224 | tf_op jit(solution)/shard_map/ppermute | solution.py:459
  7.8 0.8 %compare_select_fusion = f32[1,2,3]{1,0,2:T(1,128)S(1)} fusion(s32[1,16,3]{1,0,2:T(1,128)} %param.11, s32[]{:T(128)S(6)} %select_n.14), kind=kLoop, calls=%fused_computation | loop fusion | flops 12 | bytes 52 | tf_op jit(solution)/shard_map/jit(_where)/select_n | solution.py:461
  8.5 0.1 copy.11
  8.6 0.1 select_n.16
  8.7 0.1 broadcast_in_dim.27.bias
  8.8 3.0 %shard_map.101 = (bf16[256,512]{1,0:T(8,128)(2,1)S(1)}, bf16[256,512]{1,0:T(8,128)(2,1)S(1)}, bf16[256,512]{1,0:T(8,128)(2,1)S(1)}, bf16[128,1024]{1,0:T(8,128)(...) custom-call(f32[6,1,256]{2,1,0:T(1,128)S(1)} %broadcast_in_dim.27.bi, ...), custom_call_target="tpu_custom_call" | custom-call | flops 1000000 | bytes 4096 | tf_op jit(solution)/shard_map/pallas_call | solution.py:420
  11.8 0.1 collective-permute-start.4
  11.9 0.4 %collective-permute-start.5 = (bf16[128,1024]{1,0:T(8,128)(2,1)S(1)}, bf16[128,1024]{1,0:T(8,128)(2,1)S(1)}, u32[]{:S(2)}, u32[]{:S(2)}) collective-permute-start(bf16[128,1024]{1,0:T(8,128)(2,1)S(1)} %get-tuple-element.56.g_high), channel_id=1, source_target_pairs={{0,1},{1,0},{2,3},{3,2},{4,5},{5,4},{6,7},{7,6},{8,9},{9,8},{10,11... | collective-permute-start | bytes 786440 | tf_op jit(solution)/shard_map/ppermute | solution.py:485
  12.4 0.0 collective-permute-done.1.rim_k.chip_k
  12.4 0.0 collective-permute-done.2.rim_v.chip_v
  12.4 0.5 %shard_map.104 = (f32[512,128]{1,0:T(8,128)S(1)}, f32[2,4,256]{2,1,0:T(4,128)S(1)}, f32[4,128,256]{2,1,0:T(8,128)S(1)}) custom-call(f32[6,1,256]{2,1,0:T(1,128)S(1)} %broadcast_in_dim.27.bias, bf16[256,512]{1,0:T(8,128)(2,1)S(1)} %get-tuple-element.45.q, bf16[128,512]{1,0:T(8,128)(2,1)S(1)} %collective-permute-done.1.rim_k.chip_k, ...), custom_call_target="tpu_custom_call" | custom-call | flops 1000000 | bytes 4000 | tf_op jit(solution)/shard_map/pallas_call | solution.py:408
  12.9 0.0 collective-permute-done.rim.link
  12.9 0.6 %shard_map.105 = (bf16[2,512,128]{2,1,0:T(8,128)(2,1)S(1)}, bf16[4,64,256]{2,1,0:T(8,128)(2,1)S(1)}, bf16[4,64,256]{2,1,0:T(8,128)(2,1)S(1)}, f32[4,128,256]{2,1...) custom-call(f32[6,1,256]{2,1,0:T(1,128)S(1)} %broadcast_in_dim.27.bias, ...), custom_call_target="tpu_custom_call" | custom-call | flops 1000000 | bytes 4000 | tf_op jit(solution)/shard_map/pallas_call | solution.py:408
  13.5 0.1 collective-permute-start.3
  13.6 0.3 shard_map.106.product
  13.9 0.0 collective-permute-done.4.g_low
  13.9 0.0 collective-permute-done.5.g_high
  13.9 0.9 %collective-permute-done.3.other = bf16[4,64,256]{2,1,0:T(8,128)(2,1)S(1)} collective-permute-done((bf16[4,64,256]{2,1,0:T(8,128)(2,1)S(1)}, bf16[4,64,256]{2,1,0:T(8,128)(2,1)S(1)}, u32[]{:S(2)}, u32[]{:S(2)}) %collective-permute-start.3) | collective-permute-done | bytes 131104 | tf_op jit(solution)/shard_map/ppermute | solution.py:514
  14.9 0.3 shard_map.107
  15.2 1.9 %collective-permute-start.6 = (bf16[4,64,256]{2,1,0:T(8,128)(2,1)S(1)}, bf16[4,64,256]{2,1,0:T(8,128)(2,1)S(1)}, u32[]{:S(2)}, u32[]{:S(2)}) collective-permute-start(bf16[4,64,256]{2,1,0:T(8,128)(2,1)S(1)} %get-tuple-element.59), channel_id=1, source_target_pairs={{0,8},{8,0},{16,24},{24,16},{1,9},{9,1},{17,25},{25,17},{2,10},{10... | collective-permute-start | bytes 393224 | tf_op jit(solution)/shard_map/ppermute | solution.py:550
  17.1 1.5 %collective-permute-start.7 = (bf16[4,64,256]{2,1,0:T(8,128)(2,1)S(1)}, bf16[4,64,256]{2,1,0:T(8,128)(2,1)S(1)}, u32[]{:S(2)}, u32[]{:S(2)}) collective-permute-start(bf16[4,64,256]{2,1,0:T(8,128)(2,1)S(1)} %get-tuple-element.60), channel_id=1, source_target_pairs={{0,16},{8,24},{16,0},{24,8},{1,17},{9,25},{17,1},{25,9},{2,18},{10... | collective-permute-start | bytes 393224 | tf_op jit(solution)/shard_map/ppermute | solution.py:550
  18.7 0.1 collective-permute-start.8
  18.8 0.9 %shard_map.108 = (bf16[2,128,512]{2,1,0:T(8,128)(2,1)S(1)}, bf16[2,128,512]{2,1,0:T(8,128)(2,1)S(1)}, f32[2,4,256]{2,1,0:T(4,128)S(1)}, f32[2,512,128]{2,1,0:T(8,128)S(1)}) custom-call(bf16[256,512]{1,0:T(8,128)(2,1)S(1)} %get-tuple-element.45.q, bf16[2,128,512]{2,1,0:T(8,128)(2,1)S(1)} %collective-permute-done.rim.link, ...), custom_call_target="tpu_custom_call" | custom-call | flops 1000000 | bytes 4000 | tf_op jit(solution)/shard_map/pallas_call | solution.py:408
  19.7 1.4 %collective-permute-start.9 = (bf16[2,128,512]{2,1,0:T(8,128)(2,1)S(1)}, bf16[2,128,512]{2,1,0:T(8,128)(2,1)S(1)}, u32[]{:S(2)}, u32[]{:S(2)}) collective-permute-start(bf16[2,128,512]{2,1,0:T(8,128)(2,1)S(1)} %get-tuple-element.78), channel_id=1, source_target_pairs={{0,7},{1,2},{2,1},{3,4},{4,3},{5,6},{6,5},{7,0},{8,15},{9,10},{10,... | collective-permute-start | bytes 786440 | tf_op jit(solution)/shard_map/ppermute | solution.py:535
  21.1 2.1 %shard_map.109 = (bf16[256,512]{1,0:T(8,128)(2,1)}, f32[256,512]{1,0:T(8,128)S(1)}, f32[256,512]{1,0:T(8,128)S(1)}, f32[8,128]{1,0:T(8,128)S(1)}) custom-call(bf16[256,512]{1,0:T(8,128)(2,1)S(1)} %get-tuple-element.45.q, bf16[256,512]{1,0:T(8,128)(2,1)S(1)} %get-tuple-element.62.k, bf16[256,512]{1,0:T(8,128)(2,1)S(1)} %get-tuple-element.63.v, ...), custom_call_target="tpu_custom_call" | custom-call | flops 5000000000 | bytes 20000000 | tf_op jit(solution)/shard_map/pallas_call | solution.py:408
  23.2 2.0 %collective-permute-done.7.refs_2_ = bf16[4,64,256]{2,1,0:T(8,128)(2,1)S(1)} collective-permute-done((bf16[4,64,256]{2,1,0:T(8,128)(2,1)S(1)}, bf16[4,64,256]{2,1,0:T(8,128)(2,1)S(1)}, u32[]{:S(2)}, u32[]{:S(2)}) %collective-permute-start.7) | collective-permute-done | bytes 131104 | tf_op jit(solution)/shard_map/ppermute | solution.py:550
  25.2 0.0 collective-permute-done.8.refs_3_
  25.2 0.1 shard_map.110
  25.3 2.1 %collective-permute-start.11 = (bf16[64,256]{1,0:T(8,128)(2,1)S(1)}, bf16[64,256]{1,0:T(8,128)(2,1)S(1)}, u32[]{:S(2)}, u32[]{:S(2)}) collective-permute-start(bf16[64,256]{1,0:T(8,128)(2,1)S(1)} %get-tuple-element.82), channel_id=1, source_target_pairs={{0,6},{1,7},{2,4},{3,5},{4,2},{5,3},{6,0},{7,1},{8,14},{9,15},{10,... | collective-permute-start | bytes 98312 | tf_op jit(solution)/shard_map/ppermute | solution.py:554
  27.4 0.0 collective-permute-start.12
  27.4 2.3 %collective-permute-start.13 = (bf16[64,256]{1,0:T(8,128)(2,1)S(1)}, bf16[64,256]{1,0:T(8,128)(2,1)S(1)}, u32[]{:S(2)}, u32[]{:S(2)}) collective-permute-start(bf16[64,256]{1,0:T(8,128)(2,1)S(1)} %get-tuple-element.84), channel_id=1, source_target_pairs={{0,2},{1,3},{2,0},{3,1},{4,6},{5,7},{6,4},{7,5},{8,10},{9,11},{10,... | collective-permute-start | bytes 98312 | tf_op jit(solution)/shard_map/ppermute | solution.py:554
  29.7 1.7 %collective-permute-done.11.refs_1_ = bf16[64,256]{1,0:T(8,128)(2,1)S(1)} collective-permute-done((bf16[64,256]{1,0:T(8,128)(2,1)S(1)}, bf16[64,256]{1,0:T(8,128)(2,1)S(1)}, u32[]{:S(2)}, u32[]{:S(2)}) %collective-permute-start.11) | collective-permute-done | bytes 32800 | tf_op jit(solution)/shard_map/ppermute | solution.py:554
  31.4 0.8 %collective-permute-done.12.refs_2_ = bf16[64,256]{1,0:T(8,128)(2,1)S(1)} collective-permute-done((bf16[64,256]{1,0:T(8,128)(2,1)S(1)}, bf16[64,256]{1,0:T(8,128)(2,1)S(1)}, u32[]{:S(2)}, u32[]{:S(2)}) %collective-permute-start.12) | collective-permute-done | bytes 32800 | tf_op jit(solution)/shard_map/ppermute | solution.py:554
  32.2 0.0 collective-permute-done.13.refs_3_
  32.2 0.0 collective-permute-done.9.link_kv.refs_4_
  32.3 1.7 %collective-permute-start.14 = (bf16[64,256]{1,0:T(8,128)(2,1)S(1)}, bf16[64,256]{1,0:T(8,128)(2,1)S(1)}, u32[]{:S(2)}, u32[]{:S(2)}) collective-permute-start(bf16[64,256]{1,0:T(8,128)(2,1)S(1)} %shard_map.113.refs_0_), channel_id=1, source_target_pairs={{0,24},{8,16},{16,8},{24,0},{1,25},{9,17},{17,9},{25,1},{2,26},{10... | collective-permute-start | bytes 98312 | tf_op jit(solution)/shard_map/ppermute | solution.py:562
  34.0 1.1 %collective-permute-start.15 = (bf16[64,256]{1,0:T(8,128)(2,1)S(1)}, bf16[64,256]{1,0:T(8,128)(2,1)S(1)}, u32[]{:S(2)}, u32[]{:S(2)}) collective-permute-start(bf16[64,256]{1,0:T(8,128)(2,1)S(1)} %shard_map.113.refs_0_), channel_id=1, source_target_pairs={{0,16},{8,24},{16,0},{24,8},{1,17},{9,25},{17,1},{25,9},{2,18},{10... | collective-permute-start | bytes 98312 | tf_op jit(solution)/shard_map/ppermute | solution.py:562
  35.0 0.8 %collective-permute-start.16 = (bf16[64,256]{1,0:T(8,128)(2,1)S(1)}, bf16[64,256]{1,0:T(8,128)(2,1)S(1)}, u32[]{:S(2)}, u32[]{:S(2)}) collective-permute-start(bf16[64,256]{1,0:T(8,128)(2,1)S(1)} %shard_map.113.refs_0_), channel_id=1, source_target_pairs={{0,8},{8,0},{16,24},{24,16},{1,9},{9,1},{17,25},{25,17},{2,10},{10... | collective-permute-start | bytes 98312 | tf_op jit(solution)/shard_map/ppermute | solution.py:562
  35.8 1.3 %shard_map.111 = bf16[256,1024]{1,0:T(8,128)(2,1)} custom-call(bf16[2,512,128]{2,1,0:T(8,128)(2,1)S(1)} %get-tuple-element.52.attn_t, bf16[512,1024]{1,0:T(8,128)(2,1)S(1)} %get-tuple-element.53.w_out, bf16[64,256]{1,0:T(8,128)(2,1)S(1)} %get-tuple-element.74.before.refs_0_), custom_call_target="tpu_custom_call" | custom-call | flops 5000000000 | bytes 20000000 | tf_op jit(solution)/shard_map/pallas_call | solution.py:408
  37.1 0.9 %shard_map.112 = (bf16[256,512]{1,0:T(8,128)(2,1)}, bf16[256,512]{1,0:T(8,128)(2,1)}) custom-call(f32[256,512]{1,0:T(8,128)S(1)} %get-tuple-element.76.k_own, f32[256,512]{1,0:T(8,128)S(1)} %get-tuple-element.77.v_own, bf16[2,128,512]{2,1,0:T(8,128)(2,1)S(1)} %collective-permute-done.9.link_kv.refs_4_, bf16[2,128,512]{2,1,0:T(8,128)(2,1)S(1)} %collective-permute-done.10.chip_kv), custom_call_target="tpu_custom_call" | custom-call | flops 1000000 | bytes 4000 | tf_op jit(solution)/shard_map/pallas_call | solution.py:408
  38.0 0.0 collective-permute-done.14.refs_1_
  38.0 0.0 collective-permute-done.15.refs_2_
  38.0 1.0 %collective-permute-done.16.refs_3_ = bf16[64,256]{1,0:T(8,128)(2,1)S(1)} collective-permute-done((bf16[64,256]{1,0:T(8,128)(2,1)S(1)}, bf16[64,256]{1,0:T(8,128)(2,1)S(1)}, u32[]{:S(2)}, u32[]{:S(2)}) %collective-permute-start.16) | collective-permute-done | bytes 32800 | tf_op jit(solution)/shard_map/ppermute | solution.py:562
  39.0 0.7 %shard_map.114 = f32[64,1024]{1,0:T(8,128)} custom-call(bf16[64,256]{1,0:T(8,128)(2,1)S(1)} %shard_map.113.refs_0_, bf16[64,256]{1,0:T(8,128)(2,1)S(1)} %collective-permute-done.14.refs_1_, bf16[64,256]{1,0:T(8,128)(2,1)S(1)} %collective-permute-done.15.refs_2_, bf16[64,256]{1,0:T(8,128)(2,1)S(1)} %collective-permute-done.16.refs_3_), custom_call_target="tpu_custom_call" | custom-call | flops 1000000 | bytes 4000 | tf_op jit(solution)/shard_map/pallas_call | solution.py:408
  (4 shorter events, 0.0 us)
Async XLA Ops:
  1.6 11.3 %collective-permute-start = (bf16[2,128,512]{2,1,0:T(8,128)(2,1)S(1)}, bf16[2,128,512]{2,1,0:T(8,128)(2,1)S(1)}, u32[]{:S(2)}, u32[]{:S(2)}) collective-permute-start(bf16[2,128,512]{2,1,0:T(8,128)(2,1)S(1)} %shard_map.102), channel_id=1, source_target_pairs={{0,7},{1,2},{2,1},{3,4},{4,3},{5,6},{6,5},{7,0},{8,15},{9,10},{10,... | collective-permute-start | bytes 786440 | tf_op jit(solution)/shard_map/ppermute | solution.py:458
  7.2 5.2 %collective-permute-start.1 = (bf16[128,512]{1,0:T(8,128)(2,1)S(1)}, bf16[128,512]{1,0:T(8,128)(2,1)S(1)}, u32[]{:S(2)}, u32[]{:S(2)}) collective-permute-start(bf16[128,512]{1,0:T(8,128)(2,1)S(1)} %get-tuple-element.48), channel_id=1, source_target_pairs={{0,1},{1,0},{2,3},{3,2},{4,5},{5,4},{6,7},{7,6},{8,9},{9,8},{10,11... | collective-permute-start | bytes 393224 | tf_op jit(solution)/shard_map/ppermute | solution.py:459
  7.3 5.1 %collective-permute-start.2 = (bf16[128,512]{1,0:T(8,128)(2,1)S(1)}, bf16[128,512]{1,0:T(8,128)(2,1)S(1)}, u32[]{:S(2)}, u32[]{:S(2)}) collective-permute-start(bf16[128,512]{1,0:T(8,128)(2,1)S(1)} %get-tuple-element.49), channel_id=1, source_target_pairs={{0,1},{1,0},{2,3},{3,2},{4,5},{5,4},{6,7},{7,6},{8,9},{9,8},{10,11... | collective-permute-start | bytes 393224 | tf_op jit(solution)/shard_map/ppermute | solution.py:459
  11.8 2.1 %collective-permute-start.4 = (bf16[128,1024]{1,0:T(8,128)(2,1)S(1)}, bf16[128,1024]{1,0:T(8,128)(2,1)S(1)}, u32[]{:S(2)}, u32[]{:S(2)}) collective-permute-start(bf16[128,1024]{1,0:T(8,128)(2,1)S(1)} %get-tuple-element.55.g_low), channel_id=1, source_target_pairs={{0,1},{1,0},{2,3},{3,2},{4,5},{5,4},{6,7},{7,6},{8,9},{9,8},{10,11... | collective-permute-start | bytes 786440 | tf_op jit(solution)/shard_map/ppermute | solution.py:485
  11.9 2.0 %collective-permute-start.5 = (bf16[128,1024]{1,0:T(8,128)(2,1)S(1)}, bf16[128,1024]{1,0:T(8,128)(2,1)S(1)}, u32[]{:S(2)}, u32[]{:S(2)}) collective-permute-start(bf16[128,1024]{1,0:T(8,128)(2,1)S(1)} %get-tuple-element.56.g_high), channel_id=1, source_target_pairs={{0,1},{1,0},{2,3},{3,2},{4,5},{5,4},{6,7},{7,6},{8,9},{9,8},{10,11... | collective-permute-start | bytes 786440 | tf_op jit(solution)/shard_map/ppermute | solution.py:485
  13.5 1.4 %collective-permute-start.3 = (bf16[4,64,256]{2,1,0:T(8,128)(2,1)S(1)}, bf16[4,64,256]{2,1,0:T(8,128)(2,1)S(1)}, u32[]{:S(2)}, u32[]{:S(2)}) collective-permute-start(bf16[4,64,256]{2,1,0:T(8,128)(2,1)S(1)} %get-tuple-element.57), channel_id=1, source_target_pairs={{0,1},{1,0},{2,3},{3,2},{4,5},{5,4},{6,7},{7,6},{8,9},{9,8},{10,11... | collective-permute-start | bytes 393224 | tf_op jit(solution)/shard_map/ppermute | solution.py:514
  15.2 8.0 %collective-permute-start.6 = (bf16[4,64,256]{2,1,0:T(8,128)(2,1)S(1)}, bf16[4,64,256]{2,1,0:T(8,128)(2,1)S(1)}, u32[]{:S(2)}, u32[]{:S(2)}) collective-permute-start(bf16[4,64,256]{2,1,0:T(8,128)(2,1)S(1)} %get-tuple-element.59), channel_id=1, source_target_pairs={{0,8},{8,0},{16,24},{24,16},{1,9},{9,1},{17,25},{25,17},{2,10},{10... | collective-permute-start | bytes 393224 | tf_op jit(solution)/shard_map/ppermute | solution.py:550
  17.1 8.1 %collective-permute-start.7 = (bf16[4,64,256]{2,1,0:T(8,128)(2,1)S(1)}, bf16[4,64,256]{2,1,0:T(8,128)(2,1)S(1)}, u32[]{:S(2)}, u32[]{:S(2)}) collective-permute-start(bf16[4,64,256]{2,1,0:T(8,128)(2,1)S(1)} %get-tuple-element.60), channel_id=1, source_target_pairs={{0,16},{8,24},{16,0},{24,8},{1,17},{9,25},{17,1},{25,9},{2,18},{10... | collective-permute-start | bytes 393224 | tf_op jit(solution)/shard_map/ppermute | solution.py:550
  18.7 6.5 %collective-permute-start.8 = (bf16[4,64,256]{2,1,0:T(8,128)(2,1)S(1)}, bf16[4,64,256]{2,1,0:T(8,128)(2,1)S(1)}, u32[]{:S(2)}, u32[]{:S(2)}) collective-permute-start(bf16[4,64,256]{2,1,0:T(8,128)(2,1)S(1)} %get-tuple-element.61), channel_id=1, source_target_pairs={{0,24},{8,16},{16,8},{24,0},{1,25},{9,17},{17,9},{25,1},{2,26},{10... | collective-permute-start | bytes 393224 | tf_op jit(solution)/shard_map/ppermute | solution.py:550
  19.7 12.6 %collective-permute-start.9 = (bf16[2,128,512]{2,1,0:T(8,128)(2,1)S(1)}, bf16[2,128,512]{2,1,0:T(8,128)(2,1)S(1)}, u32[]{:S(2)}, u32[]{:S(2)}) collective-permute-start(bf16[2,128,512]{2,1,0:T(8,128)(2,1)S(1)} %get-tuple-element.78), channel_id=1, source_target_pairs={{0,7},{1,2},{2,1},{3,4},{4,3},{5,6},{6,5},{7,0},{8,15},{9,10},{10,... | collective-permute-start | bytes 786440 | tf_op jit(solution)/shard_map/ppermute | solution.py:535
  25.3 6.1 %collective-permute-start.11 = (bf16[64,256]{1,0:T(8,128)(2,1)S(1)}, bf16[64,256]{1,0:T(8,128)(2,1)S(1)}, u32[]{:S(2)}, u32[]{:S(2)}) collective-permute-start(bf16[64,256]{1,0:T(8,128)(2,1)S(1)} %get-tuple-element.82), channel_id=1, source_target_pairs={{0,6},{1,7},{2,4},{3,5},{4,2},{5,3},{6,0},{7,1},{8,14},{9,15},{10,... | collective-permute-start | bytes 98312 | tf_op jit(solution)/shard_map/ppermute | solution.py:554
  27.4 4.8 %collective-permute-start.12 = (bf16[64,256]{1,0:T(8,128)(2,1)S(1)}, bf16[64,256]{1,0:T(8,128)(2,1)S(1)}, u32[]{:S(2)}, u32[]{:S(2)}) collective-permute-start(bf16[64,256]{1,0:T(8,128)(2,1)S(1)} %get-tuple-element.83), channel_id=1, source_target_pairs={{0,4},{1,5},{2,6},{3,7},{4,0},{5,1},{6,2},{7,3},{8,12},{9,13},{10,... | collective-permute-start | bytes 98312 | tf_op jit(solution)/shard_map/ppermute | solution.py:554
  27.4 4.8 %collective-permute-start.13 = (bf16[64,256]{1,0:T(8,128)(2,1)S(1)}, bf16[64,256]{1,0:T(8,128)(2,1)S(1)}, u32[]{:S(2)}, u32[]{:S(2)}) collective-permute-start(bf16[64,256]{1,0:T(8,128)(2,1)S(1)} %get-tuple-element.84), channel_id=1, source_target_pairs={{0,2},{1,3},{2,0},{3,1},{4,6},{5,7},{6,4},{7,5},{8,10},{9,11},{10,... | collective-permute-start | bytes 98312 | tf_op jit(solution)/shard_map/ppermute | solution.py:554
  29.7 7.3 %collective-permute-start.10 = (bf16[2,128,512]{2,1,0:T(8,128)(2,1)S(1)}, bf16[2,128,512]{2,1,0:T(8,128)(2,1)S(1)}, u32[]{:S(2)}, u32[]{:S(2)}) collective-permute-start(bf16[2,128,512]{2,1,0:T(8,128)(2,1)S(1)} %get-tuple-element.79), channel_id=1, source_target_pairs={{0,1},{1,0},{2,3},{3,2},{4,5},{5,4},{6,7},{7,6},{8,9},{9,8},{10,11... | collective-permute-start | bytes 786440 | tf_op jit(solution)/shard_map/ppermute | solution.py:536
  32.3 5.7 %collective-permute-start.14 = (bf16[64,256]{1,0:T(8,128)(2,1)S(1)}, bf16[64,256]{1,0:T(8,128)(2,1)S(1)}, u32[]{:S(2)}, u32[]{:S(2)}) collective-permute-start(bf16[64,256]{1,0:T(8,128)(2,1)S(1)} %shard_map.113.refs_0_), channel_id=1, source_target_pairs={{0,24},{8,16},{16,8},{24,0},{1,25},{9,17},{17,9},{25,1},{2,26},{10... | collective-permute-start | bytes 98312 | tf_op jit(solution)/shard_map/ppermute | solution.py:562
  34.0 4.0 %collective-permute-start.15 = (bf16[64,256]{1,0:T(8,128)(2,1)S(1)}, bf16[64,256]{1,0:T(8,128)(2,1)S(1)}, u32[]{:S(2)}, u32[]{:S(2)}) collective-permute-start(bf16[64,256]{1,0:T(8,128)(2,1)S(1)} %shard_map.113.refs_0_), channel_id=1, source_target_pairs={{0,16},{8,24},{16,0},{24,8},{1,17},{9,25},{17,1},{25,9},{2,18},{10... | collective-permute-start | bytes 98312 | tf_op jit(solution)/shard_map/ppermute | solution.py:562
  35.0 3.9 %collective-permute-start.16 = (bf16[64,256]{1,0:T(8,128)(2,1)S(1)}, bf16[64,256]{1,0:T(8,128)(2,1)S(1)}, u32[]{:S(2)}, u32[]{:S(2)}) collective-permute-start(bf16[64,256]{1,0:T(8,128)(2,1)S(1)} %shard_map.113.refs_0_), channel_id=1, source_target_pairs={{0,8},{8,0},{16,24},{24,16},{1,9},{9,1},{17,25},{25,17},{2,10},{10... | collective-permute-start | bytes 98312 | tf_op jit(solution)/shard_map/ppermute | solution.py:562

commit v17 on v16

--- a/solution.py
+++ b/solution.py
@@ -385,7 +385,7 @@
 
 
 def columns_kernel(*refs):
-    pieces, weight_grad = refs[:1] + refs[-2:0:-1], refs[-1]
+    pieces, weight_grad = refs[:-1], refs[-1]
     at_dp = lax.axis_index("dp")
     cols = pieces[0].shape[1]
     for d in range(len(pieces)):
@@ -559,7 +559,7 @@
         10**6,
         *quarters, link_back,
     )
-    pieces = [piece] + [lax.ppermute(piece, "dp", swap(dp, s)) for s in range(dp - 1, 0, -1)]
+    pieces = [piece] + [lax.ppermute(piece, "dp", swap(dp, s)) for s in range(1, dp)]
     k_grad, v_grad = call(
         rim_sum_kernel, [hbm(tokens, feats)] * 2, 10**6, k_own, v_own, link_back, chip_back
     )

time: 39.9 us -> 40.3 us (1.010)
  no operation moved by 1% of the time
where the time goes in v17:
time: 40.3 us; the launch traced here: 40.1 us
  starting transfers between devices  18.8 us (47%)
  Pallas kernels  12.7 us (32%)
  waiting for transfers between devices  6.84 us (17%)
  other arithmetic  0.75 us (2%)
  between operations  0.74 us (2%)
    pallas_call x11, Pallas kernels, call(): pl.pallas_call(kernel, out_shape=outs, in_specs=[in_vmem] * len(args), ou...  7.7 us
    pallas_call x3, Pallas kernels, call_on_hbm(): pl.pallas_call(kernel, out_shape=outs, in_specs=[pl.BlockSpec(memory_spac...  4.99 us
    ppermute x1, starting transfers between devices, body(): link = lax.ppermute(to_link, 'ctx', over_links(ctx))  4.55 us
    ppermute x3, starting transfers between devices, body(): lax.ppermute(quarters[s], 'ctx', swap(ctx, 2 * s))  4.45 us
    ppermute x3, starting transfers between devices, body(): lax.ppermute(halves[s], 'dp', swap(dp, s))  3.55 us
    ppermute x3, starting transfers between devices, body(): lax.ppermute(piece, 'dp', swap(dp, s))  3.55 us
    ppermute x3, waiting for transfers between devices, body(): lax.ppermute(quarters[s], 'ctx', swap(ctx, 2 * s))  2.49 us
    ppermute x3, waiting for transfers between devices, body(): lax.ppermute(halves[s], 'dp', swap(dp, s))  2 us
  transfers between devices with their start and end apart: 17, of which 5 were waited for; matrix products, arithmetic and copies ran while one was open for 3% of the time, Pallas kernels for 27%

profile of v17, /device:TPU:0, one launch (start us, length us, event | category | flops | bytes accessed | tf_op | source)
XLA Modules:
  0.0 40.1 jit_solution(17553993709402777045)
XLA Ops:
  0.6 1.0 %shard_map.102 = bf16[2,128,512]{2,1,0:T(8,128)(2,1)S(1)} custom-call(bf16[256,512]{1,0:T(8,128)(2,1)} %bitcast.8, bf16[256,512]{1,0:T(8,128)(2,1)} %bitcast.11), custom_call_target="tpu_custom_call" | custom-call | flops 1000000 | bytes 4096 | tf_op jit(solution)/shard_map/pallas_call | solution.py:420
  1.6 4.6 %collective-permute-start = (bf16[2,128,512]{2,1,0:T(8,128)(2,1)S(1)}, bf16[2,128,512]{2,1,0:T(8,128)(2,1)S(1)}, u32[]{:S(2)}, u32[]{:S(2)}) collective-permute-start(bf16[2,128,512]{2,1,0:T(8,128)(2,1)S(1)} %shard_map.102), channel_id=1, source_target_pairs={{0,7},{1,2},{2,1},{3,4},{4,3},{5,6},{6,5},{7,0},{8,15},{9,10},{10,... | collective-permute-start | bytes 786440 | tf_op jit(solution)/shard_map/ppermute | solution.py:458
  6.2 1.0 %shard_map.103 = (bf16[128,512]{1,0:T(8,128)(2,1)S(1)}, bf16[128,512]{1,0:T(8,128)(2,1)S(1)}) custom-call(bf16[256,512]{1,0:T(8,128)(2,1)} %bitcast.9, bf16[256,512]{1,0:T(8,128)(2,1)} %bitcast.12), custom_call_target="tpu_custom_call" | custom-call | flops 1000000 | bytes 4096 | tf_op jit(solution)/shard_map/pallas_call | solution.py:420
  7.2 0.1 collective-permute-start.1
  7.3 0.5 %collective-permute-start.2 = (bf16[128,512]{1,0:T(8,128)(2,1)S(1)}, bf16[128,512]{1,0:T(8,128)(2,1)S(1)}, u32[]{:S(2)}, u32[]{:S(2)}) collective-permute-start(bf16[128,512]{1,0:T(8,128)(2,1)S(1)} %get-tuple-element.49), channel_id=1, source_target_pairs={{0,1},{1,0},{2,3},{3,2},{4,5},{5,4},{6,7},{7,6},{8,9},{9,8},{10,11... | collective-permute-start | bytes 393224 | tf_op jit(solution)/shard_map/ppermute | solution.py:459
  7.8 0.8 %compare_select_fusion = f32[1,2,3]{1,0,2:T(1,128)S(1)} fusion(s32[1,16,3]{1,0,2:T(1,128)} %param.11, s32[]{:T(128)S(6)} %select_n.14), kind=kLoop, calls=%fused_computation | loop fusion | flops 12 | bytes 52 | tf_op jit(solution)/shard_map/jit(_where)/select_n | solution.py:461
  8.5 0.1 copy.11
  8.6 0.1 select_n.16
  8.7 0.1 broadcast_in_dim.27.bias
  8.8 3.0 %shard_map.101 = (bf16[256,512]{1,0:T(8,128)(2,1)S(1)}, bf16[256,512]{1,0:T(8,128)(2,1)S(1)}, bf16[256,512]{1,0:T(8,128)(2,1)S(1)}, bf16[128,1024]{1,0:T(8,128)(...) custom-call(f32[6,1,256]{2,1,0:T(1,128)S(1)} %broadcast_in_dim.27.bi, ...), custom_call_target="tpu_custom_call" | custom-call | flops 1000000 | bytes 4096 | tf_op jit(solution)/shard_map/pallas_call | solution.py:420
  11.8 0.1 collective-permute-start.4
  11.9 0.4 %collective-permute-start.5 = (bf16[128,1024]{1,0:T(8,128)(2,1)S(1)}, bf16[128,1024]{1,0:T(8,128)(2,1)S(1)}, u32[]{:S(2)}, u32[]{:S(2)}) collective-permute-start(bf16[128,1024]{1,0:T(8,128)(2,1)S(1)} %get-tuple-element.56.g_high), channel_id=1, source_target_pairs={{0,1},{1,0},{2,3},{3,2},{4,5},{5,4},{6,7},{7,6},{8,9},{9,8},{10,11... | collective-permute-start | bytes 786440 | tf_op jit(solution)/shard_map/ppermute | solution.py:485
  12.4 0.0 collective-permute-done.1.rim_k.chip_k
  12.4 0.0 collective-permute-done.2.rim_v.chip_v
  12.4 0.5 %shard_map.104 = (f32[512,128]{1,0:T(8,128)S(1)}, f32[2,4,256]{2,1,0:T(4,128)S(1)}, f32[4,128,256]{2,1,0:T(8,128)S(1)}) custom-call(f32[6,1,256]{2,1,0:T(1,128)S(1)} %broadcast_in_dim.27.bias, bf16[256,512]{1,0:T(8,128)(2,1)S(1)} %get-tuple-element.45.q, bf16[128,512]{1,0:T(8,128)(2,1)S(1)} %collective-permute-done.1.rim_k.chip_k, ...), custom_call_target="tpu_custom_call" | custom-call | flops 1000000 | bytes 4000 | tf_op jit(solution)/shard_map/pallas_call | solution.py:408
  12.9 0.0 collective-permute-done.rim.link
  12.9 0.6 %shard_map.105 = (bf16[2,512,128]{2,1,0:T(8,128)(2,1)S(1)}, bf16[4,64,256]{2,1,0:T(8,128)(2,1)S(1)}, bf16[4,64,256]{2,1,0:T(8,128)(2,1)S(1)}, f32[4,128,256]{2,1...) custom-call(f32[6,1,256]{2,1,0:T(1,128)S(1)} %broadcast_in_dim.27.bias, ...), custom_call_target="tpu_custom_call" | custom-call | flops 1000000 | bytes 4000 | tf_op jit(solution)/shard_map/pallas_call | solution.py:408
  13.5 0.1 collective-permute-start.3
  13.6 0.3 shard_map.106.product
  13.9 0.0 collective-permute-done.4.g_low
  13.9 0.0 collective-permute-done.5.g_high
  13.9 0.9 %collective-permute-done.3.other = bf16[4,64,256]{2,1,0:T(8,128)(2,1)S(1)} collective-permute-done((bf16[4,64,256]{2,1,0:T(8,128)(2,1)S(1)}, bf16[4,64,256]{2,1,0:T(8,128)(2,1)S(1)}, u32[]{:S(2)}, u32[]{:S(2)}) %collective-permute-start.3) | collective-permute-done | bytes 131104 | tf_op jit(solution)/shard_map/ppermute | solution.py:514
  14.9 0.3 shard_map.107
  15.2 1.9 %collective-permute-start.6 = (bf16[4,64,256]{2,1,0:T(8,128)(2,1)S(1)}, bf16[4,64,256]{2,1,0:T(8,128)(2,1)S(1)}, u32[]{:S(2)}, u32[]{:S(2)}) collective-permute-start(bf16[4,64,256]{2,1,0:T(8,128)(2,1)S(1)} %get-tuple-element.59), channel_id=1, source_target_pairs={{0,8},{8,0},{16,24},{24,16},{1,9},{9,1},{17,25},{25,17},{2,10},{10... | collective-permute-start | bytes 393224 | tf_op jit(solution)/shard_map/ppermute | solution.py:550
  17.1 1.5 %collective-permute-start.7 = (bf16[4,64,256]{2,1,0:T(8,128)(2,1)S(1)}, bf16[4,64,256]{2,1,0:T(8,128)(2,1)S(1)}, u32[]{:S(2)}, u32[]{:S(2)}) collective-permute-start(bf16[4,64,256]{2,1,0:T(8,128)(2,1)S(1)} %get-tuple-element.60), channel_id=1, source_target_pairs={{0,16},{8,24},{16,0},{24,8},{1,17},{9,25},{17,1},{25,9},{2,18},{10... | collective-permute-start | bytes 393224 | tf_op jit(solution)/shard_map/ppermute | solution.py:550
  18.7 0.1 collective-permute-start.8
  18.8 0.9 %shard_map.108 = (bf16[2,128,512]{2,1,0:T(8,128)(2,1)S(1)}, bf16[2,128,512]{2,1,0:T(8,128)(2,1)S(1)}, f32[2,4,256]{2,1,0:T(4,128)S(1)}, f32[2,512,128]{2,1,0:T(8,128)S(1)}) custom-call(bf16[256,512]{1,0:T(8,128)(2,1)S(1)} %get-tuple-element.45.q, bf16[2,128,512]{2,1,0:T(8,128)(2,1)S(1)} %collective-permute-done.rim.link, ...), custom_call_target="tpu_custom_call" | custom-call | flops 1000000 | bytes 4000 | tf_op jit(solution)/shard_map/pallas_call | solution.py:408
  19.7 1.4 %collective-permute-start.9 = (bf16[2,128,512]{2,1,0:T(8,128)(2,1)S(1)}, bf16[2,128,512]{2,1,0:T(8,128)(2,1)S(1)}, u32[]{:S(2)}, u32[]{:S(2)}) collective-permute-start(bf16[2,128,512]{2,1,0:T(8,128)(2,1)S(1)} %get-tuple-element.78), channel_id=1, source_target_pairs={{0,7},{1,2},{2,1},{3,4},{4,3},{5,6},{6,5},{7,0},{8,15},{9,10},{10,... | collective-permute-start | bytes 786440 | tf_op jit(solution)/shard_map/ppermute | solution.py:535
  21.1 2.1 %shard_map.109 = (bf16[256,512]{1,0:T(8,128)(2,1)}, f32[256,512]{1,0:T(8,128)S(1)}, f32[256,512]{1,0:T(8,128)S(1)}, f32[8,128]{1,0:T(8,128)S(1)}) custom-call(bf16[256,512]{1,0:T(8,128)(2,1)S(1)} %get-tuple-element.45.q, bf16[256,512]{1,0:T(8,128)(2,1)S(1)} %get-tuple-element.62.k, bf16[256,512]{1,0:T(8,128)(2,1)S(1)} %get-tuple-element.63.v, ...), custom_call_target="tpu_custom_call" | custom-call | flops 5000000000 | bytes 20000000 | tf_op jit(solution)/shard_map/pallas_call | solution.py:408
  23.2 2.0 %collective-permute-done.7.refs_2_ = bf16[4,64,256]{2,1,0:T(8,128)(2,1)S(1)} collective-permute-done((bf16[4,64,256]{2,1,0:T(8,128)(2,1)S(1)}, bf16[4,64,256]{2,1,0:T(8,128)(2,1)S(1)}, u32[]{:S(2)}, u32[]{:S(2)}) %collective-permute-start.7) | collective-permute-done | bytes 131104 | tf_op jit(solution)/shard_map/ppermute | solution.py:550
  25.2 0.0 collective-permute-done.8.refs_3_
  25.2 0.1 shard_map.110
  25.3 2.1 %collective-permute-start.11 = (bf16[64,256]{1,0:T(8,128)(2,1)S(1)}, bf16[64,256]{1,0:T(8,128)(2,1)S(1)}, u32[]{:S(2)}, u32[]{:S(2)}) collective-permute-start(bf16[64,256]{1,0:T(8,128)(2,1)S(1)} %get-tuple-element.82), channel_id=1, source_target_pairs={{0,6},{1,7},{2,4},{3,5},{4,2},{5,3},{6,0},{7,1},{8,14},{9,15},{10,... | collective-permute-start | bytes 98312 | tf_op jit(solution)/shard_map/ppermute | solution.py:554
  27.4 0.0 collective-permute-start.12
  27.4 2.3 %collective-permute-start.13 = (bf16[64,256]{1,0:T(8,128)(2,1)S(1)}, bf16[64,256]{1,0:T(8,128)(2,1)S(1)}, u32[]{:S(2)}, u32[]{:S(2)}) collective-permute-start(bf16[64,256]{1,0:T(8,128)(2,1)S(1)} %get-tuple-element.84), channel_id=1, source_target_pairs={{0,2},{1,3},{2,0},{3,1},{4,6},{5,7},{6,4},{7,5},{8,10},{9,11},{10,... | collective-permute-start | bytes 98312 | tf_op jit(solution)/shard_map/ppermute | solution.py:554
  29.7 0.0 collective-permute-start.10
  29.7 1.7 %collective-permute-done.11.refs_1_ = bf16[64,256]{1,0:T(8,128)(2,1)S(1)} collective-permute-done((bf16[64,256]{1,0:T(8,128)(2,1)S(1)}, bf16[64,256]{1,0:T(8,128)(2,1)S(1)}, u32[]{:S(2)}, u32[]{:S(2)}) %collective-permute-start.11) | collective-permute-done | bytes 32800 | tf_op jit(solution)/shard_map/ppermute | solution.py:554
  31.4 0.8 %collective-permute-done.12.refs_2_ = bf16[64,256]{1,0:T(8,128)(2,1)S(1)} collective-permute-done((bf16[64,256]{1,0:T(8,128)(2,1)S(1)}, bf16[64,256]{1,0:T(8,128)(2,1)S(1)}, u32[]{:S(2)}, u32[]{:S(2)}) %collective-permute-start.12) | collective-permute-done | bytes 32800 | tf_op jit(solution)/shard_map/ppermute | solution.py:554
  32.3 1.3 %collective-permute-start.14 = (bf16[64,256]{1,0:T(8,128)(2,1)S(1)}, bf16[64,256]{1,0:T(8,128)(2,1)S(1)}, u32[]{:S(2)}, u32[]{:S(2)}) collective-permute-start(bf16[64,256]{1,0:T(8,128)(2,1)S(1)} %shard_map.113.refs_0_), channel_id=1, source_target_pairs={{0,8},{8,0},{16,24},{24,16},{1,9},{9,1},{17,25},{25,17},{2,10},{10... | collective-permute-start | bytes 98312 | tf_op jit(solution)/shard_map/ppermute | solution.py:562
  33.6 1.0 %collective-permute-start.15 = (bf16[64,256]{1,0:T(8,128)(2,1)S(1)}, bf16[64,256]{1,0:T(8,128)(2,1)S(1)}, u32[]{:S(2)}, u32[]{:S(2)}) collective-permute-start(bf16[64,256]{1,0:T(8,128)(2,1)S(1)} %shard_map.113.refs_0_), channel_id=1, source_target_pairs={{0,16},{8,24},{16,0},{24,8},{1,17},{9,25},{17,1},{25,9},{2,18},{10... | collective-permute-start | bytes 98312 | tf_op jit(solution)/shard_map/ppermute | solution.py:562
  34.5 1.3 %collective-permute-start.16 = (bf16[64,256]{1,0:T(8,128)(2,1)S(1)}, bf16[64,256]{1,0:T(8,128)(2,1)S(1)}, u32[]{:S(2)}, u32[]{:S(2)}) collective-permute-start(bf16[64,256]{1,0:T(8,128)(2,1)S(1)} %shard_map.113.refs_0_), channel_id=1, source_target_pairs={{0,24},{8,16},{16,8},{24,0},{1,25},{9,17},{17,9},{25,1},{2,26},{10... | collective-permute-start | bytes 98312 | tf_op jit(solution)/shard_map/ppermute | solution.py:562
  35.8 1.3 %shard_map.111 = bf16[256,1024]{1,0:T(8,128)(2,1)} custom-call(bf16[2,512,128]{2,1,0:T(8,128)(2,1)S(1)} %get-tuple-element.52.attn_t, bf16[512,1024]{1,0:T(8,128)(2,1)S(1)} %get-tuple-element.53.w_out, bf16[64,256]{1,0:T(8,128)(2,1)S(1)} %get-tuple-element.74.before.refs_0_), custom_call_target="tpu_custom_call" | custom-call | flops 5000000000 | bytes 20000000 | tf_op jit(solution)/shard_map/pallas_call | solution.py:408
  37.1 0.0 collective-permute-done.10.chip_kv
  37.1 0.9 %shard_map.112 = (bf16[256,512]{1,0:T(8,128)(2,1)}, bf16[256,512]{1,0:T(8,128)(2,1)}) custom-call(f32[256,512]{1,0:T(8,128)S(1)} %get-tuple-element.76.k_own, f32[256,512]{1,0:T(8,128)S(1)} %get-tuple-element.77.v_own, bf16[2,128,512]{2,1,0:T(8,128)(2,1)S(1)} %collective-permute-done.9.link_kv.refs_4_, bf16[2,128,512]{2,1,0:T(8,128)(2,1)S(1)} %collective-permute-done.10.chip_kv), custom_call_target="tpu_custom_call" | custom-call | flops 1000000 | bytes 4000 | tf_op jit(solution)/shard_map/pallas_call | solution.py:408
  38.0 0.0 collective-permute-done.14.refs_1_
  38.0 0.0 collective-permute-done.15.refs_2_
  38.0 1.4 %collective-permute-done.16.refs_3_ = bf16[64,256]{1,0:T(8,128)(2,1)S(1)} collective-permute-done((bf16[64,256]{1,0:T(8,128)(2,1)S(1)}, bf16[64,256]{1,0:T(8,128)(2,1)S(1)}, u32[]{:S(2)}, u32[]{:S(2)}) %collective-permute-start.16) | collective-permute-done | bytes 32800 | tf_op jit(solution)/shard_map/ppermute | solution.py:562
  39.4 0.7 %shard_map.114 = f32[64,1024]{1,0:T(8,128)} custom-call(bf16[64,256]{1,0:T(8,128)(2,1)S(1)} %shard_map.113.refs_0_, bf16[64,256]{1,0:T(8,128)(2,1)S(1)} %collective-permute-done.14.refs_1_, bf16[64,256]{1,0:T(8,128)(2,1)S(1)} %collective-permute-done.15.refs_2_, bf16[64,256]{1,0:T(8,128)(2,1)S(1)} %collective-permute-done.16.refs_3_), custom_call_target="tpu_custom_call" | custom-call | flops 1000000 | bytes 4000 | tf_op jit(solution)/shard_map/pallas_call | solution.py:408
  (4 shorter events, 0.0 us)
Async XLA Ops:
  1.6 11.3 %collective-permute-start = (bf16[2,128,512]{2,1,0:T(8,128)(2,1)S(1)}, bf16[2,128,512]{2,1,0:T(8,128)(2,1)S(1)}, u32[]{:S(2)}, u32[]{:S(2)}) collective-permute-start(bf16[2,128,512]{2,1,0:T(8,128)(2,1)S(1)} %shard_map.102), channel_id=1, source_target_pairs={{0,7},{1,2},{2,1},{3,4},{4,3},{5,6},{6,5},{7,0},{8,15},{9,10},{10,... | collective-permute-start | bytes 786440 | tf_op jit(solution)/shard_map/ppermute | solution.py:458
  7.2 5.2 %collective-permute-start.1 = (bf16[128,512]{1,0:T(8,128)(2,1)S(1)}, bf16[128,512]{1,0:T(8,128)(2,1)S(1)}, u32[]{:S(2)}, u32[]{:S(2)}) collective-permute-start(bf16[128,512]{1,0:T(8,128)(2,1)S(1)} %get-tuple-element.48), channel_id=1, source_target_pairs={{0,1},{1,0},{2,3},{3,2},{4,5},{5,4},{6,7},{7,6},{8,9},{9,8},{10,11... | collective-permute-start | bytes 393224 | tf_op jit(solution)/shard_map/ppermute | solution.py:459
  7.3 5.1 %collective-permute-start.2 = (bf16[128,512]{1,0:T(8,128)(2,1)S(1)}, bf16[128,512]{1,0:T(8,128)(2,1)S(1)}, u32[]{:S(2)}, u32[]{:S(2)}) collective-permute-start(bf16[128,512]{1,0:T(8,128)(2,1)S(1)} %get-tuple-element.49), channel_id=1, source_target_pairs={{0,1},{1,0},{2,3},{3,2},{4,5},{5,4},{6,7},{7,6},{8,9},{9,8},{10,11... | collective-permute-start | bytes 393224 | tf_op jit(solution)/shard_map/ppermute | solution.py:459
  11.8 2.1 %collective-permute-start.4 = (bf16[128,1024]{1,0:T(8,128)(2,1)S(1)}, bf16[128,1024]{1,0:T(8,128)(2,1)S(1)}, u32[]{:S(2)}, u32[]{:S(2)}) collective-permute-start(bf16[128,1024]{1,0:T(8,128)(2,1)S(1)} %get-tuple-element.55.g_low), channel_id=1, source_target_pairs={{0,1},{1,0},{2,3},{3,2},{4,5},{5,4},{6,7},{7,6},{8,9},{9,8},{10,11... | collective-permute-start | bytes 786440 | tf_op jit(solution)/shard_map/ppermute | solution.py:485
  11.9 2.0 %collective-permute-start.5 = (bf16[128,1024]{1,0:T(8,128)(2,1)S(1)}, bf16[128,1024]{1,0:T(8,128)(2,1)S(1)}, u32[]{:S(2)}, u32[]{:S(2)}) collective-permute-start(bf16[128,1024]{1,0:T(8,128)(2,1)S(1)} %get-tuple-element.56.g_high), channel_id=1, source_target_pairs={{0,1},{1,0},{2,3},{3,2},{4,5},{5,4},{6,7},{7,6},{8,9},{9,8},{10,11... | collective-permute-start | bytes 786440 | tf_op jit(solution)/shard_map/ppermute | solution.py:485
  13.5 1.4 %collective-permute-start.3 = (bf16[4,64,256]{2,1,0:T(8,128)(2,1)S(1)}, bf16[4,64,256]{2,1,0:T(8,128)(2,1)S(1)}, u32[]{:S(2)}, u32[]{:S(2)}) collective-permute-start(bf16[4,64,256]{2,1,0:T(8,128)(2,1)S(1)} %get-tuple-element.57), channel_id=1, source_target_pairs={{0,1},{1,0},{2,3},{3,2},{4,5},{5,4},{6,7},{7,6},{8,9},{9,8},{10,11... | collective-permute-start | bytes 393224 | tf_op jit(solution)/shard_map/ppermute | solution.py:514
  15.2 8.0 %collective-permute-start.6 = (bf16[4,64,256]{2,1,0:T(8,128)(2,1)S(1)}, bf16[4,64,256]{2,1,0:T(8,128)(2,1)S(1)}, u32[]{:S(2)}, u32[]{:S(2)}) collective-permute-start(bf16[4,64,256]{2,1,0:T(8,128)(2,1)S(1)} %get-tuple-element.59), channel_id=1, source_target_pairs={{0,8},{8,0},{16,24},{24,16},{1,9},{9,1},{17,25},{25,17},{2,10},{10... | collective-permute-start | bytes 393224 | tf_op jit(solution)/shard_map/ppermute | solution.py:550
  17.1 8.1 %collective-permute-start.7 = (bf16[4,64,256]{2,1,0:T(8,128)(2,1)S(1)}, bf16[4,64,256]{2,1,0:T(8,128)(2,1)S(1)}, u32[]{:S(2)}, u32[]{:S(2)}) collective-permute-start(bf16[4,64,256]{2,1,0:T(8,128)(2,1)S(1)} %get-tuple-element.60), channel_id=1, source_target_pairs={{0,16},{8,24},{16,0},{24,8},{1,17},{9,25},{17,1},{25,9},{2,18},{10... | collective-permute-start | bytes 393224 | tf_op jit(solution)/shard_map/ppermute | solution.py:550
  18.7 6.5 %collective-permute-start.8 = (bf16[4,64,256]{2,1,0:T(8,128)(2,1)S(1)}, bf16[4,64,256]{2,1,0:T(8,128)(2,1)S(1)}, u32[]{:S(2)}, u32[]{:S(2)}) collective-permute-start(bf16[4,64,256]{2,1,0:T(8,128)(2,1)S(1)} %get-tuple-element.61), channel_id=1, source_target_pairs={{0,24},{8,16},{16,8},{24,0},{1,25},{9,17},{17,9},{25,1},{2,26},{10... | collective-permute-start | bytes 393224 | tf_op jit(solution)/shard_map/ppermute | solution.py:550
  19.7 12.6 %collective-permute-start.9 = (bf16[2,128,512]{2,1,0:T(8,128)(2,1)S(1)}, bf16[2,128,512]{2,1,0:T(8,128)(2,1)S(1)}, u32[]{:S(2)}, u32[]{:S(2)}) collective-permute-start(bf16[2,128,512]{2,1,0:T(8,128)(2,1)S(1)} %get-tuple-element.78), channel_id=1, source_target_pairs={{0,7},{1,2},{2,1},{3,4},{4,3},{5,6},{6,5},{7,0},{8,15},{9,10},{10,... | collective-permute-start | bytes 786440 | tf_op jit(solution)/shard_map/ppermute | solution.py:535
  25.3 6.1 %collective-permute-start.11 = (bf16[64,256]{1,0:T(8,128)(2,1)S(1)}, bf16[64,256]{1,0:T(8,128)(2,1)S(1)}, u32[]{:S(2)}, u32[]{:S(2)}) collective-permute-start(bf16[64,256]{1,0:T(8,128)(2,1)S(1)} %get-tuple-element.82), channel_id=1, source_target_pairs={{0,6},{1,7},{2,4},{3,5},{4,2},{5,3},{6,0},{7,1},{8,14},{9,15},{10,... | collective-permute-start | bytes 98312 | tf_op jit(solution)/shard_map/ppermute | solution.py:554
  27.4 4.8 %collective-permute-start.12 = (bf16[64,256]{1,0:T(8,128)(2,1)S(1)}, bf16[64,256]{1,0:T(8,128)(2,1)S(1)}, u32[]{:S(2)}, u32[]{:S(2)}) collective-permute-start(bf16[64,256]{1,0:T(8,128)(2,1)S(1)} %get-tuple-element.83), channel_id=1, source_target_pairs={{0,4},{1,5},{2,6},{3,7},{4,0},{5,1},{6,2},{7,3},{8,12},{9,13},{10,... | collective-permute-start | bytes 98312 | tf_op jit(solution)/shard_map/ppermute | solution.py:554
  27.4 4.8 %collective-permute-start.13 = (bf16[64,256]{1,0:T(8,128)(2,1)S(1)}, bf16[64,256]{1,0:T(8,128)(2,1)S(1)}, u32[]{:S(2)}, u32[]{:S(2)}) collective-permute-start(bf16[64,256]{1,0:T(8,128)(2,1)S(1)} %get-tuple-element.84), channel_id=1, source_target_pairs={{0,2},{1,3},{2,0},{3,1},{4,6},{5,7},{6,4},{7,5},{8,10},{9,11},{10,... | collective-permute-start | bytes 98312 | tf_op jit(solution)/shard_map/ppermute | solution.py:554
  29.7 7.3 %collective-permute-start.10 = (bf16[2,128,512]{2,1,0:T(8,128)(2,1)S(1)}, bf16[2,128,512]{2,1,0:T(8,128)(2,1)S(1)}, u32[]{:S(2)}, u32[]{:S(2)}) collective-permute-start(bf16[2,128,512]{2,1,0:T(8,128)(2,1)S(1)} %get-tuple-element.79), channel_id=1, source_target_pairs={{0,1},{1,0},{2,3},{3,2},{4,5},{5,4},{6,7},{7,6},{8,9},{9,8},{10,11... | collective-permute-start | bytes 786440 | tf_op jit(solution)/shard_map/ppermute | solution.py:536
  32.3 5.7 %collective-permute-start.14 = (bf16[64,256]{1,0:T(8,128)(2,1)S(1)}, bf16[64,256]{1,0:T(8,128)(2,1)S(1)}, u32[]{:S(2)}, u32[]{:S(2)}) collective-permute-start(bf16[64,256]{1,0:T(8,128)(2,1)S(1)} %shard_map.113.refs_0_), channel_id=1, source_target_pairs={{0,8},{8,0},{16,24},{24,16},{1,9},{9,1},{17,25},{25,17},{2,10},{10... | collective-permute-start | bytes 98312 | tf_op jit(solution)/shard_map/ppermute | solution.py:562
  33.6 4.4 %collective-permute-start.15 = (bf16[64,256]{1,0:T(8,128)(2,1)S(1)}, bf16[64,256]{1,0:T(8,128)(2,1)S(1)}, u32[]{:S(2)}, u32[]{:S(2)}) collective-permute-start(bf16[64,256]{1,0:T(8,128)(2,1)S(1)} %shard_map.113.refs_0_), channel_id=1, source_target_pairs={{0,16},{8,24},{16,0},{24,8},{1,17},{9,25},{17,1},{25,9},{2,18},{10... | collective-permute-start | bytes 98312 | tf_op jit(solution)/shard_map/ppermute | solution.py:562
  34.5 4.8 %collective-permute-start.16 = (bf16[64,256]{1,0:T(8,128)(2,1)S(1)}, bf16[64,256]{1,0:T(8,128)(2,1)S(1)}, u32[]{:S(2)}, u32[]{:S(2)}) collective-permute-start(bf16[64,256]{1,0:T(8,128)(2,1)S(1)} %shard_map.113.refs_0_), channel_id=1, source_target_pairs={{0,24},{8,16},{16,8},{24,0},{1,25},{9,17},{17,9},{25,1},{2,26},{10... | collective-permute-start | bytes 98312 | tf_op jit(solution)/shard_map/ppermute | solution.py:562

commit v18 on v16

--- a/solution.py
+++ b/solution.py
@@ -551,7 +551,8 @@
     quarters = call(chips_kernel, [vmem(rows, cols)] * chips, 10**6, *halves, after)
     (output,) = call(output_kernel, [hbm(tokens, width)], 5 * 10**9, attn_t, w_out, quarters[0])
     quarters = [quarters[0]] + [
-        lax.ppermute(quarters[s], "ctx", swap(ctx, 2 * s)) for s in range(chips - 1, 0, -1)
+        lax.ppermute(quarters[s], "ctx", swap(ctx, 2 * s))
+        for s in (*range(chips // 2, chips), *range(chips // 2 - 1, 0, -1))
     ]
     (piece,) = call(
         functools.partial(piece_kernel, (dp * tokens * ctx) ** (-0.5), chips),

time: 39.9 us -> 39.9 us (level)
  starting transfers between devices: 18.8 us -> 17.9 us
  waiting for transfers between devices: 6.44 us -> 7.32 us
    ppermute x3, starting transfers between devices: 4.45 us -> 3.55 us  [body(): lax.ppermute(quarters[s], 'ctx', swap(ctx, 2 * s))]
    ppermute x3, waiting for transfers between devices: 2.49 us -> 3.28 us  [body(): lax.ppermute(quarters[s], 'ctx', swap(ctx, 2 * s))]
  transfers between devices with their start and end apart: 17 -> 17, of which waited for: 5 -> 6; matrix products, arithmetic and copies ran while one was open for 3% -> 3% of each run, Pallas kernels for 27% -> 27%
where the time goes in v18:
time: 39.9 us; the launch traced here: 39.7 us
  starting transfers between devices  17.9 us (45%)
  Pallas kernels  12.7 us (32%)
  waiting for transfers between devices  7.32 us (18%)
  other arithmetic  0.75 us (2%)
  between operations  0.74 us (2%)
    pallas_call x11, Pallas kernels, call(): pl.pallas_call(kernel, out_shape=outs, in_specs=[in_vmem] * len(args), ou...  7.71 us
    pallas_call x3, Pallas kernels, call_on_hbm(): pl.pallas_call(kernel, out_shape=outs, in_specs=[pl.BlockSpec(memory_spac...  4.99 us
    ppermute x1, starting transfers between devices, body(): link = lax.ppermute(to_link, 'ctx', over_links(ctx))  4.55 us
    ppermute x3, starting transfers between devices, body(): lax.ppermute(piece, 'dp', swap(dp, s))  3.55 us
    ppermute x3, starting transfers between devices, body(): lax.ppermute(quarters[s], 'ctx', swap(ctx, 2 * s))  3.55 us
    ppermute x3, starting transfers between devices, body(): lax.ppermute(halves[s], 'dp', swap(dp, s))  3.55 us
    ppermute x3, waiting for transfers between devices, body(): lax.ppermute(quarters[s], 'ctx', swap(ctx, 2 * s))  3.28 us
    ppermute x3, waiting for transfers between devices, body(): lax.ppermute(halves[s], 'dp', swap(dp, s))  2 us
  transfers between devices with their start and end apart: 17, of which 6 were waited for; matrix products, arithmetic and copies ran while one was open for 3% of the time, Pallas kernels for 27%

profile of v18, /device:TPU:0, one launch (start us, length us, event | category | flops | bytes accessed | tf_op | source)
XLA Modules:
  0.0 39.7 jit_solution(1965233124604891515)
XLA Ops:
  0.6 1.0 %shard_map.102 = bf16[2,128,512]{2,1,0:T(8,128)(2,1)S(1)} custom-call(bf16[256,512]{1,0:T(8,128)(2,1)} %bitcast.8, bf16[256,512]{1,0:T(8,128)(2,1)} %bitcast.11), custom_call_target="tpu_custom_call" | custom-call | flops 1000000 | bytes 4096 | tf_op jit(solution)/shard_map/pallas_call | solution.py:420
  1.6 4.6 %collective-permute-start = (bf16[2,128,512]{2,1,0:T(8,128)(2,1)S(1)}, bf16[2,128,512]{2,1,0:T(8,128)(2,1)S(1)}, u32[]{:S(2)}, u32[]{:S(2)}) collective-permute-start(bf16[2,128,512]{2,1,0:T(8,128)(2,1)S(1)} %shard_map.102), channel_id=1, source_target_pairs={{0,7},{1,2},{2,1},{3,4},{4,3},{5,6},{6,5},{7,0},{8,15},{9,10},{10,... | collective-permute-start | bytes 786440 | tf_op jit(solution)/shard_map/ppermute | solution.py:458
  6.2 1.0 %shard_map.103 = (bf16[128,512]{1,0:T(8,128)(2,1)S(1)}, bf16[128,512]{1,0:T(8,128)(2,1)S(1)}) custom-call(bf16[256,512]{1,0:T(8,128)(2,1)} %bitcast.9, bf16[256,512]{1,0:T(8,128)(2,1)} %bitcast.12), custom_call_target="tpu_custom_call" | custom-call | flops 1000000 | bytes 4096 | tf_op jit(solution)/shard_map/pallas_call | solution.py:420
  7.2 0.1 collective-permute-start.1
  7.3 0.5 %collective-permute-start.2 = (bf16[128,512]{1,0:T(8,128)(2,1)S(1)}, bf16[128,512]{1,0:T(8,128)(2,1)S(1)}, u32[]{:S(2)}, u32[]{:S(2)}) collective-permute-start(bf16[128,512]{1,0:T(8,128)(2,1)S(1)} %get-tuple-element.49), channel_id=1, source_target_pairs={{0,1},{1,0},{2,3},{3,2},{4,5},{5,4},{6,7},{7,6},{8,9},{9,8},{10,11... | collective-permute-start | bytes 393224 | tf_op jit(solution)/shard_map/ppermute | solution.py:459
  7.8 0.8 %compare_select_fusion = f32[1,2,3]{1,0,2:T(1,128)S(1)} fusion(s32[1,16,3]{1,0,2:T(1,128)} %param.11, s32[]{:T(128)S(6)} %select_n.14), kind=kLoop, calls=%fused_computation | loop fusion | flops 12 | bytes 52 | tf_op jit(solution)/shard_map/jit(_where)/select_n | solution.py:461
  8.5 0.1 copy.11
  8.6 0.1 select_n.16
  8.7 0.1 broadcast_in_dim.27.bias
  8.8 3.0 %shard_map.101 = (bf16[256,512]{1,0:T(8,128)(2,1)S(1)}, bf16[256,512]{1,0:T(8,128)(2,1)S(1)}, bf16[256,512]{1,0:T(8,128)(2,1)S(1)}, bf16[128,1024]{1,0:T(8,128)(...) custom-call(f32[6,1,256]{2,1,0:T(1,128)S(1)} %broadcast_in_dim.27.bi, ...), custom_call_target="tpu_custom_call" | custom-call | flops 1000000 | bytes 4096 | tf_op jit(solution)/shard_map/pallas_call | solution.py:420
  11.8 0.1 collective-permute-start.4
  11.9 0.4 %collective-permute-start.5 = (bf16[128,1024]{1,0:T(8,128)(2,1)S(1)}, bf16[128,1024]{1,0:T(8,128)(2,1)S(1)}, u32[]{:S(2)}, u32[]{:S(2)}) collective-permute-start(bf16[128,1024]{1,0:T(8,128)(2,1)S(1)} %get-tuple-element.56.g_high), channel_id=1, source_target_pairs={{0,1},{1,0},{2,3},{3,2},{4,5},{5,4},{6,7},{7,6},{8,9},{9,8},{10,11... | collective-permute-start | bytes 786440 | tf_op jit(solution)/shard_map/ppermute | solution.py:485
  12.4 0.0 collective-permute-done.1.rim_k.chip_k
  12.4 0.0 collective-permute-done.2.rim_v.chip_v
  12.4 0.5 %shard_map.104 = (f32[512,128]{1,0:T(8,128)S(1)}, f32[2,4,256]{2,1,0:T(4,128)S(1)}, f32[4,128,256]{2,1,0:T(8,128)S(1)}) custom-call(f32[6,1,256]{2,1,0:T(1,128)S(1)} %broadcast_in_dim.27.bias, bf16[256,512]{1,0:T(8,128)(2,1)S(1)} %get-tuple-element.45.q, bf16[128,512]{1,0:T(8,128)(2,1)S(1)} %collective-permute-done.1.rim_k.chip_k, ...), custom_call_target="tpu_custom_call" | custom-call | flops 1000000 | bytes 4000 | tf_op jit(solution)/shard_map/pallas_call | solution.py:408
  12.9 0.0 collective-permute-done.rim.link
  12.9 0.6 %shard_map.105 = (bf16[2,512,128]{2,1,0:T(8,128)(2,1)S(1)}, bf16[4,64,256]{2,1,0:T(8,128)(2,1)S(1)}, bf16[4,64,256]{2,1,0:T(8,128)(2,1)S(1)}, f32[4,128,256]{2,1...) custom-call(f32[6,1,256]{2,1,0:T(1,128)S(1)} %broadcast_in_dim.27.bias, ...), custom_call_target="tpu_custom_call" | custom-call | flops 1000000 | bytes 4000 | tf_op jit(solution)/shard_map/pallas_call | solution.py:408
  13.5 0.1 collective-permute-start.3
  13.6 0.3 shard_map.106.product
  13.9 0.0 collective-permute-done.4.g_low
  13.9 0.0 collective-permute-done.5.g_high
  13.9 0.9 %collective-permute-done.3.other = bf16[4,64,256]{2,1,0:T(8,128)(2,1)S(1)} collective-permute-done((bf16[4,64,256]{2,1,0:T(8,128)(2,1)S(1)}, bf16[4,64,256]{2,1,0:T(8,128)(2,1)S(1)}, u32[]{:S(2)}, u32[]{:S(2)}) %collective-permute-start.3) | collective-permute-done | bytes 131104 | tf_op jit(solution)/shard_map/ppermute | solution.py:514
  14.9 0.3 shard_map.107
  15.2 1.9 %collective-permute-start.6 = (bf16[4,64,256]{2,1,0:T(8,128)(2,1)S(1)}, bf16[4,64,256]{2,1,0:T(8,128)(2,1)S(1)}, u32[]{:S(2)}, u32[]{:S(2)}) collective-permute-start(bf16[4,64,256]{2,1,0:T(8,128)(2,1)S(1)} %get-tuple-element.59), channel_id=1, source_target_pairs={{0,8},{8,0},{16,24},{24,16},{1,9},{9,1},{17,25},{25,17},{2,10},{10... | collective-permute-start | bytes 393224 | tf_op jit(solution)/shard_map/ppermute | solution.py:550
  17.1 1.5 %collective-permute-start.7 = (bf16[4,64,256]{2,1,0:T(8,128)(2,1)S(1)}, bf16[4,64,256]{2,1,0:T(8,128)(2,1)S(1)}, u32[]{:S(2)}, u32[]{:S(2)}) collective-permute-start(bf16[4,64,256]{2,1,0:T(8,128)(2,1)S(1)} %get-tuple-element.60), channel_id=1, source_target_pairs={{0,16},{8,24},{16,0},{24,8},{1,17},{9,25},{17,1},{25,9},{2,18},{10... | collective-permute-start | bytes 393224 | tf_op jit(solution)/shard_map/ppermute | solution.py:550
  18.7 0.1 collective-permute-start.8
  18.8 0.9 %shard_map.108 = (bf16[2,128,512]{2,1,0:T(8,128)(2,1)S(1)}, bf16[2,128,512]{2,1,0:T(8,128)(2,1)S(1)}, f32[2,4,256]{2,1,0:T(4,128)S(1)}, f32[2,512,128]{2,1,0:T(8,128)S(1)}) custom-call(bf16[256,512]{1,0:T(8,128)(2,1)S(1)} %get-tuple-element.45.q, bf16[2,128,512]{2,1,0:T(8,128)(2,1)S(1)} %collective-permute-done.rim.link, ...), custom_call_target="tpu_custom_call" | custom-call | flops 1000000 | bytes 4000 | tf_op jit(solution)/shard_map/pallas_call | solution.py:408
  19.7 1.4 %collective-permute-start.9 = (bf16[2,128,512]{2,1,0:T(8,128)(2,1)S(1)}, bf16[2,128,512]{2,1,0:T(8,128)(2,1)S(1)}, u32[]{:S(2)}, u32[]{:S(2)}) collective-permute-start(bf16[2,128,512]{2,1,0:T(8,128)(2,1)S(1)} %get-tuple-element.78), channel_id=1, source_target_pairs={{0,7},{1,2},{2,1},{3,4},{4,3},{5,6},{6,5},{7,0},{8,15},{9,10},{10,... | collective-permute-start | bytes 786440 | tf_op jit(solution)/shard_map/ppermute | solution.py:535
  21.1 2.1 %shard_map.109 = (bf16[256,512]{1,0:T(8,128)(2,1)}, f32[256,512]{1,0:T(8,128)S(1)}, f32[256,512]{1,0:T(8,128)S(1)}, f32[8,128]{1,0:T(8,128)S(1)}) custom-call(bf16[256,512]{1,0:T(8,128)(2,1)S(1)} %get-tuple-element.45.q, bf16[256,512]{1,0:T(8,128)(2,1)S(1)} %get-tuple-element.62.k, bf16[256,512]{1,0:T(8,128)(2,1)S(1)} %get-tuple-element.63.v, ...), custom_call_target="tpu_custom_call" | custom-call | flops 5000000000 | bytes 20000000 | tf_op jit(solution)/shard_map/pallas_call | solution.py:408
  23.2 0.0 collective-permute-done.6.refs_1_
  23.2 2.0 %collective-permute-done.7.refs_2_ = bf16[4,64,256]{2,1,0:T(8,128)(2,1)S(1)} collective-permute-done((bf16[4,64,256]{2,1,0:T(8,128)(2,1)S(1)}, bf16[4,64,256]{2,1,0:T(8,128)(2,1)S(1)}, u32[]{:S(2)}, u32[]{:S(2)}) %collective-permute-start.7) | collective-permute-done | bytes 131104 | tf_op jit(solution)/shard_map/ppermute | solution.py:550
  25.2 0.0 collective-permute-done.8.refs_3_
  25.2 0.1 shard_map.110
  25.3 1.1 %collective-permute-start.11 = (bf16[64,256]{1,0:T(8,128)(2,1)S(1)}, bf16[64,256]{1,0:T(8,128)(2,1)S(1)}, u32[]{:S(2)}, u32[]{:S(2)}) collective-permute-start(bf16[64,256]{1,0:T(8,128)(2,1)S(1)} %get-tuple-element.82), channel_id=1, source_target_pairs={{0,4},{1,5},{2,6},{3,7},{4,0},{5,1},{6,2},{7,3},{8,12},{9,13},{10,... | collective-permute-start | bytes 98312 | tf_op jit(solution)/shard_map/ppermute | solution.py:554
  26.4 1.1 %collective-permute-start.12 = (bf16[64,256]{1,0:T(8,128)(2,1)S(1)}, bf16[64,256]{1,0:T(8,128)(2,1)S(1)}, u32[]{:S(2)}, u32[]{:S(2)}) collective-permute-start(bf16[64,256]{1,0:T(8,128)(2,1)S(1)} %get-tuple-element.83), channel_id=1, source_target_pairs={{0,6},{1,7},{2,4},{3,5},{4,2},{5,3},{6,0},{7,1},{8,14},{9,15},{10,... | collective-permute-start | bytes 98312 | tf_op jit(solution)/shard_map/ppermute | solution.py:554
  27.5 1.3 %collective-permute-start.13 = (bf16[64,256]{1,0:T(8,128)(2,1)S(1)}, bf16[64,256]{1,0:T(8,128)(2,1)S(1)}, u32[]{:S(2)}, u32[]{:S(2)}) collective-permute-start(bf16[64,256]{1,0:T(8,128)(2,1)S(1)} %get-tuple-element.84), channel_id=1, source_target_pairs={{0,2},{1,3},{2,0},{3,1},{4,6},{5,7},{6,4},{7,5},{8,10},{9,11},{10,... | collective-permute-start | bytes 98312 | tf_op jit(solution)/shard_map/ppermute | solution.py:554
  28.8 0.0 collective-permute-start.10
  28.8 2.2 %collective-permute-done.11.refs_1_ = bf16[64,256]{1,0:T(8,128)(2,1)S(1)} collective-permute-done((bf16[64,256]{1,0:T(8,128)(2,1)S(1)}, bf16[64,256]{1,0:T(8,128)(2,1)S(1)}, u32[]{:S(2)}, u32[]{:S(2)}) %collective-permute-start.11) | collective-permute-done | bytes 32800 | tf_op jit(solution)/shard_map/ppermute | solution.py:554
  31.1 1.0 %collective-permute-done.12.refs_2_ = bf16[64,256]{1,0:T(8,128)(2,1)S(1)} collective-permute-done((bf16[64,256]{1,0:T(8,128)(2,1)S(1)}, bf16[64,256]{1,0:T(8,128)(2,1)S(1)}, u32[]{:S(2)}, u32[]{:S(2)}) %collective-permute-start.12) | collective-permute-done | bytes 32800 | tf_op jit(solution)/shard_map/ppermute | solution.py:554
  32.2 1.9 %collective-permute-start.14 = (bf16[64,256]{1,0:T(8,128)(2,1)S(1)}, bf16[64,256]{1,0:T(8,128)(2,1)S(1)}, u32[]{:S(2)}, u32[]{:S(2)}) collective-permute-start(bf16[64,256]{1,0:T(8,128)(2,1)S(1)} %shard_map.113.refs_0_), channel_id=1, source_target_pairs={{0,24},{8,16},{16,8},{24,0},{1,25},{9,17},{17,9},{25,1},{2,26},{10... | collective-permute-start | bytes 98312 | tf_op jit(solution)/shard_map/ppermute | solution.py:563
  34.0 1.0 %collective-permute-start.15 = (bf16[64,256]{1,0:T(8,128)(2,1)S(1)}, bf16[64,256]{1,0:T(8,128)(2,1)S(1)}, u32[]{:S(2)}, u32[]{:S(2)}) collective-permute-start(bf16[64,256]{1,0:T(8,128)(2,1)S(1)} %shard_map.113.refs_0_), channel_id=1, source_target_pairs={{0,16},{8,24},{16,0},{24,8},{1,17},{9,25},{17,1},{25,9},{2,18},{10... | collective-permute-start | bytes 98312 | tf_op jit(solution)/shard_map/ppermute | solution.py:563
  35.0 0.7 %collective-permute-start.16 = (bf16[64,256]{1,0:T(8,128)(2,1)S(1)}, bf16[64,256]{1,0:T(8,128)(2,1)S(1)}, u32[]{:S(2)}, u32[]{:S(2)}) collective-permute-start(bf16[64,256]{1,0:T(8,128)(2,1)S(1)} %shard_map.113.refs_0_), channel_id=1, source_target_pairs={{0,8},{8,0},{16,24},{24,16},{1,9},{9,1},{17,25},{25,17},{2,10},{10... | collective-permute-start | bytes 98312 | tf_op jit(solution)/shard_map/ppermute | solution.py:563
  35.7 1.3 %shard_map.111 = bf16[256,1024]{1,0:T(8,128)(2,1)} custom-call(bf16[2,512,128]{2,1,0:T(8,128)(2,1)S(1)} %get-tuple-element.52.attn_t, bf16[512,1024]{1,0:T(8,128)(2,1)S(1)} %get-tuple-element.53.w_out, bf16[64,256]{1,0:T(8,128)(2,1)S(1)} %get-tuple-element.74.before.refs_0_), custom_call_target="tpu_custom_call" | custom-call | flops 5000000000 | bytes 20000000 | tf_op jit(solution)/shard_map/pallas_call | solution.py:408
  37.0 0.0 collective-permute-done.10.chip_kv
  37.0 0.9 %shard_map.112 = (bf16[256,512]{1,0:T(8,128)(2,1)}, bf16[256,512]{1,0:T(8,128)(2,1)}) custom-call(f32[256,512]{1,0:T(8,128)S(1)} %get-tuple-element.76.k_own, f32[256,512]{1,0:T(8,128)S(1)} %get-tuple-element.77.v_own, bf16[2,128,512]{2,1,0:T(8,128)(2,1)S(1)} %collective-permute-done.9.link_kv.refs_4_, bf16[2,128,512]{2,1,0:T(8,128)(2,1)S(1)} %collective-permute-done.10.chip_kv), custom_call_target="tpu_custom_call" | custom-call | flops 1000000 | bytes 4000 | tf_op jit(solution)/shard_map/pallas_call | solution.py:408
  37.9 0.1 collective-permute-done.15.refs_2_
  37.9 1.0 %collective-permute-done.16.refs_3_ = bf16[64,256]{1,0:T(8,128)(2,1)S(1)} collective-permute-done((bf16[64,256]{1,0:T(8,128)(2,1)S(1)}, bf16[64,256]{1,0:T(8,128)(2,1)S(1)}, u32[]{:S(2)}, u32[]{:S(2)}) %collective-permute-start.16) | collective-permute-done | bytes 32800 | tf_op jit(solution)/shard_map/ppermute | solution.py:563
  39.0 0.7 %shard_map.114 = f32[64,1024]{1,0:T(8,128)} custom-call(bf16[64,256]{1,0:T(8,128)(2,1)S(1)} %shard_map.113.refs_0_, bf16[64,256]{1,0:T(8,128)(2,1)S(1)} %collective-permute-done.14.refs_1_, bf16[64,256]{1,0:T(8,128)(2,1)S(1)} %collective-permute-done.15.refs_2_, bf16[64,256]{1,0:T(8,128)(2,1)S(1)} %collective-permute-done.16.refs_3_), custom_call_target="tpu_custom_call" | custom-call | flops 1000000 | bytes 4000 | tf_op jit(solution)/shard_map/pallas_call | solution.py:408
  (4 shorter events, 0.0 us)
Async XLA Ops:
  1.6 11.3 %collective-permute-start = (bf16[2,128,512]{2,1,0:T(8,128)(2,1)S(1)}, bf16[2,128,512]{2,1,0:T(8,128)(2,1)S(1)}, u32[]{:S(2)}, u32[]{:S(2)}) collective-permute-start(bf16[2,128,512]{2,1,0:T(8,128)(2,1)S(1)} %shard_map.102), channel_id=1, source_target_pairs={{0,7},{1,2},{2,1},{3,4},{4,3},{5,6},{6,5},{7,0},{8,15},{9,10},{10,... | collective-permute-start | bytes 786440 | tf_op jit(solution)/shard_map/ppermute | solution.py:458
  7.2 5.2 %collective-permute-start.1 = (bf16[128,512]{1,0:T(8,128)(2,1)S(1)}, bf16[128,512]{1,0:T(8,128)(2,1)S(1)}, u32[]{:S(2)}, u32[]{:S(2)}) collective-permute-start(bf16[128,512]{1,0:T(8,128)(2,1)S(1)} %get-tuple-element.48), channel_id=1, source_target_pairs={{0,1},{1,0},{2,3},{3,2},{4,5},{5,4},{6,7},{7,6},{8,9},{9,8},{10,11... | collective-permute-start | bytes 393224 | tf_op jit(solution)/shard_map/ppermute | solution.py:459
  7.3 5.1 %collective-permute-start.2 = (bf16[128,512]{1,0:T(8,128)(2,1)S(1)}, bf16[128,512]{1,0:T(8,128)(2,1)S(1)}, u32[]{:S(2)}, u32[]{:S(2)}) collective-permute-start(bf16[128,512]{1,0:T(8,128)(2,1)S(1)} %get-tuple-element.49), channel_id=1, source_target_pairs={{0,1},{1,0},{2,3},{3,2},{4,5},{5,4},{6,7},{7,6},{8,9},{9,8},{10,11... | collective-permute-start | bytes 393224 | tf_op jit(solution)/shard_map/ppermute | solution.py:459
  11.8 2.1 %collective-permute-start.4 = (bf16[128,1024]{1,0:T(8,128)(2,1)S(1)}, bf16[128,1024]{1,0:T(8,128)(2,1)S(1)}, u32[]{:S(2)}, u32[]{:S(2)}) collective-permute-start(bf16[128,1024]{1,0:T(8,128)(2,1)S(1)} %get-tuple-element.55.g_low), channel_id=1, source_target_pairs={{0,1},{1,0},{2,3},{3,2},{4,5},{5,4},{6,7},{7,6},{8,9},{9,8},{10,11... | collective-permute-start | bytes 786440 | tf_op jit(solution)/shard_map/ppermute | solution.py:485
  11.9 2.0 %collective-permute-start.5 = (bf16[128,1024]{1,0:T(8,128)(2,1)S(1)}, bf16[128,1024]{1,0:T(8,128)(2,1)S(1)}, u32[]{:S(2)}, u32[]{:S(2)}) collective-permute-start(bf16[128,1024]{1,0:T(8,128)(2,1)S(1)} %get-tuple-element.56.g_high), channel_id=1, source_target_pairs={{0,1},{1,0},{2,3},{3,2},{4,5},{5,4},{6,7},{7,6},{8,9},{9,8},{10,11... | collective-permute-start | bytes 786440 | tf_op jit(solution)/shard_map/ppermute | solution.py:485
  13.5 1.4 %collective-permute-start.3 = (bf16[4,64,256]{2,1,0:T(8,128)(2,1)S(1)}, bf16[4,64,256]{2,1,0:T(8,128)(2,1)S(1)}, u32[]{:S(2)}, u32[]{:S(2)}) collective-permute-start(bf16[4,64,256]{2,1,0:T(8,128)(2,1)S(1)} %get-tuple-element.57), channel_id=1, source_target_pairs={{0,1},{1,0},{2,3},{3,2},{4,5},{5,4},{6,7},{7,6},{8,9},{9,8},{10,11... | collective-permute-start | bytes 393224 | tf_op jit(solution)/shard_map/ppermute | solution.py:514
  15.2 8.0 %collective-permute-start.6 = (bf16[4,64,256]{2,1,0:T(8,128)(2,1)S(1)}, bf16[4,64,256]{2,1,0:T(8,128)(2,1)S(1)}, u32[]{:S(2)}, u32[]{:S(2)}) collective-permute-start(bf16[4,64,256]{2,1,0:T(8,128)(2,1)S(1)} %get-tuple-element.59), channel_id=1, source_target_pairs={{0,8},{8,0},{16,24},{24,16},{1,9},{9,1},{17,25},{25,17},{2,10},{10... | collective-permute-start | bytes 393224 | tf_op jit(solution)/shard_map/ppermute | solution.py:550
  17.1 8.1 %collective-permute-start.7 = (bf16[4,64,256]{2,1,0:T(8,128)(2,1)S(1)}, bf16[4,64,256]{2,1,0:T(8,128)(2,1)S(1)}, u32[]{:S(2)}, u32[]{:S(2)}) collective-permute-start(bf16[4,64,256]{2,1,0:T(8,128)(2,1)S(1)} %get-tuple-element.60), channel_id=1, source_target_pairs={{0,16},{8,24},{16,0},{24,8},{1,17},{9,25},{17,1},{25,9},{2,18},{10... | collective-permute-start | bytes 393224 | tf_op jit(solution)/shard_map/ppermute | solution.py:550
  18.7 6.5 %collective-permute-start.8 = (bf16[4,64,256]{2,1,0:T(8,128)(2,1)S(1)}, bf16[4,64,256]{2,1,0:T(8,128)(2,1)S(1)}, u32[]{:S(2)}, u32[]{:S(2)}) collective-permute-start(bf16[4,64,256]{2,1,0:T(8,128)(2,1)S(1)} %get-tuple-element.61), channel_id=1, source_target_pairs={{0,24},{8,16},{16,8},{24,0},{1,25},{9,17},{17,9},{25,1},{2,26},{10... | collective-permute-start | bytes 393224 | tf_op jit(solution)/shard_map/ppermute | solution.py:550
  19.7 12.5 %collective-permute-start.9 = (bf16[2,128,512]{2,1,0:T(8,128)(2,1)S(1)}, bf16[2,128,512]{2,1,0:T(8,128)(2,1)S(1)}, u32[]{:S(2)}, u32[]{:S(2)}) collective-permute-start(bf16[2,128,512]{2,1,0:T(8,128)(2,1)S(1)} %get-tuple-element.78), channel_id=1, source_target_pairs={{0,7},{1,2},{2,1},{3,4},{4,3},{5,6},{6,5},{7,0},{8,15},{9,10},{10,... | collective-permute-start | bytes 786440 | tf_op jit(solution)/shard_map/ppermute | solution.py:535
  25.3 5.8 %collective-permute-start.11 = (bf16[64,256]{1,0:T(8,128)(2,1)S(1)}, bf16[64,256]{1,0:T(8,128)(2,1)S(1)}, u32[]{:S(2)}, u32[]{:S(2)}) collective-permute-start(bf16[64,256]{1,0:T(8,128)(2,1)S(1)} %get-tuple-element.82), channel_id=1, source_target_pairs={{0,4},{1,5},{2,6},{3,7},{4,0},{5,1},{6,2},{7,3},{8,12},{9,13},{10,... | collective-permute-start | bytes 98312 | tf_op jit(solution)/shard_map/ppermute | solution.py:554
  26.4 5.7 %collective-permute-start.12 = (bf16[64,256]{1,0:T(8,128)(2,1)S(1)}, bf16[64,256]{1,0:T(8,128)(2,1)S(1)}, u32[]{:S(2)}, u32[]{:S(2)}) collective-permute-start(bf16[64,256]{1,0:T(8,128)(2,1)S(1)} %get-tuple-element.83), channel_id=1, source_target_pairs={{0,6},{1,7},{2,4},{3,5},{4,2},{5,3},{6,0},{7,1},{8,14},{9,15},{10,... | collective-permute-start | bytes 98312 | tf_op jit(solution)/shard_map/ppermute | solution.py:554
  27.5 4.6 %collective-permute-start.13 = (bf16[64,256]{1,0:T(8,128)(2,1)S(1)}, bf16[64,256]{1,0:T(8,128)(2,1)S(1)}, u32[]{:S(2)}, u32[]{:S(2)}) collective-permute-start(bf16[64,256]{1,0:T(8,128)(2,1)S(1)} %get-tuple-element.84), channel_id=1, source_target_pairs={{0,2},{1,3},{2,0},{3,1},{4,6},{5,7},{6,4},{7,5},{8,10},{9,11},{10,... | collective-permute-start | bytes 98312 | tf_op jit(solution)/shard_map/ppermute | solution.py:554
  28.8 8.1 %collective-permute-start.10 = (bf16[2,128,512]{2,1,0:T(8,128)(2,1)S(1)}, bf16[2,128,512]{2,1,0:T(8,128)(2,1)S(1)}, u32[]{:S(2)}, u32[]{:S(2)}) collective-permute-start(bf16[2,128,512]{2,1,0:T(8,128)(2,1)S(1)} %get-tuple-element.79), channel_id=1, source_target_pairs={{0,1},{1,0},{2,3},{3,2},{4,5},{5,4},{6,7},{7,6},{8,9},{9,8},{10,11... | collective-permute-start | bytes 786440 | tf_op jit(solution)/shard_map/ppermute | solution.py:536
  32.2 5.7 %collective-permute-start.14 = (bf16[64,256]{1,0:T(8,128)(2,1)S(1)}, bf16[64,256]{1,0:T(8,128)(2,1)S(1)}, u32[]{:S(2)}, u32[]{:S(2)}) collective-permute-start(bf16[64,256]{1,0:T(8,128)(2,1)S(1)} %shard_map.113.refs_0_), channel_id=1, source_target_pairs={{0,24},{8,16},{16,8},{24,0},{1,25},{9,17},{17,9},{25,1},{2,26},{10... | collective-permute-start | bytes 98312 | tf_op jit(solution)/shard_map/ppermute | solution.py:563
  34.0 3.9 %collective-permute-start.15 = (bf16[64,256]{1,0:T(8,128)(2,1)S(1)}, bf16[64,256]{1,0:T(8,128)(2,1)S(1)}, u32[]{:S(2)}, u32[]{:S(2)}) collective-permute-start(bf16[64,256]{1,0:T(8,128)(2,1)S(1)} %shard_map.113.refs_0_), channel_id=1, source_target_pairs={{0,16},{8,24},{16,0},{24,8},{1,17},{9,25},{17,1},{25,9},{2,18},{10... | collective-permute-start | bytes 98312 | tf_op jit(solution)/shard_map/ppermute | solution.py:563
  35.0 3.9 %collective-permute-start.16 = (bf16[64,256]{1,0:T(8,128)(2,1)S(1)}, bf16[64,256]{1,0:T(8,128)(2,1)S(1)}, u32[]{:S(2)}, u32[]{:S(2)}) collective-permute-start(bf16[64,256]{1,0:T(8,128)(2,1)S(1)} %shard_map.113.refs_0_), channel_id=1, source_target_pairs={{0,8},{8,0},{16,24},{24,16},{1,9},{9,1},{17,25},{25,17},{2,10},{10... | collective-permute-start | bytes 98312 | tf_op jit(solution)/shard_map/ppermute | solution.py:563

commit v19 on v18

--- a/solution.py
+++ b/solution.py
@@ -253,7 +253,7 @@
 
 
 def rim_kernel(
-    q, link, chip_k, chip_v, grad_t, attn_t, link_exps, chip_exps, rim_factors, before,
+    q, link, chip_k, chip_v, grad_t, attn_t, link_exps, chip_exps, rim_factors,
     link_back, chip_back, deltas, query_t, dprobs, dscores, rounded,
 ):
     blocks = q.shape[0] // BLK
@@ -292,7 +292,7 @@
 
 
 def own_backward_kernel(
-    q, k, v, grad_t, exps, factors, deltas, rim_t,
+    q, k, v, grad_t, exps, factors, deltas, rim_t, before,
     q_grad, k_own, v_own, after, dprobs, dscores, rounded,
 ):
     blocks = q.shape[0] // BLK
@@ -327,13 +327,17 @@
     after[...] = jnp.zeros_like(after)
 
 
+def send_kernel(back, before, out):
+    out[...] = back[...]
+
+
 def output_kernel(attn_t, w_out, before, output):
     for b in range(attn_t.shape[0]):
         part = dot(attn_t[b], w_out[...], ((0,), (0,)))
         output[b * BLK : (b + 1) * BLK] = part.astype(BF16)
 
 
-def halves_kernel(product, other, g_low, g_high, *outs):
+def halves_kernel(product, other, g_low, g_high, before, *outs):
     pieces, after = outs[:-1], outs[-1]
     at_dp = lax.axis_index("dp")
     chips, rows, cols = pieces[0].shape
@@ -514,12 +518,6 @@
     other = lax.ppermute(other, "ctx", swap(ctx, 1))
     other = pltpu.with_memory_space_constraint(other, pltpu.VMEM)
     (product,) = call(product_kernel, [vmem(chips * rows, width, dtype=F32)], 10**6, mine, g_low, g_high)
-    *halves, after = call(
-        halves_kernel,
-        [vmem(chips, rows, cols)] * dp + [vmem(8, 128, dtype=F32)],
-        10**6,
-        product, other, *sibling_g,
-    )
     *back, deltas, rim_t = call(
         rim_kernel,
         [
@@ -529,10 +527,17 @@
             vmem(blocks, feats, BLK, dtype=F32),
         ],
         10**6,
-        q, link, chip_k, chip_v, grad_t, attn_t, link_exps, chip_exps, rim_factors, after,
+        q, link, chip_k, chip_v, grad_t, attn_t, link_exps, chip_exps, rim_factors,
         scratch=[vmem(2, *rim_scores, dtype=F32), vmem(2, *rim_scores), vmem(2, *rim_scores)],
     )
-    link_back = lax.ppermute(back[0], "ctx", over_links(ctx))
+    *halves, after = call(
+        halves_kernel,
+        [vmem(chips, rows, cols)] * dp + [vmem(8, 128, dtype=F32)],
+        10**6,
+        product, other, *sibling_g, deltas,
+    )
+    (to_link,) = call(send_kernel, [vmem(2, RIM, feats)], 10**6, back[0], after)
+    link_back = lax.ppermute(to_link, "ctx", over_links(ctx))
     chip_back = lax.ppermute(back[1], "ctx", swap(ctx, 1))
     q_grad, k_own, v_own, after = call(
         own_backward_kernel,
@@ -543,7 +548,7 @@
             vmem(8, 128, dtype=F32),
         ],
         5 * 10**9,
-        q, k, v, grad_t, own_exps, own_factors, deltas, rim_t,
+        q, k, v, grad_t, own_exps, own_factors, deltas, rim_t, to_link,
         scratch=[vmem(*own_scores, dtype=F32), vmem(*own_scores), vmem(*own_scores)],
     )
 

time: 39.9 us -> 40 us (level)
    ppermute x1, waiting for transfers between devices: 0.95 us -> 0.04 us  [body(): other = lax.ppermute(other, 'ctx', swap(ctx, 1))]
    ppermute x3, waiting for transfers between devices: 2 us -> 2.86 us  [body(): lax.ppermute(halves[s], 'dp', swap(dp, s))]
    pallas_call x11 -> x12, Pallas kernels: 7.71 us -> 7.74 us  [call(): pl.pallas_call(kernel, out_shape=outs, in_specs=[in_vmem] * len(args), ou...]
  transfers between devices with their start and end apart: 17 -> 17, of which waited for: 6 -> 4; matrix products, arithmetic and copies ran while one was open for 3% -> 3% of each run, Pallas kernels for 27% -> 27%
where the time goes in v19:
time: 40 us; the launch traced here: 39.9 us
  starting transfers between devices  18.2 us (46%)
  Pallas kernels  12.7 us (32%)
  waiting for transfers between devices  7.16 us (18%)
  other arithmetic  0.75 us (2%)
  between operations  0.74 us (2%)
    pallas_call x12, Pallas kernels, call(): pl.pallas_call(kernel, out_shape=outs, in_specs=[in_vmem] * len(args), ou...  7.74 us
    pallas_call x3, Pallas kernels, call_on_hbm(): pl.pallas_call(kernel, out_shape=outs, in_specs=[pl.BlockSpec(memory_spac...  4.99 us
    ppermute x1, starting transfers between devices, body(): link = lax.ppermute(to_link, 'ctx', over_links(ctx))  4.55 us
    ppermute x3, starting transfers between devices, body(): lax.ppermute(piece, 'dp', swap(dp, s))  3.55 us
    ppermute x3, starting transfers between devices, body(): lax.ppermute(quarters[s], 'ctx', swap(ctx, 2 * s))  3.55 us
    ppermute x3, starting transfers between devices, body(): lax.ppermute(halves[s], 'dp', swap(dp, s))  3.55 us
    ppermute x3, waiting for transfers between devices, body(): lax.ppermute(quarters[s], 'ctx', swap(ctx, 2 * s))  3.29 us
    ppermute x3, waiting for transfers between devices, body(): lax.ppermute(halves[s], 'dp', swap(dp, s))  2.86 us
  transfers between devices with their start and end apart: 17, of which 4 were waited for; matrix products, arithmetic and copies ran while one was open for 3% of the time, Pallas kernels for 27%

profile of v19, /device:TPU:0, one launch (start us, length us, event | category | flops | bytes accessed | tf_op | source)
XLA Modules:
  0.0 39.9 jit_solution(1313273438127330068)
XLA Ops:
  0.6 1.0 %shard_map.102 = bf16[2,128,512]{2,1,0:T(8,128)(2,1)S(1)} custom-call(bf16[256,512]{1,0:T(8,128)(2,1)} %bitcast.8, bf16[256,512]{1,0:T(8,128)(2,1)} %bitcast.11), custom_call_target="tpu_custom_call" | custom-call | flops 1000000 | bytes 4096 | tf_op jit(solution)/shard_map/pallas_call | solution.py:424
  1.6 4.6 %collective-permute-start = (bf16[2,128,512]{2,1,0:T(8,128)(2,1)S(1)}, bf16[2,128,512]{2,1,0:T(8,128)(2,1)S(1)}, u32[]{:S(2)}, u32[]{:S(2)}) collective-permute-start(bf16[2,128,512]{2,1,0:T(8,128)(2,1)S(1)} %shard_map.102), channel_id=1, source_target_pairs={{0,7},{1,2},{2,1},{3,4},{4,3},{5,6},{6,5},{7,0},{8,15},{9,10},{10,... | collective-permute-start | bytes 786440 | tf_op jit(solution)/shard_map/ppermute | solution.py:462
  6.2 1.0 %shard_map.103 = (bf16[128,512]{1,0:T(8,128)(2,1)S(1)}, bf16[128,512]{1,0:T(8,128)(2,1)S(1)}) custom-call(bf16[256,512]{1,0:T(8,128)(2,1)} %bitcast.9, bf16[256,512]{1,0:T(8,128)(2,1)} %bitcast.12), custom_call_target="tpu_custom_call" | custom-call | flops 1000000 | bytes 4096 | tf_op jit(solution)/shard_map/pallas_call | solution.py:424
  7.2 0.1 collective-permute-start.1
  7.3 0.5 %collective-permute-start.2 = (bf16[128,512]{1,0:T(8,128)(2,1)S(1)}, bf16[128,512]{1,0:T(8,128)(2,1)S(1)}, u32[]{:S(2)}, u32[]{:S(2)}) collective-permute-start(bf16[128,512]{1,0:T(8,128)(2,1)S(1)} %get-tuple-element.49), channel_id=1, source_target_pairs={{0,1},{1,0},{2,3},{3,2},{4,5},{5,4},{6,7},{7,6},{8,9},{9,8},{10,11... | collective-permute-start | bytes 393224 | tf_op jit(solution)/shard_map/ppermute | solution.py:463
  7.8 0.8 %compare_select_fusion = f32[1,2,3]{1,0,2:T(1,128)S(1)} fusion(s32[1,16,3]{1,0,2:T(1,128)} %param.11, s32[]{:T(128)S(6)} %select_n.14), kind=kLoop, calls=%fused_computation | loop fusion | flops 12 | bytes 52 | tf_op jit(solution)/shard_map/jit(_where)/select_n | solution.py:465
  8.5 0.1 copy.11
  8.6 0.1 select_n.16
  8.7 0.1 broadcast_in_dim.27.bias
  8.8 3.0 %shard_map.101 = (bf16[256,512]{1,0:T(8,128)(2,1)S(1)}, bf16[256,512]{1,0:T(8,128)(2,1)S(1)}, bf16[256,512]{1,0:T(8,128)(2,1)S(1)}, bf16[128,1024]{1,0:T(8,128)(...) custom-call(f32[6,1,256]{2,1,0:T(1,128)S(1)} %broadcast_in_dim.27.bi, ...), custom_call_target="tpu_custom_call" | custom-call | flops 1000000 | bytes 4096 | tf_op jit(solution)/shard_map/pallas_call | solution.py:424
  11.8 0.2 collective-permute-start.4
  11.9 0.4 %collective-permute-start.5 = (bf16[128,1024]{1,0:T(8,128)(2,1)S(1)}, bf16[128,1024]{1,0:T(8,128)(2,1)S(1)}, u32[]{:S(2)}, u32[]{:S(2)}) collective-permute-start(bf16[128,1024]{1,0:T(8,128)(2,1)S(1)} %get-tuple-element.56.g_high), channel_id=1, source_target_pairs={{0,1},{1,0},{2,3},{3,2},{4,5},{5,4},{6,7},{7,6},{8,9},{9,8},{10,11... | collective-permute-start | bytes 786440 | tf_op jit(solution)/shard_map/ppermute | solution.py:489
  12.4 0.0 collective-permute-done.1.rim_k.chip_k
  12.4 0.0 collective-permute-done.2.rim_v.chip_v
  12.4 0.5 %shard_map.104 = (f32[512,128]{1,0:T(8,128)S(1)}, f32[2,4,256]{2,1,0:T(4,128)S(1)}, f32[4,128,256]{2,1,0:T(8,128)S(1)}) custom-call(f32[6,1,256]{2,1,0:T(1,128)S(1)} %broadcast_in_dim.27.bias, bf16[256,512]{1,0:T(8,128)(2,1)S(1)} %get-tuple-element.45.q, bf16[128,512]{1,0:T(8,128)(2,1)S(1)} %collective-permute-done.1.rim_k.chip_k, ...), custom_call_target="tpu_custom_call" | custom-call | flops 1000000 | bytes 4000 | tf_op jit(solution)/shard_map/pallas_call | solution.py:412
  12.9 0.0 collective-permute-done.rim.link
  12.9 0.6 %shard_map.105 = (bf16[2,512,128]{2,1,0:T(8,128)(2,1)S(1)}, bf16[4,64,256]{2,1,0:T(8,128)(2,1)S(1)}, bf16[4,64,256]{2,1,0:T(8,128)(2,1)S(1)}, f32[4,128,256]{2,1...) custom-call(f32[6,1,256]{2,1,0:T(1,128)S(1)} %broadcast_in_dim.27.bias, ...), custom_call_target="tpu_custom_call" | custom-call | flops 1000000 | bytes 4000 | tf_op jit(solution)/shard_map/pallas_call | solution.py:412
  13.5 0.2 collective-permute-start.3
  13.6 0.3 shard_map.106.product
  13.9 0.9 %shard_map.107 = (bf16[2,128,512]{2,1,0:T(8,128)(2,1)S(1)}, bf16[2,128,512]{2,1,0:T(8,128)(2,1)S(1)}, f32[2,4,256]{2,1,0:T(4,128)S(1)}, f32[2,512,128]{2,1,0:T(8,128)S(1)}) custom-call(bf16[256,512]{1,0:T(8,128)(2,1)S(1)} %get-tuple-element.45.q, bf16[2,128,512]{2,1,0:T(8,128)(2,1)S(1)} %collective-permute-done.rim.link, ...), custom_call_target="tpu_custom_call" | custom-call | flops 1000000 | bytes 4000 | tf_op jit(solution)/shard_map/pallas_call | solution.py:412
  14.8 0.0 collective-permute-done.4.g_low
  14.8 0.0 collective-permute-done.5.g_high
  14.8 0.0 collective-permute-done.3.other
  14.9 0.3 shard_map.108
  15.2 1.9 %collective-permute-start.6 = (bf16[4,64,256]{2,1,0:T(8,128)(2,1)S(1)}, bf16[4,64,256]{2,1,0:T(8,128)(2,1)S(1)}, u32[]{:S(2)}, u32[]{:S(2)}) collective-permute-start(bf16[4,64,256]{2,1,0:T(8,128)(2,1)S(1)} %get-tuple-element.64), channel_id=1, source_target_pairs={{0,8},{8,0},{16,24},{24,16},{1,9},{9,1},{17,25},{25,17},{2,10},{10... | collective-permute-start | bytes 393224 | tf_op jit(solution)/shard_map/ppermute | solution.py:555
  17.1 1.5 %collective-permute-start.7 = (bf16[4,64,256]{2,1,0:T(8,128)(2,1)S(1)}, bf16[4,64,256]{2,1,0:T(8,128)(2,1)S(1)}, u32[]{:S(2)}, u32[]{:S(2)}) collective-permute-start(bf16[4,64,256]{2,1,0:T(8,128)(2,1)S(1)} %get-tuple-element.65), channel_id=1, source_target_pairs={{0,16},{8,24},{16,0},{24,8},{1,17},{9,25},{17,1},{25,9},{2,18},{10... | collective-permute-start | bytes 393224 | tf_op jit(solution)/shard_map/ppermute | solution.py:555
  18.7 0.1 collective-permute-start.8
  18.8 1.7 %collective-permute-start.9 = (bf16[2,128,512]{2,1,0:T(8,128)(2,1)S(1)}, bf16[2,128,512]{2,1,0:T(8,128)(2,1)S(1)}, u32[]{:S(2)}, u32[]{:S(2)}) collective-permute-start(bf16[2,128,512]{2,1,0:T(8,128)(2,1)S(1)} %shard_map.109.before), channel_id=1, source_target_pairs={{0,7},{1,2},{2,1},{3,4},{4,3},{5,6},{6,5},{7,0},{8,15},{9,10},{10,... | collective-permute-start | bytes 786440 | tf_op jit(solution)/shard_map/ppermute | solution.py:540
  20.5 2.1 %shard_map.110 = (bf16[256,512]{1,0:T(8,128)(2,1)}, f32[256,512]{1,0:T(8,128)S(1)}, f32[256,512]{1,0:T(8,128)S(1)}, f32[8,128]{1,0:T(8,128)S(1)}) custom-call(bf16[256,512]{1,0:T(8,128)(2,1)S(1)} %get-tuple-element.45.q, bf16[256,512]{1,0:T(8,128)(2,1)S(1)} %get-tuple-element.67.k, bf16[256,512]{1,0:T(8,128)(2,1)S(1)} %get-tuple-element.68.v, ...), custom_call_target="tpu_custom_call" | custom-call | flops 5000000000 | bytes 20000000 | tf_op jit(solution)/shard_map/pallas_call | solution.py:412
  22.6 0.0 collective-permute-done.6.refs_1_
  22.6 2.9 %collective-permute-done.7.refs_2_ = bf16[4,64,256]{2,1,0:T(8,128)(2,1)S(1)} collective-permute-done((bf16[4,64,256]{2,1,0:T(8,128)(2,1)S(1)}, bf16[4,64,256]{2,1,0:T(8,128)(2,1)S(1)}, u32[]{:S(2)}, u32[]{:S(2)}) %collective-permute-start.7) | collective-permute-done | bytes 131104 | tf_op jit(solution)/shard_map/ppermute | solution.py:555
  25.5 0.0 collective-permute-done.8.refs_3_
  25.5 0.1 shard_map.111
  25.6 1.1 %collective-permute-start.11 = (bf16[64,256]{1,0:T(8,128)(2,1)S(1)}, bf16[64,256]{1,0:T(8,128)(2,1)S(1)}, u32[]{:S(2)}, u32[]{:S(2)}) collective-permute-start(bf16[64,256]{1,0:T(8,128)(2,1)S(1)} %get-tuple-element.82), channel_id=1, source_target_pairs={{0,4},{1,5},{2,6},{3,7},{4,0},{5,1},{6,2},{7,3},{8,12},{9,13},{10,... | collective-permute-start | bytes 98312 | tf_op jit(solution)/shard_map/ppermute | solution.py:559
  26.7 1.1 %collective-permute-start.12 = (bf16[64,256]{1,0:T(8,128)(2,1)S(1)}, bf16[64,256]{1,0:T(8,128)(2,1)S(1)}, u32[]{:S(2)}, u32[]{:S(2)}) collective-permute-start(bf16[64,256]{1,0:T(8,128)(2,1)S(1)} %get-tuple-element.83), channel_id=1, source_target_pairs={{0,6},{1,7},{2,4},{3,5},{4,2},{5,3},{6,0},{7,1},{8,14},{9,15},{10,... | collective-permute-start | bytes 98312 | tf_op jit(solution)/shard_map/ppermute | solution.py:559
  27.8 1.3 %collective-permute-start.13 = (bf16[64,256]{1,0:T(8,128)(2,1)S(1)}, bf16[64,256]{1,0:T(8,128)(2,1)S(1)}, u32[]{:S(2)}, u32[]{:S(2)}) collective-permute-start(bf16[64,256]{1,0:T(8,128)(2,1)S(1)} %get-tuple-element.84), channel_id=1, source_target_pairs={{0,2},{1,3},{2,0},{3,1},{4,6},{5,7},{6,4},{7,5},{8,10},{9,11},{10,... | collective-permute-start | bytes 98312 | tf_op jit(solution)/shard_map/ppermute | solution.py:559
  29.1 0.0 collective-permute-start.10
  29.1 1.6 %collective-permute-done.11.refs_1_ = bf16[64,256]{1,0:T(8,128)(2,1)S(1)} collective-permute-done((bf16[64,256]{1,0:T(8,128)(2,1)S(1)}, bf16[64,256]{1,0:T(8,128)(2,1)S(1)}, u32[]{:S(2)}, u32[]{:S(2)}) %collective-permute-start.11) | collective-permute-done | bytes 32800 | tf_op jit(solution)/shard_map/ppermute | solution.py:559
  30.7 1.7 %collective-permute-done.12.refs_2_ = bf16[64,256]{1,0:T(8,128)(2,1)S(1)} collective-permute-done((bf16[64,256]{1,0:T(8,128)(2,1)S(1)}, bf16[64,256]{1,0:T(8,128)(2,1)S(1)}, u32[]{:S(2)}, u32[]{:S(2)}) %collective-permute-start.12) | collective-permute-done | bytes 32800 | tf_op jit(solution)/shard_map/ppermute | solution.py:559
  32.4 0.0 collective-permute-done.9.link_kv.refs_4_
  32.4 1.5 %collective-permute-start.14 = (bf16[64,256]{1,0:T(8,128)(2,1)S(1)}, bf16[64,256]{1,0:T(8,128)(2,1)S(1)}, u32[]{:S(2)}, u32[]{:S(2)}) collective-permute-start(bf16[64,256]{1,0:T(8,128)(2,1)S(1)} %shard_map.114.refs_0_), channel_id=1, source_target_pairs={{0,24},{8,16},{16,8},{24,0},{1,25},{9,17},{17,9},{25,1},{2,26},{10... | collective-permute-start | bytes 98312 | tf_op jit(solution)/shard_map/ppermute | solution.py:568
  34.0 1.2 %collective-permute-start.15 = (bf16[64,256]{1,0:T(8,128)(2,1)S(1)}, bf16[64,256]{1,0:T(8,128)(2,1)S(1)}, u32[]{:S(2)}, u32[]{:S(2)}) collective-permute-start(bf16[64,256]{1,0:T(8,128)(2,1)S(1)} %shard_map.114.refs_0_), channel_id=1, source_target_pairs={{0,16},{8,24},{16,0},{24,8},{1,17},{9,25},{17,1},{25,9},{2,18},{10... | collective-permute-start | bytes 98312 | tf_op jit(solution)/shard_map/ppermute | solution.py:568
  35.2 0.8 %collective-permute-start.16 = (bf16[64,256]{1,0:T(8,128)(2,1)S(1)}, bf16[64,256]{1,0:T(8,128)(2,1)S(1)}, u32[]{:S(2)}, u32[]{:S(2)}) collective-permute-start(bf16[64,256]{1,0:T(8,128)(2,1)S(1)} %shard_map.114.refs_0_), channel_id=1, source_target_pairs={{0,8},{8,0},{16,24},{24,16},{1,9},{9,1},{17,25},{25,17},{2,10},{10... | collective-permute-start | bytes 98312 | tf_op jit(solution)/shard_map/ppermute | solution.py:568
  36.0 1.3 %shard_map.112 = bf16[256,1024]{1,0:T(8,128)(2,1)} custom-call(bf16[2,512,128]{2,1,0:T(8,128)(2,1)S(1)} %get-tuple-element.52.attn_t, bf16[512,1024]{1,0:T(8,128)(2,1)S(1)} %get-tuple-element.53.w_out, bf16[64,256]{1,0:T(8,128)(2,1)S(1)} %get-tuple-element.75.before.refs_0_), custom_call_target="tpu_custom_call" | custom-call | flops 5000000000 | bytes 20000000 | tf_op jit(solution)/shard_map/pallas_call | solution.py:412
  37.3 0.0 collective-permute-done.10.chip_kv
  37.3 0.9 %shard_map.113 = (bf16[256,512]{1,0:T(8,128)(2,1)}, bf16[256,512]{1,0:T(8,128)(2,1)}) custom-call(f32[256,512]{1,0:T(8,128)S(1)} %get-tuple-element.77.k_own, f32[256,512]{1,0:T(8,128)S(1)} %get-tuple-element.78.v_own, bf16[2,128,512]{2,1,0:T(8,128)(2,1)S(1)} %collective-permute-done.9.link_kv.refs_4_, bf16[2,128,512]{2,1,0:T(8,128)(2,1)S(1)} %collective-permute-done.10.chip_kv), custom_call_target="tpu_custom_call" | custom-call | flops 1000000 | bytes 4000 | tf_op jit(solution)/shard_map/pallas_call | solution.py:412
  38.2 0.9 %collective-permute-done.16.refs_3_ = bf16[64,256]{1,0:T(8,128)(2,1)S(1)} collective-permute-done((bf16[64,256]{1,0:T(8,128)(2,1)S(1)}, bf16[64,256]{1,0:T(8,128)(2,1)S(1)}, u32[]{:S(2)}, u32[]{:S(2)}) %collective-permute-start.16) | collective-permute-done | bytes 32800 | tf_op jit(solution)/shard_map/ppermute | solution.py:568
  39.1 0.7 %shard_map.115 = f32[64,1024]{1,0:T(8,128)} custom-call(bf16[64,256]{1,0:T(8,128)(2,1)S(1)} %shard_map.114.refs_0_, bf16[64,256]{1,0:T(8,128)(2,1)S(1)} %collective-permute-done.14.refs_1_, bf16[64,256]{1,0:T(8,128)(2,1)S(1)} %collective-permute-done.15.refs_2_, bf16[64,256]{1,0:T(8,128)(2,1)S(1)} %collective-permute-done.16.refs_3_), custom_call_target="tpu_custom_call" | custom-call | flops 1000000 | bytes 4000 | tf_op jit(solution)/shard_map/pallas_call | solution.py:412
  (5 shorter events, 0.0 us)
Async XLA Ops:
  1.6 11.3 %collective-permute-start = (bf16[2,128,512]{2,1,0:T(8,128)(2,1)S(1)}, bf16[2,128,512]{2,1,0:T(8,128)(2,1)S(1)}, u32[]{:S(2)}, u32[]{:S(2)}) collective-permute-start(bf16[2,128,512]{2,1,0:T(8,128)(2,1)S(1)} %shard_map.102), channel_id=1, source_target_pairs={{0,7},{1,2},{2,1},{3,4},{4,3},{5,6},{6,5},{7,0},{8,15},{9,10},{10,... | collective-permute-start | bytes 786440 | tf_op jit(solution)/shard_map/ppermute | solution.py:462
  7.2 5.2 %collective-permute-start.1 = (bf16[128,512]{1,0:T(8,128)(2,1)S(1)}, bf16[128,512]{1,0:T(8,128)(2,1)S(1)}, u32[]{:S(2)}, u32[]{:S(2)}) collective-permute-start(bf16[128,512]{1,0:T(8,128)(2,1)S(1)} %get-tuple-element.48), channel_id=1, source_target_pairs={{0,1},{1,0},{2,3},{3,2},{4,5},{5,4},{6,7},{7,6},{8,9},{9,8},{10,11... | collective-permute-start | bytes 393224 | tf_op jit(solution)/shard_map/ppermute | solution.py:463
  7.3 5.1 %collective-permute-start.2 = (bf16[128,512]{1,0:T(8,128)(2,1)S(1)}, bf16[128,512]{1,0:T(8,128)(2,1)S(1)}, u32[]{:S(2)}, u32[]{:S(2)}) collective-permute-start(bf16[128,512]{1,0:T(8,128)(2,1)S(1)} %get-tuple-element.49), channel_id=1, source_target_pairs={{0,1},{1,0},{2,3},{3,2},{4,5},{5,4},{6,7},{7,6},{8,9},{9,8},{10,11... | collective-permute-start | bytes 393224 | tf_op jit(solution)/shard_map/ppermute | solution.py:463
  11.8 3.0 %collective-permute-start.4 = (bf16[128,1024]{1,0:T(8,128)(2,1)S(1)}, bf16[128,1024]{1,0:T(8,128)(2,1)S(1)}, u32[]{:S(2)}, u32[]{:S(2)}) collective-permute-start(bf16[128,1024]{1,0:T(8,128)(2,1)S(1)} %get-tuple-element.55.g_low), channel_id=1, source_target_pairs={{0,1},{1,0},{2,3},{3,2},{4,5},{5,4},{6,7},{7,6},{8,9},{9,8},{10,11... | collective-permute-start | bytes 786440 | tf_op jit(solution)/shard_map/ppermute | solution.py:489
  11.9 2.9 %collective-permute-start.5 = (bf16[128,1024]{1,0:T(8,128)(2,1)S(1)}, bf16[128,1024]{1,0:T(8,128)(2,1)S(1)}, u32[]{:S(2)}, u32[]{:S(2)}) collective-permute-start(bf16[128,1024]{1,0:T(8,128)(2,1)S(1)} %get-tuple-element.56.g_high), channel_id=1, source_target_pairs={{0,1},{1,0},{2,3},{3,2},{4,5},{5,4},{6,7},{7,6},{8,9},{9,8},{10,11... | collective-permute-start | bytes 786440 | tf_op jit(solution)/shard_map/ppermute | solution.py:489
  13.5 1.4 %collective-permute-start.3 = (bf16[4,64,256]{2,1,0:T(8,128)(2,1)S(1)}, bf16[4,64,256]{2,1,0:T(8,128)(2,1)S(1)}, u32[]{:S(2)}, u32[]{:S(2)}) collective-permute-start(bf16[4,64,256]{2,1,0:T(8,128)(2,1)S(1)} %get-tuple-element.57), channel_id=1, source_target_pairs={{0,1},{1,0},{2,3},{3,2},{4,5},{5,4},{6,7},{7,6},{8,9},{9,8},{10,11... | collective-permute-start | bytes 393224 | tf_op jit(solution)/shard_map/ppermute | solution.py:518
  15.2 7.4 %collective-permute-start.6 = (bf16[4,64,256]{2,1,0:T(8,128)(2,1)S(1)}, bf16[4,64,256]{2,1,0:T(8,128)(2,1)S(1)}, u32[]{:S(2)}, u32[]{:S(2)}) collective-permute-start(bf16[4,64,256]{2,1,0:T(8,128)(2,1)S(1)} %get-tuple-element.64), channel_id=1, source_target_pairs={{0,8},{8,0},{16,24},{24,16},{1,9},{9,1},{17,25},{25,17},{2,10},{10... | collective-permute-start | bytes 393224 | tf_op jit(solution)/shard_map/ppermute | solution.py:555
  17.1 8.4 %collective-permute-start.7 = (bf16[4,64,256]{2,1,0:T(8,128)(2,1)S(1)}, bf16[4,64,256]{2,1,0:T(8,128)(2,1)S(1)}, u32[]{:S(2)}, u32[]{:S(2)}) collective-permute-start(bf16[4,64,256]{2,1,0:T(8,128)(2,1)S(1)} %get-tuple-element.65), channel_id=1, source_target_pairs={{0,16},{8,24},{16,0},{24,8},{1,17},{9,25},{17,1},{25,9},{2,18},{10... | collective-permute-start | bytes 393224 | tf_op jit(solution)/shard_map/ppermute | solution.py:555
  18.7 6.8 %collective-permute-start.8 = (bf16[4,64,256]{2,1,0:T(8,128)(2,1)S(1)}, bf16[4,64,256]{2,1,0:T(8,128)(2,1)S(1)}, u32[]{:S(2)}, u32[]{:S(2)}) collective-permute-start(bf16[4,64,256]{2,1,0:T(8,128)(2,1)S(1)} %get-tuple-element.66), channel_id=1, source_target_pairs={{0,24},{8,16},{16,8},{24,0},{1,25},{9,17},{17,9},{25,1},{2,26},{10... | collective-permute-start | bytes 393224 | tf_op jit(solution)/shard_map/ppermute | solution.py:555
  18.8 13.6 %collective-permute-start.9 = (bf16[2,128,512]{2,1,0:T(8,128)(2,1)S(1)}, bf16[2,128,512]{2,1,0:T(8,128)(2,1)S(1)}, u32[]{:S(2)}, u32[]{:S(2)}) collective-permute-start(bf16[2,128,512]{2,1,0:T(8,128)(2,1)S(1)} %shard_map.109.before), channel_id=1, source_target_pairs={{0,7},{1,2},{2,1},{3,4},{4,3},{5,6},{6,5},{7,0},{8,15},{9,10},{10,... | collective-permute-start | bytes 786440 | tf_op jit(solution)/shard_map/ppermute | solution.py:540
  25.6 5.1 %collective-permute-start.11 = (bf16[64,256]{1,0:T(8,128)(2,1)S(1)}, bf16[64,256]{1,0:T(8,128)(2,1)S(1)}, u32[]{:S(2)}, u32[]{:S(2)}) collective-permute-start(bf16[64,256]{1,0:T(8,128)(2,1)S(1)} %get-tuple-element.82), channel_id=1, source_target_pairs={{0,4},{1,5},{2,6},{3,7},{4,0},{5,1},{6,2},{7,3},{8,12},{9,13},{10,... | collective-permute-start | bytes 98312 | tf_op jit(solution)/shard_map/ppermute | solution.py:559
  26.7 5.7 %collective-permute-start.12 = (bf16[64,256]{1,0:T(8,128)(2,1)S(1)}, bf16[64,256]{1,0:T(8,128)(2,1)S(1)}, u32[]{:S(2)}, u32[]{:S(2)}) collective-permute-start(bf16[64,256]{1,0:T(8,128)(2,1)S(1)} %get-tuple-element.83), channel_id=1, source_target_pairs={{0,6},{1,7},{2,4},{3,5},{4,2},{5,3},{6,0},{7,1},{8,14},{9,15},{10,... | collective-permute-start | bytes 98312 | tf_op jit(solution)/shard_map/ppermute | solution.py:559
  27.8 4.6 %collective-permute-start.13 = (bf16[64,256]{1,0:T(8,128)(2,1)S(1)}, bf16[64,256]{1,0:T(8,128)(2,1)S(1)}, u32[]{:S(2)}, u32[]{:S(2)}) collective-permute-start(bf16[64,256]{1,0:T(8,128)(2,1)S(1)} %get-tuple-element.84), channel_id=1, source_target_pairs={{0,2},{1,3},{2,0},{3,1},{4,6},{5,7},{6,4},{7,5},{8,10},{9,11},{10,... | collective-permute-start | bytes 98312 | tf_op jit(solution)/shard_map/ppermute | solution.py:559
  29.1 8.2 %collective-permute-start.10 = (bf16[2,128,512]{2,1,0:T(8,128)(2,1)S(1)}, bf16[2,128,512]{2,1,0:T(8,128)(2,1)S(1)}, u32[]{:S(2)}, u32[]{:S(2)}) collective-permute-start(bf16[2,128,512]{2,1,0:T(8,128)(2,1)S(1)} %get-tuple-element.79), channel_id=1, source_target_pairs={{0,1},{1,0},{2,3},{3,2},{4,5},{5,4},{6,7},{7,6},{8,9},{9,8},{10,11... | collective-permute-start | bytes 786440 | tf_op jit(solution)/shard_map/ppermute | solution.py:541
  32.4 5.7 %collective-permute-start.14 = (bf16[64,256]{1,0:T(8,128)(2,1)S(1)}, bf16[64,256]{1,0:T(8,128)(2,1)S(1)}, u32[]{:S(2)}, u32[]{:S(2)}) collective-permute-start(bf16[64,256]{1,0:T(8,128)(2,1)S(1)} %shard_map.114.refs_0_), channel_id=1, source_target_pairs={{0,24},{8,16},{16,8},{24,0},{1,25},{9,17},{17,9},{25,1},{2,26},{10... | collective-permute-start | bytes 98312 | tf_op jit(solution)/shard_map/ppermute | solution.py:568
  34.0 4.2 %collective-permute-start.15 = (bf16[64,256]{1,0:T(8,128)(2,1)S(1)}, bf16[64,256]{1,0:T(8,128)(2,1)S(1)}, u32[]{:S(2)}, u32[]{:S(2)}) collective-permute-start(bf16[64,256]{1,0:T(8,128)(2,1)S(1)} %shard_map.114.refs_0_), channel_id=1, source_target_pairs={{0,16},{8,24},{16,0},{24,8},{1,17},{9,25},{17,1},{25,9},{2,18},{10... | collective-permute-start | bytes 98312 | tf_op jit(solution)/shard_map/ppermute | solution.py:568
  35.2 3.9 %collective-permute-start.16 = (bf16[64,256]{1,0:T(8,128)(2,1)S(1)}, bf16[64,256]{1,0:T(8,128)(2,1)S(1)}, u32[]{:S(2)}, u32[]{:S(2)}) collective-permute-start(bf16[64,256]{1,0:T(8,128)(2,1)S(1)} %shard_map.114.refs_0_), channel_id=1, source_target_pairs={{0,8},{8,0},{16,24},{24,16},{1,9},{9,1},{17,25},{25,17},{2,10},{10... | collective-permute-start | bytes 98312 | tf_op jit(solution)/shard_map/ppermute | solution.py:568

commit v20 on v18

--- a/solution.py
+++ b/solution.py
@@ -385,7 +385,7 @@
 
 
 def columns_kernel(*refs):
-    pieces, weight_grad = refs[:1] + refs[-2:0:-1], refs[-1]
+    pieces, weight_grad = refs[:1] + refs[2:-1] + refs[1:2], refs[-1]
     at_dp = lax.axis_index("dp")
     cols = pieces[0].shape[1]
     for d in range(len(pieces)):
@@ -560,7 +560,8 @@
         10**6,
         *quarters, link_back,
     )
-    pieces = [piece] + [lax.ppermute(piece, "dp", swap(dp, s)) for s in range(dp - 1, 0, -1)]
+    order = (dp - 1, *range(1, dp - 1))
+    pieces = [piece] + [lax.ppermute(piece, "dp", swap(dp, s)) for s in order]
     k_grad, v_grad = call(
         rim_sum_kernel, [hbm(tokens, feats)] * 2, 10**6, k_own, v_own, link_back, chip_back
     )

time: 39.9 us -> 40.1 us (level)
  no operation moved by 1% of the time
where the time goes in v20:
time: 40.1 us; the launch traced here: 39.9 us
  starting transfers between devices  17.9 us (45%)
  Pallas kernels  12.7 us (32%)
  waiting for transfers between devices  7.51 us (19%)
  other arithmetic  0.75 us (2%)
  between operations  0.74 us (2%)
    pallas_call x11, Pallas kernels, call(): pl.pallas_call(kernel, out_shape=outs, in_specs=[in_vmem] * len(args), ou...  7.71 us
    pallas_call x3, Pallas kernels, call_on_hbm(): pl.pallas_call(kernel, out_shape=outs, in_specs=[pl.BlockSpec(memory_spac...  4.99 us
    ppermute x1, starting transfers between devices, body(): link = lax.ppermute(to_link, 'ctx', over_links(ctx))  4.55 us
    ppermute x3, starting transfers between devices, body(): lax.ppermute(quarters[s], 'ctx', swap(ctx, 2 * s))  3.55 us
    ppermute x3, starting transfers between devices, body(): pieces = [piece] + [lax.ppermute(piece, 'dp', swap(dp, s)) for s in order]  3.55 us
    ppermute x3, starting transfers between devices, body(): lax.ppermute(halves[s], 'dp', swap(dp, s))  3.55 us
    ppermute x3, waiting for transfers between devices, body(): lax.ppermute(quarters[s], 'ctx', swap(ctx, 2 * s))  3.28 us
    ppermute x3, waiting for transfers between devices, body(): lax.ppermute(halves[s], 'dp', swap(dp, s))  2 us
  transfers between devices with their start and end apart: 17, of which 6 were waited for; matrix products, arithmetic and copies ran while one was open for 3% of the time, Pallas kernels for 27%

profile of v20, /device:TPU:0, one launch (start us, length us, event | category | flops | bytes accessed | tf_op | source)
XLA Modules:
  0.0 39.9 jit_solution(9371038775101997093)
XLA Ops:
  0.6 1.0 %shard_map.102 = bf16[2,128,512]{2,1,0:T(8,128)(2,1)S(1)} custom-call(bf16[256,512]{1,0:T(8,128)(2,1)} %bitcast.8, bf16[256,512]{1,0:T(8,128)(2,1)} %bitcast.11), custom_call_target="tpu_custom_call" | custom-call | flops 1000000 | bytes 4096 | tf_op jit(solution)/shard_map/pallas_call | solution.py:420
  1.6 4.6 %collective-permute-start = (bf16[2,128,512]{2,1,0:T(8,128)(2,1)S(1)}, bf16[2,128,512]{2,1,0:T(8,128)(2,1)S(1)}, u32[]{:S(2)}, u32[]{:S(2)}) collective-permute-start(bf16[2,128,512]{2,1,0:T(8,128)(2,1)S(1)} %shard_map.102), channel_id=1, source_target_pairs={{0,7},{1,2},{2,1},{3,4},{4,3},{5,6},{6,5},{7,0},{8,15},{9,10},{10,... | collective-permute-start | bytes 786440 | tf_op jit(solution)/shard_map/ppermute | solution.py:458
  6.2 1.0 %shard_map.103 = (bf16[128,512]{1,0:T(8,128)(2,1)S(1)}, bf16[128,512]{1,0:T(8,128)(2,1)S(1)}) custom-call(bf16[256,512]{1,0:T(8,128)(2,1)} %bitcast.9, bf16[256,512]{1,0:T(8,128)(2,1)} %bitcast.12), custom_call_target="tpu_custom_call" | custom-call | flops 1000000 | bytes 4096 | tf_op jit(solution)/shard_map/pallas_call | solution.py:420
  7.2 0.1 collective-permute-start.1
  7.3 0.5 %collective-permute-start.2 = (bf16[128,512]{1,0:T(8,128)(2,1)S(1)}, bf16[128,512]{1,0:T(8,128)(2,1)S(1)}, u32[]{:S(2)}, u32[]{:S(2)}) collective-permute-start(bf16[128,512]{1,0:T(8,128)(2,1)S(1)} %get-tuple-element.49), channel_id=1, source_target_pairs={{0,1},{1,0},{2,3},{3,2},{4,5},{5,4},{6,7},{7,6},{8,9},{9,8},{10,11... | collective-permute-start | bytes 393224 | tf_op jit(solution)/shard_map/ppermute | solution.py:459
  7.8 0.8 %compare_select_fusion = f32[1,2,3]{1,0,2:T(1,128)S(1)} fusion(s32[1,16,3]{1,0,2:T(1,128)} %param.11, s32[]{:T(128)S(6)} %select_n.14), kind=kLoop, calls=%fused_computation | loop fusion | flops 12 | bytes 52 | tf_op jit(solution)/shard_map/jit(_where)/select_n | solution.py:461
  8.5 0.1 copy.11
  8.6 0.1 select_n.16
  8.7 0.1 broadcast_in_dim.27.bias
  8.8 3.0 %shard_map.101 = (bf16[256,512]{1,0:T(8,128)(2,1)S(1)}, bf16[256,512]{1,0:T(8,128)(2,1)S(1)}, bf16[256,512]{1,0:T(8,128)(2,1)S(1)}, bf16[128,1024]{1,0:T(8,128)(...) custom-call(f32[6,1,256]{2,1,0:T(1,128)S(1)} %broadcast_in_dim.27.bi, ...), custom_call_target="tpu_custom_call" | custom-call | flops 1000000 | bytes 4096 | tf_op jit(solution)/shard_map/pallas_call | solution.py:420
  11.8 0.1 collective-permute-start.4
  11.9 0.4 %collective-permute-start.5 = (bf16[128,1024]{1,0:T(8,128)(2,1)S(1)}, bf16[128,1024]{1,0:T(8,128)(2,1)S(1)}, u32[]{:S(2)}, u32[]{:S(2)}) collective-permute-start(bf16[128,1024]{1,0:T(8,128)(2,1)S(1)} %get-tuple-element.56.g_high), channel_id=1, source_target_pairs={{0,1},{1,0},{2,3},{3,2},{4,5},{5,4},{6,7},{7,6},{8,9},{9,8},{10,11... | collective-permute-start | bytes 786440 | tf_op jit(solution)/shard_map/ppermute | solution.py:485
  12.4 0.0 collective-permute-done.1.rim_k.chip_k
  12.4 0.0 collective-permute-done.2.rim_v.chip_v
  12.4 0.5 %shard_map.104 = (f32[512,128]{1,0:T(8,128)S(1)}, f32[2,4,256]{2,1,0:T(4,128)S(1)}, f32[4,128,256]{2,1,0:T(8,128)S(1)}) custom-call(f32[6,1,256]{2,1,0:T(1,128)S(1)} %broadcast_in_dim.27.bias, bf16[256,512]{1,0:T(8,128)(2,1)S(1)} %get-tuple-element.45.q, bf16[128,512]{1,0:T(8,128)(2,1)S(1)} %collective-permute-done.1.rim_k.chip_k, ...), custom_call_target="tpu_custom_call" | custom-call | flops 1000000 | bytes 4000 | tf_op jit(solution)/shard_map/pallas_call | solution.py:408
  12.9 0.0 collective-permute-done.rim.link
  12.9 0.6 %shard_map.105 = (bf16[2,512,128]{2,1,0:T(8,128)(2,1)S(1)}, bf16[4,64,256]{2,1,0:T(8,128)(2,1)S(1)}, bf16[4,64,256]{2,1,0:T(8,128)(2,1)S(1)}, f32[4,128,256]{2,1...) custom-call(f32[6,1,256]{2,1,0:T(1,128)S(1)} %broadcast_in_dim.27.bias, ...), custom_call_target="tpu_custom_call" | custom-call | flops 1000000 | bytes 4000 | tf_op jit(solution)/shard_map/pallas_call | solution.py:408
  13.5 0.1 collective-permute-start.3
  13.6 0.3 shard_map.106.product
  13.9 0.0 collective-permute-done.4.g_low
  13.9 0.0 collective-permute-done.5.g_high
  13.9 0.9 %collective-permute-done.3.other = bf16[4,64,256]{2,1,0:T(8,128)(2,1)S(1)} collective-permute-done((bf16[4,64,256]{2,1,0:T(8,128)(2,1)S(1)}, bf16[4,64,256]{2,1,0:T(8,128)(2,1)S(1)}, u32[]{:S(2)}, u32[]{:S(2)}) %collective-permute-start.3) | collective-permute-done | bytes 131104 | tf_op jit(solution)/shard_map/ppermute | solution.py:514
  14.9 0.3 shard_map.107
  15.2 1.9 %collective-permute-start.6 = (bf16[4,64,256]{2,1,0:T(8,128)(2,1)S(1)}, bf16[4,64,256]{2,1,0:T(8,128)(2,1)S(1)}, u32[]{:S(2)}, u32[]{:S(2)}) collective-permute-start(bf16[4,64,256]{2,1,0:T(8,128)(2,1)S(1)} %get-tuple-element.59), channel_id=1, source_target_pairs={{0,8},{8,0},{16,24},{24,16},{1,9},{9,1},{17,25},{25,17},{2,10},{10... | collective-permute-start | bytes 393224 | tf_op jit(solution)/shard_map/ppermute | solution.py:550
  17.1 1.5 %collective-permute-start.7 = (bf16[4,64,256]{2,1,0:T(8,128)(2,1)S(1)}, bf16[4,64,256]{2,1,0:T(8,128)(2,1)S(1)}, u32[]{:S(2)}, u32[]{:S(2)}) collective-permute-start(bf16[4,64,256]{2,1,0:T(8,128)(2,1)S(1)} %get-tuple-element.60), channel_id=1, source_target_pairs={{0,16},{8,24},{16,0},{24,8},{1,17},{9,25},{17,1},{25,9},{2,18},{10... | collective-permute-start | bytes 393224 | tf_op jit(solution)/shard_map/ppermute | solution.py:550
  18.7 0.1 collective-permute-start.8
  18.8 0.9 %shard_map.108 = (bf16[2,128,512]{2,1,0:T(8,128)(2,1)S(1)}, bf16[2,128,512]{2,1,0:T(8,128)(2,1)S(1)}, f32[2,4,256]{2,1,0:T(4,128)S(1)}, f32[2,512,128]{2,1,0:T(8,128)S(1)}) custom-call(bf16[256,512]{1,0:T(8,128)(2,1)S(1)} %get-tuple-element.45.q, bf16[2,128,512]{2,1,0:T(8,128)(2,1)S(1)} %collective-permute-done.rim.link, ...), custom_call_target="tpu_custom_call" | custom-call | flops 1000000 | bytes 4000 | tf_op jit(solution)/shard_map/pallas_call | solution.py:408
  19.7 1.4 %collective-permute-start.9 = (bf16[2,128,512]{2,1,0:T(8,128)(2,1)S(1)}, bf16[2,128,512]{2,1,0:T(8,128)(2,1)S(1)}, u32[]{:S(2)}, u32[]{:S(2)}) collective-permute-start(bf16[2,128,512]{2,1,0:T(8,128)(2,1)S(1)} %get-tuple-element.78), channel_id=1, source_target_pairs={{0,7},{1,2},{2,1},{3,4},{4,3},{5,6},{6,5},{7,0},{8,15},{9,10},{10,... | collective-permute-start | bytes 786440 | tf_op jit(solution)/shard_map/ppermute | solution.py:535
  21.1 2.1 %shard_map.109 = (bf16[256,512]{1,0:T(8,128)(2,1)}, f32[256,512]{1,0:T(8,128)S(1)}, f32[256,512]{1,0:T(8,128)S(1)}, f32[8,128]{1,0:T(8,128)S(1)}) custom-call(bf16[256,512]{1,0:T(8,128)(2,1)S(1)} %get-tuple-element.45.q, bf16[256,512]{1,0:T(8,128)(2,1)S(1)} %get-tuple-element.62.k, bf16[256,512]{1,0:T(8,128)(2,1)S(1)} %get-tuple-element.63.v, ...), custom_call_target="tpu_custom_call" | custom-call | flops 5000000000 | bytes 20000000 | tf_op jit(solution)/shard_map/pallas_call | solution.py:408
  23.2 0.0 collective-permute-done.6.refs_1_
  23.2 2.0 %collective-permute-done.7.refs_2_ = bf16[4,64,256]{2,1,0:T(8,128)(2,1)S(1)} collective-permute-done((bf16[4,64,256]{2,1,0:T(8,128)(2,1)S(1)}, bf16[4,64,256]{2,1,0:T(8,128)(2,1)S(1)}, u32[]{:S(2)}, u32[]{:S(2)}) %collective-permute-start.7) | collective-permute-done | bytes 131104 | tf_op jit(solution)/shard_map/ppermute | solution.py:550
  25.2 0.1 shard_map.110
  25.3 1.1 %collective-permute-start.11 = (bf16[64,256]{1,0:T(8,128)(2,1)S(1)}, bf16[64,256]{1,0:T(8,128)(2,1)S(1)}, u32[]{:S(2)}, u32[]{:S(2)}) collective-permute-start(bf16[64,256]{1,0:T(8,128)(2,1)S(1)} %get-tuple-element.82), channel_id=1, source_target_pairs={{0,4},{1,5},{2,6},{3,7},{4,0},{5,1},{6,2},{7,3},{8,12},{9,13},{10,... | collective-permute-start | bytes 98312 | tf_op jit(solution)/shard_map/ppermute | solution.py:554
  26.4 1.1 %collective-permute-start.12 = (bf16[64,256]{1,0:T(8,128)(2,1)S(1)}, bf16[64,256]{1,0:T(8,128)(2,1)S(1)}, u32[]{:S(2)}, u32[]{:S(2)}) collective-permute-start(bf16[64,256]{1,0:T(8,128)(2,1)S(1)} %get-tuple-element.83), channel_id=1, source_target_pairs={{0,6},{1,7},{2,4},{3,5},{4,2},{5,3},{6,0},{7,1},{8,14},{9,15},{10,... | collective-permute-start | bytes 98312 | tf_op jit(solution)/shard_map/ppermute | solution.py:554
  27.5 1.3 %collective-permute-start.13 = (bf16[64,256]{1,0:T(8,128)(2,1)S(1)}, bf16[64,256]{1,0:T(8,128)(2,1)S(1)}, u32[]{:S(2)}, u32[]{:S(2)}) collective-permute-start(bf16[64,256]{1,0:T(8,128)(2,1)S(1)} %get-tuple-element.84), channel_id=1, source_target_pairs={{0,2},{1,3},{2,0},{3,1},{4,6},{5,7},{6,4},{7,5},{8,10},{9,11},{10,... | collective-permute-start | bytes 98312 | tf_op jit(solution)/shard_map/ppermute | solution.py:554
  28.8 0.0 collective-permute-start.10
  28.8 2.2 %collective-permute-done.11.refs_1_ = bf16[64,256]{1,0:T(8,128)(2,1)S(1)} collective-permute-done((bf16[64,256]{1,0:T(8,128)(2,1)S(1)}, bf16[64,256]{1,0:T(8,128)(2,1)S(1)}, u32[]{:S(2)}, u32[]{:S(2)}) %collective-permute-start.11) | collective-permute-done | bytes 32800 | tf_op jit(solution)/shard_map/ppermute | solution.py:554
  31.1 1.0 %collective-permute-done.12.refs_2_ = bf16[64,256]{1,0:T(8,128)(2,1)S(1)} collective-permute-done((bf16[64,256]{1,0:T(8,128)(2,1)S(1)}, bf16[64,256]{1,0:T(8,128)(2,1)S(1)}, u32[]{:S(2)}, u32[]{:S(2)}) %collective-permute-start.12) | collective-permute-done | bytes 32800 | tf_op jit(solution)/shard_map/ppermute | solution.py:554
  32.1 0.0 collective-permute-done.13.refs_3_
  32.2 1.9 %collective-permute-start.14 = (bf16[64,256]{1,0:T(8,128)(2,1)S(1)}, bf16[64,256]{1,0:T(8,128)(2,1)S(1)}, u32[]{:S(2)}, u32[]{:S(2)}) collective-permute-start(bf16[64,256]{1,0:T(8,128)(2,1)S(1)} %shard_map.113.refs_0_), channel_id=1, source_target_pairs={{0,24},{8,16},{16,8},{24,0},{1,25},{9,17},{17,9},{25,1},{2,26},{10... | collective-permute-start | bytes 98312 | tf_op jit(solution)/shard_map/ppermute | solution.py:564
  34.0 1.2 %collective-permute-start.15 = (bf16[64,256]{1,0:T(8,128)(2,1)S(1)}, bf16[64,256]{1,0:T(8,128)(2,1)S(1)}, u32[]{:S(2)}, u32[]{:S(2)}) collective-permute-start(bf16[64,256]{1,0:T(8,128)(2,1)S(1)} %shard_map.113.refs_0_), channel_id=1, source_target_pairs={{0,8},{8,0},{16,24},{24,16},{1,9},{9,1},{17,25},{25,17},{2,10},{10... | collective-permute-start | bytes 98312 | tf_op jit(solution)/shard_map/ppermute | solution.py:564
  35.2 0.5 %collective-permute-start.16 = (bf16[64,256]{1,0:T(8,128)(2,1)S(1)}, bf16[64,256]{1,0:T(8,128)(2,1)S(1)}, u32[]{:S(2)}, u32[]{:S(2)}) collective-permute-start(bf16[64,256]{1,0:T(8,128)(2,1)S(1)} %shard_map.113.refs_0_), channel_id=1, source_target_pairs={{0,16},{8,24},{16,0},{24,8},{1,17},{9,25},{17,1},{25,9},{2,18},{10... | collective-permute-start | bytes 98312 | tf_op jit(solution)/shard_map/ppermute | solution.py:564
  35.7 1.3 %shard_map.111 = bf16[256,1024]{1,0:T(8,128)(2,1)} custom-call(bf16[2,512,128]{2,1,0:T(8,128)(2,1)S(1)} %get-tuple-element.52.attn_t, bf16[512,1024]{1,0:T(8,128)(2,1)S(1)} %get-tuple-element.53.w_out, bf16[64,256]{1,0:T(8,128)(2,1)S(1)} %get-tuple-element.74.before.refs_0_), custom_call_target="tpu_custom_call" | custom-call | flops 5000000000 | bytes 20000000 | tf_op jit(solution)/shard_map/pallas_call | solution.py:408
  37.0 0.0 collective-permute-done.10.chip_kv
  37.0 0.9 %shard_map.112 = (bf16[256,512]{1,0:T(8,128)(2,1)}, bf16[256,512]{1,0:T(8,128)(2,1)}) custom-call(f32[256,512]{1,0:T(8,128)S(1)} %get-tuple-element.76.k_own, f32[256,512]{1,0:T(8,128)S(1)} %get-tuple-element.77.v_own, bf16[2,128,512]{2,1,0:T(8,128)(2,1)S(1)} %collective-permute-done.9.link_kv.refs_4_, bf16[2,128,512]{2,1,0:T(8,128)(2,1)S(1)} %collective-permute-done.10.chip_kv), custom_call_target="tpu_custom_call" | custom-call | flops 1000000 | bytes 4000 | tf_op jit(solution)/shard_map/pallas_call | solution.py:408
  37.9 0.1 collective-permute-done.15.refs_2_
  37.9 1.2 %collective-permute-done.16.refs_3_ = bf16[64,256]{1,0:T(8,128)(2,1)S(1)} collective-permute-done((bf16[64,256]{1,0:T(8,128)(2,1)S(1)}, bf16[64,256]{1,0:T(8,128)(2,1)S(1)}, u32[]{:S(2)}, u32[]{:S(2)}) %collective-permute-start.16) | collective-permute-done | bytes 32800 | tf_op jit(solution)/shard_map/ppermute | solution.py:564
  39.1 0.7 %shard_map.114 = f32[64,1024]{1,0:T(8,128)} custom-call(bf16[64,256]{1,0:T(8,128)(2,1)S(1)} %shard_map.113.refs_0_, bf16[64,256]{1,0:T(8,128)(2,1)S(1)} %collective-permute-done.14.refs_1_, bf16[64,256]{1,0:T(8,128)(2,1)S(1)} %collective-permute-done.15.refs_2_, bf16[64,256]{1,0:T(8,128)(2,1)S(1)} %collective-permute-done.16.refs_3_), custom_call_target="tpu_custom_call" | custom-call | flops 1000000 | bytes 4000 | tf_op jit(solution)/shard_map/pallas_call | solution.py:408
  (4 shorter events, 0.0 us)
Async XLA Ops:
  1.6 11.3 %collective-permute-start = (bf16[2,128,512]{2,1,0:T(8,128)(2,1)S(1)}, bf16[2,128,512]{2,1,0:T(8,128)(2,1)S(1)}, u32[]{:S(2)}, u32[]{:S(2)}) collective-permute-start(bf16[2,128,512]{2,1,0:T(8,128)(2,1)S(1)} %shard_map.102), channel_id=1, source_target_pairs={{0,7},{1,2},{2,1},{3,4},{4,3},{5,6},{6,5},{7,0},{8,15},{9,10},{10,... | collective-permute-start | bytes 786440 | tf_op jit(solution)/shard_map/ppermute | solution.py:458
  7.2 5.2 %collective-permute-start.1 = (bf16[128,512]{1,0:T(8,128)(2,1)S(1)}, bf16[128,512]{1,0:T(8,128)(2,1)S(1)}, u32[]{:S(2)}, u32[]{:S(2)}) collective-permute-start(bf16[128,512]{1,0:T(8,128)(2,1)S(1)} %get-tuple-element.48), channel_id=1, source_target_pairs={{0,1},{1,0},{2,3},{3,2},{4,5},{5,4},{6,7},{7,6},{8,9},{9,8},{10,11... | collective-permute-start | bytes 393224 | tf_op jit(solution)/shard_map/ppermute | solution.py:459
  7.3 5.1 %collective-permute-start.2 = (bf16[128,512]{1,0:T(8,128)(2,1)S(1)}, bf16[128,512]{1,0:T(8,128)(2,1)S(1)}, u32[]{:S(2)}, u32[]{:S(2)}) collective-permute-start(bf16[128,512]{1,0:T(8,128)(2,1)S(1)} %get-tuple-element.49), channel_id=1, source_target_pairs={{0,1},{1,0},{2,3},{3,2},{4,5},{5,4},{6,7},{7,6},{8,9},{9,8},{10,11... | collective-permute-start | bytes 393224 | tf_op jit(solution)/shard_map/ppermute | solution.py:459
  11.8 2.1 %collective-permute-start.4 = (bf16[128,1024]{1,0:T(8,128)(2,1)S(1)}, bf16[128,1024]{1,0:T(8,128)(2,1)S(1)}, u32[]{:S(2)}, u32[]{:S(2)}) collective-permute-start(bf16[128,1024]{1,0:T(8,128)(2,1)S(1)} %get-tuple-element.55.g_low), channel_id=1, source_target_pairs={{0,1},{1,0},{2,3},{3,2},{4,5},{5,4},{6,7},{7,6},{8,9},{9,8},{10,11... | collective-permute-start | bytes 786440 | tf_op jit(solution)/shard_map/ppermute | solution.py:485
  11.9 2.0 %collective-permute-start.5 = (bf16[128,1024]{1,0:T(8,128)(2,1)S(1)}, bf16[128,1024]{1,0:T(8,128)(2,1)S(1)}, u32[]{:S(2)}, u32[]{:S(2)}) collective-permute-start(bf16[128,1024]{1,0:T(8,128)(2,1)S(1)} %get-tuple-element.56.g_high), channel_id=1, source_target_pairs={{0,1},{1,0},{2,3},{3,2},{4,5},{5,4},{6,7},{7,6},{8,9},{9,8},{10,11... | collective-permute-start | bytes 786440 | tf_op jit(solution)/shard_map/ppermute | solution.py:485
  13.5 1.4 %collective-permute-start.3 = (bf16[4,64,256]{2,1,0:T(8,128)(2,1)S(1)}, bf16[4,64,256]{2,1,0:T(8,128)(2,1)S(1)}, u32[]{:S(2)}, u32[]{:S(2)}) collective-permute-start(bf16[4,64,256]{2,1,0:T(8,128)(2,1)S(1)} %get-tuple-element.57), channel_id=1, source_target_pairs={{0,1},{1,0},{2,3},{3,2},{4,5},{5,4},{6,7},{7,6},{8,9},{9,8},{10,11... | collective-permute-start | bytes 393224 | tf_op jit(solution)/shard_map/ppermute | solution.py:514
  15.2 8.0 %collective-permute-start.6 = (bf16[4,64,256]{2,1,0:T(8,128)(2,1)S(1)}, bf16[4,64,256]{2,1,0:T(8,128)(2,1)S(1)}, u32[]{:S(2)}, u32[]{:S(2)}) collective-permute-start(bf16[4,64,256]{2,1,0:T(8,128)(2,1)S(1)} %get-tuple-element.59), channel_id=1, source_target_pairs={{0,8},{8,0},{16,24},{24,16},{1,9},{9,1},{17,25},{25,17},{2,10},{10... | collective-permute-start | bytes 393224 | tf_op jit(solution)/shard_map/ppermute | solution.py:550
  17.1 8.1 %collective-permute-start.7 = (bf16[4,64,256]{2,1,0:T(8,128)(2,1)S(1)}, bf16[4,64,256]{2,1,0:T(8,128)(2,1)S(1)}, u32[]{:S(2)}, u32[]{:S(2)}) collective-permute-start(bf16[4,64,256]{2,1,0:T(8,128)(2,1)S(1)} %get-tuple-element.60), channel_id=1, source_target_pairs={{0,16},{8,24},{16,0},{24,8},{1,17},{9,25},{17,1},{25,9},{2,18},{10... | collective-permute-start | bytes 393224 | tf_op jit(solution)/shard_map/ppermute | solution.py:550
  18.7 6.5 %collective-permute-start.8 = (bf16[4,64,256]{2,1,0:T(8,128)(2,1)S(1)}, bf16[4,64,256]{2,1,0:T(8,128)(2,1)S(1)}, u32[]{:S(2)}, u32[]{:S(2)}) collective-permute-start(bf16[4,64,256]{2,1,0:T(8,128)(2,1)S(1)} %get-tuple-element.61), channel_id=1, source_target_pairs={{0,24},{8,16},{16,8},{24,0},{1,25},{9,17},{17,9},{25,1},{2,26},{10... | collective-permute-start | bytes 393224 | tf_op jit(solution)/shard_map/ppermute | solution.py:550
  19.7 12.5 %collective-permute-start.9 = (bf16[2,128,512]{2,1,0:T(8,128)(2,1)S(1)}, bf16[2,128,512]{2,1,0:T(8,128)(2,1)S(1)}, u32[]{:S(2)}, u32[]{:S(2)}) collective-permute-start(bf16[2,128,512]{2,1,0:T(8,128)(2,1)S(1)} %get-tuple-element.78), channel_id=1, source_target_pairs={{0,7},{1,2},{2,1},{3,4},{4,3},{5,6},{6,5},{7,0},{8,15},{9,10},{10,... | collective-permute-start | bytes 786440 | tf_op jit(solution)/shard_map/ppermute | solution.py:535
  25.3 5.8 %collective-permute-start.11 = (bf16[64,256]{1,0:T(8,128)(2,1)S(1)}, bf16[64,256]{1,0:T(8,128)(2,1)S(1)}, u32[]{:S(2)}, u32[]{:S(2)}) collective-permute-start(bf16[64,256]{1,0:T(8,128)(2,1)S(1)} %get-tuple-element.82), channel_id=1, source_target_pairs={{0,4},{1,5},{2,6},{3,7},{4,0},{5,1},{6,2},{7,3},{8,12},{9,13},{10,... | collective-permute-start | bytes 98312 | tf_op jit(solution)/shard_map/ppermute | solution.py:554
  26.4 5.7 %collective-permute-start.12 = (bf16[64,256]{1,0:T(8,128)(2,1)S(1)}, bf16[64,256]{1,0:T(8,128)(2,1)S(1)}, u32[]{:S(2)}, u32[]{:S(2)}) collective-permute-start(bf16[64,256]{1,0:T(8,128)(2,1)S(1)} %get-tuple-element.83), channel_id=1, source_target_pairs={{0,6},{1,7},{2,4},{3,5},{4,2},{5,3},{6,0},{7,1},{8,14},{9,15},{10,... | collective-permute-start | bytes 98312 | tf_op jit(solution)/shard_map/ppermute | solution.py:554
  27.5 4.6 %collective-permute-start.13 = (bf16[64,256]{1,0:T(8,128)(2,1)S(1)}, bf16[64,256]{1,0:T(8,128)(2,1)S(1)}, u32[]{:S(2)}, u32[]{:S(2)}) collective-permute-start(bf16[64,256]{1,0:T(8,128)(2,1)S(1)} %get-tuple-element.84), channel_id=1, source_target_pairs={{0,2},{1,3},{2,0},{3,1},{4,6},{5,7},{6,4},{7,5},{8,10},{9,11},{10,... | collective-permute-start | bytes 98312 | tf_op jit(solution)/shard_map/ppermute | solution.py:554
  28.8 8.1 %collective-permute-start.10 = (bf16[2,128,512]{2,1,0:T(8,128)(2,1)S(1)}, bf16[2,128,512]{2,1,0:T(8,128)(2,1)S(1)}, u32[]{:S(2)}, u32[]{:S(2)}) collective-permute-start(bf16[2,128,512]{2,1,0:T(8,128)(2,1)S(1)} %get-tuple-element.79), channel_id=1, source_target_pairs={{0,1},{1,0},{2,3},{3,2},{4,5},{5,4},{6,7},{7,6},{8,9},{9,8},{10,11... | collective-permute-start | bytes 786440 | tf_op jit(solution)/shard_map/ppermute | solution.py:536
  32.2 5.7 %collective-permute-start.14 = (bf16[64,256]{1,0:T(8,128)(2,1)S(1)}, bf16[64,256]{1,0:T(8,128)(2,1)S(1)}, u32[]{:S(2)}, u32[]{:S(2)}) collective-permute-start(bf16[64,256]{1,0:T(8,128)(2,1)S(1)} %shard_map.113.refs_0_), channel_id=1, source_target_pairs={{0,24},{8,16},{16,8},{24,0},{1,25},{9,17},{17,9},{25,1},{2,26},{10... | collective-permute-start | bytes 98312 | tf_op jit(solution)/shard_map/ppermute | solution.py:564
  34.0 3.9 %collective-permute-start.15 = (bf16[64,256]{1,0:T(8,128)(2,1)S(1)}, bf16[64,256]{1,0:T(8,128)(2,1)S(1)}, u32[]{:S(2)}, u32[]{:S(2)}) collective-permute-start(bf16[64,256]{1,0:T(8,128)(2,1)S(1)} %shard_map.113.refs_0_), channel_id=1, source_target_pairs={{0,8},{8,0},{16,24},{24,16},{1,9},{9,1},{17,25},{25,17},{2,10},{10... | collective-permute-start | bytes 98312 | tf_op jit(solution)/shard_map/ppermute | solution.py:564
  35.2 3.9 %collective-permute-start.16 = (bf16[64,256]{1,0:T(8,128)(2,1)S(1)}, bf16[64,256]{1,0:T(8,128)(2,1)S(1)}, u32[]{:S(2)}, u32[]{:S(2)}) collective-permute-start(bf16[64,256]{1,0:T(8,128)(2,1)S(1)} %shard_map.113.refs_0_), channel_id=1, source_target_pairs={{0,16},{8,24},{16,0},{24,8},{1,17},{9,25},{17,1},{25,9},{2,18},{10... | collective-permute-start | bytes 98312 | tf_op jit(solution)/shard_map/ppermute | solution.py:564

commit v21 on v18

--- a/solution.py
+++ b/solution.py
@@ -327,6 +327,10 @@
     after[...] = jnp.zeros_like(after)
 
 
+def send_kernel(back, before, out):
+    out[...] = back[...]
+
+
 def output_kernel(attn_t, w_out, before, output):
     for b in range(attn_t.shape[0]):
         part = dot(attn_t[b], w_out[...], ((0,), (0,)))
@@ -368,7 +372,7 @@
     refs[-1][...] = (total([part[...] for part in refs[:count]]) * scale).astype(BF16)
 
 
-def rim_sum_kernel(k_own, v_own, link_kv, chip_kv, k_grad, v_grad):
+def rim_sum_kernel(k_own, v_own, link_kv, chip_kv, k_grad, v_grad, after):
     tokens = k_own.shape[0]
     first_core = at_core() == 0
     for i, (own, grad) in enumerate(((k_own, k_grad), (v_own, v_grad))):
@@ -382,9 +386,10 @@
             if tokens > 2 * RIM:
                 grad[RIM : tokens - RIM] = own[RIM : tokens - RIM].astype(BF16)
             grad[tokens - RIM :] = (own[tokens - RIM :] + high).astype(BF16)
-
-
-def columns_kernel(*refs):
+    after[...] = jnp.zeros_like(after)
+
+
+def columns_kernel(before, *refs):
     pieces, weight_grad = refs[:1] + refs[-2:0:-1], refs[-1]
     at_dp = lax.axis_index("dp")
     cols = pieces[0].shape[1]
@@ -533,7 +538,6 @@
         scratch=[vmem(2, *rim_scores, dtype=F32), vmem(2, *rim_scores), vmem(2, *rim_scores)],
     )
     link_back = lax.ppermute(back[0], "ctx", over_links(ctx))
-    chip_back = lax.ppermute(back[1], "ctx", swap(ctx, 1))
     q_grad, k_own, v_own, after = call(
         own_backward_kernel,
         [
@@ -561,10 +565,15 @@
         *quarters, link_back,
     )
     pieces = [piece] + [lax.ppermute(piece, "dp", swap(dp, s)) for s in range(dp - 1, 0, -1)]
-    k_grad, v_grad = call(
-        rim_sum_kernel, [hbm(tokens, feats)] * 2, 10**6, k_own, v_own, link_back, chip_back
-    )
-    (weight_grad,) = call(columns_kernel, [hbm(rows, width, dtype=F32)], 10**6, *pieces)
+    (to_chip,) = call(send_kernel, [vmem(2, RIM, feats)], 10**6, back[1], piece)
+    chip_back = lax.ppermute(to_chip, "ctx", swap(ctx, 1))
+    k_grad, v_grad, after = call(
+        rim_sum_kernel,
+        [hbm(tokens, feats), hbm(tokens, feats), vmem(8, 128, dtype=F32)],
+        10**6,
+        k_own, v_own, link_back, chip_back,
+    )
+    (weight_grad,) = call(columns_kernel, [hbm(rows, width, dtype=F32)], 10**6, after, *pieces)
     return (output[None], q_grad[None], k_grad[None], v_grad[None], weight_grad)
 
 

time: 39.9 us -> 39.9 us (level)
    pallas_call x11 -> x12, Pallas kernels: 7.71 us -> 7.72 us  [call(): pl.pallas_call(kernel, out_shape=outs, in_specs=[in_vmem] * len(args), ou...]
where the time goes in v21:
time: 39.9 us; the launch traced here: 39.7 us
  starting transfers between devices  18 us (45%)
  Pallas kernels  12.7 us (32%)
  waiting for transfers between devices  7.23 us (18%)
  other arithmetic  0.75 us (2%)
  between operations  0.75 us (2%)
    pallas_call x12, Pallas kernels, call(): pl.pallas_call(kernel, out_shape=outs, in_specs=[in_vmem] * len(args), ou...  7.72 us
    pallas_call x3, Pallas kernels, call_on_hbm(): pl.pallas_call(kernel, out_shape=outs, in_specs=[pl.BlockSpec(memory_spac...  4.99 us
    ppermute x1, starting transfers between devices, body(): link = lax.ppermute(to_link, 'ctx', over_links(ctx))  4.55 us
    ppermute x3, starting transfers between devices, body(): lax.ppermute(piece, 'dp', swap(dp, s))  3.55 us
    ppermute x3, starting transfers between devices, body(): lax.ppermute(quarters[s], 'ctx', swap(ctx, 2 * s))  3.55 us
    ppermute x3, starting transfers between devices, body(): lax.ppermute(halves[s], 'dp', swap(dp, s))  3.55 us
    ppermute x3, waiting for transfers between devices, body(): lax.ppermute(quarters[s], 'ctx', swap(ctx, 2 * s))  3.28 us
    ppermute x3, waiting for transfers between devices, body(): lax.ppermute(halves[s], 'dp', swap(dp, s))  2 us
  transfers between devices with their start and end apart: 17, of which 6 were waited for; matrix products, arithmetic and copies ran while one was open for 3% of the time, Pallas kernels for 27%

profile of v21, /device:TPU:0, one launch (start us, length us, event | category | flops | bytes accessed | tf_op | source)
XLA Modules:
  0.0 39.7 jit_solution(1118486185986844103)
XLA Ops:
  0.6 1.0 %shard_map.102 = bf16[2,128,512]{2,1,0:T(8,128)(2,1)S(1)} custom-call(bf16[256,512]{1,0:T(8,128)(2,1)} %bitcast.8, bf16[256,512]{1,0:T(8,128)(2,1)} %bitcast.11), custom_call_target="tpu_custom_call" | custom-call | flops 1000000 | bytes 4096 | tf_op jit(solution)/shard_map/pallas_call | solution.py:425
  1.6 4.6 %collective-permute-start = (bf16[2,128,512]{2,1,0:T(8,128)(2,1)S(1)}, bf16[2,128,512]{2,1,0:T(8,128)(2,1)S(1)}, u32[]{:S(2)}, u32[]{:S(2)}) collective-permute-start(bf16[2,128,512]{2,1,0:T(8,128)(2,1)S(1)} %shard_map.102), channel_id=1, source_target_pairs={{0,7},{1,2},{2,1},{3,4},{4,3},{5,6},{6,5},{7,0},{8,15},{9,10},{10,... | collective-permute-start | bytes 786440 | tf_op jit(solution)/shard_map/ppermute | solution.py:463
  6.2 1.0 %shard_map.103 = (bf16[128,512]{1,0:T(8,128)(2,1)S(1)}, bf16[128,512]{1,0:T(8,128)(2,1)S(1)}) custom-call(bf16[256,512]{1,0:T(8,128)(2,1)} %bitcast.9, bf16[256,512]{1,0:T(8,128)(2,1)} %bitcast.12), custom_call_target="tpu_custom_call" | custom-call | flops 1000000 | bytes 4096 | tf_op jit(solution)/shard_map/pallas_call | solution.py:425
  7.2 0.1 collective-permute-start.1
  7.3 0.5 %collective-permute-start.2 = (bf16[128,512]{1,0:T(8,128)(2,1)S(1)}, bf16[128,512]{1,0:T(8,128)(2,1)S(1)}, u32[]{:S(2)}, u32[]{:S(2)}) collective-permute-start(bf16[128,512]{1,0:T(8,128)(2,1)S(1)} %get-tuple-element.50), channel_id=1, source_target_pairs={{0,1},{1,0},{2,3},{3,2},{4,5},{5,4},{6,7},{7,6},{8,9},{9,8},{10,11... | collective-permute-start | bytes 393224 | tf_op jit(solution)/shard_map/ppermute | solution.py:464
  7.8 0.8 %compare_select_fusion = f32[1,2,3]{1,0,2:T(1,128)S(1)} fusion(s32[1,16,3]{1,0,2:T(1,128)} %param.11, s32[]{:T(128)S(6)} %select_n.14), kind=kLoop, calls=%fused_computation | loop fusion | flops 12 | bytes 52 | tf_op jit(solution)/shard_map/jit(_where)/select_n | solution.py:466
  8.5 0.1 copy.11
  8.6 0.1 select_n.16
  8.7 0.1 broadcast_in_dim.27.bias
  8.8 3.0 %shard_map.101 = (bf16[256,512]{1,0:T(8,128)(2,1)S(1)}, bf16[256,512]{1,0:T(8,128)(2,1)S(1)}, bf16[256,512]{1,0:T(8,128)(2,1)S(1)}, bf16[128,1024]{1,0:T(8,128)(...) custom-call(f32[6,1,256]{2,1,0:T(1,128)S(1)} %broadcast_in_dim.27.bi, ...), custom_call_target="tpu_custom_call" | custom-call | flops 1000000 | bytes 4096 | tf_op jit(solution)/shard_map/pallas_call | solution.py:425
  11.8 0.1 collective-permute-start.4
  11.9 0.4 %collective-permute-start.5 = (bf16[128,1024]{1,0:T(8,128)(2,1)S(1)}, bf16[128,1024]{1,0:T(8,128)(2,1)S(1)}, u32[]{:S(2)}, u32[]{:S(2)}) collective-permute-start(bf16[128,1024]{1,0:T(8,128)(2,1)S(1)} %get-tuple-element.57.g_high), channel_id=1, source_target_pairs={{0,1},{1,0},{2,3},{3,2},{4,5},{5,4},{6,7},{7,6},{8,9},{9,8},{10,11... | collective-permute-start | bytes 786440 | tf_op jit(solution)/shard_map/ppermute | solution.py:490
  12.4 0.0 collective-permute-done.1.rim_k.chip_k
  12.4 0.0 collective-permute-done.2.rim_v.chip_v
  12.4 0.5 %shard_map.104 = (f32[512,128]{1,0:T(8,128)S(1)}, f32[2,4,256]{2,1,0:T(4,128)S(1)}, f32[4,128,256]{2,1,0:T(8,128)S(1)}) custom-call(f32[6,1,256]{2,1,0:T(1,128)S(1)} %broadcast_in_dim.27.bias, bf16[256,512]{1,0:T(8,128)(2,1)S(1)} %get-tuple-element.46.q, bf16[128,512]{1,0:T(8,128)(2,1)S(1)} %collective-permute-done.1.rim_k.chip_k, ...), custom_call_target="tpu_custom_call" | custom-call | flops 1000000 | bytes 4000 | tf_op jit(solution)/shard_map/pallas_call | solution.py:413
  12.9 0.0 collective-permute-done.rim.link
  12.9 0.6 %shard_map.105 = (bf16[2,512,128]{2,1,0:T(8,128)(2,1)S(1)}, bf16[4,64,256]{2,1,0:T(8,128)(2,1)S(1)}, bf16[4,64,256]{2,1,0:T(8,128)(2,1)S(1)}, f32[4,128,256]{2,1...) custom-call(f32[6,1,256]{2,1,0:T(1,128)S(1)} %broadcast_in_dim.27.bias, ...), custom_call_target="tpu_custom_call" | custom-call | flops 1000000 | bytes 4000 | tf_op jit(solution)/shard_map/pallas_call | solution.py:413
  13.5 0.1 collective-permute-start.3
  13.6 0.3 shard_map.106.product
  13.9 0.0 collective-permute-done.4.g_low
  13.9 0.0 collective-permute-done.5.g_high
  13.9 0.9 %collective-permute-done.3.other = bf16[4,64,256]{2,1,0:T(8,128)(2,1)S(1)} collective-permute-done((bf16[4,64,256]{2,1,0:T(8,128)(2,1)S(1)}, bf16[4,64,256]{2,1,0:T(8,128)(2,1)S(1)}, u32[]{:S(2)}, u32[]{:S(2)}) %collective-permute-start.3) | collective-permute-done | bytes 131104 | tf_op jit(solution)/shard_map/ppermute | solution.py:519
  14.9 0.3 shard_map.107
  15.2 1.9 %collective-permute-start.6 = (bf16[4,64,256]{2,1,0:T(8,128)(2,1)S(1)}, bf16[4,64,256]{2,1,0:T(8,128)(2,1)S(1)}, u32[]{:S(2)}, u32[]{:S(2)}) collective-permute-start(bf16[4,64,256]{2,1,0:T(8,128)(2,1)S(1)} %get-tuple-element.60), channel_id=1, source_target_pairs={{0,8},{8,0},{16,24},{24,16},{1,9},{9,1},{17,25},{25,17},{2,10},{10... | collective-permute-start | bytes 393224 | tf_op jit(solution)/shard_map/ppermute | solution.py:554
  17.1 1.5 %collective-permute-start.7 = (bf16[4,64,256]{2,1,0:T(8,128)(2,1)S(1)}, bf16[4,64,256]{2,1,0:T(8,128)(2,1)S(1)}, u32[]{:S(2)}, u32[]{:S(2)}) collective-permute-start(bf16[4,64,256]{2,1,0:T(8,128)(2,1)S(1)} %get-tuple-element.61), channel_id=1, source_target_pairs={{0,16},{8,24},{16,0},{24,8},{1,17},{9,25},{17,1},{25,9},{2,18},{10... | collective-permute-start | bytes 393224 | tf_op jit(solution)/shard_map/ppermute | solution.py:554
  18.7 0.1 collective-permute-start.8
  18.8 0.9 %shard_map.108 = (bf16[2,128,512]{2,1,0:T(8,128)(2,1)S(1)}, bf16[2,128,512]{2,1,0:T(8,128)(2,1)S(1)}, f32[2,4,256]{2,1,0:T(4,128)S(1)}, f32[2,512,128]{2,1,0:T(8,128)S(1)}) custom-call(bf16[256,512]{1,0:T(8,128)(2,1)S(1)} %get-tuple-element.46.q, bf16[2,128,512]{2,1,0:T(8,128)(2,1)S(1)} %collective-permute-done.rim.link, ...), custom_call_target="tpu_custom_call" | custom-call | flops 1000000 | bytes 4000 | tf_op jit(solution)/shard_map/pallas_call | solution.py:413
  19.7 1.4 %collective-permute-start.9 = (bf16[2,128,512]{2,1,0:T(8,128)(2,1)S(1)}, bf16[2,128,512]{2,1,0:T(8,128)(2,1)S(1)}, u32[]{:S(2)}, u32[]{:S(2)}) collective-permute-start(bf16[2,128,512]{2,1,0:T(8,128)(2,1)S(1)} %get-tuple-element.79), channel_id=1, source_target_pairs={{0,7},{1,2},{2,1},{3,4},{4,3},{5,6},{6,5},{7,0},{8,15},{9,10},{10,... | collective-permute-start | bytes 786440 | tf_op jit(solution)/shard_map/ppermute | solution.py:540
  21.1 2.1 %shard_map.109 = (bf16[256,512]{1,0:T(8,128)(2,1)}, f32[256,512]{1,0:T(8,128)S(1)}, f32[256,512]{1,0:T(8,128)S(1)}, f32[8,128]{1,0:T(8,128)S(1)}) custom-call(bf16[256,512]{1,0:T(8,128)(2,1)S(1)} %get-tuple-element.46.q, bf16[256,512]{1,0:T(8,128)(2,1)S(1)} %get-tuple-element.63.k, bf16[256,512]{1,0:T(8,128)(2,1)S(1)} %get-tuple-element.64.v, ...), custom_call_target="tpu_custom_call" | custom-call | flops 5000000000 | bytes 20000000 | tf_op jit(solution)/shard_map/pallas_call | solution.py:413
  23.2 0.0 collective-permute-done.6.refs_1_
  23.2 2.0 %collective-permute-done.7.refs_2_ = bf16[4,64,256]{2,1,0:T(8,128)(2,1)S(1)} collective-permute-done((bf16[4,64,256]{2,1,0:T(8,128)(2,1)S(1)}, bf16[4,64,256]{2,1,0:T(8,128)(2,1)S(1)}, u32[]{:S(2)}, u32[]{:S(2)}) %collective-permute-start.7) | collective-permute-done | bytes 131104 | tf_op jit(solution)/shard_map/ppermute | solution.py:554
  25.2 0.0 collective-permute-done.8.refs_3_
  25.2 0.1 shard_map.110
  25.3 1.1 %collective-permute-start.10 = (bf16[64,256]{1,0:T(8,128)(2,1)S(1)}, bf16[64,256]{1,0:T(8,128)(2,1)S(1)}, u32[]{:S(2)}, u32[]{:S(2)}) collective-permute-start(bf16[64,256]{1,0:T(8,128)(2,1)S(1)} %get-tuple-element.81), channel_id=1, source_target_pairs={{0,4},{1,5},{2,6},{3,7},{4,0},{5,1},{6,2},{7,3},{8,12},{9,13},{10,... | collective-permute-start | bytes 98312 | tf_op jit(solution)/shard_map/ppermute | solution.py:558
  26.4 1.1 %collective-permute-start.11 = (bf16[64,256]{1,0:T(8,128)(2,1)S(1)}, bf16[64,256]{1,0:T(8,128)(2,1)S(1)}, u32[]{:S(2)}, u32[]{:S(2)}) collective-permute-start(bf16[64,256]{1,0:T(8,128)(2,1)S(1)} %get-tuple-element.82), channel_id=1, source_target_pairs={{0,6},{1,7},{2,4},{3,5},{4,2},{5,3},{6,0},{7,1},{8,14},{9,15},{10,... | collective-permute-start | bytes 98312 | tf_op jit(solution)/shard_map/ppermute | solution.py:558
  27.5 1.3 %collective-permute-start.12 = (bf16[64,256]{1,0:T(8,128)(2,1)S(1)}, bf16[64,256]{1,0:T(8,128)(2,1)S(1)}, u32[]{:S(2)}, u32[]{:S(2)}) collective-permute-start(bf16[64,256]{1,0:T(8,128)(2,1)S(1)} %get-tuple-element.83), channel_id=1, source_target_pairs={{0,2},{1,3},{2,0},{3,1},{4,6},{5,7},{6,4},{7,5},{8,10},{9,11},{10,... | collective-permute-start | bytes 98312 | tf_op jit(solution)/shard_map/ppermute | solution.py:558
  28.8 2.2 %collective-permute-done.10.refs_1_ = bf16[64,256]{1,0:T(8,128)(2,1)S(1)} collective-permute-done((bf16[64,256]{1,0:T(8,128)(2,1)S(1)}, bf16[64,256]{1,0:T(8,128)(2,1)S(1)}, u32[]{:S(2)}, u32[]{:S(2)}) %collective-permute-start.10) | collective-permute-done | bytes 32800 | tf_op jit(solution)/shard_map/ppermute | solution.py:558
  31.1 1.0 %collective-permute-done.11.refs_2_ = bf16[64,256]{1,0:T(8,128)(2,1)S(1)} collective-permute-done((bf16[64,256]{1,0:T(8,128)(2,1)S(1)}, bf16[64,256]{1,0:T(8,128)(2,1)S(1)}, u32[]{:S(2)}, u32[]{:S(2)}) %collective-permute-start.11) | collective-permute-done | bytes 32800 | tf_op jit(solution)/shard_map/ppermute | solution.py:558
  32.1 0.0 collective-permute-done.12.refs_3_
  32.2 1.9 %collective-permute-start.14 = (bf16[64,256]{1,0:T(8,128)(2,1)S(1)}, bf16[64,256]{1,0:T(8,128)(2,1)S(1)}, u32[]{:S(2)}, u32[]{:S(2)}) collective-permute-start(bf16[64,256]{1,0:T(8,128)(2,1)S(1)} %shard_map.112.before.refs_0_), channel_id=1, source_target_pairs={{0,24},{8,16},{16,8},{24,0},{1,25},{9,17},{17,9},{25,1},{2,26},{10... | collective-permute-start | bytes 98312 | tf_op jit(solution)/shard_map/ppermute | solution.py:567
  34.0 1.0 %collective-permute-start.15 = (bf16[64,256]{1,0:T(8,128)(2,1)S(1)}, bf16[64,256]{1,0:T(8,128)(2,1)S(1)}, u32[]{:S(2)}, u32[]{:S(2)}) collective-permute-start(bf16[64,256]{1,0:T(8,128)(2,1)S(1)} %shard_map.112.before.refs_0_), channel_id=1, source_target_pairs={{0,16},{8,24},{16,0},{24,8},{1,17},{9,25},{17,1},{25,9},{2,18},{10... | collective-permute-start | bytes 98312 | tf_op jit(solution)/shard_map/ppermute | solution.py:567
  35.0 0.7 %collective-permute-start.16 = (bf16[64,256]{1,0:T(8,128)(2,1)S(1)}, bf16[64,256]{1,0:T(8,128)(2,1)S(1)}, u32[]{:S(2)}, u32[]{:S(2)}) collective-permute-start(bf16[64,256]{1,0:T(8,128)(2,1)S(1)} %shard_map.112.before.refs_0_), channel_id=1, source_target_pairs={{0,8},{8,0},{16,24},{24,16},{1,9},{9,1},{17,25},{25,17},{2,10},{10... | collective-permute-start | bytes 98312 | tf_op jit(solution)/shard_map/ppermute | solution.py:567
  35.7 0.1 collective-permute-start.13
  35.8 1.3 %shard_map.111 = bf16[256,1024]{1,0:T(8,128)(2,1)} custom-call(bf16[2,512,128]{2,1,0:T(8,128)(2,1)S(1)} %get-tuple-element.53.attn_t, bf16[512,1024]{1,0:T(8,128)(2,1)S(1)} %get-tuple-element.54.w_out, bf16[64,256]{1,0:T(8,128)(2,1)S(1)} %get-tuple-element.75.before.refs_0_), custom_call_target="tpu_custom_call" | custom-call | flops 5000000000 | bytes 20000000 | tf_op jit(solution)/shard_map/pallas_call | solution.py:413
  37.1 0.3 collective-permute-done.13.chip_kv
  37.3 0.9 %shard_map.114 = (bf16[256,512]{1,0:T(8,128)(2,1)}, bf16[256,512]{1,0:T(8,128)(2,1)}, f32[8,128]{1,0:T(8,128)S(1)}) custom-call(f32[256,512]{1,0:T(8,128)S(1)} %get-tuple-element.77.k_own, f32[256,512]{1,0:T(8,128)S(1)} %get-tuple-element.78.v_own, bf16[2,128,512]{2,1,0:T(8,128)(2,1)S(1)} %collective-permute-done.9.refs_4_.link_kv, ...), custom_call_target="tpu_custom_call" | custom-call | flops 1000000 | bytes 4000 | tf_op jit(solution)/shard_map/pallas_call | solution.py:413
  38.2 0.7 %collective-permute-done.16.refs_3_ = bf16[64,256]{1,0:T(8,128)(2,1)S(1)} collective-permute-done((bf16[64,256]{1,0:T(8,128)(2,1)S(1)}, bf16[64,256]{1,0:T(8,128)(2,1)S(1)}, u32[]{:S(2)}, u32[]{:S(2)}) %collective-permute-start.16) | collective-permute-done | bytes 32800 | tf_op jit(solution)/shard_map/ppermute | solution.py:567
  39.0 0.7 %shard_map.115 = f32[64,1024]{1,0:T(8,128)} custom-call(f32[8,128]{1,0:T(8,128)S(1)} %get-tuple-element.86.before, bf16[64,256]{1,0:T(8,128)(2,1)S(1)} %shard_map.112.before.refs_0_, bf16[64,256]{1,0:T(8,128)(2,1)S(1)} %collective-permute-done.14.refs_1_, bf16[64,256]{1,0:T(8,128)(2,1)S(1)} %collective-permute-done.15.refs_2_, ...), custom_call_target="tpu_custom_call" | custom-call | flops 1000000 | bytes 4000 | tf_op jit(solution)/shard_map/pallas_call | solution.py:413
  (5 shorter events, 0.0 us)
Async XLA Ops:
  1.6 11.3 %collective-permute-start = (bf16[2,128,512]{2,1,0:T(8,128)(2,1)S(1)}, bf16[2,128,512]{2,1,0:T(8,128)(2,1)S(1)}, u32[]{:S(2)}, u32[]{:S(2)}) collective-permute-start(bf16[2,128,512]{2,1,0:T(8,128)(2,1)S(1)} %shard_map.102), channel_id=1, source_target_pairs={{0,7},{1,2},{2,1},{3,4},{4,3},{5,6},{6,5},{7,0},{8,15},{9,10},{10,... | collective-permute-start | bytes 786440 | tf_op jit(solution)/shard_map/ppermute | solution.py:463
  7.2 5.2 %collective-permute-start.1 = (bf16[128,512]{1,0:T(8,128)(2,1)S(1)}, bf16[128,512]{1,0:T(8,128)(2,1)S(1)}, u32[]{:S(2)}, u32[]{:S(2)}) collective-permute-start(bf16[128,512]{1,0:T(8,128)(2,1)S(1)} %get-tuple-element.49), channel_id=1, source_target_pairs={{0,1},{1,0},{2,3},{3,2},{4,5},{5,4},{6,7},{7,6},{8,9},{9,8},{10,11... | collective-permute-start | bytes 393224 | tf_op jit(solution)/shard_map/ppermute | solution.py:464
  7.3 5.1 %collective-permute-start.2 = (bf16[128,512]{1,0:T(8,128)(2,1)S(1)}, bf16[128,512]{1,0:T(8,128)(2,1)S(1)}, u32[]{:S(2)}, u32[]{:S(2)}) collective-permute-start(bf16[128,512]{1,0:T(8,128)(2,1)S(1)} %get-tuple-element.50), channel_id=1, source_target_pairs={{0,1},{1,0},{2,3},{3,2},{4,5},{5,4},{6,7},{7,6},{8,9},{9,8},{10,11... | collective-permute-start | bytes 393224 | tf_op jit(solution)/shard_map/ppermute | solution.py:464
  11.8 2.1 %collective-permute-start.4 = (bf16[128,1024]{1,0:T(8,128)(2,1)S(1)}, bf16[128,1024]{1,0:T(8,128)(2,1)S(1)}, u32[]{:S(2)}, u32[]{:S(2)}) collective-permute-start(bf16[128,1024]{1,0:T(8,128)(2,1)S(1)} %get-tuple-element.56.g_low), channel_id=1, source_target_pairs={{0,1},{1,0},{2,3},{3,2},{4,5},{5,4},{6,7},{7,6},{8,9},{9,8},{10,11... | collective-permute-start | bytes 786440 | tf_op jit(solution)/shard_map/ppermute | solution.py:490
  11.9 2.0 %collective-permute-start.5 = (bf16[128,1024]{1,0:T(8,128)(2,1)S(1)}, bf16[128,1024]{1,0:T(8,128)(2,1)S(1)}, u32[]{:S(2)}, u32[]{:S(2)}) collective-permute-start(bf16[128,1024]{1,0:T(8,128)(2,1)S(1)} %get-tuple-element.57.g_high), channel_id=1, source_target_pairs={{0,1},{1,0},{2,3},{3,2},{4,5},{5,4},{6,7},{7,6},{8,9},{9,8},{10,11... | collective-permute-start | bytes 786440 | tf_op jit(solution)/shard_map/ppermute | solution.py:490
  13.5 1.4 %collective-permute-start.3 = (bf16[4,64,256]{2,1,0:T(8,128)(2,1)S(1)}, bf16[4,64,256]{2,1,0:T(8,128)(2,1)S(1)}, u32[]{:S(2)}, u32[]{:S(2)}) collective-permute-start(bf16[4,64,256]{2,1,0:T(8,128)(2,1)S(1)} %get-tuple-element.58), channel_id=1, source_target_pairs={{0,1},{1,0},{2,3},{3,2},{4,5},{5,4},{6,7},{7,6},{8,9},{9,8},{10,11... | collective-permute-start | bytes 393224 | tf_op jit(solution)/shard_map/ppermute | solution.py:519
  15.2 8.0 %collective-permute-start.6 = (bf16[4,64,256]{2,1,0:T(8,128)(2,1)S(1)}, bf16[4,64,256]{2,1,0:T(8,128)(2,1)S(1)}, u32[]{:S(2)}, u32[]{:S(2)}) collective-permute-start(bf16[4,64,256]{2,1,0:T(8,128)(2,1)S(1)} %get-tuple-element.60), channel_id=1, source_target_pairs={{0,8},{8,0},{16,24},{24,16},{1,9},{9,1},{17,25},{25,17},{2,10},{10... | collective-permute-start | bytes 393224 | tf_op jit(solution)/shard_map/ppermute | solution.py:554
  17.1 8.1 %collective-permute-start.7 = (bf16[4,64,256]{2,1,0:T(8,128)(2,1)S(1)}, bf16[4,64,256]{2,1,0:T(8,128)(2,1)S(1)}, u32[]{:S(2)}, u32[]{:S(2)}) collective-permute-start(bf16[4,64,256]{2,1,0:T(8,128)(2,1)S(1)} %get-tuple-element.61), channel_id=1, source_target_pairs={{0,16},{8,24},{16,0},{24,8},{1,17},{9,25},{17,1},{25,9},{2,18},{10... | collective-permute-start | bytes 393224 | tf_op jit(solution)/shard_map/ppermute | solution.py:554
  18.7 6.5 %collective-permute-start.8 = (bf16[4,64,256]{2,1,0:T(8,128)(2,1)S(1)}, bf16[4,64,256]{2,1,0:T(8,128)(2,1)S(1)}, u32[]{:S(2)}, u32[]{:S(2)}) collective-permute-start(bf16[4,64,256]{2,1,0:T(8,128)(2,1)S(1)} %get-tuple-element.62), channel_id=1, source_target_pairs={{0,24},{8,16},{16,8},{24,0},{1,25},{9,17},{17,9},{25,1},{2,26},{10... | collective-permute-start | bytes 393224 | tf_op jit(solution)/shard_map/ppermute | solution.py:554
  19.7 12.5 %collective-permute-start.9 = (bf16[2,128,512]{2,1,0:T(8,128)(2,1)S(1)}, bf16[2,128,512]{2,1,0:T(8,128)(2,1)S(1)}, u32[]{:S(2)}, u32[]{:S(2)}) collective-permute-start(bf16[2,128,512]{2,1,0:T(8,128)(2,1)S(1)} %get-tuple-element.79), channel_id=1, source_target_pairs={{0,7},{1,2},{2,1},{3,4},{4,3},{5,6},{6,5},{7,0},{8,15},{9,10},{10,... | collective-permute-start | bytes 786440 | tf_op jit(solution)/shard_map/ppermute | solution.py:540
  25.3 5.8 %collective-permute-start.10 = (bf16[64,256]{1,0:T(8,128)(2,1)S(1)}, bf16[64,256]{1,0:T(8,128)(2,1)S(1)}, u32[]{:S(2)}, u32[]{:S(2)}) collective-permute-start(bf16[64,256]{1,0:T(8,128)(2,1)S(1)} %get-tuple-element.81), channel_id=1, source_target_pairs={{0,4},{1,5},{2,6},{3,7},{4,0},{5,1},{6,2},{7,3},{8,12},{9,13},{10,... | collective-permute-start | bytes 98312 | tf_op jit(solution)/shard_map/ppermute | solution.py:558
  26.4 5.7 %collective-permute-start.11 = (bf16[64,256]{1,0:T(8,128)(2,1)S(1)}, bf16[64,256]{1,0:T(8,128)(2,1)S(1)}, u32[]{:S(2)}, u32[]{:S(2)}) collective-permute-start(bf16[64,256]{1,0:T(8,128)(2,1)S(1)} %get-tuple-element.82), channel_id=1, source_target_pairs={{0,6},{1,7},{2,4},{3,5},{4,2},{5,3},{6,0},{7,1},{8,14},{9,15},{10,... | collective-permute-start | bytes 98312 | tf_op jit(solution)/shard_map/ppermute | solution.py:558
  27.5 4.6 %collective-permute-start.12 = (bf16[64,256]{1,0:T(8,128)(2,1)S(1)}, bf16[64,256]{1,0:T(8,128)(2,1)S(1)}, u32[]{:S(2)}, u32[]{:S(2)}) collective-permute-start(bf16[64,256]{1,0:T(8,128)(2,1)S(1)} %get-tuple-element.83), channel_id=1, source_target_pairs={{0,2},{1,3},{2,0},{3,1},{4,6},{5,7},{6,4},{7,5},{8,10},{9,11},{10,... | collective-permute-start | bytes 98312 | tf_op jit(solution)/shard_map/ppermute | solution.py:558
  32.2 6.1 %collective-permute-start.14 = (bf16[64,256]{1,0:T(8,128)(2,1)S(1)}, bf16[64,256]{1,0:T(8,128)(2,1)S(1)}, u32[]{:S(2)}, u32[]{:S(2)}) collective-permute-start(bf16[64,256]{1,0:T(8,128)(2,1)S(1)} %shard_map.112.before.refs_0_), channel_id=1, source_target_pairs={{0,24},{8,16},{16,8},{24,0},{1,25},{9,17},{17,9},{25,1},{2,26},{10... | collective-permute-start | bytes 98312 | tf_op jit(solution)/shard_map/ppermute | solution.py:567
  34.0 4.2 %collective-permute-start.15 = (bf16[64,256]{1,0:T(8,128)(2,1)S(1)}, bf16[64,256]{1,0:T(8,128)(2,1)S(1)}, u32[]{:S(2)}, u32[]{:S(2)}) collective-permute-start(bf16[64,256]{1,0:T(8,128)(2,1)S(1)} %shard_map.112.before.refs_0_), channel_id=1, source_target_pairs={{0,16},{8,24},{16,0},{24,8},{1,17},{9,25},{17,1},{25,9},{2,18},{10... | collective-permute-start | bytes 98312 | tf_op jit(solution)/shard_map/ppermute | solution.py:567
  35.0 3.9 %collective-permute-start.16 = (bf16[64,256]{1,0:T(8,128)(2,1)S(1)}, bf16[64,256]{1,0:T(8,128)(2,1)S(1)}, u32[]{:S(2)}, u32[]{:S(2)}) collective-permute-start(bf16[64,256]{1,0:T(8,128)(2,1)S(1)} %shard_map.112.before.refs_0_), channel_id=1, source_target_pairs={{0,8},{8,0},{16,24},{24,16},{1,9},{9,1},{17,25},{25,17},{2,10},{10... | collective-permute-start | bytes 98312 | tf_op jit(solution)/shard_map/ppermute | solution.py:567
  35.7 1.6 %collective-permute-start.13 = (bf16[2,128,512]{2,1,0:T(8,128)(2,1)S(1)}, bf16[2,128,512]{2,1,0:T(8,128)(2,1)S(1)}, u32[]{:S(2)}, u32[]{:S(2)}) collective-permute-start(bf16[2,128,512]{2,1,0:T(8,128)(2,1)S(1)} %shard_map.113), channel_id=1, source_target_pairs={{0,1},{1,0},{2,3},{3,2},{4,5},{5,4},{6,7},{7,6},{8,9},{9,8},{10,11... | collective-permute-start | bytes 786440 | tf_op jit(solution)/shard_map/ppermute | solution.py:569

commit v22 on v19

--- a/solution.py
+++ b/solution.py
@@ -372,7 +372,7 @@
     refs[-1][...] = (total([part[...] for part in refs[:count]]) * scale).astype(BF16)
 
 
-def rim_sum_kernel(k_own, v_own, link_kv, chip_kv, k_grad, v_grad):
+def rim_sum_kernel(k_own, v_own, link_kv, chip_kv, k_grad, v_grad, after):
     tokens = k_own.shape[0]
     first_core = at_core() == 0
     for i, (own, grad) in enumerate(((k_own, k_grad), (v_own, v_grad))):
@@ -386,9 +386,10 @@
             if tokens > 2 * RIM:
                 grad[RIM : tokens - RIM] = own[RIM : tokens - RIM].astype(BF16)
             grad[tokens - RIM :] = (own[tokens - RIM :] + high).astype(BF16)
-
-
-def columns_kernel(*refs):
+    after[...] = jnp.zeros_like(after)
+
+
+def columns_kernel(before, *refs):
     pieces, weight_grad = refs[:1] + refs[-2:0:-1], refs[-1]
     at_dp = lax.axis_index("dp")
     cols = pieces[0].shape[1]
@@ -538,7 +539,6 @@
     )
     (to_link,) = call(send_kernel, [vmem(2, RIM, feats)], 10**6, back[0], after)
     link_back = lax.ppermute(to_link, "ctx", over_links(ctx))
-    chip_back = lax.ppermute(back[1], "ctx", swap(ctx, 1))
     q_grad, k_own, v_own, after = call(
         own_backward_kernel,
         [
@@ -566,10 +566,15 @@
         *quarters, link_back,
     )
     pieces = [piece] + [lax.ppermute(piece, "dp", swap(dp, s)) for s in range(dp - 1, 0, -1)]
-    k_grad, v_grad = call(
-        rim_sum_kernel, [hbm(tokens, feats)] * 2, 10**6, k_own, v_own, link_back, chip_back
-    )
-    (weight_grad,) = call(columns_kernel, [hbm(rows, width, dtype=F32)], 10**6, *pieces)
+    (to_chip,) = call(send_kernel, [vmem(2, RIM, feats)], 10**6, back[1], piece)
+    chip_back = lax.ppermute(to_chip, "ctx", swap(ctx, 1))
+    k_grad, v_grad, after = call(
+        rim_sum_kernel,
+        [hbm(tokens, feats), hbm(tokens, feats), vmem(8, 128, dtype=F32)],
+        10**6,
+        k_own, v_own, link_back, chip_back,
+    )
+    (weight_grad,) = call(columns_kernel, [hbm(rows, width, dtype=F32)], 10**6, after, *pieces)
     return (output[None], q_grad[None], k_grad[None], v_grad[None], weight_grad)
 
 

time: 40 us -> 40 us (level)
    pallas_call x12 -> x13, Pallas kernels: 7.74 us -> 7.73 us  [call(): pl.pallas_call(kernel, out_shape=outs, in_specs=[in_vmem] * len(args), ou...]
  transfers between devices with their start and end apart: 17 -> 17, of which waited for: 4 -> 6; matrix products, arithmetic and copies ran while one was open for 3% -> 3% of each run, Pallas kernels for 27% -> 27%
where the time goes in v22:
time: 40 us; the launch traced here: 39.8 us
  starting transfers between devices  18.3 us (46%)
  Pallas kernels  12.7 us (32%)
  waiting for transfers between devices  7.1 us (18%)
  other arithmetic  0.75 us (2%)
  between operations  0.75 us (2%)
    pallas_call x13, Pallas kernels, call(): pl.pallas_call(kernel, out_shape=outs, in_specs=[in_vmem] * len(args), ou...  7.73 us
    pallas_call x3, Pallas kernels, call_on_hbm(): pl.pallas_call(kernel, out_shape=outs, in_specs=[pl.BlockSpec(memory_spac...  5 us
    ppermute x1, starting transfers between devices, body(): link = lax.ppermute(to_link, 'ctx', over_links(ctx))  4.55 us
    ppermute x3, starting transfers between devices, body(): lax.ppermute(piece, 'dp', swap(dp, s))  3.55 us
    ppermute x3, starting transfers between devices, body(): lax.ppermute(quarters[s], 'ctx', swap(ctx, 2 * s))  3.55 us
    ppermute x3, starting transfers between devices, body(): lax.ppermute(halves[s], 'dp', swap(dp, s))  3.55 us
    ppermute x3, waiting for transfers between devices, body(): lax.ppermute(quarters[s], 'ctx', swap(ctx, 2 * s))  3.29 us
    ppermute x3, waiting for transfers between devices, body(): lax.ppermute(halves[s], 'dp', swap(dp, s))  2.89 us
  transfers between devices with their start and end apart: 17, of which 6 were waited for; matrix products, arithmetic and copies ran while one was open for 3% of the time, Pallas kernels for 27%

profile of v22, /device:TPU:0, one launch (start us, length us, event | category | flops | bytes accessed | tf_op | source)
XLA Modules:
  0.0 39.8 jit_solution(17107844230737613787)
XLA Ops:
  0.6 1.0 %shard_map.102 = bf16[2,128,512]{2,1,0:T(8,128)(2,1)S(1)} custom-call(bf16[256,512]{1,0:T(8,128)(2,1)} %bitcast.8, bf16[256,512]{1,0:T(8,128)(2,1)} %bitcast.11), custom_call_target="tpu_custom_call" | custom-call | flops 1000000 | bytes 4096 | tf_op jit(solution)/shard_map/pallas_call | solution.py:425
  1.6 4.6 %collective-permute-start = (bf16[2,128,512]{2,1,0:T(8,128)(2,1)S(1)}, bf16[2,128,512]{2,1,0:T(8,128)(2,1)S(1)}, u32[]{:S(2)}, u32[]{:S(2)}) collective-permute-start(bf16[2,128,512]{2,1,0:T(8,128)(2,1)S(1)} %shard_map.102), channel_id=1, source_target_pairs={{0,7},{1,2},{2,1},{3,4},{4,3},{5,6},{6,5},{7,0},{8,15},{9,10},{10,... | collective-permute-start | bytes 786440 | tf_op jit(solution)/shard_map/ppermute | solution.py:463
  6.2 1.0 %shard_map.103 = (bf16[128,512]{1,0:T(8,128)(2,1)S(1)}, bf16[128,512]{1,0:T(8,128)(2,1)S(1)}) custom-call(bf16[256,512]{1,0:T(8,128)(2,1)} %bitcast.9, bf16[256,512]{1,0:T(8,128)(2,1)} %bitcast.12), custom_call_target="tpu_custom_call" | custom-call | flops 1000000 | bytes 4096 | tf_op jit(solution)/shard_map/pallas_call | solution.py:425
  7.2 0.1 collective-permute-start.1
  7.3 0.5 %collective-permute-start.2 = (bf16[128,512]{1,0:T(8,128)(2,1)S(1)}, bf16[128,512]{1,0:T(8,128)(2,1)S(1)}, u32[]{:S(2)}, u32[]{:S(2)}) collective-permute-start(bf16[128,512]{1,0:T(8,128)(2,1)S(1)} %get-tuple-element.50), channel_id=1, source_target_pairs={{0,1},{1,0},{2,3},{3,2},{4,5},{5,4},{6,7},{7,6},{8,9},{9,8},{10,11... | collective-permute-start | bytes 393224 | tf_op jit(solution)/shard_map/ppermute | solution.py:464
  7.8 0.8 %compare_select_fusion = f32[1,2,3]{1,0,2:T(1,128)S(1)} fusion(s32[1,16,3]{1,0,2:T(1,128)} %param.11, s32[]{:T(128)S(6)} %select_n.14), kind=kLoop, calls=%fused_computation | loop fusion | flops 12 | bytes 52 | tf_op jit(solution)/shard_map/jit(_where)/select_n | solution.py:466
  8.5 0.1 copy.11
  8.6 0.1 select_n.16
  8.7 0.1 broadcast_in_dim.27.bias
  8.8 3.0 %shard_map.101 = (bf16[256,512]{1,0:T(8,128)(2,1)S(1)}, bf16[256,512]{1,0:T(8,128)(2,1)S(1)}, bf16[256,512]{1,0:T(8,128)(2,1)S(1)}, bf16[128,1024]{1,0:T(8,128)(...) custom-call(f32[6,1,256]{2,1,0:T(1,128)S(1)} %broadcast_in_dim.27.bi, ...), custom_call_target="tpu_custom_call" | custom-call | flops 1000000 | bytes 4096 | tf_op jit(solution)/shard_map/pallas_call | solution.py:425
  11.8 0.1 collective-permute-start.4
  11.9 0.4 %collective-permute-start.5 = (bf16[128,1024]{1,0:T(8,128)(2,1)S(1)}, bf16[128,1024]{1,0:T(8,128)(2,1)S(1)}, u32[]{:S(2)}, u32[]{:S(2)}) collective-permute-start(bf16[128,1024]{1,0:T(8,128)(2,1)S(1)} %get-tuple-element.57.g_high), channel_id=1, source_target_pairs={{0,1},{1,0},{2,3},{3,2},{4,5},{5,4},{6,7},{7,6},{8,9},{9,8},{10,11... | collective-permute-start | bytes 786440 | tf_op jit(solution)/shard_map/ppermute | solution.py:490
  12.4 0.0 collective-permute-done.1.rim_k.chip_k
  12.4 0.0 collective-permute-done.2.rim_v.chip_v
  12.4 0.5 %shard_map.104 = (f32[512,128]{1,0:T(8,128)S(1)}, f32[2,4,256]{2,1,0:T(4,128)S(1)}, f32[4,128,256]{2,1,0:T(8,128)S(1)}) custom-call(f32[6,1,256]{2,1,0:T(1,128)S(1)} %broadcast_in_dim.27.bias, bf16[256,512]{1,0:T(8,128)(2,1)S(1)} %get-tuple-element.46.q, bf16[128,512]{1,0:T(8,128)(2,1)S(1)} %collective-permute-done.1.rim_k.chip_k, ...), custom_call_target="tpu_custom_call" | custom-call | flops 1000000 | bytes 4000 | tf_op jit(solution)/shard_map/pallas_call | solution.py:413
  12.9 0.0 collective-permute-done.rim.link
  12.9 0.6 %shard_map.105 = (bf16[2,512,128]{2,1,0:T(8,128)(2,1)S(1)}, bf16[4,64,256]{2,1,0:T(8,128)(2,1)S(1)}, bf16[4,64,256]{2,1,0:T(8,128)(2,1)S(1)}, f32[4,128,256]{2,1...) custom-call(f32[6,1,256]{2,1,0:T(1,128)S(1)} %broadcast_in_dim.27.bias, ...), custom_call_target="tpu_custom_call" | custom-call | flops 1000000 | bytes 4000 | tf_op jit(solution)/shard_map/pallas_call | solution.py:413
  13.5 0.1 collective-permute-start.3
  13.6 0.3 shard_map.106.product
  13.9 0.9 %shard_map.107 = (bf16[2,128,512]{2,1,0:T(8,128)(2,1)S(1)}, bf16[2,128,512]{2,1,0:T(8,128)(2,1)S(1)}, f32[2,4,256]{2,1,0:T(4,128)S(1)}, f32[2,512,128]{2,1,0:T(8,128)S(1)}) custom-call(bf16[256,512]{1,0:T(8,128)(2,1)S(1)} %get-tuple-element.46.q, bf16[2,128,512]{2,1,0:T(8,128)(2,1)S(1)} %collective-permute-done.rim.link, ...), custom_call_target="tpu_custom_call" | custom-call | flops 1000000 | bytes 4000 | tf_op jit(solution)/shard_map/pallas_call | solution.py:413
  14.8 0.0 collective-permute-done.4.g_low
  14.8 0.1 collective-permute-done.3.other
  14.9 0.3 shard_map.108
  15.2 1.9 %collective-permute-start.6 = (bf16[4,64,256]{2,1,0:T(8,128)(2,1)S(1)}, bf16[4,64,256]{2,1,0:T(8,128)(2,1)S(1)}, u32[]{:S(2)}, u32[]{:S(2)}) collective-permute-start(bf16[4,64,256]{2,1,0:T(8,128)(2,1)S(1)} %get-tuple-element.65), channel_id=1, source_target_pairs={{0,8},{8,0},{16,24},{24,16},{1,9},{9,1},{17,25},{25,17},{2,10},{10... | collective-permute-start | bytes 393224 | tf_op jit(solution)/shard_map/ppermute | solution.py:555
  17.1 1.5 %collective-permute-start.7 = (bf16[4,64,256]{2,1,0:T(8,128)(2,1)S(1)}, bf16[4,64,256]{2,1,0:T(8,128)(2,1)S(1)}, u32[]{:S(2)}, u32[]{:S(2)}) collective-permute-start(bf16[4,64,256]{2,1,0:T(8,128)(2,1)S(1)} %get-tuple-element.66), channel_id=1, source_target_pairs={{0,16},{8,24},{16,0},{24,8},{1,17},{9,25},{17,1},{25,9},{2,18},{10... | collective-permute-start | bytes 393224 | tf_op jit(solution)/shard_map/ppermute | solution.py:555
  18.7 0.1 collective-permute-start.8
  18.8 1.7 %collective-permute-start.9 = (bf16[2,128,512]{2,1,0:T(8,128)(2,1)S(1)}, bf16[2,128,512]{2,1,0:T(8,128)(2,1)S(1)}, u32[]{:S(2)}, u32[]{:S(2)}) collective-permute-start(bf16[2,128,512]{2,1,0:T(8,128)(2,1)S(1)} %shard_map.109.before), channel_id=1, source_target_pairs={{0,7},{1,2},{2,1},{3,4},{4,3},{5,6},{6,5},{7,0},{8,15},{9,10},{10,... | collective-permute-start | bytes 786440 | tf_op jit(solution)/shard_map/ppermute | solution.py:541
  20.5 2.1 %shard_map.110 = (bf16[256,512]{1,0:T(8,128)(2,1)}, f32[256,512]{1,0:T(8,128)S(1)}, f32[256,512]{1,0:T(8,128)S(1)}, f32[8,128]{1,0:T(8,128)S(1)}) custom-call(bf16[256,512]{1,0:T(8,128)(2,1)S(1)} %get-tuple-element.46.q, bf16[256,512]{1,0:T(8,128)(2,1)S(1)} %get-tuple-element.68.k, bf16[256,512]{1,0:T(8,128)(2,1)S(1)} %get-tuple-element.69.v, ...), custom_call_target="tpu_custom_call" | custom-call | flops 5000000000 | bytes 20000000 | tf_op jit(solution)/shard_map/pallas_call | solution.py:413
  22.6 0.0 collective-permute-done.6.refs_1_
  22.6 2.9 %collective-permute-done.7.refs_2_ = bf16[4,64,256]{2,1,0:T(8,128)(2,1)S(1)} collective-permute-done((bf16[4,64,256]{2,1,0:T(8,128)(2,1)S(1)}, bf16[4,64,256]{2,1,0:T(8,128)(2,1)S(1)}, u32[]{:S(2)}, u32[]{:S(2)}) %collective-permute-start.7) | collective-permute-done | bytes 131104 | tf_op jit(solution)/shard_map/ppermute | solution.py:555
  25.5 0.1 shard_map.111
  25.6 1.1 %collective-permute-start.10 = (bf16[64,256]{1,0:T(8,128)(2,1)S(1)}, bf16[64,256]{1,0:T(8,128)(2,1)S(1)}, u32[]{:S(2)}, u32[]{:S(2)}) collective-permute-start(bf16[64,256]{1,0:T(8,128)(2,1)S(1)} %get-tuple-element.81), channel_id=1, source_target_pairs={{0,4},{1,5},{2,6},{3,7},{4,0},{5,1},{6,2},{7,3},{8,12},{9,13},{10,... | collective-permute-start | bytes 98312 | tf_op jit(solution)/shard_map/ppermute | solution.py:559
  26.7 1.1 %collective-permute-start.11 = (bf16[64,256]{1,0:T(8,128)(2,1)S(1)}, bf16[64,256]{1,0:T(8,128)(2,1)S(1)}, u32[]{:S(2)}, u32[]{:S(2)}) collective-permute-start(bf16[64,256]{1,0:T(8,128)(2,1)S(1)} %get-tuple-element.82), channel_id=1, source_target_pairs={{0,6},{1,7},{2,4},{3,5},{4,2},{5,3},{6,0},{7,1},{8,14},{9,15},{10,... | collective-permute-start | bytes 98312 | tf_op jit(solution)/shard_map/ppermute | solution.py:559
  27.8 1.3 %collective-permute-start.12 = (bf16[64,256]{1,0:T(8,128)(2,1)S(1)}, bf16[64,256]{1,0:T(8,128)(2,1)S(1)}, u32[]{:S(2)}, u32[]{:S(2)}) collective-permute-start(bf16[64,256]{1,0:T(8,128)(2,1)S(1)} %get-tuple-element.83), channel_id=1, source_target_pairs={{0,2},{1,3},{2,0},{3,1},{4,6},{5,7},{6,4},{7,5},{8,10},{9,11},{10,... | collective-permute-start | bytes 98312 | tf_op jit(solution)/shard_map/ppermute | solution.py:559
  29.1 1.6 %collective-permute-done.10.refs_1_ = bf16[64,256]{1,0:T(8,128)(2,1)S(1)} collective-permute-done((bf16[64,256]{1,0:T(8,128)(2,1)S(1)}, bf16[64,256]{1,0:T(8,128)(2,1)S(1)}, u32[]{:S(2)}, u32[]{:S(2)}) %collective-permute-start.10) | collective-permute-done | bytes 32800 | tf_op jit(solution)/shard_map/ppermute | solution.py:559
  30.7 1.7 %collective-permute-done.11.refs_2_ = bf16[64,256]{1,0:T(8,128)(2,1)S(1)} collective-permute-done((bf16[64,256]{1,0:T(8,128)(2,1)S(1)}, bf16[64,256]{1,0:T(8,128)(2,1)S(1)}, u32[]{:S(2)}, u32[]{:S(2)}) %collective-permute-start.11) | collective-permute-done | bytes 32800 | tf_op jit(solution)/shard_map/ppermute | solution.py:559
  32.4 0.0 collective-permute-done.9.refs_4_.link_kv
  32.4 1.5 %collective-permute-start.14 = (bf16[64,256]{1,0:T(8,128)(2,1)S(1)}, bf16[64,256]{1,0:T(8,128)(2,1)S(1)}, u32[]{:S(2)}, u32[]{:S(2)}) collective-permute-start(bf16[64,256]{1,0:T(8,128)(2,1)S(1)} %shard_map.113.before.refs_0_), channel_id=1, source_target_pairs={{0,24},{8,16},{16,8},{24,0},{1,25},{9,17},{17,9},{25,1},{2,26},{10... | collective-permute-start | bytes 98312 | tf_op jit(solution)/shard_map/ppermute | solution.py:568
  34.0 1.2 %collective-permute-start.15 = (bf16[64,256]{1,0:T(8,128)(2,1)S(1)}, bf16[64,256]{1,0:T(8,128)(2,1)S(1)}, u32[]{:S(2)}, u32[]{:S(2)}) collective-permute-start(bf16[64,256]{1,0:T(8,128)(2,1)S(1)} %shard_map.113.before.refs_0_), channel_id=1, source_target_pairs={{0,16},{8,24},{16,0},{24,8},{1,17},{9,25},{17,1},{25,9},{2,18},{10... | collective-permute-start | bytes 98312 | tf_op jit(solution)/shard_map/ppermute | solution.py:568
  35.2 0.8 %collective-permute-start.16 = (bf16[64,256]{1,0:T(8,128)(2,1)S(1)}, bf16[64,256]{1,0:T(8,128)(2,1)S(1)}, u32[]{:S(2)}, u32[]{:S(2)}) collective-permute-start(bf16[64,256]{1,0:T(8,128)(2,1)S(1)} %shard_map.113.before.refs_0_), channel_id=1, source_target_pairs={{0,8},{8,0},{16,24},{24,16},{1,9},{9,1},{17,25},{25,17},{2,10},{10... | collective-permute-start | bytes 98312 | tf_op jit(solution)/shard_map/ppermute | solution.py:568
  36.0 0.1 collective-permute-start.13
  36.1 1.3 %shard_map.112 = bf16[256,1024]{1,0:T(8,128)(2,1)} custom-call(bf16[2,512,128]{2,1,0:T(8,128)(2,1)S(1)} %get-tuple-element.53.attn_t, bf16[512,1024]{1,0:T(8,128)(2,1)S(1)} %get-tuple-element.54.w_out, bf16[64,256]{1,0:T(8,128)(2,1)S(1)} %get-tuple-element.76.before.refs_0_), custom_call_target="tpu_custom_call" | custom-call | flops 5000000000 | bytes 20000000 | tf_op jit(solution)/shard_map/pallas_call | solution.py:413
  37.4 0.2 collective-permute-done.13.chip_kv
  37.6 0.9 %shard_map.115 = (bf16[256,512]{1,0:T(8,128)(2,1)}, bf16[256,512]{1,0:T(8,128)(2,1)}, f32[8,128]{1,0:T(8,128)S(1)}) custom-call(f32[256,512]{1,0:T(8,128)S(1)} %get-tuple-element.78.k_own, f32[256,512]{1,0:T(8,128)S(1)} %get-tuple-element.79.v_own, bf16[2,128,512]{2,1,0:T(8,128)(2,1)S(1)} %collective-permute-done.9.refs_4_.link_kv, ...), custom_call_target="tpu_custom_call" | custom-call | flops 1000000 | bytes 4000 | tf_op jit(solution)/shard_map/pallas_call | solution.py:413
  38.5 0.0 collective-permute-done.14.refs_1_
  38.5 0.0 collective-permute-done.15.refs_2_
  38.5 0.6 %collective-permute-done.16.refs_3_ = bf16[64,256]{1,0:T(8,128)(2,1)S(1)} collective-permute-done((bf16[64,256]{1,0:T(8,128)(2,1)S(1)}, bf16[64,256]{1,0:T(8,128)(2,1)S(1)}, u32[]{:S(2)}, u32[]{:S(2)}) %collective-permute-start.16) | collective-permute-done | bytes 32800 | tf_op jit(solution)/shard_map/ppermute | solution.py:568
  39.1 0.7 %shard_map.116 = f32[64,1024]{1,0:T(8,128)} custom-call(f32[8,128]{1,0:T(8,128)S(1)} %get-tuple-element.86.before, bf16[64,256]{1,0:T(8,128)(2,1)S(1)} %shard_map.113.before.refs_0_, bf16[64,256]{1,0:T(8,128)(2,1)S(1)} %collective-permute-done.14.refs_1_, bf16[64,256]{1,0:T(8,128)(2,1)S(1)} %collective-permute-done.15.refs_2_, ...), custom_call_target="tpu_custom_call" | custom-call | flops 1000000 | bytes 4000 | tf_op jit(solution)/shard_map/pallas_call | solution.py:413
  (6 shorter events, 0.1 us)
Async XLA Ops:
  1.6 11.3 %collective-permute-start = (bf16[2,128,512]{2,1,0:T(8,128)(2,1)S(1)}, bf16[2,128,512]{2,1,0:T(8,128)(2,1)S(1)}, u32[]{:S(2)}, u32[]{:S(2)}) collective-permute-start(bf16[2,128,512]{2,1,0:T(8,128)(2,1)S(1)} %shard_map.102), channel_id=1, source_target_pairs={{0,7},{1,2},{2,1},{3,4},{4,3},{5,6},{6,5},{7,0},{8,15},{9,10},{10,... | collective-permute-start | bytes 786440 | tf_op jit(solution)/shard_map/ppermute | solution.py:463
  7.2 5.2 %collective-permute-start.1 = (bf16[128,512]{1,0:T(8,128)(2,1)S(1)}, bf16[128,512]{1,0:T(8,128)(2,1)S(1)}, u32[]{:S(2)}, u32[]{:S(2)}) collective-permute-start(bf16[128,512]{1,0:T(8,128)(2,1)S(1)} %get-tuple-element.49), channel_id=1, source_target_pairs={{0,1},{1,0},{2,3},{3,2},{4,5},{5,4},{6,7},{7,6},{8,9},{9,8},{10,11... | collective-permute-start | bytes 393224 | tf_op jit(solution)/shard_map/ppermute | solution.py:464
  7.3 5.1 %collective-permute-start.2 = (bf16[128,512]{1,0:T(8,128)(2,1)S(1)}, bf16[128,512]{1,0:T(8,128)(2,1)S(1)}, u32[]{:S(2)}, u32[]{:S(2)}) collective-permute-start(bf16[128,512]{1,0:T(8,128)(2,1)S(1)} %get-tuple-element.50), channel_id=1, source_target_pairs={{0,1},{1,0},{2,3},{3,2},{4,5},{5,4},{6,7},{7,6},{8,9},{9,8},{10,11... | collective-permute-start | bytes 393224 | tf_op jit(solution)/shard_map/ppermute | solution.py:464
  11.8 3.0 %collective-permute-start.4 = (bf16[128,1024]{1,0:T(8,128)(2,1)S(1)}, bf16[128,1024]{1,0:T(8,128)(2,1)S(1)}, u32[]{:S(2)}, u32[]{:S(2)}) collective-permute-start(bf16[128,1024]{1,0:T(8,128)(2,1)S(1)} %get-tuple-element.56.g_low), channel_id=1, source_target_pairs={{0,1},{1,0},{2,3},{3,2},{4,5},{5,4},{6,7},{7,6},{8,9},{9,8},{10,11... | collective-permute-start | bytes 786440 | tf_op jit(solution)/shard_map/ppermute | solution.py:490
  11.9 2.9 %collective-permute-start.5 = (bf16[128,1024]{1,0:T(8,128)(2,1)S(1)}, bf16[128,1024]{1,0:T(8,128)(2,1)S(1)}, u32[]{:S(2)}, u32[]{:S(2)}) collective-permute-start(bf16[128,1024]{1,0:T(8,128)(2,1)S(1)} %get-tuple-element.57.g_high), channel_id=1, source_target_pairs={{0,1},{1,0},{2,3},{3,2},{4,5},{5,4},{6,7},{7,6},{8,9},{9,8},{10,11... | collective-permute-start | bytes 786440 | tf_op jit(solution)/shard_map/ppermute | solution.py:490
  13.5 1.4 %collective-permute-start.3 = (bf16[4,64,256]{2,1,0:T(8,128)(2,1)S(1)}, bf16[4,64,256]{2,1,0:T(8,128)(2,1)S(1)}, u32[]{:S(2)}, u32[]{:S(2)}) collective-permute-start(bf16[4,64,256]{2,1,0:T(8,128)(2,1)S(1)} %get-tuple-element.58), channel_id=1, source_target_pairs={{0,1},{1,0},{2,3},{3,2},{4,5},{5,4},{6,7},{7,6},{8,9},{9,8},{10,11... | collective-permute-start | bytes 393224 | tf_op jit(solution)/shard_map/ppermute | solution.py:519
  15.2 7.4 %collective-permute-start.6 = (bf16[4,64,256]{2,1,0:T(8,128)(2,1)S(1)}, bf16[4,64,256]{2,1,0:T(8,128)(2,1)S(1)}, u32[]{:S(2)}, u32[]{:S(2)}) collective-permute-start(bf16[4,64,256]{2,1,0:T(8,128)(2,1)S(1)} %get-tuple-element.65), channel_id=1, source_target_pairs={{0,8},{8,0},{16,24},{24,16},{1,9},{9,1},{17,25},{25,17},{2,10},{10... | collective-permute-start | bytes 393224 | tf_op jit(solution)/shard_map/ppermute | solution.py:555
  17.1 8.4 %collective-permute-start.7 = (bf16[4,64,256]{2,1,0:T(8,128)(2,1)S(1)}, bf16[4,64,256]{2,1,0:T(8,128)(2,1)S(1)}, u32[]{:S(2)}, u32[]{:S(2)}) collective-permute-start(bf16[4,64,256]{2,1,0:T(8,128)(2,1)S(1)} %get-tuple-element.66), channel_id=1, source_target_pairs={{0,16},{8,24},{16,0},{24,8},{1,17},{9,25},{17,1},{25,9},{2,18},{10... | collective-permute-start | bytes 393224 | tf_op jit(solution)/shard_map/ppermute | solution.py:555
  18.7 6.8 %collective-permute-start.8 = (bf16[4,64,256]{2,1,0:T(8,128)(2,1)S(1)}, bf16[4,64,256]{2,1,0:T(8,128)(2,1)S(1)}, u32[]{:S(2)}, u32[]{:S(2)}) collective-permute-start(bf16[4,64,256]{2,1,0:T(8,128)(2,1)S(1)} %get-tuple-element.67), channel_id=1, source_target_pairs={{0,24},{8,16},{16,8},{24,0},{1,25},{9,17},{17,9},{25,1},{2,26},{10... | collective-permute-start | bytes 393224 | tf_op jit(solution)/shard_map/ppermute | solution.py:555
  18.8 13.6 %collective-permute-start.9 = (bf16[2,128,512]{2,1,0:T(8,128)(2,1)S(1)}, bf16[2,128,512]{2,1,0:T(8,128)(2,1)S(1)}, u32[]{:S(2)}, u32[]{:S(2)}) collective-permute-start(bf16[2,128,512]{2,1,0:T(8,128)(2,1)S(1)} %shard_map.109.before), channel_id=1, source_target_pairs={{0,7},{1,2},{2,1},{3,4},{4,3},{5,6},{6,5},{7,0},{8,15},{9,10},{10,... | collective-permute-start | bytes 786440 | tf_op jit(solution)/shard_map/ppermute | solution.py:541
  25.6 5.1 %collective-permute-start.10 = (bf16[64,256]{1,0:T(8,128)(2,1)S(1)}, bf16[64,256]{1,0:T(8,128)(2,1)S(1)}, u32[]{:S(2)}, u32[]{:S(2)}) collective-permute-start(bf16[64,256]{1,0:T(8,128)(2,1)S(1)} %get-tuple-element.81), channel_id=1, source_target_pairs={{0,4},{1,5},{2,6},{3,7},{4,0},{5,1},{6,2},{7,3},{8,12},{9,13},{10,... | collective-permute-start | bytes 98312 | tf_op jit(solution)/shard_map/ppermute | solution.py:559
  26.7 5.7 %collective-permute-start.11 = (bf16[64,256]{1,0:T(8,128)(2,1)S(1)}, bf16[64,256]{1,0:T(8,128)(2,1)S(1)}, u32[]{:S(2)}, u32[]{:S(2)}) collective-permute-start(bf16[64,256]{1,0:T(8,128)(2,1)S(1)} %get-tuple-element.82), channel_id=1, source_target_pairs={{0,6},{1,7},{2,4},{3,5},{4,2},{5,3},{6,0},{7,1},{8,14},{9,15},{10,... | collective-permute-start | bytes 98312 | tf_op jit(solution)/shard_map/ppermute | solution.py:559
  27.8 4.6 %collective-permute-start.12 = (bf16[64,256]{1,0:T(8,128)(2,1)S(1)}, bf16[64,256]{1,0:T(8,128)(2,1)S(1)}, u32[]{:S(2)}, u32[]{:S(2)}) collective-permute-start(bf16[64,256]{1,0:T(8,128)(2,1)S(1)} %get-tuple-element.83), channel_id=1, source_target_pairs={{0,2},{1,3},{2,0},{3,1},{4,6},{5,7},{6,4},{7,5},{8,10},{9,11},{10,... | collective-permute-start | bytes 98312 | tf_op jit(solution)/shard_map/ppermute | solution.py:559
  32.4 6.1 %collective-permute-start.14 = (bf16[64,256]{1,0:T(8,128)(2,1)S(1)}, bf16[64,256]{1,0:T(8,128)(2,1)S(1)}, u32[]{:S(2)}, u32[]{:S(2)}) collective-permute-start(bf16[64,256]{1,0:T(8,128)(2,1)S(1)} %shard_map.113.before.refs_0_), channel_id=1, source_target_pairs={{0,24},{8,16},{16,8},{24,0},{1,25},{9,17},{17,9},{25,1},{2,26},{10... | collective-permute-start | bytes 98312 | tf_op jit(solution)/shard_map/ppermute | solution.py:568
  34.0 4.5 %collective-permute-start.15 = (bf16[64,256]{1,0:T(8,128)(2,1)S(1)}, bf16[64,256]{1,0:T(8,128)(2,1)S(1)}, u32[]{:S(2)}, u32[]{:S(2)}) collective-permute-start(bf16[64,256]{1,0:T(8,128)(2,1)S(1)} %shard_map.113.before.refs_0_), channel_id=1, source_target_pairs={{0,16},{8,24},{16,0},{24,8},{1,17},{9,25},{17,1},{25,9},{2,18},{10... | collective-permute-start | bytes 98312 | tf_op jit(solution)/shard_map/ppermute | solution.py:568
  35.2 3.9 %collective-permute-start.16 = (bf16[64,256]{1,0:T(8,128)(2,1)S(1)}, bf16[64,256]{1,0:T(8,128)(2,1)S(1)}, u32[]{:S(2)}, u32[]{:S(2)}) collective-permute-start(bf16[64,256]{1,0:T(8,128)(2,1)S(1)} %shard_map.113.before.refs_0_), channel_id=1, source_target_pairs={{0,8},{8,0},{16,24},{24,16},{1,9},{9,1},{17,25},{25,17},{2,10},{10... | collective-permute-start | bytes 98312 | tf_op jit(solution)/shard_map/ppermute | solution.py:568
  36.0 1.6 %collective-permute-start.13 = (bf16[2,128,512]{2,1,0:T(8,128)(2,1)S(1)}, bf16[2,128,512]{2,1,0:T(8,128)(2,1)S(1)}, u32[]{:S(2)}, u32[]{:S(2)}) collective-permute-start(bf16[2,128,512]{2,1,0:T(8,128)(2,1)S(1)} %shard_map.114), channel_id=1, source_target_pairs={{0,1},{1,0},{2,3},{3,2},{4,5},{5,4},{6,7},{7,6},{8,9},{9,8},{10,11... | collective-permute-start | bytes 786440 | tf_op jit(solution)/shard_map/ppermute | solution.py:570

commit v23 on v18

--- a/solution.py
+++ b/solution.py
@@ -547,7 +547,7 @@
         scratch=[vmem(*own_scores, dtype=F32), vmem(*own_scores), vmem(*own_scores)],
     )
 
-    halves = [halves[0]] + [lax.ppermute(halves[s], "dp", swap(dp, s)) for s in range(1, dp)]
+    halves = [halves[0]] + [lax.ppermute(halves[s], "dp", swap(dp, s)) for s in (dp - 1, *range(1, dp - 1))]
     quarters = call(chips_kernel, [vmem(rows, cols)] * chips, 10**6, *halves, after)
     (output,) = call(output_kernel, [hbm(tokens, width)], 5 * 10**9, attn_t, w_out, quarters[0])
     quarters = [quarters[0]] + [

time: 39.9 us -> 39.9 us (level)
  no operation moved by 1% of the time
where the time goes in v23:
time: 39.9 us; the launch traced here: 39.7 us
  starting transfers between devices  17.9 us (45%)
  Pallas kernels  12.7 us (32%)
  waiting for transfers between devices  7.34 us (18%)
  other arithmetic  0.75 us (2%)
  between operations  0.74 us (2%)
    pallas_call x11, Pallas kernels, call(): pl.pallas_call(kernel, out_shape=outs, in_specs=[in_vmem] * len(args), ou...  7.7 us
    pallas_call x3, Pallas kernels, call_on_hbm(): pl.pallas_call(kernel, out_shape=outs, in_specs=[pl.BlockSpec(memory_spac...  4.99 us
    ppermute x1, starting transfers between devices, body(): link = lax.ppermute(to_link, 'ctx', over_links(ctx))  4.55 us
    ppermute x3, starting transfers between devices, body(): lax.ppermute(quarters[s], 'ctx', swap(ctx, 2 * s))  3.55 us
    ppermute x3, starting transfers between devices, body(): lax.ppermute(halves[s], 'dp', swap(dp, s))  3.55 us
    ppermute x3, starting transfers between devices, body(): lax.ppermute(piece, 'dp', swap(dp, s))  3.55 us
    ppermute x3, waiting for transfers between devices, body(): lax.ppermute(quarters[s], 'ctx', swap(ctx, 2 * s))  3.27 us
    ppermute x3, waiting for transfers between devices, body(): lax.ppermute(halves[s], 'dp', swap(dp, s))  1.76 us
  transfers between devices with their start and end apart: 17, of which 6 were waited for; matrix products, arithmetic and copies ran while one was open for 3% of the time, Pallas kernels for 27%

profile of v23, /device:TPU:0, one launch (start us, length us, event | category | flops | bytes accessed | tf_op | source)
XLA Modules:
  0.0 39.7 jit_solution(16534524119981474559)
XLA Ops:
  0.6 1.0 %shard_map.102 = bf16[2,128,512]{2,1,0:T(8,128)(2,1)S(1)} custom-call(bf16[256,512]{1,0:T(8,128)(2,1)} %bitcast.8, bf16[256,512]{1,0:T(8,128)(2,1)} %bitcast.11), custom_call_target="tpu_custom_call" | custom-call | flops 1000000 | bytes 4096 | tf_op jit(solution)/shard_map/pallas_call | solution.py:420
  1.6 4.6 %collective-permute-start = (bf16[2,128,512]{2,1,0:T(8,128)(2,1)S(1)}, bf16[2,128,512]{2,1,0:T(8,128)(2,1)S(1)}, u32[]{:S(2)}, u32[]{:S(2)}) collective-permute-start(bf16[2,128,512]{2,1,0:T(8,128)(2,1)S(1)} %shard_map.102), channel_id=1, source_target_pairs={{0,7},{1,2},{2,1},{3,4},{4,3},{5,6},{6,5},{7,0},{8,15},{9,10},{10,... | collective-permute-start | bytes 786440 | tf_op jit(solution)/shard_map/ppermute | solution.py:458
  6.2 1.0 %shard_map.103 = (bf16[128,512]{1,0:T(8,128)(2,1)S(1)}, bf16[128,512]{1,0:T(8,128)(2,1)S(1)}) custom-call(bf16[256,512]{1,0:T(8,128)(2,1)} %bitcast.9, bf16[256,512]{1,0:T(8,128)(2,1)} %bitcast.12), custom_call_target="tpu_custom_call" | custom-call | flops 1000000 | bytes 4096 | tf_op jit(solution)/shard_map/pallas_call | solution.py:420
  7.2 0.1 collective-permute-start.1
  7.3 0.5 %collective-permute-start.2 = (bf16[128,512]{1,0:T(8,128)(2,1)S(1)}, bf16[128,512]{1,0:T(8,128)(2,1)S(1)}, u32[]{:S(2)}, u32[]{:S(2)}) collective-permute-start(bf16[128,512]{1,0:T(8,128)(2,1)S(1)} %get-tuple-element.49), channel_id=1, source_target_pairs={{0,1},{1,0},{2,3},{3,2},{4,5},{5,4},{6,7},{7,6},{8,9},{9,8},{10,11... | collective-permute-start | bytes 393224 | tf_op jit(solution)/shard_map/ppermute | solution.py:459
  7.8 0.8 %compare_select_fusion = f32[1,2,3]{1,0,2:T(1,128)S(1)} fusion(s32[1,16,3]{1,0,2:T(1,128)} %param.11, s32[]{:T(128)S(6)} %select_n.14), kind=kLoop, calls=%fused_computation | loop fusion | flops 12 | bytes 52 | tf_op jit(solution)/shard_map/jit(_where)/select_n | solution.py:461
  8.5 0.1 copy.11
  8.6 0.1 select_n.16
  8.7 0.1 broadcast_in_dim.27.bias
  8.8 3.0 %shard_map.101 = (bf16[256,512]{1,0:T(8,128)(2,1)S(1)}, bf16[256,512]{1,0:T(8,128)(2,1)S(1)}, bf16[256,512]{1,0:T(8,128)(2,1)S(1)}, bf16[128,1024]{1,0:T(8,128)(...) custom-call(f32[6,1,256]{2,1,0:T(1,128)S(1)} %broadcast_in_dim.27.bi, ...), custom_call_target="tpu_custom_call" | custom-call | flops 1000000 | bytes 4096 | tf_op jit(solution)/shard_map/pallas_call | solution.py:420
  11.8 0.1 collective-permute-start.4
  11.9 0.4 %collective-permute-start.5 = (bf16[128,1024]{1,0:T(8,128)(2,1)S(1)}, bf16[128,1024]{1,0:T(8,128)(2,1)S(1)}, u32[]{:S(2)}, u32[]{:S(2)}) collective-permute-start(bf16[128,1024]{1,0:T(8,128)(2,1)S(1)} %get-tuple-element.56.g_high), channel_id=1, source_target_pairs={{0,1},{1,0},{2,3},{3,2},{4,5},{5,4},{6,7},{7,6},{8,9},{9,8},{10,11... | collective-permute-start | bytes 786440 | tf_op jit(solution)/shard_map/ppermute | solution.py:485
  12.4 0.0 collective-permute-done.1.rim_k.chip_k
  12.4 0.0 collective-permute-done.2.rim_v.chip_v
  12.4 0.5 %shard_map.104 = (f32[512,128]{1,0:T(8,128)S(1)}, f32[2,4,256]{2,1,0:T(4,128)S(1)}, f32[4,128,256]{2,1,0:T(8,128)S(1)}) custom-call(f32[6,1,256]{2,1,0:T(1,128)S(1)} %broadcast_in_dim.27.bias, bf16[256,512]{1,0:T(8,128)(2,1)S(1)} %get-tuple-element.45.q, bf16[128,512]{1,0:T(8,128)(2,1)S(1)} %collective-permute-done.1.rim_k.chip_k, ...), custom_call_target="tpu_custom_call" | custom-call | flops 1000000 | bytes 4000 | tf_op jit(solution)/shard_map/pallas_call | solution.py:408
  12.9 0.0 collective-permute-done.rim.link
  12.9 0.6 %shard_map.105 = (bf16[2,512,128]{2,1,0:T(8,128)(2,1)S(1)}, bf16[4,64,256]{2,1,0:T(8,128)(2,1)S(1)}, bf16[4,64,256]{2,1,0:T(8,128)(2,1)S(1)}, f32[4,128,256]{2,1...) custom-call(f32[6,1,256]{2,1,0:T(1,128)S(1)} %broadcast_in_dim.27.bias, ...), custom_call_target="tpu_custom_call" | custom-call | flops 1000000 | bytes 4000 | tf_op jit(solution)/shard_map/pallas_call | solution.py:408
  13.5 0.1 collective-permute-start.3
  13.6 0.3 shard_map.106.product
  13.9 0.0 collective-permute-done.5.g_high
  13.9 0.9 %collective-permute-done.3.other = bf16[4,64,256]{2,1,0:T(8,128)(2,1)S(1)} collective-permute-done((bf16[4,64,256]{2,1,0:T(8,128)(2,1)S(1)}, bf16[4,64,256]{2,1,0:T(8,128)(2,1)S(1)}, u32[]{:S(2)}, u32[]{:S(2)}) %collective-permute-start.3) | collective-permute-done | bytes 131104 | tf_op jit(solution)/shard_map/ppermute | solution.py:514
  14.9 0.3 shard_map.107
  15.2 2.9 %collective-permute-start.6 = (bf16[4,64,256]{2,1,0:T(8,128)(2,1)S(1)}, bf16[4,64,256]{2,1,0:T(8,128)(2,1)S(1)}, u32[]{:S(2)}, u32[]{:S(2)}) collective-permute-start(bf16[4,64,256]{2,1,0:T(8,128)(2,1)S(1)} %get-tuple-element.59), channel_id=1, source_target_pairs={{0,24},{8,16},{16,8},{24,0},{1,25},{9,17},{17,9},{25,1},{2,26},{10... | collective-permute-start | bytes 393224 | tf_op jit(solution)/shard_map/ppermute | solution.py:550
  18.1 0.5 %collective-permute-start.7 = (bf16[4,64,256]{2,1,0:T(8,128)(2,1)S(1)}, bf16[4,64,256]{2,1,0:T(8,128)(2,1)S(1)}, u32[]{:S(2)}, u32[]{:S(2)}) collective-permute-start(bf16[4,64,256]{2,1,0:T(8,128)(2,1)S(1)} %get-tuple-element.60), channel_id=1, source_target_pairs={{0,8},{8,0},{16,24},{24,16},{1,9},{9,1},{17,25},{25,17},{2,10},{10... | collective-permute-start | bytes 393224 | tf_op jit(solution)/shard_map/ppermute | solution.py:550
  18.6 0.1 collective-permute-start.8
  18.8 0.9 %shard_map.108 = (bf16[2,128,512]{2,1,0:T(8,128)(2,1)S(1)}, bf16[2,128,512]{2,1,0:T(8,128)(2,1)S(1)}, f32[2,4,256]{2,1,0:T(4,128)S(1)}, f32[2,512,128]{2,1,0:T(8,128)S(1)}) custom-call(bf16[256,512]{1,0:T(8,128)(2,1)S(1)} %get-tuple-element.45.q, bf16[2,128,512]{2,1,0:T(8,128)(2,1)S(1)} %collective-permute-done.rim.link, ...), custom_call_target="tpu_custom_call" | custom-call | flops 1000000 | bytes 4000 | tf_op jit(solution)/shard_map/pallas_call | solution.py:408
  19.7 1.4 %collective-permute-start.9 = (bf16[2,128,512]{2,1,0:T(8,128)(2,1)S(1)}, bf16[2,128,512]{2,1,0:T(8,128)(2,1)S(1)}, u32[]{:S(2)}, u32[]{:S(2)}) collective-permute-start(bf16[2,128,512]{2,1,0:T(8,128)(2,1)S(1)} %get-tuple-element.78), channel_id=1, source_target_pairs={{0,7},{1,2},{2,1},{3,4},{4,3},{5,6},{6,5},{7,0},{8,15},{9,10},{10,... | collective-permute-start | bytes 786440 | tf_op jit(solution)/shard_map/ppermute | solution.py:535
  21.1 2.1 %shard_map.109 = (bf16[256,512]{1,0:T(8,128)(2,1)}, f32[256,512]{1,0:T(8,128)S(1)}, f32[256,512]{1,0:T(8,128)S(1)}, f32[8,128]{1,0:T(8,128)S(1)}) custom-call(bf16[256,512]{1,0:T(8,128)(2,1)S(1)} %get-tuple-element.45.q, bf16[256,512]{1,0:T(8,128)(2,1)S(1)} %get-tuple-element.62.k, bf16[256,512]{1,0:T(8,128)(2,1)S(1)} %get-tuple-element.63.v, ...), custom_call_target="tpu_custom_call" | custom-call | flops 5000000000 | bytes 20000000 | tf_op jit(solution)/shard_map/pallas_call | solution.py:408
  23.2 1.8 %collective-permute-done.7.refs_2_ = bf16[4,64,256]{2,1,0:T(8,128)(2,1)S(1)} collective-permute-done((bf16[4,64,256]{2,1,0:T(8,128)(2,1)S(1)}, bf16[4,64,256]{2,1,0:T(8,128)(2,1)S(1)}, u32[]{:S(2)}, u32[]{:S(2)}) %collective-permute-start.7) | collective-permute-done | bytes 131104 | tf_op jit(solution)/shard_map/ppermute | solution.py:550
  25.0 0.1 shard_map.110
  25.1 1.1 %collective-permute-start.11 = (bf16[64,256]{1,0:T(8,128)(2,1)S(1)}, bf16[64,256]{1,0:T(8,128)(2,1)S(1)}, u32[]{:S(2)}, u32[]{:S(2)}) collective-permute-start(bf16[64,256]{1,0:T(8,128)(2,1)S(1)} %get-tuple-element.82), channel_id=1, source_target_pairs={{0,4},{1,5},{2,6},{3,7},{4,0},{5,1},{6,2},{7,3},{8,12},{9,13},{10,... | collective-permute-start | bytes 98312 | tf_op jit(solution)/shard_map/ppermute | solution.py:554
  26.2 1.1 %collective-permute-start.12 = (bf16[64,256]{1,0:T(8,128)(2,1)S(1)}, bf16[64,256]{1,0:T(8,128)(2,1)S(1)}, u32[]{:S(2)}, u32[]{:S(2)}) collective-permute-start(bf16[64,256]{1,0:T(8,128)(2,1)S(1)} %get-tuple-element.83), channel_id=1, source_target_pairs={{0,6},{1,7},{2,4},{3,5},{4,2},{5,3},{6,0},{7,1},{8,14},{9,15},{10,... | collective-permute-start | bytes 98312 | tf_op jit(solution)/shard_map/ppermute | solution.py:554
  27.3 1.3 %collective-permute-start.13 = (bf16[64,256]{1,0:T(8,128)(2,1)S(1)}, bf16[64,256]{1,0:T(8,128)(2,1)S(1)}, u32[]{:S(2)}, u32[]{:S(2)}) collective-permute-start(bf16[64,256]{1,0:T(8,128)(2,1)S(1)} %get-tuple-element.84), channel_id=1, source_target_pairs={{0,2},{1,3},{2,0},{3,1},{4,6},{5,7},{6,4},{7,5},{8,10},{9,11},{10,... | collective-permute-start | bytes 98312 | tf_op jit(solution)/shard_map/ppermute | solution.py:554
  28.6 0.0 collective-permute-start.10
  28.6 2.5 %collective-permute-done.11.refs_1_ = bf16[64,256]{1,0:T(8,128)(2,1)S(1)} collective-permute-done((bf16[64,256]{1,0:T(8,128)(2,1)S(1)}, bf16[64,256]{1,0:T(8,128)(2,1)S(1)}, u32[]{:S(2)}, u32[]{:S(2)}) %collective-permute-start.11) | collective-permute-done | bytes 32800 | tf_op jit(solution)/shard_map/ppermute | solution.py:554
  31.1 0.8 %collective-permute-done.12.refs_2_ = bf16[64,256]{1,0:T(8,128)(2,1)S(1)} collective-permute-done((bf16[64,256]{1,0:T(8,128)(2,1)S(1)}, bf16[64,256]{1,0:T(8,128)(2,1)S(1)}, u32[]{:S(2)}, u32[]{:S(2)}) %collective-permute-start.12) | collective-permute-done | bytes 32800 | tf_op jit(solution)/shard_map/ppermute | solution.py:554
  31.9 0.0 collective-permute-done.13.refs_3_
  31.9 0.0 collective-permute-done.9.link_kv.refs_4_
  31.9 2.6 %collective-permute-start.14 = (bf16[64,256]{1,0:T(8,128)(2,1)S(1)}, bf16[64,256]{1,0:T(8,128)(2,1)S(1)}, u32[]{:S(2)}, u32[]{:S(2)}) collective-permute-start(bf16[64,256]{1,0:T(8,128)(2,1)S(1)} %shard_map.113.refs_0_), channel_id=1, source_target_pairs={{0,24},{8,16},{16,8},{24,0},{1,25},{9,17},{17,9},{25,1},{2,26},{10... | collective-permute-start | bytes 98312 | tf_op jit(solution)/shard_map/ppermute | solution.py:563
  34.5 0.6 %collective-permute-start.15 = (bf16[64,256]{1,0:T(8,128)(2,1)S(1)}, bf16[64,256]{1,0:T(8,128)(2,1)S(1)}, u32[]{:S(2)}, u32[]{:S(2)}) collective-permute-start(bf16[64,256]{1,0:T(8,128)(2,1)S(1)} %shard_map.113.refs_0_), channel_id=1, source_target_pairs={{0,16},{8,24},{16,0},{24,8},{1,17},{9,25},{17,1},{25,9},{2,18},{10... | collective-permute-start | bytes 98312 | tf_op jit(solution)/shard_map/ppermute | solution.py:563
  35.0 0.4 %collective-permute-start.16 = (bf16[64,256]{1,0:T(8,128)(2,1)S(1)}, bf16[64,256]{1,0:T(8,128)(2,1)S(1)}, u32[]{:S(2)}, u32[]{:S(2)}) collective-permute-start(bf16[64,256]{1,0:T(8,128)(2,1)S(1)} %shard_map.113.refs_0_), channel_id=1, source_target_pairs={{0,8},{8,0},{16,24},{24,16},{1,9},{9,1},{17,25},{25,17},{2,10},{10... | collective-permute-start | bytes 98312 | tf_op jit(solution)/shard_map/ppermute | solution.py:563
  35.5 1.3 %shard_map.111 = bf16[256,1024]{1,0:T(8,128)(2,1)} custom-call(bf16[2,512,128]{2,1,0:T(8,128)(2,1)S(1)} %get-tuple-element.52.attn_t, bf16[512,1024]{1,0:T(8,128)(2,1)S(1)} %get-tuple-element.53.w_out, bf16[64,256]{1,0:T(8,128)(2,1)S(1)} %get-tuple-element.74.before.refs_0_), custom_call_target="tpu_custom_call" | custom-call | flops 5000000000 | bytes 20000000 | tf_op jit(solution)/shard_map/pallas_call | solution.py:408
  36.7 0.0 collective-permute-done.10.chip_kv
  36.7 0.9 %shard_map.112 = (bf16[256,512]{1,0:T(8,128)(2,1)}, bf16[256,512]{1,0:T(8,128)(2,1)}) custom-call(f32[256,512]{1,0:T(8,128)S(1)} %get-tuple-element.76.k_own, f32[256,512]{1,0:T(8,128)S(1)} %get-tuple-element.77.v_own, bf16[2,128,512]{2,1,0:T(8,128)(2,1)S(1)} %collective-permute-done.9.link_kv.refs_4_, bf16[2,128,512]{2,1,0:T(8,128)(2,1)S(1)} %collective-permute-done.10.chip_kv), custom_call_target="tpu_custom_call" | custom-call | flops 1000000 | bytes 4000 | tf_op jit(solution)/shard_map/pallas_call | solution.py:408
  37.6 0.0 collective-permute-done.14.refs_1_
  37.6 0.8 %collective-permute-done.15.refs_2_ = bf16[64,256]{1,0:T(8,128)(2,1)S(1)} collective-permute-done((bf16[64,256]{1,0:T(8,128)(2,1)S(1)}, bf16[64,256]{1,0:T(8,128)(2,1)S(1)}, u32[]{:S(2)}, u32[]{:S(2)}) %collective-permute-start.15) | collective-permute-done | bytes 32800 | tf_op jit(solution)/shard_map/ppermute | solution.py:563
  38.4 0.6 %collective-permute-done.16.refs_3_ = bf16[64,256]{1,0:T(8,128)(2,1)S(1)} collective-permute-done((bf16[64,256]{1,0:T(8,128)(2,1)S(1)}, bf16[64,256]{1,0:T(8,128)(2,1)S(1)}, u32[]{:S(2)}, u32[]{:S(2)}) %collective-permute-start.16) | collective-permute-done | bytes 32800 | tf_op jit(solution)/shard_map/ppermute | solution.py:563
  39.0 0.7 %shard_map.114 = f32[64,1024]{1,0:T(8,128)} custom-call(bf16[64,256]{1,0:T(8,128)(2,1)S(1)} %shard_map.113.refs_0_, bf16[64,256]{1,0:T(8,128)(2,1)S(1)} %collective-permute-done.14.refs_1_, bf16[64,256]{1,0:T(8,128)(2,1)S(1)} %collective-permute-done.15.refs_2_, bf16[64,256]{1,0:T(8,128)(2,1)S(1)} %collective-permute-done.16.refs_3_), custom_call_target="tpu_custom_call" | custom-call | flops 1000000 | bytes 4000 | tf_op jit(solution)/shard_map/pallas_call | solution.py:408
  (4 shorter events, 0.0 us)
Async XLA Ops:
  1.6 11.3 %collective-permute-start = (bf16[2,128,512]{2,1,0:T(8,128)(2,1)S(1)}, bf16[2,128,512]{2,1,0:T(8,128)(2,1)S(1)}, u32[]{:S(2)}, u32[]{:S(2)}) collective-permute-start(bf16[2,128,512]{2,1,0:T(8,128)(2,1)S(1)} %shard_map.102), channel_id=1, source_target_pairs={{0,7},{1,2},{2,1},{3,4},{4,3},{5,6},{6,5},{7,0},{8,15},{9,10},{10,... | collective-permute-start | bytes 786440 | tf_op jit(solution)/shard_map/ppermute | solution.py:458
  7.2 5.2 %collective-permute-start.1 = (bf16[128,512]{1,0:T(8,128)(2,1)S(1)}, bf16[128,512]{1,0:T(8,128)(2,1)S(1)}, u32[]{:S(2)}, u32[]{:S(2)}) collective-permute-start(bf16[128,512]{1,0:T(8,128)(2,1)S(1)} %get-tuple-element.48), channel_id=1, source_target_pairs={{0,1},{1,0},{2,3},{3,2},{4,5},{5,4},{6,7},{7,6},{8,9},{9,8},{10,11... | collective-permute-start | bytes 393224 | tf_op jit(solution)/shard_map/ppermute | solution.py:459
  7.3 5.1 %collective-permute-start.2 = (bf16[128,512]{1,0:T(8,128)(2,1)S(1)}, bf16[128,512]{1,0:T(8,128)(2,1)S(1)}, u32[]{:S(2)}, u32[]{:S(2)}) collective-permute-start(bf16[128,512]{1,0:T(8,128)(2,1)S(1)} %get-tuple-element.49), channel_id=1, source_target_pairs={{0,1},{1,0},{2,3},{3,2},{4,5},{5,4},{6,7},{7,6},{8,9},{9,8},{10,11... | collective-permute-start | bytes 393224 | tf_op jit(solution)/shard_map/ppermute | solution.py:459
  11.8 2.1 %collective-permute-start.4 = (bf16[128,1024]{1,0:T(8,128)(2,1)S(1)}, bf16[128,1024]{1,0:T(8,128)(2,1)S(1)}, u32[]{:S(2)}, u32[]{:S(2)}) collective-permute-start(bf16[128,1024]{1,0:T(8,128)(2,1)S(1)} %get-tuple-element.55.g_low), channel_id=1, source_target_pairs={{0,1},{1,0},{2,3},{3,2},{4,5},{5,4},{6,7},{7,6},{8,9},{9,8},{10,11... | collective-permute-start | bytes 786440 | tf_op jit(solution)/shard_map/ppermute | solution.py:485
  11.9 2.0 %collective-permute-start.5 = (bf16[128,1024]{1,0:T(8,128)(2,1)S(1)}, bf16[128,1024]{1,0:T(8,128)(2,1)S(1)}, u32[]{:S(2)}, u32[]{:S(2)}) collective-permute-start(bf16[128,1024]{1,0:T(8,128)(2,1)S(1)} %get-tuple-element.56.g_high), channel_id=1, source_target_pairs={{0,1},{1,0},{2,3},{3,2},{4,5},{5,4},{6,7},{7,6},{8,9},{9,8},{10,11... | collective-permute-start | bytes 786440 | tf_op jit(solution)/shard_map/ppermute | solution.py:485
  13.5 1.4 %collective-permute-start.3 = (bf16[4,64,256]{2,1,0:T(8,128)(2,1)S(1)}, bf16[4,64,256]{2,1,0:T(8,128)(2,1)S(1)}, u32[]{:S(2)}, u32[]{:S(2)}) collective-permute-start(bf16[4,64,256]{2,1,0:T(8,128)(2,1)S(1)} %get-tuple-element.57), channel_id=1, source_target_pairs={{0,1},{1,0},{2,3},{3,2},{4,5},{5,4},{6,7},{7,6},{8,9},{9,8},{10,11... | collective-permute-start | bytes 393224 | tf_op jit(solution)/shard_map/ppermute | solution.py:514
  15.2 8.0 %collective-permute-start.6 = (bf16[4,64,256]{2,1,0:T(8,128)(2,1)S(1)}, bf16[4,64,256]{2,1,0:T(8,128)(2,1)S(1)}, u32[]{:S(2)}, u32[]{:S(2)}) collective-permute-start(bf16[4,64,256]{2,1,0:T(8,128)(2,1)S(1)} %get-tuple-element.59), channel_id=1, source_target_pairs={{0,24},{8,16},{16,8},{24,0},{1,25},{9,17},{17,9},{25,1},{2,26},{10... | collective-permute-start | bytes 393224 | tf_op jit(solution)/shard_map/ppermute | solution.py:550
  18.1 6.9 %collective-permute-start.7 = (bf16[4,64,256]{2,1,0:T(8,128)(2,1)S(1)}, bf16[4,64,256]{2,1,0:T(8,128)(2,1)S(1)}, u32[]{:S(2)}, u32[]{:S(2)}) collective-permute-start(bf16[4,64,256]{2,1,0:T(8,128)(2,1)S(1)} %get-tuple-element.60), channel_id=1, source_target_pairs={{0,8},{8,0},{16,24},{24,16},{1,9},{9,1},{17,25},{25,17},{2,10},{10... | collective-permute-start | bytes 393224 | tf_op jit(solution)/shard_map/ppermute | solution.py:550
  18.6 6.4 %collective-permute-start.8 = (bf16[4,64,256]{2,1,0:T(8,128)(2,1)S(1)}, bf16[4,64,256]{2,1,0:T(8,128)(2,1)S(1)}, u32[]{:S(2)}, u32[]{:S(2)}) collective-permute-start(bf16[4,64,256]{2,1,0:T(8,128)(2,1)S(1)} %get-tuple-element.61), channel_id=1, source_target_pairs={{0,16},{8,24},{16,0},{24,8},{1,17},{9,25},{17,1},{25,9},{2,18},{10... | collective-permute-start | bytes 393224 | tf_op jit(solution)/shard_map/ppermute | solution.py:550
  19.7 12.2 %collective-permute-start.9 = (bf16[2,128,512]{2,1,0:T(8,128)(2,1)S(1)}, bf16[2,128,512]{2,1,0:T(8,128)(2,1)S(1)}, u32[]{:S(2)}, u32[]{:S(2)}) collective-permute-start(bf16[2,128,512]{2,1,0:T(8,128)(2,1)S(1)} %get-tuple-element.78), channel_id=1, source_target_pairs={{0,7},{1,2},{2,1},{3,4},{4,3},{5,6},{6,5},{7,0},{8,15},{9,10},{10,... | collective-permute-start | bytes 786440 | tf_op jit(solution)/shard_map/ppermute | solution.py:535
  25.1 6.0 %collective-permute-start.11 = (bf16[64,256]{1,0:T(8,128)(2,1)S(1)}, bf16[64,256]{1,0:T(8,128)(2,1)S(1)}, u32[]{:S(2)}, u32[]{:S(2)}) collective-permute-start(bf16[64,256]{1,0:T(8,128)(2,1)S(1)} %get-tuple-element.82), channel_id=1, source_target_pairs={{0,4},{1,5},{2,6},{3,7},{4,0},{5,1},{6,2},{7,3},{8,12},{9,13},{10,... | collective-permute-start | bytes 98312 | tf_op jit(solution)/shard_map/ppermute | solution.py:554
  26.2 5.7 %collective-permute-start.12 = (bf16[64,256]{1,0:T(8,128)(2,1)S(1)}, bf16[64,256]{1,0:T(8,128)(2,1)S(1)}, u32[]{:S(2)}, u32[]{:S(2)}) collective-permute-start(bf16[64,256]{1,0:T(8,128)(2,1)S(1)} %get-tuple-element.83), channel_id=1, source_target_pairs={{0,6},{1,7},{2,4},{3,5},{4,2},{5,3},{6,0},{7,1},{8,14},{9,15},{10,... | collective-permute-start | bytes 98312 | tf_op jit(solution)/shard_map/ppermute | solution.py:554
  27.3 4.6 %collective-permute-start.13 = (bf16[64,256]{1,0:T(8,128)(2,1)S(1)}, bf16[64,256]{1,0:T(8,128)(2,1)S(1)}, u32[]{:S(2)}, u32[]{:S(2)}) collective-permute-start(bf16[64,256]{1,0:T(8,128)(2,1)S(1)} %get-tuple-element.84), channel_id=1, source_target_pairs={{0,2},{1,3},{2,0},{3,1},{4,6},{5,7},{6,4},{7,5},{8,10},{9,11},{10,... | collective-permute-start | bytes 98312 | tf_op jit(solution)/shard_map/ppermute | solution.py:554
  28.6 8.1 %collective-permute-start.10 = (bf16[2,128,512]{2,1,0:T(8,128)(2,1)S(1)}, bf16[2,128,512]{2,1,0:T(8,128)(2,1)S(1)}, u32[]{:S(2)}, u32[]{:S(2)}) collective-permute-start(bf16[2,128,512]{2,1,0:T(8,128)(2,1)S(1)} %get-tuple-element.79), channel_id=1, source_target_pairs={{0,1},{1,0},{2,3},{3,2},{4,5},{5,4},{6,7},{7,6},{8,9},{9,8},{10,11... | collective-permute-start | bytes 786440 | tf_op jit(solution)/shard_map/ppermute | solution.py:536
  31.9 5.7 %collective-permute-start.14 = (bf16[64,256]{1,0:T(8,128)(2,1)S(1)}, bf16[64,256]{1,0:T(8,128)(2,1)S(1)}, u32[]{:S(2)}, u32[]{:S(2)}) collective-permute-start(bf16[64,256]{1,0:T(8,128)(2,1)S(1)} %shard_map.113.refs_0_), channel_id=1, source_target_pairs={{0,24},{8,16},{16,8},{24,0},{1,25},{9,17},{17,9},{25,1},{2,26},{10... | collective-permute-start | bytes 98312 | tf_op jit(solution)/shard_map/ppermute | solution.py:563
  34.5 3.9 %collective-permute-start.15 = (bf16[64,256]{1,0:T(8,128)(2,1)S(1)}, bf16[64,256]{1,0:T(8,128)(2,1)S(1)}, u32[]{:S(2)}, u32[]{:S(2)}) collective-permute-start(bf16[64,256]{1,0:T(8,128)(2,1)S(1)} %shard_map.113.refs_0_), channel_id=1, source_target_pairs={{0,16},{8,24},{16,0},{24,8},{1,17},{9,25},{17,1},{25,9},{2,18},{10... | collective-permute-start | bytes 98312 | tf_op jit(solution)/shard_map/ppermute | solution.py:563
  35.0 3.9 %collective-permute-start.16 = (bf16[64,256]{1,0:T(8,128)(2,1)S(1)}, bf16[64,256]{1,0:T(8,128)(2,1)S(1)}, u32[]{:S(2)}, u32[]{:S(2)}) collective-permute-start(bf16[64,256]{1,0:T(8,128)(2,1)S(1)} %shard_map.113.refs_0_), channel_id=1, source_target_pairs={{0,8},{8,0},{16,24},{24,16},{1,9},{9,1},{17,25},{25,17},{2,10},{10... | collective-permute-start | bytes 98312 | tf_op jit(solution)/shard_map/ppermute | solution.py:563
